TPU v7x, 32 devices: a whole 2x2x4 slice. The times are simulated.
32 devices in a mesh: island: 2 (over y), blk: 4 (over z), sub: 2 (over x), pair: 2 (over core).
Axes of the slice: x: 2, y: 2, z: 4, core: 2. Of those that a mesh axis runs over, the one named last changes fastest.
Arguments:
- embeddings: bfloat16 [6144, 768], P(('island', 'blk', 'sub', 'pair')), parts along dimension 0, may hold values from -6 to 6
- group_of: int32 [6144, 1], P(('island', 'blk', 'sub', 'pair')), parts along dimension 0, may hold values from 0 to 3; in each aligned block of 192 rows (0 to 191, 192 to 383, ...) at most 96 rows name the same one
- cluster_id: int32 [6144], P(('island', 'blk', 'sub', 'pair')), parts along dimension 0, may hold values from 0 to 47
Outputs:
- neighbour_mean: bfloat16 [6144, 768], P(('island', 'blk', 'sub', 'pair')), parts along dimension 0
There are 2 independent parts, one for each index of `island`. A program takes and returns all parts, laid end to end along the dimension named above; each array names one. Nothing has to cross between parts.
Inputs may be any that keep to these rules, and one draw needn't show every extreme that they name: `group_of`: among the rows of one device, at most 96 name the same group; this bound is reached in every draw.
All inputs are finite; a program needn't handle non-finite values.
Results may differ from a plain program's by a relative error of at most 0.0045.
Values may be sent and summed in bfloat16 or wider, within the bound.
No kernel may reach another device: no remote copies, remote signals or barrier semaphores. Data moves between devices by JAX's collectives and lax.ppermute only.
A program may use at most 64 MiB of HBM per device.

v0:
```python
import jax
import jax.numpy as jnp
from jax import lax
from jax.sharding import PartitionSpec as P


def unit_scale(rows_in):
    wide = rows_in.astype(jnp.float32)
    return lax.rsqrt(jnp.sum(wide * wide, axis=1) + 1e-06)


def tile_weights(left_rows, left_clust, left_scale, right_rows, right_clust, right_scale):
    grams = lax.dot_general(
        left_rows, right_rows, (((1,), (1,)), ((), ())), preferred_element_type=jnp.float32
    )
    cosine = grams * left_scale[:, None] * right_scale[None, :]
    same = (left_clust[:, None] == right_clust[None, :]).astype(jnp.float32)
    return jax.nn.sigmoid(8.0 * cosine - 2.0) * same


def per_device(embeddings, group_of, cluster_id):
    rows_here, width = embeddings.shape
    n_sub = lax.axis_size("sub")
    n_pair = lax.axis_size("pair")
    groups = n_sub * n_pair
    capacity = 2 * rows_here // groups
    slots = groups * capacity
    target = group_of[:, 0]
    onehot = (target[:, None] == jnp.arange(groups, dtype=jnp.int32)[None, :]).astype(jnp.int32)
    position = jnp.sum((jnp.cumsum(onehot, axis=0) - onehot) * onehot, axis=1)
    send_rows = (
        jnp.zeros((groups, capacity, width), jnp.bfloat16).at[target, position].set(embeddings)
    )
    send_clust = jnp.full((groups, capacity), -1, jnp.int32).at[target, position].set(cluster_id)
    recv_rows, recv_clust = (
        lax.all_to_all(send_rows, ("sub", "pair"), split_axis=0, concat_axis=0, tiled=True),
        lax.all_to_all(send_clust, ("sub", "pair"), split_axis=0, concat_axis=0, tiled=True),
    )
    own_rows = recv_rows.reshape(slots, width)
    own_clust = recv_clust.reshape(slots)
    own_scale = unit_scale(own_rows)
    piece_rows = lax.all_gather(own_rows, "blk", axis=0, tiled=True)
    piece_clust = lax.all_gather(own_clust, "blk", axis=0, tiled=True)
    weight = tile_weights(
        own_rows, own_clust, own_scale, piece_rows, piece_clust, unit_scale(piece_rows)
    )
    numer_add = jnp.dot(weight.astype(jnp.bfloat16), piece_rows, preferred_element_type=jnp.float32)
    denom = jnp.sum(weight, axis=1)
    result = (numer_add / denom[:, None]).astype(jnp.bfloat16).reshape(groups, capacity, width)
    returned = lax.all_to_all(result, ("sub", "pair"), split_axis=0, concat_axis=0, tiled=True)
    return returned[target, position]


def solution(mesh):
    return jax.shard_map(
        per_device,
        mesh=mesh,
        in_specs=(
            P(("island", "blk", "sub", "pair"), None),
            P(("island", "blk", "sub", "pair"), None),
            P(("island", "blk", "sub", "pair")),
        ),
        out_specs=P(("island", "blk", "sub", "pair"), None),
        check_vma=False,
    )
```

profile of v0, /device:TPU:0, one launch (start us, length us, event | category | flops | bytes accessed | tf_op | source)
XLA Modules:
  0.0 121.4 jit_solution(1983517281829665574)
XLA Ops:
  6.5 0.0 all-gather.3.cloned.1.call-start
  6.5 0.7 iota_compare_fusion
  7.2 1.2 %reduce-window.6 = s32[4,2,128]{2,1,0:T(2,128)S(1)} reduce-window(s32[4,2,128]{2,1,0:T(2,128)S(1)} %reshape.57, s32[]{:T(128)} %constant.12.clone.1), window={size=1x1x128 pad=0_0x0_0x127_0}, to_apply=%region_0.0 | reduce-window | flops 130048 | bytes 8196 | tf_op jit(solution)/shard_map/reduce-window
  8.5 0.1 slice.18
  8.5 0.1 copy.8
  8.7 0.1 copy.9
  8.8 0.1 add_bitcast_fusion
  8.9 0.7 fusion.11
  9.6 0.7 or_select_fusion
  10.3 0.0 copy-start.2
  10.3 18.1 %scatter_fusion.1 = bf16[4,96,768]{2,1,0:T(8,128)(2,1)S(1)} fusion(bf16[4,96,768]{2,1,0:T(8,128)(2,1)S(1)} %broadcast_in_dim.5, s32[192]{0:T(256)S(1)} %bitcast.26, bf16[192,768]{1,0:T(8,128)(2,1)} %param.3), kind=kCustom, calls=%fused_computation.2 | custom fusion | bytes 886272 | tf_op jit(solution)/shard_map/scatter | solution.py:32
  28.5 13.7 %all_to_all.19 = bf16[4,96,768]{2,1,0:T(8,128)(2,1)} all-to-all(bf16[4,96,768]{2,1,0:T(8,128)(2,1)S(1)} %scatter_fusion.1), channel_id=1, replica_groups=mesh['island'=2,'blk'=4,'sub'=2,'pair'=2] {'sub','pair'}, dimensions={0} | all-to-all | bytes 1179648 | tf_op jit(solution)/shard_map/all_to_all | solution.py:36
  42.1 0.0 copy-start
  42.1 0.0 all-gather.3.cloned.1.call-update
  42.2 0.0 copy-done.2
  42.2 9.4 %scatter_fusion = s32[4,96]{1,0:T(4,128)S(1)} fusion(s32[4,96]{1,0:T(4,128)S(1)} %broadcast_in_dim.4, s32[192]{0:T(256)S(1)} %bitcast.27, s32[192]{0:T(256)S(1)} %copy-done.2), kind=kCustom, calls=%fused_computation.1 | custom fusion | bytes 3840 | tf_op jit(solution)/shard_map/scatter | solution.py:34
  51.6 6.1 %all_to_all.20 = s32[4,1,96]{2,1,0:T(1,128)S(1)} all-to-all(s32[4,1,96]{2,1,0:T(1,128)S(1)} %bitcast.25), channel_id=1, replica_groups=mesh['island'=2,'blk'=4,'sub'=2,'pair'=2] {'sub','pair'}, dimensions={0} | all-to-all | bytes 3072 | tf_op jit(solution)/shard_map/all_to_all | solution.py:37
  57.6 0.1 reshape.76
  57.7 0.5 broadcast.149
  58.2 0.7 reduce.7
  58.9 0.1 eq.44
  59.0 12.8 %all-gather = s32[4,1,384]{2,1,0:T(1,128)S(1)} all-gather(s32[1,1,384]{2,1,0:T(1,128)S(1)} %reshape.76), channel_id=1, replica_groups=mesh['island'=2,'blk'=4,'sub'=2,'pair'=2] {'blk'}, dimensions={0}, use_global_device_ids=true | all-gather | bytes 7680 | tf_op jit(solution)/shard_map/all_gather | solution.py:43
  71.8 0.0 copy-done
  71.8 0.2 multiply_reduce_fusion.1
  72.0 0.1 rsqrt.18
  72.1 21.5 %all-gather.3.cloned.1.call-done = bf16[1536,768]{1,0:T(8,128)(2,1)} async-done(((bf16[384,768]{1,0:T(8,128)(2,1)}), bf16[1536,768]{1,0:T(8,128)(2,1)}) %all-gather.3.cloned.1.call-update) | async-done | bytes 2359312 | tf_op jit(solution)/shard_map/all_gather | solution.py:42
  93.6 0.0 copy-start.1
  93.6 2.3 %multiply_reduce_fusion = f32[1536]{0:T(1024)S(1)} fusion(bf16[1536,768]{1,0:T(8,128)(2,1)} %all-gather.3.cloned.1.call-done), kind=kLoop, calls=%fused_computation.3 | loop fusion | flops 3537408 | bytes 2365440 | tf_op jit(solution)/shard_map/reduce_sum | solution.py:9
  96.0 0.0 copy-done.1
  96.0 1.6 %fusion.14 = (f32[384]{0:T(512)S(1)}, bf16[384,1536]{1,0:T(8,128)(2,1)S(1)}) fusion(f32[1536]{0:T(1024)S(1)} %add_rsqrt_fusion, f32[384]{0:T(512)S(1)} %rsqrt.18, bf16[384,768]{1,0:T(8,128)(2,1)S(1)} %bitcast.30, bf16[1536,768]{1,0:T(8,128)(2,1)S(1)} %copy-done.1, s32[1536]{0:T(1024)S(1)} %reshape.77, s32[384]{0:T(512)S(1)} %eq.44), kind=kOutput, calls=%fused_computation.33 | convolution fusion | flops 912457344 | bytes 4145664 | tf_op jit(solution)/shard_map/dot_general | solution.py:13
  97.5 1.1 fusion.8
  98.6 12.0 %all_to_all.21 = bf16[4,96,768]{2,1,0:T(8,128)(2,1)S(1)} all-to-all(bf16[4,96,768]{2,1,0:T(8,128)(2,1)S(1)} %bitcast.31), channel_id=1, replica_groups=mesh['island'=2,'blk'=4,'sub'=2,'pair'=2] {'sub','pair'}, dimensions={0} | all-to-all | bytes 1179648 | tf_op jit(solution)/shard_map/all_to_all | solution.py:50
  110.7 3.9 %gather_fusion = bf16[192,768]{1,0:T(8,128)(2,1)} fusion(bf16[4,96,768]{2,1,0:T(8,128)(2,1)S(1)} %all_to_all.21, s32[192]{0:T(256)S(1)} %bitcast.28), kind=kCustom, calls=%fused_computation | custom fusion | bytes 591360 | tf_op jit(solution)/shard_map/gather | solution.py:51
  (11 shorter events, 0.2 us)
Async XLA Ops:
  6.5 87.1 %all-gather.3.cloned.1.call-start = ((), (), s32[]{:S(2)}) async-start(), calls=%async_computation.3 | async-start | bytes 2949120 | tf_op jit(solution)/shard_map/all_gather | solution.py:42
  10.3 31.9 %copy-start.2 = (s32[192]{0:T(256)S(1)}, s32[192]{0:T(256)}, u32[]{:S(2)}) copy-start(s32[192]{0:T(256)} %param.5) | copy-start | bytes 2308
  42.1 29.7 %copy-start = (bf16[4,96,768]{2,1,0:T(8,128)(2,1)S(1)}, bf16[4,96,768]{2,1,0:T(8,128)(2,1)}, u32[]{:S(2)}) copy-start(bf16[4,96,768]{2,1,0:T(8,128)(2,1)} %all_to_all.19) | copy-start | bytes 1769476
  93.6 2.4 %copy-start.1 = (bf16[1536,768]{1,0:T(8,128)(2,1)S(1)}, bf16[1536,768]{1,0:T(8,128)(2,1)}, u32[]{:S(2)}) copy-start(bf16[1536,768]{1,0:T(8,128)(2,1)} %all-gather.3.cloned.1.call-done) | copy-start | bytes 7077892
Sparse Core Ops, SparseCore 0:
  42.3 51.2 all-gather.2
where the time goes:
time: 122 us; the launch traced here: 121 us
  blocking collectives  44.6 us (37%)
  local copies, waits for them, and re-layouts  32.6 us (27%)
  waiting for transfers between devices  21.5 us (18%)
  between operations  13.5 us (11%)
  other arithmetic  6.66 us (5%)
  matrix products  2.65 us (2%)
    all_gather x1, waiting for transfers between devices, per_device(): piece_rows = lax.all_gather(own_rows, 'blk', axis=0, tiled=True)  21.5 us
    scatter x1, local copies, waits for them, and re-layouts, per_device(): jnp.zeros((groups, capacity, width), jnp.bfloat16).at[target, position]  18.1 us
    all_to_all x1, blocking collectives, per_device(): lax.all_to_all(send_rows, ('sub', 'pair'), split_axis=0, concat_axis=0, t...  13.7 us
    all_gather x1, blocking collectives, per_device(): piece_clust = lax.all_gather(own_clust, 'blk', axis=0, tiled=True)  12.8 us
    all_to_all x1, blocking collectives, per_device(): lax.all_to_all(result, ('sub', 'pair'), split_axis=0, concat_axis=0, tile...  12 us
    scatter x1, local copies, waits for them, and re-layouts, per_device(): jnp.full((groups, capacity), -1, jnp.int32).at[target, position]  9.38 us
    all_to_all x1, blocking collectives, per_device(): lax.all_to_all(send_clust, ('sub', 'pair'), split_axis=0, concat_axis=0,...  6.09 us
    gather x1, local copies, waits for them, and re-layouts, per_device(): return returned[target, position]  3.9 us
  transfers between devices with their start and end apart: 1, of which 1 were waited for; matrix products, arithmetic and copies ran while one was open for 9% of the time, Pallas kernels for 0%

commit v1 on v0

v1 whole, which is shorter than its diff:
```python
import functools

import jax
import jax.numpy as jnp
from jax import lax
from jax.experimental import pallas as pl
from jax.experimental.pallas import tpu as pltpu
from jax.sharding import PartitionSpec as P

F32 = jnp.float32
BF16 = jnp.bfloat16
VMEM_BYTES = 24 * 1024 * 1024
GATHER_LIMIT = 8 * 1024 * 1024


def unit_scale(rows_in):
    wide = rows_in.astype(F32)
    return lax.rsqrt(jnp.sum(wide * wide, axis=1) + 1e-06)


def tile_weights(left_rows, left_clust, left_scale, right_rows, right_clust, right_scale):
    grams = lax.dot_general(
        left_rows, right_rows, (((1,), (1,)), ((), ())), preferred_element_type=F32
    )
    cosine = grams * left_scale[:, None] * right_scale[None, :]
    same = (left_clust[:, None] == right_clust[None, :]).astype(F32)
    return jax.nn.sigmoid(8.0 * cosine - 2.0) * same


def by_group(embeddings, group_of, cluster_id):
    rows_here, width = embeddings.shape
    groups = lax.axis_size("sub") * lax.axis_size("pair")
    capacity = 2 * rows_here // groups
    slots = groups * capacity
    target = group_of[:, 0]
    onehot = (target[:, None] == jnp.arange(groups, dtype=jnp.int32)[None, :]).astype(jnp.int32)
    position = jnp.sum((jnp.cumsum(onehot, axis=0) - onehot) * onehot, axis=1)
    send_rows = jnp.zeros((groups, capacity, width), BF16).at[target, position].set(embeddings)
    send_clust = jnp.full((groups, capacity), -1, jnp.int32).at[target, position].set(cluster_id)
    recv_rows, recv_clust = (
        lax.all_to_all(send_rows, ("sub", "pair"), split_axis=0, concat_axis=0, tiled=True),
        lax.all_to_all(send_clust, ("sub", "pair"), split_axis=0, concat_axis=0, tiled=True),
    )
    own_rows = recv_rows.reshape(slots, width)
    own_clust = recv_clust.reshape(slots)
    own_scale = unit_scale(own_rows)
    piece_rows = lax.all_gather(own_rows, "blk", axis=0, tiled=True)
    piece_clust = lax.all_gather(own_clust, "blk", axis=0, tiled=True)
    weight = tile_weights(
        own_rows, own_clust, own_scale, piece_rows, piece_clust, unit_scale(piece_rows)
    )
    numer = jnp.dot(weight.astype(BF16), piece_rows, preferred_element_type=F32)
    denom = jnp.sum(weight, axis=1)
    result = (numer / denom[:, None]).astype(BF16).reshape(groups, capacity, width)
    returned = lax.all_to_all(result, ("sub", "pair"), split_axis=0, concat_axis=0, tiled=True)
    return returned[target, position]


def diagonal(size):
    shape = (size, size)
    return lax.broadcasted_iota(jnp.int32, shape, 0) == lax.broadcasted_iota(jnp.int32, shape, 1)


def to_column(row):
    size = row.shape[1]
    return jnp.sum(jnp.where(diagonal(size), row, jnp.zeros_like(row)), axis=1, keepdims=True)


def to_row(column):
    size = column.shape[0]
    return jnp.sum(jnp.where(diagonal(size), column, jnp.zeros_like(column)), axis=0, keepdims=True)


def scale_column(rows):
    wide = rows.astype(F32)
    return lax.rsqrt(jnp.sum(wide * wide, axis=1, keepdims=True) + 1e-06)


def step_kernel(n_blocks, first, *refs):
    refs = list(refs)
    left = [refs.pop(0), refs.pop(0)]
    left_key = [refs.pop(0), refs.pop(0)]
    right = [refs.pop(0) for _ in range(n_blocks)]
    right_key = [refs.pop(0) for _ in range(n_blocks)]
    before = None if first else [refs.pop(0), refs.pop(0)]
    out = refs
    width = left[0].shape[1]
    right_rows = [ref[...] for ref in right]
    right_scale = [to_row(scale_column(rows)) for rows in right_rows]
    for side in range(2):
        rows = left[side][...]
        key = to_column(left_key[side][...])
        scale = scale_column(rows) * 4.0
        numer = None if first else before[side][:, :width]
        denom = None if first else before[side][:, width:]
        for block in range(n_blocks):
            grams = lax.dot_general(
                rows, right_rows[block], (((1,), (1,)), ((), ())), preferred_element_type=F32
            )
            half = jnp.tanh(grams * scale * right_scale[block] - 1.0)
            weight = jnp.where(key == right_key[block][...], 0.5 + 0.5 * half, 0.0)
            add = jnp.dot(weight.astype(BF16), right_rows[block], preferred_element_type=F32)
            add_denom = jnp.sum(weight, axis=1, keepdims=True)
            numer = add if numer is None else numer + add
            denom = add_denom if denom is None else denom + add_denom
        out[side][:, :width] = numer
        out[side][:, width:] = jnp.broadcast_to(denom, (rows.shape[0], 128))


def mean_kernel(own, other, out):
    width = out.shape[1]
    denom = own[:, width : width + 1] + other[:, width : width + 1]
    out[...] = ((own[:, :width] + other[:, :width]) / denom).astype(BF16)


def whole_in_vmem(count):
    return [pl.BlockSpec(memory_space=pltpu.VMEM)] * count


def step(left, left_key, right, right_key, before):
    rows_here, width = left[0].shape
    args = list(left) + list(left_key) + list(right) + list(right_key)
    aliases = {}
    if before is not None:
        aliases = {len(args): 0, len(args) + 1: 1}
        args += list(before)
    shape = jax.ShapeDtypeStruct((rows_here, width + 128), F32)
    return pl.pallas_call(
        functools.partial(step_kernel, len(right), before is None),
        out_shape=[shape, shape],
        in_specs=whole_in_vmem(len(args)),
        out_specs=whole_in_vmem(2),
        input_output_aliases=aliases,
        compiler_params=pltpu.CompilerParams(vmem_limit_bytes=VMEM_BYTES),
    )(*args)


def folded_ring(size):
    return [0] + list(range(1, size, 2)) + list(range(2, size, 2))[::-1]


def by_block(embeddings, group_of, cluster_id):
    rows_here, width = embeddings.shape
    n_blk = lax.axis_size("blk")
    order = folded_ring(n_blk)
    swap = [(0, 1), (1, 0)]

    def along(rows, steps):
        return lax.ppermute(
            rows, "blk", [(order[i], order[(i + steps) % n_blk]) for i in range(n_blk)]
        )

    def across(rows):
        return lax.ppermute(rows, "sub", swap)

    def along_across(rows, steps):
        perm = []
        for i in range(n_blk):
            for j in range(2):
                perm.append((order[i] * 2 + j, order[(i + steps) % n_blk] * 2 + 1 - j))
        return lax.ppermute(rows, ("blk", "sub"), perm)

    def other_core(rows):
        return lax.ppermute(rows, "pair", swap)

    key = group_of.reshape(1, rows_here) * 65536 + cluster_id.reshape(1, rows_here)
    left = (embeddings, other_core(embeddings))
    left_key = (key, other_core(key))
    moved = embeddings
    total = None
    for steps in range(n_blk):
        if steps:
            moved = along(moved, 1)
        right = (moved, across(moved))
        if steps:
            right_key = (along(key, steps), along_across(key, steps))
        else:
            right_key = (key, across(key))
        total = step(left, left_key, right, right_key, total)
    own, others = total
    back = other_core(others)
    return pl.pallas_call(
        mean_kernel,
        out_shape=jax.ShapeDtypeStruct((rows_here, width), BF16),
        in_specs=whole_in_vmem(2),
        out_specs=pl.BlockSpec(memory_space=pltpu.VMEM),
        compiler_params=pltpu.CompilerParams(vmem_limit_bytes=VMEM_BYTES),
    )(own, back)


def per_device(embeddings, group_of, cluster_id):
    rows_here, width = embeddings.shape
    devices = lax.axis_size("blk") * lax.axis_size("sub") * lax.axis_size("pair")
    small = devices * rows_here * width * 2 <= GATHER_LIMIT
    if small and lax.axis_size("sub") == 2 and lax.axis_size("pair") == 2:
        return by_block(embeddings, group_of, cluster_id)
    return by_group(embeddings, group_of, cluster_id)


def solution(mesh):
    return jax.shard_map(
        per_device,
        mesh=mesh,
        in_specs=(
            P(("island", "blk", "sub", "pair"), None),
            P(("island", "blk", "sub", "pair"), None),
            P(("island", "blk", "sub", "pair")),
        ),
        out_specs=P(("island", "blk", "sub", "pair"), None),
        check_vma=False,
    )
```

time: 122 us -> 62.1 us (0.51)
  blocking collectives: 44.6 us -> 0 us
  local copies, waits for them, and re-layouts: 32.6 us -> 1.64 us
  starting transfers between devices: 0.01 us -> 20.4 us
  between operations: 13.5 us -> 0.09 us
  waiting for transfers between devices: 21.5 us -> 32.5 us
  Pallas kernels: 0 us -> 6.63 us
  other arithmetic: 6.66 us -> 0.68 us
  matrix products: 2.65 us -> 0 us
    ppermute x0 -> x17, waiting for transfers between devices: none -> 32.5 us  [the longest x6 16.4 us: along(): lax.ppermute(rows, 'blk', [(order[i], order[(i + steps) % n_blk]) for i i...]
    all_to_all x3 -> x0, blocking collectives: 31.8 us -> none  [the longest x1 13.7 us: per_device(): lax.all_to_all(send_rows, ('sub', 'pair'), split_axis=0, concat_axis=0, t...]
    scatter x2 -> x0, local copies, waits for them, and re-layouts: 27.5 us -> none  [the longest x1 18.1 us: per_device(): jnp.zeros((groups, capacity, width), jnp.bfloat16).at[target, position]]
    all_gather x1 -> x0, waiting for transfers between devices: 21.5 us -> none  [per_device(): piece_rows = lax.all_gather(own_rows, 'blk', axis=0, tiled=True)]
    ppermute x0 -> x17, starting transfers between devices: none -> 20.4 us  [the longest x6 11.3 us: along(): lax.ppermute(rows, 'blk', [(order[i], order[(i + steps) % n_blk]) for i i...]
    all_gather x1 -> x0, blocking collectives: 12.8 us -> none  [per_device(): piece_clust = lax.all_gather(own_clust, 'blk', axis=0, tiled=True)]
    pallas_call x0 -> x5, Pallas kernels: none -> 6.63 us  [the longest x4 5.79 us: step(): pl.pallas_call(functools.partial(step_kernel, len(right), before is None)...]
    gather x1 -> x0, local copies, waits for them, and re-layouts: 3.9 us -> none  [per_device(): return returned[target, position]]
  transfers between devices with their start and end apart: 1 -> 17, of which waited for: 1 -> 9; matrix products, arithmetic and copies ran while one was open for 9% -> 1% of each run, Pallas kernels for 0% -> 7%
where the time goes in v1:
time: 62.1 us; the launch traced here: 62 us
  waiting for transfers between devices  32.5 us (52%)
  starting transfers between devices  20.4 us (33%)
  Pallas kernels  6.63 us (11%)
  local copies, waits for them, and re-layouts  1.64 us (3%)
  other arithmetic  0.68 us (1%)
    ppermute x6, waiting for transfers between devices, along(): lax.ppermute(rows, 'blk', [(order[i], order[(i + steps) % n_blk]) for i i...  16.4 us
    ppermute x6, starting transfers between devices, along(): lax.ppermute(rows, 'blk', [(order[i], order[(i + steps) % n_blk]) for i i...  11.3 us
    ppermute x5, waiting for transfers between devices, across(): return lax.ppermute(rows, 'sub', swap)  11.2 us
    pallas_call x4, Pallas kernels, step(): pl.pallas_call(functools.partial(step_kernel, len(right), before is None)...  5.79 us
    ppermute x5, starting transfers between devices, across(): return lax.ppermute(rows, 'sub', swap)  4.59 us
    ppermute x3, starting transfers between devices, along_across(): return lax.ppermute(rows, ('blk', 'sub'), perm)  4.38 us
    ppermute x3, waiting for transfers between devices, along_across(): return lax.ppermute(rows, ('blk', 'sub'), perm)  2.84 us
    ppermute x3, waiting for transfers between devices, other_core(): return lax.ppermute(rows, 'pair', swap)  2.14 us
  transfers between devices with their start and end apart: 17, of which 9 were waited for; matrix products, arithmetic and copies ran while one was open for 1% of the time, Pallas kernels for 7%

profile of v1, /device:TPU:0, one launch (start us, length us, event | category | flops | bytes accessed | tf_op | source)
XLA Modules:
  0.0 62.0 jit_solution(18185950248386350384)
XLA Ops:
  0.0 3.0 %collective-permute-start.2 = (bf16[192,768]{1,0:T(8,128)(2,1)}, bf16[192,768]{1,0:T(8,128)(2,1)S(1)}, u32[]{:S(2)}, u32[]{:S(2)}) collective-permute-start(bf16[192,768]{1,0:T(8,128)(2,1)} %refs_0_.7), channel_id=1, source_target_pairs={{0,4},{4,12},{12,8},{8,0},{1,5},{5,13},{13,9},{9,1},{2,6},{6,14},{... | collective-permute-start | bytes 884744 | tf_op jit(solution)/shard_map/ppermute | solution.py:149
  3.0 8.2 %collective-permute-done.2.refs_4_ = bf16[192,768]{1,0:T(8,128)(2,1)S(1)} collective-permute-done((bf16[192,768]{1,0:T(8,128)(2,1)}, bf16[192,768]{1,0:T(8,128)(2,1)S(1)}, u32[]{:S(2)}, u32[]{:S(2)}) %collective-permute-start.2) | collective-permute-done | bytes 294944 | tf_op jit(solution)/shard_map/ppermute | solution.py:149
  11.3 0.9 %collective-permute-start.3 = (bf16[192,768]{1,0:T(8,128)(2,1)S(1)}, bf16[192,768]{1,0:T(8,128)(2,1)S(1)}, u32[]{:S(2)}, u32[]{:S(2)}) collective-permute-start(bf16[192,768]{1,0:T(8,128)(2,1)S(1)} %collective-permute-done.2.refs_4_), channel_id=1, source_target_pairs={{0,4},{4,12},{12,8},{8,0},{1,5},{5,13},{13,9},{9,1},{2,6},{6,14},{... | collective-permute-start | bytes 884744 | tf_op jit(solution)/shard_map/ppermute | solution.py:149
  12.2 8.1 %collective-permute-done.3.refs_4_ = bf16[192,768]{1,0:T(8,128)(2,1)S(1)} collective-permute-done((bf16[192,768]{1,0:T(8,128)(2,1)S(1)}, bf16[192,768]{1,0:T(8,128)(2,1)S(1)}, u32[]{:S(2)}, u32[]{:S(2)}) %collective-permute-start.3) | collective-permute-done | bytes 294944 | tf_op jit(solution)/shard_map/ppermute | solution.py:149
  20.3 0.5 collective-permute-start.4
  20.9 0.7 %broadcast_multiply_fusion = s32[192,1]{0,1:T(1,128)S(1)} fusion(s32[192,1]{0,1:T(1,128)} %param.4), kind=kLoop, calls=%fused_computation | loop fusion | flops 192 | bytes 1536 | tf_op jit(solution)/shard_map/mul | solution.py:166
  21.5 0.0 copy-start.1
  21.6 0.7 %copy-done.1 = s32[192]{0:T(256)S(1)} copy-done((s32[192]{0:T(256)S(1)}, s32[192]{0:T(256)}, u32[]{:S(2)}) %copy-start.1) | copy-done | bytes 792
  22.2 0.0 collective-permute-start.1
  22.2 1.5 %collective-permute-start.15 = (s32[1,192]{1,0:T(1,128)S(1)}, s32[1,192]{1,0:T(1,128)S(1)}, u32[]{:S(2)}, u32[]{:S(2)}) collective-permute-start(s32[1,192]{1,0:T(1,128)S(1)} %bitcast.3), channel_id=1, source_target_pairs={{0,2},{2,0},{1,3},{3,1},{4,6},{6,4},{5,7},{7,5},{8,10},{10,8},{9,1... | collective-permute-start | bytes 2312 | tf_op jit(solution)/shard_map/ppermute | solution.py:154
  23.7 3.4 %collective-permute-start.12 = (s32[1,192]{1,0:T(1,128)S(1)}, s32[1,192]{1,0:T(1,128)S(1)}, u32[]{:S(2)}, u32[]{:S(2)}) collective-permute-start(s32[1,192]{1,0:T(1,128)S(1)} %bitcast.4), channel_id=1, source_target_pairs={{0,4},{4,12},{12,8},{8,0},{1,5},{5,13},{13,9},{9,1},{2,6},{6,14},{... | collective-permute-start | bytes 2312 | tf_op jit(solution)/shard_map/ppermute | solution.py:149
  27.1 0.0 collective-permute-start.13
  27.1 0.0 collective-permute-done.1.refs_3_
  27.1 0.0 collective-permute-start
  27.1 0.0 collective-permute-done.15.refs_7_
  27.1 2.4 %collective-permute-start.10 = (s32[1,192]{1,0:T(1,128)S(1)}, s32[1,192]{1,0:T(1,128)S(1)}, u32[]{:S(2)}, u32[]{:S(2)}) collective-permute-start(s32[1,192]{1,0:T(1,128)S(1)} %bitcast.6), channel_id=1, source_target_pairs={{0,14},{2,12},{4,10},{6,8},{12,2},{14,0},{8,6},{10,4},{1,15},{3,13... | collective-permute-start | bytes 2312 | tf_op jit(solution)/shard_map/ppermute | solution.py:161
  29.6 0.0 collective-permute-done.12.refs_6_
  29.6 0.5 collective-permute-start.14
  30.1 2.4 %collective-permute-done.13.refs_7_ = s32[1,192]{1,0:T(1,128)S(1)} collective-permute-done((s32[1,192]{1,0:T(1,128)S(1)}, s32[1,192]{1,0:T(1,128)S(1)}, u32[]{:S(2)}, u32[]{:S(2)}) %collective-permute-start.13) | collective-permute-done | bytes 800 | tf_op jit(solution)/shard_map/ppermute | solution.py:161
  32.5 0.5 collective-permute-start.11
  33.0 0.5 collective-permute-done.10.refs_7_
  33.5 1.5 %collective-permute-start.8 = (bf16[192,768]{1,0:T(8,128)(2,1)S(1)}, bf16[192,768]{1,0:T(8,128)(2,1)S(1)}, u32[]{:S(2)}, u32[]{:S(2)}) collective-permute-start(bf16[192,768]{1,0:T(8,128)(2,1)S(1)} %collective-permute-done.3.refs_4_), channel_id=1, source_target_pairs={{0,2},{2,0},{1,3},{3,1},{4,6},{6,4},{5,7},{7,5},{8,10},{10,8},{9,1... | collective-permute-start | bytes 884744 | tf_op jit(solution)/shard_map/ppermute | solution.py:154
  34.9 0.0 collective-permute-done.4.refs_4_
  34.9 0.6 collective-permute-start.5
  35.5 0.0 collective-permute-done.refs_1_
  35.5 1.4 %collective-permute-start.9 = (s32[1,192]{1,0:T(1,128)S(1)}, s32[1,192]{1,0:T(1,128)S(1)}, u32[]{:S(2)}, u32[]{:S(2)}) collective-permute-start(s32[1,192]{1,0:T(1,128)S(1)} %bitcast.7), channel_id=1, source_target_pairs={{0,12},{4,8},{12,0},{8,4},{1,13},{5,9},{13,1},{9,5},{2,14},{6,10},... | collective-permute-start | bytes 2312 | tf_op jit(solution)/shard_map/ppermute | solution.py:149
  36.9 2.8 %collective-permute-done.14.refs_5_ = bf16[192,768]{1,0:T(8,128)(2,1)S(1)} collective-permute-done((bf16[192,768]{1,0:T(8,128)(2,1)}, bf16[192,768]{1,0:T(8,128)(2,1)S(1)}, u32[]{:S(2)}, u32[]{:S(2)}) %collective-permute-start.14) | collective-permute-done | bytes 294944 | tf_op jit(solution)/shard_map/ppermute | solution.py:154
  39.7 2.0 %collective-permute-start.6 = (s32[1,192]{1,0:T(1,128)S(1)}, s32[1,192]{1,0:T(1,128)S(1)}, u32[]{:S(2)}, u32[]{:S(2)}) collective-permute-start(s32[1,192]{1,0:T(1,128)S(1)} %bitcast.8), channel_id=1, source_target_pairs={{0,8},{4,0},{12,4},{8,12},{1,9},{5,1},{13,5},{9,13},{2,10},{6,2},{... | collective-permute-start | bytes 2312 | tf_op jit(solution)/shard_map/ppermute | solution.py:149
  41.7 4.3 %collective-permute-done.11.refs_5_ = bf16[192,768]{1,0:T(8,128)(2,1)S(1)} collective-permute-done((bf16[192,768]{1,0:T(8,128)(2,1)S(1)}, bf16[192,768]{1,0:T(8,128)(2,1)S(1)}, u32[]{:S(2)}, u32[]{:S(2)}) %collective-permute-start.11) | collective-permute-done | bytes 294944 | tf_op jit(solution)/shard_map/ppermute | solution.py:154
  46.0 2.0 %collective-permute-start.7 = (s32[1,192]{1,0:T(1,128)S(1)}, s32[1,192]{1,0:T(1,128)S(1)}, u32[]{:S(2)}, u32[]{:S(2)}) collective-permute-start(s32[1,192]{1,0:T(1,128)S(1)} %bitcast.9), channel_id=1, source_target_pairs={{0,10},{2,8},{4,2},{6,0},{12,6},{14,4},{8,14},{10,12},{1,11},{3,9}... | collective-permute-start | bytes 2312 | tf_op jit(solution)/shard_map/ppermute | solution.py:161
  48.0 0.0 copy-start
  48.0 1.0 %copy-done = bf16[192,768]{1,0:T(8,128)(2,1)S(1)} copy-done((bf16[192,768]{1,0:T(8,128)(2,1)S(1)}, bf16[192,768]{1,0:T(8,128)(2,1)}, u32[]{:S(2)}) %copy-start) | copy-done | bytes 294936
  48.9 1.3 %shard_map.37 = (f32[192,896]{1,0:T(8,128)S(1)}, f32[192,896]{1,0:T(8,128)S(1)}) custom-call(bf16[192,768]{1,0:T(8,128)(2,1)S(1)} %copy-done, bf16[192,768]{1,0:T(8,128)(2,1)S(1)} %collective-permute-done.refs_1_, s32[1,192]{1,0:T(1,128)S(1)} %bitcast.10, s32[1,192]{1,0:T(1,128)S(1)} %collective-permute-done.1.refs_3_, bf16[192,768]{1,0:T(8,128)(2,1)S(1)} %copy-done, ...), custom_call_target="tpu_custom_call" | custom-call | tf_op jit(solution)/shard_map/pallas_call | solution.py:128
  50.2 1.5 %shard_map.38 = (f32[192,896]{1,0:T(8,128)S(1)}, f32[192,896]{1,0:T(8,128)S(1)}) custom-call(bf16[192,768]{1,0:T(8,128)(2,1)S(1)} %copy-done, bf16[192,768]{1,0:T(8,128)(2,1)S(1)} %collective-permute-done.refs_1_, s32[1,192]{1,0:T(1,128)S(1)} %bitcast.12, s32[1,192]{1,0:T(1,128)S(1)} %collective-permute-done.1.refs_3_, ...), custom_call_target="tpu_custom_call", output_to_operand_aliasing={{0}: (8, {}), {1}: (9, {})} | custom-call | tf_op jit(solution)/shard_map/pallas_call | solution.py:128
  51.7 0.0 collective-permute-done.9.refs_6_
  51.7 0.6 collective-permute-done.8.refs_5_
  52.4 1.5 %shard_map.39 = (f32[192,896]{1,0:T(8,128)S(1)}, f32[192,896]{1,0:T(8,128)S(1)}) custom-call(bf16[192,768]{1,0:T(8,128)(2,1)S(1)} %copy-done, bf16[192,768]{1,0:T(8,128)(2,1)S(1)} %collective-permute-done.refs_1_, s32[1,192]{1,0:T(1,128)S(1)} %bitcast.13, s32[1,192]{1,0:T(1,128)S(1)} %collective-permute-done.1.refs_3_, ...), custom_call_target="tpu_custom_call", output_to_operand_aliasing={{0}: (8, {}), {1}: (9, {})} | custom-call | tf_op jit(solution)/shard_map/pallas_call | solution.py:128
  53.9 0.0 collective-permute-done.6.refs_6_
  53.9 0.0 collective-permute-done.7.refs_7_
  53.9 3.5 %collective-permute-done.5.refs_5_ = bf16[192,768]{1,0:T(8,128)(2,1)S(1)} collective-permute-done((bf16[192,768]{1,0:T(8,128)(2,1)S(1)}, bf16[192,768]{1,0:T(8,128)(2,1)S(1)}, u32[]{:S(2)}, u32[]{:S(2)}) %collective-permute-start.5) | collective-permute-done | bytes 294944 | tf_op jit(solution)/shard_map/ppermute | solution.py:154
  57.4 1.5 %shard_map.40 = (f32[192,896]{1,0:T(8,128)S(1)}, f32[192,896]{1,0:T(8,128)S(1)}) custom-call(bf16[192,768]{1,0:T(8,128)(2,1)S(1)} %copy-done, bf16[192,768]{1,0:T(8,128)(2,1)S(1)} %collective-permute-done.refs_1_, s32[1,192]{1,0:T(1,128)S(1)} %bitcast.14, s32[1,192]{1,0:T(1,128)S(1)} %collective-permute-done.1.refs_3_, ...), custom_call_target="tpu_custom_call", output_to_operand_aliasing={{0}: (8, {}), {1}: (9, {})} | custom-call | tf_op jit(solution)/shard_map/pallas_call | solution.py:128
  58.9 0.1 collective-permute-start.16
  59.0 2.1 %collective-permute-done.16.other = f32[192,896]{1,0:T(8,128)S(1)} collective-permute-done((f32[192,896]{1,0:T(8,128)S(1)}, f32[192,896]{1,0:T(8,128)S(1)}, u32[]{:S(2)}, u32[]{:S(2)}) %collective-permute-start.16) | collective-permute-done | bytes 688160 | tf_op jit(solution)/shard_map/ppermute | solution.py:164
  61.1 0.8 %shard_map.41 = bf16[192,768]{1,0:T(8,128)(2,1)} custom-call(f32[192,896]{1,0:T(8,128)S(1)} %get-tuple-element.19.own, f32[192,896]{1,0:T(8,128)S(1)} %collective-permute-done.16.other), custom_call_target="tpu_custom_call" | custom-call | tf_op jit(solution)/shard_map/pallas_call | solution.py:182
  (1 shorter events, 0.0 us)
Async XLA Ops:
  0.0 11.3 %collective-permute-start.2 = (bf16[192,768]{1,0:T(8,128)(2,1)}, bf16[192,768]{1,0:T(8,128)(2,1)S(1)}, u32[]{:S(2)}, u32[]{:S(2)}) collective-permute-start(bf16[192,768]{1,0:T(8,128)(2,1)} %refs_0_.7), channel_id=1, source_target_pairs={{0,4},{4,12},{12,8},{8,0},{1,5},{5,13},{13,9},{9,1},{2,6},{6,14},{... | collective-permute-start | bytes 884744 | tf_op jit(solution)/shard_map/ppermute | solution.py:149
  11.3 9.1 %collective-permute-start.3 = (bf16[192,768]{1,0:T(8,128)(2,1)S(1)}, bf16[192,768]{1,0:T(8,128)(2,1)S(1)}, u32[]{:S(2)}, u32[]{:S(2)}) collective-permute-start(bf16[192,768]{1,0:T(8,128)(2,1)S(1)} %collective-permute-done.2.refs_4_), channel_id=1, source_target_pairs={{0,4},{4,12},{12,8},{8,0},{1,5},{5,13},{13,9},{9,1},{2,6},{6,14},{... | collective-permute-start | bytes 884744 | tf_op jit(solution)/shard_map/ppermute | solution.py:149
  20.3 14.6 %collective-permute-start.4 = (bf16[192,768]{1,0:T(8,128)(2,1)S(1)}, bf16[192,768]{1,0:T(8,128)(2,1)S(1)}, u32[]{:S(2)}, u32[]{:S(2)}) collective-permute-start(bf16[192,768]{1,0:T(8,128)(2,1)S(1)} %collective-permute-done.3.refs_4_), channel_id=1, source_target_pairs={{0,4},{4,12},{12,8},{8,0},{1,5},{5,13},{13,9},{9,1},{2,6},{6,14},{... | collective-permute-start | bytes 884744 | tf_op jit(solution)/shard_map/ppermute | solution.py:149
  21.5 0.7 %copy-start.1 = (s32[192]{0:T(256)S(1)}, s32[192]{0:T(256)}, u32[]{:S(2)}) copy-start(s32[192]{0:T(256)} %param.5) | copy-start | bytes 2308
  22.2 4.9 %collective-permute-start.1 = (s32[1,192]{1,0:T(1,128)S(1)}, s32[1,192]{1,0:T(1,128)S(1)}, u32[]{:S(2)}, u32[]{:S(2)}) collective-permute-start(s32[1,192]{1,0:T(1,128)S(1)} %bitcast.2), channel_id=1, source_target_pairs={{0,1},{1,0},{2,3},{3,2},{4,5},{5,4},{6,7},{7,6},{8,9},{9,8},{10,11... | collective-permute-start | bytes 2312 | tf_op jit(solution)/shard_map/ppermute | solution.py:164
  22.2 4.9 %collective-permute-start.15 = (s32[1,192]{1,0:T(1,128)S(1)}, s32[1,192]{1,0:T(1,128)S(1)}, u32[]{:S(2)}, u32[]{:S(2)}) collective-permute-start(s32[1,192]{1,0:T(1,128)S(1)} %bitcast.3), channel_id=1, source_target_pairs={{0,2},{2,0},{1,3},{3,1},{4,6},{6,4},{5,7},{7,5},{8,10},{10,8},{9,1... | collective-permute-start | bytes 2312 | tf_op jit(solution)/shard_map/ppermute | solution.py:154
  23.7 5.8 %collective-permute-start.12 = (s32[1,192]{1,0:T(1,128)S(1)}, s32[1,192]{1,0:T(1,128)S(1)}, u32[]{:S(2)}, u32[]{:S(2)}) collective-permute-start(s32[1,192]{1,0:T(1,128)S(1)} %bitcast.4), channel_id=1, source_target_pairs={{0,4},{4,12},{12,8},{8,0},{1,5},{5,13},{13,9},{9,1},{2,6},{6,14},{... | collective-permute-start | bytes 2312 | tf_op jit(solution)/shard_map/ppermute | solution.py:149
  27.1 5.4 %collective-permute-start.13 = (s32[1,192]{1,0:T(1,128)S(1)}, s32[1,192]{1,0:T(1,128)S(1)}, u32[]{:S(2)}, u32[]{:S(2)}) collective-permute-start(s32[1,192]{1,0:T(1,128)S(1)} %bitcast.5), channel_id=1, source_target_pairs={{0,6},{2,4},{4,14},{6,12},{12,10},{14,8},{8,2},{10,0},{1,7},{3,5},... | collective-permute-start | bytes 2312 | tf_op jit(solution)/shard_map/ppermute | solution.py:161
  27.1 8.4 %collective-permute-start = (bf16[192,768]{1,0:T(8,128)(2,1)}, bf16[192,768]{1,0:T(8,128)(2,1)S(1)}, u32[]{:S(2)}, u32[]{:S(2)}) collective-permute-start(bf16[192,768]{1,0:T(8,128)(2,1)} %refs_0_.7), channel_id=1, source_target_pairs={{0,1},{1,0},{2,3},{3,2},{4,5},{5,4},{6,7},{7,6},{8,9},{9,8},{10,11... | collective-permute-start | bytes 884744 | tf_op jit(solution)/shard_map/ppermute | solution.py:164
  27.1 6.3 %collective-permute-start.10 = (s32[1,192]{1,0:T(1,128)S(1)}, s32[1,192]{1,0:T(1,128)S(1)}, u32[]{:S(2)}, u32[]{:S(2)}) collective-permute-start(s32[1,192]{1,0:T(1,128)S(1)} %bitcast.6), channel_id=1, source_target_pairs={{0,14},{2,12},{4,10},{6,8},{12,2},{14,0},{8,6},{10,4},{1,15},{3,13... | collective-permute-start | bytes 2312 | tf_op jit(solution)/shard_map/ppermute | solution.py:161
  29.6 10.1 %collective-permute-start.14 = (bf16[192,768]{1,0:T(8,128)(2,1)}, bf16[192,768]{1,0:T(8,128)(2,1)S(1)}, u32[]{:S(2)}, u32[]{:S(2)}) collective-permute-start(bf16[192,768]{1,0:T(8,128)(2,1)} %refs_0_.7), channel_id=1, source_target_pairs={{0,2},{2,0},{1,3},{3,1},{4,6},{6,4},{5,7},{7,5},{8,10},{10,8},{9,1... | collective-permute-start | bytes 884744 | tf_op jit(solution)/shard_map/ppermute | solution.py:154
  32.5 13.5 %collective-permute-start.11 = (bf16[192,768]{1,0:T(8,128)(2,1)S(1)}, bf16[192,768]{1,0:T(8,128)(2,1)S(1)}, u32[]{:S(2)}, u32[]{:S(2)}) collective-permute-start(bf16[192,768]{1,0:T(8,128)(2,1)S(1)} %collective-permute-done.2.refs_4_), channel_id=1, source_target_pairs={{0,2},{2,0},{1,3},{3,1},{4,6},{6,4},{5,7},{7,5},{8,10},{10,8},{9,1... | collective-permute-start | bytes 884744 | tf_op jit(solution)/shard_map/ppermute | solution.py:154
  33.5 18.9 %collective-permute-start.8 = (bf16[192,768]{1,0:T(8,128)(2,1)S(1)}, bf16[192,768]{1,0:T(8,128)(2,1)S(1)}, u32[]{:S(2)}, u32[]{:S(2)}) collective-permute-start(bf16[192,768]{1,0:T(8,128)(2,1)S(1)} %collective-permute-done.3.refs_4_), channel_id=1, source_target_pairs={{0,2},{2,0},{1,3},{3,1},{4,6},{6,4},{5,7},{7,5},{8,10},{10,8},{9,1... | collective-permute-start | bytes 884744 | tf_op jit(solution)/shard_map/ppermute | solution.py:154
  34.9 22.5 %collective-permute-start.5 = (bf16[192,768]{1,0:T(8,128)(2,1)S(1)}, bf16[192,768]{1,0:T(8,128)(2,1)S(1)}, u32[]{:S(2)}, u32[]{:S(2)}) collective-permute-start(bf16[192,768]{1,0:T(8,128)(2,1)S(1)} %collective-permute-done.4.refs_4_), channel_id=1, source_target_pairs={{0,2},{2,0},{1,3},{3,1},{4,6},{6,4},{5,7},{7,5},{8,10},{10,8},{9,1... | collective-permute-start | bytes 884744 | tf_op jit(solution)/shard_map/ppermute | solution.py:154
  35.5 16.2 %collective-permute-start.9 = (s32[1,192]{1,0:T(1,128)S(1)}, s32[1,192]{1,0:T(1,128)S(1)}, u32[]{:S(2)}, u32[]{:S(2)}) collective-permute-start(s32[1,192]{1,0:T(1,128)S(1)} %bitcast.7), channel_id=1, source_target_pairs={{0,12},{4,8},{12,0},{8,4},{1,13},{5,9},{13,1},{9,5},{2,14},{6,10},... | collective-permute-start | bytes 2312 | tf_op jit(solution)/shard_map/ppermute | solution.py:149
  39.7 14.2 %collective-permute-start.6 = (s32[1,192]{1,0:T(1,128)S(1)}, s32[1,192]{1,0:T(1,128)S(1)}, u32[]{:S(2)}, u32[]{:S(2)}) collective-permute-start(s32[1,192]{1,0:T(1,128)S(1)} %bitcast.8), channel_id=1, source_target_pairs={{0,8},{4,0},{12,4},{8,12},{1,9},{5,1},{13,5},{9,13},{2,10},{6,2},{... | collective-permute-start | bytes 2312 | tf_op jit(solution)/shard_map/ppermute | solution.py:149
  46.0 7.9 %collective-permute-start.7 = (s32[1,192]{1,0:T(1,128)S(1)}, s32[1,192]{1,0:T(1,128)S(1)}, u32[]{:S(2)}, u32[]{:S(2)}) collective-permute-start(s32[1,192]{1,0:T(1,128)S(1)} %bitcast.9), channel_id=1, source_target_pairs={{0,10},{2,8},{4,2},{6,0},{12,6},{14,4},{8,14},{10,12},{1,11},{3,9}... | collective-permute-start | bytes 2312 | tf_op jit(solution)/shard_map/ppermute | solution.py:161
  48.0 1.0 %copy-start = (bf16[192,768]{1,0:T(8,128)(2,1)S(1)}, bf16[192,768]{1,0:T(8,128)(2,1)}, u32[]{:S(2)}) copy-start(bf16[192,768]{1,0:T(8,128)(2,1)} %refs_0_.7) | copy-start | bytes 884740
  58.9 2.2 %collective-permute-start.16 = (f32[192,896]{1,0:T(8,128)S(1)}, f32[192,896]{1,0:T(8,128)S(1)}, u32[]{:S(2)}, u32[]{:S(2)}) collective-permute-start(f32[192,896]{1,0:T(8,128)S(1)} %get-tuple-element.20), channel_id=1, source_target_pairs={{0,1},{1,0},{2,3},{3,2},{4,5},{5,4},{6,7},{7,6},{8,9},{9,8},{10,11... | collective-permute-start | bytes 2064392 | tf_op jit(solution)/shard_map/ppermute | solution.py:164

commit v2 on v0

v2 whole, which is shorter than its diff:
```python
import functools

import jax
import jax.numpy as jnp
from jax import lax
from jax.experimental import pallas as pl
from jax.experimental.pallas import tpu as pltpu
from jax.sharding import PartitionSpec as P

F32 = jnp.float32
BF16 = jnp.bfloat16
VMEM_BYTES = 24 * 1024 * 1024
GATHER_LIMIT = 8 * 1024 * 1024


def unit_scale(rows_in):
    wide = rows_in.astype(F32)
    return lax.rsqrt(jnp.sum(wide * wide, axis=1) + 1e-06)


def tile_weights(left_rows, left_clust, left_scale, right_rows, right_clust, right_scale):
    grams = lax.dot_general(
        left_rows, right_rows, (((1,), (1,)), ((), ())), preferred_element_type=F32
    )
    cosine = grams * left_scale[:, None] * right_scale[None, :]
    same = (left_clust[:, None] == right_clust[None, :]).astype(F32)
    return jax.nn.sigmoid(8.0 * cosine - 2.0) * same


def by_group(embeddings, group_of, cluster_id):
    rows_here, width = embeddings.shape
    groups = lax.axis_size("sub") * lax.axis_size("pair")
    capacity = 2 * rows_here // groups
    slots = groups * capacity
    target = group_of[:, 0]
    onehot = (target[:, None] == jnp.arange(groups, dtype=jnp.int32)[None, :]).astype(jnp.int32)
    position = jnp.sum((jnp.cumsum(onehot, axis=0) - onehot) * onehot, axis=1)
    send_rows = jnp.zeros((groups, capacity, width), BF16).at[target, position].set(embeddings)
    send_clust = jnp.full((groups, capacity), -1, jnp.int32).at[target, position].set(cluster_id)
    recv_rows, recv_clust = (
        lax.all_to_all(send_rows, ("sub", "pair"), split_axis=0, concat_axis=0, tiled=True),
        lax.all_to_all(send_clust, ("sub", "pair"), split_axis=0, concat_axis=0, tiled=True),
    )
    own_rows = recv_rows.reshape(slots, width)
    own_clust = recv_clust.reshape(slots)
    own_scale = unit_scale(own_rows)
    piece_rows = lax.all_gather(own_rows, "blk", axis=0, tiled=True)
    piece_clust = lax.all_gather(own_clust, "blk", axis=0, tiled=True)
    weight = tile_weights(
        own_rows, own_clust, own_scale, piece_rows, piece_clust, unit_scale(piece_rows)
    )
    numer = jnp.dot(weight.astype(BF16), piece_rows, preferred_element_type=F32)
    denom = jnp.sum(weight, axis=1)
    result = (numer / denom[:, None]).astype(BF16).reshape(groups, capacity, width)
    returned = lax.all_to_all(result, ("sub", "pair"), split_axis=0, concat_axis=0, tiled=True)
    return returned[target, position]


def diagonal(size):
    shape = (size, size)
    return lax.broadcasted_iota(jnp.int32, shape, 0) == lax.broadcasted_iota(jnp.int32, shape, 1)


def to_column(row):
    size = row.shape[1]
    return jnp.sum(jnp.where(diagonal(size), row, jnp.zeros_like(row)), axis=1, keepdims=True)


def to_row(column):
    size = column.shape[0]
    return jnp.sum(jnp.where(diagonal(size), column, jnp.zeros_like(column)), axis=0, keepdims=True)


def scale_column(rows):
    wide = rows.astype(F32)
    return lax.rsqrt(jnp.sum(wide * wide, axis=1, keepdims=True) + 1e-06)


def pack_kernel(rows, group, cluster, whole, first, second):
    rows_here, width = rows.shape
    half = rows_here // 2
    line = lax.broadcasted_iota(jnp.int32, (8, rows_here), 0)
    named = jnp.where(line == 0, group[...], jnp.where(line == 1, cluster[...], 0))
    named = named.astype(F32).astype(BF16)
    whole[:rows_here, :] = rows[...]
    whole[rows_here:, :] = jnp.zeros((8, width), BF16)
    whole[rows_here:, :rows_here] = named
    first[:half, :] = rows[:half, :]
    first[half:, :] = jnp.zeros((8, width), BF16)
    first[half:, :rows_here] = named
    second[...] = rows[half:, :]


def key_row(named):
    wide = named.astype(F32)
    return wide[0:1, :] * 256.0 + wide[1:2, :]


def from_whole(ref):
    rows_here = ref.shape[0] - 8
    return ref[:rows_here, :], key_row(ref[rows_here:, :rows_here])


def from_halves(first, second):
    half = second.shape[0]
    rows = jnp.concatenate([first[:half, :], second[...]], axis=0)
    return rows, key_row(first[half:, : 2 * half])


def add_blocks(left, blocks, numer, denom):
    rows, key = left
    key = to_column(key)
    scale = scale_column(rows) * 4.0
    for right_rows, right_key, right_scale in blocks:
        grams = lax.dot_general(
            rows, right_rows, (((1,), (1,)), ((), ())), preferred_element_type=F32
        )
        half = jnp.tanh(grams * scale * right_scale - 1.0)
        weight = jnp.where(key == right_key, 0.5 + 0.5 * half, 0.0)
        add = jnp.dot(weight.astype(BF16), right_rows, preferred_element_type=F32)
        add_denom = jnp.sum(weight, axis=1, keepdims=True)
        numer = add if numer is None else numer + add
        denom = add_denom if denom is None else denom + add_denom
    return numer, denom


def with_scale(block):
    rows, key = block
    return rows, key, to_row(scale_column(rows))


def step_kernel(n_blocks, first, *refs):
    refs = list(refs)
    left = [from_whole(refs.pop(0)), from_whole(refs.pop(0))]
    blocks = [with_scale(left[0])] if first else []
    for _ in range(n_blocks):
        blocks.append(with_scale(from_halves(refs.pop(0), refs.pop(0))))
    before = None if first else [refs.pop(0), refs.pop(0)]
    width = left[0][0].shape[1]
    for side in range(2):
        numer = None if first else before[side][:, :width]
        denom = None if first else before[side][:, width : width + 1]
        numer, denom = add_blocks(left[side], blocks, numer, denom)
        refs[side][:, :width] = numer
        refs[side][:, width:] = jnp.broadcast_to(denom, (numer.shape[0], 128))


def last_kernel(own, first, second, first_other, second_other, mine, theirs, out):
    width = out.shape[1]
    blocks = [
        with_scale(from_halves(first, second)),
        with_scale(from_halves(first_other, second_other)),
    ]
    numer = mine[:, :width] + theirs[:, :width]
    denom = mine[:, width : width + 1] + theirs[:, width : width + 1]
    numer, denom = add_blocks(from_whole(own), blocks, numer, denom)
    out[...] = (numer / denom).astype(BF16)


def whole_in_vmem(count):
    return [pl.BlockSpec(memory_space=pltpu.VMEM)] * count


def call(kernel, shapes, args, aliases={}):
    return pl.pallas_call(
        kernel,
        out_shape=shapes,
        in_specs=whole_in_vmem(len(args)),
        out_specs=whole_in_vmem(len(shapes)),
        input_output_aliases=aliases,
        compiler_params=pltpu.CompilerParams(vmem_limit_bytes=VMEM_BYTES),
    )(*args)


def step(left, right, before):
    rows_here, width = left[0].shape
    args = list(left) + [half for block in right for half in block]
    aliases = {}
    if before is not None:
        aliases = {len(args): 0, len(args) + 1: 1}
        args += list(before)
    shape = jax.ShapeDtypeStruct((rows_here - 8, width + 128), F32)
    return call(
        functools.partial(step_kernel, len(right), before is None), [shape, shape], args, aliases
    )


def folded_ring(size):
    return [0] + list(range(1, size, 2)) + list(range(2, size, 2))[::-1]


def together(*arrays):
    return lax.optimization_barrier(arrays)


def by_block(embeddings, group_of, cluster_id):
    rows_here, width = embeddings.shape
    half = rows_here // 2
    n_blk = lax.axis_size("blk")
    order = folded_ring(n_blk)
    swap = [(0, 1), (1, 0)]

    def along(rows):
        return lax.ppermute(rows, "blk", [(order[i - 1], order[i]) for i in range(n_blk)])

    def across(rows):
        return lax.ppermute(rows, "sub", swap)

    def other_core(rows):
        return lax.ppermute(rows, "pair", swap)

    whole, first, second = call(
        pack_kernel,
        [
            jax.ShapeDtypeStruct((rows_here + 8, width), BF16),
            jax.ShapeDtypeStruct((half + 8, width), BF16),
            jax.ShapeDtypeStruct((half, width), BF16),
        ],
        [embeddings, group_of.reshape(1, rows_here), cluster_id.reshape(1, rows_here)],
    )
    along_by = [(first, second)]
    across_by = []
    for s in range(1, n_blk):
        moved = [along(piece) for piece in along_by[-1]]
        swapped = [across(piece) for piece in along_by[-1]]
        pairs = [together(m, w) for m, w in zip(moved, swapped)]
        along_by.append(tuple(pair[0] for pair in pairs))
        across_by.append(tuple(pair[1] for pair in pairs))
    left = (whole, other_core(whole))
    early = n_blk // 2
    total = step(left, across_by[:early] + along_by[1:early], None)
    far, total = together(along_by[-1][0], total)
    last_first = across(far)
    last_second = along(across_by[-1][1])
    mine, theirs = step(left, across_by[early:] + along_by[early:], total)
    last_first, last_second, theirs = together(last_first, last_second, other_core(theirs))
    (out,) = call(
        last_kernel,
        [jax.ShapeDtypeStruct((rows_here, width), BF16)],
        [
            whole,
            last_first,
            last_second,
            other_core(last_first),
            other_core(last_second),
            mine,
            theirs,
        ],
    )
    return out


def per_device(embeddings, group_of, cluster_id):
    rows_here, width = embeddings.shape
    devices = lax.axis_size("blk") * lax.axis_size("sub") * lax.axis_size("pair")
    small = devices * rows_here * width * 2 <= GATHER_LIMIT
    if small and lax.axis_size("sub") == 2 and lax.axis_size("pair") == 2:
        return by_block(embeddings, group_of, cluster_id)
    return by_group(embeddings, group_of, cluster_id)


def solution(mesh):
    return jax.shard_map(
        per_device,
        mesh=mesh,
        in_specs=(
            P(("island", "blk", "sub", "pair"), None),
            P(("island", "blk", "sub", "pair"), None),
            P(("island", "blk", "sub", "pair")),
        ),
        out_specs=P(("island", "blk", "sub", "pair"), None),
        check_vma=False,
    )
```

time: 122 us -> 44.3 us (0.36)
  blocking collectives: 44.6 us -> 0 us
  local copies, waits for them, and re-layouts: 32.6 us -> 1.65 us
  starting transfers between devices: 0.01 us -> 24.5 us
  between operations: 13.5 us -> 0.06 us
  waiting for transfers between devices: 21.5 us -> 12 us
  other arithmetic: 6.66 us -> 0 us
  Pallas kernels: 0 us -> 5.96 us
  matrix products: 2.65 us -> 0 us
    all_to_all x3 -> x0, blocking collectives: 31.8 us -> none  [the longest x1 13.7 us: per_device(): lax.all_to_all(send_rows, ('sub', 'pair'), split_axis=0, concat_axis=0, t...]
    scatter x2 -> x0, local copies, waits for them, and re-layouts: 27.5 us -> none  [the longest x1 18.1 us: per_device(): jnp.zeros((groups, capacity, width), jnp.bfloat16).at[target, position]]
    ppermute x0 -> x18, starting transfers between devices: none -> 24.5 us  [the longest x7 13.5 us: along(): lax.ppermute(rows, 'blk', [(order[i - 1], order[i]) for i in range(n_blk)])]
    all_gather x1 -> x0, waiting for transfers between devices: 21.5 us -> none  [per_device(): piece_rows = lax.all_gather(own_rows, 'blk', axis=0, tiled=True)]
    all_gather x1 -> x0, blocking collectives: 12.8 us -> none  [per_device(): piece_clust = lax.all_gather(own_clust, 'blk', axis=0, tiled=True)]
    ppermute x0 -> x18, waiting for transfers between devices: none -> 12 us  [the longest x7 8.8 us: along(): lax.ppermute(rows, 'blk', [(order[i - 1], order[i]) for i in range(n_blk)])]
    pallas_call x0 -> x4, Pallas kernels: none -> 5.96 us  [call(): pl.pallas_call(kernel, out_shape=shapes, in_specs=whole_in_vmem(len(args)...]
    gather x1 -> x0, local copies, waits for them, and re-layouts: 3.9 us -> none  [per_device(): return returned[target, position]]
  transfers between devices with their start and end apart: 1 -> 18, of which waited for: 1 -> 6; matrix products, arithmetic and copies ran while one was open for 9% -> 0% of each run, Pallas kernels for 0% -> 6%
where the time goes in v2:
time: 44.3 us; the launch traced here: 44.2 us
  starting transfers between devices  24.5 us (55%)
  waiting for transfers between devices  12 us (27%)
  Pallas kernels  5.96 us (13%)
  local copies, waits for them, and re-layouts  1.65 us (4%)
    ppermute x7, starting transfers between devices, along(): lax.ppermute(rows, 'blk', [(order[i - 1], order[i]) for i in range(n_blk)])  13.5 us
    ppermute x7, starting transfers between devices, across(): return lax.ppermute(rows, 'sub', swap)  10.4 us
    ppermute x7, waiting for transfers between devices, along(): lax.ppermute(rows, 'blk', [(order[i - 1], order[i]) for i in range(n_blk)])  8.8 us
    pallas_call x4, Pallas kernels, call(): pl.pallas_call(kernel, out_shape=shapes, in_specs=whole_in_vmem(len(args)...  5.96 us
    ppermute x7, waiting for transfers between devices, across(): return lax.ppermute(rows, 'sub', swap)  2.13 us
    unnamed x6, local copies, waits for them, and re-layouts  1.65 us
    ppermute x4, waiting for transfers between devices, other_core(): return lax.ppermute(rows, 'pair', swap)  1.1 us
  transfers between devices with their start and end apart: 18, of which 6 were waited for; matrix products, arithmetic and copies ran while one was open for 0% of the time, Pallas kernels for 6%

profile of v2, /device:TPU:0, one launch (start us, length us, event | category | flops | bytes accessed | tf_op | source)
XLA Modules:
  0.0 44.2 jit_solution(12612688041009139806)
XLA Ops:
  0.0 0.0 copy-start.2
  0.0 0.0 copy-start.1
  0.0 0.7 %copy-done.2 = s32[192]{0:T(256)S(1)} copy-done((s32[192]{0:T(256)S(1)}, s32[192]{0:T(256)}, u32[]{:S(2)}) %copy-start.2) | copy-done | bytes 792
  0.7 0.0 copy-done.1
  0.7 0.0 copy-start
  0.7 1.0 %copy-done = bf16[192,768]{1,0:T(8,128)(2,1)S(1)} copy-done((bf16[192,768]{1,0:T(8,128)(2,1)S(1)}, bf16[192,768]{1,0:T(8,128)(2,1)}, u32[]{:S(2)}) %copy-start) | copy-done | bytes 294936
  1.7 3.1 %collective-permute-start = (bf16[104,768]{1,0:T(8,128)(2,1)S(1)}, bf16[104,768]{1,0:T(8,128)(2,1)S(1)}, u32[]{:S(2)}, u32[]{:S(2)}) collective-permute-start(bf16[104,768]{1,0:T(8,128)(2,1)S(1)} %get-tuple-element.31), channel_id=1, source_target_pairs={{8,0},{0,4},{4,12},{12,8},{9,1},{1,5},{5,13},{13,9},{10,2},{2,6},{... | collective-permute-start | bytes 479240 | tf_op jit(solution)/shard_map/ppermute | solution.py:204
  4.8 1.5 %collective-permute-start.1 = (bf16[104,768]{1,0:T(8,128)(2,1)S(1)}, bf16[104,768]{1,0:T(8,128)(2,1)S(1)}, u32[]{:S(2)}, u32[]{:S(2)}) collective-permute-start(bf16[104,768]{1,0:T(8,128)(2,1)S(1)} %get-tuple-element.31), channel_id=1, source_target_pairs={{0,2},{2,0},{1,3},{3,1},{4,6},{6,4},{5,7},{7,5},{8,10},{10,8},{9,1... | collective-permute-start | bytes 479240 | tf_op jit(solution)/shard_map/ppermute | solution.py:207
  6.3 2.6 %collective-permute-start.7 = (bf16[96,768]{1,0:T(8,128)(2,1)S(1)}, bf16[96,768]{1,0:T(8,128)(2,1)S(1)}, u32[]{:S(2)}, u32[]{:S(2)}) collective-permute-start(bf16[96,768]{1,0:T(8,128)(2,1)S(1)} %get-tuple-element.36), channel_id=1, source_target_pairs={{8,0},{0,4},{4,12},{12,8},{9,1},{1,5},{5,13},{13,9},{10,2},{2,6},{... | collective-permute-start | bytes 442376 | tf_op jit(solution)/shard_map/ppermute | solution.py:204
  8.9 0.5 %collective-permute-start.8 = (bf16[96,768]{1,0:T(8,128)(2,1)S(1)}, bf16[96,768]{1,0:T(8,128)(2,1)S(1)}, u32[]{:S(2)}, u32[]{:S(2)}) collective-permute-start(bf16[96,768]{1,0:T(8,128)(2,1)S(1)} %get-tuple-element.36), channel_id=1, source_target_pairs={{0,2},{2,0},{1,3},{3,1},{4,6},{6,4},{5,7},{7,5},{8,10},{10,8},{9,1... | collective-permute-start | bytes 442376 | tf_op jit(solution)/shard_map/ppermute | solution.py:207
  9.4 1.3 %collective-permute-done.refs_6_ = bf16[104,768]{1,0:T(8,128)(2,1)S(1)} collective-permute-done((bf16[104,768]{1,0:T(8,128)(2,1)S(1)}, bf16[104,768]{1,0:T(8,128)(2,1)S(1)}, u32[]{:S(2)}, u32[]{:S(2)}) %collective-permute-start) | collective-permute-done | bytes 159776 | tf_op jit(solution)/shard_map/ppermute | solution.py:204
  10.7 0.0 collective-permute-done.1.refs_2_
  10.7 3.7 %collective-permute-start.2 = (bf16[104,768]{1,0:T(8,128)(2,1)S(1)}, bf16[104,768]{1,0:T(8,128)(2,1)S(1)}, u32[]{:S(2)}, u32[]{:S(2)}) collective-permute-start(bf16[104,768]{1,0:T(8,128)(2,1)S(1)} %collective-permute-done.refs_6_), channel_id=1, source_target_pairs={{8,0},{0,4},{4,12},{12,8},{9,1},{1,5},{5,13},{13,9},{10,2},{2,6},{... | collective-permute-start | bytes 479240 | tf_op jit(solution)/shard_map/ppermute | solution.py:204
  14.4 1.5 %collective-permute-start.3 = (bf16[104,768]{1,0:T(8,128)(2,1)S(1)}, bf16[104,768]{1,0:T(8,128)(2,1)S(1)}, u32[]{:S(2)}, u32[]{:S(2)}) collective-permute-start(bf16[104,768]{1,0:T(8,128)(2,1)S(1)} %collective-permute-done.refs_6_), channel_id=1, source_target_pairs={{0,2},{2,0},{1,3},{3,1},{4,6},{6,4},{5,7},{7,5},{8,10},{10,8},{9,1... | collective-permute-start | bytes 479240 | tf_op jit(solution)/shard_map/ppermute | solution.py:207
  15.9 0.0 collective-permute-start.6
  15.9 0.0 collective-permute-done.7.refs_7_
  15.9 0.0 collective-permute-done.8.refs_3_
  15.9 0.6 %collective-permute-start.10 = (bf16[96,768]{1,0:T(8,128)(2,1)S(1)}, bf16[96,768]{1,0:T(8,128)(2,1)S(1)}, u32[]{:S(2)}, u32[]{:S(2)}) collective-permute-start(bf16[96,768]{1,0:T(8,128)(2,1)S(1)} %collective-permute-done.7.refs_7_), channel_id=1, source_target_pairs={{0,2},{2,0},{1,3},{3,1},{4,6},{6,4},{5,7},{7,5},{8,10},{10,8},{9,1... | collective-permute-start | bytes 442376 | tf_op jit(solution)/shard_map/ppermute | solution.py:207
  16.5 1.7 %collective-permute-start.9 = (bf16[96,768]{1,0:T(8,128)(2,1)S(1)}, bf16[96,768]{1,0:T(8,128)(2,1)S(1)}, u32[]{:S(2)}, u32[]{:S(2)}) collective-permute-start(bf16[96,768]{1,0:T(8,128)(2,1)S(1)} %collective-permute-done.7.refs_7_), channel_id=1, source_target_pairs={{8,0},{0,4},{4,12},{12,8},{9,1},{1,5},{5,13},{13,9},{10,2},{2,6},{... | collective-permute-start | bytes 442376 | tf_op jit(solution)/shard_map/ppermute | solution.py:204
  18.2 0.0 collective-permute-done.2.refs_4_
  18.2 2.1 %collective-permute-done.3.refs_4_ = bf16[104,768]{1,0:T(8,128)(2,1)S(1)} collective-permute-done((bf16[104,768]{1,0:T(8,128)(2,1)S(1)}, bf16[104,768]{1,0:T(8,128)(2,1)S(1)}, u32[]{:S(2)}, u32[]{:S(2)}) %collective-permute-start.3) | collective-permute-done | bytes 159776 | tf_op jit(solution)/shard_map/ppermute | solution.py:207
  20.3 0.9 %collective-permute-start.4 = (bf16[104,768]{1,0:T(8,128)(2,1)S(1)}, bf16[104,768]{1,0:T(8,128)(2,1)S(1)}, u32[]{:S(2)}, u32[]{:S(2)}) collective-permute-start(bf16[104,768]{1,0:T(8,128)(2,1)S(1)} %collective-permute-done.2.refs_4_), channel_id=1, source_target_pairs={{8,0},{0,4},{4,12},{12,8},{9,1},{1,5},{5,13},{13,9},{10,2},{2,6},{... | collective-permute-start | bytes 479240 | tf_op jit(solution)/shard_map/ppermute | solution.py:204
  21.2 2.5 %collective-permute-start.5 = (bf16[104,768]{1,0:T(8,128)(2,1)S(1)}, bf16[104,768]{1,0:T(8,128)(2,1)S(1)}, u32[]{:S(2)}, u32[]{:S(2)}) collective-permute-start(bf16[104,768]{1,0:T(8,128)(2,1)S(1)} %collective-permute-done.2.refs_4_), channel_id=1, source_target_pairs={{0,2},{2,0},{1,3},{3,1},{4,6},{6,4},{5,7},{7,5},{8,10},{10,8},{9,1... | collective-permute-start | bytes 479240 | tf_op jit(solution)/shard_map/ppermute | solution.py:207
  23.7 0.0 collective-permute-done.10.refs_5_
  23.7 0.4 collective-permute-done.9.refs_5_
  24.1 0.9 %collective-permute-start.12 = (bf16[96,768]{1,0:T(8,128)(2,1)S(1)}, bf16[96,768]{1,0:T(8,128)(2,1)S(1)}, u32[]{:S(2)}, u32[]{:S(2)}) collective-permute-start(bf16[96,768]{1,0:T(8,128)(2,1)S(1)} %collective-permute-done.9.refs_5_), channel_id=1, source_target_pairs={{8,0},{0,4},{4,12},{12,8},{9,1},{1,5},{5,13},{13,9},{10,2},{2,6},{... | collective-permute-start | bytes 442376 | tf_op jit(solution)/shard_map/ppermute | solution.py:204
  25.0 1.8 %collective-permute-start.13 = (bf16[96,768]{1,0:T(8,128)(2,1)S(1)}, bf16[96,768]{1,0:T(8,128)(2,1)S(1)}, u32[]{:S(2)}, u32[]{:S(2)}) collective-permute-start(bf16[96,768]{1,0:T(8,128)(2,1)S(1)} %collective-permute-done.9.refs_5_), channel_id=1, source_target_pairs={{0,2},{2,0},{1,3},{3,1},{4,6},{6,4},{5,7},{7,5},{8,10},{10,8},{9,1... | collective-permute-start | bytes 442376 | tf_op jit(solution)/shard_map/ppermute | solution.py:207
  26.8 0.0 collective-permute-done.6.refs_1_
  26.8 2.5 %shard_map.38 = (f32[192,896]{1,0:T(8,128)S(1)}, f32[192,896]{1,0:T(8,128)S(1)}) custom-call(bf16[200,768]{1,0:T(8,128)(2,1)S(1)} %get-tuple-element.30.refs_0_.own, bf16[200,768]{1,0:T(8,128)(2,1)S(1)} %collective-permute-done.6.refs_1_, bf16[104,768]{1,0:T(8,128)(2,1)S(1)} %collective-permute-done.1.refs_2_, ...), custom_call_target="tpu_custom_call" | custom-call | tf_op jit(solution)/shard_map/pallas_call | solution.py:165
  29.3 0.9 %collective-permute-done.12.refs_7_ = bf16[96,768]{1,0:T(8,128)(2,1)S(1)} collective-permute-done((bf16[96,768]{1,0:T(8,128)(2,1)S(1)}, bf16[96,768]{1,0:T(8,128)(2,1)S(1)}, u32[]{:S(2)}, u32[]{:S(2)}) %collective-permute-start.12) | collective-permute-done | bytes 147488 | tf_op jit(solution)/shard_map/ppermute | solution.py:204
  30.1 0.0 collective-permute-done.13.refs_3_
  30.1 0.0 collective-permute-done.4.refs_6_
  30.2 0.0 collective-permute-done.5.refs_2_
  30.2 1.8 %shard_map.39 = (f32[192,896]{1,0:T(8,128)S(1)}, f32[192,896]{1,0:T(8,128)S(1)}) custom-call(bf16[200,768]{1,0:T(8,128)(2,1)S(1)} %get-tuple-element.30.refs_0_.own, bf16[200,768]{1,0:T(8,128)(2,1)S(1)} %collective-permute-done.6.refs_1_, bf16[104,768]{1,0:T(8,128)(2,1)S(1)} %collective-permute-done.5.refs_2_, ...), custom_call_target="tpu_custom_call", output_to_operand_aliasing={{0}: (8, {}), {1}: (9, {})} | custom-call | tf_op jit(solution)/shard_map/pallas_call | solution.py:165
  32.0 0.1 collective-permute-start.15
  32.1 2.0 %collective-permute-start.11 = (bf16[104,768]{1,0:T(8,128)(2,1)S(1)}, bf16[104,768]{1,0:T(8,128)(2,1)S(1)}, u32[]{:S(2)}, u32[]{:S(2)}) collective-permute-start(bf16[104,768]{1,0:T(8,128)(2,1)S(1)} %collective-permute-done.4.refs_6_), channel_id=1, source_target_pairs={{0,2},{2,0},{1,3},{3,1},{4,6},{6,4},{5,7},{7,5},{8,10},{10,8},{9,1... | collective-permute-start | bytes 479240 | tf_op jit(solution)/shard_map/ppermute | solution.py:207
  34.1 0.6 %collective-permute-start.14 = (bf16[96,768]{1,0:T(8,128)(2,1)S(1)}, bf16[96,768]{1,0:T(8,128)(2,1)S(1)}, u32[]{:S(2)}, u32[]{:S(2)}) collective-permute-start(bf16[96,768]{1,0:T(8,128)(2,1)S(1)} %collective-permute-done.13.refs_3_), channel_id=1, source_target_pairs={{8,0},{0,4},{4,12},{12,8},{9,1},{1,5},{5,13},{13,9},{10,2},{2,6},{... | collective-permute-start | bytes 442376 | tf_op jit(solution)/shard_map/ppermute | solution.py:204
  34.8 6.2 %collective-permute-done.14.second = bf16[96,768]{1,0:T(8,128)(2,1)S(1)} collective-permute-done((bf16[96,768]{1,0:T(8,128)(2,1)S(1)}, bf16[96,768]{1,0:T(8,128)(2,1)S(1)}, u32[]{:S(2)}, u32[]{:S(2)}) %collective-permute-start.14) | collective-permute-done | bytes 147488 | tf_op jit(solution)/shard_map/ppermute | solution.py:204
  40.9 0.0 collective-permute-done.11.first
  40.9 0.0 collective-permute-done.15.theirs
  40.9 0.0 collective-permute-start.16
  40.9 0.5 %collective-permute-start.17 = (bf16[96,768]{1,0:T(8,128)(2,1)S(1)}, bf16[96,768]{1,0:T(8,128)(2,1)S(1)}, u32[]{:S(2)}, u32[]{:S(2)}) collective-permute-start(bf16[96,768]{1,0:T(8,128)(2,1)S(1)} %collective-permute-done.14.second), channel_id=1, source_target_pairs={{0,1},{1,0},{2,3},{3,2},{4,5},{5,4},{6,7},{7,6},{8,9},{9,8},{10,11... | collective-permute-start | bytes 442376 | tf_op jit(solution)/shard_map/ppermute | solution.py:210
  41.4 1.1 %collective-permute-done.17.second_other = bf16[96,768]{1,0:T(8,128)(2,1)S(1)} collective-permute-done((bf16[96,768]{1,0:T(8,128)(2,1)S(1)}, bf16[96,768]{1,0:T(8,128)(2,1)S(1)}, u32[]{:S(2)}, u32[]{:S(2)}) %collective-permute-start.17) | collective-permute-done | bytes 147488 | tf_op jit(solution)/shard_map/ppermute | solution.py:210
  42.5 0.0 collective-permute-done.16.first_other
  42.5 1.6 %shard_map.40 = bf16[192,768]{1,0:T(8,128)(2,1)} custom-call(bf16[200,768]{1,0:T(8,128)(2,1)S(1)} %get-tuple-element.30.refs_0_.own, bf16[104,768]{1,0:T(8,128)(2,1)S(1)} %collective-permute-done.11.first, bf16[96,768]{1,0:T(8,128)(2,1)S(1)} %collective-permute-done.14.second, bf16[104,768]{1,0:T(8,128)(2,1)S(1)} %collective-permute-done.16.first_other, ...), custom_call_target="tpu_custom_call" | custom-call | tf_op jit(solution)/shard_map/pallas_call | solution.py:165
  (1 shorter events, 0.0 us)
Async XLA Ops:
  0.0 0.7 %copy-start.2 = (s32[192]{0:T(256)S(1)}, s32[192]{0:T(256)}, u32[]{:S(2)}) copy-start(s32[192]{0:T(256)} %param.5) | copy-start | bytes 2308
  0.0 0.7 %copy-start.1 = (s32[192,1]{0,1:T(1,128)S(1)}, s32[192,1]{0,1:T(1,128)}, u32[]{:S(2)}) copy-start(s32[192,1]{0,1:T(1,128)} %param.4) | copy-start | bytes 2308
  0.7 1.0 %copy-start = (bf16[192,768]{1,0:T(8,128)(2,1)S(1)}, bf16[192,768]{1,0:T(8,128)(2,1)}, u32[]{:S(2)}) copy-start(bf16[192,768]{1,0:T(8,128)(2,1)} %rows.1) | copy-start | bytes 884740
  1.7 9.0 %collective-permute-start = (bf16[104,768]{1,0:T(8,128)(2,1)S(1)}, bf16[104,768]{1,0:T(8,128)(2,1)S(1)}, u32[]{:S(2)}, u32[]{:S(2)}) collective-permute-start(bf16[104,768]{1,0:T(8,128)(2,1)S(1)} %get-tuple-element.31), channel_id=1, source_target_pairs={{8,0},{0,4},{4,12},{12,8},{9,1},{1,5},{5,13},{13,9},{10,2},{2,6},{... | collective-permute-start | bytes 479240 | tf_op jit(solution)/shard_map/ppermute | solution.py:204
  4.8 6.0 %collective-permute-start.1 = (bf16[104,768]{1,0:T(8,128)(2,1)S(1)}, bf16[104,768]{1,0:T(8,128)(2,1)S(1)}, u32[]{:S(2)}, u32[]{:S(2)}) collective-permute-start(bf16[104,768]{1,0:T(8,128)(2,1)S(1)} %get-tuple-element.31), channel_id=1, source_target_pairs={{0,2},{2,0},{1,3},{3,1},{4,6},{6,4},{5,7},{7,5},{8,10},{10,8},{9,1... | collective-permute-start | bytes 479240 | tf_op jit(solution)/shard_map/ppermute | solution.py:207
  6.3 9.6 %collective-permute-start.7 = (bf16[96,768]{1,0:T(8,128)(2,1)S(1)}, bf16[96,768]{1,0:T(8,128)(2,1)S(1)}, u32[]{:S(2)}, u32[]{:S(2)}) collective-permute-start(bf16[96,768]{1,0:T(8,128)(2,1)S(1)} %get-tuple-element.36), channel_id=1, source_target_pairs={{8,0},{0,4},{4,12},{12,8},{9,1},{1,5},{5,13},{13,9},{10,2},{2,6},{... | collective-permute-start | bytes 442376 | tf_op jit(solution)/shard_map/ppermute | solution.py:204
  8.9 7.0 %collective-permute-start.8 = (bf16[96,768]{1,0:T(8,128)(2,1)S(1)}, bf16[96,768]{1,0:T(8,128)(2,1)S(1)}, u32[]{:S(2)}, u32[]{:S(2)}) collective-permute-start(bf16[96,768]{1,0:T(8,128)(2,1)S(1)} %get-tuple-element.36), channel_id=1, source_target_pairs={{0,2},{2,0},{1,3},{3,1},{4,6},{6,4},{5,7},{7,5},{8,10},{10,8},{9,1... | collective-permute-start | bytes 442376 | tf_op jit(solution)/shard_map/ppermute | solution.py:207
  10.7 7.5 %collective-permute-start.2 = (bf16[104,768]{1,0:T(8,128)(2,1)S(1)}, bf16[104,768]{1,0:T(8,128)(2,1)S(1)}, u32[]{:S(2)}, u32[]{:S(2)}) collective-permute-start(bf16[104,768]{1,0:T(8,128)(2,1)S(1)} %collective-permute-done.refs_6_), channel_id=1, source_target_pairs={{8,0},{0,4},{4,12},{12,8},{9,1},{1,5},{5,13},{13,9},{10,2},{2,6},{... | collective-permute-start | bytes 479240 | tf_op jit(solution)/shard_map/ppermute | solution.py:204
  14.4 5.9 %collective-permute-start.3 = (bf16[104,768]{1,0:T(8,128)(2,1)S(1)}, bf16[104,768]{1,0:T(8,128)(2,1)S(1)}, u32[]{:S(2)}, u32[]{:S(2)}) collective-permute-start(bf16[104,768]{1,0:T(8,128)(2,1)S(1)} %collective-permute-done.refs_6_), channel_id=1, source_target_pairs={{0,2},{2,0},{1,3},{3,1},{4,6},{6,4},{5,7},{7,5},{8,10},{10,8},{9,1... | collective-permute-start | bytes 479240 | tf_op jit(solution)/shard_map/ppermute | solution.py:207
  15.9 10.9 %collective-permute-start.6 = (bf16[200,768]{1,0:T(8,128)(2,1)S(1)}, bf16[200,768]{1,0:T(8,128)(2,1)S(1)}, u32[]{:S(2)}, u32[]{:S(2)}) collective-permute-start(bf16[200,768]{1,0:T(8,128)(2,1)S(1)} %get-tuple-element.30.refs_0_.own), channel_id=1, source_target_pairs={{0,1},{1,0},{2,3},{3,2},{4,5},{5,4},{6,7},{7,6},{8,9},{9,8},{10,11... | collective-permute-start | bytes 921608 | tf_op jit(solution)/shard_map/ppermute | solution.py:210
  15.9 7.8 %collective-permute-start.10 = (bf16[96,768]{1,0:T(8,128)(2,1)S(1)}, bf16[96,768]{1,0:T(8,128)(2,1)S(1)}, u32[]{:S(2)}, u32[]{:S(2)}) collective-permute-start(bf16[96,768]{1,0:T(8,128)(2,1)S(1)} %collective-permute-done.7.refs_7_), channel_id=1, source_target_pairs={{0,2},{2,0},{1,3},{3,1},{4,6},{6,4},{5,7},{7,5},{8,10},{10,8},{9,1... | collective-permute-start | bytes 442376 | tf_op jit(solution)/shard_map/ppermute | solution.py:207
  16.5 7.6 %collective-permute-start.9 = (bf16[96,768]{1,0:T(8,128)(2,1)S(1)}, bf16[96,768]{1,0:T(8,128)(2,1)S(1)}, u32[]{:S(2)}, u32[]{:S(2)}) collective-permute-start(bf16[96,768]{1,0:T(8,128)(2,1)S(1)} %collective-permute-done.7.refs_7_), channel_id=1, source_target_pairs={{8,0},{0,4},{4,12},{12,8},{9,1},{1,5},{5,13},{13,9},{10,2},{2,6},{... | collective-permute-start | bytes 442376 | tf_op jit(solution)/shard_map/ppermute | solution.py:204
  20.3 9.8 %collective-permute-start.4 = (bf16[104,768]{1,0:T(8,128)(2,1)S(1)}, bf16[104,768]{1,0:T(8,128)(2,1)S(1)}, u32[]{:S(2)}, u32[]{:S(2)}) collective-permute-start(bf16[104,768]{1,0:T(8,128)(2,1)S(1)} %collective-permute-done.2.refs_4_), channel_id=1, source_target_pairs={{8,0},{0,4},{4,12},{12,8},{9,1},{1,5},{5,13},{13,9},{10,2},{2,6},{... | collective-permute-start | bytes 479240 | tf_op jit(solution)/shard_map/ppermute | solution.py:204
  21.2 8.9 %collective-permute-start.5 = (bf16[104,768]{1,0:T(8,128)(2,1)S(1)}, bf16[104,768]{1,0:T(8,128)(2,1)S(1)}, u32[]{:S(2)}, u32[]{:S(2)}) collective-permute-start(bf16[104,768]{1,0:T(8,128)(2,1)S(1)} %collective-permute-done.2.refs_4_), channel_id=1, source_target_pairs={{0,2},{2,0},{1,3},{3,1},{4,6},{6,4},{5,7},{7,5},{8,10},{10,8},{9,1... | collective-permute-start | bytes 479240 | tf_op jit(solution)/shard_map/ppermute | solution.py:207
  24.1 6.0 %collective-permute-start.12 = (bf16[96,768]{1,0:T(8,128)(2,1)S(1)}, bf16[96,768]{1,0:T(8,128)(2,1)S(1)}, u32[]{:S(2)}, u32[]{:S(2)}) collective-permute-start(bf16[96,768]{1,0:T(8,128)(2,1)S(1)} %collective-permute-done.9.refs_5_), channel_id=1, source_target_pairs={{8,0},{0,4},{4,12},{12,8},{9,1},{1,5},{5,13},{13,9},{10,2},{2,6},{... | collective-permute-start | bytes 442376 | tf_op jit(solution)/shard_map/ppermute | solution.py:204
  25.0 5.1 %collective-permute-start.13 = (bf16[96,768]{1,0:T(8,128)(2,1)S(1)}, bf16[96,768]{1,0:T(8,128)(2,1)S(1)}, u32[]{:S(2)}, u32[]{:S(2)}) collective-permute-start(bf16[96,768]{1,0:T(8,128)(2,1)S(1)} %collective-permute-done.9.refs_5_), channel_id=1, source_target_pairs={{0,2},{2,0},{1,3},{3,1},{4,6},{6,4},{5,7},{7,5},{8,10},{10,8},{9,1... | collective-permute-start | bytes 442376 | tf_op jit(solution)/shard_map/ppermute | solution.py:207
  32.0 9.0 %collective-permute-start.15 = (f32[192,896]{1,0:T(8,128)S(1)}, f32[192,896]{1,0:T(8,128)S(1)}, u32[]{:S(2)}, u32[]{:S(2)}) collective-permute-start(f32[192,896]{1,0:T(8,128)S(1)} %get-tuple-element.50), channel_id=1, source_target_pairs={{0,1},{1,0},{2,3},{3,2},{4,5},{5,4},{6,7},{7,6},{8,9},{9,8},{10,11... | collective-permute-start | bytes 2064392 | tf_op jit(solution)/shard_map/ppermute | solution.py:210
  32.1 8.9 %collective-permute-start.11 = (bf16[104,768]{1,0:T(8,128)(2,1)S(1)}, bf16[104,768]{1,0:T(8,128)(2,1)S(1)}, u32[]{:S(2)}, u32[]{:S(2)}) collective-permute-start(bf16[104,768]{1,0:T(8,128)(2,1)S(1)} %collective-permute-done.4.refs_6_), channel_id=1, source_target_pairs={{0,2},{2,0},{1,3},{3,1},{4,6},{6,4},{5,7},{7,5},{8,10},{10,8},{9,1... | collective-permute-start | bytes 479240 | tf_op jit(solution)/shard_map/ppermute | solution.py:207
  34.1 6.8 %collective-permute-start.14 = (bf16[96,768]{1,0:T(8,128)(2,1)S(1)}, bf16[96,768]{1,0:T(8,128)(2,1)S(1)}, u32[]{:S(2)}, u32[]{:S(2)}) collective-permute-start(bf16[96,768]{1,0:T(8,128)(2,1)S(1)} %collective-permute-done.13.refs_3_), channel_id=1, source_target_pairs={{8,0},{0,4},{4,12},{12,8},{9,1},{1,5},{5,13},{13,9},{10,2},{2,6},{... | collective-permute-start | bytes 442376 | tf_op jit(solution)/shard_map/ppermute | solution.py:204
  40.9 1.6 %collective-permute-start.16 = (bf16[104,768]{1,0:T(8,128)(2,1)S(1)}, bf16[104,768]{1,0:T(8,128)(2,1)S(1)}, u32[]{:S(2)}, u32[]{:S(2)}) collective-permute-start(bf16[104,768]{1,0:T(8,128)(2,1)S(1)} %collective-permute-done.11.first), channel_id=1, source_target_pairs={{0,1},{1,0},{2,3},{3,2},{4,5},{5,4},{6,7},{7,6},{8,9},{9,8},{10,11... | collective-permute-start | bytes 479240 | tf_op jit(solution)/shard_map/ppermute | solution.py:210
  40.9 1.6 %collective-permute-start.17 = (bf16[96,768]{1,0:T(8,128)(2,1)S(1)}, bf16[96,768]{1,0:T(8,128)(2,1)S(1)}, u32[]{:S(2)}, u32[]{:S(2)}) collective-permute-start(bf16[96,768]{1,0:T(8,128)(2,1)S(1)} %collective-permute-done.14.second), channel_id=1, source_target_pairs={{0,1},{1,0},{2,3},{3,2},{4,5},{5,4},{6,7},{7,6},{8,9},{9,8},{10,11... | collective-permute-start | bytes 442376 | tf_op jit(solution)/shard_map/ppermute | solution.py:210

commit v3 on v2

--- a/solution.py
+++ b/solution.py
@@ -10,6 +10,7 @@
 F32 = jnp.float32
 BF16 = jnp.bfloat16
 VMEM_BYTES = 24 * 1024 * 1024
+PACK_BYTES = 48 * 1024 * 1024
 GATHER_LIMIT = 8 * 1024 * 1024
 
 
@@ -76,19 +77,28 @@
     return lax.rsqrt(jnp.sum(wide * wide, axis=1, keepdims=True) + 1e-06)
 
 
-def pack_kernel(rows, group, cluster, whole, first, second):
+def pack_kernel(rows, group, cluster, whole, first, second, group_here, cluster_here, sems):
     rows_here, width = rows.shape
     half = rows_here // 2
+    copies = [
+        pltpu.make_async_copy(group, group_here, sems.at[0]),
+        pltpu.make_async_copy(cluster, cluster_here, sems.at[1]),
+        pltpu.make_async_copy(rows.at[:half, :], first.at[:half, :], sems.at[2]),
+        pltpu.make_async_copy(rows.at[half:, :], second, sems.at[3]),
+        pltpu.make_async_copy(rows, whole.at[:rows_here, :], sems.at[4]),
+    ]
+    for copy in copies:
+        copy.start()
+    copies[0].wait()
+    copies[1].wait()
     line = lax.broadcasted_iota(jnp.int32, (8, rows_here), 0)
-    named = jnp.where(line == 0, group[...], jnp.where(line == 1, cluster[...], 0))
+    named = jnp.where(line == 0, group_here[...], jnp.where(line == 1, cluster_here[...], 0))
     named = named.astype(F32).astype(BF16)
-    whole[:rows_here, :] = rows[...]
-    whole[rows_here:, :] = jnp.zeros((8, width), BF16)
-    whole[rows_here:, :rows_here] = named
-    first[:half, :] = rows[:half, :]
-    first[half:, :] = jnp.zeros((8, width), BF16)
-    first[half:, :rows_here] = named
-    second[...] = rows[half:, :]
+    for out, top in ((whole, rows_here), (first, half)):
+        out[top:, :] = jnp.zeros((8, width), BF16)
+        out[top:, :rows_here] = named
+    for copy in copies[2:]:
+        copy.wait()
 
 
 def key_row(named):
@@ -129,32 +139,44 @@
     return rows, key, to_row(scale_column(rows))
 
 
-def step_kernel(n_blocks, first, *refs):
+def take_blocks(refs, count):
+    return [with_scale(from_halves(refs.pop(0), refs.pop(0))) for _ in range(count)]
+
+
+def add_side(left, blocks, before, out):
+    width = left[0].shape[1]
+    numer = None if before is None else before[:, :width]
+    denom = None if before is None else before[:, width : width + 1]
+    numer, denom = add_blocks(left, blocks, numer, denom)
+    out[:, :width] = numer
+    out[:, width:] = jnp.broadcast_to(denom, (numer.shape[0], 128))
+
+
+def start_kernel(n_blocks, own, other, *refs):
     refs = list(refs)
-    left = [from_whole(refs.pop(0)), from_whole(refs.pop(0))]
-    blocks = [with_scale(left[0])] if first else []
-    for _ in range(n_blocks):
-        blocks.append(with_scale(from_halves(refs.pop(0), refs.pop(0))))
-    before = None if first else [refs.pop(0), refs.pop(0)]
-    width = left[0][0].shape[1]
+    left = [from_whole(own), from_whole(other)]
+    blocks = [with_scale(left[0])] + take_blocks(refs, n_blocks)
     for side in range(2):
-        numer = None if first else before[side][:, :width]
-        denom = None if first else before[side][:, width : width + 1]
-        numer, denom = add_blocks(left[side], blocks, numer, denom)
-        refs[side][:, :width] = numer
-        refs[side][:, width:] = jnp.broadcast_to(denom, (numer.shape[0], 128))
-
-
-def last_kernel(own, first, second, first_other, second_other, mine, theirs, out):
+        add_side(left[side], blocks, None, refs[side])
+
+
+def both_kernel(n_blocks, own, other, *refs):
+    refs = list(refs)
+    blocks = take_blocks(refs, n_blocks)
+    for side, left in enumerate((own, other)):
+        add_side(from_whole(left), blocks, refs[side], refs[2 + side])
+
+
+def one_kernel(n_blocks, left, *refs):
+    refs = list(refs)
+    blocks = take_blocks(refs, n_blocks)
+    add_side(from_whole(left), blocks, refs[0], refs[1])
+
+
+def mean_kernel(mine, theirs, out):
     width = out.shape[1]
-    blocks = [
-        with_scale(from_halves(first, second)),
-        with_scale(from_halves(first_other, second_other)),
-    ]
-    numer = mine[:, :width] + theirs[:, :width]
     denom = mine[:, width : width + 1] + theirs[:, width : width + 1]
-    numer, denom = add_blocks(from_whole(own), blocks, numer, denom)
-    out[...] = (numer / denom).astype(BF16)
+    out[...] = ((mine[:, :width] + theirs[:, :width]) / denom).astype(BF16)
 
 
 def whole_in_vmem(count):
@@ -172,52 +194,74 @@
     )(*args)
 
 
-def step(left, right, before):
-    rows_here, width = left[0].shape
-    args = list(left) + [half for block in right for half in block]
-    aliases = {}
-    if before is not None:
-        aliases = {len(args): 0, len(args) + 1: 1}
-        args += list(before)
-    shape = jax.ShapeDtypeStruct((rows_here - 8, width + 128), F32)
-    return call(
-        functools.partial(step_kernel, len(right), before is None), [shape, shape], args, aliases
-    )
-
-
-def folded_ring(size):
-    return [0] + list(range(1, size, 2)) + list(range(2, size, 2))[::-1]
-
-
-def together(*arrays):
-    return lax.optimization_barrier(arrays)
-
-
-def by_block(embeddings, group_of, cluster_id):
+def pack(embeddings, group_of, cluster_id):
     rows_here, width = embeddings.shape
     half = rows_here // 2
-    n_blk = lax.axis_size("blk")
-    order = folded_ring(n_blk)
-    swap = [(0, 1), (1, 0)]
-
-    def along(rows):
-        return lax.ppermute(rows, "blk", [(order[i - 1], order[i]) for i in range(n_blk)])
-
-    def across(rows):
-        return lax.ppermute(rows, "sub", swap)
-
-    def other_core(rows):
-        return lax.ppermute(rows, "pair", swap)
-
-    whole, first, second = call(
+    line = (1, rows_here)
+    return pl.pallas_call(
         pack_kernel,
-        [
+        out_shape=[
             jax.ShapeDtypeStruct((rows_here + 8, width), BF16),
             jax.ShapeDtypeStruct((half + 8, width), BF16),
             jax.ShapeDtypeStruct((half, width), BF16),
         ],
-        [embeddings, group_of.reshape(1, rows_here), cluster_id.reshape(1, rows_here)],
-    )
+        in_specs=[pl.BlockSpec(memory_space=pltpu.HBM)] * 3,
+        out_specs=whole_in_vmem(3),
+        scratch_shapes=[
+            pltpu.VMEM(line, jnp.int32),
+            pltpu.VMEM(line, jnp.int32),
+            pltpu.SemaphoreType.DMA((5,)),
+        ],
+        compiler_params=pltpu.CompilerParams(vmem_limit_bytes=PACK_BYTES),
+    )(embeddings, group_of.reshape(line), cluster_id.reshape(line))
+
+
+def start_both(left, right):
+    rows_here, width = left[0].shape
+    shape = jax.ShapeDtypeStruct((rows_here - 8, width + 128), F32)
+    args = list(left) + [half for block in right for half in block]
+    return call(functools.partial(start_kernel, len(right)), [shape, shape], args)
+
+
+def add_both(left, right, before):
+    args = list(left) + [half for block in right for half in block] + list(before)
+    at = len(args) - 2
+    shapes = [jax.ShapeDtypeStruct(total.shape, F32) for total in before]
+    return call(
+        functools.partial(both_kernel, len(right)), shapes, args, {at: 0, at + 1: 1}
+    )
+
+
+def add_one(left, right, before):
+    args = [left] + [half for block in right for half in block] + [before]
+    shapes = [jax.ShapeDtypeStruct(before.shape, F32)]
+    return call(functools.partial(one_kernel, len(right)), shapes, args, {len(args) - 1: 0})[0]
+
+
+def folded_ring(size):
+    return [0] + list(range(1, size, 2)) + list(range(2, size, 2))[::-1]
+
+
+def together(*arrays):
+    return lax.optimization_barrier(arrays)
+
+
+def by_block(embeddings, group_of, cluster_id):
+    rows_here, width = embeddings.shape
+    n_blk = lax.axis_size("blk")
+    order = folded_ring(n_blk)
+    swap = [(0, 1), (1, 0)]
+
+    def along(rows):
+        return lax.ppermute(rows, "blk", [(order[i - 1], order[i]) for i in range(n_blk)])
+
+    def across(rows):
+        return lax.ppermute(rows, "sub", swap)
+
+    def other_core(rows):
+        return lax.ppermute(rows, "pair", swap)
+
+    whole, first, second = pack(embeddings, group_of, cluster_id)
     along_by = [(first, second)]
     across_by = []
     for s in range(1, n_blk):
@@ -227,25 +271,14 @@
         along_by.append(tuple(pair[0] for pair in pairs))
         across_by.append(tuple(pair[1] for pair in pairs))
     left = (whole, other_core(whole))
-    early = n_blk // 2
-    total = step(left, across_by[:early] + along_by[1:early], None)
-    far, total = together(along_by[-1][0], total)
-    last_first = across(far)
-    last_second = along(across_by[-1][1])
-    mine, theirs = step(left, across_by[early:] + along_by[early:], total)
-    last_first, last_second, theirs = together(last_first, last_second, other_core(theirs))
+    total = start_both(left, across_by[:-1] + along_by[1:-1])
+    far_first, mine, theirs = together(along_by[-1][0], *total)
+    last = (across(far_first), along(across_by[-1][1]))
+    mine, theirs = add_both(left, [across_by[-1], along_by[-1]], (mine, theirs))
+    theirs = other_core(add_one(left[1], [last], theirs))
+    mine = add_one(left[0], [last], mine)
     (out,) = call(
-        last_kernel,
-        [jax.ShapeDtypeStruct((rows_here, width), BF16)],
-        [
-            whole,
-            last_first,
-            last_second,
-            other_core(last_first),
-            other_core(last_second),
-            mine,
-            theirs,
-        ],
+        mean_kernel, [jax.ShapeDtypeStruct((rows_here, width), BF16)], [mine, theirs]
     )
     return out
 

time: 44.3 us -> 41.3 us (0.932)
  waiting for transfers between devices: 12 us -> 8.59 us
  Pallas kernels: 5.96 us -> 7.19 us
  starting transfers between devices: 24.5 us -> 23.6 us
    ppermute x7, waiting for transfers between devices: 8.8 us -> 4.39 us  [along(): lax.ppermute(rows, 'blk', [(order[i - 1], order[i]) for i in range(n_blk)])]
    ppermute x7, starting transfers between devices: 10.4 us -> 8.73 us  [across(): return lax.ppermute(rows, 'sub', swap)]
    ppermute x7, starting transfers between devices: 13.5 us -> 14.8 us  [along(): lax.ppermute(rows, 'blk', [(order[i - 1], order[i]) for i in range(n_blk)])]
    pallas_call x4 -> x5, Pallas kernels: 5.96 us -> 6.71 us  [call(): pl.pallas_call(kernel, out_shape=shapes, in_specs=whole_in_vmem(len(args)...]
    ppermute x7, waiting for transfers between devices: 2.13 us -> 2.68 us  [across(): return lax.ppermute(rows, 'sub', swap)]
    ppermute x4 -> x2, starting transfers between devices: 0.58 us -> 0.07 us  [other_core(): return lax.ppermute(rows, 'pair', swap)]
    pallas_call x0 -> x1, Pallas kernels: none -> 0.48 us  [pack(): pl.pallas_call(pack_kernel, out_shape=[jax.ShapeDtypeStruct((rows_here +...]
    ppermute x4 -> x2, waiting for transfers between devices: 1.1 us -> 1.52 us  [other_core(): return lax.ppermute(rows, 'pair', swap)]
  transfers between devices with their start and end apart: 18 -> 16, of which waited for: 6 -> 6; matrix products, arithmetic and copies ran while one was open for 0% -> 0% of each run, Pallas kernels for 6% -> 13%
where the time goes in v3:
time: 41.3 us; the launch traced here: 41.1 us
  starting transfers between devices  23.6 us (57%)
  waiting for transfers between devices  8.59 us (21%)
  Pallas kernels  7.19 us (17%)
  local copies, waits for them, and re-layouts  1.65 us (4%)
    ppermute x7, starting transfers between devices, along(): lax.ppermute(rows, 'blk', [(order[i - 1], order[i]) for i in range(n_blk)])  14.8 us
    ppermute x7, starting transfers between devices, across(): return lax.ppermute(rows, 'sub', swap)  8.73 us
    pallas_call x5, Pallas kernels, call(): pl.pallas_call(kernel, out_shape=shapes, in_specs=whole_in_vmem(len(args)...  6.71 us
    ppermute x7, waiting for transfers between devices, along(): lax.ppermute(rows, 'blk', [(order[i - 1], order[i]) for i in range(n_blk)])  4.39 us
    ppermute x7, waiting for transfers between devices, across(): return lax.ppermute(rows, 'sub', swap)  2.68 us
    unnamed x6, local copies, waits for them, and re-layouts  1.65 us
    ppermute x2, waiting for transfers between devices, other_core(): return lax.ppermute(rows, 'pair', swap)  1.52 us
  transfers between devices with their start and end apart: 16, of which 6 were waited for; matrix products, arithmetic and copies ran while one was open for 0% of the time, Pallas kernels for 13%

profile of v3, /device:TPU:0, one launch (start us, length us, event | category | flops | bytes accessed | tf_op | source)
XLA Modules:
  0.0 41.1 jit_solution(8001613059592592525)
XLA Ops:
  0.0 0.0 copy-start.2
  0.0 0.0 copy-start.1
  0.0 0.7 %copy-done.2 = s32[192]{0:T(256)S(1)} copy-done((s32[192]{0:T(256)S(1)}, s32[192]{0:T(256)}, u32[]{:S(2)}) %copy-start.2) | copy-done | bytes 792
  0.7 0.0 copy-done.1
  0.7 0.0 copy-start
  0.7 1.0 %copy-done = bf16[192,768]{1,0:T(8,128)(2,1)S(1)} copy-done((bf16[192,768]{1,0:T(8,128)(2,1)S(1)}, bf16[192,768]{1,0:T(8,128)(2,1)}, u32[]{:S(2)}) %copy-start) | copy-done | bytes 294936
  1.7 0.5 %shard_map.37 = (bf16[200,768]{1,0:T(8,128)(2,1)S(1)}, bf16[104,768]{1,0:T(8,128)(2,1)S(1)}, bf16[96,768]{1,0:T(8,128)(2,1)S(1)}) custom-call(bf16[192,768]{1,0:T(8,128)(2,1)S(1)} %copy-done, s32[1,192]{1,0:T(1,128)S(1)} %bitcast.2, s32[1,192]{1,0:T(1,128)S(1)} %bitcast.3), custom_call_target="tpu_custom_call" | custom-call | tf_op jit(solution)/shard_map/pallas_call | solution.py:201
  2.1 3.1 %collective-permute-start = (bf16[104,768]{1,0:T(8,128)(2,1)S(1)}, bf16[104,768]{1,0:T(8,128)(2,1)S(1)}, u32[]{:S(2)}, u32[]{:S(2)}) collective-permute-start(bf16[104,768]{1,0:T(8,128)(2,1)S(1)} %get-tuple-element.28), channel_id=1, source_target_pairs={{8,0},{0,4},{4,12},{12,8},{9,1},{1,5},{5,13},{13,9},{10,2},{2,6},{... | collective-permute-start | bytes 479240 | tf_op jit(solution)/shard_map/ppermute | solution.py:256
  5.2 1.5 %collective-permute-start.1 = (bf16[104,768]{1,0:T(8,128)(2,1)S(1)}, bf16[104,768]{1,0:T(8,128)(2,1)S(1)}, u32[]{:S(2)}, u32[]{:S(2)}) collective-permute-start(bf16[104,768]{1,0:T(8,128)(2,1)S(1)} %get-tuple-element.28), channel_id=1, source_target_pairs={{0,2},{2,0},{1,3},{3,1},{4,6},{6,4},{5,7},{7,5},{8,10},{10,8},{9,1... | collective-permute-start | bytes 479240 | tf_op jit(solution)/shard_map/ppermute | solution.py:259
  6.7 2.6 %collective-permute-start.7 = (bf16[96,768]{1,0:T(8,128)(2,1)S(1)}, bf16[96,768]{1,0:T(8,128)(2,1)S(1)}, u32[]{:S(2)}, u32[]{:S(2)}) collective-permute-start(bf16[96,768]{1,0:T(8,128)(2,1)S(1)} %get-tuple-element.33), channel_id=1, source_target_pairs={{8,0},{0,4},{4,12},{12,8},{9,1},{1,5},{5,13},{13,9},{10,2},{2,6},{... | collective-permute-start | bytes 442376 | tf_op jit(solution)/shard_map/ppermute | solution.py:256
  9.3 0.5 %collective-permute-start.8 = (bf16[96,768]{1,0:T(8,128)(2,1)S(1)}, bf16[96,768]{1,0:T(8,128)(2,1)S(1)}, u32[]{:S(2)}, u32[]{:S(2)}) collective-permute-start(bf16[96,768]{1,0:T(8,128)(2,1)S(1)} %get-tuple-element.33), channel_id=1, source_target_pairs={{0,2},{2,0},{1,3},{3,1},{4,6},{6,4},{5,7},{7,5},{8,10},{10,8},{9,1... | collective-permute-start | bytes 442376 | tf_op jit(solution)/shard_map/ppermute | solution.py:259
  9.8 1.3 %collective-permute-done.refs_4_ = bf16[104,768]{1,0:T(8,128)(2,1)S(1)} collective-permute-done((bf16[104,768]{1,0:T(8,128)(2,1)S(1)}, bf16[104,768]{1,0:T(8,128)(2,1)S(1)}, u32[]{:S(2)}, u32[]{:S(2)}) %collective-permute-start) | collective-permute-done | bytes 159776 | tf_op jit(solution)/shard_map/ppermute | solution.py:256
  11.2 0.0 collective-permute-done.1.refs_0_
  11.2 3.7 %collective-permute-start.2 = (bf16[104,768]{1,0:T(8,128)(2,1)S(1)}, bf16[104,768]{1,0:T(8,128)(2,1)S(1)}, u32[]{:S(2)}, u32[]{:S(2)}) collective-permute-start(bf16[104,768]{1,0:T(8,128)(2,1)S(1)} %collective-permute-done.refs_4_), channel_id=1, source_target_pairs={{8,0},{0,4},{4,12},{12,8},{9,1},{1,5},{5,13},{13,9},{10,2},{2,6},{... | collective-permute-start | bytes 479240 | tf_op jit(solution)/shard_map/ppermute | solution.py:256
  14.8 1.5 %collective-permute-start.3 = (bf16[104,768]{1,0:T(8,128)(2,1)S(1)}, bf16[104,768]{1,0:T(8,128)(2,1)S(1)}, u32[]{:S(2)}, u32[]{:S(2)}) collective-permute-start(bf16[104,768]{1,0:T(8,128)(2,1)S(1)} %collective-permute-done.refs_4_), channel_id=1, source_target_pairs={{0,2},{2,0},{1,3},{3,1},{4,6},{6,4},{5,7},{7,5},{8,10},{10,8},{9,1... | collective-permute-start | bytes 479240 | tf_op jit(solution)/shard_map/ppermute | solution.py:259
  16.3 0.0 collective-permute-start.6
  16.3 0.0 collective-permute-done.7.refs_5_
  16.3 0.0 collective-permute-done.8.refs_1_
  16.4 0.6 %collective-permute-start.10 = (bf16[96,768]{1,0:T(8,128)(2,1)S(1)}, bf16[96,768]{1,0:T(8,128)(2,1)S(1)}, u32[]{:S(2)}, u32[]{:S(2)}) collective-permute-start(bf16[96,768]{1,0:T(8,128)(2,1)S(1)} %collective-permute-done.7.refs_5_), channel_id=1, source_target_pairs={{0,2},{2,0},{1,3},{3,1},{4,6},{6,4},{5,7},{7,5},{8,10},{10,8},{9,1... | collective-permute-start | bytes 442376 | tf_op jit(solution)/shard_map/ppermute | solution.py:259
  17.0 1.7 %collective-permute-start.9 = (bf16[96,768]{1,0:T(8,128)(2,1)S(1)}, bf16[96,768]{1,0:T(8,128)(2,1)S(1)}, u32[]{:S(2)}, u32[]{:S(2)}) collective-permute-start(bf16[96,768]{1,0:T(8,128)(2,1)S(1)} %collective-permute-done.7.refs_5_), channel_id=1, source_target_pairs={{8,0},{0,4},{4,12},{12,8},{9,1},{1,5},{5,13},{13,9},{10,2},{2,6},{... | collective-permute-start | bytes 442376 | tf_op jit(solution)/shard_map/ppermute | solution.py:256
  18.7 0.0 collective-permute-done.2.refs_6_
  18.7 2.1 %collective-permute-done.3.refs_2_ = bf16[104,768]{1,0:T(8,128)(2,1)S(1)} collective-permute-done((bf16[104,768]{1,0:T(8,128)(2,1)S(1)}, bf16[104,768]{1,0:T(8,128)(2,1)S(1)}, u32[]{:S(2)}, u32[]{:S(2)}) %collective-permute-start.3) | collective-permute-done | bytes 159776 | tf_op jit(solution)/shard_map/ppermute | solution.py:259
  20.8 0.9 %collective-permute-start.4 = (bf16[104,768]{1,0:T(8,128)(2,1)S(1)}, bf16[104,768]{1,0:T(8,128)(2,1)S(1)}, u32[]{:S(2)}, u32[]{:S(2)}) collective-permute-start(bf16[104,768]{1,0:T(8,128)(2,1)S(1)} %collective-permute-done.2.refs_6_), channel_id=1, source_target_pairs={{8,0},{0,4},{4,12},{12,8},{9,1},{1,5},{5,13},{13,9},{10,2},{2,6},{... | collective-permute-start | bytes 479240 | tf_op jit(solution)/shard_map/ppermute | solution.py:256
  21.7 2.5 %collective-permute-start.5 = (bf16[104,768]{1,0:T(8,128)(2,1)S(1)}, bf16[104,768]{1,0:T(8,128)(2,1)S(1)}, u32[]{:S(2)}, u32[]{:S(2)}) collective-permute-start(bf16[104,768]{1,0:T(8,128)(2,1)S(1)} %collective-permute-done.2.refs_6_), channel_id=1, source_target_pairs={{0,2},{2,0},{1,3},{3,1},{4,6},{6,4},{5,7},{7,5},{8,10},{10,8},{9,1... | collective-permute-start | bytes 479240 | tf_op jit(solution)/shard_map/ppermute | solution.py:259
  24.1 0.0 collective-permute-done.10.refs_3_
  24.1 0.4 %collective-permute-done.9.refs_7_ = bf16[96,768]{1,0:T(8,128)(2,1)S(1)} collective-permute-done((bf16[96,768]{1,0:T(8,128)(2,1)S(1)}, bf16[96,768]{1,0:T(8,128)(2,1)S(1)}, u32[]{:S(2)}, u32[]{:S(2)}) %collective-permute-start.9) | collective-permute-done | bytes 147488 | tf_op jit(solution)/shard_map/ppermute | solution.py:256
  24.5 0.9 %collective-permute-start.12 = (bf16[96,768]{1,0:T(8,128)(2,1)S(1)}, bf16[96,768]{1,0:T(8,128)(2,1)S(1)}, u32[]{:S(2)}, u32[]{:S(2)}) collective-permute-start(bf16[96,768]{1,0:T(8,128)(2,1)S(1)} %collective-permute-done.9.refs_7_), channel_id=1, source_target_pairs={{8,0},{0,4},{4,12},{12,8},{9,1},{1,5},{5,13},{13,9},{10,2},{2,6},{... | collective-permute-start | bytes 442376 | tf_op jit(solution)/shard_map/ppermute | solution.py:256
  25.4 1.8 %collective-permute-start.13 = (bf16[96,768]{1,0:T(8,128)(2,1)S(1)}, bf16[96,768]{1,0:T(8,128)(2,1)S(1)}, u32[]{:S(2)}, u32[]{:S(2)}) collective-permute-start(bf16[96,768]{1,0:T(8,128)(2,1)S(1)} %collective-permute-done.9.refs_7_), channel_id=1, source_target_pairs={{0,2},{2,0},{1,3},{3,1},{4,6},{6,4},{5,7},{7,5},{8,10},{10,8},{9,1... | collective-permute-start | bytes 442376 | tf_op jit(solution)/shard_map/ppermute | solution.py:259
  27.3 0.0 collective-permute-done.6.other.left
  27.3 3.2 %shard_map.38 = (f32[192,896]{1,0:T(8,128)S(1)}, f32[192,896]{1,0:T(8,128)S(1)}) custom-call(bf16[200,768]{1,0:T(8,128)(2,1)S(1)} %get-tuple-element.27.own.left, bf16[200,768]{1,0:T(8,128)(2,1)S(1)} %collective-permute-done.6.other.left, bf16[104,768]{1,0:T(8,128)(2,1)S(1)} %collective-permute-done.1.refs_0_, ...), custom_call_target="tpu_custom_call" | custom-call | tf_op jit(solution)/shard_map/pallas_call | solution.py:187
  30.5 0.0 collective-permute-done.4.refs_2_
  30.5 0.0 collective-permute-done.5.refs_0_
  30.5 0.3 collective-permute-start.11
  30.8 0.0 collective-permute-done.12.refs_3_
  30.8 0.5 %collective-permute-done.13.refs_1_ = bf16[96,768]{1,0:T(8,128)(2,1)S(1)} collective-permute-done((bf16[96,768]{1,0:T(8,128)(2,1)S(1)}, bf16[96,768]{1,0:T(8,128)(2,1)S(1)}, u32[]{:S(2)}, u32[]{:S(2)}) %collective-permute-start.13) | collective-permute-done | bytes 147488 | tf_op jit(solution)/shard_map/ppermute | solution.py:259
  31.4 2.0 %collective-permute-start.14 = (bf16[96,768]{1,0:T(8,128)(2,1)S(1)}, bf16[96,768]{1,0:T(8,128)(2,1)S(1)}, u32[]{:S(2)}, u32[]{:S(2)}) collective-permute-start(bf16[96,768]{1,0:T(8,128)(2,1)S(1)} %collective-permute-done.13.refs_1_), channel_id=1, source_target_pairs={{8,0},{0,4},{4,12},{12,8},{9,1},{1,5},{5,13},{13,9},{10,2},{2,6},{... | collective-permute-start | bytes 442376 | tf_op jit(solution)/shard_map/ppermute | solution.py:256
  33.4 1.4 %shard_map.39 = (f32[192,896]{1,0:T(8,128)S(1)}, f32[192,896]{1,0:T(8,128)S(1)}) custom-call(bf16[200,768]{1,0:T(8,128)(2,1)S(1)} %get-tuple-element.27.own.left, bf16[200,768]{1,0:T(8,128)(2,1)S(1)} %collective-permute-done.6.other.left, bf16[104,768]{1,0:T(8,128)(2,1)S(1)} %collective-permute-done.5.refs_0_, ...), custom_call_target="tpu_custom_call", output_to_operand_aliasing={{0}: (6, {}), {1}: (7, {})} | custom-call | tf_op jit(solution)/shard_map/pallas_call | solution.py:187
  34.8 2.6 %collective-permute-done.14.refs_1_ = bf16[96,768]{1,0:T(8,128)(2,1)S(1)} collective-permute-done((bf16[96,768]{1,0:T(8,128)(2,1)S(1)}, bf16[96,768]{1,0:T(8,128)(2,1)S(1)}, u32[]{:S(2)}, u32[]{:S(2)}) %collective-permute-start.14) | collective-permute-done | bytes 147488 | tf_op jit(solution)/shard_map/ppermute | solution.py:256
  37.4 0.0 collective-permute-done.11.refs_0_
  37.4 0.6 %shard_map.41 = f32[192,896]{1,0:T(8,128)S(1)} custom-call(bf16[200,768]{1,0:T(8,128)(2,1)S(1)} %collective-permute-done.6.other.left, bf16[104,768]{1,0:T(8,128)(2,1)S(1)} %collective-permute-done.11.refs_0_, bf16[96,768]{1,0:T(8,128)(2,1)S(1)} %collective-permute-done.14.refs_1_, ...), custom_call_target="tpu_custom_call", output_to_operand_aliasing={{}: (3, {})} | custom-call | tf_op jit(solution)/shard_map/pallas_call | solution.py:187
  38.0 0.1 collective-permute-start.15
  38.1 0.6 %shard_map.40.mine = f32[192,896]{1,0:T(8,128)S(1)} custom-call(bf16[200,768]{1,0:T(8,128)(2,1)S(1)} %get-tuple-element.27.own.left, bf16[104,768]{1,0:T(8,128)(2,1)S(1)} %collective-permute-done.11.refs_0_, bf16[96,768]{1,0:T(8,128)(2,1)S(1)} %collective-permute-done.14.refs_1_, ...), custom_call_target="tpu_custom_call", output_to_operand_aliasing={{}: (3, {})} | custom-call | tf_op jit(solution)/shard_map/pallas_call | solution.py:187
  38.7 1.5 %collective-permute-done.15.theirs = f32[192,896]{1,0:T(8,128)S(1)} collective-permute-done((f32[192,896]{1,0:T(8,128)S(1)}, f32[192,896]{1,0:T(8,128)S(1)}, u32[]{:S(2)}, u32[]{:S(2)}) %collective-permute-start.15) | collective-permute-done | bytes 688160 | tf_op jit(solution)/shard_map/ppermute | solution.py:262
  40.3 0.8 %shard_map.42 = bf16[192,768]{1,0:T(8,128)(2,1)} custom-call(f32[192,896]{1,0:T(8,128)S(1)} %shard_map.40.mine, f32[192,896]{1,0:T(8,128)S(1)} %collective-permute-done.15.theirs), custom_call_target="tpu_custom_call" | custom-call | tf_op jit(solution)/shard_map/pallas_call | solution.py:187
Async XLA Ops:
  0.0 0.7 %copy-start.2 = (s32[192]{0:T(256)S(1)}, s32[192]{0:T(256)}, u32[]{:S(2)}) copy-start(s32[192]{0:T(256)} %param.5) | copy-start | bytes 2308
  0.0 0.7 %copy-start.1 = (s32[192,1]{0,1:T(1,128)S(1)}, s32[192,1]{0,1:T(1,128)}, u32[]{:S(2)}) copy-start(s32[192,1]{0,1:T(1,128)} %param.4) | copy-start | bytes 2308
  0.7 1.0 %copy-start = (bf16[192,768]{1,0:T(8,128)(2,1)S(1)}, bf16[192,768]{1,0:T(8,128)(2,1)}, u32[]{:S(2)}) copy-start(bf16[192,768]{1,0:T(8,128)(2,1)} %rows.1) | copy-start | bytes 884740
  2.1 9.0 %collective-permute-start = (bf16[104,768]{1,0:T(8,128)(2,1)S(1)}, bf16[104,768]{1,0:T(8,128)(2,1)S(1)}, u32[]{:S(2)}, u32[]{:S(2)}) collective-permute-start(bf16[104,768]{1,0:T(8,128)(2,1)S(1)} %get-tuple-element.28), channel_id=1, source_target_pairs={{8,0},{0,4},{4,12},{12,8},{9,1},{1,5},{5,13},{13,9},{10,2},{2,6},{... | collective-permute-start | bytes 479240 | tf_op jit(solution)/shard_map/ppermute | solution.py:256
  5.2 6.0 %collective-permute-start.1 = (bf16[104,768]{1,0:T(8,128)(2,1)S(1)}, bf16[104,768]{1,0:T(8,128)(2,1)S(1)}, u32[]{:S(2)}, u32[]{:S(2)}) collective-permute-start(bf16[104,768]{1,0:T(8,128)(2,1)S(1)} %get-tuple-element.28), channel_id=1, source_target_pairs={{0,2},{2,0},{1,3},{3,1},{4,6},{6,4},{5,7},{7,5},{8,10},{10,8},{9,1... | collective-permute-start | bytes 479240 | tf_op jit(solution)/shard_map/ppermute | solution.py:259
  6.7 9.6 %collective-permute-start.7 = (bf16[96,768]{1,0:T(8,128)(2,1)S(1)}, bf16[96,768]{1,0:T(8,128)(2,1)S(1)}, u32[]{:S(2)}, u32[]{:S(2)}) collective-permute-start(bf16[96,768]{1,0:T(8,128)(2,1)S(1)} %get-tuple-element.33), channel_id=1, source_target_pairs={{8,0},{0,4},{4,12},{12,8},{9,1},{1,5},{5,13},{13,9},{10,2},{2,6},{... | collective-permute-start | bytes 442376 | tf_op jit(solution)/shard_map/ppermute | solution.py:256
  9.3 7.0 %collective-permute-start.8 = (bf16[96,768]{1,0:T(8,128)(2,1)S(1)}, bf16[96,768]{1,0:T(8,128)(2,1)S(1)}, u32[]{:S(2)}, u32[]{:S(2)}) collective-permute-start(bf16[96,768]{1,0:T(8,128)(2,1)S(1)} %get-tuple-element.33), channel_id=1, source_target_pairs={{0,2},{2,0},{1,3},{3,1},{4,6},{6,4},{5,7},{7,5},{8,10},{10,8},{9,1... | collective-permute-start | bytes 442376 | tf_op jit(solution)/shard_map/ppermute | solution.py:259
  11.2 7.5 %collective-permute-start.2 = (bf16[104,768]{1,0:T(8,128)(2,1)S(1)}, bf16[104,768]{1,0:T(8,128)(2,1)S(1)}, u32[]{:S(2)}, u32[]{:S(2)}) collective-permute-start(bf16[104,768]{1,0:T(8,128)(2,1)S(1)} %collective-permute-done.refs_4_), channel_id=1, source_target_pairs={{8,0},{0,4},{4,12},{12,8},{9,1},{1,5},{5,13},{13,9},{10,2},{2,6},{... | collective-permute-start | bytes 479240 | tf_op jit(solution)/shard_map/ppermute | solution.py:256
  14.8 5.9 %collective-permute-start.3 = (bf16[104,768]{1,0:T(8,128)(2,1)S(1)}, bf16[104,768]{1,0:T(8,128)(2,1)S(1)}, u32[]{:S(2)}, u32[]{:S(2)}) collective-permute-start(bf16[104,768]{1,0:T(8,128)(2,1)S(1)} %collective-permute-done.refs_4_), channel_id=1, source_target_pairs={{0,2},{2,0},{1,3},{3,1},{4,6},{6,4},{5,7},{7,5},{8,10},{10,8},{9,1... | collective-permute-start | bytes 479240 | tf_op jit(solution)/shard_map/ppermute | solution.py:259
  16.3 10.9 %collective-permute-start.6 = (bf16[200,768]{1,0:T(8,128)(2,1)S(1)}, bf16[200,768]{1,0:T(8,128)(2,1)S(1)}, u32[]{:S(2)}, u32[]{:S(2)}) collective-permute-start(bf16[200,768]{1,0:T(8,128)(2,1)S(1)} %get-tuple-element.27.own.left), channel_id=1, source_target_pairs={{0,1},{1,0},{2,3},{3,2},{4,5},{5,4},{6,7},{7,6},{8,9},{9,8},{10,11... | collective-permute-start | bytes 921608 | tf_op jit(solution)/shard_map/ppermute | solution.py:262
  16.4 7.8 %collective-permute-start.10 = (bf16[96,768]{1,0:T(8,128)(2,1)S(1)}, bf16[96,768]{1,0:T(8,128)(2,1)S(1)}, u32[]{:S(2)}, u32[]{:S(2)}) collective-permute-start(bf16[96,768]{1,0:T(8,128)(2,1)S(1)} %collective-permute-done.7.refs_5_), channel_id=1, source_target_pairs={{0,2},{2,0},{1,3},{3,1},{4,6},{6,4},{5,7},{7,5},{8,10},{10,8},{9,1... | collective-permute-start | bytes 442376 | tf_op jit(solution)/shard_map/ppermute | solution.py:259
  17.0 7.6 %collective-permute-start.9 = (bf16[96,768]{1,0:T(8,128)(2,1)S(1)}, bf16[96,768]{1,0:T(8,128)(2,1)S(1)}, u32[]{:S(2)}, u32[]{:S(2)}) collective-permute-start(bf16[96,768]{1,0:T(8,128)(2,1)S(1)} %collective-permute-done.7.refs_5_), channel_id=1, source_target_pairs={{8,0},{0,4},{4,12},{12,8},{9,1},{1,5},{5,13},{13,9},{10,2},{2,6},{... | collective-permute-start | bytes 442376 | tf_op jit(solution)/shard_map/ppermute | solution.py:256
  20.8 9.7 %collective-permute-start.4 = (bf16[104,768]{1,0:T(8,128)(2,1)S(1)}, bf16[104,768]{1,0:T(8,128)(2,1)S(1)}, u32[]{:S(2)}, u32[]{:S(2)}) collective-permute-start(bf16[104,768]{1,0:T(8,128)(2,1)S(1)} %collective-permute-done.2.refs_6_), channel_id=1, source_target_pairs={{8,0},{0,4},{4,12},{12,8},{9,1},{1,5},{5,13},{13,9},{10,2},{2,6},{... | collective-permute-start | bytes 479240 | tf_op jit(solution)/shard_map/ppermute | solution.py:256
  21.7 8.8 %collective-permute-start.5 = (bf16[104,768]{1,0:T(8,128)(2,1)S(1)}, bf16[104,768]{1,0:T(8,128)(2,1)S(1)}, u32[]{:S(2)}, u32[]{:S(2)}) collective-permute-start(bf16[104,768]{1,0:T(8,128)(2,1)S(1)} %collective-permute-done.2.refs_6_), channel_id=1, source_target_pairs={{0,2},{2,0},{1,3},{3,1},{4,6},{6,4},{5,7},{7,5},{8,10},{10,8},{9,1... | collective-permute-start | bytes 479240 | tf_op jit(solution)/shard_map/ppermute | solution.py:259
  24.5 6.3 %collective-permute-start.12 = (bf16[96,768]{1,0:T(8,128)(2,1)S(1)}, bf16[96,768]{1,0:T(8,128)(2,1)S(1)}, u32[]{:S(2)}, u32[]{:S(2)}) collective-permute-start(bf16[96,768]{1,0:T(8,128)(2,1)S(1)} %collective-permute-done.9.refs_7_), channel_id=1, source_target_pairs={{8,0},{0,4},{4,12},{12,8},{9,1},{1,5},{5,13},{13,9},{10,2},{2,6},{... | collective-permute-start | bytes 442376 | tf_op jit(solution)/shard_map/ppermute | solution.py:256
  25.4 5.9 %collective-permute-start.13 = (bf16[96,768]{1,0:T(8,128)(2,1)S(1)}, bf16[96,768]{1,0:T(8,128)(2,1)S(1)}, u32[]{:S(2)}, u32[]{:S(2)}) collective-permute-start(bf16[96,768]{1,0:T(8,128)(2,1)S(1)} %collective-permute-done.9.refs_7_), channel_id=1, source_target_pairs={{0,2},{2,0},{1,3},{3,1},{4,6},{6,4},{5,7},{7,5},{8,10},{10,8},{9,1... | collective-permute-start | bytes 442376 | tf_op jit(solution)/shard_map/ppermute | solution.py:259
  30.5 6.9 %collective-permute-start.11 = (bf16[104,768]{1,0:T(8,128)(2,1)S(1)}, bf16[104,768]{1,0:T(8,128)(2,1)S(1)}, u32[]{:S(2)}, u32[]{:S(2)}) collective-permute-start(bf16[104,768]{1,0:T(8,128)(2,1)S(1)} %collective-permute-done.4.refs_2_), channel_id=1, source_target_pairs={{0,2},{2,0},{1,3},{3,1},{4,6},{6,4},{5,7},{7,5},{8,10},{10,8},{9,1... | collective-permute-start | bytes 479240 | tf_op jit(solution)/shard_map/ppermute | solution.py:259
  31.4 6.0 %collective-permute-start.14 = (bf16[96,768]{1,0:T(8,128)(2,1)S(1)}, bf16[96,768]{1,0:T(8,128)(2,1)S(1)}, u32[]{:S(2)}, u32[]{:S(2)}) collective-permute-start(bf16[96,768]{1,0:T(8,128)(2,1)S(1)} %collective-permute-done.13.refs_1_), channel_id=1, source_target_pairs={{8,0},{0,4},{4,12},{12,8},{9,1},{1,5},{5,13},{13,9},{10,2},{2,6},{... | collective-permute-start | bytes 442376 | tf_op jit(solution)/shard_map/ppermute | solution.py:256
  38.0 2.2 %collective-permute-start.15 = (f32[192,896]{1,0:T(8,128)S(1)}, f32[192,896]{1,0:T(8,128)S(1)}, u32[]{:S(2)}, u32[]{:S(2)}) collective-permute-start(f32[192,896]{1,0:T(8,128)S(1)} %shard_map.41), channel_id=1, source_target_pairs={{0,1},{1,0},{2,3},{3,2},{4,5},{5,4},{6,7},{7,6},{8,9},{9,8},{10,11... | collective-permute-start | bytes 2064392 | tf_op jit(solution)/shard_map/ppermute | solution.py:262

commit v4 on v3

--- a/solution.py
+++ b/solution.py
@@ -264,16 +264,20 @@
     whole, first, second = pack(embeddings, group_of, cluster_id)
     along_by = [(first, second)]
     across_by = []
+    other = other_core(whole)
+    in_flight = [other]
     for s in range(1, n_blk):
-        moved = [along(piece) for piece in along_by[-1]]
-        swapped = [across(piece) for piece in along_by[-1]]
-        pairs = [together(m, w) for m, w in zip(moved, swapped)]
-        along_by.append(tuple(pair[0] for pair in pairs))
-        across_by.append(tuple(pair[1] for pair in pairs))
-    left = (whole, other_core(whole))
+        pieces = along_by.pop()
+        if s > 1:
+            pieces = tuple(together(piece, in_flight.pop(0))[0] for piece in pieces)
+        along_by += [pieces, tuple(along(piece) for piece in pieces)]
+        across_by.append(tuple(across(piece) for piece in pieces))
+        in_flight += across_by[-1]
+    left = (whole, other)
     total = start_both(left, across_by[:-1] + along_by[1:-1])
-    far_first, mine, theirs = together(along_by[-1][0], *total)
-    last = (across(far_first), along(across_by[-1][1]))
+    far_first, _, mine, theirs = together(along_by[-1][0], across_by[-1][0], *total)
+    near_second, _ = together(across_by[-1][1], along_by[-1][1])
+    last = (across(far_first), along(near_second))
     mine, theirs = add_both(left, [across_by[-1], along_by[-1]], (mine, theirs))
     theirs = other_core(add_one(left[1], [last], theirs))
     mine = add_one(left[0], [last], mine)

time: 41.3 us -> 43.8 us (1.061)
  starting transfers between devices: 23.6 us -> 26.2 us
    ppermute x7, starting transfers between devices: 14.8 us -> 17.1 us  [along(): lax.ppermute(rows, 'blk', [(order[i - 1], order[i]) for i in range(n_blk)])]
    ppermute x7, waiting for transfers between devices: 4.39 us -> 3.62 us  [along(): lax.ppermute(rows, 'blk', [(order[i - 1], order[i]) for i in range(n_blk)])]
    ppermute x7, waiting for transfers between devices: 2.68 us -> 3.31 us  [across(): return lax.ppermute(rows, 'sub', swap)]
    ppermute x2, starting transfers between devices: 0.07 us -> 0.59 us  [other_core(): return lax.ppermute(rows, 'pair', swap)]
  transfers between devices with their start and end apart: 16 -> 16, of which waited for: 6 -> 5; matrix products, arithmetic and copies ran while one was open for 0% -> 0% of each run, Pallas kernels for 13% -> 12%
where the time goes in v4:
time: 43.8 us; the launch traced here: 43.6 us
  starting transfers between devices  26.2 us (60%)
  waiting for transfers between devices  8.45 us (19%)
  Pallas kernels  7.2 us (16%)
  local copies, waits for them, and re-layouts  1.65 us (4%)
    ppermute x7, starting transfers between devices, along(): lax.ppermute(rows, 'blk', [(order[i - 1], order[i]) for i in range(n_blk)])  17.1 us
    ppermute x7, starting transfers between devices, across(): return lax.ppermute(rows, 'sub', swap)  8.59 us
    pallas_call x5, Pallas kernels, call(): pl.pallas_call(kernel, out_shape=shapes, in_specs=whole_in_vmem(len(args)...  6.72 us
    ppermute x7, waiting for transfers between devices, along(): lax.ppermute(rows, 'blk', [(order[i - 1], order[i]) for i in range(n_blk)])  3.62 us
    ppermute x7, waiting for transfers between devices, across(): return lax.ppermute(rows, 'sub', swap)  3.31 us
    unnamed x6, local copies, waits for them, and re-layouts  1.65 us
    ppermute x2, waiting for transfers between devices, other_core(): return lax.ppermute(rows, 'pair', swap)  1.52 us
  transfers between devices with their start and end apart: 16, of which 5 were waited for; matrix products, arithmetic and copies ran while one was open for 0% of the time, Pallas kernels for 12%

profile of v4, /device:TPU:0, one launch (start us, length us, event | category | flops | bytes accessed | tf_op | source)
XLA Modules:
  0.0 43.6 jit_solution(12471152240786649430)
XLA Ops:
  0.0 0.0 copy-start.2
  0.0 0.0 copy-start.1
  0.0 0.7 %copy-done.2 = s32[192]{0:T(256)S(1)} copy-done((s32[192]{0:T(256)S(1)}, s32[192]{0:T(256)}, u32[]{:S(2)}) %copy-start.2) | copy-done | bytes 792
  0.7 0.0 copy-done.1
  0.7 0.0 copy-start
  0.7 1.0 %copy-done = bf16[192,768]{1,0:T(8,128)(2,1)S(1)} copy-done((bf16[192,768]{1,0:T(8,128)(2,1)S(1)}, bf16[192,768]{1,0:T(8,128)(2,1)}, u32[]{:S(2)}) %copy-start) | copy-done | bytes 294936
  1.7 0.5 %shard_map.37 = (bf16[200,768]{1,0:T(8,128)(2,1)S(1)}, bf16[104,768]{1,0:T(8,128)(2,1)S(1)}, bf16[96,768]{1,0:T(8,128)(2,1)S(1)}) custom-call(bf16[192,768]{1,0:T(8,128)(2,1)S(1)} %copy-done, s32[1,192]{1,0:T(1,128)S(1)} %bitcast.2, s32[1,192]{1,0:T(1,128)S(1)} %bitcast.3), custom_call_target="tpu_custom_call" | custom-call | tf_op jit(solution)/shard_map/pallas_call | solution.py:201
  2.1 0.5 %collective-permute-start.1 = (bf16[200,768]{1,0:T(8,128)(2,1)S(1)}, bf16[200,768]{1,0:T(8,128)(2,1)S(1)}, u32[]{:S(2)}, u32[]{:S(2)}) collective-permute-start(bf16[200,768]{1,0:T(8,128)(2,1)S(1)} %get-tuple-element.20.own.left), channel_id=1, source_target_pairs={{0,1},{1,0},{2,3},{3,2},{4,5},{5,4},{6,7},{7,6},{8,9},{9,8},{10,11... | collective-permute-start | bytes 921608 | tf_op jit(solution)/shard_map/ppermute | solution.py:262
  2.7 2.6 %collective-permute-start = (bf16[104,768]{1,0:T(8,128)(2,1)S(1)}, bf16[104,768]{1,0:T(8,128)(2,1)S(1)}, u32[]{:S(2)}, u32[]{:S(2)}) collective-permute-start(bf16[104,768]{1,0:T(8,128)(2,1)S(1)} %get-tuple-element.21), channel_id=1, source_target_pairs={{8,0},{0,4},{4,12},{12,8},{9,1},{1,5},{5,13},{13,9},{10,2},{2,6},{... | collective-permute-start | bytes 479240 | tf_op jit(solution)/shard_map/ppermute | solution.py:256
  5.3 1.5 %collective-permute-start.6 = (bf16[104,768]{1,0:T(8,128)(2,1)S(1)}, bf16[104,768]{1,0:T(8,128)(2,1)S(1)}, u32[]{:S(2)}, u32[]{:S(2)}) collective-permute-start(bf16[104,768]{1,0:T(8,128)(2,1)S(1)} %get-tuple-element.21), channel_id=1, source_target_pairs={{0,2},{2,0},{1,3},{3,1},{4,6},{6,4},{5,7},{7,5},{8,10},{10,8},{9,1... | collective-permute-start | bytes 479240 | tf_op jit(solution)/shard_map/ppermute | solution.py:259
  6.8 2.6 %collective-permute-start.8 = (bf16[96,768]{1,0:T(8,128)(2,1)S(1)}, bf16[96,768]{1,0:T(8,128)(2,1)S(1)}, u32[]{:S(2)}, u32[]{:S(2)}) collective-permute-start(bf16[96,768]{1,0:T(8,128)(2,1)S(1)} %get-tuple-element.23), channel_id=1, source_target_pairs={{8,0},{0,4},{4,12},{12,8},{9,1},{1,5},{5,13},{13,9},{10,2},{2,6},{... | collective-permute-start | bytes 442376 | tf_op jit(solution)/shard_map/ppermute | solution.py:256
  9.4 1.9 %collective-permute-done.refs_4_ = bf16[104,768]{1,0:T(8,128)(2,1)S(1)} collective-permute-done((bf16[104,768]{1,0:T(8,128)(2,1)S(1)}, bf16[104,768]{1,0:T(8,128)(2,1)S(1)}, u32[]{:S(2)}, u32[]{:S(2)}) %collective-permute-start) | collective-permute-done | bytes 159776 | tf_op jit(solution)/shard_map/ppermute | solution.py:256
  11.3 0.0 collective-permute-done.1.other.left
  11.3 1.0 %collective-permute-start.2 = (bf16[104,768]{1,0:T(8,128)(2,1)S(1)}, bf16[104,768]{1,0:T(8,128)(2,1)S(1)}, u32[]{:S(2)}, u32[]{:S(2)}) collective-permute-start(bf16[104,768]{1,0:T(8,128)(2,1)S(1)} %collective-permute-done.refs_4_), channel_id=1, source_target_pairs={{8,0},{0,4},{4,12},{12,8},{9,1},{1,5},{5,13},{13,9},{10,2},{2,6},{... | collective-permute-start | bytes 479240 | tf_op jit(solution)/shard_map/ppermute | solution.py:256
  12.3 1.5 %collective-permute-start.3 = (bf16[96,768]{1,0:T(8,128)(2,1)S(1)}, bf16[96,768]{1,0:T(8,128)(2,1)S(1)}, u32[]{:S(2)}, u32[]{:S(2)}) collective-permute-start(bf16[96,768]{1,0:T(8,128)(2,1)S(1)} %get-tuple-element.23), channel_id=1, source_target_pairs={{0,2},{2,0},{1,3},{3,1},{4,6},{6,4},{5,7},{7,5},{8,10},{10,8},{9,1... | collective-permute-start | bytes 442376 | tf_op jit(solution)/shard_map/ppermute | solution.py:259
  13.8 0.5 %collective-permute-start.7 = (bf16[104,768]{1,0:T(8,128)(2,1)S(1)}, bf16[104,768]{1,0:T(8,128)(2,1)S(1)}, u32[]{:S(2)}, u32[]{:S(2)}) collective-permute-start(bf16[104,768]{1,0:T(8,128)(2,1)S(1)} %collective-permute-done.refs_4_), channel_id=1, source_target_pairs={{0,2},{2,0},{1,3},{3,1},{4,6},{6,4},{5,7},{7,5},{8,10},{10,8},{9,1... | collective-permute-start | bytes 479240 | tf_op jit(solution)/shard_map/ppermute | solution.py:259
  14.3 0.0 collective-permute-done.8.refs_5_
  14.4 0.0 collective-permute-done.6.refs_0_
  14.4 3.4 %collective-permute-start.10 = (bf16[96,768]{1,0:T(8,128)(2,1)S(1)}, bf16[96,768]{1,0:T(8,128)(2,1)S(1)}, u32[]{:S(2)}, u32[]{:S(2)}) collective-permute-start(bf16[96,768]{1,0:T(8,128)(2,1)S(1)} %collective-permute-done.8.refs_5_), channel_id=1, source_target_pairs={{8,0},{0,4},{4,12},{12,8},{9,1},{1,5},{5,13},{13,9},{10,2},{2,6},{... | collective-permute-start | bytes 442376 | tf_op jit(solution)/shard_map/ppermute | solution.py:256
  17.7 1.0 %collective-permute-done.3.refs_1_ = bf16[96,768]{1,0:T(8,128)(2,1)S(1)} collective-permute-done((bf16[96,768]{1,0:T(8,128)(2,1)S(1)}, bf16[96,768]{1,0:T(8,128)(2,1)S(1)}, u32[]{:S(2)}, u32[]{:S(2)}) %collective-permute-start.3) | collective-permute-done | bytes 147488 | tf_op jit(solution)/shard_map/ppermute | solution.py:259
  18.7 0.0 collective-permute-done.2.refs_6_
  18.7 3.4 %collective-permute-start.4 = (bf16[104,768]{1,0:T(8,128)(2,1)S(1)}, bf16[104,768]{1,0:T(8,128)(2,1)S(1)}, u32[]{:S(2)}, u32[]{:S(2)}) collective-permute-start(bf16[104,768]{1,0:T(8,128)(2,1)S(1)} %collective-permute-done.2.refs_6_), channel_id=1, source_target_pairs={{8,0},{0,4},{4,12},{12,8},{9,1},{1,5},{5,13},{13,9},{10,2},{2,6},{... | collective-permute-start | bytes 479240 | tf_op jit(solution)/shard_map/ppermute | solution.py:256
  22.1 1.5 %collective-permute-start.5 = (bf16[104,768]{1,0:T(8,128)(2,1)S(1)}, bf16[104,768]{1,0:T(8,128)(2,1)S(1)}, u32[]{:S(2)}, u32[]{:S(2)}) collective-permute-start(bf16[104,768]{1,0:T(8,128)(2,1)S(1)} %collective-permute-done.2.refs_6_), channel_id=1, source_target_pairs={{0,2},{2,0},{1,3},{3,1},{4,6},{6,4},{5,7},{7,5},{8,10},{10,8},{9,1... | collective-permute-start | bytes 479240 | tf_op jit(solution)/shard_map/ppermute | solution.py:259
  23.6 0.5 %collective-permute-start.9 = (bf16[96,768]{1,0:T(8,128)(2,1)S(1)}, bf16[96,768]{1,0:T(8,128)(2,1)S(1)}, u32[]{:S(2)}, u32[]{:S(2)}) collective-permute-start(bf16[96,768]{1,0:T(8,128)(2,1)S(1)} %collective-permute-done.8.refs_5_), channel_id=1, source_target_pairs={{0,2},{2,0},{1,3},{3,1},{4,6},{6,4},{5,7},{7,5},{8,10},{10,8},{9,1... | collective-permute-start | bytes 442376 | tf_op jit(solution)/shard_map/ppermute | solution.py:259
  24.1 0.0 collective-permute-done.10.refs_7_
  24.1 0.0 collective-permute-done.7.refs_2_
  24.1 1.5 %collective-permute-start.12 = (bf16[96,768]{1,0:T(8,128)(2,1)S(1)}, bf16[96,768]{1,0:T(8,128)(2,1)S(1)}, u32[]{:S(2)}, u32[]{:S(2)}) collective-permute-start(bf16[96,768]{1,0:T(8,128)(2,1)S(1)} %collective-permute-done.10.refs_7_), channel_id=1, source_target_pairs={{0,2},{2,0},{1,3},{3,1},{4,6},{6,4},{5,7},{7,5},{8,10},{10,8},{9,1... | collective-permute-start | bytes 442376 | tf_op jit(solution)/shard_map/ppermute | solution.py:259
  25.6 1.2 %collective-permute-start.13 = (bf16[96,768]{1,0:T(8,128)(2,1)S(1)}, bf16[96,768]{1,0:T(8,128)(2,1)S(1)}, u32[]{:S(2)}, u32[]{:S(2)}) collective-permute-start(bf16[96,768]{1,0:T(8,128)(2,1)S(1)} %collective-permute-done.10.refs_7_), channel_id=1, source_target_pairs={{8,0},{0,4},{4,12},{12,8},{9,1},{1,5},{5,13},{13,9},{10,2},{2,6},{... | collective-permute-start | bytes 442376 | tf_op jit(solution)/shard_map/ppermute | solution.py:256
  26.8 2.3 %collective-permute-done.9.refs_3_ = bf16[96,768]{1,0:T(8,128)(2,1)S(1)} collective-permute-done((bf16[96,768]{1,0:T(8,128)(2,1)S(1)}, bf16[96,768]{1,0:T(8,128)(2,1)S(1)}, u32[]{:S(2)}, u32[]{:S(2)}) %collective-permute-start.9) | collective-permute-done | bytes 147488 | tf_op jit(solution)/shard_map/ppermute | solution.py:259
  29.1 3.2 %shard_map.38 = (f32[192,896]{1,0:T(8,128)S(1)}, f32[192,896]{1,0:T(8,128)S(1)}) custom-call(bf16[200,768]{1,0:T(8,128)(2,1)S(1)} %get-tuple-element.20.own.left, bf16[200,768]{1,0:T(8,128)(2,1)S(1)} %collective-permute-done.1.other.left, bf16[104,768]{1,0:T(8,128)(2,1)S(1)} %collective-permute-done.6.refs_0_, ...), custom_call_target="tpu_custom_call" | custom-call | tf_op jit(solution)/shard_map/pallas_call | solution.py:187
  32.3 0.0 collective-permute-done.4.refs_2_
  32.3 0.0 collective-permute-done.5.refs_0_
  32.3 1.6 %collective-permute-start.11 = (bf16[104,768]{1,0:T(8,128)(2,1)S(1)}, bf16[104,768]{1,0:T(8,128)(2,1)S(1)}, u32[]{:S(2)}, u32[]{:S(2)}) collective-permute-start(bf16[104,768]{1,0:T(8,128)(2,1)S(1)} %collective-permute-done.4.refs_2_), channel_id=1, source_target_pairs={{0,2},{2,0},{1,3},{3,1},{4,6},{6,4},{5,7},{7,5},{8,10},{10,8},{9,1... | collective-permute-start | bytes 479240 | tf_op jit(solution)/shard_map/ppermute | solution.py:259
  33.9 0.0 collective-permute-done.12.refs_1_
  33.9 0.0 collective-permute-done.13.refs_3_
  33.9 2.9 %collective-permute-start.14 = (bf16[96,768]{1,0:T(8,128)(2,1)S(1)}, bf16[96,768]{1,0:T(8,128)(2,1)S(1)}, u32[]{:S(2)}, u32[]{:S(2)}) collective-permute-start(bf16[96,768]{1,0:T(8,128)(2,1)S(1)} %collective-permute-done.12.refs_1_), channel_id=1, source_target_pairs={{8,0},{0,4},{4,12},{12,8},{9,1},{1,5},{5,13},{13,9},{10,2},{2,6},{... | collective-permute-start | bytes 442376 | tf_op jit(solution)/shard_map/ppermute | solution.py:256
  36.8 1.5 %shard_map.39 = (f32[192,896]{1,0:T(8,128)S(1)}, f32[192,896]{1,0:T(8,128)S(1)}) custom-call(bf16[200,768]{1,0:T(8,128)(2,1)S(1)} %get-tuple-element.20.own.left, bf16[200,768]{1,0:T(8,128)(2,1)S(1)} %collective-permute-done.1.other.left, bf16[104,768]{1,0:T(8,128)(2,1)S(1)} %collective-permute-done.5.refs_0_, ...), custom_call_target="tpu_custom_call", output_to_operand_aliasing={{0}: (6, {}), {1}: (7, {})} | custom-call | tf_op jit(solution)/shard_map/pallas_call | solution.py:187
  38.2 1.7 %collective-permute-done.14.refs_1_ = bf16[96,768]{1,0:T(8,128)(2,1)S(1)} collective-permute-done((bf16[96,768]{1,0:T(8,128)(2,1)S(1)}, bf16[96,768]{1,0:T(8,128)(2,1)S(1)}, u32[]{:S(2)}, u32[]{:S(2)}) %collective-permute-start.14) | collective-permute-done | bytes 147488 | tf_op jit(solution)/shard_map/ppermute | solution.py:256
  39.9 0.0 collective-permute-done.11.refs_0_
  39.9 0.6 %shard_map.41 = f32[192,896]{1,0:T(8,128)S(1)} custom-call(bf16[200,768]{1,0:T(8,128)(2,1)S(1)} %collective-permute-done.1.other.left, bf16[104,768]{1,0:T(8,128)(2,1)S(1)} %collective-permute-done.11.refs_0_, bf16[96,768]{1,0:T(8,128)(2,1)S(1)} %collective-permute-done.14.refs_1_, ...), custom_call_target="tpu_custom_call", output_to_operand_aliasing={{}: (3, {})} | custom-call | tf_op jit(solution)/shard_map/pallas_call | solution.py:187
  40.6 0.1 collective-permute-start.15
  40.6 0.6 %shard_map.40.mine = f32[192,896]{1,0:T(8,128)S(1)} custom-call(bf16[200,768]{1,0:T(8,128)(2,1)S(1)} %get-tuple-element.20.own.left, bf16[104,768]{1,0:T(8,128)(2,1)S(1)} %collective-permute-done.11.refs_0_, bf16[96,768]{1,0:T(8,128)(2,1)S(1)} %collective-permute-done.14.refs_1_, ...), custom_call_target="tpu_custom_call", output_to_operand_aliasing={{}: (3, {})} | custom-call | tf_op jit(solution)/shard_map/pallas_call | solution.py:187
  41.2 1.5 %collective-permute-done.15.theirs = f32[192,896]{1,0:T(8,128)S(1)} collective-permute-done((f32[192,896]{1,0:T(8,128)S(1)}, f32[192,896]{1,0:T(8,128)S(1)}, u32[]{:S(2)}, u32[]{:S(2)}) %collective-permute-start.15) | collective-permute-done | bytes 688160 | tf_op jit(solution)/shard_map/ppermute | solution.py:262
  42.8 0.8 %shard_map.42 = bf16[192,768]{1,0:T(8,128)(2,1)} custom-call(f32[192,896]{1,0:T(8,128)S(1)} %shard_map.40.mine, f32[192,896]{1,0:T(8,128)S(1)} %collective-permute-done.15.theirs), custom_call_target="tpu_custom_call" | custom-call | tf_op jit(solution)/shard_map/pallas_call | solution.py:187
Async XLA Ops:
  0.0 0.7 %copy-start.2 = (s32[192]{0:T(256)S(1)}, s32[192]{0:T(256)}, u32[]{:S(2)}) copy-start(s32[192]{0:T(256)} %param.5) | copy-start | bytes 2308
  0.0 0.7 %copy-start.1 = (s32[192,1]{0,1:T(1,128)S(1)}, s32[192,1]{0,1:T(1,128)}, u32[]{:S(2)}) copy-start(s32[192,1]{0,1:T(1,128)} %param.4) | copy-start | bytes 2308
  0.7 1.0 %copy-start = (bf16[192,768]{1,0:T(8,128)(2,1)S(1)}, bf16[192,768]{1,0:T(8,128)(2,1)}, u32[]{:S(2)}) copy-start(bf16[192,768]{1,0:T(8,128)(2,1)} %rows.1) | copy-start | bytes 884740
  2.1 9.1 %collective-permute-start.1 = (bf16[200,768]{1,0:T(8,128)(2,1)S(1)}, bf16[200,768]{1,0:T(8,128)(2,1)S(1)}, u32[]{:S(2)}, u32[]{:S(2)}) collective-permute-start(bf16[200,768]{1,0:T(8,128)(2,1)S(1)} %get-tuple-element.20.own.left), channel_id=1, source_target_pairs={{0,1},{1,0},{2,3},{3,2},{4,5},{5,4},{6,7},{7,6},{8,9},{9,8},{10,11... | collective-permute-start | bytes 921608 | tf_op jit(solution)/shard_map/ppermute | solution.py:262
  2.7 8.6 %collective-permute-start = (bf16[104,768]{1,0:T(8,128)(2,1)S(1)}, bf16[104,768]{1,0:T(8,128)(2,1)S(1)}, u32[]{:S(2)}, u32[]{:S(2)}) collective-permute-start(bf16[104,768]{1,0:T(8,128)(2,1)S(1)} %get-tuple-element.21), channel_id=1, source_target_pairs={{8,0},{0,4},{4,12},{12,8},{9,1},{1,5},{5,13},{13,9},{10,2},{2,6},{... | collective-permute-start | bytes 479240 | tf_op jit(solution)/shard_map/ppermute | solution.py:256
  5.3 9.1 %collective-permute-start.6 = (bf16[104,768]{1,0:T(8,128)(2,1)S(1)}, bf16[104,768]{1,0:T(8,128)(2,1)S(1)}, u32[]{:S(2)}, u32[]{:S(2)}) collective-permute-start(bf16[104,768]{1,0:T(8,128)(2,1)S(1)} %get-tuple-element.21), channel_id=1, source_target_pairs={{0,2},{2,0},{1,3},{3,1},{4,6},{6,4},{5,7},{7,5},{8,10},{10,8},{9,1... | collective-permute-start | bytes 479240 | tf_op jit(solution)/shard_map/ppermute | solution.py:259
  6.8 7.6 %collective-permute-start.8 = (bf16[96,768]{1,0:T(8,128)(2,1)S(1)}, bf16[96,768]{1,0:T(8,128)(2,1)S(1)}, u32[]{:S(2)}, u32[]{:S(2)}) collective-permute-start(bf16[96,768]{1,0:T(8,128)(2,1)S(1)} %get-tuple-element.23), channel_id=1, source_target_pairs={{8,0},{0,4},{4,12},{12,8},{9,1},{1,5},{5,13},{13,9},{10,2},{2,6},{... | collective-permute-start | bytes 442376 | tf_op jit(solution)/shard_map/ppermute | solution.py:256
  11.3 7.4 %collective-permute-start.2 = (bf16[104,768]{1,0:T(8,128)(2,1)S(1)}, bf16[104,768]{1,0:T(8,128)(2,1)S(1)}, u32[]{:S(2)}, u32[]{:S(2)}) collective-permute-start(bf16[104,768]{1,0:T(8,128)(2,1)S(1)} %collective-permute-done.refs_4_), channel_id=1, source_target_pairs={{8,0},{0,4},{4,12},{12,8},{9,1},{1,5},{5,13},{13,9},{10,2},{2,6},{... | collective-permute-start | bytes 479240 | tf_op jit(solution)/shard_map/ppermute | solution.py:256
  12.3 6.4 %collective-permute-start.3 = (bf16[96,768]{1,0:T(8,128)(2,1)S(1)}, bf16[96,768]{1,0:T(8,128)(2,1)S(1)}, u32[]{:S(2)}, u32[]{:S(2)}) collective-permute-start(bf16[96,768]{1,0:T(8,128)(2,1)S(1)} %get-tuple-element.23), channel_id=1, source_target_pairs={{0,2},{2,0},{1,3},{3,1},{4,6},{6,4},{5,7},{7,5},{8,10},{10,8},{9,1... | collective-permute-start | bytes 442376 | tf_op jit(solution)/shard_map/ppermute | solution.py:259
  13.8 10.3 %collective-permute-start.7 = (bf16[104,768]{1,0:T(8,128)(2,1)S(1)}, bf16[104,768]{1,0:T(8,128)(2,1)S(1)}, u32[]{:S(2)}, u32[]{:S(2)}) collective-permute-start(bf16[104,768]{1,0:T(8,128)(2,1)S(1)} %collective-permute-done.refs_4_), channel_id=1, source_target_pairs={{0,2},{2,0},{1,3},{3,1},{4,6},{6,4},{5,7},{7,5},{8,10},{10,8},{9,1... | collective-permute-start | bytes 479240 | tf_op jit(solution)/shard_map/ppermute | solution.py:259
  14.4 9.8 %collective-permute-start.10 = (bf16[96,768]{1,0:T(8,128)(2,1)S(1)}, bf16[96,768]{1,0:T(8,128)(2,1)S(1)}, u32[]{:S(2)}, u32[]{:S(2)}) collective-permute-start(bf16[96,768]{1,0:T(8,128)(2,1)S(1)} %collective-permute-done.8.refs_5_), channel_id=1, source_target_pairs={{8,0},{0,4},{4,12},{12,8},{9,1},{1,5},{5,13},{13,9},{10,2},{2,6},{... | collective-permute-start | bytes 442376 | tf_op jit(solution)/shard_map/ppermute | solution.py:256
  18.7 13.6 %collective-permute-start.4 = (bf16[104,768]{1,0:T(8,128)(2,1)S(1)}, bf16[104,768]{1,0:T(8,128)(2,1)S(1)}, u32[]{:S(2)}, u32[]{:S(2)}) collective-permute-start(bf16[104,768]{1,0:T(8,128)(2,1)S(1)} %collective-permute-done.2.refs_6_), channel_id=1, source_target_pairs={{8,0},{0,4},{4,12},{12,8},{9,1},{1,5},{5,13},{13,9},{10,2},{2,6},{... | collective-permute-start | bytes 479240 | tf_op jit(solution)/shard_map/ppermute | solution.py:256
  22.1 10.2 %collective-permute-start.5 = (bf16[104,768]{1,0:T(8,128)(2,1)S(1)}, bf16[104,768]{1,0:T(8,128)(2,1)S(1)}, u32[]{:S(2)}, u32[]{:S(2)}) collective-permute-start(bf16[104,768]{1,0:T(8,128)(2,1)S(1)} %collective-permute-done.2.refs_6_), channel_id=1, source_target_pairs={{0,2},{2,0},{1,3},{3,1},{4,6},{6,4},{5,7},{7,5},{8,10},{10,8},{9,1... | collective-permute-start | bytes 479240 | tf_op jit(solution)/shard_map/ppermute | solution.py:259
  23.6 5.5 %collective-permute-start.9 = (bf16[96,768]{1,0:T(8,128)(2,1)S(1)}, bf16[96,768]{1,0:T(8,128)(2,1)S(1)}, u32[]{:S(2)}, u32[]{:S(2)}) collective-permute-start(bf16[96,768]{1,0:T(8,128)(2,1)S(1)} %collective-permute-done.8.refs_5_), channel_id=1, source_target_pairs={{0,2},{2,0},{1,3},{3,1},{4,6},{6,4},{5,7},{7,5},{8,10},{10,8},{9,1... | collective-permute-start | bytes 442376 | tf_op jit(solution)/shard_map/ppermute | solution.py:259
  24.1 9.8 %collective-permute-start.12 = (bf16[96,768]{1,0:T(8,128)(2,1)S(1)}, bf16[96,768]{1,0:T(8,128)(2,1)S(1)}, u32[]{:S(2)}, u32[]{:S(2)}) collective-permute-start(bf16[96,768]{1,0:T(8,128)(2,1)S(1)} %collective-permute-done.10.refs_7_), channel_id=1, source_target_pairs={{0,2},{2,0},{1,3},{3,1},{4,6},{6,4},{5,7},{7,5},{8,10},{10,8},{9,1... | collective-permute-start | bytes 442376 | tf_op jit(solution)/shard_map/ppermute | solution.py:259
  25.6 8.3 %collective-permute-start.13 = (bf16[96,768]{1,0:T(8,128)(2,1)S(1)}, bf16[96,768]{1,0:T(8,128)(2,1)S(1)}, u32[]{:S(2)}, u32[]{:S(2)}) collective-permute-start(bf16[96,768]{1,0:T(8,128)(2,1)S(1)} %collective-permute-done.10.refs_7_), channel_id=1, source_target_pairs={{8,0},{0,4},{4,12},{12,8},{9,1},{1,5},{5,13},{13,9},{10,2},{2,6},{... | collective-permute-start | bytes 442376 | tf_op jit(solution)/shard_map/ppermute | solution.py:256
  32.3 7.6 %collective-permute-start.11 = (bf16[104,768]{1,0:T(8,128)(2,1)S(1)}, bf16[104,768]{1,0:T(8,128)(2,1)S(1)}, u32[]{:S(2)}, u32[]{:S(2)}) collective-permute-start(bf16[104,768]{1,0:T(8,128)(2,1)S(1)} %collective-permute-done.4.refs_2_), channel_id=1, source_target_pairs={{0,2},{2,0},{1,3},{3,1},{4,6},{6,4},{5,7},{7,5},{8,10},{10,8},{9,1... | collective-permute-start | bytes 479240 | tf_op jit(solution)/shard_map/ppermute | solution.py:259
  33.9 6.0 %collective-permute-start.14 = (bf16[96,768]{1,0:T(8,128)(2,1)S(1)}, bf16[96,768]{1,0:T(8,128)(2,1)S(1)}, u32[]{:S(2)}, u32[]{:S(2)}) collective-permute-start(bf16[96,768]{1,0:T(8,128)(2,1)S(1)} %collective-permute-done.12.refs_1_), channel_id=1, source_target_pairs={{8,0},{0,4},{4,12},{12,8},{9,1},{1,5},{5,13},{13,9},{10,2},{2,6},{... | collective-permute-start | bytes 442376 | tf_op jit(solution)/shard_map/ppermute | solution.py:256
  40.6 2.2 %collective-permute-start.15 = (f32[192,896]{1,0:T(8,128)S(1)}, f32[192,896]{1,0:T(8,128)S(1)}, u32[]{:S(2)}, u32[]{:S(2)}) collective-permute-start(f32[192,896]{1,0:T(8,128)S(1)} %shard_map.41), channel_id=1, source_target_pairs={{0,1},{1,0},{2,3},{3,2},{4,5},{5,4},{6,7},{7,6},{8,9},{9,8},{10,11... | collective-permute-start | bytes 2064392 | tf_op jit(solution)/shard_map/ppermute | solution.py:262

commit v5 on v4

--- a/solution.py
+++ b/solution.py
@@ -77,15 +77,12 @@
     return lax.rsqrt(jnp.sum(wide * wide, axis=1, keepdims=True) + 1e-06)
 
 
-def pack_kernel(rows, group, cluster, whole, first, second, group_here, cluster_here, sems):
+def pack_kernel(rows, group, cluster, out, group_here, cluster_here, sems):
     rows_here, width = rows.shape
-    half = rows_here // 2
     copies = [
         pltpu.make_async_copy(group, group_here, sems.at[0]),
         pltpu.make_async_copy(cluster, cluster_here, sems.at[1]),
-        pltpu.make_async_copy(rows.at[:half, :], first.at[:half, :], sems.at[2]),
-        pltpu.make_async_copy(rows.at[half:, :], second, sems.at[3]),
-        pltpu.make_async_copy(rows, whole.at[:rows_here, :], sems.at[4]),
+        pltpu.make_async_copy(rows, out.at[:rows_here, :], sems.at[2]),
     ]
     for copy in copies:
         copy.start()
@@ -93,12 +90,9 @@
     copies[1].wait()
     line = lax.broadcasted_iota(jnp.int32, (8, rows_here), 0)
     named = jnp.where(line == 0, group_here[...], jnp.where(line == 1, cluster_here[...], 0))
-    named = named.astype(F32).astype(BF16)
-    for out, top in ((whole, rows_here), (first, half)):
-        out[top:, :] = jnp.zeros((8, width), BF16)
-        out[top:, :rows_here] = named
-    for copy in copies[2:]:
-        copy.wait()
+    out[rows_here:, :] = jnp.zeros((8, width), BF16)
+    out[rows_here:, :rows_here] = named.astype(F32).astype(BF16)
+    copies[2].wait()
 
 
 def key_row(named):
@@ -112,9 +106,9 @@
 
 
 def from_halves(first, second):
-    half = second.shape[0]
-    rows = jnp.concatenate([first[:half, :], second[...]], axis=0)
-    return rows, key_row(first[half:, : 2 * half])
+    half = first.shape[0]
+    rows = jnp.concatenate([first[...], second[:half, :]], axis=0)
+    return rows, key_row(second[half:, : 2 * half])
 
 
 def add_blocks(left, blocks, numer, denom):
@@ -139,10 +133,6 @@
     return rows, key, to_row(scale_column(rows))
 
 
-def take_blocks(refs, count):
-    return [with_scale(from_halves(refs.pop(0), refs.pop(0))) for _ in range(count)]
-
-
 def add_side(left, blocks, before, out):
     width = left[0].shape[1]
     numer = None if before is None else before[:, :width]
@@ -153,24 +143,20 @@
 
 
 def start_kernel(n_blocks, own, other, *refs):
-    refs = list(refs)
     left = [from_whole(own), from_whole(other)]
-    blocks = [with_scale(left[0])] + take_blocks(refs, n_blocks)
+    blocks = [with_scale(left[0])] + [with_scale(from_whole(ref)) for ref in refs[:n_blocks]]
     for side in range(2):
-        add_side(left[side], blocks, None, refs[side])
+        add_side(left[side], blocks, None, refs[n_blocks + side])
 
 
 def both_kernel(n_blocks, own, other, *refs):
-    refs = list(refs)
-    blocks = take_blocks(refs, n_blocks)
+    blocks = [with_scale(from_whole(ref)) for ref in refs[:n_blocks]]
     for side, left in enumerate((own, other)):
-        add_side(from_whole(left), blocks, refs[side], refs[2 + side])
-
-
-def one_kernel(n_blocks, left, *refs):
-    refs = list(refs)
-    blocks = take_blocks(refs, n_blocks)
-    add_side(from_whole(left), blocks, refs[0], refs[1])
+        add_side(from_whole(left), blocks, refs[n_blocks + side], refs[n_blocks + 2 + side])
+
+
+def last_kernel(left, first, second, before, out):
+    add_side(from_whole(left), [with_scale(from_halves(first, second))], before, out)
 
 
 def mean_kernel(mine, theirs, out):
@@ -196,21 +182,16 @@
 
 def pack(embeddings, group_of, cluster_id):
     rows_here, width = embeddings.shape
-    half = rows_here // 2
     line = (1, rows_here)
     return pl.pallas_call(
         pack_kernel,
-        out_shape=[
-            jax.ShapeDtypeStruct((rows_here + 8, width), BF16),
-            jax.ShapeDtypeStruct((half + 8, width), BF16),
-            jax.ShapeDtypeStruct((half, width), BF16),
-        ],
-        in_specs=[pl.BlockSpec(memory_space=pltpu.HBM)] * 3,
-        out_specs=whole_in_vmem(3),
+        out_shape=jax.ShapeDtypeStruct((rows_here + 8, width), BF16),
+        in_specs=[pl.BlockSpec(memory_space=pl.ANY)] * 3,
+        out_specs=pl.BlockSpec(memory_space=pltpu.VMEM),
         scratch_shapes=[
             pltpu.VMEM(line, jnp.int32),
             pltpu.VMEM(line, jnp.int32),
-            pltpu.SemaphoreType.DMA((5,)),
+            pltpu.SemaphoreType.DMA((3,)),
         ],
         compiler_params=pltpu.CompilerParams(vmem_limit_bytes=PACK_BYTES),
     )(embeddings, group_of.reshape(line), cluster_id.reshape(line))
@@ -219,12 +200,13 @@
 def start_both(left, right):
     rows_here, width = left[0].shape
     shape = jax.ShapeDtypeStruct((rows_here - 8, width + 128), F32)
-    args = list(left) + [half for block in right for half in block]
-    return call(functools.partial(start_kernel, len(right)), [shape, shape], args)
+    return call(
+        functools.partial(start_kernel, len(right)), [shape, shape], list(left) + list(right)
+    )
 
 
 def add_both(left, right, before):
-    args = list(left) + [half for block in right for half in block] + list(before)
+    args = list(left) + list(right) + list(before)
     at = len(args) - 2
     shapes = [jax.ShapeDtypeStruct(total.shape, F32) for total in before]
     return call(
@@ -232,10 +214,9 @@
     )
 
 
-def add_one(left, right, before):
-    args = [left] + [half for block in right for half in block] + [before]
+def add_last(left, halves, before):
     shapes = [jax.ShapeDtypeStruct(before.shape, F32)]
-    return call(functools.partial(one_kernel, len(right)), shapes, args, {len(args) - 1: 0})[0]
+    return call(last_kernel, shapes, [left, *halves, before], {3: 0})[0]
 
 
 def folded_ring(size):
@@ -261,26 +242,25 @@
     def other_core(rows):
         return lax.ppermute(rows, "pair", swap)
 
-    whole, first, second = pack(embeddings, group_of, cluster_id)
-    along_by = [(first, second)]
+    block = pack(embeddings, group_of, cluster_id)
+    along_by = [block]
     across_by = []
-    other = other_core(whole)
+    other = other_core(block)
     in_flight = [other]
     for s in range(1, n_blk):
-        pieces = along_by.pop()
         if s > 1:
-            pieces = tuple(together(piece, in_flight.pop(0))[0] for piece in pieces)
-        along_by += [pieces, tuple(along(piece) for piece in pieces)]
-        across_by.append(tuple(across(piece) for piece in pieces))
-        in_flight += across_by[-1]
-    left = (whole, other)
+            along_by[-1], _ = together(along_by[-1], in_flight.pop(0))
+        across_by.append(across(along_by[-1]))
+        in_flight.append(across_by[-1])
+        along_by.append(along(along_by[-1]))
+    left = (block, other)
     total = start_both(left, across_by[:-1] + along_by[1:-1])
-    far_first, _, mine, theirs = together(along_by[-1][0], across_by[-1][0], *total)
-    near_second, _ = together(across_by[-1][1], along_by[-1][1])
-    last = (across(far_first), along(near_second))
-    mine, theirs = add_both(left, [across_by[-1], along_by[-1]], (mine, theirs))
-    theirs = other_core(add_one(left[1], [last], theirs))
-    mine = add_one(left[0], [last], mine)
+    half = rows_here // 2
+    far, near, mine, theirs = together(along_by[-1], across_by[-1], *total)
+    halves = (along(near[:half]), across(far[half:]))
+    mine, theirs = add_both(left, [near, far], (mine, theirs))
+    theirs = other_core(add_last(other, halves, theirs))
+    mine = add_last(block, halves, mine)
     (out,) = call(
         mean_kernel, [jax.ShapeDtypeStruct((rows_here, width), BF16)], [mine, theirs]
     )

time: 43.8 us -> 44.6 us (1.018)
  waiting for transfers between devices: 8.45 us -> 25.1 us
  starting transfers between devices: 26.2 us -> 10.6 us
    ppermute x7 -> x4, waiting for transfers between devices: 3.62 us -> 20.9 us  [along(): lax.ppermute(rows, 'blk', [(order[i - 1], order[i]) for i in range(n_blk)])]
    ppermute x7 -> x4, starting transfers between devices: 17.1 us -> 4.71 us  [along(): lax.ppermute(rows, 'blk', [(order[i - 1], order[i]) for i in range(n_blk)])]
    ppermute x7 -> x4, starting transfers between devices: 8.59 us -> 5.31 us  [across(): return lax.ppermute(rows, 'sub', swap)]
    ppermute x7 -> x4, waiting for transfers between devices: 3.31 us -> 2.74 us  [across(): return lax.ppermute(rows, 'sub', swap)]
  transfers between devices with their start and end apart: 16 -> 10, of which waited for: 5 -> 6; matrix products, arithmetic and copies ran while one was open for 0% -> 0% of each run, Pallas kernels for 12% -> 12%
where the time goes in v5:
time: 44.6 us; the launch traced here: 44.4 us
  waiting for transfers between devices  25.1 us (56%)
  starting transfers between devices  10.6 us (24%)
  Pallas kernels  6.97 us (16%)
  local copies, waits for them, and re-layouts  1.68 us (4%)
    ppermute x4, waiting for transfers between devices, along(): lax.ppermute(rows, 'blk', [(order[i - 1], order[i]) for i in range(n_blk)])  20.9 us
    pallas_call x5, Pallas kernels, call(): pl.pallas_call(kernel, out_shape=shapes, in_specs=whole_in_vmem(len(args)...  6.87 us
    ppermute x4, starting transfers between devices, across(): return lax.ppermute(rows, 'sub', swap)  5.31 us
    ppermute x4, starting transfers between devices, along(): lax.ppermute(rows, 'blk', [(order[i - 1], order[i]) for i in range(n_blk)])  4.71 us
    ppermute x4, waiting for transfers between devices, across(): return lax.ppermute(rows, 'sub', swap)  2.74 us
    unnamed x6, local copies, waits for them, and re-layouts  1.65 us
    ppermute x2, waiting for transfers between devices, other_core(): return lax.ppermute(rows, 'pair', swap)  1.52 us
  transfers between devices with their start and end apart: 10, of which 6 were waited for; matrix products, arithmetic and copies ran while one was open for 0% of the time, Pallas kernels for 12%

profile of v5, /device:TPU:0, one launch (start us, length us, event | category | flops | bytes accessed | tf_op | source)
XLA Modules:
  0.0 44.4 jit_solution(4507053453087129031)
XLA Ops:
  0.0 0.0 copy-start.2
  0.0 0.0 copy-start.1
  0.0 0.7 %copy-done.2 = s32[192]{0:T(256)S(1)} copy-done((s32[192]{0:T(256)S(1)}, s32[192]{0:T(256)}, u32[]{:S(2)}) %copy-start.2) | copy-done | bytes 792
  0.7 0.0 copy-done.1
  0.7 0.0 copy-start
  0.7 1.0 %copy-done = bf16[192,768]{1,0:T(8,128)(2,1)S(1)} copy-done((bf16[192,768]{1,0:T(8,128)(2,1)S(1)}, bf16[192,768]{1,0:T(8,128)(2,1)}, u32[]{:S(2)}) %copy-start) | copy-done | bytes 294936
  1.7 0.1 shard_map.37.own.left
  1.8 0.5 %collective-permute-start.1 = (bf16[200,768]{1,0:T(8,128)(2,1)S(1)}, bf16[200,768]{1,0:T(8,128)(2,1)S(1)}, u32[]{:S(2)}, u32[]{:S(2)}) collective-permute-start(bf16[200,768]{1,0:T(8,128)(2,1)S(1)} %shard_map.37.own.left), channel_id=1, source_target_pairs={{0,1},{1,0},{2,3},{3,2},{4,5},{5,4},{6,7},{7,6},{8,9},{9,8},{10,11... | collective-permute-start | bytes 921608 | tf_op jit(solution)/shard_map/ppermute | solution.py:243
  2.3 2.6 %collective-permute-start = (bf16[200,768]{1,0:T(8,128)(2,1)S(1)}, bf16[200,768]{1,0:T(8,128)(2,1)S(1)}, u32[]{:S(2)}, u32[]{:S(2)}) collective-permute-start(bf16[200,768]{1,0:T(8,128)(2,1)S(1)} %shard_map.37.own.left), channel_id=1, source_target_pairs={{8,0},{0,4},{4,12},{12,8},{9,1},{1,5},{5,13},{13,9},{10,2},{2,6},{... | collective-permute-start | bytes 921608 | tf_op jit(solution)/shard_map/ppermute | solution.py:237
  4.9 1.5 %collective-permute-start.3 = (bf16[200,768]{1,0:T(8,128)(2,1)S(1)}, bf16[200,768]{1,0:T(8,128)(2,1)S(1)}, u32[]{:S(2)}, u32[]{:S(2)}) collective-permute-start(bf16[200,768]{1,0:T(8,128)(2,1)S(1)} %shard_map.37.own.left), channel_id=1, source_target_pairs={{0,2},{2,0},{1,3},{3,1},{4,6},{6,4},{5,7},{7,5},{8,10},{10,8},{9,1... | collective-permute-start | bytes 921608 | tf_op jit(solution)/shard_map/ppermute | solution.py:240
  6.4 0.0 collective-permute-done.1.other.left
  6.4 7.4 %collective-permute-done.refs_2_ = bf16[200,768]{1,0:T(8,128)(2,1)S(1)} collective-permute-done((bf16[200,768]{1,0:T(8,128)(2,1)S(1)}, bf16[200,768]{1,0:T(8,128)(2,1)S(1)}, u32[]{:S(2)}, u32[]{:S(2)}) %collective-permute-start) | collective-permute-done | bytes 307232 | tf_op jit(solution)/shard_map/ppermute | solution.py:237
  13.8 0.8 %collective-permute-start.2 = (bf16[200,768]{1,0:T(8,128)(2,1)S(1)}, bf16[200,768]{1,0:T(8,128)(2,1)S(1)}, u32[]{:S(2)}, u32[]{:S(2)}) collective-permute-start(bf16[200,768]{1,0:T(8,128)(2,1)S(1)} %collective-permute-done.refs_2_), channel_id=1, source_target_pairs={{8,0},{0,4},{4,12},{12,8},{9,1},{1,5},{5,13},{13,9},{10,2},{2,6},{... | collective-permute-start | bytes 921608 | tf_op jit(solution)/shard_map/ppermute | solution.py:237
  14.6 1.5 %collective-permute-start.6 = (bf16[200,768]{1,0:T(8,128)(2,1)S(1)}, bf16[200,768]{1,0:T(8,128)(2,1)S(1)}, u32[]{:S(2)}, u32[]{:S(2)}) collective-permute-start(bf16[200,768]{1,0:T(8,128)(2,1)S(1)} %collective-permute-done.refs_2_), channel_id=1, source_target_pairs={{0,2},{2,0},{1,3},{3,1},{4,6},{6,4},{5,7},{7,5},{8,10},{10,8},{9,1... | collective-permute-start | bytes 921608 | tf_op jit(solution)/shard_map/ppermute | solution.py:240
  16.1 0.0 collective-permute-done.3.refs_0_
  16.1 7.6 %collective-permute-done.2.refs_3_ = bf16[200,768]{1,0:T(8,128)(2,1)S(1)} collective-permute-done((bf16[200,768]{1,0:T(8,128)(2,1)S(1)}, bf16[200,768]{1,0:T(8,128)(2,1)S(1)}, u32[]{:S(2)}, u32[]{:S(2)}) %collective-permute-start.2) | collective-permute-done | bytes 307232 | tf_op jit(solution)/shard_map/ppermute | solution.py:237
  23.7 1.3 %collective-permute-start.5 = (bf16[200,768]{1,0:T(8,128)(2,1)S(1)}, bf16[200,768]{1,0:T(8,128)(2,1)S(1)}, u32[]{:S(2)}, u32[]{:S(2)}) collective-permute-start(bf16[200,768]{1,0:T(8,128)(2,1)S(1)} %collective-permute-done.2.refs_3_), channel_id=1, source_target_pairs={{0,2},{2,0},{1,3},{3,1},{4,6},{6,4},{5,7},{7,5},{8,10},{10,8},{9,1... | collective-permute-start | bytes 921608 | tf_op jit(solution)/shard_map/ppermute | solution.py:240
  25.1 0.8 %collective-permute-start.4 = (bf16[200,768]{1,0:T(8,128)(2,1)S(1)}, bf16[200,768]{1,0:T(8,128)(2,1)S(1)}, u32[]{:S(2)}, u32[]{:S(2)}) collective-permute-start(bf16[200,768]{1,0:T(8,128)(2,1)S(1)} %collective-permute-done.2.refs_3_), channel_id=1, source_target_pairs={{8,0},{0,4},{4,12},{12,8},{9,1},{1,5},{5,13},{13,9},{10,2},{2,6},{... | collective-permute-start | bytes 921608 | tf_op jit(solution)/shard_map/ppermute | solution.py:237
  25.9 0.0 collective-permute-done.6.refs_1_
  25.9 3.3 %shard_map.38 = (f32[192,896]{1,0:T(8,128)S(1)}, f32[192,896]{1,0:T(8,128)S(1)}) custom-call(bf16[200,768]{1,0:T(8,128)(2,1)S(1)} %shard_map.37.own.left, bf16[200,768]{1,0:T(8,128)(2,1)S(1)} %collective-permute-done.1.other.left, bf16[200,768]{1,0:T(8,128)(2,1)S(1)} %collective-permute-done.3.refs_0_, bf16[200,768]{1,0:T(8,128)(2,1)S(1)} %collective-permute-done.6.refs_1_, ...), custom_call_target="tpu_custom_call" | custom-call | tf_op jit(solution)/shard_map/pallas_call | solution.py:173
  29.2 2.7 %collective-permute-done.5.refs_0_ = bf16[200,768]{1,0:T(8,128)(2,1)S(1)} collective-permute-done((bf16[200,768]{1,0:T(8,128)(2,1)S(1)}, bf16[200,768]{1,0:T(8,128)(2,1)S(1)}, u32[]{:S(2)}, u32[]{:S(2)}) %collective-permute-start.5) | collective-permute-done | bytes 307232 | tf_op jit(solution)/shard_map/ppermute | solution.py:240
  31.9 1.7 %collective-permute-done.4.refs_1_ = bf16[200,768]{1,0:T(8,128)(2,1)S(1)} collective-permute-done((bf16[200,768]{1,0:T(8,128)(2,1)S(1)}, bf16[200,768]{1,0:T(8,128)(2,1)S(1)}, u32[]{:S(2)}, u32[]{:S(2)}) %collective-permute-start.4) | collective-permute-done | bytes 307232 | tf_op jit(solution)/shard_map/ppermute | solution.py:237
  33.7 1.0 %collective-permute-start.8 = (bf16[104,768]{1,0:T(8,128)(2,1)S(1)}, bf16[104,768]{1,0:T(8,128)(2,1)S(1)}, u32[]{:S(2)}, u32[]{:S(2)}) collective-permute-start(bf16[104,768]{1,0:T(8,128)(2,1)S(1)} %slice.7), channel_id=1, source_target_pairs={{0,2},{2,0},{1,3},{3,1},{4,6},{6,4},{5,7},{7,5},{8,10},{10,8},{9,1... | collective-permute-start | bytes 479240 | tf_op jit(solution)/shard_map/ppermute | solution.py:240
  34.7 0.5 %collective-permute-start.7 = (bf16[96,768]{1,0:T(8,128)(2,1)S(1)}, bf16[96,768]{1,0:T(8,128)(2,1)S(1)}, u32[]{:S(2)}, u32[]{:S(2)}) collective-permute-start(bf16[96,768]{1,0:T(8,128)(2,1)S(1)} %slice.6), channel_id=1, source_target_pairs={{8,0},{0,4},{4,12},{12,8},{9,1},{1,5},{5,13},{13,9},{10,2},{2,6},{... | collective-permute-start | bytes 442376 | tf_op jit(solution)/shard_map/ppermute | solution.py:237
  35.1 1.5 %shard_map.39 = (f32[192,896]{1,0:T(8,128)S(1)}, f32[192,896]{1,0:T(8,128)S(1)}) custom-call(bf16[200,768]{1,0:T(8,128)(2,1)S(1)} %shard_map.37.own.left, bf16[200,768]{1,0:T(8,128)(2,1)S(1)} %collective-permute-done.1.other.left, bf16[200,768]{1,0:T(8,128)(2,1)S(1)} %collective-permute-done.5.refs_0_, ...), custom_call_target="tpu_custom_call", output_to_operand_aliasing={{0}: (4, {}), {1}: (5, {})} | custom-call | tf_op jit(solution)/shard_map/pallas_call | solution.py:173
  36.6 4.1 %collective-permute-done.7.first = bf16[96,768]{1,0:T(8,128)(2,1)S(1)} collective-permute-done((bf16[96,768]{1,0:T(8,128)(2,1)S(1)}, bf16[96,768]{1,0:T(8,128)(2,1)S(1)}, u32[]{:S(2)}, u32[]{:S(2)}) %collective-permute-start.7) | collective-permute-done | bytes 147488 | tf_op jit(solution)/shard_map/ppermute | solution.py:237
  40.8 0.0 collective-permute-done.8.second
  40.8 0.6 %shard_map.41 = f32[192,896]{1,0:T(8,128)S(1)} custom-call(bf16[200,768]{1,0:T(8,128)(2,1)S(1)} %collective-permute-done.1.other.left, bf16[96,768]{1,0:T(8,128)(2,1)S(1)} %collective-permute-done.7.first, bf16[104,768]{1,0:T(8,128)(2,1)S(1)} %collective-permute-done.8.second, f32[192,896]{1,0:T(8,128)S(1)} %get-tuple-element.24.before), custom_call_target="tpu_custom_call", output_to_operand_aliasing={{}: (3, {})} | custom-call | tf_op jit(solution)/shard_map/pallas_call | solution.py:173
  41.4 0.1 collective-permute-start.9
  41.4 0.6 %shard_map.40.mine = f32[192,896]{1,0:T(8,128)S(1)} custom-call(bf16[200,768]{1,0:T(8,128)(2,1)S(1)} %shard_map.37.own.left, bf16[96,768]{1,0:T(8,128)(2,1)S(1)} %collective-permute-done.7.first, bf16[104,768]{1,0:T(8,128)(2,1)S(1)} %collective-permute-done.8.second, f32[192,896]{1,0:T(8,128)S(1)} %get-tuple-element.23.before), custom_call_target="tpu_custom_call", output_to_operand_aliasing={{}: (3, {})} | custom-call | tf_op jit(solution)/shard_map/pallas_call | solution.py:173
  42.1 1.5 %collective-permute-done.9.theirs = f32[192,896]{1,0:T(8,128)S(1)} collective-permute-done((f32[192,896]{1,0:T(8,128)S(1)}, f32[192,896]{1,0:T(8,128)S(1)}, u32[]{:S(2)}, u32[]{:S(2)}) %collective-permute-start.9) | collective-permute-done | bytes 688160 | tf_op jit(solution)/shard_map/ppermute | solution.py:243
  43.6 0.8 %shard_map.42 = bf16[192,768]{1,0:T(8,128)(2,1)} custom-call(f32[192,896]{1,0:T(8,128)S(1)} %shard_map.40.mine, f32[192,896]{1,0:T(8,128)S(1)} %collective-permute-done.9.theirs), custom_call_target="tpu_custom_call" | custom-call | tf_op jit(solution)/shard_map/pallas_call | solution.py:173
  (2 shorter events, 0.0 us)
Async XLA Ops:
  0.0 0.7 %copy-start.2 = (s32[192]{0:T(256)S(1)}, s32[192]{0:T(256)}, u32[]{:S(2)}) copy-start(s32[192]{0:T(256)} %param.5) | copy-start | bytes 2308
  0.0 0.7 %copy-start.1 = (s32[192,1]{0,1:T(1,128)S(1)}, s32[192,1]{0,1:T(1,128)}, u32[]{:S(2)}) copy-start(s32[192,1]{0,1:T(1,128)} %param.4) | copy-start | bytes 2308
  0.7 1.0 %copy-start = (bf16[192,768]{1,0:T(8,128)(2,1)S(1)}, bf16[192,768]{1,0:T(8,128)(2,1)}, u32[]{:S(2)}) copy-start(bf16[192,768]{1,0:T(8,128)(2,1)} %rows.1) | copy-start | bytes 884740
  1.8 4.7 %collective-permute-start.1 = (bf16[200,768]{1,0:T(8,128)(2,1)S(1)}, bf16[200,768]{1,0:T(8,128)(2,1)S(1)}, u32[]{:S(2)}, u32[]{:S(2)}) collective-permute-start(bf16[200,768]{1,0:T(8,128)(2,1)S(1)} %shard_map.37.own.left), channel_id=1, source_target_pairs={{0,1},{1,0},{2,3},{3,2},{4,5},{5,4},{6,7},{7,6},{8,9},{9,8},{10,11... | collective-permute-start | bytes 921608 | tf_op jit(solution)/shard_map/ppermute | solution.py:243
  2.3 11.5 %collective-permute-start = (bf16[200,768]{1,0:T(8,128)(2,1)S(1)}, bf16[200,768]{1,0:T(8,128)(2,1)S(1)}, u32[]{:S(2)}, u32[]{:S(2)}) collective-permute-start(bf16[200,768]{1,0:T(8,128)(2,1)S(1)} %shard_map.37.own.left), channel_id=1, source_target_pairs={{8,0},{0,4},{4,12},{12,8},{9,1},{1,5},{5,13},{13,9},{10,2},{2,6},{... | collective-permute-start | bytes 921608 | tf_op jit(solution)/shard_map/ppermute | solution.py:237
  4.9 11.2 %collective-permute-start.3 = (bf16[200,768]{1,0:T(8,128)(2,1)S(1)}, bf16[200,768]{1,0:T(8,128)(2,1)S(1)}, u32[]{:S(2)}, u32[]{:S(2)}) collective-permute-start(bf16[200,768]{1,0:T(8,128)(2,1)S(1)} %shard_map.37.own.left), channel_id=1, source_target_pairs={{0,2},{2,0},{1,3},{3,1},{4,6},{6,4},{5,7},{7,5},{8,10},{10,8},{9,1... | collective-permute-start | bytes 921608 | tf_op jit(solution)/shard_map/ppermute | solution.py:240
  13.8 9.9 %collective-permute-start.2 = (bf16[200,768]{1,0:T(8,128)(2,1)S(1)}, bf16[200,768]{1,0:T(8,128)(2,1)S(1)}, u32[]{:S(2)}, u32[]{:S(2)}) collective-permute-start(bf16[200,768]{1,0:T(8,128)(2,1)S(1)} %collective-permute-done.refs_2_), channel_id=1, source_target_pairs={{8,0},{0,4},{4,12},{12,8},{9,1},{1,5},{5,13},{13,9},{10,2},{2,6},{... | collective-permute-start | bytes 921608 | tf_op jit(solution)/shard_map/ppermute | solution.py:237
  14.6 11.2 %collective-permute-start.6 = (bf16[200,768]{1,0:T(8,128)(2,1)S(1)}, bf16[200,768]{1,0:T(8,128)(2,1)S(1)}, u32[]{:S(2)}, u32[]{:S(2)}) collective-permute-start(bf16[200,768]{1,0:T(8,128)(2,1)S(1)} %collective-permute-done.refs_2_), channel_id=1, source_target_pairs={{0,2},{2,0},{1,3},{3,1},{4,6},{6,4},{5,7},{7,5},{8,10},{10,8},{9,1... | collective-permute-start | bytes 921608 | tf_op jit(solution)/shard_map/ppermute | solution.py:240
  23.7 8.2 %collective-permute-start.5 = (bf16[200,768]{1,0:T(8,128)(2,1)S(1)}, bf16[200,768]{1,0:T(8,128)(2,1)S(1)}, u32[]{:S(2)}, u32[]{:S(2)}) collective-permute-start(bf16[200,768]{1,0:T(8,128)(2,1)S(1)} %collective-permute-done.2.refs_3_), channel_id=1, source_target_pairs={{0,2},{2,0},{1,3},{3,1},{4,6},{6,4},{5,7},{7,5},{8,10},{10,8},{9,1... | collective-permute-start | bytes 921608 | tf_op jit(solution)/shard_map/ppermute | solution.py:240
  25.1 8.6 %collective-permute-start.4 = (bf16[200,768]{1,0:T(8,128)(2,1)S(1)}, bf16[200,768]{1,0:T(8,128)(2,1)S(1)}, u32[]{:S(2)}, u32[]{:S(2)}) collective-permute-start(bf16[200,768]{1,0:T(8,128)(2,1)S(1)} %collective-permute-done.2.refs_3_), channel_id=1, source_target_pairs={{8,0},{0,4},{4,12},{12,8},{9,1},{1,5},{5,13},{13,9},{10,2},{2,6},{... | collective-permute-start | bytes 921608 | tf_op jit(solution)/shard_map/ppermute | solution.py:237
  33.7 7.1 %collective-permute-start.8 = (bf16[104,768]{1,0:T(8,128)(2,1)S(1)}, bf16[104,768]{1,0:T(8,128)(2,1)S(1)}, u32[]{:S(2)}, u32[]{:S(2)}) collective-permute-start(bf16[104,768]{1,0:T(8,128)(2,1)S(1)} %slice.7), channel_id=1, source_target_pairs={{0,2},{2,0},{1,3},{3,1},{4,6},{6,4},{5,7},{7,5},{8,10},{10,8},{9,1... | collective-permute-start | bytes 479240 | tf_op jit(solution)/shard_map/ppermute | solution.py:240
  34.7 6.1 %collective-permute-start.7 = (bf16[96,768]{1,0:T(8,128)(2,1)S(1)}, bf16[96,768]{1,0:T(8,128)(2,1)S(1)}, u32[]{:S(2)}, u32[]{:S(2)}) collective-permute-start(bf16[96,768]{1,0:T(8,128)(2,1)S(1)} %slice.6), channel_id=1, source_target_pairs={{8,0},{0,4},{4,12},{12,8},{9,1},{1,5},{5,13},{13,9},{10,2},{2,6},{... | collective-permute-start | bytes 442376 | tf_op jit(solution)/shard_map/ppermute | solution.py:237
  41.4 2.2 %collective-permute-start.9 = (f32[192,896]{1,0:T(8,128)S(1)}, f32[192,896]{1,0:T(8,128)S(1)}, u32[]{:S(2)}, u32[]{:S(2)}) collective-permute-start(f32[192,896]{1,0:T(8,128)S(1)} %shard_map.41), channel_id=1, source_target_pairs={{0,1},{1,0},{2,3},{3,2},{4,5},{5,4},{6,7},{7,6},{8,9},{9,8},{10,11... | collective-permute-start | bytes 2064392 | tf_op jit(solution)/shard_map/ppermute | solution.py:243

commit v6 on v3

--- a/solution.py
+++ b/solution.py
@@ -10,7 +10,7 @@
 F32 = jnp.float32
 BF16 = jnp.bfloat16
 VMEM_BYTES = 24 * 1024 * 1024
-PACK_BYTES = 48 * 1024 * 1024
+PACK_BYTES = 56 * 1024 * 1024
 GATHER_LIMIT = 8 * 1024 * 1024
 
 
@@ -77,44 +77,78 @@
     return lax.rsqrt(jnp.sum(wide * wide, axis=1, keepdims=True) + 1e-06)
 
 
-def pack_kernel(rows, group, cluster, whole, first, second, group_here, cluster_here, sems):
+def name_lines(rows_here):
+    return -(-rows_here // 128)
+
+
+def slab_copies(rows, top, count, out, sems, first):
+    copies = []
+    for slab in range(rows.shape[1] // 128):
+        source = rows.at[top : top + count, slab * 128 : (slab + 1) * 128]
+        target = out.at[slab * count : (slab + 1) * count, :]
+        copies.append(pltpu.make_async_copy(source, target, sems.at[first + slab]))
+    return copies
+
+
+def pack_kernel(rows, group, cluster, whole, first, second, group_here, cluster_here, names, sems):
     rows_here, width = rows.shape
     half = rows_here // 2
-    copies = [
+    slabs = width // 128
+    loads = [
         pltpu.make_async_copy(group, group_here, sems.at[0]),
         pltpu.make_async_copy(cluster, cluster_here, sems.at[1]),
-        pltpu.make_async_copy(rows.at[:half, :], first.at[:half, :], sems.at[2]),
-        pltpu.make_async_copy(rows.at[half:, :], second, sems.at[3]),
-        pltpu.make_async_copy(rows, whole.at[:rows_here, :], sems.at[4]),
     ]
-    for copy in copies:
+    copies = slab_copies(rows, 0, half, first, sems, 4)
+    copies += slab_copies(rows, half, half, second, sems, 4 + slabs)
+    copies += slab_copies(rows, 0, rows_here, whole, sems, 4 + 2 * slabs)
+    for copy in loads + copies:
         copy.start()
-    copies[0].wait()
-    copies[1].wait()
-    line = lax.broadcasted_iota(jnp.int32, (8, rows_here), 0)
-    named = jnp.where(line == 0, group_here[...], jnp.where(line == 1, cluster_here[...], 0))
-    named = named.astype(F32).astype(BF16)
-    for out, top in ((whole, rows_here), (first, half)):
-        out[top:, :] = jnp.zeros((8, width), BF16)
-        out[top:, :rows_here] = named
-    for copy in copies[2:]:
+    for copy in loads:
         copy.wait()
-
-
-def key_row(named):
-    wide = named.astype(F32)
-    return wide[0:1, :] * 256.0 + wide[1:2, :]
-
-
-def from_whole(ref):
-    rows_here = ref.shape[0] - 8
-    return ref[:rows_here, :], key_row(ref[rows_here:, :rows_here])
-
-
-def from_halves(first, second):
-    half = second.shape[0]
-    rows = jnp.concatenate([first[:half, :], second[...]], axis=0)
-    return rows, key_row(first[half:, : 2 * half])
+    line_at = lax.broadcasted_iota(jnp.int32, names.shape, 0)
+    lines = name_lines(rows_here)
+    named = jnp.zeros(names.shape, jnp.int32)
+    for kind, ref in enumerate((group_here, cluster_here)):
+        for line in range(lines):
+            part = ref[:, line * 128 : (line + 1) * 128]
+            if part.shape[1] < 128:
+                rest = jnp.zeros((1, 128 - part.shape[1]), jnp.int32)
+                part = jnp.concatenate([part, rest], axis=1)
+            named = jnp.where(line_at == kind * lines + line, part, named)
+    names[...] = named.astype(F32).astype(BF16)
+    stores = [
+        pltpu.make_async_copy(names, whole.at[slabs * rows_here :, :], sems.at[2]),
+        pltpu.make_async_copy(names, first.at[slabs * half :, :], sems.at[3]),
+    ]
+    for copy in stores:
+        copy.start()
+    for copy in copies + stores:
+        copy.wait()
+
+
+def from_slabs(ref, count):
+    slabs = [ref[top : top + count, :] for top in range(0, ref.shape[0] // count * count, count)]
+    return jnp.concatenate(slabs, axis=1)
+
+
+def key_row(ref, rows_here):
+    wide = ref[ref.shape[0] - 8 :, :].astype(F32)
+    lines = name_lines(rows_here)
+    kinds = []
+    for kind in range(2):
+        parts = [wide[kind * lines + line : kind * lines + line + 1, :] for line in range(lines)]
+        kinds.append(jnp.concatenate(parts, axis=1)[:, :rows_here])
+    return kinds[0] * 256.0 + kinds[1]
+
+
+def from_whole(ref, rows_here):
+    return from_slabs(ref, rows_here), key_row(ref, rows_here)
+
+
+def from_halves(first, second, rows_here):
+    half = rows_here // 2
+    rows = jnp.concatenate([from_slabs(first, half), from_slabs(second, half)], axis=0)
+    return rows, key_row(first, rows_here)
 
 
 def add_blocks(left, blocks, numer, denom):
@@ -139,8 +173,10 @@
     return rows, key, to_row(scale_column(rows))
 
 
-def take_blocks(refs, count):
-    return [with_scale(from_halves(refs.pop(0), refs.pop(0))) for _ in range(count)]
+def take_blocks(refs, count, rows_here):
+    return [
+        with_scale(from_halves(refs.pop(0), refs.pop(0), rows_here)) for _ in range(count)
+    ]
 
 
 def add_side(left, blocks, before, out):
@@ -154,23 +190,26 @@
 
 def start_kernel(n_blocks, own, other, *refs):
     refs = list(refs)
-    left = [from_whole(own), from_whole(other)]
-    blocks = [with_scale(left[0])] + take_blocks(refs, n_blocks)
+    rows_here = refs[-1].shape[0]
+    left = [from_whole(own, rows_here), from_whole(other, rows_here)]
+    blocks = [with_scale(left[0])] + take_blocks(refs, n_blocks, rows_here)
     for side in range(2):
         add_side(left[side], blocks, None, refs[side])
 
 
 def both_kernel(n_blocks, own, other, *refs):
     refs = list(refs)
-    blocks = take_blocks(refs, n_blocks)
+    rows_here = refs[-1].shape[0]
+    blocks = take_blocks(refs, n_blocks, rows_here)
     for side, left in enumerate((own, other)):
-        add_side(from_whole(left), blocks, refs[side], refs[2 + side])
+        add_side(from_whole(left, rows_here), blocks, refs[side], refs[2 + side])
 
 
 def one_kernel(n_blocks, left, *refs):
     refs = list(refs)
-    blocks = take_blocks(refs, n_blocks)
-    add_side(from_whole(left), blocks, refs[0], refs[1])
+    rows_here = refs[-1].shape[0]
+    blocks = take_blocks(refs, n_blocks, rows_here)
+    add_side(from_whole(left, rows_here), blocks, refs[0], refs[1])
 
 
 def mean_kernel(mine, theirs, out):
@@ -197,29 +236,30 @@
 def pack(embeddings, group_of, cluster_id):
     rows_here, width = embeddings.shape
     half = rows_here // 2
+    slabs = width // 128
     line = (1, rows_here)
     return pl.pallas_call(
         pack_kernel,
         out_shape=[
-            jax.ShapeDtypeStruct((rows_here + 8, width), BF16),
-            jax.ShapeDtypeStruct((half + 8, width), BF16),
-            jax.ShapeDtypeStruct((half, width), BF16),
+            jax.ShapeDtypeStruct((slabs * rows_here + 8, 128), BF16),
+            jax.ShapeDtypeStruct((slabs * half + 8, 128), BF16),
+            jax.ShapeDtypeStruct((slabs * half, 128), BF16),
         ],
-        in_specs=[pl.BlockSpec(memory_space=pltpu.HBM)] * 3,
-        out_specs=whole_in_vmem(3),
+        in_specs=[pl.BlockSpec(memory_space=pl.ANY)] * 3,
+        out_specs=[pl.BlockSpec(memory_space=pl.ANY)] * 3,
         scratch_shapes=[
             pltpu.VMEM(line, jnp.int32),
             pltpu.VMEM(line, jnp.int32),
-            pltpu.SemaphoreType.DMA((5,)),
+            pltpu.VMEM((8, 128), BF16),
+            pltpu.SemaphoreType.DMA((4 + 3 * slabs,)),
         ],
         compiler_params=pltpu.CompilerParams(vmem_limit_bytes=PACK_BYTES),
     )(embeddings, group_of.reshape(line), cluster_id.reshape(line))
 
 
-def start_both(left, right):
-    rows_here, width = left[0].shape
-    shape = jax.ShapeDtypeStruct((rows_here - 8, width + 128), F32)
+def start_both(left, right, shape):
     args = list(left) + [half for block in right for half in block]
+    shape = jax.ShapeDtypeStruct(shape, F32)
     return call(functools.partial(start_kernel, len(right)), [shape, shape], args)
 
 
@@ -271,7 +311,7 @@
         along_by.append(tuple(pair[0] for pair in pairs))
         across_by.append(tuple(pair[1] for pair in pairs))
     left = (whole, other_core(whole))
-    total = start_both(left, across_by[:-1] + along_by[1:-1])
+    total = start_both(left, across_by[:-1] + along_by[1:-1], (rows_here, width + 128))
     far_first, mine, theirs = together(along_by[-1][0], *total)
     last = (across(far_first), along(across_by[-1][1]))
     mine, theirs = add_both(left, [across_by[-1], along_by[-1]], (mine, theirs))
@@ -287,7 +327,8 @@
     rows_here, width = embeddings.shape
     devices = lax.axis_size("blk") * lax.axis_size("sub") * lax.axis_size("pair")
     small = devices * rows_here * width * 2 <= GATHER_LIMIT
-    if small and lax.axis_size("sub") == 2 and lax.axis_size("pair") == 2:
+    fits = width % 128 == 0 and rows_here % 32 == 0 and rows_here <= 512
+    if small and fits and lax.axis_size("sub") == 2 and lax.axis_size("pair") == 2:
         return by_block(embeddings, group_of, cluster_id)
     return by_group(embeddings, group_of, cluster_id)
 

time: 41.3 us -> 58.5 us (1.42)
  Pallas kernels: 7.19 us -> 25.8 us
  starting transfers between devices: 23.6 us -> 22.9 us
    pallas_call x1, Pallas kernels: 0.48 us -> 19.2 us  [pack(): pl.pallas_call(pack_kernel, out_shape=[jax.ShapeDtypeStruct((slabs * rows...]
    ppermute x7, waiting for transfers between devices: 2.68 us -> 1.91 us  [across(): return lax.ppermute(rows, 'sub', swap)]
    ppermute x7, waiting for transfers between devices: 4.39 us -> 5.14 us  [along(): lax.ppermute(rows, 'blk', [(order[i - 1], order[i]) for i in range(n_blk)])]
    ppermute x7, starting transfers between devices: 14.8 us -> 14.2 us  [along(): lax.ppermute(rows, 'blk', [(order[i - 1], order[i]) for i in range(n_blk)])]
    unnamed x6 -> x4, local copies, waits for them, and re-layouts: 1.65 us -> 1.23 us
  transfers between devices with their start and end apart: 16 -> 16, of which waited for: 6 -> 5; matrix products, arithmetic and copies ran while one was open for 0% -> 0% of each run, Pallas kernels for 13% -> 9%
where the time goes in v6:
time: 58.5 us; the launch traced here: 58.4 us
  Pallas kernels  25.8 us (44%)
  starting transfers between devices  22.9 us (39%)
  waiting for transfers between devices  8.31 us (14%)
  local copies, waits for them, and re-layouts  1.23 us (2%)
    pallas_call x1, Pallas kernels, pack(): pl.pallas_call(pack_kernel, out_shape=[jax.ShapeDtypeStruct((slabs * rows...  19.2 us
    ppermute x7, starting transfers between devices, along(): lax.ppermute(rows, 'blk', [(order[i - 1], order[i]) for i in range(n_blk)])  14.2 us
    ppermute x7, starting transfers between devices, across(): return lax.ppermute(rows, 'sub', swap)  8.67 us
    pallas_call x5, Pallas kernels, call(): pl.pallas_call(kernel, out_shape=shapes, in_specs=whole_in_vmem(len(args)...  6.68 us
    ppermute x7, waiting for transfers between devices, along(): lax.ppermute(rows, 'blk', [(order[i - 1], order[i]) for i in range(n_blk)])  5.14 us
    ppermute x7, waiting for transfers between devices, across(): return lax.ppermute(rows, 'sub', swap)  1.91 us
    ppermute x2, waiting for transfers between devices, other_core(): return lax.ppermute(rows, 'pair', swap)  1.26 us
    unnamed x4, local copies, waits for them, and re-layouts  1.23 us
  transfers between devices with their start and end apart: 16, of which 5 were waited for; matrix products, arithmetic and copies ran while one was open for 0% of the time, Pallas kernels for 9%

profile of v6, /device:TPU:0, one launch (start us, length us, event | category | flops | bytes accessed | tf_op | source)
XLA Modules:
  0.0 58.4 jit_solution(16106303892756471945)
XLA Ops:
  0.0 19.2 %shard_map.37 = (bf16[1160,128]{1,0:T(8,128)(2,1)}, bf16[584,128]{1,0:T(8,128)(2,1)}, bf16[576,128]{1,0:T(8,128)(2,1)}) custom-call(bf16[192,768]{1,0:T(8,128)(2,1)} %rows.1, s32[1,192]{1,0:T(1,128)} %bitcast.2, s32[1,192]{1,0:T(1,128)} %bitcast.3), custom_call_target="tpu_custom_call" | custom-call | tf_op jit(solution)/shard_map/pallas_call | solution.py:241
  19.2 3.1 %collective-permute-start = (bf16[584,128]{1,0:T(8,128)(2,1)}, bf16[584,128]{1,0:T(8,128)(2,1)S(1)}, u32[]{:S(2)}, u32[]{:S(2)}) collective-permute-start(bf16[584,128]{1,0:T(8,128)(2,1)} %get-tuple-element.28), channel_id=1, source_target_pairs={{8,0},{0,4},{4,12},{12,8},{9,1},{1,5},{5,13},{13,9},{10,2},{2,6},{... | collective-permute-start | bytes 448520 | tf_op jit(solution)/shard_map/ppermute | solution.py:296
  22.3 1.5 %collective-permute-start.1 = (bf16[584,128]{1,0:T(8,128)(2,1)}, bf16[584,128]{1,0:T(8,128)(2,1)S(1)}, u32[]{:S(2)}, u32[]{:S(2)}) collective-permute-start(bf16[584,128]{1,0:T(8,128)(2,1)} %get-tuple-element.28), channel_id=1, source_target_pairs={{0,2},{2,0},{1,3},{3,1},{4,6},{6,4},{5,7},{7,5},{8,10},{10,8},{9,1... | collective-permute-start | bytes 448520 | tf_op jit(solution)/shard_map/ppermute | solution.py:299
  23.7 2.6 %collective-permute-start.7 = (bf16[576,128]{1,0:T(8,128)(2,1)}, bf16[576,128]{1,0:T(8,128)(2,1)S(1)}, u32[]{:S(2)}, u32[]{:S(2)}) collective-permute-start(bf16[576,128]{1,0:T(8,128)(2,1)} %get-tuple-element.33), channel_id=1, source_target_pairs={{8,0},{0,4},{4,12},{12,8},{9,1},{1,5},{5,13},{13,9},{10,2},{2,6},{... | collective-permute-start | bytes 442376 | tf_op jit(solution)/shard_map/ppermute | solution.py:296
  26.3 0.5 collective-permute-start.8
  26.9 1.1 %collective-permute-done.refs_4_ = bf16[584,128]{1,0:T(8,128)(2,1)S(1)} collective-permute-done((bf16[584,128]{1,0:T(8,128)(2,1)}, bf16[584,128]{1,0:T(8,128)(2,1)S(1)}, u32[]{:S(2)}, u32[]{:S(2)}) %collective-permute-start) | collective-permute-done | bytes 149536 | tf_op jit(solution)/shard_map/ppermute | solution.py:296
  27.9 0.0 collective-permute-done.1.refs_0_
  27.9 3.9 %collective-permute-start.2 = (bf16[584,128]{1,0:T(8,128)(2,1)S(1)}, bf16[584,128]{1,0:T(8,128)(2,1)S(1)}, u32[]{:S(2)}, u32[]{:S(2)}) collective-permute-start(bf16[584,128]{1,0:T(8,128)(2,1)S(1)} %collective-permute-done.refs_4_), channel_id=1, source_target_pairs={{8,0},{0,4},{4,12},{12,8},{9,1},{1,5},{5,13},{13,9},{10,2},{2,6},{... | collective-permute-start | bytes 448520 | tf_op jit(solution)/shard_map/ppermute | solution.py:296
  31.9 1.5 %collective-permute-start.3 = (bf16[584,128]{1,0:T(8,128)(2,1)S(1)}, bf16[584,128]{1,0:T(8,128)(2,1)S(1)}, u32[]{:S(2)}, u32[]{:S(2)}) collective-permute-start(bf16[584,128]{1,0:T(8,128)(2,1)S(1)} %collective-permute-done.refs_4_), channel_id=1, source_target_pairs={{0,2},{2,0},{1,3},{3,1},{4,6},{6,4},{5,7},{7,5},{8,10},{10,8},{9,1... | collective-permute-start | bytes 448520 | tf_op jit(solution)/shard_map/ppermute | solution.py:299
  33.4 0.0 collective-permute-start.6
  33.4 0.0 collective-permute-done.7.refs_5_
  33.4 0.0 collective-permute-done.8.refs_1_
  33.4 0.6 %collective-permute-start.10 = (bf16[576,128]{1,0:T(8,128)(2,1)S(1)}, bf16[576,128]{1,0:T(8,128)(2,1)S(1)}, u32[]{:S(2)}, u32[]{:S(2)}) collective-permute-start(bf16[576,128]{1,0:T(8,128)(2,1)S(1)} %collective-permute-done.7.refs_5_), channel_id=1, source_target_pairs={{0,2},{2,0},{1,3},{3,1},{4,6},{6,4},{5,7},{7,5},{8,10},{10,8},{9,1... | collective-permute-start | bytes 442376 | tf_op jit(solution)/shard_map/ppermute | solution.py:299
  34.0 1.7 %collective-permute-start.9 = (bf16[576,128]{1,0:T(8,128)(2,1)S(1)}, bf16[576,128]{1,0:T(8,128)(2,1)S(1)}, u32[]{:S(2)}, u32[]{:S(2)}) collective-permute-start(bf16[576,128]{1,0:T(8,128)(2,1)S(1)} %collective-permute-done.7.refs_5_), channel_id=1, source_target_pairs={{8,0},{0,4},{4,12},{12,8},{9,1},{1,5},{5,13},{13,9},{10,2},{2,6},{... | collective-permute-start | bytes 442376 | tf_op jit(solution)/shard_map/ppermute | solution.py:296
  35.7 0.0 collective-permute-done.2.refs_6_
  35.7 1.9 %collective-permute-done.3.refs_2_ = bf16[584,128]{1,0:T(8,128)(2,1)S(1)} collective-permute-done((bf16[584,128]{1,0:T(8,128)(2,1)S(1)}, bf16[584,128]{1,0:T(8,128)(2,1)S(1)}, u32[]{:S(2)}, u32[]{:S(2)}) %collective-permute-start.3) | collective-permute-done | bytes 149536 | tf_op jit(solution)/shard_map/ppermute | solution.py:299
  37.6 0.9 %collective-permute-start.4 = (bf16[584,128]{1,0:T(8,128)(2,1)S(1)}, bf16[584,128]{1,0:T(8,128)(2,1)S(1)}, u32[]{:S(2)}, u32[]{:S(2)}) collective-permute-start(bf16[584,128]{1,0:T(8,128)(2,1)S(1)} %collective-permute-done.2.refs_6_), channel_id=1, source_target_pairs={{8,0},{0,4},{4,12},{12,8},{9,1},{1,5},{5,13},{13,9},{10,2},{2,6},{... | collective-permute-start | bytes 448520 | tf_op jit(solution)/shard_map/ppermute | solution.py:296
  38.5 2.5 %collective-permute-start.5 = (bf16[584,128]{1,0:T(8,128)(2,1)S(1)}, bf16[584,128]{1,0:T(8,128)(2,1)S(1)}, u32[]{:S(2)}, u32[]{:S(2)}) collective-permute-start(bf16[584,128]{1,0:T(8,128)(2,1)S(1)} %collective-permute-done.2.refs_6_), channel_id=1, source_target_pairs={{0,2},{2,0},{1,3},{3,1},{4,6},{6,4},{5,7},{7,5},{8,10},{10,8},{9,1... | collective-permute-start | bytes 448520 | tf_op jit(solution)/shard_map/ppermute | solution.py:299
  40.9 0.0 collective-permute-done.10.refs_3_
  40.9 0.7 %collective-permute-done.9.refs_7_ = bf16[576,128]{1,0:T(8,128)(2,1)S(1)} collective-permute-done((bf16[576,128]{1,0:T(8,128)(2,1)S(1)}, bf16[576,128]{1,0:T(8,128)(2,1)S(1)}, u32[]{:S(2)}, u32[]{:S(2)}) %collective-permute-start.9) | collective-permute-done | bytes 147488 | tf_op jit(solution)/shard_map/ppermute | solution.py:296
  41.6 0.8 %collective-permute-start.12 = (bf16[576,128]{1,0:T(8,128)(2,1)S(1)}, bf16[576,128]{1,0:T(8,128)(2,1)S(1)}, u32[]{:S(2)}, u32[]{:S(2)}) collective-permute-start(bf16[576,128]{1,0:T(8,128)(2,1)S(1)} %collective-permute-done.9.refs_7_), channel_id=1, source_target_pairs={{8,0},{0,4},{4,12},{12,8},{9,1},{1,5},{5,13},{13,9},{10,2},{2,6},{... | collective-permute-start | bytes 442376 | tf_op jit(solution)/shard_map/ppermute | solution.py:296
  42.4 1.7 %collective-permute-start.13 = (bf16[576,128]{1,0:T(8,128)(2,1)S(1)}, bf16[576,128]{1,0:T(8,128)(2,1)S(1)}, u32[]{:S(2)}, u32[]{:S(2)}) collective-permute-start(bf16[576,128]{1,0:T(8,128)(2,1)S(1)} %collective-permute-done.9.refs_7_), channel_id=1, source_target_pairs={{0,2},{2,0},{1,3},{3,1},{4,6},{6,4},{5,7},{7,5},{8,10},{10,8},{9,1... | collective-permute-start | bytes 442376 | tf_op jit(solution)/shard_map/ppermute | solution.py:299
  44.1 0.0 collective-permute-done.6.other.left
  44.1 0.0 copy-start
  44.1 1.0 %copy-done = bf16[1160,128]{1,0:T(8,128)(2,1)S(1)} copy-done((bf16[1160,128]{1,0:T(8,128)(2,1)S(1)}, bf16[1160,128]{1,0:T(8,128)(2,1)}, u32[]{:S(2)}) %copy-start) | copy-done | bytes 296984
  45.0 3.2 %shard_map.38 = (f32[192,896]{1,0:T(8,128)S(1)}, f32[192,896]{1,0:T(8,128)S(1)}) custom-call(bf16[1160,128]{1,0:T(8,128)(2,1)S(1)} %copy-done, bf16[1160,128]{1,0:T(8,128)(2,1)S(1)} %collective-permute-done.6.other.left, bf16[584,128]{1,0:T(8,128)(2,1)S(1)} %collective-permute-done.1.refs_0_, bf16[576,128]{1,0:T(8,128)(2,1)S(1)} %collective-permute-done.8.refs_1_, ...), custom_call_target="tpu_custom_call" | custom-call | tf_op jit(solution)/shard_map/pallas_call | solution.py:226
  48.2 0.0 collective-permute-done.4.refs_2_
  48.2 0.0 collective-permute-done.5.refs_0_
  48.2 0.4 collective-permute-start.11
  48.6 0.0 collective-permute-done.12.refs_3_
  48.6 0.0 collective-permute-done.13.refs_1_
  48.6 1.2 %collective-permute-start.14 = (bf16[576,128]{1,0:T(8,128)(2,1)S(1)}, bf16[576,128]{1,0:T(8,128)(2,1)S(1)}, u32[]{:S(2)}, u32[]{:S(2)}) collective-permute-start(bf16[576,128]{1,0:T(8,128)(2,1)S(1)} %collective-permute-done.13.refs_1_), channel_id=1, source_target_pairs={{8,0},{0,4},{4,12},{12,8},{9,1},{1,5},{5,13},{13,9},{10,2},{2,6},{... | collective-permute-start | bytes 442376 | tf_op jit(solution)/shard_map/ppermute | solution.py:296
  49.8 1.4 %shard_map.39 = (f32[192,896]{1,0:T(8,128)S(1)}, f32[192,896]{1,0:T(8,128)S(1)}) custom-call(bf16[1160,128]{1,0:T(8,128)(2,1)S(1)} %copy-done, bf16[1160,128]{1,0:T(8,128)(2,1)S(1)} %collective-permute-done.6.other.left, bf16[584,128]{1,0:T(8,128)(2,1)S(1)} %collective-permute-done.5.refs_0_, ...), custom_call_target="tpu_custom_call", output_to_operand_aliasing={{0}: (6, {}), {1}: (7, {})} | custom-call | tf_op jit(solution)/shard_map/pallas_call | solution.py:226
  51.3 3.4 %collective-permute-done.14.refs_1_ = bf16[576,128]{1,0:T(8,128)(2,1)S(1)} collective-permute-done((bf16[576,128]{1,0:T(8,128)(2,1)S(1)}, bf16[576,128]{1,0:T(8,128)(2,1)S(1)}, u32[]{:S(2)}, u32[]{:S(2)}) %collective-permute-start.14) | collective-permute-done | bytes 147488 | tf_op jit(solution)/shard_map/ppermute | solution.py:296
  54.7 0.0 collective-permute-done.11.refs_0_
  54.7 0.0 copy-start.1
  54.7 0.6 %shard_map.41 = f32[192,896]{1,0:T(8,128)S(1)} custom-call(bf16[1160,128]{1,0:T(8,128)(2,1)S(1)} %collective-permute-done.6.other.left, bf16[584,128]{1,0:T(8,128)(2,1)S(1)} %collective-permute-done.11.refs_0_, bf16[576,128]{1,0:T(8,128)(2,1)S(1)} %collective-permute-done.14.refs_1_, ...), custom_call_target="tpu_custom_call", output_to_operand_aliasing={{}: (3, {})} | custom-call | tf_op jit(solution)/shard_map/pallas_call | solution.py:226
  55.3 0.1 collective-permute-start.15
  55.4 0.3 copy-done.1
  55.6 0.6 %shard_map.40.mine = f32[192,896]{1,0:T(8,128)S(1)} custom-call(bf16[1160,128]{1,0:T(8,128)(2,1)S(1)} %copy-done.1, bf16[584,128]{1,0:T(8,128)(2,1)S(1)} %collective-permute-done.11.refs_0_, bf16[576,128]{1,0:T(8,128)(2,1)S(1)} %collective-permute-done.14.refs_1_, f32[192,896]{1,0:T(8,128)S(1)} %get-tuple-element.47.refs_2_), custom_call_target="tpu_custom_call", output_to_operand_aliasing={{}: (3, {})} | custom-call | tf_op jit(solution)/shard_map/pallas_call | solution.py:226
  56.3 1.3 %collective-permute-done.15.theirs = f32[192,896]{1,0:T(8,128)S(1)} collective-permute-done((f32[192,896]{1,0:T(8,128)S(1)}, f32[192,896]{1,0:T(8,128)S(1)}, u32[]{:S(2)}, u32[]{:S(2)}) %collective-permute-start.15) | collective-permute-done | bytes 688160 | tf_op jit(solution)/shard_map/ppermute | solution.py:302
  57.5 0.8 %shard_map.42 = bf16[192,768]{1,0:T(8,128)(2,1)} custom-call(f32[192,896]{1,0:T(8,128)S(1)} %shard_map.40.mine, f32[192,896]{1,0:T(8,128)S(1)} %collective-permute-done.15.theirs), custom_call_target="tpu_custom_call" | custom-call | tf_op jit(solution)/shard_map/pallas_call | solution.py:226
Async XLA Ops:
  19.2 8.8 %collective-permute-start = (bf16[584,128]{1,0:T(8,128)(2,1)}, bf16[584,128]{1,0:T(8,128)(2,1)S(1)}, u32[]{:S(2)}, u32[]{:S(2)}) collective-permute-start(bf16[584,128]{1,0:T(8,128)(2,1)} %get-tuple-element.28), channel_id=1, source_target_pairs={{8,0},{0,4},{4,12},{12,8},{9,1},{1,5},{5,13},{13,9},{10,2},{2,6},{... | collective-permute-start | bytes 448520 | tf_op jit(solution)/shard_map/ppermute | solution.py:296
  22.3 5.7 %collective-permute-start.1 = (bf16[584,128]{1,0:T(8,128)(2,1)}, bf16[584,128]{1,0:T(8,128)(2,1)S(1)}, u32[]{:S(2)}, u32[]{:S(2)}) collective-permute-start(bf16[584,128]{1,0:T(8,128)(2,1)} %get-tuple-element.28), channel_id=1, source_target_pairs={{0,2},{2,0},{1,3},{3,1},{4,6},{6,4},{5,7},{7,5},{8,10},{10,8},{9,1... | collective-permute-start | bytes 448520 | tf_op jit(solution)/shard_map/ppermute | solution.py:299
  23.7 9.6 %collective-permute-start.7 = (bf16[576,128]{1,0:T(8,128)(2,1)}, bf16[576,128]{1,0:T(8,128)(2,1)S(1)}, u32[]{:S(2)}, u32[]{:S(2)}) collective-permute-start(bf16[576,128]{1,0:T(8,128)(2,1)} %get-tuple-element.33), channel_id=1, source_target_pairs={{8,0},{0,4},{4,12},{12,8},{9,1},{1,5},{5,13},{13,9},{10,2},{2,6},{... | collective-permute-start | bytes 442376 | tf_op jit(solution)/shard_map/ppermute | solution.py:296
  26.3 7.0 %collective-permute-start.8 = (bf16[576,128]{1,0:T(8,128)(2,1)}, bf16[576,128]{1,0:T(8,128)(2,1)S(1)}, u32[]{:S(2)}, u32[]{:S(2)}) collective-permute-start(bf16[576,128]{1,0:T(8,128)(2,1)} %get-tuple-element.33), channel_id=1, source_target_pairs={{0,2},{2,0},{1,3},{3,1},{4,6},{6,4},{5,7},{7,5},{8,10},{10,8},{9,1... | collective-permute-start | bytes 442376 | tf_op jit(solution)/shard_map/ppermute | solution.py:299
  27.9 7.7 %collective-permute-start.2 = (bf16[584,128]{1,0:T(8,128)(2,1)S(1)}, bf16[584,128]{1,0:T(8,128)(2,1)S(1)}, u32[]{:S(2)}, u32[]{:S(2)}) collective-permute-start(bf16[584,128]{1,0:T(8,128)(2,1)S(1)} %collective-permute-done.refs_4_), channel_id=1, source_target_pairs={{8,0},{0,4},{4,12},{12,8},{9,1},{1,5},{5,13},{13,9},{10,2},{2,6},{... | collective-permute-start | bytes 448520 | tf_op jit(solution)/shard_map/ppermute | solution.py:296
  31.9 5.7 %collective-permute-start.3 = (bf16[584,128]{1,0:T(8,128)(2,1)S(1)}, bf16[584,128]{1,0:T(8,128)(2,1)S(1)}, u32[]{:S(2)}, u32[]{:S(2)}) collective-permute-start(bf16[584,128]{1,0:T(8,128)(2,1)S(1)} %collective-permute-done.refs_4_), channel_id=1, source_target_pairs={{0,2},{2,0},{1,3},{3,1},{4,6},{6,4},{5,7},{7,5},{8,10},{10,8},{9,1... | collective-permute-start | bytes 448520 | tf_op jit(solution)/shard_map/ppermute | solution.py:299
  33.4 10.7 %collective-permute-start.6 = (bf16[1160,128]{1,0:T(8,128)(2,1)}, bf16[1160,128]{1,0:T(8,128)(2,1)S(1)}, u32[]{:S(2)}, u32[]{:S(2)}) collective-permute-start(bf16[1160,128]{1,0:T(8,128)(2,1)} %get-tuple-element.27.own.left), channel_id=1, source_target_pairs={{0,1},{1,0},{2,3},{3,2},{4,5},{5,4},{6,7},{7,6},{8,9},{9,8},{10,11... | collective-permute-start | bytes 890888 | tf_op jit(solution)/shard_map/ppermute | solution.py:302
  33.4 7.5 %collective-permute-start.10 = (bf16[576,128]{1,0:T(8,128)(2,1)S(1)}, bf16[576,128]{1,0:T(8,128)(2,1)S(1)}, u32[]{:S(2)}, u32[]{:S(2)}) collective-permute-start(bf16[576,128]{1,0:T(8,128)(2,1)S(1)} %collective-permute-done.7.refs_5_), channel_id=1, source_target_pairs={{0,2},{2,0},{1,3},{3,1},{4,6},{6,4},{5,7},{7,5},{8,10},{10,8},{9,1... | collective-permute-start | bytes 442376 | tf_op jit(solution)/shard_map/ppermute | solution.py:299
  34.0 7.6 %collective-permute-start.9 = (bf16[576,128]{1,0:T(8,128)(2,1)S(1)}, bf16[576,128]{1,0:T(8,128)(2,1)S(1)}, u32[]{:S(2)}, u32[]{:S(2)}) collective-permute-start(bf16[576,128]{1,0:T(8,128)(2,1)S(1)} %collective-permute-done.7.refs_5_), channel_id=1, source_target_pairs={{8,0},{0,4},{4,12},{12,8},{9,1},{1,5},{5,13},{13,9},{10,2},{2,6},{... | collective-permute-start | bytes 442376 | tf_op jit(solution)/shard_map/ppermute | solution.py:296
  37.6 10.6 %collective-permute-start.4 = (bf16[584,128]{1,0:T(8,128)(2,1)S(1)}, bf16[584,128]{1,0:T(8,128)(2,1)S(1)}, u32[]{:S(2)}, u32[]{:S(2)}) collective-permute-start(bf16[584,128]{1,0:T(8,128)(2,1)S(1)} %collective-permute-done.2.refs_6_), channel_id=1, source_target_pairs={{8,0},{0,4},{4,12},{12,8},{9,1},{1,5},{5,13},{13,9},{10,2},{2,6},{... | collective-permute-start | bytes 448520 | tf_op jit(solution)/shard_map/ppermute | solution.py:296
  38.5 9.8 %collective-permute-start.5 = (bf16[584,128]{1,0:T(8,128)(2,1)S(1)}, bf16[584,128]{1,0:T(8,128)(2,1)S(1)}, u32[]{:S(2)}, u32[]{:S(2)}) collective-permute-start(bf16[584,128]{1,0:T(8,128)(2,1)S(1)} %collective-permute-done.2.refs_6_), channel_id=1, source_target_pairs={{0,2},{2,0},{1,3},{3,1},{4,6},{6,4},{5,7},{7,5},{8,10},{10,8},{9,1... | collective-permute-start | bytes 448520 | tf_op jit(solution)/shard_map/ppermute | solution.py:299
  41.6 7.1 %collective-permute-start.12 = (bf16[576,128]{1,0:T(8,128)(2,1)S(1)}, bf16[576,128]{1,0:T(8,128)(2,1)S(1)}, u32[]{:S(2)}, u32[]{:S(2)}) collective-permute-start(bf16[576,128]{1,0:T(8,128)(2,1)S(1)} %collective-permute-done.9.refs_7_), channel_id=1, source_target_pairs={{8,0},{0,4},{4,12},{12,8},{9,1},{1,5},{5,13},{13,9},{10,2},{2,6},{... | collective-permute-start | bytes 442376 | tf_op jit(solution)/shard_map/ppermute | solution.py:296
  42.4 6.3 %collective-permute-start.13 = (bf16[576,128]{1,0:T(8,128)(2,1)S(1)}, bf16[576,128]{1,0:T(8,128)(2,1)S(1)}, u32[]{:S(2)}, u32[]{:S(2)}) collective-permute-start(bf16[576,128]{1,0:T(8,128)(2,1)S(1)} %collective-permute-done.9.refs_7_), channel_id=1, source_target_pairs={{0,2},{2,0},{1,3},{3,1},{4,6},{6,4},{5,7},{7,5},{8,10},{10,8},{9,1... | collective-permute-start | bytes 442376 | tf_op jit(solution)/shard_map/ppermute | solution.py:299
  44.1 1.0 %copy-start = (bf16[1160,128]{1,0:T(8,128)(2,1)S(1)}, bf16[1160,128]{1,0:T(8,128)(2,1)}, u32[]{:S(2)}) copy-start(bf16[1160,128]{1,0:T(8,128)(2,1)} %get-tuple-element.27.own.left) | copy-start | bytes 890884
  48.2 6.4 %collective-permute-start.11 = (bf16[584,128]{1,0:T(8,128)(2,1)S(1)}, bf16[584,128]{1,0:T(8,128)(2,1)S(1)}, u32[]{:S(2)}, u32[]{:S(2)}) collective-permute-start(bf16[584,128]{1,0:T(8,128)(2,1)S(1)} %collective-permute-done.4.refs_2_), channel_id=1, source_target_pairs={{0,2},{2,0},{1,3},{3,1},{4,6},{6,4},{5,7},{7,5},{8,10},{10,8},{9,1... | collective-permute-start | bytes 448520 | tf_op jit(solution)/shard_map/ppermute | solution.py:299
  48.6 6.0 %collective-permute-start.14 = (bf16[576,128]{1,0:T(8,128)(2,1)S(1)}, bf16[576,128]{1,0:T(8,128)(2,1)S(1)}, u32[]{:S(2)}, u32[]{:S(2)}) collective-permute-start(bf16[576,128]{1,0:T(8,128)(2,1)S(1)} %collective-permute-done.13.refs_1_), channel_id=1, source_target_pairs={{8,0},{0,4},{4,12},{12,8},{9,1},{1,5},{5,13},{13,9},{10,2},{2,6},{... | collective-permute-start | bytes 442376 | tf_op jit(solution)/shard_map/ppermute | solution.py:296
  54.7 1.0 %copy-start.1 = (bf16[1160,128]{1,0:T(8,128)(2,1)S(1)}, bf16[1160,128]{1,0:T(8,128)(2,1)}, u32[]{:S(2)}) copy-start(bf16[1160,128]{1,0:T(8,128)(2,1)} %get-tuple-element.27.own.left) | copy-start | bytes 890884
  55.3 2.2 %collective-permute-start.15 = (f32[192,896]{1,0:T(8,128)S(1)}, f32[192,896]{1,0:T(8,128)S(1)}, u32[]{:S(2)}, u32[]{:S(2)}) collective-permute-start(f32[192,896]{1,0:T(8,128)S(1)} %shard_map.41), channel_id=1, source_target_pairs={{0,1},{1,0},{2,3},{3,2},{4,5},{5,4},{6,7},{7,6},{8,9},{9,8},{10,11... | collective-permute-start | bytes 2064392 | tf_op jit(solution)/shard_map/ppermute | solution.py:302

commit v7 on v0

v7 whole, which is shorter than its diff:
```python
import functools

import jax
import jax.numpy as jnp
from jax import lax
from jax.experimental import pallas as pl
from jax.experimental.pallas import tpu as pltpu
from jax.sharding import PartitionSpec as P

F32 = jnp.float32
BF16 = jnp.bfloat16
VMEM_BYTES = 24 * 1024 * 1024
GATHER_LIMIT = 8 * 1024 * 1024


def unit_scale(rows_in):
    wide = rows_in.astype(F32)
    return lax.rsqrt(jnp.sum(wide * wide, axis=1) + 1e-06)


def tile_weights(left_rows, left_clust, left_scale, right_rows, right_clust, right_scale):
    grams = lax.dot_general(
        left_rows, right_rows, (((1,), (1,)), ((), ())), preferred_element_type=F32
    )
    cosine = grams * left_scale[:, None] * right_scale[None, :]
    same = (left_clust[:, None] == right_clust[None, :]).astype(F32)
    return jax.nn.sigmoid(8.0 * cosine - 2.0) * same


def by_group(embeddings, group_of, cluster_id):
    rows_here, width = embeddings.shape
    groups = lax.axis_size("sub") * lax.axis_size("pair")
    capacity = 2 * rows_here // groups
    slots = groups * capacity
    target = group_of[:, 0]
    onehot = (target[:, None] == jnp.arange(groups, dtype=jnp.int32)[None, :]).astype(jnp.int32)
    position = jnp.sum((jnp.cumsum(onehot, axis=0) - onehot) * onehot, axis=1)
    send_rows = jnp.zeros((groups, capacity, width), BF16).at[target, position].set(embeddings)
    send_clust = jnp.full((groups, capacity), -1, jnp.int32).at[target, position].set(cluster_id)
    recv_rows, recv_clust = (
        lax.all_to_all(send_rows, ("sub", "pair"), split_axis=0, concat_axis=0, tiled=True),
        lax.all_to_all(send_clust, ("sub", "pair"), split_axis=0, concat_axis=0, tiled=True),
    )
    own_rows = recv_rows.reshape(slots, width)
    own_clust = recv_clust.reshape(slots)
    own_scale = unit_scale(own_rows)
    piece_rows = lax.all_gather(own_rows, "blk", axis=0, tiled=True)
    piece_clust = lax.all_gather(own_clust, "blk", axis=0, tiled=True)
    weight = tile_weights(
        own_rows, own_clust, own_scale, piece_rows, piece_clust, unit_scale(piece_rows)
    )
    numer = jnp.dot(weight.astype(BF16), piece_rows, preferred_element_type=F32)
    denom = jnp.sum(weight, axis=1)
    result = (numer / denom[:, None]).astype(BF16).reshape(groups, capacity, width)
    returned = lax.all_to_all(result, ("sub", "pair"), split_axis=0, concat_axis=0, tiled=True)
    return returned[target, position]


def diagonal(size):
    shape = (size, size)
    return lax.broadcasted_iota(jnp.int32, shape, 0) == lax.broadcasted_iota(jnp.int32, shape, 1)


def to_column(row):
    size = row.shape[1]
    return jnp.sum(jnp.where(diagonal(size), row, jnp.zeros_like(row)), axis=1, keepdims=True)


def to_row(column):
    size = column.shape[0]
    return jnp.sum(jnp.where(diagonal(size), column, jnp.zeros_like(column)), axis=0, keepdims=True)


def scale_column(rows):
    wide = rows.astype(F32)
    return lax.rsqrt(jnp.sum(wide * wide, axis=1, keepdims=True) + 1e-06)


def name_lines(rows_here):
    return -(-rows_here // 128)


def pack_kernel(rows, group, cluster, out):
    rows_here, width = rows.shape
    slabs = width // 128
    for slab in range(slabs):
        out[slab * rows_here : (slab + 1) * rows_here, :] = rows[
            :, slab * 128 : (slab + 1) * 128
        ]
    line_at = lax.broadcasted_iota(jnp.int32, (8, 128), 0)
    lines = name_lines(rows_here)
    named = jnp.zeros((8, 128), jnp.int32)
    for kind, ref in enumerate((group, cluster)):
        for line in range(lines):
            part = ref[:, line * 128 : (line + 1) * 128]
            if part.shape[1] < 128:
                rest = jnp.zeros((1, 128 - part.shape[1]), jnp.int32)
                part = jnp.concatenate([part, rest], axis=1)
            named = jnp.where(line_at == kind * lines + line, part, named)
    out[slabs * rows_here :, :] = named.astype(F32).astype(BF16)


def from_slabs(ref, count):
    slabs = [ref[top : top + count, :] for top in range(0, ref.shape[0] // count * count, count)]
    return jnp.concatenate(slabs, axis=1)


def key_row(ref, rows_here):
    wide = ref[ref.shape[0] - 8 :, :].astype(F32)
    lines = name_lines(rows_here)
    kinds = []
    for kind in range(2):
        parts = [wide[kind * lines + line : kind * lines + line + 1, :] for line in range(lines)]
        kinds.append(jnp.concatenate(parts, axis=1)[:, :rows_here])
    return kinds[0] * 256.0 + kinds[1]


def computes():
    return lax.axis_index("pair") == 0


def with_scale(ref, rows_here):
    rows = from_slabs(ref, rows_here)
    return rows, key_row(ref, rows_here), to_row(scale_column(rows))


def add_blocks(left, info, blocks, numer, denom):
    key = info[:, 0:1]
    scale = info[:, 1:2]
    for right_rows, right_key, right_scale in blocks:
        grams = lax.dot_general(
            left, right_rows, (((1,), (1,)), ((), ())), preferred_element_type=F32
        )
        half = jnp.tanh(grams * scale * right_scale - 1.0)
        weight = jnp.where(key == right_key, 0.5 + 0.5 * half, 0.0)
        add = jnp.dot(weight.astype(BF16), right_rows, preferred_element_type=F32)
        add_denom = jnp.sum(weight, axis=1, keepdims=True)
        numer = add if numer is None else numer + add
        denom = add_denom if denom is None else denom + add_denom
    return numer, denom


def left_rows(own, other, rows_here):
    return jnp.concatenate([from_slabs(own, rows_here), from_slabs(other, rows_here)], axis=0)


def start_kernel(own, other, numer_out, denom_out, info_out):
    @pl.when(computes())
    def _():
        rows_here = numer_out.shape[0] // 2
        left = left_rows(own, other, rows_here)
        key = jnp.concatenate([to_column(key_row(ref, rows_here)) for ref in (own, other)], axis=0)
        scale = scale_column(left)
        lane = lax.broadcasted_iota(jnp.int32, info_out.shape, 1)
        info = jnp.where(lane == 0, key, 4.0 * scale)
        info_out[...] = info
        blocks = [
            (
                left[top : top + rows_here],
                key_row(ref, rows_here),
                to_row(scale[top : top + rows_here]),
            )
            for top, ref in ((0, own), (rows_here, other))
        ]
        numer, denom = add_blocks(left, info, blocks, None, None)
        numer_out[...] = numer
        denom_out[...] = jnp.broadcast_to(denom, denom_out.shape)


def add_kernel(n_blocks, own, other, info, *refs):
    numer_in, denom_in, numer_out, denom_out = refs[n_blocks:]

    @pl.when(computes())
    def _():
        rows_here = numer_out.shape[0] // 2
        left = left_rows(own, other, rows_here)
        blocks = [with_scale(ref, rows_here) for ref in refs[:n_blocks]]
        numer, denom = add_blocks(left, info[...], blocks, numer_in[...], denom_in[:, 0:1])
        numer_out[...] = numer
        denom_out[...] = jnp.broadcast_to(denom, denom_out.shape)


def last_kernel(own, other, info, right, numer_in, denom_in, mine, theirs):
    @pl.when(computes())
    def _():
        rows_here = mine.shape[0]
        left = left_rows(own, other, rows_here)
        blocks = [with_scale(right, rows_here)]
        numer, denom = add_blocks(left, info[...], blocks, numer_in[...], denom_in[:, 0:1])
        means = (numer / denom).astype(BF16)
        mine[...] = means[:rows_here]
        theirs[...] = means[rows_here:]


def out_kernel(mine, back, out):
    @pl.when(computes())
    def _():
        out[...] = mine[...]

    @pl.when(jnp.logical_not(computes()))
    def _():
        out[...] = back[...]


def whole_in_vmem(count):
    return [pl.BlockSpec(memory_space=pltpu.VMEM)] * count


def call(kernel, shapes, args, aliases={}):
    return pl.pallas_call(
        kernel,
        out_shape=[jax.ShapeDtypeStruct(shape, dtype) for shape, dtype in shapes],
        in_specs=whole_in_vmem(len(args)),
        out_specs=whole_in_vmem(len(shapes)),
        input_output_aliases=aliases,
        compiler_params=pltpu.CompilerParams(vmem_limit_bytes=VMEM_BYTES),
    )(*args)


def add_to(total, left, right):
    args = [*left, *right, *total]
    at = len(args) - 2
    shapes = [(array.shape, F32) for array in total]
    return call(functools.partial(add_kernel, len(right)), shapes, args, {at: 0, at + 1: 1})


def folded_ring(size):
    return [0] + list(range(1, size, 2)) + list(range(2, size, 2))[::-1]


def together(*arrays):
    return lax.optimization_barrier(arrays)


def by_block(embeddings, group_of, cluster_id):
    rows_here, width = embeddings.shape
    n_blk = lax.axis_size("blk")
    order = folded_ring(n_blk)
    line = (1, rows_here)

    def along(rows, core):
        hops = [(2 * order[i - 1] + core, 2 * order[i] + core) for i in range(n_blk)]
        return lax.ppermute(rows, ("blk", "pair"), hops)

    def across(rows):
        return lax.ppermute(rows, ("sub", "pair"), [(1, 2), (3, 0)])

    def hand(rows):
        return lax.ppermute(rows, "pair", [(1, 0)])

    (block,) = call(
        pack_kernel,
        [((width // 128 * rows_here + 8, 128), BF16)],
        [embeddings, group_of.reshape(line), cluster_id.reshape(line)],
    )
    other = lax.ppermute(block, "pair", [(0, 1), (1, 0)])
    moving = [block, other]
    crossed = [across(block), across(other)]
    handed = [None, None]
    moving += [along(block, 1), along(other, 1)]
    numer, denom, info = call(
        start_kernel,
        [((2 * rows_here, width), F32), ((2 * rows_here, 128), F32), ((2 * rows_here, 128), F32)],
        [block, other],
    )
    left = (block, other, info)
    total = (numer, denom)
    last = 2 * n_blk - 1
    for k in range(2, last + 1):
        ready = [crossed[k - 2]]
        if k > 3:
            ready.append(handed[k - 2])
        moving[k], *rest = together(moving[k], *total, *ready)
        total, ready = rest[:2], rest[2:]
        if k + 2 <= last:
            moving.append(along(moving[k], 1))
        if k < last:
            crossed.append(across(moving[k]))
        else:
            crossed.append(along(crossed[k - 2], 0))
        handed.append(hand(moving[k]))
        total = add_to(total, left, ready)
    total = add_to(total, left, [crossed[last - 1], handed[last - 1], handed[last]])
    mine, theirs = call(
        last_kernel,
        [((rows_here, width), BF16)] * 2,
        [*left, crossed[last], *total],
    )
    back = lax.ppermute(theirs, "pair", [(0, 1)])
    (out,) = call(out_kernel, [((rows_here, width), BF16)], [mine, back])
    return out


def per_device(embeddings, group_of, cluster_id):
    rows_here, width = embeddings.shape
    devices = lax.axis_size("blk") * lax.axis_size("sub") * lax.axis_size("pair")
    small = devices * rows_here * width * 2 <= GATHER_LIMIT
    fits = width % 128 == 0 and rows_here % 32 == 0 and rows_here <= 512
    if small and fits and lax.axis_size("sub") == 2 and lax.axis_size("pair") == 2:
        return by_block(embeddings, group_of, cluster_id)
    return by_group(embeddings, group_of, cluster_id)


def solution(mesh):
    return jax.shard_map(
        per_device,
        mesh=mesh,
        in_specs=(
            P(("island", "blk", "sub", "pair"), None),
            P(("island", "blk", "sub", "pair"), None),
            P(("island", "blk", "sub", "pair")),
        ),
        out_specs=P(("island", "blk", "sub", "pair"), None),
        check_vma=False,
    )
```

time: 122 us -> 56.1 us (0.46)
  blocking collectives: 44.6 us -> 0 us
  local copies, waits for them, and re-layouts: 32.6 us -> 2.32 us
  starting transfers between devices: 0.01 us -> 25.4 us
  between operations: 13.5 us -> 0.37 us
  Pallas kernels: 0 us -> 13.1 us
  waiting for transfers between devices: 21.5 us -> 14.5 us
  other arithmetic: 6.66 us -> 0 us
  matrix products: 2.65 us -> 0 us
    all_to_all x3 -> x0, blocking collectives: 31.8 us -> none  [the longest x1 13.7 us: per_device(): lax.all_to_all(send_rows, ('sub', 'pair'), split_axis=0, concat_axis=0, t...]
    scatter x2 -> x0, local copies, waits for them, and re-layouts: 27.5 us -> none  [the longest x1 18.1 us: per_device(): jnp.zeros((groups, capacity, width), jnp.bfloat16).at[target, position]]
    ppermute x0 -> x22, starting transfers between devices: none -> 25.4 us  [the longest x7 9.03 us: across(): return lax.ppermute(rows, ('sub', 'pair'), [(1, 2), (3, 0)])]
    all_gather x1 -> x0, waiting for transfers between devices: 21.5 us -> none  [per_device(): piece_rows = lax.all_gather(own_rows, 'blk', axis=0, tiled=True)]
    ppermute x0 -> x22, waiting for transfers between devices: none -> 14.5 us  [the longest x7 9.95 us: across(): return lax.ppermute(rows, ('sub', 'pair'), [(1, 2), (3, 0)])]
    pallas_call x0 -> x11, Pallas kernels: none -> 13.1 us  [call(): pl.pallas_call(kernel, out_shape=[jax.ShapeDtypeStruct(shape, dtype) for...]
    all_gather x1 -> x0, blocking collectives: 12.8 us -> none  [per_device(): piece_clust = lax.all_gather(own_clust, 'blk', axis=0, tiled=True)]
    gather x1 -> x0, local copies, waits for them, and re-layouts: 3.9 us -> none  [per_device(): return returned[target, position]]
  transfers between devices with their start and end apart: 1 -> 22, of which waited for: 1 -> 5; matrix products, arithmetic and copies ran while one was open for 9% -> 0% of each run, Pallas kernels for 0% -> 20%
where the time goes in v7:
time: 56.1 us; the launch traced here: 55.6 us
  starting transfers between devices  25.4 us (45%)
  waiting for transfers between devices  14.5 us (26%)
  Pallas kernels  13.1 us (23%)
  local copies, waits for them, and re-layouts  2.32 us (4%)
    pallas_call x11, Pallas kernels, call(): pl.pallas_call(kernel, out_shape=[jax.ShapeDtypeStruct(shape, dtype) for...  13.1 us
    ppermute x7, waiting for transfers between devices, across(): return lax.ppermute(rows, ('sub', 'pair'), [(1, 2), (3, 0)])  9.95 us
    ppermute x7, starting transfers between devices, across(): return lax.ppermute(rows, ('sub', 'pair'), [(1, 2), (3, 0)])  9.03 us
    ppermute x6, starting transfers between devices, hand(): return lax.ppermute(rows, 'pair', [(1, 0)])  7.74 us
    ppermute x7, starting transfers between devices, along(): return lax.ppermute(rows, ('blk', 'pair'), hops)  6.76 us
    ppermute x7, waiting for transfers between devices, along(): return lax.ppermute(rows, ('blk', 'pair'), hops)  3.31 us
    unnamed x6, local copies, waits for them, and re-layouts  2.32 us
    ppermute x1, starting transfers between devices, by_block(): back = lax.ppermute(theirs, 'pair', [(0, 1)])  1.31 us
  transfers between devices with their start and end apart: 22, of which 5 were waited for; matrix products, arithmetic and copies ran while one was open for 0% of the time, Pallas kernels for 20%

profile of v7, /device:TPU:0, one launch (start us, length us, event | category | flops | bytes accessed | tf_op | source)
XLA Modules:
  0.0 55.6 jit_solution(8025397543554920056)
XLA Ops:
  0.0 0.0 copy-start
  0.0 1.0 %copy-done = bf16[192,768]{1,0:T(8,128)(2,1)S(1)} copy-done((bf16[192,768]{1,0:T(8,128)(2,1)S(1)}, bf16[192,768]{1,0:T(8,128)(2,1)}, u32[]{:S(2)}) %copy-start) | copy-done | bytes 294936
  1.0 0.0 copy-start.1
  1.0 0.7 %copy-done.1 = s32[192,1]{0,1:T(1,128)S(1)} copy-done((s32[192,1]{0,1:T(1,128)S(1)}, s32[192,1]{0,1:T(1,128)}, u32[]{:S(2)}) %copy-start.1) | copy-done | bytes 792
  1.6 0.0 copy-start.2
  1.6 0.7 %copy-done.2 = s32[192]{0:T(256)S(1)} copy-done((s32[192]{0:T(256)S(1)}, s32[192]{0:T(256)}, u32[]{:S(2)}) %copy-start.2) | copy-done | bytes 792
  2.3 0.1 shard_map.37.own
  2.4 0.5 collective-permute-start
  2.9 0.7 %collective-permute-start.2 = (bf16[1160,128]{1,0:T(8,128)(2,1)S(1)}, bf16[1160,128]{1,0:T(8,128)(2,1)S(1)}, u32[]{:S(2)}, u32[]{:S(2)}) collective-permute-start(bf16[1160,128]{1,0:T(8,128)(2,1)S(1)} %shard_map.37.own), channel_id=1, source_target_pairs={{9,1},{1,5},{5,13},{13,9},{11,3},{3,7},{7,15},{15,11},{25,17},{17,... | collective-permute-start | bytes 890888 | tf_op jit(solution)/shard_map/ppermute | solution.py:243
  3.6 1.3 %collective-permute-start.3 = (bf16[1160,128]{1,0:T(8,128)(2,1)S(1)}, bf16[1160,128]{1,0:T(8,128)(2,1)S(1)}, u32[]{:S(2)}, u32[]{:S(2)}) collective-permute-start(bf16[1160,128]{1,0:T(8,128)(2,1)S(1)} %shard_map.37.own), channel_id=1, source_target_pairs={{1,2},{3,0},{5,6},{7,4},{9,10},{11,8},{13,14},{15,12},{17,18},{19,... | collective-permute-start | bytes 890888 | tf_op jit(solution)/shard_map/ppermute | solution.py:246
  4.9 0.0 collective-permute-done.other
  4.9 0.7 %collective-permute-start.1 = (bf16[1160,128]{1,0:T(8,128)(2,1)S(1)}, bf16[1160,128]{1,0:T(8,128)(2,1)S(1)}, u32[]{:S(2)}, u32[]{:S(2)}) collective-permute-start(bf16[1160,128]{1,0:T(8,128)(2,1)S(1)} %collective-permute-done.other), channel_id=1, source_target_pairs={{9,1},{1,5},{5,13},{13,9},{11,3},{3,7},{7,15},{15,11},{25,17},{17,... | collective-permute-start | bytes 890888 | tf_op jit(solution)/shard_map/ppermute | solution.py:243
  5.6 1.3 %collective-permute-start.4 = (bf16[1160,128]{1,0:T(8,128)(2,1)S(1)}, bf16[1160,128]{1,0:T(8,128)(2,1)S(1)}, u32[]{:S(2)}, u32[]{:S(2)}) collective-permute-start(bf16[1160,128]{1,0:T(8,128)(2,1)S(1)} %collective-permute-done.other), channel_id=1, source_target_pairs={{1,2},{3,0},{5,6},{7,4},{9,10},{11,8},{13,14},{15,12},{17,18},{19,... | collective-permute-start | bytes 890888 | tf_op jit(solution)/shard_map/ppermute | solution.py:246
  6.9 1.2 %shard_map.38 = (f32[384,768]{1,0:T(8,128)S(1)}, f32[384,128]{1,0:T(8,128)S(1)}, f32[384,128]{1,0:T(8,128)S(1)}) custom-call(bf16[1160,128]{1,0:T(8,128)(2,1)S(1)} %shard_map.37.own, bf16[1160,128]{1,0:T(8,128)(2,1)S(1)} %collective-permute-done.other), custom_call_target="tpu_custom_call" | custom-call | tf_op jit(solution)/shard_map/pallas_call | solution.py:210
  8.1 0.0 collective-permute-done.2
  8.1 6.3 %collective-permute-done.3.refs_0_ = bf16[1160,128]{1,0:T(8,128)(2,1)S(1)} collective-permute-done((bf16[1160,128]{1,0:T(8,128)(2,1)S(1)}, bf16[1160,128]{1,0:T(8,128)(2,1)S(1)}, u32[]{:S(2)}, u32[]{:S(2)}) %collective-permute-start.3) | collective-permute-done | bytes 296992 | tf_op jit(solution)/shard_map/ppermute | solution.py:246
  14.4 0.7 %collective-permute-start.6 = (bf16[1160,128]{1,0:T(8,128)(2,1)S(1)}, bf16[1160,128]{1,0:T(8,128)(2,1)S(1)}, u32[]{:S(2)}, u32[]{:S(2)}) collective-permute-start(bf16[1160,128]{1,0:T(8,128)(2,1)S(1)} %collective-permute-done.2), channel_id=1, source_target_pairs={{9,1},{1,5},{5,13},{13,9},{11,3},{3,7},{7,15},{15,11},{25,17},{17,... | collective-permute-start | bytes 890888 | tf_op jit(solution)/shard_map/ppermute | solution.py:243
  15.1 1.3 %collective-permute-start.7 = (bf16[1160,128]{1,0:T(8,128)(2,1)S(1)}, bf16[1160,128]{1,0:T(8,128)(2,1)S(1)}, u32[]{:S(2)}, u32[]{:S(2)}) collective-permute-start(bf16[1160,128]{1,0:T(8,128)(2,1)S(1)} %collective-permute-done.2), channel_id=1, source_target_pairs={{1,2},{3,0},{5,6},{7,4},{9,10},{11,8},{13,14},{15,12},{17,18},{19,... | collective-permute-start | bytes 890888 | tf_op jit(solution)/shard_map/ppermute | solution.py:246
  16.4 1.3 %collective-permute-start.8 = (bf16[1160,128]{1,0:T(8,128)(2,1)S(1)}, bf16[1160,128]{1,0:T(8,128)(2,1)S(1)}, u32[]{:S(2)}, u32[]{:S(2)}) collective-permute-start(bf16[1160,128]{1,0:T(8,128)(2,1)S(1)} %collective-permute-done.2), channel_id=1, source_target_pairs={{1,0},{3,2},{5,4},{7,6},{9,8},{11,10},{13,12},{15,14},{17,16},{19,... | collective-permute-start | bytes 890888 | tf_op jit(solution)/shard_map/ppermute | solution.py:249
  17.7 0.9 %shard_map.39 = (f32[384,768]{1,0:T(8,128)S(1)}, f32[384,128]{1,0:T(8,128)S(1)}) custom-call(bf16[1160,128]{1,0:T(8,128)(2,1)S(1)} %shard_map.37.own, bf16[1160,128]{1,0:T(8,128)(2,1)S(1)} %collective-permute-done.other, f32[384,128]{1,0:T(8,128)S(1)} %get-tuple-element.52.info, ...), custom_call_target="tpu_custom_call", output_to_operand_aliasing={{0}: (4, {}), {1}: (5, {})} | custom-call | tf_op jit(solution)/shard_map/pallas_call | solution.py:210
  18.6 0.0 collective-permute-done.1
  18.6 1.3 %collective-permute-done.4.refs_0_ = bf16[1160,128]{1,0:T(8,128)(2,1)S(1)} collective-permute-done((bf16[1160,128]{1,0:T(8,128)(2,1)S(1)}, bf16[1160,128]{1,0:T(8,128)(2,1)S(1)}, u32[]{:S(2)}, u32[]{:S(2)}) %collective-permute-start.4) | collective-permute-done | bytes 296992 | tf_op jit(solution)/shard_map/ppermute | solution.py:246
  20.0 1.3 %collective-permute-start.10 = (bf16[1160,128]{1,0:T(8,128)(2,1)S(1)}, bf16[1160,128]{1,0:T(8,128)(2,1)S(1)}, u32[]{:S(2)}, u32[]{:S(2)}) collective-permute-start(bf16[1160,128]{1,0:T(8,128)(2,1)S(1)} %collective-permute-done.1), channel_id=1, source_target_pairs={{1,0},{3,2},{5,4},{7,6},{9,8},{11,10},{13,12},{15,14},{17,16},{19,... | collective-permute-start | bytes 890888 | tf_op jit(solution)/shard_map/ppermute | solution.py:249
  21.2 0.7 %collective-permute-start.5 = (bf16[1160,128]{1,0:T(8,128)(2,1)S(1)}, bf16[1160,128]{1,0:T(8,128)(2,1)S(1)}, u32[]{:S(2)}, u32[]{:S(2)}) collective-permute-start(bf16[1160,128]{1,0:T(8,128)(2,1)S(1)} %collective-permute-done.1), channel_id=1, source_target_pairs={{9,1},{1,5},{5,13},{13,9},{11,3},{3,7},{7,15},{15,11},{25,17},{17,... | collective-permute-start | bytes 890888 | tf_op jit(solution)/shard_map/ppermute | solution.py:243
  21.9 0.9 %shard_map.40 = (f32[384,768]{1,0:T(8,128)S(1)}, f32[384,128]{1,0:T(8,128)S(1)}) custom-call(bf16[1160,128]{1,0:T(8,128)(2,1)S(1)} %shard_map.37.own, bf16[1160,128]{1,0:T(8,128)(2,1)S(1)} %collective-permute-done.other, f32[384,128]{1,0:T(8,128)S(1)} %get-tuple-element.52.info, ...), custom_call_target="tpu_custom_call", output_to_operand_aliasing={{0}: (4, {}), {1}: (5, {})} | custom-call | tf_op jit(solution)/shard_map/pallas_call | solution.py:210
  22.9 0.0 collective-permute-done.6
  22.9 1.3 %collective-permute-start.9 = (bf16[1160,128]{1,0:T(8,128)(2,1)S(1)}, bf16[1160,128]{1,0:T(8,128)(2,1)S(1)}, u32[]{:S(2)}, u32[]{:S(2)}) collective-permute-start(bf16[1160,128]{1,0:T(8,128)(2,1)S(1)} %collective-permute-done.1), channel_id=1, source_target_pairs={{1,2},{3,0},{5,6},{7,4},{9,10},{11,8},{13,14},{15,12},{17,18},{19,... | collective-permute-start | bytes 890888 | tf_op jit(solution)/shard_map/ppermute | solution.py:246
  24.2 0.0 collective-permute-done.7.refs_0_
  24.2 0.0 collective-permute-done.8.refs_1_
  24.2 0.7 %collective-permute-start.13 = (bf16[1160,128]{1,0:T(8,128)(2,1)S(1)}, bf16[1160,128]{1,0:T(8,128)(2,1)S(1)}, u32[]{:S(2)}, u32[]{:S(2)}) collective-permute-start(bf16[1160,128]{1,0:T(8,128)(2,1)S(1)} %collective-permute-done.6), channel_id=1, source_target_pairs={{9,1},{1,5},{5,13},{13,9},{11,3},{3,7},{7,15},{15,11},{25,17},{17,... | collective-permute-start | bytes 890888 | tf_op jit(solution)/shard_map/ppermute | solution.py:243
  24.9 1.3 %collective-permute-start.14 = (bf16[1160,128]{1,0:T(8,128)(2,1)S(1)}, bf16[1160,128]{1,0:T(8,128)(2,1)S(1)}, u32[]{:S(2)}, u32[]{:S(2)}) collective-permute-start(bf16[1160,128]{1,0:T(8,128)(2,1)S(1)} %collective-permute-done.6), channel_id=1, source_target_pairs={{1,2},{3,0},{5,6},{7,4},{9,10},{11,8},{13,14},{15,12},{17,18},{19,... | collective-permute-start | bytes 890888 | tf_op jit(solution)/shard_map/ppermute | solution.py:246
  26.2 0.0 collective-permute-done.10.refs_1_
  26.2 1.3 %collective-permute-start.15 = (bf16[1160,128]{1,0:T(8,128)(2,1)S(1)}, bf16[1160,128]{1,0:T(8,128)(2,1)S(1)}, u32[]{:S(2)}, u32[]{:S(2)}) collective-permute-start(bf16[1160,128]{1,0:T(8,128)(2,1)S(1)} %collective-permute-done.6), channel_id=1, source_target_pairs={{1,0},{3,2},{5,4},{7,6},{9,8},{11,10},{13,12},{15,14},{17,16},{19,... | collective-permute-start | bytes 890888 | tf_op jit(solution)/shard_map/ppermute | solution.py:249
  27.5 1.6 %shard_map.41 = (f32[384,768]{1,0:T(8,128)S(1)}, f32[384,128]{1,0:T(8,128)S(1)}) custom-call(bf16[1160,128]{1,0:T(8,128)(2,1)S(1)} %shard_map.37.own, bf16[1160,128]{1,0:T(8,128)(2,1)S(1)} %collective-permute-done.other, f32[384,128]{1,0:T(8,128)S(1)} %get-tuple-element.52.info, ...), custom_call_target="tpu_custom_call", output_to_operand_aliasing={{0}: (5, {}), {1}: (6, {})} | custom-call | tf_op jit(solution)/shard_map/pallas_call | solution.py:210
  29.1 0.0 collective-permute-done.5
  29.1 2.3 %collective-permute-done.9.refs_0_ = bf16[1160,128]{1,0:T(8,128)(2,1)S(1)} collective-permute-done((bf16[1160,128]{1,0:T(8,128)(2,1)S(1)}, bf16[1160,128]{1,0:T(8,128)(2,1)S(1)}, u32[]{:S(2)}, u32[]{:S(2)}) %collective-permute-start.9) | collective-permute-done | bytes 296992 | tf_op jit(solution)/shard_map/ppermute | solution.py:246
  31.4 1.3 %collective-permute-start.11 = (bf16[1160,128]{1,0:T(8,128)(2,1)S(1)}, bf16[1160,128]{1,0:T(8,128)(2,1)S(1)}, u32[]{:S(2)}, u32[]{:S(2)}) collective-permute-start(bf16[1160,128]{1,0:T(8,128)(2,1)S(1)} %collective-permute-done.5), channel_id=1, source_target_pairs={{1,2},{3,0},{5,6},{7,4},{9,10},{11,8},{13,14},{15,12},{17,18},{19,... | collective-permute-start | bytes 890888 | tf_op jit(solution)/shard_map/ppermute | solution.py:246
  32.7 0.7 %collective-permute-start.18 = (bf16[1160,128]{1,0:T(8,128)(2,1)S(1)}, bf16[1160,128]{1,0:T(8,128)(2,1)S(1)}, u32[]{:S(2)}, u32[]{:S(2)}) collective-permute-start(bf16[1160,128]{1,0:T(8,128)(2,1)S(1)} %collective-permute-done.5), channel_id=1, source_target_pairs={{9,1},{1,5},{5,13},{13,9},{11,3},{3,7},{7,15},{15,11},{25,17},{17,... | collective-permute-start | bytes 890888 | tf_op jit(solution)/shard_map/ppermute | solution.py:243
  33.4 0.0 collective-permute-done.13
  33.4 1.3 %collective-permute-start.19 = (bf16[1160,128]{1,0:T(8,128)(2,1)S(1)}, bf16[1160,128]{1,0:T(8,128)(2,1)S(1)}, u32[]{:S(2)}, u32[]{:S(2)}) collective-permute-start(bf16[1160,128]{1,0:T(8,128)(2,1)S(1)} %collective-permute-done.5), channel_id=1, source_target_pairs={{1,0},{3,2},{5,4},{7,6},{9,8},{11,10},{13,12},{15,14},{17,16},{19,... | collective-permute-start | bytes 890888 | tf_op jit(solution)/shard_map/ppermute | solution.py:249
  34.7 1.6 %shard_map.42 = (f32[384,768]{1,0:T(8,128)S(1)}, f32[384,128]{1,0:T(8,128)S(1)}) custom-call(bf16[1160,128]{1,0:T(8,128)(2,1)S(1)} %shard_map.37.own, bf16[1160,128]{1,0:T(8,128)(2,1)S(1)} %collective-permute-done.other, f32[384,128]{1,0:T(8,128)S(1)} %get-tuple-element.52.info, ...), custom_call_target="tpu_custom_call", output_to_operand_aliasing={{0}: (5, {}), {1}: (6, {})} | custom-call | tf_op jit(solution)/shard_map/pallas_call | solution.py:210
  36.3 0.0 collective-permute-done.14.refs_0_
  36.3 0.0 collective-permute-done.15.refs_1_
  36.3 1.3 %collective-permute-start.16 = (bf16[1160,128]{1,0:T(8,128)(2,1)S(1)}, bf16[1160,128]{1,0:T(8,128)(2,1)S(1)}, u32[]{:S(2)}, u32[]{:S(2)}) collective-permute-start(bf16[1160,128]{1,0:T(8,128)(2,1)S(1)} %collective-permute-done.13), channel_id=1, source_target_pairs={{1,2},{3,0},{5,6},{7,4},{9,10},{11,8},{13,14},{15,12},{17,18},{19,... | collective-permute-start | bytes 890888 | tf_op jit(solution)/shard_map/ppermute | solution.py:246
  37.6 1.3 %collective-permute-start.17 = (bf16[1160,128]{1,0:T(8,128)(2,1)S(1)}, bf16[1160,128]{1,0:T(8,128)(2,1)S(1)}, u32[]{:S(2)}, u32[]{:S(2)}) collective-permute-start(bf16[1160,128]{1,0:T(8,128)(2,1)S(1)} %collective-permute-done.13), channel_id=1, source_target_pairs={{1,0},{3,2},{5,4},{7,6},{9,8},{11,10},{13,12},{15,14},{17,16},{19,... | collective-permute-start | bytes 890888 | tf_op jit(solution)/shard_map/ppermute | solution.py:249
  38.9 1.6 %shard_map.43 = (f32[384,768]{1,0:T(8,128)S(1)}, f32[384,128]{1,0:T(8,128)S(1)}) custom-call(bf16[1160,128]{1,0:T(8,128)(2,1)S(1)} %shard_map.37.own, bf16[1160,128]{1,0:T(8,128)(2,1)S(1)} %collective-permute-done.other, f32[384,128]{1,0:T(8,128)S(1)} %get-tuple-element.52.info, ...), custom_call_target="tpu_custom_call", output_to_operand_aliasing={{0}: (5, {}), {1}: (6, {})} | custom-call | tf_op jit(solution)/shard_map/pallas_call | solution.py:210
  40.6 0.0 collective-permute-done.11.refs_0_
  40.6 0.0 collective-permute-done.18
  40.6 0.0 collective-permute-done.19.refs_1_
  40.6 1.3 %collective-permute-start.20 = (bf16[1160,128]{1,0:T(8,128)(2,1)S(1)}, bf16[1160,128]{1,0:T(8,128)(2,1)S(1)}, u32[]{:S(2)}, u32[]{:S(2)}) collective-permute-start(bf16[1160,128]{1,0:T(8,128)(2,1)S(1)} %collective-permute-done.18), channel_id=1, source_target_pairs={{1,0},{3,2},{5,4},{7,6},{9,8},{11,10},{13,12},{15,14},{17,16},{19,... | collective-permute-start | bytes 890888 | tf_op jit(solution)/shard_map/ppermute | solution.py:249
  41.9 2.7 %collective-permute-start.12 = (bf16[1160,128]{1,0:T(8,128)(2,1)S(1)}, bf16[1160,128]{1,0:T(8,128)(2,1)S(1)}, u32[]{:S(2)}, u32[]{:S(2)}) collective-permute-start(bf16[1160,128]{1,0:T(8,128)(2,1)S(1)} %collective-permute-done.11.refs_0_), channel_id=1, source_target_pairs={{8,0},{0,4},{4,12},{12,8},{10,2},{2,6},{6,14},{14,10},{24,16},{16,... | collective-permute-start | bytes 890888 | tf_op jit(solution)/shard_map/ppermute | solution.py:243
  44.6 1.6 %shard_map.44 = (f32[384,768]{1,0:T(8,128)S(1)}, f32[384,128]{1,0:T(8,128)S(1)}) custom-call(bf16[1160,128]{1,0:T(8,128)(2,1)S(1)} %shard_map.37.own, bf16[1160,128]{1,0:T(8,128)(2,1)S(1)} %collective-permute-done.other, f32[384,128]{1,0:T(8,128)S(1)} %get-tuple-element.52.info, ...), custom_call_target="tpu_custom_call", output_to_operand_aliasing={{0}: (5, {}), {1}: (6, {})} | custom-call | tf_op jit(solution)/shard_map/pallas_call | solution.py:210
  46.3 0.0 collective-permute-done.16.refs_0_
  46.3 0.0 collective-permute-done.17.refs_1_
  46.3 0.0 collective-permute-done.20.refs_2_
  46.3 1.9 %shard_map.45 = (f32[384,768]{1,0:T(8,128)S(1)}, f32[384,128]{1,0:T(8,128)S(1)}) custom-call(bf16[1160,128]{1,0:T(8,128)(2,1)S(1)} %shard_map.37.own, bf16[1160,128]{1,0:T(8,128)(2,1)S(1)} %collective-permute-done.other, f32[384,128]{1,0:T(8,128)S(1)} %get-tuple-element.52.info, ...), custom_call_target="tpu_custom_call", output_to_operand_aliasing={{0}: (6, {}), {1}: (7, {})} | custom-call | tf_op jit(solution)/shard_map/pallas_call | solution.py:210
  48.2 3.3 %collective-permute-done.12.right = bf16[1160,128]{1,0:T(8,128)(2,1)S(1)} collective-permute-done((bf16[1160,128]{1,0:T(8,128)(2,1)S(1)}, bf16[1160,128]{1,0:T(8,128)(2,1)S(1)}, u32[]{:S(2)}, u32[]{:S(2)}) %collective-permute-start.12) | collective-permute-done | bytes 296992 | tf_op jit(solution)/shard_map/ppermute | solution.py:243
  51.5 0.9 %shard_map.46 = (bf16[192,768]{1,0:T(8,128)(2,1)S(1)}, bf16[192,768]{1,0:T(8,128)(2,1)S(1)}) custom-call(bf16[1160,128]{1,0:T(8,128)(2,1)S(1)} %shard_map.37.own, bf16[1160,128]{1,0:T(8,128)(2,1)S(1)} %collective-permute-done.other, f32[384,128]{1,0:T(8,128)S(1)} %get-tuple-element.52.info, bf16[1160,128]{1,0:T(8,128)(2,1)S(1)} %collective-permute-done.12.right, ...), custom_call_target="tpu_custom_call" | custom-call | tf_op jit(solution)/shard_map/pallas_call | solution.py:210
  52.3 1.3 %collective-permute-start.21 = (bf16[192,768]{1,0:T(8,128)(2,1)S(1)}, bf16[192,768]{1,0:T(8,128)(2,1)S(1)}, u32[]{:S(2)}, u32[]{:S(2)}) collective-permute-start(bf16[192,768]{1,0:T(8,128)(2,1)S(1)} %get-tuple-element.98), channel_id=1, source_target_pairs={{0,1},{2,3},{4,5},{6,7},{8,9},{10,11},{12,13},{14,15},{16,17},{18,... | collective-permute-start | bytes 884744 | tf_op jit(solution)/shard_map/ppermute | solution.py:289
  53.7 1.2 %collective-permute-done.21.back = bf16[192,768]{1,0:T(8,128)(2,1)S(1)} collective-permute-done((bf16[192,768]{1,0:T(8,128)(2,1)S(1)}, bf16[192,768]{1,0:T(8,128)(2,1)S(1)}, u32[]{:S(2)}, u32[]{:S(2)}) %collective-permute-start.21) | collective-permute-done | bytes 294944 | tf_op jit(solution)/shard_map/ppermute | solution.py:289
  54.8 0.7 %shard_map.47 = bf16[192,768]{1,0:T(8,128)(2,1)} custom-call(bf16[192,768]{1,0:T(8,128)(2,1)S(1)} %get-tuple-element.97.mine, bf16[192,768]{1,0:T(8,128)(2,1)S(1)} %collective-permute-done.21.back), custom_call_target="tpu_custom_call" | custom-call | tf_op jit(solution)/shard_map/pallas_call | solution.py:210
Async XLA Ops:
  0.0 1.0 %copy-start = (bf16[192,768]{1,0:T(8,128)(2,1)S(1)}, bf16[192,768]{1,0:T(8,128)(2,1)}, u32[]{:S(2)}) copy-start(bf16[192,768]{1,0:T(8,128)(2,1)} %rows.1) | copy-start | bytes 884740
  1.0 0.7 %copy-start.1 = (s32[192,1]{0,1:T(1,128)S(1)}, s32[192,1]{0,1:T(1,128)}, u32[]{:S(2)}) copy-start(s32[192,1]{0,1:T(1,128)} %param.4) | copy-start | bytes 2308
  1.6 0.7 %copy-start.2 = (s32[192]{0:T(256)S(1)}, s32[192]{0:T(256)}, u32[]{:S(2)}) copy-start(s32[192]{0:T(256)} %param.5) | copy-start | bytes 2308
  2.4 2.5 %collective-permute-start = (bf16[1160,128]{1,0:T(8,128)(2,1)S(1)}, bf16[1160,128]{1,0:T(8,128)(2,1)S(1)}, u32[]{:S(2)}, u32[]{:S(2)}) collective-permute-start(bf16[1160,128]{1,0:T(8,128)(2,1)S(1)} %shard_map.37.own), channel_id=1, source_target_pairs={{0,1},{1,0},{2,3},{3,2},{4,5},{5,4},{6,7},{7,6},{8,9},{9,8},{10,11... | collective-permute-start | bytes 890888 | tf_op jit(solution)/shard_map/ppermute | solution.py:256
  2.9 5.2 %collective-permute-start.2 = (bf16[1160,128]{1,0:T(8,128)(2,1)S(1)}, bf16[1160,128]{1,0:T(8,128)(2,1)S(1)}, u32[]{:S(2)}, u32[]{:S(2)}) collective-permute-start(bf16[1160,128]{1,0:T(8,128)(2,1)S(1)} %shard_map.37.own), channel_id=1, source_target_pairs={{9,1},{1,5},{5,13},{13,9},{11,3},{3,7},{7,15},{15,11},{25,17},{17,... | collective-permute-start | bytes 890888 | tf_op jit(solution)/shard_map/ppermute | solution.py:243
  3.6 10.8 %collective-permute-start.3 = (bf16[1160,128]{1,0:T(8,128)(2,1)S(1)}, bf16[1160,128]{1,0:T(8,128)(2,1)S(1)}, u32[]{:S(2)}, u32[]{:S(2)}) collective-permute-start(bf16[1160,128]{1,0:T(8,128)(2,1)S(1)} %shard_map.37.own), channel_id=1, source_target_pairs={{1,2},{3,0},{5,6},{7,4},{9,10},{11,8},{13,14},{15,12},{17,18},{19,... | collective-permute-start | bytes 890888 | tf_op jit(solution)/shard_map/ppermute | solution.py:246
  4.9 13.7 %collective-permute-start.1 = (bf16[1160,128]{1,0:T(8,128)(2,1)S(1)}, bf16[1160,128]{1,0:T(8,128)(2,1)S(1)}, u32[]{:S(2)}, u32[]{:S(2)}) collective-permute-start(bf16[1160,128]{1,0:T(8,128)(2,1)S(1)} %collective-permute-done.other), channel_id=1, source_target_pairs={{9,1},{1,5},{5,13},{13,9},{11,3},{3,7},{7,15},{15,11},{25,17},{17,... | collective-permute-start | bytes 890888 | tf_op jit(solution)/shard_map/ppermute | solution.py:243
  5.6 14.4 %collective-permute-start.4 = (bf16[1160,128]{1,0:T(8,128)(2,1)S(1)}, bf16[1160,128]{1,0:T(8,128)(2,1)S(1)}, u32[]{:S(2)}, u32[]{:S(2)}) collective-permute-start(bf16[1160,128]{1,0:T(8,128)(2,1)S(1)} %collective-permute-done.other), channel_id=1, source_target_pairs={{1,2},{3,0},{5,6},{7,4},{9,10},{11,8},{13,14},{15,12},{17,18},{19,... | collective-permute-start | bytes 890888 | tf_op jit(solution)/shard_map/ppermute | solution.py:246
  14.4 8.4 %collective-permute-start.6 = (bf16[1160,128]{1,0:T(8,128)(2,1)S(1)}, bf16[1160,128]{1,0:T(8,128)(2,1)S(1)}, u32[]{:S(2)}, u32[]{:S(2)}) collective-permute-start(bf16[1160,128]{1,0:T(8,128)(2,1)S(1)} %collective-permute-done.2), channel_id=1, source_target_pairs={{9,1},{1,5},{5,13},{13,9},{11,3},{3,7},{7,15},{15,11},{25,17},{17,... | collective-permute-start | bytes 890888 | tf_op jit(solution)/shard_map/ppermute | solution.py:243
  15.1 9.1 %collective-permute-start.7 = (bf16[1160,128]{1,0:T(8,128)(2,1)S(1)}, bf16[1160,128]{1,0:T(8,128)(2,1)S(1)}, u32[]{:S(2)}, u32[]{:S(2)}) collective-permute-start(bf16[1160,128]{1,0:T(8,128)(2,1)S(1)} %collective-permute-done.2), channel_id=1, source_target_pairs={{1,2},{3,0},{5,6},{7,4},{9,10},{11,8},{13,14},{15,12},{17,18},{19,... | collective-permute-start | bytes 890888 | tf_op jit(solution)/shard_map/ppermute | solution.py:246
  16.4 7.8 %collective-permute-start.8 = (bf16[1160,128]{1,0:T(8,128)(2,1)S(1)}, bf16[1160,128]{1,0:T(8,128)(2,1)S(1)}, u32[]{:S(2)}, u32[]{:S(2)}) collective-permute-start(bf16[1160,128]{1,0:T(8,128)(2,1)S(1)} %collective-permute-done.2), channel_id=1, source_target_pairs={{1,0},{3,2},{5,4},{7,6},{9,8},{11,10},{13,12},{15,14},{17,16},{19,... | collective-permute-start | bytes 890888 | tf_op jit(solution)/shard_map/ppermute | solution.py:249
  20.0 6.2 %collective-permute-start.10 = (bf16[1160,128]{1,0:T(8,128)(2,1)S(1)}, bf16[1160,128]{1,0:T(8,128)(2,1)S(1)}, u32[]{:S(2)}, u32[]{:S(2)}) collective-permute-start(bf16[1160,128]{1,0:T(8,128)(2,1)S(1)} %collective-permute-done.1), channel_id=1, source_target_pairs={{1,0},{3,2},{5,4},{7,6},{9,8},{11,10},{13,12},{15,14},{17,16},{19,... | collective-permute-start | bytes 890888 | tf_op jit(solution)/shard_map/ppermute | solution.py:249
  21.2 7.9 %collective-permute-start.5 = (bf16[1160,128]{1,0:T(8,128)(2,1)S(1)}, bf16[1160,128]{1,0:T(8,128)(2,1)S(1)}, u32[]{:S(2)}, u32[]{:S(2)}) collective-permute-start(bf16[1160,128]{1,0:T(8,128)(2,1)S(1)} %collective-permute-done.1), channel_id=1, source_target_pairs={{9,1},{1,5},{5,13},{13,9},{11,3},{3,7},{7,15},{15,11},{25,17},{17,... | collective-permute-start | bytes 890888 | tf_op jit(solution)/shard_map/ppermute | solution.py:243
  22.9 8.5 %collective-permute-start.9 = (bf16[1160,128]{1,0:T(8,128)(2,1)S(1)}, bf16[1160,128]{1,0:T(8,128)(2,1)S(1)}, u32[]{:S(2)}, u32[]{:S(2)}) collective-permute-start(bf16[1160,128]{1,0:T(8,128)(2,1)S(1)} %collective-permute-done.1), channel_id=1, source_target_pairs={{1,2},{3,0},{5,6},{7,4},{9,10},{11,8},{13,14},{15,12},{17,18},{19,... | collective-permute-start | bytes 890888 | tf_op jit(solution)/shard_map/ppermute | solution.py:246
  24.2 9.2 %collective-permute-start.13 = (bf16[1160,128]{1,0:T(8,128)(2,1)S(1)}, bf16[1160,128]{1,0:T(8,128)(2,1)S(1)}, u32[]{:S(2)}, u32[]{:S(2)}) collective-permute-start(bf16[1160,128]{1,0:T(8,128)(2,1)S(1)} %collective-permute-done.6), channel_id=1, source_target_pairs={{9,1},{1,5},{5,13},{13,9},{11,3},{3,7},{7,15},{15,11},{25,17},{17,... | collective-permute-start | bytes 890888 | tf_op jit(solution)/shard_map/ppermute | solution.py:243
  24.9 11.5 %collective-permute-start.14 = (bf16[1160,128]{1,0:T(8,128)(2,1)S(1)}, bf16[1160,128]{1,0:T(8,128)(2,1)S(1)}, u32[]{:S(2)}, u32[]{:S(2)}) collective-permute-start(bf16[1160,128]{1,0:T(8,128)(2,1)S(1)} %collective-permute-done.6), channel_id=1, source_target_pairs={{1,2},{3,0},{5,6},{7,4},{9,10},{11,8},{13,14},{15,12},{17,18},{19,... | collective-permute-start | bytes 890888 | tf_op jit(solution)/shard_map/ppermute | solution.py:246
  26.2 10.2 %collective-permute-start.15 = (bf16[1160,128]{1,0:T(8,128)(2,1)S(1)}, bf16[1160,128]{1,0:T(8,128)(2,1)S(1)}, u32[]{:S(2)}, u32[]{:S(2)}) collective-permute-start(bf16[1160,128]{1,0:T(8,128)(2,1)S(1)} %collective-permute-done.6), channel_id=1, source_target_pairs={{1,0},{3,2},{5,4},{7,6},{9,8},{11,10},{13,12},{15,14},{17,16},{19,... | collective-permute-start | bytes 890888 | tf_op jit(solution)/shard_map/ppermute | solution.py:249
  31.4 9.2 %collective-permute-start.11 = (bf16[1160,128]{1,0:T(8,128)(2,1)S(1)}, bf16[1160,128]{1,0:T(8,128)(2,1)S(1)}, u32[]{:S(2)}, u32[]{:S(2)}) collective-permute-start(bf16[1160,128]{1,0:T(8,128)(2,1)S(1)} %collective-permute-done.5), channel_id=1, source_target_pairs={{1,2},{3,0},{5,6},{7,4},{9,10},{11,8},{13,14},{15,12},{17,18},{19,... | collective-permute-start | bytes 890888 | tf_op jit(solution)/shard_map/ppermute | solution.py:246
  32.7 7.9 %collective-permute-start.18 = (bf16[1160,128]{1,0:T(8,128)(2,1)S(1)}, bf16[1160,128]{1,0:T(8,128)(2,1)S(1)}, u32[]{:S(2)}, u32[]{:S(2)}) collective-permute-start(bf16[1160,128]{1,0:T(8,128)(2,1)S(1)} %collective-permute-done.5), channel_id=1, source_target_pairs={{9,1},{1,5},{5,13},{13,9},{11,3},{3,7},{7,15},{15,11},{25,17},{17,... | collective-permute-start | bytes 890888 | tf_op jit(solution)/shard_map/ppermute | solution.py:243
  33.4 7.2 %collective-permute-start.19 = (bf16[1160,128]{1,0:T(8,128)(2,1)S(1)}, bf16[1160,128]{1,0:T(8,128)(2,1)S(1)}, u32[]{:S(2)}, u32[]{:S(2)}) collective-permute-start(bf16[1160,128]{1,0:T(8,128)(2,1)S(1)} %collective-permute-done.5), channel_id=1, source_target_pairs={{1,0},{3,2},{5,4},{7,6},{9,8},{11,10},{13,12},{15,14},{17,16},{19,... | collective-permute-start | bytes 890888 | tf_op jit(solution)/shard_map/ppermute | solution.py:249
  36.3 9.9 %collective-permute-start.16 = (bf16[1160,128]{1,0:T(8,128)(2,1)S(1)}, bf16[1160,128]{1,0:T(8,128)(2,1)S(1)}, u32[]{:S(2)}, u32[]{:S(2)}) collective-permute-start(bf16[1160,128]{1,0:T(8,128)(2,1)S(1)} %collective-permute-done.13), channel_id=1, source_target_pairs={{1,2},{3,0},{5,6},{7,4},{9,10},{11,8},{13,14},{15,12},{17,18},{19,... | collective-permute-start | bytes 890888 | tf_op jit(solution)/shard_map/ppermute | solution.py:246
  37.6 8.6 %collective-permute-start.17 = (bf16[1160,128]{1,0:T(8,128)(2,1)S(1)}, bf16[1160,128]{1,0:T(8,128)(2,1)S(1)}, u32[]{:S(2)}, u32[]{:S(2)}) collective-permute-start(bf16[1160,128]{1,0:T(8,128)(2,1)S(1)} %collective-permute-done.13), channel_id=1, source_target_pairs={{1,0},{3,2},{5,4},{7,6},{9,8},{11,10},{13,12},{15,14},{17,16},{19,... | collective-permute-start | bytes 890888 | tf_op jit(solution)/shard_map/ppermute | solution.py:249
  40.6 5.7 %collective-permute-start.20 = (bf16[1160,128]{1,0:T(8,128)(2,1)S(1)}, bf16[1160,128]{1,0:T(8,128)(2,1)S(1)}, u32[]{:S(2)}, u32[]{:S(2)}) collective-permute-start(bf16[1160,128]{1,0:T(8,128)(2,1)S(1)} %collective-permute-done.18), channel_id=1, source_target_pairs={{1,0},{3,2},{5,4},{7,6},{9,8},{11,10},{13,12},{15,14},{17,16},{19,... | collective-permute-start | bytes 890888 | tf_op jit(solution)/shard_map/ppermute | solution.py:249
  41.9 9.5 %collective-permute-start.12 = (bf16[1160,128]{1,0:T(8,128)(2,1)S(1)}, bf16[1160,128]{1,0:T(8,128)(2,1)S(1)}, u32[]{:S(2)}, u32[]{:S(2)}) collective-permute-start(bf16[1160,128]{1,0:T(8,128)(2,1)S(1)} %collective-permute-done.11.refs_0_), channel_id=1, source_target_pairs={{8,0},{0,4},{4,12},{12,8},{10,2},{2,6},{6,14},{14,10},{24,16},{16,... | collective-permute-start | bytes 890888 | tf_op jit(solution)/shard_map/ppermute | solution.py:243
  52.3 2.5 %collective-permute-start.21 = (bf16[192,768]{1,0:T(8,128)(2,1)S(1)}, bf16[192,768]{1,0:T(8,128)(2,1)S(1)}, u32[]{:S(2)}, u32[]{:S(2)}) collective-permute-start(bf16[192,768]{1,0:T(8,128)(2,1)S(1)} %get-tuple-element.98), channel_id=1, source_target_pairs={{0,1},{2,3},{4,5},{6,7},{8,9},{10,11},{12,13},{14,15},{16,17},{18,... | collective-permute-start | bytes 884744 | tf_op jit(solution)/shard_map/ppermute | solution.py:289

commit v8 on v7

--- a/solution.py
+++ b/solution.py
@@ -240,20 +240,21 @@
 
     def along(rows, core):
         hops = [(2 * order[i - 1] + core, 2 * order[i] + core) for i in range(n_blk)]
-        return lax.ppermute(rows, ("blk", "pair"), hops)
+        stay = [(2 * i + 1 - core, 2 * i + 1 - core) for i in range(n_blk)]
+        return lax.ppermute(rows, ("blk", "pair"), hops + stay)
 
     def across(rows):
-        return lax.ppermute(rows, ("sub", "pair"), [(1, 2), (3, 0)])
+        return lax.ppermute(rows, ("sub", "pair"), [(1, 2), (3, 0), (0, 1), (2, 3)])
 
     def hand(rows):
-        return lax.ppermute(rows, "pair", [(1, 0)])
+        return lax.ppermute(rows, "pair", [(0, 1), (1, 0)])
 
     (block,) = call(
         pack_kernel,
         [((width // 128 * rows_here + 8, 128), BF16)],
         [embeddings, group_of.reshape(line), cluster_id.reshape(line)],
     )
-    other = lax.ppermute(block, "pair", [(0, 1), (1, 0)])
+    other = hand(block)
     moving = [block, other]
     crossed = [across(block), across(other)]
     handed = [None, None]
@@ -286,7 +287,7 @@
         [((rows_here, width), BF16)] * 2,
         [*left, crossed[last], *total],
     )
-    back = lax.ppermute(theirs, "pair", [(0, 1)])
+    back = hand(theirs)
     (out,) = call(out_kernel, [((rows_here, width), BF16)], [mine, back])
     return out
 

time: 56.1 us -> 49.6 us (0.88)
  waiting for transfers between devices: 14.5 us -> 5.86 us
  starting transfers between devices: 25.4 us -> 27.8 us
    ppermute x22, waiting for transfers between devices: 14.5 us -> 5.86 us  [the longest x7 2.31 us: along(): return lax.ppermute(rows, ('blk', 'pair'), hops + stay)]
    ppermute x22, starting transfers between devices: 25.4 us -> 27.8 us  [the longest x7 14.4 us: across(): return lax.ppermute(rows, ('sub', 'pair'), [(1, 2), (3, 0), (0, 1), (2, 3)])]
  transfers between devices with their start and end apart: 22 -> 22, of which waited for: 5 -> 4; matrix products, arithmetic and copies ran while one was open for 0% -> 0% of each run, Pallas kernels for 20% -> 23%
where the time goes in v8:
time: 49.6 us; the launch traced here: 49.3 us
  starting transfers between devices  27.8 us (56%)
  Pallas kernels  13 us (26%)
  waiting for transfers between devices  5.86 us (12%)
  local copies, waits for them, and re-layouts  2.32 us (5%)
    ppermute x7, starting transfers between devices, across(): return lax.ppermute(rows, ('sub', 'pair'), [(1, 2), (3, 0), (0, 1), (2, 3)])  14.4 us
    pallas_call x11, Pallas kernels, call(): pl.pallas_call(kernel, out_shape=[jax.ShapeDtypeStruct(shape, dtype) for...  13 us
    ppermute x7, starting transfers between devices, along(): return lax.ppermute(rows, ('blk', 'pair'), hops + stay)  7.7 us
    ppermute x8, starting transfers between devices, hand(): return lax.ppermute(rows, 'pair', [(0, 1), (1, 0)])  5.72 us
    unnamed x6, local copies, waits for them, and re-layouts  2.32 us
    ppermute x7, waiting for transfers between devices, along(): return lax.ppermute(rows, ('blk', 'pair'), hops + stay)  2.31 us
    ppermute x7, waiting for transfers between devices, across(): return lax.ppermute(rows, ('sub', 'pair'), [(1, 2), (3, 0), (0, 1), (2, 3)])  1.96 us
    ppermute x8, waiting for transfers between devices, hand(): return lax.ppermute(rows, 'pair', [(0, 1), (1, 0)])  1.59 us
  transfers between devices with their start and end apart: 22, of which 4 were waited for; matrix products, arithmetic and copies ran while one was open for 0% of the time, Pallas kernels for 23%

profile of v8, /device:TPU:0, one launch (start us, length us, event | category | flops | bytes accessed | tf_op | source)
XLA Modules:
  0.0 49.3 jit_solution(2083967170278599806)
XLA Ops:
  0.0 0.0 copy-start
  0.0 1.0 %copy-done = bf16[192,768]{1,0:T(8,128)(2,1)S(1)} copy-done((bf16[192,768]{1,0:T(8,128)(2,1)S(1)}, bf16[192,768]{1,0:T(8,128)(2,1)}, u32[]{:S(2)}) %copy-start) | copy-done | bytes 294936
  1.0 0.0 copy-start.1
  1.0 0.7 %copy-done.1 = s32[192,1]{0,1:T(1,128)S(1)} copy-done((s32[192,1]{0,1:T(1,128)S(1)}, s32[192,1]{0,1:T(1,128)}, u32[]{:S(2)}) %copy-start.1) | copy-done | bytes 792
  1.6 0.0 copy-start.2
  1.6 0.7 %copy-done.2 = s32[192]{0:T(256)S(1)} copy-done((s32[192]{0:T(256)S(1)}, s32[192]{0:T(256)}, u32[]{:S(2)}) %copy-start.2) | copy-done | bytes 792
  2.3 0.1 shard_map.37.own
  2.4 0.5 %collective-permute-start = (bf16[1160,128]{1,0:T(8,128)(2,1)S(1)}, bf16[1160,128]{1,0:T(8,128)(2,1)S(1)}, u32[]{:S(2)}, u32[]{:S(2)}) collective-permute-start(bf16[1160,128]{1,0:T(8,128)(2,1)S(1)} %shard_map.37.own), channel_id=1, source_target_pairs={{0,1},{1,0},{2,3},{3,2},{4,5},{5,4},{6,7},{7,6},{8,9},{9,8},{10,11... | collective-permute-start | bytes 890888 | tf_op jit(solution)/shard_map/ppermute | solution.py:250
  2.9 0.7 %collective-permute-start.2 = (bf16[1160,128]{1,0:T(8,128)(2,1)S(1)}, bf16[1160,128]{1,0:T(8,128)(2,1)S(1)}, u32[]{:S(2)}, u32[]{:S(2)}) collective-permute-start(bf16[1160,128]{1,0:T(8,128)(2,1)S(1)} %shard_map.37.own), channel_id=1, source_target_pairs={{9,1},{1,5},{5,13},{13,9},{0,0},{4,4},{8,8},{12,12},{11,3},{3,7},{... | collective-permute-start | bytes 890888 | tf_op jit(solution)/shard_map/ppermute | solution.py:244
  3.6 4.1 %collective-permute-start.3 = (bf16[1160,128]{1,0:T(8,128)(2,1)S(1)}, bf16[1160,128]{1,0:T(8,128)(2,1)S(1)}, u32[]{:S(2)}, u32[]{:S(2)}) collective-permute-start(bf16[1160,128]{1,0:T(8,128)(2,1)S(1)} %shard_map.37.own), channel_id=1, source_target_pairs={{1,2},{3,0},{0,1},{2,3},{5,6},{7,4},{4,5},{6,7},{9,10},{11,8},{8,9... | collective-permute-start | bytes 890888 | tf_op jit(solution)/shard_map/ppermute | solution.py:247
  7.7 0.0 collective-permute-done.other
  7.7 0.7 %collective-permute-start.1 = (bf16[1160,128]{1,0:T(8,128)(2,1)S(1)}, bf16[1160,128]{1,0:T(8,128)(2,1)S(1)}, u32[]{:S(2)}, u32[]{:S(2)}) collective-permute-start(bf16[1160,128]{1,0:T(8,128)(2,1)S(1)} %collective-permute-done.other), channel_id=1, source_target_pairs={{9,1},{1,5},{5,13},{13,9},{0,0},{4,4},{8,8},{12,12},{11,3},{3,7},{... | collective-permute-start | bytes 890888 | tf_op jit(solution)/shard_map/ppermute | solution.py:244
  8.3 3.6 %collective-permute-start.4 = (bf16[1160,128]{1,0:T(8,128)(2,1)S(1)}, bf16[1160,128]{1,0:T(8,128)(2,1)S(1)}, u32[]{:S(2)}, u32[]{:S(2)}) collective-permute-start(bf16[1160,128]{1,0:T(8,128)(2,1)S(1)} %collective-permute-done.other), channel_id=1, source_target_pairs={{1,2},{3,0},{0,1},{2,3},{5,6},{7,4},{4,5},{6,7},{9,10},{11,8},{8,9... | collective-permute-start | bytes 890888 | tf_op jit(solution)/shard_map/ppermute | solution.py:247
  12.0 1.2 %shard_map.38 = (f32[384,768]{1,0:T(8,128)S(1)}, f32[384,128]{1,0:T(8,128)S(1)}, f32[384,128]{1,0:T(8,128)S(1)}) custom-call(bf16[1160,128]{1,0:T(8,128)(2,1)S(1)} %shard_map.37.own, bf16[1160,128]{1,0:T(8,128)(2,1)S(1)} %collective-permute-done.other), custom_call_target="tpu_custom_call" | custom-call | tf_op jit(solution)/shard_map/pallas_call | solution.py:210
  13.1 0.0 collective-permute-done.2
  13.1 0.0 collective-permute-done.3.refs_0_
  13.2 0.7 %collective-permute-start.6 = (bf16[1160,128]{1,0:T(8,128)(2,1)S(1)}, bf16[1160,128]{1,0:T(8,128)(2,1)S(1)}, u32[]{:S(2)}, u32[]{:S(2)}) collective-permute-start(bf16[1160,128]{1,0:T(8,128)(2,1)S(1)} %collective-permute-done.2), channel_id=1, source_target_pairs={{9,1},{1,5},{5,13},{13,9},{0,0},{4,4},{8,8},{12,12},{11,3},{3,7},{... | collective-permute-start | bytes 890888 | tf_op jit(solution)/shard_map/ppermute | solution.py:244
  13.9 1.8 %collective-permute-start.7 = (bf16[1160,128]{1,0:T(8,128)(2,1)S(1)}, bf16[1160,128]{1,0:T(8,128)(2,1)S(1)}, u32[]{:S(2)}, u32[]{:S(2)}) collective-permute-start(bf16[1160,128]{1,0:T(8,128)(2,1)S(1)} %collective-permute-done.2), channel_id=1, source_target_pairs={{1,2},{3,0},{0,1},{2,3},{5,6},{7,4},{4,5},{6,7},{9,10},{11,8},{8,9... | collective-permute-start | bytes 890888 | tf_op jit(solution)/shard_map/ppermute | solution.py:247
  15.6 0.1 collective-permute-start.8
  15.7 0.9 %shard_map.39 = (f32[384,768]{1,0:T(8,128)S(1)}, f32[384,128]{1,0:T(8,128)S(1)}) custom-call(bf16[1160,128]{1,0:T(8,128)(2,1)S(1)} %shard_map.37.own, bf16[1160,128]{1,0:T(8,128)(2,1)S(1)} %collective-permute-done.other, f32[384,128]{1,0:T(8,128)S(1)} %get-tuple-element.52.info, ...), custom_call_target="tpu_custom_call", output_to_operand_aliasing={{0}: (4, {}), {1}: (5, {})} | custom-call | tf_op jit(solution)/shard_map/pallas_call | solution.py:210
  16.6 0.0 collective-permute-done.1
  16.6 0.9 %collective-permute-done.4.refs_0_ = bf16[1160,128]{1,0:T(8,128)(2,1)S(1)} collective-permute-done((bf16[1160,128]{1,0:T(8,128)(2,1)S(1)}, bf16[1160,128]{1,0:T(8,128)(2,1)S(1)}, u32[]{:S(2)}, u32[]{:S(2)}) %collective-permute-start.4) | collective-permute-done | bytes 296992 | tf_op jit(solution)/shard_map/ppermute | solution.py:247
  17.5 0.0 collective-permute-start.10
  17.5 0.7 %collective-permute-start.5 = (bf16[1160,128]{1,0:T(8,128)(2,1)S(1)}, bf16[1160,128]{1,0:T(8,128)(2,1)S(1)}, u32[]{:S(2)}, u32[]{:S(2)}) collective-permute-start(bf16[1160,128]{1,0:T(8,128)(2,1)S(1)} %collective-permute-done.1), channel_id=1, source_target_pairs={{9,1},{1,5},{5,13},{13,9},{0,0},{4,4},{8,8},{12,12},{11,3},{3,7},{... | collective-permute-start | bytes 890888 | tf_op jit(solution)/shard_map/ppermute | solution.py:244
  18.2 0.9 %shard_map.40 = (f32[384,768]{1,0:T(8,128)S(1)}, f32[384,128]{1,0:T(8,128)S(1)}) custom-call(bf16[1160,128]{1,0:T(8,128)(2,1)S(1)} %shard_map.37.own, bf16[1160,128]{1,0:T(8,128)(2,1)S(1)} %collective-permute-done.other, f32[384,128]{1,0:T(8,128)S(1)} %get-tuple-element.52.info, ...), custom_call_target="tpu_custom_call", output_to_operand_aliasing={{0}: (4, {}), {1}: (5, {})} | custom-call | tf_op jit(solution)/shard_map/pallas_call | solution.py:210
  19.1 0.0 collective-permute-done.6
  19.1 2.8 %collective-permute-start.9 = (bf16[1160,128]{1,0:T(8,128)(2,1)S(1)}, bf16[1160,128]{1,0:T(8,128)(2,1)S(1)}, u32[]{:S(2)}, u32[]{:S(2)}) collective-permute-start(bf16[1160,128]{1,0:T(8,128)(2,1)S(1)} %collective-permute-done.1), channel_id=1, source_target_pairs={{1,2},{3,0},{0,1},{2,3},{5,6},{7,4},{4,5},{6,7},{9,10},{11,8},{8,9... | collective-permute-start | bytes 890888 | tf_op jit(solution)/shard_map/ppermute | solution.py:247
  21.9 0.0 collective-permute-done.7.refs_0_
  21.9 0.0 collective-permute-done.8.refs_1_
  21.9 0.7 %collective-permute-start.13 = (bf16[1160,128]{1,0:T(8,128)(2,1)S(1)}, bf16[1160,128]{1,0:T(8,128)(2,1)S(1)}, u32[]{:S(2)}, u32[]{:S(2)}) collective-permute-start(bf16[1160,128]{1,0:T(8,128)(2,1)S(1)} %collective-permute-done.6), channel_id=1, source_target_pairs={{9,1},{1,5},{5,13},{13,9},{0,0},{4,4},{8,8},{12,12},{11,3},{3,7},{... | collective-permute-start | bytes 890888 | tf_op jit(solution)/shard_map/ppermute | solution.py:244
  22.6 2.1 %collective-permute-start.14 = (bf16[1160,128]{1,0:T(8,128)(2,1)S(1)}, bf16[1160,128]{1,0:T(8,128)(2,1)S(1)}, u32[]{:S(2)}, u32[]{:S(2)}) collective-permute-start(bf16[1160,128]{1,0:T(8,128)(2,1)S(1)} %collective-permute-done.6), channel_id=1, source_target_pairs={{1,2},{3,0},{0,1},{2,3},{5,6},{7,4},{4,5},{6,7},{9,10},{11,8},{8,9... | collective-permute-start | bytes 890888 | tf_op jit(solution)/shard_map/ppermute | solution.py:247
  24.7 0.0 collective-permute-done.10.refs_1_
  24.7 0.1 collective-permute-start.15
  24.8 1.6 %shard_map.41 = (f32[384,768]{1,0:T(8,128)S(1)}, f32[384,128]{1,0:T(8,128)S(1)}) custom-call(bf16[1160,128]{1,0:T(8,128)(2,1)S(1)} %shard_map.37.own, bf16[1160,128]{1,0:T(8,128)(2,1)S(1)} %collective-permute-done.other, f32[384,128]{1,0:T(8,128)S(1)} %get-tuple-element.52.info, ...), custom_call_target="tpu_custom_call", output_to_operand_aliasing={{0}: (5, {}), {1}: (6, {})} | custom-call | tf_op jit(solution)/shard_map/pallas_call | solution.py:210
  26.4 0.0 collective-permute-done.5
  26.4 1.0 %collective-permute-done.9.refs_0_ = bf16[1160,128]{1,0:T(8,128)(2,1)S(1)} collective-permute-done((bf16[1160,128]{1,0:T(8,128)(2,1)S(1)}, bf16[1160,128]{1,0:T(8,128)(2,1)S(1)}, u32[]{:S(2)}, u32[]{:S(2)}) %collective-permute-start.9) | collective-permute-done | bytes 296992 | tf_op jit(solution)/shard_map/ppermute | solution.py:247
  27.4 0.0 collective-permute-start.11
  27.4 0.7 %collective-permute-start.18 = (bf16[1160,128]{1,0:T(8,128)(2,1)S(1)}, bf16[1160,128]{1,0:T(8,128)(2,1)S(1)}, u32[]{:S(2)}, u32[]{:S(2)}) collective-permute-start(bf16[1160,128]{1,0:T(8,128)(2,1)S(1)} %collective-permute-done.5), channel_id=1, source_target_pairs={{9,1},{1,5},{5,13},{13,9},{0,0},{4,4},{8,8},{12,12},{11,3},{3,7},{... | collective-permute-start | bytes 890888 | tf_op jit(solution)/shard_map/ppermute | solution.py:244
  28.1 0.0 collective-permute-done.13
  28.1 4.0 %collective-permute-start.19 = (bf16[1160,128]{1,0:T(8,128)(2,1)S(1)}, bf16[1160,128]{1,0:T(8,128)(2,1)S(1)}, u32[]{:S(2)}, u32[]{:S(2)}) collective-permute-start(bf16[1160,128]{1,0:T(8,128)(2,1)S(1)} %collective-permute-done.5), channel_id=1, source_target_pairs={{0,1},{1,0},{2,3},{3,2},{4,5},{5,4},{6,7},{7,6},{8,9},{9,8},{10,11... | collective-permute-start | bytes 890888 | tf_op jit(solution)/shard_map/ppermute | solution.py:250
  32.1 1.6 %shard_map.42 = (f32[384,768]{1,0:T(8,128)S(1)}, f32[384,128]{1,0:T(8,128)S(1)}) custom-call(bf16[1160,128]{1,0:T(8,128)(2,1)S(1)} %shard_map.37.own, bf16[1160,128]{1,0:T(8,128)(2,1)S(1)} %collective-permute-done.other, f32[384,128]{1,0:T(8,128)S(1)} %get-tuple-element.52.info, ...), custom_call_target="tpu_custom_call", output_to_operand_aliasing={{0}: (5, {}), {1}: (6, {})} | custom-call | tf_op jit(solution)/shard_map/pallas_call | solution.py:210
  33.8 0.0 collective-permute-done.14.refs_0_
  33.8 0.0 collective-permute-done.15.refs_1_
  33.8 0.1 collective-permute-start.16
  33.8 0.6 %collective-permute-start.17 = (bf16[1160,128]{1,0:T(8,128)(2,1)S(1)}, bf16[1160,128]{1,0:T(8,128)(2,1)S(1)}, u32[]{:S(2)}, u32[]{:S(2)}) collective-permute-start(bf16[1160,128]{1,0:T(8,128)(2,1)S(1)} %collective-permute-done.13), channel_id=1, source_target_pairs={{0,1},{1,0},{2,3},{3,2},{4,5},{5,4},{6,7},{7,6},{8,9},{9,8},{10,11... | collective-permute-start | bytes 890888 | tf_op jit(solution)/shard_map/ppermute | solution.py:250
  34.5 1.6 %shard_map.43 = (f32[384,768]{1,0:T(8,128)S(1)}, f32[384,128]{1,0:T(8,128)S(1)}) custom-call(bf16[1160,128]{1,0:T(8,128)(2,1)S(1)} %shard_map.37.own, bf16[1160,128]{1,0:T(8,128)(2,1)S(1)} %collective-permute-done.other, f32[384,128]{1,0:T(8,128)S(1)} %get-tuple-element.52.info, ...), custom_call_target="tpu_custom_call", output_to_operand_aliasing={{0}: (5, {}), {1}: (6, {})} | custom-call | tf_op jit(solution)/shard_map/pallas_call | solution.py:210
  36.1 0.0 collective-permute-done.11.refs_0_
  36.1 0.0 collective-permute-done.18
  36.1 0.0 collective-permute-done.19.refs_1_
  36.1 0.3 collective-permute-start.20
  36.5 3.7 %collective-permute-start.12 = (bf16[1160,128]{1,0:T(8,128)(2,1)S(1)}, bf16[1160,128]{1,0:T(8,128)(2,1)S(1)}, u32[]{:S(2)}, u32[]{:S(2)}) collective-permute-start(bf16[1160,128]{1,0:T(8,128)(2,1)S(1)} %collective-permute-done.11.refs_0_), channel_id=1, source_target_pairs={{8,0},{0,4},{4,12},{12,8},{1,1},{5,5},{9,9},{13,13},{10,2},{2,6},{... | collective-permute-start | bytes 890888 | tf_op jit(solution)/shard_map/ppermute | solution.py:244
  40.2 1.6 %shard_map.44 = (f32[384,768]{1,0:T(8,128)S(1)}, f32[384,128]{1,0:T(8,128)S(1)}) custom-call(bf16[1160,128]{1,0:T(8,128)(2,1)S(1)} %shard_map.37.own, bf16[1160,128]{1,0:T(8,128)(2,1)S(1)} %collective-permute-done.other, f32[384,128]{1,0:T(8,128)S(1)} %get-tuple-element.52.info, ...), custom_call_target="tpu_custom_call", output_to_operand_aliasing={{0}: (5, {}), {1}: (6, {})} | custom-call | tf_op jit(solution)/shard_map/pallas_call | solution.py:210
  41.8 0.0 collective-permute-done.16.refs_0_
  41.8 0.0 collective-permute-done.17.refs_1_
  41.8 0.0 collective-permute-done.20.refs_2_
  41.8 1.9 %shard_map.45 = (f32[384,768]{1,0:T(8,128)S(1)}, f32[384,128]{1,0:T(8,128)S(1)}) custom-call(bf16[1160,128]{1,0:T(8,128)(2,1)S(1)} %shard_map.37.own, bf16[1160,128]{1,0:T(8,128)(2,1)S(1)} %collective-permute-done.other, f32[384,128]{1,0:T(8,128)S(1)} %get-tuple-element.52.info, ...), custom_call_target="tpu_custom_call", output_to_operand_aliasing={{0}: (6, {}), {1}: (7, {})} | custom-call | tf_op jit(solution)/shard_map/pallas_call | solution.py:210
  43.7 2.3 %collective-permute-done.12.right = bf16[1160,128]{1,0:T(8,128)(2,1)S(1)} collective-permute-done((bf16[1160,128]{1,0:T(8,128)(2,1)S(1)}, bf16[1160,128]{1,0:T(8,128)(2,1)S(1)}, u32[]{:S(2)}, u32[]{:S(2)}) %collective-permute-start.12) | collective-permute-done | bytes 296992 | tf_op jit(solution)/shard_map/ppermute | solution.py:244
  46.0 0.9 %shard_map.46 = (bf16[192,768]{1,0:T(8,128)(2,1)S(1)}, bf16[192,768]{1,0:T(8,128)(2,1)S(1)}) custom-call(bf16[1160,128]{1,0:T(8,128)(2,1)S(1)} %shard_map.37.own, bf16[1160,128]{1,0:T(8,128)(2,1)S(1)} %collective-permute-done.other, f32[384,128]{1,0:T(8,128)S(1)} %get-tuple-element.52.info, bf16[1160,128]{1,0:T(8,128)(2,1)S(1)} %collective-permute-done.12.right, ...), custom_call_target="tpu_custom_call" | custom-call | tf_op jit(solution)/shard_map/pallas_call | solution.py:210
  46.9 0.1 collective-permute-start.21
  47.0 1.6 %collective-permute-done.21.back = bf16[192,768]{1,0:T(8,128)(2,1)S(1)} collective-permute-done((bf16[192,768]{1,0:T(8,128)(2,1)S(1)}, bf16[192,768]{1,0:T(8,128)(2,1)S(1)}, u32[]{:S(2)}, u32[]{:S(2)}) %collective-permute-start.21) | collective-permute-done | bytes 294944 | tf_op jit(solution)/shard_map/ppermute | solution.py:250
  48.5 0.7 %shard_map.47 = bf16[192,768]{1,0:T(8,128)(2,1)} custom-call(bf16[192,768]{1,0:T(8,128)(2,1)S(1)} %get-tuple-element.97.mine, bf16[192,768]{1,0:T(8,128)(2,1)S(1)} %collective-permute-done.21.back), custom_call_target="tpu_custom_call" | custom-call | tf_op jit(solution)/shard_map/pallas_call | solution.py:210
Async XLA Ops:
  0.0 1.0 %copy-start = (bf16[192,768]{1,0:T(8,128)(2,1)S(1)}, bf16[192,768]{1,0:T(8,128)(2,1)}, u32[]{:S(2)}) copy-start(bf16[192,768]{1,0:T(8,128)(2,1)} %rows.1) | copy-start | bytes 884740
  1.0 0.7 %copy-start.1 = (s32[192,1]{0,1:T(1,128)S(1)}, s32[192,1]{0,1:T(1,128)}, u32[]{:S(2)}) copy-start(s32[192,1]{0,1:T(1,128)} %param.4) | copy-start | bytes 2308
  1.6 0.7 %copy-start.2 = (s32[192]{0:T(256)S(1)}, s32[192]{0:T(256)}, u32[]{:S(2)}) copy-start(s32[192]{0:T(256)} %param.5) | copy-start | bytes 2308
  2.4 5.3 %collective-permute-start = (bf16[1160,128]{1,0:T(8,128)(2,1)S(1)}, bf16[1160,128]{1,0:T(8,128)(2,1)S(1)}, u32[]{:S(2)}, u32[]{:S(2)}) collective-permute-start(bf16[1160,128]{1,0:T(8,128)(2,1)S(1)} %shard_map.37.own), channel_id=1, source_target_pairs={{0,1},{1,0},{2,3},{3,2},{4,5},{5,4},{6,7},{7,6},{8,9},{9,8},{10,11... | collective-permute-start | bytes 890888 | tf_op jit(solution)/shard_map/ppermute | solution.py:250
  2.9 10.2 %collective-permute-start.2 = (bf16[1160,128]{1,0:T(8,128)(2,1)S(1)}, bf16[1160,128]{1,0:T(8,128)(2,1)S(1)}, u32[]{:S(2)}, u32[]{:S(2)}) collective-permute-start(bf16[1160,128]{1,0:T(8,128)(2,1)S(1)} %shard_map.37.own), channel_id=1, source_target_pairs={{9,1},{1,5},{5,13},{13,9},{0,0},{4,4},{8,8},{12,12},{11,3},{3,7},{... | collective-permute-start | bytes 890888 | tf_op jit(solution)/shard_map/ppermute | solution.py:244
  3.6 9.6 %collective-permute-start.3 = (bf16[1160,128]{1,0:T(8,128)(2,1)S(1)}, bf16[1160,128]{1,0:T(8,128)(2,1)S(1)}, u32[]{:S(2)}, u32[]{:S(2)}) collective-permute-start(bf16[1160,128]{1,0:T(8,128)(2,1)S(1)} %shard_map.37.own), channel_id=1, source_target_pairs={{1,2},{3,0},{0,1},{2,3},{5,6},{7,4},{4,5},{6,7},{9,10},{11,8},{8,9... | collective-permute-start | bytes 890888 | tf_op jit(solution)/shard_map/ppermute | solution.py:247
  7.7 8.9 %collective-permute-start.1 = (bf16[1160,128]{1,0:T(8,128)(2,1)S(1)}, bf16[1160,128]{1,0:T(8,128)(2,1)S(1)}, u32[]{:S(2)}, u32[]{:S(2)}) collective-permute-start(bf16[1160,128]{1,0:T(8,128)(2,1)S(1)} %collective-permute-done.other), channel_id=1, source_target_pairs={{9,1},{1,5},{5,13},{13,9},{0,0},{4,4},{8,8},{12,12},{11,3},{3,7},{... | collective-permute-start | bytes 890888 | tf_op jit(solution)/shard_map/ppermute | solution.py:244
  8.3 9.1 %collective-permute-start.4 = (bf16[1160,128]{1,0:T(8,128)(2,1)S(1)}, bf16[1160,128]{1,0:T(8,128)(2,1)S(1)}, u32[]{:S(2)}, u32[]{:S(2)}) collective-permute-start(bf16[1160,128]{1,0:T(8,128)(2,1)S(1)} %collective-permute-done.other), channel_id=1, source_target_pairs={{1,2},{3,0},{0,1},{2,3},{5,6},{7,4},{4,5},{6,7},{9,10},{11,8},{8,9... | collective-permute-start | bytes 890888 | tf_op jit(solution)/shard_map/ppermute | solution.py:247
  13.2 5.9 %collective-permute-start.6 = (bf16[1160,128]{1,0:T(8,128)(2,1)S(1)}, bf16[1160,128]{1,0:T(8,128)(2,1)S(1)}, u32[]{:S(2)}, u32[]{:S(2)}) collective-permute-start(bf16[1160,128]{1,0:T(8,128)(2,1)S(1)} %collective-permute-done.2), channel_id=1, source_target_pairs={{9,1},{1,5},{5,13},{13,9},{0,0},{4,4},{8,8},{12,12},{11,3},{3,7},{... | collective-permute-start | bytes 890888 | tf_op jit(solution)/shard_map/ppermute | solution.py:244
  13.9 8.1 %collective-permute-start.7 = (bf16[1160,128]{1,0:T(8,128)(2,1)S(1)}, bf16[1160,128]{1,0:T(8,128)(2,1)S(1)}, u32[]{:S(2)}, u32[]{:S(2)}) collective-permute-start(bf16[1160,128]{1,0:T(8,128)(2,1)S(1)} %collective-permute-done.2), channel_id=1, source_target_pairs={{1,2},{3,0},{0,1},{2,3},{5,6},{7,4},{4,5},{6,7},{9,10},{11,8},{8,9... | collective-permute-start | bytes 890888 | tf_op jit(solution)/shard_map/ppermute | solution.py:247
  15.6 6.3 %collective-permute-start.8 = (bf16[1160,128]{1,0:T(8,128)(2,1)S(1)}, bf16[1160,128]{1,0:T(8,128)(2,1)S(1)}, u32[]{:S(2)}, u32[]{:S(2)}) collective-permute-start(bf16[1160,128]{1,0:T(8,128)(2,1)S(1)} %collective-permute-done.2), channel_id=1, source_target_pairs={{0,1},{1,0},{2,3},{3,2},{4,5},{5,4},{6,7},{7,6},{8,9},{9,8},{10,11... | collective-permute-start | bytes 890888 | tf_op jit(solution)/shard_map/ppermute | solution.py:250
  17.5 7.2 %collective-permute-start.10 = (bf16[1160,128]{1,0:T(8,128)(2,1)S(1)}, bf16[1160,128]{1,0:T(8,128)(2,1)S(1)}, u32[]{:S(2)}, u32[]{:S(2)}) collective-permute-start(bf16[1160,128]{1,0:T(8,128)(2,1)S(1)} %collective-permute-done.1), channel_id=1, source_target_pairs={{0,1},{1,0},{2,3},{3,2},{4,5},{5,4},{6,7},{7,6},{8,9},{9,8},{10,11... | collective-permute-start | bytes 890888 | tf_op jit(solution)/shard_map/ppermute | solution.py:250
  17.5 8.9 %collective-permute-start.5 = (bf16[1160,128]{1,0:T(8,128)(2,1)S(1)}, bf16[1160,128]{1,0:T(8,128)(2,1)S(1)}, u32[]{:S(2)}, u32[]{:S(2)}) collective-permute-start(bf16[1160,128]{1,0:T(8,128)(2,1)S(1)} %collective-permute-done.1), channel_id=1, source_target_pairs={{9,1},{1,5},{5,13},{13,9},{0,0},{4,4},{8,8},{12,12},{11,3},{3,7},{... | collective-permute-start | bytes 890888 | tf_op jit(solution)/shard_map/ppermute | solution.py:244
  19.1 8.4 %collective-permute-start.9 = (bf16[1160,128]{1,0:T(8,128)(2,1)S(1)}, bf16[1160,128]{1,0:T(8,128)(2,1)S(1)}, u32[]{:S(2)}, u32[]{:S(2)}) collective-permute-start(bf16[1160,128]{1,0:T(8,128)(2,1)S(1)} %collective-permute-done.1), channel_id=1, source_target_pairs={{1,2},{3,0},{0,1},{2,3},{5,6},{7,4},{4,5},{6,7},{9,10},{11,8},{8,9... | collective-permute-start | bytes 890888 | tf_op jit(solution)/shard_map/ppermute | solution.py:247
  21.9 6.2 %collective-permute-start.13 = (bf16[1160,128]{1,0:T(8,128)(2,1)S(1)}, bf16[1160,128]{1,0:T(8,128)(2,1)S(1)}, u32[]{:S(2)}, u32[]{:S(2)}) collective-permute-start(bf16[1160,128]{1,0:T(8,128)(2,1)S(1)} %collective-permute-done.6), channel_id=1, source_target_pairs={{9,1},{1,5},{5,13},{13,9},{0,0},{4,4},{8,8},{12,12},{11,3},{3,7},{... | collective-permute-start | bytes 890888 | tf_op jit(solution)/shard_map/ppermute | solution.py:244
  22.6 11.2 %collective-permute-start.14 = (bf16[1160,128]{1,0:T(8,128)(2,1)S(1)}, bf16[1160,128]{1,0:T(8,128)(2,1)S(1)}, u32[]{:S(2)}, u32[]{:S(2)}) collective-permute-start(bf16[1160,128]{1,0:T(8,128)(2,1)S(1)} %collective-permute-done.6), channel_id=1, source_target_pairs={{1,2},{3,0},{0,1},{2,3},{5,6},{7,4},{4,5},{6,7},{9,10},{11,8},{8,9... | collective-permute-start | bytes 890888 | tf_op jit(solution)/shard_map/ppermute | solution.py:247
  24.7 9.1 %collective-permute-start.15 = (bf16[1160,128]{1,0:T(8,128)(2,1)S(1)}, bf16[1160,128]{1,0:T(8,128)(2,1)S(1)}, u32[]{:S(2)}, u32[]{:S(2)}) collective-permute-start(bf16[1160,128]{1,0:T(8,128)(2,1)S(1)} %collective-permute-done.6), channel_id=1, source_target_pairs={{0,1},{1,0},{2,3},{3,2},{4,5},{5,4},{6,7},{7,6},{8,9},{9,8},{10,11... | collective-permute-start | bytes 890888 | tf_op jit(solution)/shard_map/ppermute | solution.py:250
  27.4 8.7 %collective-permute-start.11 = (bf16[1160,128]{1,0:T(8,128)(2,1)S(1)}, bf16[1160,128]{1,0:T(8,128)(2,1)S(1)}, u32[]{:S(2)}, u32[]{:S(2)}) collective-permute-start(bf16[1160,128]{1,0:T(8,128)(2,1)S(1)} %collective-permute-done.5), channel_id=1, source_target_pairs={{1,2},{3,0},{0,1},{2,3},{5,6},{7,4},{4,5},{6,7},{9,10},{11,8},{8,9... | collective-permute-start | bytes 890888 | tf_op jit(solution)/shard_map/ppermute | solution.py:247
  27.4 8.7 %collective-permute-start.18 = (bf16[1160,128]{1,0:T(8,128)(2,1)S(1)}, bf16[1160,128]{1,0:T(8,128)(2,1)S(1)}, u32[]{:S(2)}, u32[]{:S(2)}) collective-permute-start(bf16[1160,128]{1,0:T(8,128)(2,1)S(1)} %collective-permute-done.5), channel_id=1, source_target_pairs={{9,1},{1,5},{5,13},{13,9},{0,0},{4,4},{8,8},{12,12},{11,3},{3,7},{... | collective-permute-start | bytes 890888 | tf_op jit(solution)/shard_map/ppermute | solution.py:244
  28.1 8.0 %collective-permute-start.19 = (bf16[1160,128]{1,0:T(8,128)(2,1)S(1)}, bf16[1160,128]{1,0:T(8,128)(2,1)S(1)}, u32[]{:S(2)}, u32[]{:S(2)}) collective-permute-start(bf16[1160,128]{1,0:T(8,128)(2,1)S(1)} %collective-permute-done.5), channel_id=1, source_target_pairs={{0,1},{1,0},{2,3},{3,2},{4,5},{5,4},{6,7},{7,6},{8,9},{9,8},{10,11... | collective-permute-start | bytes 890888 | tf_op jit(solution)/shard_map/ppermute | solution.py:250
  33.8 8.0 %collective-permute-start.16 = (bf16[1160,128]{1,0:T(8,128)(2,1)S(1)}, bf16[1160,128]{1,0:T(8,128)(2,1)S(1)}, u32[]{:S(2)}, u32[]{:S(2)}) collective-permute-start(bf16[1160,128]{1,0:T(8,128)(2,1)S(1)} %collective-permute-done.13), channel_id=1, source_target_pairs={{1,2},{3,0},{0,1},{2,3},{5,6},{7,4},{4,5},{6,7},{9,10},{11,8},{8,9... | collective-permute-start | bytes 890888 | tf_op jit(solution)/shard_map/ppermute | solution.py:247
  33.8 8.0 %collective-permute-start.17 = (bf16[1160,128]{1,0:T(8,128)(2,1)S(1)}, bf16[1160,128]{1,0:T(8,128)(2,1)S(1)}, u32[]{:S(2)}, u32[]{:S(2)}) collective-permute-start(bf16[1160,128]{1,0:T(8,128)(2,1)S(1)} %collective-permute-done.13), channel_id=1, source_target_pairs={{0,1},{1,0},{2,3},{3,2},{4,5},{5,4},{6,7},{7,6},{8,9},{9,8},{10,11... | collective-permute-start | bytes 890888 | tf_op jit(solution)/shard_map/ppermute | solution.py:250
  36.1 5.7 %collective-permute-start.20 = (bf16[1160,128]{1,0:T(8,128)(2,1)S(1)}, bf16[1160,128]{1,0:T(8,128)(2,1)S(1)}, u32[]{:S(2)}, u32[]{:S(2)}) collective-permute-start(bf16[1160,128]{1,0:T(8,128)(2,1)S(1)} %collective-permute-done.18), channel_id=1, source_target_pairs={{0,1},{1,0},{2,3},{3,2},{4,5},{5,4},{6,7},{7,6},{8,9},{9,8},{10,11... | collective-permute-start | bytes 890888 | tf_op jit(solution)/shard_map/ppermute | solution.py:250
  36.5 9.5 %collective-permute-start.12 = (bf16[1160,128]{1,0:T(8,128)(2,1)S(1)}, bf16[1160,128]{1,0:T(8,128)(2,1)S(1)}, u32[]{:S(2)}, u32[]{:S(2)}) collective-permute-start(bf16[1160,128]{1,0:T(8,128)(2,1)S(1)} %collective-permute-done.11.refs_0_), channel_id=1, source_target_pairs={{8,0},{0,4},{4,12},{12,8},{1,1},{5,5},{9,9},{13,13},{10,2},{2,6},{... | collective-permute-start | bytes 890888 | tf_op jit(solution)/shard_map/ppermute | solution.py:244
  46.9 1.6 %collective-permute-start.21 = (bf16[192,768]{1,0:T(8,128)(2,1)S(1)}, bf16[192,768]{1,0:T(8,128)(2,1)S(1)}, u32[]{:S(2)}, u32[]{:S(2)}) collective-permute-start(bf16[192,768]{1,0:T(8,128)(2,1)S(1)} %get-tuple-element.98), channel_id=1, source_target_pairs={{0,1},{1,0},{2,3},{3,2},{4,5},{5,4},{6,7},{7,6},{8,9},{9,8},{10,11... | collective-permute-start | bytes 884744 | tf_op jit(solution)/shard_map/ppermute | solution.py:250

commit v9 on v6

v9 whole, which is shorter than its diff:
```python
import functools

import jax
import jax.numpy as jnp
from jax import lax
from jax.experimental import pallas as pl
from jax.experimental.pallas import tpu as pltpu
from jax.sharding import PartitionSpec as P

F32 = jnp.float32
BF16 = jnp.bfloat16
VMEM_BYTES = 24 * 1024 * 1024
GATHER_LIMIT = 8 * 1024 * 1024


def unit_scale(rows_in):
    wide = rows_in.astype(F32)
    return lax.rsqrt(jnp.sum(wide * wide, axis=1) + 1e-06)


def tile_weights(left_rows, left_clust, left_scale, right_rows, right_clust, right_scale):
    grams = lax.dot_general(
        left_rows, right_rows, (((1,), (1,)), ((), ())), preferred_element_type=F32
    )
    cosine = grams * left_scale[:, None] * right_scale[None, :]
    same = (left_clust[:, None] == right_clust[None, :]).astype(F32)
    return jax.nn.sigmoid(8.0 * cosine - 2.0) * same


def by_group(embeddings, group_of, cluster_id):
    rows_here, width = embeddings.shape
    groups = lax.axis_size("sub") * lax.axis_size("pair")
    capacity = 2 * rows_here // groups
    slots = groups * capacity
    target = group_of[:, 0]
    onehot = (target[:, None] == jnp.arange(groups, dtype=jnp.int32)[None, :]).astype(jnp.int32)
    position = jnp.sum((jnp.cumsum(onehot, axis=0) - onehot) * onehot, axis=1)
    send_rows = jnp.zeros((groups, capacity, width), BF16).at[target, position].set(embeddings)
    send_clust = jnp.full((groups, capacity), -1, jnp.int32).at[target, position].set(cluster_id)
    recv_rows, recv_clust = (
        lax.all_to_all(send_rows, ("sub", "pair"), split_axis=0, concat_axis=0, tiled=True),
        lax.all_to_all(send_clust, ("sub", "pair"), split_axis=0, concat_axis=0, tiled=True),
    )
    own_rows = recv_rows.reshape(slots, width)
    own_clust = recv_clust.reshape(slots)
    own_scale = unit_scale(own_rows)
    piece_rows = lax.all_gather(own_rows, "blk", axis=0, tiled=True)
    piece_clust = lax.all_gather(own_clust, "blk", axis=0, tiled=True)
    weight = tile_weights(
        own_rows, own_clust, own_scale, piece_rows, piece_clust, unit_scale(piece_rows)
    )
    numer = jnp.dot(weight.astype(BF16), piece_rows, preferred_element_type=F32)
    denom = jnp.sum(weight, axis=1)
    result = (numer / denom[:, None]).astype(BF16).reshape(groups, capacity, width)
    returned = lax.all_to_all(result, ("sub", "pair"), split_axis=0, concat_axis=0, tiled=True)
    return returned[target, position]


def diagonal(size):
    shape = (size, size)
    return lax.broadcasted_iota(jnp.int32, shape, 0) == lax.broadcasted_iota(jnp.int32, shape, 1)


def to_column(row):
    size = row.shape[1]
    return jnp.sum(jnp.where(diagonal(size), row, jnp.zeros_like(row)), axis=1, keepdims=True)


def to_row(column):
    size = column.shape[0]
    return jnp.sum(jnp.where(diagonal(size), column, jnp.zeros_like(column)), axis=0, keepdims=True)


def scale_column(rows):
    wide = rows.astype(F32)
    return lax.rsqrt(jnp.sum(wide * wide, axis=1, keepdims=True) + 1e-06)


def name_lines(rows_here):
    return -(-rows_here // 128)


def pack_kernel(rows, group, cluster, whole, first, second):
    rows_here, width = rows.shape
    slabs = width // 128
    half = rows_here // 2
    for slab in range(slabs):
        columns = rows[:, slab * 128 : (slab + 1) * 128]
        whole[slab * rows_here : (slab + 1) * rows_here, :] = columns
        first[slab * half : (slab + 1) * half, :] = columns[:half]
        second[slab * half : (slab + 1) * half, :] = columns[half:]
    line_at = lax.broadcasted_iota(jnp.int32, (8, 128), 0)
    lines = name_lines(rows_here)
    named = jnp.zeros((8, 128), jnp.int32)
    for kind, ref in enumerate((group, cluster)):
        for line in range(lines):
            part = ref[:, line * 128 : (line + 1) * 128]
            if part.shape[1] < 128:
                rest = jnp.zeros((1, 128 - part.shape[1]), jnp.int32)
                part = jnp.concatenate([part, rest], axis=1)
            named = jnp.where(line_at == kind * lines + line, part, named)
    named = named.astype(F32).astype(BF16)
    whole[slabs * rows_here :, :] = named
    first[slabs * half :, :] = named


def from_slabs(ref, count):
    slabs = [ref[top : top + count, :] for top in range(0, ref.shape[0] // count * count, count)]
    return jnp.concatenate(slabs, axis=1)


def key_row(ref, rows_here):
    wide = ref[ref.shape[0] - 8 :, :].astype(F32)
    lines = name_lines(rows_here)
    kinds = []
    for kind in range(2):
        parts = [wide[kind * lines + line : kind * lines + line + 1, :] for line in range(lines)]
        kinds.append(jnp.concatenate(parts, axis=1)[:, :rows_here])
    return kinds[0] * 256.0 + kinds[1]


def from_halves(first, second, rows_here):
    half = rows_here // 2
    rows = jnp.concatenate([from_slabs(first, half), from_slabs(second, half)], axis=0)
    return rows, key_row(first, rows_here)


def add_blocks(left, key, scale, blocks, numer, denom):
    scale = 4.0 * scale
    for right_rows, right_key, right_scale in blocks:
        grams = lax.dot_general(
            left, right_rows, (((1,), (1,)), ((), ())), preferred_element_type=F32
        )
        half = jnp.tanh(grams * scale * right_scale - 1.0)
        weight = jnp.where(key == right_key, 0.5 + 0.5 * half, 0.0)
        add = jnp.dot(weight.astype(BF16), right_rows, preferred_element_type=F32)
        add_denom = jnp.sum(weight, axis=1, keepdims=True)
        numer = add if numer is None else numer + add
        denom = add_denom if denom is None else denom + add_denom
    return numer, denom


def left_of(refs, rows_here):
    rows = jnp.concatenate([from_slabs(ref, rows_here) for ref in refs], axis=0)
    key = jnp.concatenate([to_column(key_row(ref, rows_here)) for ref in refs], axis=0)
    return rows, key, scale_column(rows)


def take_blocks(refs, count, rows_here):
    blocks = []
    for _ in range(count):
        rows, key = from_halves(refs.pop(0), refs.pop(0), rows_here)
        blocks.append((rows, key, to_row(scale_column(rows))))
    return blocks


def store_sides(numer, denom, outs):
    rows_here, wide = outs[0].shape
    for side, out in enumerate(outs):
        top = side * rows_here
        out[:, : wide - 128] = numer[top : top + rows_here]
        out[:, wide - 128 :] = jnp.broadcast_to(denom[top : top + rows_here], (rows_here, 128))


def start_kernel(n_blocks, own, other, *refs):
    refs = list(refs)
    rows_here = refs[-1].shape[0]
    left, key, scale = left_of((own, other), rows_here)
    first = (left[:rows_here], key_row(own, rows_here), to_row(scale[:rows_here]))
    blocks = [first] + take_blocks(refs, n_blocks, rows_here)
    store_sides(*add_blocks(left, key, scale, blocks, None, None), refs)


def both_kernel(n_blocks, own, other, *refs):
    refs = list(refs)
    rows_here, wide = refs[-1].shape
    left, key, scale = left_of((own, other), rows_here)
    blocks = take_blocks(refs, n_blocks, rows_here)
    numer = jnp.concatenate([ref[:, : wide - 128] for ref in refs[:2]], axis=0)
    denom = jnp.concatenate([ref[:, wide - 128 : wide - 127] for ref in refs[:2]], axis=0)
    store_sides(*add_blocks(left, key, scale, blocks, numer, denom), refs[2:])


def one_kernel(n_blocks, left, *refs):
    refs = list(refs)
    rows_here, wide = refs[-1].shape
    blocks = take_blocks(refs, n_blocks, rows_here)
    numer = refs[0][:, : wide - 128]
    denom = refs[0][:, wide - 128 : wide - 127]
    store_sides(*add_blocks(*left_of((left,), rows_here), blocks, numer, denom), refs[1:])


def mean_kernel(mine, theirs, out):
    width = out.shape[1]
    denom = mine[:, width : width + 1] + theirs[:, width : width + 1]
    out[...] = ((mine[:, :width] + theirs[:, :width]) / denom).astype(BF16)


def whole_in_vmem(count):
    return [pl.BlockSpec(memory_space=pltpu.VMEM)] * count


def call(kernel, shapes, args, aliases={}):
    return pl.pallas_call(
        kernel,
        out_shape=[jax.ShapeDtypeStruct(shape, dtype) for shape, dtype in shapes],
        in_specs=whole_in_vmem(len(args)),
        out_specs=whole_in_vmem(len(shapes)),
        input_output_aliases=aliases,
        compiler_params=pltpu.CompilerParams(vmem_limit_bytes=VMEM_BYTES),
    )(*args)


def start_both(left, right, shape):
    args = list(left) + [half for block in right for half in block]
    return call(functools.partial(start_kernel, len(right)), [(shape, F32)] * 2, args)


def add_both(left, right, before):
    args = list(left) + [half for block in right for half in block] + list(before)
    at = len(args) - 2
    shapes = [(total.shape, F32) for total in before]
    return call(
        functools.partial(both_kernel, len(right)), shapes, args, {at: 0, at + 1: 1}
    )


def add_one(left, right, before):
    args = [left] + [half for block in right for half in block] + [before]
    shapes = [(before.shape, F32)]
    return call(functools.partial(one_kernel, len(right)), shapes, args, {len(args) - 1: 0})[0]


def folded_ring(size):
    return [0] + list(range(1, size, 2)) + list(range(2, size, 2))[::-1]


def together(*arrays):
    return lax.optimization_barrier(arrays)


def by_block(embeddings, group_of, cluster_id):
    rows_here, width = embeddings.shape
    half = rows_here // 2
    slabs = width // 128
    n_blk = lax.axis_size("blk")
    order = folded_ring(n_blk)
    line = (1, rows_here)

    def along(rows):
        hops = [
            (2 * order[i - 1] + core, 2 * order[i] + 1 - core)
            for i in range(n_blk)
            for core in range(2)
        ]
        return lax.ppermute(rows, ("blk", "pair"), hops)

    def across(rows):
        return lax.ppermute(rows, ("sub", "pair"), [(0, 3), (1, 2), (2, 1), (3, 0)])

    def other_core(rows):
        return lax.ppermute(rows, "pair", [(0, 1), (1, 0)])

    whole, first, second = call(
        pack_kernel,
        [
            ((slabs * rows_here + 8, 128), BF16),
            ((slabs * half + 8, 128), BF16),
            ((slabs * half, 128), BF16),
        ],
        [embeddings, group_of.reshape(line), cluster_id.reshape(line)],
    )
    along_by = [(first, second)]
    across_by = []
    for s in range(1, n_blk):
        moved = [along(piece) for piece in along_by[-1]]
        swapped = [across(piece) for piece in along_by[-1]]
        pairs = [together(m, w) for m, w in zip(moved, swapped)]
        along_by.append(tuple(pair[0] for pair in pairs))
        across_by.append(tuple(pair[1] for pair in pairs))
    left = (whole, other_core(whole))
    total = start_both(left, across_by[:-1] + along_by[1:-1], (rows_here, width + 128))
    far_first, mine, theirs = together(along_by[-1][0], *total)
    last = (across(far_first), along(across_by[-1][1]))
    mine, theirs = add_both(left, [across_by[-1], along_by[-1]], (mine, theirs))
    theirs = other_core(add_one(left[1], [last], theirs))
    mine = add_one(left[0], [last], mine)
    (out,) = call(mean_kernel, [((rows_here, width), BF16)], [mine, theirs])
    return out


def per_device(embeddings, group_of, cluster_id):
    rows_here, width = embeddings.shape
    devices = lax.axis_size("blk") * lax.axis_size("sub") * lax.axis_size("pair")
    small = devices * rows_here * width * 2 <= GATHER_LIMIT
    fits = width % 128 == 0 and rows_here % 32 == 0 and rows_here <= 512
    if small and fits and lax.axis_size("sub") == 2 and lax.axis_size("pair") == 2:
        return by_block(embeddings, group_of, cluster_id)
    return by_group(embeddings, group_of, cluster_id)


def solution(mesh):
    return jax.shard_map(
        per_device,
        mesh=mesh,
        in_specs=(
            P(("island", "blk", "sub", "pair"), None),
            P(("island", "blk", "sub", "pair"), None),
            P(("island", "blk", "sub", "pair")),
        ),
        out_specs=P(("island", "blk", "sub", "pair"), None),
        check_vma=False,
    )
```

time: 58.5 us -> 40.5 us (0.69)
  Pallas kernels: 25.8 us -> 6.5 us
  waiting for transfers between devices: 8.31 us -> 13.2 us
  starting transfers between devices: 22.9 us -> 19 us
    pallas_call x6, Pallas kernels: 25.8 us -> 6.5 us  [call(): pl.pallas_call(kernel, out_shape=[jax.ShapeDtypeStruct(shape, dtype) for...]
    ppermute x16, waiting for transfers between devices: 8.31 us -> 13.2 us  [the longest x7 5.9 us: across(): return lax.ppermute(rows, ('sub', 'pair'), [(0, 3), (1, 2), (2, 1), (3, 0)])]
    ppermute x16, starting transfers between devices: 22.9 us -> 19 us  [the longest x7 12 us: along(): return lax.ppermute(rows, ('blk', 'pair'), hops)]
    unnamed x4 -> x6, local copies, waits for them, and re-layouts: 1.23 us -> 1.65 us
  transfers between devices with their start and end apart: 16 -> 16, of which waited for: 5 -> 7; matrix products, arithmetic and copies ran while one was open for 0% -> 0% of each run, Pallas kernels for 9% -> 12%
where the time goes in v9:
time: 40.5 us; the launch traced here: 40.4 us
  starting transfers between devices  19 us (47%)
  waiting for transfers between devices  13.2 us (33%)
  Pallas kernels  6.5 us (16%)
  local copies, waits for them, and re-layouts  1.65 us (4%)
    ppermute x7, starting transfers between devices, along(): return lax.ppermute(rows, ('blk', 'pair'), hops)  12 us
    pallas_call x6, Pallas kernels, call(): pl.pallas_call(kernel, out_shape=[jax.ShapeDtypeStruct(shape, dtype) for...  6.5 us
    ppermute x7, waiting for transfers between devices, across(): return lax.ppermute(rows, ('sub', 'pair'), [(0, 3), (1, 2), (2, 1), (3, 0)])  5.9 us
    ppermute x7, waiting for transfers between devices, along(): return lax.ppermute(rows, ('blk', 'pair'), hops)  5.85 us
    ppermute x7, starting transfers between devices, across(): return lax.ppermute(rows, ('sub', 'pair'), [(0, 3), (1, 2), (2, 1), (3, 0)])  5.15 us
    ppermute x2, starting transfers between devices, other_core(): return lax.ppermute(rows, 'pair', [(0, 1), (1, 0)])  1.79 us
    unnamed x6, local copies, waits for them, and re-layouts  1.65 us
    ppermute x2, waiting for transfers between devices, other_core(): return lax.ppermute(rows, 'pair', [(0, 1), (1, 0)])  1.42 us
  transfers between devices with their start and end apart: 16, of which 7 were waited for; matrix products, arithmetic and copies ran while one was open for 0% of the time, Pallas kernels for 12%

profile of v9, /device:TPU:0, one launch (start us, length us, event | category | flops | bytes accessed | tf_op | source)
XLA Modules:
  0.0 40.4 jit_solution(2197564461332783051)
XLA Ops:
  0.0 0.0 copy-start.2
  0.0 0.0 copy-start.1
  0.0 0.7 %copy-done.2 = s32[192]{0:T(256)S(1)} copy-done((s32[192]{0:T(256)S(1)}, s32[192]{0:T(256)}, u32[]{:S(2)}) %copy-start.2) | copy-done | bytes 792
  0.7 0.0 copy-done.1
  0.7 0.0 copy-start
  0.7 1.0 %copy-done = bf16[192,768]{1,0:T(8,128)(2,1)S(1)} copy-done((bf16[192,768]{1,0:T(8,128)(2,1)S(1)}, bf16[192,768]{1,0:T(8,128)(2,1)}, u32[]{:S(2)}) %copy-start) | copy-done | bytes 294936
  1.7 0.1 shard_map.37
  1.7 2.5 %collective-permute-start = (bf16[584,128]{1,0:T(8,128)(2,1)S(1)}, bf16[584,128]{1,0:T(8,128)(2,1)S(1)}, u32[]{:S(2)}, u32[]{:S(2)}) collective-permute-start(bf16[584,128]{1,0:T(8,128)(2,1)S(1)} %get-tuple-element.28), channel_id=1, source_target_pairs={{8,1},{9,0},{0,5},{1,4},{4,13},{5,12},{12,9},{13,8},{10,3},{11,2},... | collective-permute-start | bytes 448520 | tf_op jit(solution)/shard_map/ppermute | solution.py:256
  4.3 1.8 %collective-permute-start.1 = (bf16[584,128]{1,0:T(8,128)(2,1)S(1)}, bf16[584,128]{1,0:T(8,128)(2,1)S(1)}, u32[]{:S(2)}, u32[]{:S(2)}) collective-permute-start(bf16[584,128]{1,0:T(8,128)(2,1)S(1)} %get-tuple-element.28), channel_id=1, source_target_pairs={{0,3},{1,2},{2,1},{3,0},{4,7},{5,6},{6,5},{7,4},{8,11},{9,10},{10,... | collective-permute-start | bytes 448520 | tf_op jit(solution)/shard_map/ppermute | solution.py:259
  6.0 2.0 %collective-permute-start.7 = (bf16[576,128]{1,0:T(8,128)(2,1)S(1)}, bf16[576,128]{1,0:T(8,128)(2,1)S(1)}, u32[]{:S(2)}, u32[]{:S(2)}) collective-permute-start(bf16[576,128]{1,0:T(8,128)(2,1)S(1)} %get-tuple-element.33), channel_id=1, source_target_pairs={{8,1},{9,0},{0,5},{1,4},{4,13},{5,12},{12,9},{13,8},{10,3},{11,2},... | collective-permute-start | bytes 442376 | tf_op jit(solution)/shard_map/ppermute | solution.py:256
  8.1 0.8 %collective-permute-start.8 = (bf16[576,128]{1,0:T(8,128)(2,1)S(1)}, bf16[576,128]{1,0:T(8,128)(2,1)S(1)}, u32[]{:S(2)}, u32[]{:S(2)}) collective-permute-start(bf16[576,128]{1,0:T(8,128)(2,1)S(1)} %get-tuple-element.33), channel_id=1, source_target_pairs={{0,3},{1,2},{2,1},{3,0},{4,7},{5,6},{6,5},{7,4},{8,11},{9,10},{10,... | collective-permute-start | bytes 442376 | tf_op jit(solution)/shard_map/ppermute | solution.py:259
  8.9 0.0 collective-permute-done.refs_4_
  8.9 0.8 %collective-permute-done.1.refs_0_ = bf16[584,128]{1,0:T(8,128)(2,1)S(1)} collective-permute-done((bf16[584,128]{1,0:T(8,128)(2,1)S(1)}, bf16[584,128]{1,0:T(8,128)(2,1)S(1)}, u32[]{:S(2)}, u32[]{:S(2)}) %collective-permute-start.1) | collective-permute-done | bytes 149536 | tf_op jit(solution)/shard_map/ppermute | solution.py:259
  9.7 3.9 %collective-permute-start.2 = (bf16[584,128]{1,0:T(8,128)(2,1)S(1)}, bf16[584,128]{1,0:T(8,128)(2,1)S(1)}, u32[]{:S(2)}, u32[]{:S(2)}) collective-permute-start(bf16[584,128]{1,0:T(8,128)(2,1)S(1)} %collective-permute-done.refs_4_), channel_id=1, source_target_pairs={{8,1},{9,0},{0,5},{1,4},{4,13},{5,12},{12,9},{13,8},{10,3},{11,2},... | collective-permute-start | bytes 448520 | tf_op jit(solution)/shard_map/ppermute | solution.py:256
  13.6 0.0 collective-permute-start.3
  13.6 1.6 %collective-permute-start.6 = (bf16[1160,128]{1,0:T(8,128)(2,1)S(1)}, bf16[1160,128]{1,0:T(8,128)(2,1)S(1)}, u32[]{:S(2)}, u32[]{:S(2)}) collective-permute-start(bf16[1160,128]{1,0:T(8,128)(2,1)S(1)} %get-tuple-element.27.own.left), channel_id=1, source_target_pairs={{0,1},{1,0},{2,3},{3,2},{4,5},{5,4},{6,7},{7,6},{8,9},{9,8},{10,11... | collective-permute-start | bytes 890888 | tf_op jit(solution)/shard_map/ppermute | solution.py:262
  15.2 0.0 collective-permute-done.7.refs_5_
  15.2 0.0 collective-permute-done.8.refs_1_
  15.2 0.2 collective-permute-start.10
  15.4 1.2 %collective-permute-start.9 = (bf16[576,128]{1,0:T(8,128)(2,1)S(1)}, bf16[576,128]{1,0:T(8,128)(2,1)S(1)}, u32[]{:S(2)}, u32[]{:S(2)}) collective-permute-start(bf16[576,128]{1,0:T(8,128)(2,1)S(1)} %collective-permute-done.7.refs_5_), channel_id=1, source_target_pairs={{8,1},{9,0},{0,5},{1,4},{4,13},{5,12},{12,9},{13,8},{10,3},{11,2},... | collective-permute-start | bytes 442376 | tf_op jit(solution)/shard_map/ppermute | solution.py:256
  16.6 0.0 collective-permute-done.2.refs_6_
  16.6 3.1 %collective-permute-done.3.refs_2_ = bf16[584,128]{1,0:T(8,128)(2,1)S(1)} collective-permute-done((bf16[584,128]{1,0:T(8,128)(2,1)S(1)}, bf16[584,128]{1,0:T(8,128)(2,1)S(1)}, u32[]{:S(2)}, u32[]{:S(2)}) %collective-permute-start.3) | collective-permute-done | bytes 149536 | tf_op jit(solution)/shard_map/ppermute | solution.py:259
  19.7 0.9 %collective-permute-start.4 = (bf16[584,128]{1,0:T(8,128)(2,1)S(1)}, bf16[584,128]{1,0:T(8,128)(2,1)S(1)}, u32[]{:S(2)}, u32[]{:S(2)}) collective-permute-start(bf16[584,128]{1,0:T(8,128)(2,1)S(1)} %collective-permute-done.2.refs_6_), channel_id=1, source_target_pairs={{8,1},{9,0},{0,5},{1,4},{4,13},{5,12},{12,9},{13,8},{10,3},{11,2},... | collective-permute-start | bytes 448520 | tf_op jit(solution)/shard_map/ppermute | solution.py:256
  20.6 0.6 %collective-permute-start.5 = (bf16[584,128]{1,0:T(8,128)(2,1)S(1)}, bf16[584,128]{1,0:T(8,128)(2,1)S(1)}, u32[]{:S(2)}, u32[]{:S(2)}) collective-permute-start(bf16[584,128]{1,0:T(8,128)(2,1)S(1)} %collective-permute-done.2.refs_6_), channel_id=1, source_target_pairs={{0,3},{1,2},{2,1},{3,0},{4,7},{5,6},{6,5},{7,4},{8,11},{9,10},{10,... | collective-permute-start | bytes 448520 | tf_op jit(solution)/shard_map/ppermute | solution.py:259
  21.2 1.7 %collective-permute-done.10.refs_3_ = bf16[576,128]{1,0:T(8,128)(2,1)S(1)} collective-permute-done((bf16[576,128]{1,0:T(8,128)(2,1)S(1)}, bf16[576,128]{1,0:T(8,128)(2,1)S(1)}, u32[]{:S(2)}, u32[]{:S(2)}) %collective-permute-start.10) | collective-permute-done | bytes 147488 | tf_op jit(solution)/shard_map/ppermute | solution.py:259
  22.9 0.0 collective-permute-done.9.refs_7_
  22.9 0.4 %collective-permute-start.12 = (bf16[576,128]{1,0:T(8,128)(2,1)S(1)}, bf16[576,128]{1,0:T(8,128)(2,1)S(1)}, u32[]{:S(2)}, u32[]{:S(2)}) collective-permute-start(bf16[576,128]{1,0:T(8,128)(2,1)S(1)} %collective-permute-done.9.refs_7_), channel_id=1, source_target_pairs={{8,1},{9,0},{0,5},{1,4},{4,13},{5,12},{12,9},{13,8},{10,3},{11,2},... | collective-permute-start | bytes 442376 | tf_op jit(solution)/shard_map/ppermute | solution.py:256
  23.3 1.0 %collective-permute-start.13 = (bf16[576,128]{1,0:T(8,128)(2,1)S(1)}, bf16[576,128]{1,0:T(8,128)(2,1)S(1)}, u32[]{:S(2)}, u32[]{:S(2)}) collective-permute-start(bf16[576,128]{1,0:T(8,128)(2,1)S(1)} %collective-permute-done.9.refs_7_), channel_id=1, source_target_pairs={{0,3},{1,2},{2,1},{3,0},{4,7},{5,6},{6,5},{7,4},{8,11},{9,10},{10,... | collective-permute-start | bytes 442376 | tf_op jit(solution)/shard_map/ppermute | solution.py:259
  24.3 0.0 collective-permute-done.6.other.left
  24.4 2.7 %shard_map.38 = (f32[192,896]{1,0:T(8,128)S(1)}, f32[192,896]{1,0:T(8,128)S(1)}) custom-call(bf16[1160,128]{1,0:T(8,128)(2,1)S(1)} %get-tuple-element.27.own.left, bf16[1160,128]{1,0:T(8,128)(2,1)S(1)} %collective-permute-done.6.other.left, bf16[584,128]{1,0:T(8,128)(2,1)S(1)} %collective-permute-done.1.refs_0_, ...), custom_call_target="tpu_custom_call" | custom-call | tf_op jit(solution)/shard_map/pallas_call | solution.py:204
  27.1 0.0 collective-permute-done.4.refs_2_
  27.1 0.0 collective-permute-done.5.refs_0_
  27.1 0.8 %collective-permute-start.11 = (bf16[584,128]{1,0:T(8,128)(2,1)S(1)}, bf16[584,128]{1,0:T(8,128)(2,1)S(1)}, u32[]{:S(2)}, u32[]{:S(2)}) collective-permute-start(bf16[584,128]{1,0:T(8,128)(2,1)S(1)} %collective-permute-done.4.refs_2_), channel_id=1, source_target_pairs={{0,3},{1,2},{2,1},{3,0},{4,7},{5,6},{6,5},{7,4},{8,11},{9,10},{10,... | collective-permute-start | bytes 448520 | tf_op jit(solution)/shard_map/ppermute | solution.py:259
  27.9 1.8 %collective-permute-done.12.refs_3_ = bf16[576,128]{1,0:T(8,128)(2,1)S(1)} collective-permute-done((bf16[576,128]{1,0:T(8,128)(2,1)S(1)}, bf16[576,128]{1,0:T(8,128)(2,1)S(1)}, u32[]{:S(2)}, u32[]{:S(2)}) %collective-permute-start.12) | collective-permute-done | bytes 147488 | tf_op jit(solution)/shard_map/ppermute | solution.py:256
  29.7 0.2 collective-permute-done.13.refs_1_
  29.9 1.1 %collective-permute-start.14 = (bf16[576,128]{1,0:T(8,128)(2,1)S(1)}, bf16[576,128]{1,0:T(8,128)(2,1)S(1)}, u32[]{:S(2)}, u32[]{:S(2)}) collective-permute-start(bf16[576,128]{1,0:T(8,128)(2,1)S(1)} %collective-permute-done.13.refs_1_), channel_id=1, source_target_pairs={{8,1},{9,0},{0,5},{1,4},{4,13},{5,12},{12,9},{13,8},{10,3},{11,2},... | collective-permute-start | bytes 442376 | tf_op jit(solution)/shard_map/ppermute | solution.py:256
  31.1 1.6 %shard_map.39 = (f32[192,896]{1,0:T(8,128)S(1)}, f32[192,896]{1,0:T(8,128)S(1)}) custom-call(bf16[1160,128]{1,0:T(8,128)(2,1)S(1)} %get-tuple-element.27.own.left, bf16[1160,128]{1,0:T(8,128)(2,1)S(1)} %collective-permute-done.6.other.left, bf16[584,128]{1,0:T(8,128)(2,1)S(1)} %collective-permute-done.5.refs_0_, ...), custom_call_target="tpu_custom_call", output_to_operand_aliasing={{0}: (6, {}), {1}: (7, {})} | custom-call | tf_op jit(solution)/shard_map/pallas_call | solution.py:204
  32.7 4.0 %collective-permute-done.14.refs_1_ = bf16[576,128]{1,0:T(8,128)(2,1)S(1)} collective-permute-done((bf16[576,128]{1,0:T(8,128)(2,1)S(1)}, bf16[576,128]{1,0:T(8,128)(2,1)S(1)}, u32[]{:S(2)}, u32[]{:S(2)}) %collective-permute-start.14) | collective-permute-done | bytes 147488 | tf_op jit(solution)/shard_map/ppermute | solution.py:256
  36.7 0.0 collective-permute-done.11.refs_0_
  36.7 0.6 %shard_map.41 = f32[192,896]{1,0:T(8,128)S(1)} custom-call(bf16[1160,128]{1,0:T(8,128)(2,1)S(1)} %collective-permute-done.6.other.left, bf16[584,128]{1,0:T(8,128)(2,1)S(1)} %collective-permute-done.11.refs_0_, bf16[576,128]{1,0:T(8,128)(2,1)S(1)} %collective-permute-done.14.refs_1_, ...), custom_call_target="tpu_custom_call", output_to_operand_aliasing={{}: (3, {})} | custom-call | tf_op jit(solution)/shard_map/pallas_call | solution.py:204
  37.3 0.2 collective-permute-start.15
  37.5 0.6 %shard_map.40.mine = f32[192,896]{1,0:T(8,128)S(1)} custom-call(bf16[1160,128]{1,0:T(8,128)(2,1)S(1)} %get-tuple-element.27.own.left, bf16[584,128]{1,0:T(8,128)(2,1)S(1)} %collective-permute-done.11.refs_0_, bf16[576,128]{1,0:T(8,128)(2,1)S(1)} %collective-permute-done.14.refs_1_, ...), custom_call_target="tpu_custom_call", output_to_operand_aliasing={{}: (3, {})} | custom-call | tf_op jit(solution)/shard_map/pallas_call | solution.py:204
  38.1 1.4 %collective-permute-done.15.theirs = f32[192,896]{1,0:T(8,128)S(1)} collective-permute-done((f32[192,896]{1,0:T(8,128)S(1)}, f32[192,896]{1,0:T(8,128)S(1)}, u32[]{:S(2)}, u32[]{:S(2)}) %collective-permute-start.15) | collective-permute-done | bytes 688160 | tf_op jit(solution)/shard_map/ppermute | solution.py:262
  39.5 0.8 %shard_map.42 = bf16[192,768]{1,0:T(8,128)(2,1)} custom-call(f32[192,896]{1,0:T(8,128)S(1)} %shard_map.40.mine, f32[192,896]{1,0:T(8,128)S(1)} %collective-permute-done.15.theirs), custom_call_target="tpu_custom_call" | custom-call | tf_op jit(solution)/shard_map/pallas_call | solution.py:204
Async XLA Ops:
  0.0 0.7 %copy-start.2 = (s32[192]{0:T(256)S(1)}, s32[192]{0:T(256)}, u32[]{:S(2)}) copy-start(s32[192]{0:T(256)} %param.5) | copy-start | bytes 2308
  0.0 0.7 %copy-start.1 = (s32[192,1]{0,1:T(1,128)S(1)}, s32[192,1]{0,1:T(1,128)}, u32[]{:S(2)}) copy-start(s32[192,1]{0,1:T(1,128)} %param.4) | copy-start | bytes 2308
  0.7 1.0 %copy-start = (bf16[192,768]{1,0:T(8,128)(2,1)S(1)}, bf16[192,768]{1,0:T(8,128)(2,1)}, u32[]{:S(2)}) copy-start(bf16[192,768]{1,0:T(8,128)(2,1)} %rows.1) | copy-start | bytes 884740
  1.7 7.1 %collective-permute-start = (bf16[584,128]{1,0:T(8,128)(2,1)S(1)}, bf16[584,128]{1,0:T(8,128)(2,1)S(1)}, u32[]{:S(2)}, u32[]{:S(2)}) collective-permute-start(bf16[584,128]{1,0:T(8,128)(2,1)S(1)} %get-tuple-element.28), channel_id=1, source_target_pairs={{8,1},{9,0},{0,5},{1,4},{4,13},{5,12},{12,9},{13,8},{10,3},{11,2},... | collective-permute-start | bytes 448520 | tf_op jit(solution)/shard_map/ppermute | solution.py:256
  4.3 5.5 %collective-permute-start.1 = (bf16[584,128]{1,0:T(8,128)(2,1)S(1)}, bf16[584,128]{1,0:T(8,128)(2,1)S(1)}, u32[]{:S(2)}, u32[]{:S(2)}) collective-permute-start(bf16[584,128]{1,0:T(8,128)(2,1)S(1)} %get-tuple-element.28), channel_id=1, source_target_pairs={{0,3},{1,2},{2,1},{3,0},{4,7},{5,6},{6,5},{7,4},{8,11},{9,10},{10,... | collective-permute-start | bytes 448520 | tf_op jit(solution)/shard_map/ppermute | solution.py:259
  6.0 9.2 %collective-permute-start.7 = (bf16[576,128]{1,0:T(8,128)(2,1)S(1)}, bf16[576,128]{1,0:T(8,128)(2,1)S(1)}, u32[]{:S(2)}, u32[]{:S(2)}) collective-permute-start(bf16[576,128]{1,0:T(8,128)(2,1)S(1)} %get-tuple-element.33), channel_id=1, source_target_pairs={{8,1},{9,0},{0,5},{1,4},{4,13},{5,12},{12,9},{13,8},{10,3},{11,2},... | collective-permute-start | bytes 442376 | tf_op jit(solution)/shard_map/ppermute | solution.py:256
  8.1 7.1 %collective-permute-start.8 = (bf16[576,128]{1,0:T(8,128)(2,1)S(1)}, bf16[576,128]{1,0:T(8,128)(2,1)S(1)}, u32[]{:S(2)}, u32[]{:S(2)}) collective-permute-start(bf16[576,128]{1,0:T(8,128)(2,1)S(1)} %get-tuple-element.33), channel_id=1, source_target_pairs={{0,3},{1,2},{2,1},{3,0},{4,7},{5,6},{6,5},{7,4},{8,11},{9,10},{10,... | collective-permute-start | bytes 442376 | tf_op jit(solution)/shard_map/ppermute | solution.py:259
  9.7 6.9 %collective-permute-start.2 = (bf16[584,128]{1,0:T(8,128)(2,1)S(1)}, bf16[584,128]{1,0:T(8,128)(2,1)S(1)}, u32[]{:S(2)}, u32[]{:S(2)}) collective-permute-start(bf16[584,128]{1,0:T(8,128)(2,1)S(1)} %collective-permute-done.refs_4_), channel_id=1, source_target_pairs={{8,1},{9,0},{0,5},{1,4},{4,13},{5,12},{12,9},{13,8},{10,3},{11,2},... | collective-permute-start | bytes 448520 | tf_op jit(solution)/shard_map/ppermute | solution.py:256
  13.6 6.1 %collective-permute-start.3 = (bf16[584,128]{1,0:T(8,128)(2,1)S(1)}, bf16[584,128]{1,0:T(8,128)(2,1)S(1)}, u32[]{:S(2)}, u32[]{:S(2)}) collective-permute-start(bf16[584,128]{1,0:T(8,128)(2,1)S(1)} %collective-permute-done.refs_4_), channel_id=1, source_target_pairs={{0,3},{1,2},{2,1},{3,0},{4,7},{5,6},{6,5},{7,4},{8,11},{9,10},{10,... | collective-permute-start | bytes 448520 | tf_op jit(solution)/shard_map/ppermute | solution.py:259
  13.6 10.8 %collective-permute-start.6 = (bf16[1160,128]{1,0:T(8,128)(2,1)S(1)}, bf16[1160,128]{1,0:T(8,128)(2,1)S(1)}, u32[]{:S(2)}, u32[]{:S(2)}) collective-permute-start(bf16[1160,128]{1,0:T(8,128)(2,1)S(1)} %get-tuple-element.27.own.left), channel_id=1, source_target_pairs={{0,1},{1,0},{2,3},{3,2},{4,5},{5,4},{6,7},{7,6},{8,9},{9,8},{10,11... | collective-permute-start | bytes 890888 | tf_op jit(solution)/shard_map/ppermute | solution.py:262
  15.2 7.7 %collective-permute-start.10 = (bf16[576,128]{1,0:T(8,128)(2,1)S(1)}, bf16[576,128]{1,0:T(8,128)(2,1)S(1)}, u32[]{:S(2)}, u32[]{:S(2)}) collective-permute-start(bf16[576,128]{1,0:T(8,128)(2,1)S(1)} %collective-permute-done.7.refs_5_), channel_id=1, source_target_pairs={{0,3},{1,2},{2,1},{3,0},{4,7},{5,6},{6,5},{7,4},{8,11},{9,10},{10,... | collective-permute-start | bytes 442376 | tf_op jit(solution)/shard_map/ppermute | solution.py:259
  15.4 7.5 %collective-permute-start.9 = (bf16[576,128]{1,0:T(8,128)(2,1)S(1)}, bf16[576,128]{1,0:T(8,128)(2,1)S(1)}, u32[]{:S(2)}, u32[]{:S(2)}) collective-permute-start(bf16[576,128]{1,0:T(8,128)(2,1)S(1)} %collective-permute-done.7.refs_5_), channel_id=1, source_target_pairs={{8,1},{9,0},{0,5},{1,4},{4,13},{5,12},{12,9},{13,8},{10,3},{11,2},... | collective-permute-start | bytes 442376 | tf_op jit(solution)/shard_map/ppermute | solution.py:256
  19.7 7.3 %collective-permute-start.4 = (bf16[584,128]{1,0:T(8,128)(2,1)S(1)}, bf16[584,128]{1,0:T(8,128)(2,1)S(1)}, u32[]{:S(2)}, u32[]{:S(2)}) collective-permute-start(bf16[584,128]{1,0:T(8,128)(2,1)S(1)} %collective-permute-done.2.refs_6_), channel_id=1, source_target_pairs={{8,1},{9,0},{0,5},{1,4},{4,13},{5,12},{12,9},{13,8},{10,3},{11,2},... | collective-permute-start | bytes 448520 | tf_op jit(solution)/shard_map/ppermute | solution.py:256
  20.6 6.4 %collective-permute-start.5 = (bf16[584,128]{1,0:T(8,128)(2,1)S(1)}, bf16[584,128]{1,0:T(8,128)(2,1)S(1)}, u32[]{:S(2)}, u32[]{:S(2)}) collective-permute-start(bf16[584,128]{1,0:T(8,128)(2,1)S(1)} %collective-permute-done.2.refs_6_), channel_id=1, source_target_pairs={{0,3},{1,2},{2,1},{3,0},{4,7},{5,6},{6,5},{7,4},{8,11},{9,10},{10,... | collective-permute-start | bytes 448520 | tf_op jit(solution)/shard_map/ppermute | solution.py:259
  22.9 6.8 %collective-permute-start.12 = (bf16[576,128]{1,0:T(8,128)(2,1)S(1)}, bf16[576,128]{1,0:T(8,128)(2,1)S(1)}, u32[]{:S(2)}, u32[]{:S(2)}) collective-permute-start(bf16[576,128]{1,0:T(8,128)(2,1)S(1)} %collective-permute-done.9.refs_7_), channel_id=1, source_target_pairs={{8,1},{9,0},{0,5},{1,4},{4,13},{5,12},{12,9},{13,8},{10,3},{11,2},... | collective-permute-start | bytes 442376 | tf_op jit(solution)/shard_map/ppermute | solution.py:256
  23.3 6.6 %collective-permute-start.13 = (bf16[576,128]{1,0:T(8,128)(2,1)S(1)}, bf16[576,128]{1,0:T(8,128)(2,1)S(1)}, u32[]{:S(2)}, u32[]{:S(2)}) collective-permute-start(bf16[576,128]{1,0:T(8,128)(2,1)S(1)} %collective-permute-done.9.refs_7_), channel_id=1, source_target_pairs={{0,3},{1,2},{2,1},{3,0},{4,7},{5,6},{6,5},{7,4},{8,11},{9,10},{10,... | collective-permute-start | bytes 442376 | tf_op jit(solution)/shard_map/ppermute | solution.py:259
  27.1 9.6 %collective-permute-start.11 = (bf16[584,128]{1,0:T(8,128)(2,1)S(1)}, bf16[584,128]{1,0:T(8,128)(2,1)S(1)}, u32[]{:S(2)}, u32[]{:S(2)}) collective-permute-start(bf16[584,128]{1,0:T(8,128)(2,1)S(1)} %collective-permute-done.4.refs_2_), channel_id=1, source_target_pairs={{0,3},{1,2},{2,1},{3,0},{4,7},{5,6},{6,5},{7,4},{8,11},{9,10},{10,... | collective-permute-start | bytes 448520 | tf_op jit(solution)/shard_map/ppermute | solution.py:259
  29.9 6.8 %collective-permute-start.14 = (bf16[576,128]{1,0:T(8,128)(2,1)S(1)}, bf16[576,128]{1,0:T(8,128)(2,1)S(1)}, u32[]{:S(2)}, u32[]{:S(2)}) collective-permute-start(bf16[576,128]{1,0:T(8,128)(2,1)S(1)} %collective-permute-done.13.refs_1_), channel_id=1, source_target_pairs={{8,1},{9,0},{0,5},{1,4},{4,13},{5,12},{12,9},{13,8},{10,3},{11,2},... | collective-permute-start | bytes 442376 | tf_op jit(solution)/shard_map/ppermute | solution.py:256
  37.3 2.2 %collective-permute-start.15 = (f32[192,896]{1,0:T(8,128)S(1)}, f32[192,896]{1,0:T(8,128)S(1)}, u32[]{:S(2)}, u32[]{:S(2)}) collective-permute-start(f32[192,896]{1,0:T(8,128)S(1)} %shard_map.41), channel_id=1, source_target_pairs={{0,1},{1,0},{2,3},{3,2},{4,5},{5,4},{6,7},{7,6},{8,9},{9,8},{10,11... | collective-permute-start | bytes 2064392 | tf_op jit(solution)/shard_map/ppermute | solution.py:262

commit v10 on v9

--- a/solution.py
+++ b/solution.py
@@ -272,15 +272,24 @@
     )
     along_by = [(first, second)]
     across_by = []
+    other = other_core(whole)
     for s in range(1, n_blk):
-        moved = [along(piece) for piece in along_by[-1]]
-        swapped = [across(piece) for piece in along_by[-1]]
-        pairs = [together(m, w) for m, w in zip(moved, swapped)]
-        along_by.append(tuple(pair[0] for pair in pairs))
-        across_by.append(tuple(pair[1] for pair in pairs))
-    left = (whole, other_core(whole))
+        near, far = along_by[-1]
+        if s == 2:
+            other, far, *ended = together(other, far, *across_by[-1])
+        elif s > 2:
+            far, *ended = together(far, *across_by[-1])
+        if s > 1:
+            along_by[-1], across_by[-1] = (near, far), tuple(ended)
+        across_by.append((across(near), across(far)))
+        along_by.append((along(near), along(far)))
+    left = (whole, other)
     total = start_both(left, across_by[:-1] + along_by[1:-1], (rows_here, width + 128))
     far_first, mine, theirs = together(along_by[-1][0], *total)
+    along_by[-1], across_by[-1] = (
+        (far_first, along_by[-1][1]),
+        together(*across_by[-1], along_by[-1][1])[:2],
+    )
     last = (across(far_first), along(across_by[-1][1]))
     mine, theirs = add_both(left, [across_by[-1], along_by[-1]], (mine, theirs))
     theirs = other_core(add_one(left[1], [last], theirs))

time: 40.5 us -> 41.5 us (1.025)
  starting transfers between devices: 19 us -> 20.9 us
  waiting for transfers between devices: 13.2 us -> 12.2 us
    ppermute x7, waiting for transfers between devices: 5.9 us -> 2.6 us  [across(): return lax.ppermute(rows, ('sub', 'pair'), [(0, 3), (1, 2), (2, 1), (3, 0)])]
    ppermute x7, waiting for transfers between devices: 5.85 us -> 8.17 us  [along(): return lax.ppermute(rows, ('blk', 'pair'), hops)]
    ppermute x7, starting transfers between devices: 5.15 us -> 7.04 us  [across(): return lax.ppermute(rows, ('sub', 'pair'), [(0, 3), (1, 2), (2, 1), (3, 0)])]
    ppermute x7, starting transfers between devices: 12 us -> 13.2 us  [along(): return lax.ppermute(rows, ('blk', 'pair'), hops)]
    ppermute x2, starting transfers between devices: 1.79 us -> 0.7 us  [other_core(): return lax.ppermute(rows, 'pair', [(0, 1), (1, 0)])]
  transfers between devices with their start and end apart: 16 -> 16, of which waited for: 7 -> 8; matrix products, arithmetic and copies ran while one was open for 0% -> 0% of each run, Pallas kernels for 12% -> 12%
where the time goes in v10:
time: 41.5 us; the launch traced here: 41.3 us
  starting transfers between devices  20.9 us (50%)
  waiting for transfers between devices  12.2 us (29%)
  Pallas kernels  6.5 us (16%)
  local copies, waits for them, and re-layouts  1.65 us (4%)
    ppermute x7, starting transfers between devices, along(): return lax.ppermute(rows, ('blk', 'pair'), hops)  13.2 us
    ppermute x7, waiting for transfers between devices, along(): return lax.ppermute(rows, ('blk', 'pair'), hops)  8.17 us
    ppermute x7, starting transfers between devices, across(): return lax.ppermute(rows, ('sub', 'pair'), [(0, 3), (1, 2), (2, 1), (3, 0)])  7.04 us
    pallas_call x6, Pallas kernels, call(): pl.pallas_call(kernel, out_shape=[jax.ShapeDtypeStruct(shape, dtype) for...  6.5 us
    ppermute x7, waiting for transfers between devices, across(): return lax.ppermute(rows, ('sub', 'pair'), [(0, 3), (1, 2), (2, 1), (3, 0)])  2.6 us
    unnamed x6, local copies, waits for them, and re-layouts  1.65 us
    ppermute x2, waiting for transfers between devices, other_core(): return lax.ppermute(rows, 'pair', [(0, 1), (1, 0)])  1.42 us
  transfers between devices with their start and end apart: 16, of which 8 were waited for; matrix products, arithmetic and copies ran while one was open for 0% of the time, Pallas kernels for 12%

profile of v10, /device:TPU:0, one launch (start us, length us, event | category | flops | bytes accessed | tf_op | source)
XLA Modules:
  0.0 41.3 jit_solution(521115355301332091)
XLA Ops:
  0.0 0.0 copy-start.2
  0.0 0.0 copy-start.1
  0.0 0.7 %copy-done.2 = s32[192]{0:T(256)S(1)} copy-done((s32[192]{0:T(256)S(1)}, s32[192]{0:T(256)}, u32[]{:S(2)}) %copy-start.2) | copy-done | bytes 792
  0.7 0.0 copy-done.1
  0.7 0.0 copy-start
  0.7 1.0 %copy-done = bf16[192,768]{1,0:T(8,128)(2,1)S(1)} copy-done((bf16[192,768]{1,0:T(8,128)(2,1)S(1)}, bf16[192,768]{1,0:T(8,128)(2,1)}, u32[]{:S(2)}) %copy-start) | copy-done | bytes 294936
  1.7 0.1 shard_map.37
  1.7 0.5 %collective-permute-start.3 = (bf16[1160,128]{1,0:T(8,128)(2,1)S(1)}, bf16[1160,128]{1,0:T(8,128)(2,1)S(1)}, u32[]{:S(2)}, u32[]{:S(2)}) collective-permute-start(bf16[1160,128]{1,0:T(8,128)(2,1)S(1)} %get-tuple-element.24.own.left), channel_id=1, source_target_pairs={{0,1},{1,0},{2,3},{3,2},{4,5},{5,4},{6,7},{7,6},{8,9},{9,8},{10,11... | collective-permute-start | bytes 890888 | tf_op jit(solution)/shard_map/ppermute | solution.py:262
  2.3 2.7 %collective-permute-start = (bf16[584,128]{1,0:T(8,128)(2,1)S(1)}, bf16[584,128]{1,0:T(8,128)(2,1)S(1)}, u32[]{:S(2)}, u32[]{:S(2)}) collective-permute-start(bf16[584,128]{1,0:T(8,128)(2,1)S(1)} %get-tuple-element.25), channel_id=1, source_target_pairs={{8,1},{9,0},{0,5},{1,4},{4,13},{5,12},{12,9},{13,8},{10,3},{11,2},... | collective-permute-start | bytes 448520 | tf_op jit(solution)/shard_map/ppermute | solution.py:256
  4.9 1.2 %collective-permute-start.5 = (bf16[584,128]{1,0:T(8,128)(2,1)S(1)}, bf16[584,128]{1,0:T(8,128)(2,1)S(1)}, u32[]{:S(2)}, u32[]{:S(2)}) collective-permute-start(bf16[584,128]{1,0:T(8,128)(2,1)S(1)} %get-tuple-element.25), channel_id=1, source_target_pairs={{0,3},{1,2},{2,1},{3,0},{4,7},{5,6},{6,5},{7,4},{8,11},{9,10},{10,... | collective-permute-start | bytes 448520 | tf_op jit(solution)/shard_map/ppermute | solution.py:259
  6.1 2.6 %collective-permute-start.4 = (bf16[576,128]{1,0:T(8,128)(2,1)S(1)}, bf16[576,128]{1,0:T(8,128)(2,1)S(1)}, u32[]{:S(2)}, u32[]{:S(2)}) collective-permute-start(bf16[576,128]{1,0:T(8,128)(2,1)S(1)} %get-tuple-element.26), channel_id=1, source_target_pairs={{8,1},{9,0},{0,5},{1,4},{4,13},{5,12},{12,9},{13,8},{10,3},{11,2},... | collective-permute-start | bytes 442376 | tf_op jit(solution)/shard_map/ppermute | solution.py:256
  8.7 0.2 collective-permute-start.6
  9.0 1.2 %collective-permute-done.refs_4_ = bf16[584,128]{1,0:T(8,128)(2,1)S(1)} collective-permute-done((bf16[584,128]{1,0:T(8,128)(2,1)S(1)}, bf16[584,128]{1,0:T(8,128)(2,1)S(1)}, u32[]{:S(2)}, u32[]{:S(2)}) %collective-permute-start) | collective-permute-done | bytes 149536 | tf_op jit(solution)/shard_map/ppermute | solution.py:256
  10.2 0.7 %collective-permute-start.1 = (bf16[584,128]{1,0:T(8,128)(2,1)S(1)}, bf16[584,128]{1,0:T(8,128)(2,1)S(1)}, u32[]{:S(2)}, u32[]{:S(2)}) collective-permute-start(bf16[584,128]{1,0:T(8,128)(2,1)S(1)} %collective-permute-done.refs_4_), channel_id=1, source_target_pairs={{8,1},{9,0},{0,5},{1,4},{4,13},{5,12},{12,9},{13,8},{10,3},{11,2},... | collective-permute-start | bytes 448520 | tf_op jit(solution)/shard_map/ppermute | solution.py:256
  10.8 2.5 %collective-permute-done.4.refs_5_ = bf16[576,128]{1,0:T(8,128)(2,1)S(1)} collective-permute-done((bf16[576,128]{1,0:T(8,128)(2,1)S(1)}, bf16[576,128]{1,0:T(8,128)(2,1)S(1)}, u32[]{:S(2)}, u32[]{:S(2)}) %collective-permute-start.4) | collective-permute-done | bytes 147488 | tf_op jit(solution)/shard_map/ppermute | solution.py:256
  13.3 1.2 %collective-permute-start.8 = (bf16[584,128]{1,0:T(8,128)(2,1)S(1)}, bf16[584,128]{1,0:T(8,128)(2,1)S(1)}, u32[]{:S(2)}, u32[]{:S(2)}) collective-permute-start(bf16[584,128]{1,0:T(8,128)(2,1)S(1)} %collective-permute-done.refs_4_), channel_id=1, source_target_pairs={{0,3},{1,2},{2,1},{3,0},{4,7},{5,6},{6,5},{7,4},{8,11},{9,10},{10,... | collective-permute-start | bytes 448520 | tf_op jit(solution)/shard_map/ppermute | solution.py:259
  14.5 0.2 collective-permute-done.6.refs_1_
  14.7 0.0 collective-permute-done.5.refs_0_
  14.7 0.0 collective-permute-done.3.other.left
  14.7 2.0 %collective-permute-start.7 = (bf16[576,128]{1,0:T(8,128)(2,1)S(1)}, bf16[576,128]{1,0:T(8,128)(2,1)S(1)}, u32[]{:S(2)}, u32[]{:S(2)}) collective-permute-start(bf16[576,128]{1,0:T(8,128)(2,1)S(1)} %collective-permute-done.4.refs_5_), channel_id=1, source_target_pairs={{8,1},{9,0},{0,5},{1,4},{4,13},{5,12},{12,9},{13,8},{10,3},{11,2},... | collective-permute-start | bytes 442376 | tf_op jit(solution)/shard_map/ppermute | solution.py:256
  16.6 1.3 %collective-permute-start.9 = (bf16[576,128]{1,0:T(8,128)(2,1)S(1)}, bf16[576,128]{1,0:T(8,128)(2,1)S(1)}, u32[]{:S(2)}, u32[]{:S(2)}) collective-permute-start(bf16[576,128]{1,0:T(8,128)(2,1)S(1)} %collective-permute-done.4.refs_5_), channel_id=1, source_target_pairs={{0,3},{1,2},{2,1},{3,0},{4,7},{5,6},{6,5},{7,4},{8,11},{9,10},{10,... | collective-permute-start | bytes 442376 | tf_op jit(solution)/shard_map/ppermute | solution.py:259
  17.9 0.0 collective-permute-done.1.refs_6_
  17.9 0.9 %collective-permute-start.2 = (bf16[584,128]{1,0:T(8,128)(2,1)S(1)}, bf16[584,128]{1,0:T(8,128)(2,1)S(1)}, u32[]{:S(2)}, u32[]{:S(2)}) collective-permute-start(bf16[584,128]{1,0:T(8,128)(2,1)S(1)} %collective-permute-done.1.refs_6_), channel_id=1, source_target_pairs={{8,1},{9,0},{0,5},{1,4},{4,13},{5,12},{12,9},{13,8},{10,3},{11,2},... | collective-permute-start | bytes 448520 | tf_op jit(solution)/shard_map/ppermute | solution.py:256
  18.7 1.4 %collective-permute-start.11 = (bf16[584,128]{1,0:T(8,128)(2,1)S(1)}, bf16[584,128]{1,0:T(8,128)(2,1)S(1)}, u32[]{:S(2)}, u32[]{:S(2)}) collective-permute-start(bf16[584,128]{1,0:T(8,128)(2,1)S(1)} %collective-permute-done.1.refs_6_), channel_id=1, source_target_pairs={{0,3},{1,2},{2,1},{3,0},{4,7},{5,6},{6,5},{7,4},{8,11},{9,10},{10,... | collective-permute-start | bytes 448520 | tf_op jit(solution)/shard_map/ppermute | solution.py:259
  20.2 0.0 collective-permute-done.8.refs_2_
  20.2 1.1 %collective-permute-done.7.refs_7_ = bf16[576,128]{1,0:T(8,128)(2,1)S(1)} collective-permute-done((bf16[576,128]{1,0:T(8,128)(2,1)S(1)}, bf16[576,128]{1,0:T(8,128)(2,1)S(1)}, u32[]{:S(2)}, u32[]{:S(2)}) %collective-permute-start.7) | collective-permute-done | bytes 147488 | tf_op jit(solution)/shard_map/ppermute | solution.py:256
  21.3 1.2 %collective-permute-done.9.refs_3_ = bf16[576,128]{1,0:T(8,128)(2,1)S(1)} collective-permute-done((bf16[576,128]{1,0:T(8,128)(2,1)S(1)}, bf16[576,128]{1,0:T(8,128)(2,1)S(1)}, u32[]{:S(2)}, u32[]{:S(2)}) %collective-permute-start.9) | collective-permute-done | bytes 147488 | tf_op jit(solution)/shard_map/ppermute | solution.py:259
  22.4 2.4 %collective-permute-start.13 = (bf16[576,128]{1,0:T(8,128)(2,1)S(1)}, bf16[576,128]{1,0:T(8,128)(2,1)S(1)}, u32[]{:S(2)}, u32[]{:S(2)}) collective-permute-start(bf16[576,128]{1,0:T(8,128)(2,1)S(1)} %collective-permute-done.7.refs_7_), channel_id=1, source_target_pairs={{8,1},{9,0},{0,5},{1,4},{4,13},{5,12},{12,9},{13,8},{10,3},{11,2},... | collective-permute-start | bytes 442376 | tf_op jit(solution)/shard_map/ppermute | solution.py:256
  24.8 0.0 collective-permute-start.12
  24.8 2.7 %shard_map.38 = (f32[192,896]{1,0:T(8,128)S(1)}, f32[192,896]{1,0:T(8,128)S(1)}) custom-call(bf16[1160,128]{1,0:T(8,128)(2,1)S(1)} %get-tuple-element.24.own.left, bf16[1160,128]{1,0:T(8,128)(2,1)S(1)} %collective-permute-done.3.other.left, bf16[584,128]{1,0:T(8,128)(2,1)S(1)} %collective-permute-done.5.refs_0_, ...), custom_call_target="tpu_custom_call" | custom-call | tf_op jit(solution)/shard_map/pallas_call | solution.py:204
  27.5 0.0 collective-permute-done.2.refs_2_
  27.5 1.8 %collective-permute-start.10 = (bf16[584,128]{1,0:T(8,128)(2,1)S(1)}, bf16[584,128]{1,0:T(8,128)(2,1)S(1)}, u32[]{:S(2)}, u32[]{:S(2)}) collective-permute-start(bf16[584,128]{1,0:T(8,128)(2,1)S(1)} %collective-permute-done.2.refs_2_), channel_id=1, source_target_pairs={{0,3},{1,2},{2,1},{3,0},{4,7},{5,6},{6,5},{7,4},{8,11},{9,10},{10,... | collective-permute-start | bytes 448520 | tf_op jit(solution)/shard_map/ppermute | solution.py:259
  29.3 0.0 collective-permute-done.11.refs_0_
  29.3 0.0 collective-permute-done.13.refs_3_
  29.4 1.3 %collective-permute-done.12.refs_1_ = bf16[576,128]{1,0:T(8,128)(2,1)S(1)} collective-permute-done((bf16[576,128]{1,0:T(8,128)(2,1)S(1)}, bf16[576,128]{1,0:T(8,128)(2,1)S(1)}, u32[]{:S(2)}, u32[]{:S(2)}) %collective-permute-start.12) | collective-permute-done | bytes 147488 | tf_op jit(solution)/shard_map/ppermute | solution.py:259
  30.6 2.0 %collective-permute-start.14 = (bf16[576,128]{1,0:T(8,128)(2,1)S(1)}, bf16[576,128]{1,0:T(8,128)(2,1)S(1)}, u32[]{:S(2)}, u32[]{:S(2)}) collective-permute-start(bf16[576,128]{1,0:T(8,128)(2,1)S(1)} %collective-permute-done.12.refs_1_), channel_id=1, source_target_pairs={{8,1},{9,0},{0,5},{1,4},{4,13},{5,12},{12,9},{13,8},{10,3},{11,2},... | collective-permute-start | bytes 442376 | tf_op jit(solution)/shard_map/ppermute | solution.py:256
  32.6 1.6 %shard_map.39 = (f32[192,896]{1,0:T(8,128)S(1)}, f32[192,896]{1,0:T(8,128)S(1)}) custom-call(bf16[1160,128]{1,0:T(8,128)(2,1)S(1)} %get-tuple-element.24.own.left, bf16[1160,128]{1,0:T(8,128)(2,1)S(1)} %collective-permute-done.3.other.left, bf16[584,128]{1,0:T(8,128)(2,1)S(1)} %collective-permute-done.11.refs_0_, ...), custom_call_target="tpu_custom_call", output_to_operand_aliasing={{0}: (6, {}), {1}: (7, {})} | custom-call | tf_op jit(solution)/shard_map/pallas_call | solution.py:204
  34.2 0.0 collective-permute-done.10.refs_0_
  34.2 3.4 %collective-permute-done.14.refs_1_ = bf16[576,128]{1,0:T(8,128)(2,1)S(1)} collective-permute-done((bf16[576,128]{1,0:T(8,128)(2,1)S(1)}, bf16[576,128]{1,0:T(8,128)(2,1)S(1)}, u32[]{:S(2)}, u32[]{:S(2)}) %collective-permute-start.14) | collective-permute-done | bytes 147488 | tf_op jit(solution)/shard_map/ppermute | solution.py:256
  37.6 0.6 %shard_map.41 = f32[192,896]{1,0:T(8,128)S(1)} custom-call(bf16[1160,128]{1,0:T(8,128)(2,1)S(1)} %collective-permute-done.3.other.left, bf16[584,128]{1,0:T(8,128)(2,1)S(1)} %collective-permute-done.10.refs_0_, bf16[576,128]{1,0:T(8,128)(2,1)S(1)} %collective-permute-done.14.refs_1_, ...), custom_call_target="tpu_custom_call", output_to_operand_aliasing={{}: (3, {})} | custom-call | tf_op jit(solution)/shard_map/pallas_call | solution.py:204
  38.2 0.2 collective-permute-start.15
  38.4 0.6 %shard_map.40.mine = f32[192,896]{1,0:T(8,128)S(1)} custom-call(bf16[1160,128]{1,0:T(8,128)(2,1)S(1)} %get-tuple-element.24.own.left, bf16[584,128]{1,0:T(8,128)(2,1)S(1)} %collective-permute-done.10.refs_0_, bf16[576,128]{1,0:T(8,128)(2,1)S(1)} %collective-permute-done.14.refs_1_, ...), custom_call_target="tpu_custom_call", output_to_operand_aliasing={{}: (3, {})} | custom-call | tf_op jit(solution)/shard_map/pallas_call | solution.py:204
  39.0 1.4 %collective-permute-done.15.theirs = f32[192,896]{1,0:T(8,128)S(1)} collective-permute-done((f32[192,896]{1,0:T(8,128)S(1)}, f32[192,896]{1,0:T(8,128)S(1)}, u32[]{:S(2)}, u32[]{:S(2)}) %collective-permute-start.15) | collective-permute-done | bytes 688160 | tf_op jit(solution)/shard_map/ppermute | solution.py:262
  40.5 0.8 %shard_map.42 = bf16[192,768]{1,0:T(8,128)(2,1)} custom-call(f32[192,896]{1,0:T(8,128)S(1)} %shard_map.40.mine, f32[192,896]{1,0:T(8,128)S(1)} %collective-permute-done.15.theirs), custom_call_target="tpu_custom_call" | custom-call | tf_op jit(solution)/shard_map/pallas_call | solution.py:204
Async XLA Ops:
  0.0 0.7 %copy-start.2 = (s32[192]{0:T(256)S(1)}, s32[192]{0:T(256)}, u32[]{:S(2)}) copy-start(s32[192]{0:T(256)} %param.5) | copy-start | bytes 2308
  0.0 0.7 %copy-start.1 = (s32[192,1]{0,1:T(1,128)S(1)}, s32[192,1]{0,1:T(1,128)}, u32[]{:S(2)}) copy-start(s32[192,1]{0,1:T(1,128)} %param.4) | copy-start | bytes 2308
  0.7 1.0 %copy-start = (bf16[192,768]{1,0:T(8,128)(2,1)S(1)}, bf16[192,768]{1,0:T(8,128)(2,1)}, u32[]{:S(2)}) copy-start(bf16[192,768]{1,0:T(8,128)(2,1)} %rows.1) | copy-start | bytes 884740
  1.7 12.9 %collective-permute-start.3 = (bf16[1160,128]{1,0:T(8,128)(2,1)S(1)}, bf16[1160,128]{1,0:T(8,128)(2,1)S(1)}, u32[]{:S(2)}, u32[]{:S(2)}) collective-permute-start(bf16[1160,128]{1,0:T(8,128)(2,1)S(1)} %get-tuple-element.24.own.left), channel_id=1, source_target_pairs={{0,1},{1,0},{2,3},{3,2},{4,5},{5,4},{6,7},{7,6},{8,9},{9,8},{10,11... | collective-permute-start | bytes 890888 | tf_op jit(solution)/shard_map/ppermute | solution.py:262
  2.3 7.9 %collective-permute-start = (bf16[584,128]{1,0:T(8,128)(2,1)S(1)}, bf16[584,128]{1,0:T(8,128)(2,1)S(1)}, u32[]{:S(2)}, u32[]{:S(2)}) collective-permute-start(bf16[584,128]{1,0:T(8,128)(2,1)S(1)} %get-tuple-element.25), channel_id=1, source_target_pairs={{8,1},{9,0},{0,5},{1,4},{4,13},{5,12},{12,9},{13,8},{10,3},{11,2},... | collective-permute-start | bytes 448520 | tf_op jit(solution)/shard_map/ppermute | solution.py:256
  4.9 9.7 %collective-permute-start.5 = (bf16[584,128]{1,0:T(8,128)(2,1)S(1)}, bf16[584,128]{1,0:T(8,128)(2,1)S(1)}, u32[]{:S(2)}, u32[]{:S(2)}) collective-permute-start(bf16[584,128]{1,0:T(8,128)(2,1)S(1)} %get-tuple-element.25), channel_id=1, source_target_pairs={{0,3},{1,2},{2,1},{3,0},{4,7},{5,6},{6,5},{7,4},{8,11},{9,10},{10,... | collective-permute-start | bytes 448520 | tf_op jit(solution)/shard_map/ppermute | solution.py:259
  6.1 7.2 %collective-permute-start.4 = (bf16[576,128]{1,0:T(8,128)(2,1)S(1)}, bf16[576,128]{1,0:T(8,128)(2,1)S(1)}, u32[]{:S(2)}, u32[]{:S(2)}) collective-permute-start(bf16[576,128]{1,0:T(8,128)(2,1)S(1)} %get-tuple-element.26), channel_id=1, source_target_pairs={{8,1},{9,0},{0,5},{1,4},{4,13},{5,12},{12,9},{13,8},{10,3},{11,2},... | collective-permute-start | bytes 442376 | tf_op jit(solution)/shard_map/ppermute | solution.py:256
  8.7 5.9 %collective-permute-start.6 = (bf16[576,128]{1,0:T(8,128)(2,1)S(1)}, bf16[576,128]{1,0:T(8,128)(2,1)S(1)}, u32[]{:S(2)}, u32[]{:S(2)}) collective-permute-start(bf16[576,128]{1,0:T(8,128)(2,1)S(1)} %get-tuple-element.26), channel_id=1, source_target_pairs={{0,3},{1,2},{2,1},{3,0},{4,7},{5,6},{6,5},{7,4},{8,11},{9,10},{10,... | collective-permute-start | bytes 442376 | tf_op jit(solution)/shard_map/ppermute | solution.py:259
  10.2 7.7 %collective-permute-start.1 = (bf16[584,128]{1,0:T(8,128)(2,1)S(1)}, bf16[584,128]{1,0:T(8,128)(2,1)S(1)}, u32[]{:S(2)}, u32[]{:S(2)}) collective-permute-start(bf16[584,128]{1,0:T(8,128)(2,1)S(1)} %collective-permute-done.refs_4_), channel_id=1, source_target_pairs={{8,1},{9,0},{0,5},{1,4},{4,13},{5,12},{12,9},{13,8},{10,3},{11,2},... | collective-permute-start | bytes 448520 | tf_op jit(solution)/shard_map/ppermute | solution.py:256
  13.3 6.9 %collective-permute-start.8 = (bf16[584,128]{1,0:T(8,128)(2,1)S(1)}, bf16[584,128]{1,0:T(8,128)(2,1)S(1)}, u32[]{:S(2)}, u32[]{:S(2)}) collective-permute-start(bf16[584,128]{1,0:T(8,128)(2,1)S(1)} %collective-permute-done.refs_4_), channel_id=1, source_target_pairs={{0,3},{1,2},{2,1},{3,0},{4,7},{5,6},{6,5},{7,4},{8,11},{9,10},{10,... | collective-permute-start | bytes 448520 | tf_op jit(solution)/shard_map/ppermute | solution.py:259
  14.7 6.6 %collective-permute-start.7 = (bf16[576,128]{1,0:T(8,128)(2,1)S(1)}, bf16[576,128]{1,0:T(8,128)(2,1)S(1)}, u32[]{:S(2)}, u32[]{:S(2)}) collective-permute-start(bf16[576,128]{1,0:T(8,128)(2,1)S(1)} %collective-permute-done.4.refs_5_), channel_id=1, source_target_pairs={{8,1},{9,0},{0,5},{1,4},{4,13},{5,12},{12,9},{13,8},{10,3},{11,2},... | collective-permute-start | bytes 442376 | tf_op jit(solution)/shard_map/ppermute | solution.py:256
  16.6 5.8 %collective-permute-start.9 = (bf16[576,128]{1,0:T(8,128)(2,1)S(1)}, bf16[576,128]{1,0:T(8,128)(2,1)S(1)}, u32[]{:S(2)}, u32[]{:S(2)}) collective-permute-start(bf16[576,128]{1,0:T(8,128)(2,1)S(1)} %collective-permute-done.4.refs_5_), channel_id=1, source_target_pairs={{0,3},{1,2},{2,1},{3,0},{4,7},{5,6},{6,5},{7,4},{8,11},{9,10},{10,... | collective-permute-start | bytes 442376 | tf_op jit(solution)/shard_map/ppermute | solution.py:259
  17.9 9.7 %collective-permute-start.2 = (bf16[584,128]{1,0:T(8,128)(2,1)S(1)}, bf16[584,128]{1,0:T(8,128)(2,1)S(1)}, u32[]{:S(2)}, u32[]{:S(2)}) collective-permute-start(bf16[584,128]{1,0:T(8,128)(2,1)S(1)} %collective-permute-done.1.refs_6_), channel_id=1, source_target_pairs={{8,1},{9,0},{0,5},{1,4},{4,13},{5,12},{12,9},{13,8},{10,3},{11,2},... | collective-permute-start | bytes 448520 | tf_op jit(solution)/shard_map/ppermute | solution.py:256
  18.7 10.6 %collective-permute-start.11 = (bf16[584,128]{1,0:T(8,128)(2,1)S(1)}, bf16[584,128]{1,0:T(8,128)(2,1)S(1)}, u32[]{:S(2)}, u32[]{:S(2)}) collective-permute-start(bf16[584,128]{1,0:T(8,128)(2,1)S(1)} %collective-permute-done.1.refs_6_), channel_id=1, source_target_pairs={{0,3},{1,2},{2,1},{3,0},{4,7},{5,6},{6,5},{7,4},{8,11},{9,10},{10,... | collective-permute-start | bytes 448520 | tf_op jit(solution)/shard_map/ppermute | solution.py:259
  22.4 6.9 %collective-permute-start.13 = (bf16[576,128]{1,0:T(8,128)(2,1)S(1)}, bf16[576,128]{1,0:T(8,128)(2,1)S(1)}, u32[]{:S(2)}, u32[]{:S(2)}) collective-permute-start(bf16[576,128]{1,0:T(8,128)(2,1)S(1)} %collective-permute-done.7.refs_7_), channel_id=1, source_target_pairs={{8,1},{9,0},{0,5},{1,4},{4,13},{5,12},{12,9},{13,8},{10,3},{11,2},... | collective-permute-start | bytes 442376 | tf_op jit(solution)/shard_map/ppermute | solution.py:256
  24.8 5.8 %collective-permute-start.12 = (bf16[576,128]{1,0:T(8,128)(2,1)S(1)}, bf16[576,128]{1,0:T(8,128)(2,1)S(1)}, u32[]{:S(2)}, u32[]{:S(2)}) collective-permute-start(bf16[576,128]{1,0:T(8,128)(2,1)S(1)} %collective-permute-done.7.refs_7_), channel_id=1, source_target_pairs={{0,3},{1,2},{2,1},{3,0},{4,7},{5,6},{6,5},{7,4},{8,11},{9,10},{10,... | collective-permute-start | bytes 442376 | tf_op jit(solution)/shard_map/ppermute | solution.py:259
  27.5 6.7 %collective-permute-start.10 = (bf16[584,128]{1,0:T(8,128)(2,1)S(1)}, bf16[584,128]{1,0:T(8,128)(2,1)S(1)}, u32[]{:S(2)}, u32[]{:S(2)}) collective-permute-start(bf16[584,128]{1,0:T(8,128)(2,1)S(1)} %collective-permute-done.2.refs_2_), channel_id=1, source_target_pairs={{0,3},{1,2},{2,1},{3,0},{4,7},{5,6},{6,5},{7,4},{8,11},{9,10},{10,... | collective-permute-start | bytes 448520 | tf_op jit(solution)/shard_map/ppermute | solution.py:259
  30.6 7.0 %collective-permute-start.14 = (bf16[576,128]{1,0:T(8,128)(2,1)S(1)}, bf16[576,128]{1,0:T(8,128)(2,1)S(1)}, u32[]{:S(2)}, u32[]{:S(2)}) collective-permute-start(bf16[576,128]{1,0:T(8,128)(2,1)S(1)} %collective-permute-done.12.refs_1_), channel_id=1, source_target_pairs={{8,1},{9,0},{0,5},{1,4},{4,13},{5,12},{12,9},{13,8},{10,3},{11,2},... | collective-permute-start | bytes 442376 | tf_op jit(solution)/shard_map/ppermute | solution.py:256
  38.2 2.2 %collective-permute-start.15 = (f32[192,896]{1,0:T(8,128)S(1)}, f32[192,896]{1,0:T(8,128)S(1)}, u32[]{:S(2)}, u32[]{:S(2)}) collective-permute-start(f32[192,896]{1,0:T(8,128)S(1)} %shard_map.41), channel_id=1, source_target_pairs={{0,1},{1,0},{2,3},{3,2},{4,5},{5,4},{6,7},{7,6},{8,9},{9,8},{10,11... | collective-permute-start | bytes 2064392 | tf_op jit(solution)/shard_map/ppermute | solution.py:262

commit v11 on v9

--- a/solution.py
+++ b/solution.py
@@ -280,8 +280,8 @@
         across_by.append(tuple(pair[1] for pair in pairs))
     left = (whole, other_core(whole))
     total = start_both(left, across_by[:-1] + along_by[1:-1], (rows_here, width + 128))
-    far_first, mine, theirs = together(along_by[-1][0], *total)
-    last = (across(far_first), along(across_by[-1][1]))
+    near_first, _, mine, theirs = together(across_by[-1][0], along_by[-1][0], *total)
+    last = (along(near_first), across(along_by[-1][1]))
     mine, theirs = add_both(left, [across_by[-1], along_by[-1]], (mine, theirs))
     theirs = other_core(add_one(left[1], [last], theirs))
     mine = add_one(left[0], [last], mine)

time: 40.5 us -> 39.6 us (0.978)
  waiting for transfers between devices: 13.2 us -> 12 us
    ppermute x7, waiting for transfers between devices: 5.85 us -> 1.38 us  [along(): return lax.ppermute(rows, ('blk', 'pair'), hops)]
    ppermute x7, waiting for transfers between devices: 5.9 us -> 9.23 us  [across(): return lax.ppermute(rows, ('sub', 'pair'), [(0, 3), (1, 2), (2, 1), (3, 0)])]
  transfers between devices with their start and end apart: 16 -> 16, of which waited for: 7 -> 7; matrix products, arithmetic and copies ran while one was open for 0% -> 0% of each run, Pallas kernels for 12% -> 13%
where the time goes in v11:
time: 39.6 us; the launch traced here: 39.5 us
  starting transfers between devices  19.2 us (48%)
  waiting for transfers between devices  12 us (30%)
  Pallas kernels  6.5 us (16%)
  local copies, waits for them, and re-layouts  1.65 us (4%)
    ppermute x7, starting transfers between devices, along(): return lax.ppermute(rows, ('blk', 'pair'), hops)  12.2 us
    ppermute x7, waiting for transfers between devices, across(): return lax.ppermute(rows, ('sub', 'pair'), [(0, 3), (1, 2), (2, 1), (3, 0)])  9.23 us
    pallas_call x6, Pallas kernels, call(): pl.pallas_call(kernel, out_shape=[jax.ShapeDtypeStruct(shape, dtype) for...  6.5 us
    ppermute x7, starting transfers between devices, across(): return lax.ppermute(rows, ('sub', 'pair'), [(0, 3), (1, 2), (2, 1), (3, 0)])  5.22 us
    ppermute x2, starting transfers between devices, other_core(): return lax.ppermute(rows, 'pair', [(0, 1), (1, 0)])  1.79 us
    unnamed x6, local copies, waits for them, and re-layouts  1.65 us
    ppermute x2, waiting for transfers between devices, other_core(): return lax.ppermute(rows, 'pair', [(0, 1), (1, 0)])  1.42 us
    ppermute x7, waiting for transfers between devices, along(): return lax.ppermute(rows, ('blk', 'pair'), hops)  1.38 us
  transfers between devices with their start and end apart: 16, of which 7 were waited for; matrix products, arithmetic and copies ran while one was open for 0% of the time, Pallas kernels for 13%

profile of v11, /device:TPU:0, one launch (start us, length us, event | category | flops | bytes accessed | tf_op | source)
XLA Modules:
  0.0 39.5 jit_solution(2834204114544736683)
XLA Ops:
  0.0 0.0 copy-start.2
  0.0 0.0 copy-start.1
  0.0 0.7 %copy-done.2 = s32[192]{0:T(256)S(1)} copy-done((s32[192]{0:T(256)S(1)}, s32[192]{0:T(256)}, u32[]{:S(2)}) %copy-start.2) | copy-done | bytes 792
  0.7 0.0 copy-done.1
  0.7 0.0 copy-start
  0.7 1.0 %copy-done = bf16[192,768]{1,0:T(8,128)(2,1)S(1)} copy-done((bf16[192,768]{1,0:T(8,128)(2,1)S(1)}, bf16[192,768]{1,0:T(8,128)(2,1)}, u32[]{:S(2)}) %copy-start) | copy-done | bytes 294936
  1.7 0.1 shard_map.37
  1.7 2.5 %collective-permute-start = (bf16[584,128]{1,0:T(8,128)(2,1)S(1)}, bf16[584,128]{1,0:T(8,128)(2,1)S(1)}, u32[]{:S(2)}, u32[]{:S(2)}) collective-permute-start(bf16[584,128]{1,0:T(8,128)(2,1)S(1)} %get-tuple-element.28), channel_id=1, source_target_pairs={{8,1},{9,0},{0,5},{1,4},{4,13},{5,12},{12,9},{13,8},{10,3},{11,2},... | collective-permute-start | bytes 448520 | tf_op jit(solution)/shard_map/ppermute | solution.py:256
  4.3 1.8 %collective-permute-start.1 = (bf16[584,128]{1,0:T(8,128)(2,1)S(1)}, bf16[584,128]{1,0:T(8,128)(2,1)S(1)}, u32[]{:S(2)}, u32[]{:S(2)}) collective-permute-start(bf16[584,128]{1,0:T(8,128)(2,1)S(1)} %get-tuple-element.28), channel_id=1, source_target_pairs={{0,3},{1,2},{2,1},{3,0},{4,7},{5,6},{6,5},{7,4},{8,11},{9,10},{10,... | collective-permute-start | bytes 448520 | tf_op jit(solution)/shard_map/ppermute | solution.py:259
  6.0 2.0 %collective-permute-start.7 = (bf16[576,128]{1,0:T(8,128)(2,1)S(1)}, bf16[576,128]{1,0:T(8,128)(2,1)S(1)}, u32[]{:S(2)}, u32[]{:S(2)}) collective-permute-start(bf16[576,128]{1,0:T(8,128)(2,1)S(1)} %get-tuple-element.34), channel_id=1, source_target_pairs={{8,1},{9,0},{0,5},{1,4},{4,13},{5,12},{12,9},{13,8},{10,3},{11,2},... | collective-permute-start | bytes 442376 | tf_op jit(solution)/shard_map/ppermute | solution.py:256
  8.1 0.8 %collective-permute-start.8 = (bf16[576,128]{1,0:T(8,128)(2,1)S(1)}, bf16[576,128]{1,0:T(8,128)(2,1)S(1)}, u32[]{:S(2)}, u32[]{:S(2)}) collective-permute-start(bf16[576,128]{1,0:T(8,128)(2,1)S(1)} %get-tuple-element.34), channel_id=1, source_target_pairs={{0,3},{1,2},{2,1},{3,0},{4,7},{5,6},{6,5},{7,4},{8,11},{9,10},{10,... | collective-permute-start | bytes 442376 | tf_op jit(solution)/shard_map/ppermute | solution.py:259
  8.9 0.0 collective-permute-done.refs_4_
  8.9 0.8 %collective-permute-done.1.refs_0_ = bf16[584,128]{1,0:T(8,128)(2,1)S(1)} collective-permute-done((bf16[584,128]{1,0:T(8,128)(2,1)S(1)}, bf16[584,128]{1,0:T(8,128)(2,1)S(1)}, u32[]{:S(2)}, u32[]{:S(2)}) %collective-permute-start.1) | collective-permute-done | bytes 149536 | tf_op jit(solution)/shard_map/ppermute | solution.py:259
  9.7 3.9 %collective-permute-start.2 = (bf16[584,128]{1,0:T(8,128)(2,1)S(1)}, bf16[584,128]{1,0:T(8,128)(2,1)S(1)}, u32[]{:S(2)}, u32[]{:S(2)}) collective-permute-start(bf16[584,128]{1,0:T(8,128)(2,1)S(1)} %collective-permute-done.refs_4_), channel_id=1, source_target_pairs={{8,1},{9,0},{0,5},{1,4},{4,13},{5,12},{12,9},{13,8},{10,3},{11,2},... | collective-permute-start | bytes 448520 | tf_op jit(solution)/shard_map/ppermute | solution.py:256
  13.6 0.0 collective-permute-start.3
  13.6 1.6 %collective-permute-start.6 = (bf16[1160,128]{1,0:T(8,128)(2,1)S(1)}, bf16[1160,128]{1,0:T(8,128)(2,1)S(1)}, u32[]{:S(2)}, u32[]{:S(2)}) collective-permute-start(bf16[1160,128]{1,0:T(8,128)(2,1)S(1)} %get-tuple-element.27.own.left), channel_id=1, source_target_pairs={{0,1},{1,0},{2,3},{3,2},{4,5},{5,4},{6,7},{7,6},{8,9},{9,8},{10,11... | collective-permute-start | bytes 890888 | tf_op jit(solution)/shard_map/ppermute | solution.py:262
  15.2 0.0 collective-permute-done.7.refs_5_
  15.2 0.0 collective-permute-done.8.refs_1_
  15.2 0.2 collective-permute-start.10
  15.4 1.2 %collective-permute-start.9 = (bf16[576,128]{1,0:T(8,128)(2,1)S(1)}, bf16[576,128]{1,0:T(8,128)(2,1)S(1)}, u32[]{:S(2)}, u32[]{:S(2)}) collective-permute-start(bf16[576,128]{1,0:T(8,128)(2,1)S(1)} %collective-permute-done.7.refs_5_), channel_id=1, source_target_pairs={{8,1},{9,0},{0,5},{1,4},{4,13},{5,12},{12,9},{13,8},{10,3},{11,2},... | collective-permute-start | bytes 442376 | tf_op jit(solution)/shard_map/ppermute | solution.py:256
  16.6 0.0 collective-permute-done.2.refs_6_
  16.6 3.1 %collective-permute-done.3.refs_2_ = bf16[584,128]{1,0:T(8,128)(2,1)S(1)} collective-permute-done((bf16[584,128]{1,0:T(8,128)(2,1)S(1)}, bf16[584,128]{1,0:T(8,128)(2,1)S(1)}, u32[]{:S(2)}, u32[]{:S(2)}) %collective-permute-start.3) | collective-permute-done | bytes 149536 | tf_op jit(solution)/shard_map/ppermute | solution.py:259
  19.7 0.9 %collective-permute-start.4 = (bf16[584,128]{1,0:T(8,128)(2,1)S(1)}, bf16[584,128]{1,0:T(8,128)(2,1)S(1)}, u32[]{:S(2)}, u32[]{:S(2)}) collective-permute-start(bf16[584,128]{1,0:T(8,128)(2,1)S(1)} %collective-permute-done.2.refs_6_), channel_id=1, source_target_pairs={{8,1},{9,0},{0,5},{1,4},{4,13},{5,12},{12,9},{13,8},{10,3},{11,2},... | collective-permute-start | bytes 448520 | tf_op jit(solution)/shard_map/ppermute | solution.py:256
  20.6 0.6 %collective-permute-start.5 = (bf16[584,128]{1,0:T(8,128)(2,1)S(1)}, bf16[584,128]{1,0:T(8,128)(2,1)S(1)}, u32[]{:S(2)}, u32[]{:S(2)}) collective-permute-start(bf16[584,128]{1,0:T(8,128)(2,1)S(1)} %collective-permute-done.2.refs_6_), channel_id=1, source_target_pairs={{0,3},{1,2},{2,1},{3,0},{4,7},{5,6},{6,5},{7,4},{8,11},{9,10},{10,... | collective-permute-start | bytes 448520 | tf_op jit(solution)/shard_map/ppermute | solution.py:259
  21.2 1.7 %collective-permute-done.10.refs_3_ = bf16[576,128]{1,0:T(8,128)(2,1)S(1)} collective-permute-done((bf16[576,128]{1,0:T(8,128)(2,1)S(1)}, bf16[576,128]{1,0:T(8,128)(2,1)S(1)}, u32[]{:S(2)}, u32[]{:S(2)}) %collective-permute-start.10) | collective-permute-done | bytes 147488 | tf_op jit(solution)/shard_map/ppermute | solution.py:259
  22.9 0.0 collective-permute-done.9.refs_7_
  22.9 0.4 %collective-permute-start.12 = (bf16[576,128]{1,0:T(8,128)(2,1)S(1)}, bf16[576,128]{1,0:T(8,128)(2,1)S(1)}, u32[]{:S(2)}, u32[]{:S(2)}) collective-permute-start(bf16[576,128]{1,0:T(8,128)(2,1)S(1)} %collective-permute-done.9.refs_7_), channel_id=1, source_target_pairs={{8,1},{9,0},{0,5},{1,4},{4,13},{5,12},{12,9},{13,8},{10,3},{11,2},... | collective-permute-start | bytes 442376 | tf_op jit(solution)/shard_map/ppermute | solution.py:256
  23.3 1.0 %collective-permute-start.13 = (bf16[576,128]{1,0:T(8,128)(2,1)S(1)}, bf16[576,128]{1,0:T(8,128)(2,1)S(1)}, u32[]{:S(2)}, u32[]{:S(2)}) collective-permute-start(bf16[576,128]{1,0:T(8,128)(2,1)S(1)} %collective-permute-done.9.refs_7_), channel_id=1, source_target_pairs={{0,3},{1,2},{2,1},{3,0},{4,7},{5,6},{6,5},{7,4},{8,11},{9,10},{10,... | collective-permute-start | bytes 442376 | tf_op jit(solution)/shard_map/ppermute | solution.py:259
  24.3 0.0 collective-permute-done.6.other.left
  24.4 2.7 %shard_map.38 = (f32[192,896]{1,0:T(8,128)S(1)}, f32[192,896]{1,0:T(8,128)S(1)}) custom-call(bf16[1160,128]{1,0:T(8,128)(2,1)S(1)} %get-tuple-element.27.own.left, bf16[1160,128]{1,0:T(8,128)(2,1)S(1)} %collective-permute-done.6.other.left, bf16[584,128]{1,0:T(8,128)(2,1)S(1)} %collective-permute-done.1.refs_0_, ...), custom_call_target="tpu_custom_call" | custom-call | tf_op jit(solution)/shard_map/pallas_call | solution.py:204
  27.1 0.0 collective-permute-done.4.refs_2_
  27.1 0.0 collective-permute-done.5.refs_0_
  27.1 1.3 %collective-permute-start.11 = (bf16[584,128]{1,0:T(8,128)(2,1)S(1)}, bf16[584,128]{1,0:T(8,128)(2,1)S(1)}, u32[]{:S(2)}, u32[]{:S(2)}) collective-permute-start(bf16[584,128]{1,0:T(8,128)(2,1)S(1)} %collective-permute-done.5.refs_0_), channel_id=1, source_target_pairs={{8,1},{9,0},{0,5},{1,4},{4,13},{5,12},{12,9},{13,8},{10,3},{11,2},... | collective-permute-start | bytes 448520 | tf_op jit(solution)/shard_map/ppermute | solution.py:256
  28.4 1.3 %collective-permute-done.12.refs_3_ = bf16[576,128]{1,0:T(8,128)(2,1)S(1)} collective-permute-done((bf16[576,128]{1,0:T(8,128)(2,1)S(1)}, bf16[576,128]{1,0:T(8,128)(2,1)S(1)}, u32[]{:S(2)}, u32[]{:S(2)}) %collective-permute-start.12) | collective-permute-done | bytes 147488 | tf_op jit(solution)/shard_map/ppermute | solution.py:256
  29.7 0.2 collective-permute-done.13.refs_1_
  29.9 0.9 %collective-permute-start.14 = (bf16[576,128]{1,0:T(8,128)(2,1)S(1)}, bf16[576,128]{1,0:T(8,128)(2,1)S(1)}, u32[]{:S(2)}, u32[]{:S(2)}) collective-permute-start(bf16[576,128]{1,0:T(8,128)(2,1)S(1)} %collective-permute-done.12.refs_3_), channel_id=1, source_target_pairs={{0,3},{1,2},{2,1},{3,0},{4,7},{5,6},{6,5},{7,4},{8,11},{9,10},{10,... | collective-permute-start | bytes 442376 | tf_op jit(solution)/shard_map/ppermute | solution.py:259
  30.8 1.6 %shard_map.39 = (f32[192,896]{1,0:T(8,128)S(1)}, f32[192,896]{1,0:T(8,128)S(1)}) custom-call(bf16[1160,128]{1,0:T(8,128)(2,1)S(1)} %get-tuple-element.27.own.left, bf16[1160,128]{1,0:T(8,128)(2,1)S(1)} %collective-permute-done.6.other.left, bf16[584,128]{1,0:T(8,128)(2,1)S(1)} %collective-permute-done.5.refs_0_, ...), custom_call_target="tpu_custom_call", output_to_operand_aliasing={{0}: (6, {}), {1}: (7, {})} | custom-call | tf_op jit(solution)/shard_map/pallas_call | solution.py:204
  32.5 3.3 %collective-permute-done.14.refs_1_ = bf16[576,128]{1,0:T(8,128)(2,1)S(1)} collective-permute-done((bf16[576,128]{1,0:T(8,128)(2,1)S(1)}, bf16[576,128]{1,0:T(8,128)(2,1)S(1)}, u32[]{:S(2)}, u32[]{:S(2)}) %collective-permute-start.14) | collective-permute-done | bytes 147488 | tf_op jit(solution)/shard_map/ppermute | solution.py:259
  35.8 0.0 collective-permute-done.11.refs_0_
  35.8 0.6 %shard_map.41 = f32[192,896]{1,0:T(8,128)S(1)} custom-call(bf16[1160,128]{1,0:T(8,128)(2,1)S(1)} %collective-permute-done.6.other.left, bf16[584,128]{1,0:T(8,128)(2,1)S(1)} %collective-permute-done.11.refs_0_, bf16[576,128]{1,0:T(8,128)(2,1)S(1)} %collective-permute-done.14.refs_1_, ...), custom_call_target="tpu_custom_call", output_to_operand_aliasing={{}: (3, {})} | custom-call | tf_op jit(solution)/shard_map/pallas_call | solution.py:204
  36.4 0.2 collective-permute-start.15
  36.6 0.6 %shard_map.40.mine = f32[192,896]{1,0:T(8,128)S(1)} custom-call(bf16[1160,128]{1,0:T(8,128)(2,1)S(1)} %get-tuple-element.27.own.left, bf16[584,128]{1,0:T(8,128)(2,1)S(1)} %collective-permute-done.11.refs_0_, bf16[576,128]{1,0:T(8,128)(2,1)S(1)} %collective-permute-done.14.refs_1_, ...), custom_call_target="tpu_custom_call", output_to_operand_aliasing={{}: (3, {})} | custom-call | tf_op jit(solution)/shard_map/pallas_call | solution.py:204
  37.2 1.4 %collective-permute-done.15.theirs = f32[192,896]{1,0:T(8,128)S(1)} collective-permute-done((f32[192,896]{1,0:T(8,128)S(1)}, f32[192,896]{1,0:T(8,128)S(1)}, u32[]{:S(2)}, u32[]{:S(2)}) %collective-permute-start.15) | collective-permute-done | bytes 688160 | tf_op jit(solution)/shard_map/ppermute | solution.py:262
  38.6 0.8 %shard_map.42 = bf16[192,768]{1,0:T(8,128)(2,1)} custom-call(f32[192,896]{1,0:T(8,128)S(1)} %shard_map.40.mine, f32[192,896]{1,0:T(8,128)S(1)} %collective-permute-done.15.theirs), custom_call_target="tpu_custom_call" | custom-call | tf_op jit(solution)/shard_map/pallas_call | solution.py:204
Async XLA Ops:
  0.0 0.7 %copy-start.2 = (s32[192]{0:T(256)S(1)}, s32[192]{0:T(256)}, u32[]{:S(2)}) copy-start(s32[192]{0:T(256)} %param.5) | copy-start | bytes 2308
  0.0 0.7 %copy-start.1 = (s32[192,1]{0,1:T(1,128)S(1)}, s32[192,1]{0,1:T(1,128)}, u32[]{:S(2)}) copy-start(s32[192,1]{0,1:T(1,128)} %param.4) | copy-start | bytes 2308
  0.7 1.0 %copy-start = (bf16[192,768]{1,0:T(8,128)(2,1)S(1)}, bf16[192,768]{1,0:T(8,128)(2,1)}, u32[]{:S(2)}) copy-start(bf16[192,768]{1,0:T(8,128)(2,1)} %rows.1) | copy-start | bytes 884740
  1.7 7.1 %collective-permute-start = (bf16[584,128]{1,0:T(8,128)(2,1)S(1)}, bf16[584,128]{1,0:T(8,128)(2,1)S(1)}, u32[]{:S(2)}, u32[]{:S(2)}) collective-permute-start(bf16[584,128]{1,0:T(8,128)(2,1)S(1)} %get-tuple-element.28), channel_id=1, source_target_pairs={{8,1},{9,0},{0,5},{1,4},{4,13},{5,12},{12,9},{13,8},{10,3},{11,2},... | collective-permute-start | bytes 448520 | tf_op jit(solution)/shard_map/ppermute | solution.py:256
  4.3 5.5 %collective-permute-start.1 = (bf16[584,128]{1,0:T(8,128)(2,1)S(1)}, bf16[584,128]{1,0:T(8,128)(2,1)S(1)}, u32[]{:S(2)}, u32[]{:S(2)}) collective-permute-start(bf16[584,128]{1,0:T(8,128)(2,1)S(1)} %get-tuple-element.28), channel_id=1, source_target_pairs={{0,3},{1,2},{2,1},{3,0},{4,7},{5,6},{6,5},{7,4},{8,11},{9,10},{10,... | collective-permute-start | bytes 448520 | tf_op jit(solution)/shard_map/ppermute | solution.py:259
  6.0 9.2 %collective-permute-start.7 = (bf16[576,128]{1,0:T(8,128)(2,1)S(1)}, bf16[576,128]{1,0:T(8,128)(2,1)S(1)}, u32[]{:S(2)}, u32[]{:S(2)}) collective-permute-start(bf16[576,128]{1,0:T(8,128)(2,1)S(1)} %get-tuple-element.34), channel_id=1, source_target_pairs={{8,1},{9,0},{0,5},{1,4},{4,13},{5,12},{12,9},{13,8},{10,3},{11,2},... | collective-permute-start | bytes 442376 | tf_op jit(solution)/shard_map/ppermute | solution.py:256
  8.1 7.1 %collective-permute-start.8 = (bf16[576,128]{1,0:T(8,128)(2,1)S(1)}, bf16[576,128]{1,0:T(8,128)(2,1)S(1)}, u32[]{:S(2)}, u32[]{:S(2)}) collective-permute-start(bf16[576,128]{1,0:T(8,128)(2,1)S(1)} %get-tuple-element.34), channel_id=1, source_target_pairs={{0,3},{1,2},{2,1},{3,0},{4,7},{5,6},{6,5},{7,4},{8,11},{9,10},{10,... | collective-permute-start | bytes 442376 | tf_op jit(solution)/shard_map/ppermute | solution.py:259
  9.7 6.9 %collective-permute-start.2 = (bf16[584,128]{1,0:T(8,128)(2,1)S(1)}, bf16[584,128]{1,0:T(8,128)(2,1)S(1)}, u32[]{:S(2)}, u32[]{:S(2)}) collective-permute-start(bf16[584,128]{1,0:T(8,128)(2,1)S(1)} %collective-permute-done.refs_4_), channel_id=1, source_target_pairs={{8,1},{9,0},{0,5},{1,4},{4,13},{5,12},{12,9},{13,8},{10,3},{11,2},... | collective-permute-start | bytes 448520 | tf_op jit(solution)/shard_map/ppermute | solution.py:256
  13.6 6.1 %collective-permute-start.3 = (bf16[584,128]{1,0:T(8,128)(2,1)S(1)}, bf16[584,128]{1,0:T(8,128)(2,1)S(1)}, u32[]{:S(2)}, u32[]{:S(2)}) collective-permute-start(bf16[584,128]{1,0:T(8,128)(2,1)S(1)} %collective-permute-done.refs_4_), channel_id=1, source_target_pairs={{0,3},{1,2},{2,1},{3,0},{4,7},{5,6},{6,5},{7,4},{8,11},{9,10},{10,... | collective-permute-start | bytes 448520 | tf_op jit(solution)/shard_map/ppermute | solution.py:259
  13.6 10.8 %collective-permute-start.6 = (bf16[1160,128]{1,0:T(8,128)(2,1)S(1)}, bf16[1160,128]{1,0:T(8,128)(2,1)S(1)}, u32[]{:S(2)}, u32[]{:S(2)}) collective-permute-start(bf16[1160,128]{1,0:T(8,128)(2,1)S(1)} %get-tuple-element.27.own.left), channel_id=1, source_target_pairs={{0,1},{1,0},{2,3},{3,2},{4,5},{5,4},{6,7},{7,6},{8,9},{9,8},{10,11... | collective-permute-start | bytes 890888 | tf_op jit(solution)/shard_map/ppermute | solution.py:262
  15.2 7.7 %collective-permute-start.10 = (bf16[576,128]{1,0:T(8,128)(2,1)S(1)}, bf16[576,128]{1,0:T(8,128)(2,1)S(1)}, u32[]{:S(2)}, u32[]{:S(2)}) collective-permute-start(bf16[576,128]{1,0:T(8,128)(2,1)S(1)} %collective-permute-done.7.refs_5_), channel_id=1, source_target_pairs={{0,3},{1,2},{2,1},{3,0},{4,7},{5,6},{6,5},{7,4},{8,11},{9,10},{10,... | collective-permute-start | bytes 442376 | tf_op jit(solution)/shard_map/ppermute | solution.py:259
  15.4 7.5 %collective-permute-start.9 = (bf16[576,128]{1,0:T(8,128)(2,1)S(1)}, bf16[576,128]{1,0:T(8,128)(2,1)S(1)}, u32[]{:S(2)}, u32[]{:S(2)}) collective-permute-start(bf16[576,128]{1,0:T(8,128)(2,1)S(1)} %collective-permute-done.7.refs_5_), channel_id=1, source_target_pairs={{8,1},{9,0},{0,5},{1,4},{4,13},{5,12},{12,9},{13,8},{10,3},{11,2},... | collective-permute-start | bytes 442376 | tf_op jit(solution)/shard_map/ppermute | solution.py:256
  19.7 7.3 %collective-permute-start.4 = (bf16[584,128]{1,0:T(8,128)(2,1)S(1)}, bf16[584,128]{1,0:T(8,128)(2,1)S(1)}, u32[]{:S(2)}, u32[]{:S(2)}) collective-permute-start(bf16[584,128]{1,0:T(8,128)(2,1)S(1)} %collective-permute-done.2.refs_6_), channel_id=1, source_target_pairs={{8,1},{9,0},{0,5},{1,4},{4,13},{5,12},{12,9},{13,8},{10,3},{11,2},... | collective-permute-start | bytes 448520 | tf_op jit(solution)/shard_map/ppermute | solution.py:256
  20.6 6.4 %collective-permute-start.5 = (bf16[584,128]{1,0:T(8,128)(2,1)S(1)}, bf16[584,128]{1,0:T(8,128)(2,1)S(1)}, u32[]{:S(2)}, u32[]{:S(2)}) collective-permute-start(bf16[584,128]{1,0:T(8,128)(2,1)S(1)} %collective-permute-done.2.refs_6_), channel_id=1, source_target_pairs={{0,3},{1,2},{2,1},{3,0},{4,7},{5,6},{6,5},{7,4},{8,11},{9,10},{10,... | collective-permute-start | bytes 448520 | tf_op jit(solution)/shard_map/ppermute | solution.py:259
  22.9 6.8 %collective-permute-start.12 = (bf16[576,128]{1,0:T(8,128)(2,1)S(1)}, bf16[576,128]{1,0:T(8,128)(2,1)S(1)}, u32[]{:S(2)}, u32[]{:S(2)}) collective-permute-start(bf16[576,128]{1,0:T(8,128)(2,1)S(1)} %collective-permute-done.9.refs_7_), channel_id=1, source_target_pairs={{8,1},{9,0},{0,5},{1,4},{4,13},{5,12},{12,9},{13,8},{10,3},{11,2},... | collective-permute-start | bytes 442376 | tf_op jit(solution)/shard_map/ppermute | solution.py:256
  23.3 6.6 %collective-permute-start.13 = (bf16[576,128]{1,0:T(8,128)(2,1)S(1)}, bf16[576,128]{1,0:T(8,128)(2,1)S(1)}, u32[]{:S(2)}, u32[]{:S(2)}) collective-permute-start(bf16[576,128]{1,0:T(8,128)(2,1)S(1)} %collective-permute-done.9.refs_7_), channel_id=1, source_target_pairs={{0,3},{1,2},{2,1},{3,0},{4,7},{5,6},{6,5},{7,4},{8,11},{9,10},{10,... | collective-permute-start | bytes 442376 | tf_op jit(solution)/shard_map/ppermute | solution.py:259
  27.1 8.7 %collective-permute-start.11 = (bf16[584,128]{1,0:T(8,128)(2,1)S(1)}, bf16[584,128]{1,0:T(8,128)(2,1)S(1)}, u32[]{:S(2)}, u32[]{:S(2)}) collective-permute-start(bf16[584,128]{1,0:T(8,128)(2,1)S(1)} %collective-permute-done.5.refs_0_), channel_id=1, source_target_pairs={{8,1},{9,0},{0,5},{1,4},{4,13},{5,12},{12,9},{13,8},{10,3},{11,2},... | collective-permute-start | bytes 448520 | tf_op jit(solution)/shard_map/ppermute | solution.py:256
  29.9 5.9 %collective-permute-start.14 = (bf16[576,128]{1,0:T(8,128)(2,1)S(1)}, bf16[576,128]{1,0:T(8,128)(2,1)S(1)}, u32[]{:S(2)}, u32[]{:S(2)}) collective-permute-start(bf16[576,128]{1,0:T(8,128)(2,1)S(1)} %collective-permute-done.12.refs_3_), channel_id=1, source_target_pairs={{0,3},{1,2},{2,1},{3,0},{4,7},{5,6},{6,5},{7,4},{8,11},{9,10},{10,... | collective-permute-start | bytes 442376 | tf_op jit(solution)/shard_map/ppermute | solution.py:259
  36.4 2.2 %collective-permute-start.15 = (f32[192,896]{1,0:T(8,128)S(1)}, f32[192,896]{1,0:T(8,128)S(1)}, u32[]{:S(2)}, u32[]{:S(2)}) collective-permute-start(f32[192,896]{1,0:T(8,128)S(1)} %shard_map.41), channel_id=1, source_target_pairs={{0,1},{1,0},{2,3},{3,2},{4,5},{5,4},{6,7},{7,6},{8,9},{9,8},{10,11... | collective-permute-start | bytes 2064392 | tf_op jit(solution)/shard_map/ppermute | solution.py:262

commit v12 on v11

--- a/solution.py
+++ b/solution.py
@@ -181,19 +181,43 @@
     store_sides(*add_blocks(left, key, scale, blocks, numer, denom), refs[2:])
 
 
-def one_kernel(n_blocks, left, *refs):
-    refs = list(refs)
+def half_of(first, second, rows_here):
+    half = rows_here // 2
+    rows = from_slabs(first if second is None else second, half)
+    top = 0 if second is None else half
+    key = to_column(key_row(first, rows_here))[top : top + half]
+    return rows, to_row(key), to_row(scale_column(rows))
+
+
+def first_half_kernel(own, other, first, *refs):
     rows_here, wide = refs[-1].shape
-    blocks = take_blocks(refs, n_blocks, rows_here)
-    numer = refs[0][:, : wide - 128]
-    denom = refs[0][:, wide - 128 : wide - 127]
-    store_sides(*add_blocks(*left_of((left,), rows_here), blocks, numer, denom), refs[1:])
+    left, key, scale = left_of((own, other), rows_here)
+    blocks = [half_of(first, None, rows_here)]
+    numer = jnp.concatenate([ref[:, : wide - 128] for ref in refs[:2]], axis=0)
+    denom = jnp.concatenate([ref[:, wide - 128 : wide - 127] for ref in refs[:2]], axis=0)
+    store_sides(*add_blocks(left, key, scale, blocks, numer, denom), refs[2:])
+
+
+def second_half_kernel(left, first, second, before, out):
+    rows_here, wide = before.shape
+    width = wide - 128
+    blocks = [half_of(first, second, rows_here)]
+    sides = left_of((left,), rows_here)
+    numer, denom = add_blocks(*sides, blocks, before[:, :width], before[:, width : width + 1])
+    if out.dtype == F32:
+        store_sides(numer, denom, [out])
+    else:
+        high = denom.astype(BF16).astype(F32)
+        lane = lax.broadcasted_iota(jnp.int32, (rows_here, 128), 1)
+        out[:, :width] = numer.astype(BF16)
+        out[:, width:] = jnp.where(lane == 0, high, denom - high).astype(BF16)
 
 
 def mean_kernel(mine, theirs, out):
     width = out.shape[1]
-    denom = mine[:, width : width + 1] + theirs[:, width : width + 1]
-    out[...] = ((mine[:, :width] + theirs[:, :width]) / denom).astype(BF16)
+    parts = theirs[:, width:].astype(F32)
+    denom = mine[:, width : width + 1] + (parts[:, 0:1] + parts[:, 1:2])
+    out[...] = ((mine[:, :width] + theirs[:, :width].astype(F32)) / denom).astype(BF16)
 
 
 def whole_in_vmem(count):
@@ -225,10 +249,13 @@
     )
 
 
-def add_one(left, right, before):
-    args = [left] + [half for block in right for half in block] + [before]
-    shapes = [(before.shape, F32)]
-    return call(functools.partial(one_kernel, len(right)), shapes, args, {len(args) - 1: 0})[0]
+def add_first_half(left, first, before):
+    shapes = [(total.shape, F32) for total in before]
+    return call(first_half_kernel, shapes, [*left, first, *before], {3: 0, 4: 1})
+
+
+def add_second_half(left, halves, before, dtype):
+    return call(second_half_kernel, [(before.shape, dtype)], [left, *halves, before])[0]
 
 
 def folded_ring(size):
@@ -283,8 +310,9 @@
     near_first, _, mine, theirs = together(across_by[-1][0], along_by[-1][0], *total)
     last = (along(near_first), across(along_by[-1][1]))
     mine, theirs = add_both(left, [across_by[-1], along_by[-1]], (mine, theirs))
-    theirs = other_core(add_one(left[1], [last], theirs))
-    mine = add_one(left[0], [last], mine)
+    mine, theirs = add_first_half(left, last[0], (mine, theirs))
+    theirs = other_core(add_second_half(left[1], last, theirs, BF16))
+    mine = add_second_half(left[0], last, mine, F32)
     (out,) = call(mean_kernel, [((rows_here, width), BF16)], [mine, theirs])
     return out
 

time: 39.6 us -> 39.1 us (0.987)
  waiting for transfers between devices: 12 us -> 10.8 us
  Pallas kernels: 6.5 us -> 7.24 us
    ppermute x7, waiting for transfers between devices: 9.23 us -> 7.38 us  [across(): return lax.ppermute(rows, ('sub', 'pair'), [(0, 3), (1, 2), (2, 1), (3, 0)])]
    ppermute x7, waiting for transfers between devices: 1.38 us -> 2.41 us  [along(): return lax.ppermute(rows, ('blk', 'pair'), hops)]
    pallas_call x6 -> x7, Pallas kernels: 6.5 us -> 7.24 us  [call(): pl.pallas_call(kernel, out_shape=[jax.ShapeDtypeStruct(shape, dtype) for...]
    ppermute x2, waiting for transfers between devices: 1.42 us -> 0.99 us  [other_core(): return lax.ppermute(rows, 'pair', [(0, 1), (1, 0)])]
  transfers between devices with their start and end apart: 16 -> 16, of which waited for: 7 -> 8; matrix products, arithmetic and copies ran while one was open for 0% -> 0% of each run, Pallas kernels for 13% -> 15%
where the time goes in v12:
time: 39.1 us; the launch traced here: 39 us
  starting transfers between devices  19.2 us (49%)
  waiting for transfers between devices  10.8 us (28%)
  Pallas kernels  7.24 us (19%)
  local copies, waits for them, and re-layouts  1.65 us (4%)
    ppermute x7, starting transfers between devices, along(): return lax.ppermute(rows, ('blk', 'pair'), hops)  12.2 us
    ppermute x7, waiting for transfers between devices, across(): return lax.ppermute(rows, ('sub', 'pair'), [(0, 3), (1, 2), (2, 1), (3, 0)])  7.38 us
    pallas_call x7, Pallas kernels, call(): pl.pallas_call(kernel, out_shape=[jax.ShapeDtypeStruct(shape, dtype) for...  7.24 us
    ppermute x7, starting transfers between devices, across(): return lax.ppermute(rows, ('sub', 'pair'), [(0, 3), (1, 2), (2, 1), (3, 0)])  5.22 us
    ppermute x7, waiting for transfers between devices, along(): return lax.ppermute(rows, ('blk', 'pair'), hops)  2.41 us
    ppermute x2, starting transfers between devices, other_core(): return lax.ppermute(rows, 'pair', [(0, 1), (1, 0)])  1.79 us
    unnamed x6, local copies, waits for them, and re-layouts  1.65 us
    ppermute x2, waiting for transfers between devices, other_core(): return lax.ppermute(rows, 'pair', [(0, 1), (1, 0)])  0.99 us
  transfers between devices with their start and end apart: 16, of which 8 were waited for; matrix products, arithmetic and copies ran while one was open for 0% of the time, Pallas kernels for 15%

profile of v12, /device:TPU:0, one launch (start us, length us, event | category | flops | bytes accessed | tf_op | source)
XLA Modules:
  0.0 39.0 jit_solution(13434313089569502695)
XLA Ops:
  0.0 0.0 copy-start.2
  0.0 0.0 copy-start.1
  0.0 0.7 %copy-done.2 = s32[192]{0:T(256)S(1)} copy-done((s32[192]{0:T(256)S(1)}, s32[192]{0:T(256)}, u32[]{:S(2)}) %copy-start.2) | copy-done | bytes 792
  0.7 0.0 copy-done.1
  0.7 0.0 copy-start
  0.7 1.0 %copy-done = bf16[192,768]{1,0:T(8,128)(2,1)S(1)} copy-done((bf16[192,768]{1,0:T(8,128)(2,1)S(1)}, bf16[192,768]{1,0:T(8,128)(2,1)}, u32[]{:S(2)}) %copy-start) | copy-done | bytes 294936
  1.7 0.1 shard_map.37
  1.7 2.5 %collective-permute-start = (bf16[584,128]{1,0:T(8,128)(2,1)S(1)}, bf16[584,128]{1,0:T(8,128)(2,1)S(1)}, u32[]{:S(2)}, u32[]{:S(2)}) collective-permute-start(bf16[584,128]{1,0:T(8,128)(2,1)S(1)} %get-tuple-element.30), channel_id=1, source_target_pairs={{8,1},{9,0},{0,5},{1,4},{4,13},{5,12},{12,9},{13,8},{10,3},{11,2},... | collective-permute-start | bytes 448520 | tf_op jit(solution)/shard_map/ppermute | solution.py:283
  4.3 1.8 %collective-permute-start.1 = (bf16[584,128]{1,0:T(8,128)(2,1)S(1)}, bf16[584,128]{1,0:T(8,128)(2,1)S(1)}, u32[]{:S(2)}, u32[]{:S(2)}) collective-permute-start(bf16[584,128]{1,0:T(8,128)(2,1)S(1)} %get-tuple-element.30), channel_id=1, source_target_pairs={{0,3},{1,2},{2,1},{3,0},{4,7},{5,6},{6,5},{7,4},{8,11},{9,10},{10,... | collective-permute-start | bytes 448520 | tf_op jit(solution)/shard_map/ppermute | solution.py:286
  6.0 2.0 %collective-permute-start.7 = (bf16[576,128]{1,0:T(8,128)(2,1)S(1)}, bf16[576,128]{1,0:T(8,128)(2,1)S(1)}, u32[]{:S(2)}, u32[]{:S(2)}) collective-permute-start(bf16[576,128]{1,0:T(8,128)(2,1)S(1)} %get-tuple-element.36), channel_id=1, source_target_pairs={{8,1},{9,0},{0,5},{1,4},{4,13},{5,12},{12,9},{13,8},{10,3},{11,2},... | collective-permute-start | bytes 442376 | tf_op jit(solution)/shard_map/ppermute | solution.py:283
  8.1 0.8 %collective-permute-start.8 = (bf16[576,128]{1,0:T(8,128)(2,1)S(1)}, bf16[576,128]{1,0:T(8,128)(2,1)S(1)}, u32[]{:S(2)}, u32[]{:S(2)}) collective-permute-start(bf16[576,128]{1,0:T(8,128)(2,1)S(1)} %get-tuple-element.36), channel_id=1, source_target_pairs={{0,3},{1,2},{2,1},{3,0},{4,7},{5,6},{6,5},{7,4},{8,11},{9,10},{10,... | collective-permute-start | bytes 442376 | tf_op jit(solution)/shard_map/ppermute | solution.py:286
  8.9 0.0 collective-permute-done.refs_4_
  8.9 0.8 %collective-permute-done.1.refs_0_ = bf16[584,128]{1,0:T(8,128)(2,1)S(1)} collective-permute-done((bf16[584,128]{1,0:T(8,128)(2,1)S(1)}, bf16[584,128]{1,0:T(8,128)(2,1)S(1)}, u32[]{:S(2)}, u32[]{:S(2)}) %collective-permute-start.1) | collective-permute-done | bytes 149536 | tf_op jit(solution)/shard_map/ppermute | solution.py:286
  9.7 3.9 %collective-permute-start.2 = (bf16[584,128]{1,0:T(8,128)(2,1)S(1)}, bf16[584,128]{1,0:T(8,128)(2,1)S(1)}, u32[]{:S(2)}, u32[]{:S(2)}) collective-permute-start(bf16[584,128]{1,0:T(8,128)(2,1)S(1)} %collective-permute-done.refs_4_), channel_id=1, source_target_pairs={{8,1},{9,0},{0,5},{1,4},{4,13},{5,12},{12,9},{13,8},{10,3},{11,2},... | collective-permute-start | bytes 448520 | tf_op jit(solution)/shard_map/ppermute | solution.py:283
  13.6 0.0 collective-permute-start.3
  13.6 1.6 %collective-permute-start.6 = (bf16[1160,128]{1,0:T(8,128)(2,1)S(1)}, bf16[1160,128]{1,0:T(8,128)(2,1)S(1)}, u32[]{:S(2)}, u32[]{:S(2)}) collective-permute-start(bf16[1160,128]{1,0:T(8,128)(2,1)S(1)} %get-tuple-element.29.own.left), channel_id=1, source_target_pairs={{0,1},{1,0},{2,3},{3,2},{4,5},{5,4},{6,7},{7,6},{8,9},{9,8},{10,11... | collective-permute-start | bytes 890888 | tf_op jit(solution)/shard_map/ppermute | solution.py:289
  15.2 0.0 collective-permute-done.7.refs_5_
  15.2 0.0 collective-permute-done.8.refs_1_
  15.2 0.2 collective-permute-start.10
  15.4 1.2 %collective-permute-start.9 = (bf16[576,128]{1,0:T(8,128)(2,1)S(1)}, bf16[576,128]{1,0:T(8,128)(2,1)S(1)}, u32[]{:S(2)}, u32[]{:S(2)}) collective-permute-start(bf16[576,128]{1,0:T(8,128)(2,1)S(1)} %collective-permute-done.7.refs_5_), channel_id=1, source_target_pairs={{8,1},{9,0},{0,5},{1,4},{4,13},{5,12},{12,9},{13,8},{10,3},{11,2},... | collective-permute-start | bytes 442376 | tf_op jit(solution)/shard_map/ppermute | solution.py:283
  16.6 0.0 collective-permute-done.2.refs_6_
  16.6 3.1 %collective-permute-done.3.refs_2_ = bf16[584,128]{1,0:T(8,128)(2,1)S(1)} collective-permute-done((bf16[584,128]{1,0:T(8,128)(2,1)S(1)}, bf16[584,128]{1,0:T(8,128)(2,1)S(1)}, u32[]{:S(2)}, u32[]{:S(2)}) %collective-permute-start.3) | collective-permute-done | bytes 149536 | tf_op jit(solution)/shard_map/ppermute | solution.py:286
  19.7 0.9 %collective-permute-start.4 = (bf16[584,128]{1,0:T(8,128)(2,1)S(1)}, bf16[584,128]{1,0:T(8,128)(2,1)S(1)}, u32[]{:S(2)}, u32[]{:S(2)}) collective-permute-start(bf16[584,128]{1,0:T(8,128)(2,1)S(1)} %collective-permute-done.2.refs_6_), channel_id=1, source_target_pairs={{8,1},{9,0},{0,5},{1,4},{4,13},{5,12},{12,9},{13,8},{10,3},{11,2},... | collective-permute-start | bytes 448520 | tf_op jit(solution)/shard_map/ppermute | solution.py:283
  20.6 0.6 %collective-permute-start.5 = (bf16[584,128]{1,0:T(8,128)(2,1)S(1)}, bf16[584,128]{1,0:T(8,128)(2,1)S(1)}, u32[]{:S(2)}, u32[]{:S(2)}) collective-permute-start(bf16[584,128]{1,0:T(8,128)(2,1)S(1)} %collective-permute-done.2.refs_6_), channel_id=1, source_target_pairs={{0,3},{1,2},{2,1},{3,0},{4,7},{5,6},{6,5},{7,4},{8,11},{9,10},{10,... | collective-permute-start | bytes 448520 | tf_op jit(solution)/shard_map/ppermute | solution.py:286
  21.2 1.7 %collective-permute-done.10.refs_3_ = bf16[576,128]{1,0:T(8,128)(2,1)S(1)} collective-permute-done((bf16[576,128]{1,0:T(8,128)(2,1)S(1)}, bf16[576,128]{1,0:T(8,128)(2,1)S(1)}, u32[]{:S(2)}, u32[]{:S(2)}) %collective-permute-start.10) | collective-permute-done | bytes 147488 | tf_op jit(solution)/shard_map/ppermute | solution.py:286
  22.9 0.0 collective-permute-done.9.refs_7_
  22.9 0.4 %collective-permute-start.12 = (bf16[576,128]{1,0:T(8,128)(2,1)S(1)}, bf16[576,128]{1,0:T(8,128)(2,1)S(1)}, u32[]{:S(2)}, u32[]{:S(2)}) collective-permute-start(bf16[576,128]{1,0:T(8,128)(2,1)S(1)} %collective-permute-done.9.refs_7_), channel_id=1, source_target_pairs={{8,1},{9,0},{0,5},{1,4},{4,13},{5,12},{12,9},{13,8},{10,3},{11,2},... | collective-permute-start | bytes 442376 | tf_op jit(solution)/shard_map/ppermute | solution.py:283
  23.3 1.0 %collective-permute-start.13 = (bf16[576,128]{1,0:T(8,128)(2,1)S(1)}, bf16[576,128]{1,0:T(8,128)(2,1)S(1)}, u32[]{:S(2)}, u32[]{:S(2)}) collective-permute-start(bf16[576,128]{1,0:T(8,128)(2,1)S(1)} %collective-permute-done.9.refs_7_), channel_id=1, source_target_pairs={{0,3},{1,2},{2,1},{3,0},{4,7},{5,6},{6,5},{7,4},{8,11},{9,10},{10,... | collective-permute-start | bytes 442376 | tf_op jit(solution)/shard_map/ppermute | solution.py:286
  24.3 0.0 collective-permute-done.6.other.left
  24.4 2.7 %shard_map.38 = (f32[192,896]{1,0:T(8,128)S(1)}, f32[192,896]{1,0:T(8,128)S(1)}) custom-call(bf16[1160,128]{1,0:T(8,128)(2,1)S(1)} %get-tuple-element.29.own.left, bf16[1160,128]{1,0:T(8,128)(2,1)S(1)} %collective-permute-done.6.other.left, bf16[584,128]{1,0:T(8,128)(2,1)S(1)} %collective-permute-done.1.refs_0_, ...), custom_call_target="tpu_custom_call" | custom-call | tf_op jit(solution)/shard_map/pallas_call | solution.py:228
  27.0 0.0 collective-permute-done.4.refs_2_
  27.0 0.0 collective-permute-done.5.refs_0_
  27.1 1.3 %collective-permute-start.11 = (bf16[584,128]{1,0:T(8,128)(2,1)S(1)}, bf16[584,128]{1,0:T(8,128)(2,1)S(1)}, u32[]{:S(2)}, u32[]{:S(2)}) collective-permute-start(bf16[584,128]{1,0:T(8,128)(2,1)S(1)} %collective-permute-done.5.refs_0_), channel_id=1, source_target_pairs={{8,1},{9,0},{0,5},{1,4},{4,13},{5,12},{12,9},{13,8},{10,3},{11,2},... | collective-permute-start | bytes 448520 | tf_op jit(solution)/shard_map/ppermute | solution.py:283
  28.4 1.4 %collective-permute-done.12.refs_3_ = bf16[576,128]{1,0:T(8,128)(2,1)S(1)} collective-permute-done((bf16[576,128]{1,0:T(8,128)(2,1)S(1)}, bf16[576,128]{1,0:T(8,128)(2,1)S(1)}, u32[]{:S(2)}, u32[]{:S(2)}) %collective-permute-start.12) | collective-permute-done | bytes 147488 | tf_op jit(solution)/shard_map/ppermute | solution.py:283
  29.7 0.2 collective-permute-done.13.refs_1_
  29.9 0.9 %collective-permute-start.14 = (bf16[576,128]{1,0:T(8,128)(2,1)S(1)}, bf16[576,128]{1,0:T(8,128)(2,1)S(1)}, u32[]{:S(2)}, u32[]{:S(2)}) collective-permute-start(bf16[576,128]{1,0:T(8,128)(2,1)S(1)} %collective-permute-done.12.refs_3_), channel_id=1, source_target_pairs={{0,3},{1,2},{2,1},{3,0},{4,7},{5,6},{6,5},{7,4},{8,11},{9,10},{10,... | collective-permute-start | bytes 442376 | tf_op jit(solution)/shard_map/ppermute | solution.py:286
  30.8 1.6 %shard_map.39 = (f32[192,896]{1,0:T(8,128)S(1)}, f32[192,896]{1,0:T(8,128)S(1)}) custom-call(bf16[1160,128]{1,0:T(8,128)(2,1)S(1)} %get-tuple-element.29.own.left, bf16[1160,128]{1,0:T(8,128)(2,1)S(1)} %collective-permute-done.6.other.left, bf16[584,128]{1,0:T(8,128)(2,1)S(1)} %collective-permute-done.5.refs_0_, ...), custom_call_target="tpu_custom_call", output_to_operand_aliasing={{0}: (6, {}), {1}: (7, {})} | custom-call | tf_op jit(solution)/shard_map/pallas_call | solution.py:228
  32.5 1.0 %collective-permute-done.11.first = bf16[584,128]{1,0:T(8,128)(2,1)S(1)} collective-permute-done((bf16[584,128]{1,0:T(8,128)(2,1)S(1)}, bf16[584,128]{1,0:T(8,128)(2,1)S(1)}, u32[]{:S(2)}, u32[]{:S(2)}) %collective-permute-start.11) | collective-permute-done | bytes 149536 | tf_op jit(solution)/shard_map/ppermute | solution.py:283
  33.5 0.8 %shard_map.40 = (f32[192,896]{1,0:T(8,128)S(1)}, f32[192,896]{1,0:T(8,128)S(1)}) custom-call(bf16[1160,128]{1,0:T(8,128)(2,1)S(1)} %get-tuple-element.29.own.left, bf16[1160,128]{1,0:T(8,128)(2,1)S(1)} %collective-permute-done.6.other.left, bf16[584,128]{1,0:T(8,128)(2,1)S(1)} %collective-permute-done.11.first, ...), custom_call_target="tpu_custom_call", output_to_operand_aliasing={{0}: (3, {}), {1}: (4, {})} | custom-call | tf_op jit(solution)/shard_map/pallas_call | solution.py:228
  34.3 1.5 %collective-permute-done.14.second = bf16[576,128]{1,0:T(8,128)(2,1)S(1)} collective-permute-done((bf16[576,128]{1,0:T(8,128)(2,1)S(1)}, bf16[576,128]{1,0:T(8,128)(2,1)S(1)}, u32[]{:S(2)}, u32[]{:S(2)}) %collective-permute-start.14) | collective-permute-done | bytes 147488 | tf_op jit(solution)/shard_map/ppermute | solution.py:286
  35.8 0.5 %shard_map.42 = bf16[192,896]{1,0:T(8,128)(2,1)S(1)} custom-call(bf16[1160,128]{1,0:T(8,128)(2,1)S(1)} %collective-permute-done.6.other.left, bf16[584,128]{1,0:T(8,128)(2,1)S(1)} %collective-permute-done.11.first, bf16[576,128]{1,0:T(8,128)(2,1)S(1)} %collective-permute-done.14.second, f32[192,896]{1,0:T(8,128)S(1)} %get-tuple-element.52.before), custom_call_target="tpu_custom_call" | custom-call | tf_op jit(solution)/shard_map/pallas_call | solution.py:228
  36.3 0.2 collective-permute-start.15
  36.5 0.5 %shard_map.41.mine = f32[192,896]{1,0:T(8,128)S(1)} custom-call(bf16[1160,128]{1,0:T(8,128)(2,1)S(1)} %get-tuple-element.29.own.left, bf16[584,128]{1,0:T(8,128)(2,1)S(1)} %collective-permute-done.11.first, bf16[576,128]{1,0:T(8,128)(2,1)S(1)} %collective-permute-done.14.second, f32[192,896]{1,0:T(8,128)S(1)} %get-tuple-element.51.before), custom_call_target="tpu_custom_call" | custom-call | tf_op jit(solution)/shard_map/pallas_call | solution.py:228
  37.1 1.0 %collective-permute-done.15.theirs = bf16[192,896]{1,0:T(8,128)(2,1)S(1)} collective-permute-done((bf16[192,896]{1,0:T(8,128)(2,1)S(1)}, bf16[192,896]{1,0:T(8,128)(2,1)S(1)}, u32[]{:S(2)}, u32[]{:S(2)}) %collective-permute-start.15) | collective-permute-done | bytes 344096 | tf_op jit(solution)/shard_map/ppermute | solution.py:289
  38.1 0.9 %shard_map.43 = bf16[192,768]{1,0:T(8,128)(2,1)} custom-call(f32[192,896]{1,0:T(8,128)S(1)} %shard_map.41.mine, bf16[192,896]{1,0:T(8,128)(2,1)S(1)} %collective-permute-done.15.theirs), custom_call_target="tpu_custom_call" | custom-call | tf_op jit(solution)/shard_map/pallas_call | solution.py:228
Async XLA Ops:
  0.0 0.7 %copy-start.2 = (s32[192]{0:T(256)S(1)}, s32[192]{0:T(256)}, u32[]{:S(2)}) copy-start(s32[192]{0:T(256)} %param.5) | copy-start | bytes 2308
  0.0 0.7 %copy-start.1 = (s32[192,1]{0,1:T(1,128)S(1)}, s32[192,1]{0,1:T(1,128)}, u32[]{:S(2)}) copy-start(s32[192,1]{0,1:T(1,128)} %param.4) | copy-start | bytes 2308
  0.7 1.0 %copy-start = (bf16[192,768]{1,0:T(8,128)(2,1)S(1)}, bf16[192,768]{1,0:T(8,128)(2,1)}, u32[]{:S(2)}) copy-start(bf16[192,768]{1,0:T(8,128)(2,1)} %rows.1) | copy-start | bytes 884740
  1.7 7.1 %collective-permute-start = (bf16[584,128]{1,0:T(8,128)(2,1)S(1)}, bf16[584,128]{1,0:T(8,128)(2,1)S(1)}, u32[]{:S(2)}, u32[]{:S(2)}) collective-permute-start(bf16[584,128]{1,0:T(8,128)(2,1)S(1)} %get-tuple-element.30), channel_id=1, source_target_pairs={{8,1},{9,0},{0,5},{1,4},{4,13},{5,12},{12,9},{13,8},{10,3},{11,2},... | collective-permute-start | bytes 448520 | tf_op jit(solution)/shard_map/ppermute | solution.py:283
  4.3 5.5 %collective-permute-start.1 = (bf16[584,128]{1,0:T(8,128)(2,1)S(1)}, bf16[584,128]{1,0:T(8,128)(2,1)S(1)}, u32[]{:S(2)}, u32[]{:S(2)}) collective-permute-start(bf16[584,128]{1,0:T(8,128)(2,1)S(1)} %get-tuple-element.30), channel_id=1, source_target_pairs={{0,3},{1,2},{2,1},{3,0},{4,7},{5,6},{6,5},{7,4},{8,11},{9,10},{10,... | collective-permute-start | bytes 448520 | tf_op jit(solution)/shard_map/ppermute | solution.py:286
  6.0 9.2 %collective-permute-start.7 = (bf16[576,128]{1,0:T(8,128)(2,1)S(1)}, bf16[576,128]{1,0:T(8,128)(2,1)S(1)}, u32[]{:S(2)}, u32[]{:S(2)}) collective-permute-start(bf16[576,128]{1,0:T(8,128)(2,1)S(1)} %get-tuple-element.36), channel_id=1, source_target_pairs={{8,1},{9,0},{0,5},{1,4},{4,13},{5,12},{12,9},{13,8},{10,3},{11,2},... | collective-permute-start | bytes 442376 | tf_op jit(solution)/shard_map/ppermute | solution.py:283
  8.1 7.1 %collective-permute-start.8 = (bf16[576,128]{1,0:T(8,128)(2,1)S(1)}, bf16[576,128]{1,0:T(8,128)(2,1)S(1)}, u32[]{:S(2)}, u32[]{:S(2)}) collective-permute-start(bf16[576,128]{1,0:T(8,128)(2,1)S(1)} %get-tuple-element.36), channel_id=1, source_target_pairs={{0,3},{1,2},{2,1},{3,0},{4,7},{5,6},{6,5},{7,4},{8,11},{9,10},{10,... | collective-permute-start | bytes 442376 | tf_op jit(solution)/shard_map/ppermute | solution.py:286
  9.7 6.9 %collective-permute-start.2 = (bf16[584,128]{1,0:T(8,128)(2,1)S(1)}, bf16[584,128]{1,0:T(8,128)(2,1)S(1)}, u32[]{:S(2)}, u32[]{:S(2)}) collective-permute-start(bf16[584,128]{1,0:T(8,128)(2,1)S(1)} %collective-permute-done.refs_4_), channel_id=1, source_target_pairs={{8,1},{9,0},{0,5},{1,4},{4,13},{5,12},{12,9},{13,8},{10,3},{11,2},... | collective-permute-start | bytes 448520 | tf_op jit(solution)/shard_map/ppermute | solution.py:283
  13.6 6.1 %collective-permute-start.3 = (bf16[584,128]{1,0:T(8,128)(2,1)S(1)}, bf16[584,128]{1,0:T(8,128)(2,1)S(1)}, u32[]{:S(2)}, u32[]{:S(2)}) collective-permute-start(bf16[584,128]{1,0:T(8,128)(2,1)S(1)} %collective-permute-done.refs_4_), channel_id=1, source_target_pairs={{0,3},{1,2},{2,1},{3,0},{4,7},{5,6},{6,5},{7,4},{8,11},{9,10},{10,... | collective-permute-start | bytes 448520 | tf_op jit(solution)/shard_map/ppermute | solution.py:286
  13.6 10.8 %collective-permute-start.6 = (bf16[1160,128]{1,0:T(8,128)(2,1)S(1)}, bf16[1160,128]{1,0:T(8,128)(2,1)S(1)}, u32[]{:S(2)}, u32[]{:S(2)}) collective-permute-start(bf16[1160,128]{1,0:T(8,128)(2,1)S(1)} %get-tuple-element.29.own.left), channel_id=1, source_target_pairs={{0,1},{1,0},{2,3},{3,2},{4,5},{5,4},{6,7},{7,6},{8,9},{9,8},{10,11... | collective-permute-start | bytes 890888 | tf_op jit(solution)/shard_map/ppermute | solution.py:289
  15.2 7.7 %collective-permute-start.10 = (bf16[576,128]{1,0:T(8,128)(2,1)S(1)}, bf16[576,128]{1,0:T(8,128)(2,1)S(1)}, u32[]{:S(2)}, u32[]{:S(2)}) collective-permute-start(bf16[576,128]{1,0:T(8,128)(2,1)S(1)} %collective-permute-done.7.refs_5_), channel_id=1, source_target_pairs={{0,3},{1,2},{2,1},{3,0},{4,7},{5,6},{6,5},{7,4},{8,11},{9,10},{10,... | collective-permute-start | bytes 442376 | tf_op jit(solution)/shard_map/ppermute | solution.py:286
  15.4 7.5 %collective-permute-start.9 = (bf16[576,128]{1,0:T(8,128)(2,1)S(1)}, bf16[576,128]{1,0:T(8,128)(2,1)S(1)}, u32[]{:S(2)}, u32[]{:S(2)}) collective-permute-start(bf16[576,128]{1,0:T(8,128)(2,1)S(1)} %collective-permute-done.7.refs_5_), channel_id=1, source_target_pairs={{8,1},{9,0},{0,5},{1,4},{4,13},{5,12},{12,9},{13,8},{10,3},{11,2},... | collective-permute-start | bytes 442376 | tf_op jit(solution)/shard_map/ppermute | solution.py:283
  19.7 7.3 %collective-permute-start.4 = (bf16[584,128]{1,0:T(8,128)(2,1)S(1)}, bf16[584,128]{1,0:T(8,128)(2,1)S(1)}, u32[]{:S(2)}, u32[]{:S(2)}) collective-permute-start(bf16[584,128]{1,0:T(8,128)(2,1)S(1)} %collective-permute-done.2.refs_6_), channel_id=1, source_target_pairs={{8,1},{9,0},{0,5},{1,4},{4,13},{5,12},{12,9},{13,8},{10,3},{11,2},... | collective-permute-start | bytes 448520 | tf_op jit(solution)/shard_map/ppermute | solution.py:283
  20.6 6.4 %collective-permute-start.5 = (bf16[584,128]{1,0:T(8,128)(2,1)S(1)}, bf16[584,128]{1,0:T(8,128)(2,1)S(1)}, u32[]{:S(2)}, u32[]{:S(2)}) collective-permute-start(bf16[584,128]{1,0:T(8,128)(2,1)S(1)} %collective-permute-done.2.refs_6_), channel_id=1, source_target_pairs={{0,3},{1,2},{2,1},{3,0},{4,7},{5,6},{6,5},{7,4},{8,11},{9,10},{10,... | collective-permute-start | bytes 448520 | tf_op jit(solution)/shard_map/ppermute | solution.py:286
  22.9 6.8 %collective-permute-start.12 = (bf16[576,128]{1,0:T(8,128)(2,1)S(1)}, bf16[576,128]{1,0:T(8,128)(2,1)S(1)}, u32[]{:S(2)}, u32[]{:S(2)}) collective-permute-start(bf16[576,128]{1,0:T(8,128)(2,1)S(1)} %collective-permute-done.9.refs_7_), channel_id=1, source_target_pairs={{8,1},{9,0},{0,5},{1,4},{4,13},{5,12},{12,9},{13,8},{10,3},{11,2},... | collective-permute-start | bytes 442376 | tf_op jit(solution)/shard_map/ppermute | solution.py:283
  23.3 6.6 %collective-permute-start.13 = (bf16[576,128]{1,0:T(8,128)(2,1)S(1)}, bf16[576,128]{1,0:T(8,128)(2,1)S(1)}, u32[]{:S(2)}, u32[]{:S(2)}) collective-permute-start(bf16[576,128]{1,0:T(8,128)(2,1)S(1)} %collective-permute-done.9.refs_7_), channel_id=1, source_target_pairs={{0,3},{1,2},{2,1},{3,0},{4,7},{5,6},{6,5},{7,4},{8,11},{9,10},{10,... | collective-permute-start | bytes 442376 | tf_op jit(solution)/shard_map/ppermute | solution.py:286
  27.1 6.4 %collective-permute-start.11 = (bf16[584,128]{1,0:T(8,128)(2,1)S(1)}, bf16[584,128]{1,0:T(8,128)(2,1)S(1)}, u32[]{:S(2)}, u32[]{:S(2)}) collective-permute-start(bf16[584,128]{1,0:T(8,128)(2,1)S(1)} %collective-permute-done.5.refs_0_), channel_id=1, source_target_pairs={{8,1},{9,0},{0,5},{1,4},{4,13},{5,12},{12,9},{13,8},{10,3},{11,2},... | collective-permute-start | bytes 448520 | tf_op jit(solution)/shard_map/ppermute | solution.py:283
  29.9 5.9 %collective-permute-start.14 = (bf16[576,128]{1,0:T(8,128)(2,1)S(1)}, bf16[576,128]{1,0:T(8,128)(2,1)S(1)}, u32[]{:S(2)}, u32[]{:S(2)}) collective-permute-start(bf16[576,128]{1,0:T(8,128)(2,1)S(1)} %collective-permute-done.12.refs_3_), channel_id=1, source_target_pairs={{0,3},{1,2},{2,1},{3,0},{4,7},{5,6},{6,5},{7,4},{8,11},{9,10},{10,... | collective-permute-start | bytes 442376 | tf_op jit(solution)/shard_map/ppermute | solution.py:286
  36.3 1.7 %collective-permute-start.15 = (bf16[192,896]{1,0:T(8,128)(2,1)S(1)}, bf16[192,896]{1,0:T(8,128)(2,1)S(1)}, u32[]{:S(2)}, u32[]{:S(2)}) collective-permute-start(bf16[192,896]{1,0:T(8,128)(2,1)S(1)} %shard_map.42), channel_id=1, source_target_pairs={{0,1},{1,0},{2,3},{3,2},{4,5},{5,4},{6,7},{7,6},{8,9},{9,8},{10,11... | collective-permute-start | bytes 1032200 | tf_op jit(solution)/shard_map/ppermute | solution.py:289

commit v13 on v11

--- a/solution.py
+++ b/solution.py
@@ -10,6 +10,7 @@
 F32 = jnp.float32
 BF16 = jnp.bfloat16
 VMEM_BYTES = 24 * 1024 * 1024
+PARTS = 3
 GATHER_LIMIT = 8 * 1024 * 1024
 
 
@@ -102,6 +103,7 @@
     named = named.astype(F32).astype(BF16)
     whole[slabs * rows_here :, :] = named
     first[slabs * half :, :] = named
+    second[slabs * half :, :] = named
 
 
 def from_slabs(ref, count):
@@ -125,8 +127,9 @@
     return rows, key_row(first, rows_here)
 
 
-def add_blocks(left, key, scale, blocks, numer, denom):
-    scale = 4.0 * scale
+def add_blocks(left, info, blocks, numer, denom):
+    key = info[: left.shape[0], 0:1]
+    scale = info[: left.shape[0], 1:2]
     for right_rows, right_key, right_scale in blocks:
         grams = lax.dot_general(
             left, right_rows, (((1,), (1,)), ((), ())), preferred_element_type=F32
@@ -140,10 +143,8 @@
     return numer, denom
 
 
-def left_of(refs, rows_here):
-    rows = jnp.concatenate([from_slabs(ref, rows_here) for ref in refs], axis=0)
-    key = jnp.concatenate([to_column(key_row(ref, rows_here)) for ref in refs], axis=0)
-    return rows, key, scale_column(rows)
+def left_rows(refs, rows_here):
+    return jnp.concatenate([from_slabs(ref, rows_here) for ref in refs], axis=0)
 
 
 def take_blocks(refs, count, rows_here):
@@ -164,36 +165,64 @@
 
 def start_kernel(n_blocks, own, other, *refs):
     refs = list(refs)
-    rows_here = refs[-1].shape[0]
-    left, key, scale = left_of((own, other), rows_here)
+    rows_here = refs[-1].shape[0] // 2
+    left = left_rows((own, other), rows_here)
+    key = jnp.concatenate([to_column(key_row(ref, rows_here)) for ref in (own, other)], axis=0)
+    scale = scale_column(left)
+    info = refs.pop()
+    lane = lax.broadcasted_iota(jnp.int32, info.shape, 1)
+    info[...] = jnp.where(lane == 0, key, 4.0 * scale)
     first = (left[:rows_here], key_row(own, rows_here), to_row(scale[:rows_here]))
     blocks = [first] + take_blocks(refs, n_blocks, rows_here)
-    store_sides(*add_blocks(left, key, scale, blocks, None, None), refs)
-
-
-def both_kernel(n_blocks, own, other, *refs):
+    store_sides(*add_blocks(left, info, blocks, None, None), refs)
+
+
+def both_kernel(n_blocks, own, other, info, *refs):
     refs = list(refs)
     rows_here, wide = refs[-1].shape
-    left, key, scale = left_of((own, other), rows_here)
+    left = left_rows((own, other), rows_here)
     blocks = take_blocks(refs, n_blocks, rows_here)
     numer = jnp.concatenate([ref[:, : wide - 128] for ref in refs[:2]], axis=0)
     denom = jnp.concatenate([ref[:, wide - 128 : wide - 127] for ref in refs[:2]], axis=0)
-    store_sides(*add_blocks(left, key, scale, blocks, numer, denom), refs[2:])
-
-
-def one_kernel(n_blocks, left, *refs):
-    refs = list(refs)
-    rows_here, wide = refs[-1].shape
-    blocks = take_blocks(refs, n_blocks, rows_here)
-    numer = refs[0][:, : wide - 128]
-    denom = refs[0][:, wide - 128 : wide - 127]
-    store_sides(*add_blocks(*left_of((left,), rows_here), blocks, numer, denom), refs[1:])
-
-
-def mean_kernel(mine, theirs, out):
-    width = out.shape[1]
-    denom = mine[:, width : width + 1] + theirs[:, width : width + 1]
-    out[...] = ((mine[:, :width] + theirs[:, :width]) / denom).astype(BF16)
+    store_sides(*add_blocks(left, info, blocks, numer, denom), refs[2:])
+
+
+def half_of(piece, top, rows_here):
+    rows = from_slabs(piece, rows_here // 2)
+    key = to_column(key_row(piece, rows_here))[top : top + rows_here // 2]
+    return rows, to_row(key), to_row(scale_column(rows))
+
+
+def first_half_kernel(own, other, info, first, mine_in, theirs_in, mine, *theirs):
+    rows_here, wide = mine.shape
+    width = wide - 128
+    left = left_rows((own, other), rows_here)
+    blocks = [half_of(first, 0, rows_here)]
+    numer = jnp.concatenate([ref[:, :width] for ref in (mine_in, theirs_in)], axis=0)
+    denom = jnp.concatenate([ref[:, width : width + 1] for ref in (mine_in, theirs_in)], axis=0)
+    numer, denom = add_blocks(left, info, blocks, numer, denom)
+    store_sides(numer[:rows_here], denom[:rows_here], [mine])
+    denom = denom[rows_here:]
+    high = denom.astype(BF16).astype(F32)
+    lane = lax.broadcasted_iota(jnp.int32, (rows_here, 128), 1)
+    pair = jnp.where(lane == 0, high, denom - high).astype(BF16)
+    count = rows_here // len(theirs)
+    for part, out in enumerate(theirs):
+        top = part * count
+        out[:, :width] = numer[rows_here + top : rows_here + top + count].astype(BF16)
+        out[:, width:] = pair[top : top + count]
+
+
+def last_kernel(own, info, second, second_other, mine, *refs):
+    out = refs[-1]
+    rows_here, width = out.shape
+    theirs = jnp.concatenate([ref[...] for ref in refs[:-1]], axis=0)
+    blocks = [half_of(ref, rows_here // 2, rows_here) for ref in (second, second_other)]
+    parts = theirs[:, width:].astype(F32)
+    numer = mine[:, :width] + theirs[:, :width].astype(F32)
+    denom = mine[:, width : width + 1] + (parts[:, 0:1] + parts[:, 1:2])
+    numer, denom = add_blocks(left_rows((own,), rows_here), info, blocks, numer, denom)
+    out[...] = (numer / denom).astype(BF16)
 
 
 def whole_in_vmem(count):
@@ -212,8 +241,10 @@
 
 
 def start_both(left, right, shape):
+    rows_here = shape[0]
     args = list(left) + [half for block in right for half in block]
-    return call(functools.partial(start_kernel, len(right)), [(shape, F32)] * 2, args)
+    shapes = [(shape, F32), (shape, F32), ((2 * rows_here, 128), F32)]
+    return call(functools.partial(start_kernel, len(right)), shapes, args)
 
 
 def add_both(left, right, before):
@@ -225,10 +256,10 @@
     )
 
 
-def add_one(left, right, before):
-    args = [left] + [half for block in right for half in block] + [before]
-    shapes = [(before.shape, F32)]
-    return call(functools.partial(one_kernel, len(right)), shapes, args, {len(args) - 1: 0})[0]
+def add_first_half(left, first, before):
+    rows_here, wide = before[0].shape
+    shapes = [((rows_here, wide), F32)] + [((rows_here // PARTS, wide), BF16)] * PARTS
+    return call(first_half_kernel, shapes, [*left, first, *before], {4: 0})
 
 
 def folded_ring(size):
@@ -266,7 +297,7 @@
         [
             ((slabs * rows_here + 8, 128), BF16),
             ((slabs * half + 8, 128), BF16),
-            ((slabs * half, 128), BF16),
+            ((slabs * half + 8, 128), BF16),
         ],
         [embeddings, group_of.reshape(line), cluster_id.reshape(line)],
     )
@@ -279,13 +310,20 @@
         along_by.append(tuple(pair[0] for pair in pairs))
         across_by.append(tuple(pair[1] for pair in pairs))
     left = (whole, other_core(whole))
-    total = start_both(left, across_by[:-1] + along_by[1:-1], (rows_here, width + 128))
-    near_first, _, mine, theirs = together(across_by[-1][0], along_by[-1][0], *total)
-    last = (along(near_first), across(along_by[-1][1]))
+    mine, theirs, info = start_both(
+        left, across_by[:-1] + along_by[1:-1], (rows_here, width + 128)
+    )
+    left = (*left, info)
+    near_first, _, mine, theirs = together(across_by[-1][0], along_by[-1][0], mine, theirs)
+    last_first, last_second = along(near_first), across(along_by[-1][1])
     mine, theirs = add_both(left, [across_by[-1], along_by[-1]], (mine, theirs))
-    theirs = other_core(add_one(left[1], [last], theirs))
-    mine = add_one(left[0], [last], mine)
-    (out,) = call(mean_kernel, [((rows_here, width), BF16)], [mine, theirs])
+    mine, *theirs = add_first_half(left, last_first, (mine, theirs))
+    last_second, *back = together(last_second, *[other_core(part) for part in theirs])
+    (out,) = call(
+        last_kernel,
+        [((rows_here, width), BF16)],
+        [whole, info, last_second, other_core(last_second), mine, *back],
+    )
     return out
 
 
@@ -293,7 +331,7 @@
     rows_here, width = embeddings.shape
     devices = lax.axis_size("blk") * lax.axis_size("sub") * lax.axis_size("pair")
     small = devices * rows_here * width * 2 <= GATHER_LIMIT
-    fits = width % 128 == 0 and rows_here % 32 == 0 and rows_here <= 512
+    fits = width % 128 == 0 and rows_here % (32 * PARTS) == 0 and rows_here <= 512
     if small and fits and lax.axis_size("sub") == 2 and lax.axis_size("pair") == 2:
         return by_block(embeddings, group_of, cluster_id)
     return by_group(embeddings, group_of, cluster_id)

time: 39.6 us -> 39.5 us (level)
  waiting for transfers between devices: 12 us -> 9.38 us
  starting transfers between devices: 19.2 us -> 21.5 us
    ppermute x7, waiting for transfers between devices: 9.23 us -> 6.11 us  [across(): return lax.ppermute(rows, ('sub', 'pair'), [(0, 3), (1, 2), (2, 1), (3, 0)])]
    ppermute x2 -> x5, starting transfers between devices: 1.79 us -> 3.13 us  [other_core(): return lax.ppermute(rows, 'pair', [(0, 1), (1, 0)])]
    ppermute x7, starting transfers between devices: 5.22 us -> 6.41 us  [across(): return lax.ppermute(rows, ('sub', 'pair'), [(0, 3), (1, 2), (2, 1), (3, 0)])]
    ppermute x2 -> x5, waiting for transfers between devices: 1.42 us -> 1.82 us  [other_core(): return lax.ppermute(rows, 'pair', [(0, 1), (1, 0)])]
    pallas_call x6 -> x5, Pallas kernels: 6.5 us -> 6.78 us  [call(): pl.pallas_call(kernel, out_shape=[jax.ShapeDtypeStruct(shape, dtype) for...]
  transfers between devices with their start and end apart: 16 -> 19, of which waited for: 7 -> 13; matrix products, arithmetic and copies ran while one was open for 0% -> 0% of each run, Pallas kernels for 13% -> 13%
where the time goes in v13:
time: 39.5 us; the launch traced here: 39.4 us
  starting transfers between devices  21.5 us (54%)
  waiting for transfers between devices  9.38 us (24%)
  Pallas kernels  6.78 us (17%)
  local copies, waits for them, and re-layouts  1.65 us (4%)
    ppermute x7, starting transfers between devices, along(): return lax.ppermute(rows, ('blk', 'pair'), hops)  12 us
    pallas_call x5, Pallas kernels, call(): pl.pallas_call(kernel, out_shape=[jax.ShapeDtypeStruct(shape, dtype) for...  6.78 us
    ppermute x7, starting transfers between devices, across(): return lax.ppermute(rows, ('sub', 'pair'), [(0, 3), (1, 2), (2, 1), (3, 0)])  6.41 us
    ppermute x7, waiting for transfers between devices, across(): return lax.ppermute(rows, ('sub', 'pair'), [(0, 3), (1, 2), (2, 1), (3, 0)])  6.11 us
    ppermute x5, starting transfers between devices, other_core(): return lax.ppermute(rows, 'pair', [(0, 1), (1, 0)])  3.13 us
    ppermute x5, waiting for transfers between devices, other_core(): return lax.ppermute(rows, 'pair', [(0, 1), (1, 0)])  1.82 us
    unnamed x6, local copies, waits for them, and re-layouts  1.65 us
    ppermute x7, waiting for transfers between devices, along(): return lax.ppermute(rows, ('blk', 'pair'), hops)  1.46 us
  transfers between devices with their start and end apart: 19, of which 13 were waited for; matrix products, arithmetic and copies ran while one was open for 0% of the time, Pallas kernels for 13%

profile of v13, /device:TPU:0, one launch (start us, length us, event | category | flops | bytes accessed | tf_op | source)
XLA Modules:
  0.0 39.4 jit_solution(13917792361164981699)
XLA Ops:
  0.0 0.0 copy-start.2
  0.0 0.0 copy-start.1
  0.0 0.7 %copy-done.2 = s32[192]{0:T(256)S(1)} copy-done((s32[192]{0:T(256)S(1)}, s32[192]{0:T(256)}, u32[]{:S(2)}) %copy-start.2) | copy-done | bytes 792
  0.7 0.0 copy-done.1
  0.7 0.0 copy-start
  0.7 1.0 %copy-done = bf16[192,768]{1,0:T(8,128)(2,1)S(1)} copy-done((bf16[192,768]{1,0:T(8,128)(2,1)S(1)}, bf16[192,768]{1,0:T(8,128)(2,1)}, u32[]{:S(2)}) %copy-start) | copy-done | bytes 294936
  1.7 0.1 shard_map.37
  1.7 2.5 %collective-permute-start.1 = (bf16[584,128]{1,0:T(8,128)(2,1)S(1)}, bf16[584,128]{1,0:T(8,128)(2,1)S(1)}, u32[]{:S(2)}, u32[]{:S(2)}) collective-permute-start(bf16[584,128]{1,0:T(8,128)(2,1)S(1)} %get-tuple-element.37), channel_id=1, source_target_pairs={{8,1},{9,0},{0,5},{1,4},{4,13},{5,12},{12,9},{13,8},{10,3},{11,2},... | collective-permute-start | bytes 448520 | tf_op jit(solution)/shard_map/ppermute | solution.py:287
  4.3 1.8 %collective-permute-start.2 = (bf16[584,128]{1,0:T(8,128)(2,1)S(1)}, bf16[584,128]{1,0:T(8,128)(2,1)S(1)}, u32[]{:S(2)}, u32[]{:S(2)}) collective-permute-start(bf16[584,128]{1,0:T(8,128)(2,1)S(1)} %get-tuple-element.37), channel_id=1, source_target_pairs={{0,3},{1,2},{2,1},{3,0},{4,7},{5,6},{6,5},{7,4},{8,11},{9,10},{10,... | collective-permute-start | bytes 448520 | tf_op jit(solution)/shard_map/ppermute | solution.py:290
  6.0 2.0 %collective-permute-start.3 = (bf16[584,128]{1,0:T(8,128)(2,1)S(1)}, bf16[584,128]{1,0:T(8,128)(2,1)S(1)}, u32[]{:S(2)}, u32[]{:S(2)}) collective-permute-start(bf16[584,128]{1,0:T(8,128)(2,1)S(1)} %get-tuple-element.39), channel_id=1, source_target_pairs={{8,1},{9,0},{0,5},{1,4},{4,13},{5,12},{12,9},{13,8},{10,3},{11,2},... | collective-permute-start | bytes 448520 | tf_op jit(solution)/shard_map/ppermute | solution.py:287
  8.1 0.8 %collective-permute-start.4 = (bf16[584,128]{1,0:T(8,128)(2,1)S(1)}, bf16[584,128]{1,0:T(8,128)(2,1)S(1)}, u32[]{:S(2)}, u32[]{:S(2)}) collective-permute-start(bf16[584,128]{1,0:T(8,128)(2,1)S(1)} %get-tuple-element.39), channel_id=1, source_target_pairs={{0,3},{1,2},{2,1},{3,0},{4,7},{5,6},{6,5},{7,4},{8,11},{9,10},{10,... | collective-permute-start | bytes 448520 | tf_op jit(solution)/shard_map/ppermute | solution.py:290
  8.9 0.0 collective-permute-done.1.refs_4_
  8.9 0.8 %collective-permute-done.2.refs_0_ = bf16[584,128]{1,0:T(8,128)(2,1)S(1)} collective-permute-done((bf16[584,128]{1,0:T(8,128)(2,1)S(1)}, bf16[584,128]{1,0:T(8,128)(2,1)S(1)}, u32[]{:S(2)}, u32[]{:S(2)}) %collective-permute-start.2) | collective-permute-done | bytes 149536 | tf_op jit(solution)/shard_map/ppermute | solution.py:290
  9.7 3.9 %collective-permute-start.5 = (bf16[584,128]{1,0:T(8,128)(2,1)S(1)}, bf16[584,128]{1,0:T(8,128)(2,1)S(1)}, u32[]{:S(2)}, u32[]{:S(2)}) collective-permute-start(bf16[584,128]{1,0:T(8,128)(2,1)S(1)} %collective-permute-done.1.refs_4_), channel_id=1, source_target_pairs={{8,1},{9,0},{0,5},{1,4},{4,13},{5,12},{12,9},{13,8},{10,3},{11,2},... | collective-permute-start | bytes 448520 | tf_op jit(solution)/shard_map/ppermute | solution.py:287
  13.6 0.0 collective-permute-start.6
  13.6 1.6 %collective-permute-start = (bf16[1160,128]{1,0:T(8,128)(2,1)S(1)}, bf16[1160,128]{1,0:T(8,128)(2,1)S(1)}, u32[]{:S(2)}, u32[]{:S(2)}) collective-permute-start(bf16[1160,128]{1,0:T(8,128)(2,1)S(1)} %get-tuple-element.36.own), channel_id=1, source_target_pairs={{0,1},{1,0},{2,3},{3,2},{4,5},{5,4},{6,7},{7,6},{8,9},{9,8},{10,11... | collective-permute-start | bytes 890888 | tf_op jit(solution)/shard_map/ppermute | solution.py:293
  15.2 0.0 collective-permute-done.3.refs_5_
  15.2 0.0 collective-permute-done.4.refs_1_
  15.2 0.8 %collective-permute-start.7 = (bf16[584,128]{1,0:T(8,128)(2,1)S(1)}, bf16[584,128]{1,0:T(8,128)(2,1)S(1)}, u32[]{:S(2)}, u32[]{:S(2)}) collective-permute-start(bf16[584,128]{1,0:T(8,128)(2,1)S(1)} %collective-permute-done.3.refs_5_), channel_id=1, source_target_pairs={{8,1},{9,0},{0,5},{1,4},{4,13},{5,12},{12,9},{13,8},{10,3},{11,2},... | collective-permute-start | bytes 448520 | tf_op jit(solution)/shard_map/ppermute | solution.py:287
  16.0 0.6 %collective-permute-start.8 = (bf16[584,128]{1,0:T(8,128)(2,1)S(1)}, bf16[584,128]{1,0:T(8,128)(2,1)S(1)}, u32[]{:S(2)}, u32[]{:S(2)}) collective-permute-start(bf16[584,128]{1,0:T(8,128)(2,1)S(1)} %collective-permute-done.3.refs_5_), channel_id=1, source_target_pairs={{0,3},{1,2},{2,1},{3,0},{4,7},{5,6},{6,5},{7,4},{8,11},{9,10},{10,... | collective-permute-start | bytes 448520 | tf_op jit(solution)/shard_map/ppermute | solution.py:290
  16.6 0.1 collective-permute-done.5.refs_6_
  16.7 3.0 %collective-permute-done.6.refs_2_ = bf16[584,128]{1,0:T(8,128)(2,1)S(1)} collective-permute-done((bf16[584,128]{1,0:T(8,128)(2,1)S(1)}, bf16[584,128]{1,0:T(8,128)(2,1)S(1)}, u32[]{:S(2)}, u32[]{:S(2)}) %collective-permute-start.6) | collective-permute-done | bytes 149536 | tf_op jit(solution)/shard_map/ppermute | solution.py:290
  19.7 0.4 %collective-permute-start.12 = (bf16[584,128]{1,0:T(8,128)(2,1)S(1)}, bf16[584,128]{1,0:T(8,128)(2,1)S(1)}, u32[]{:S(2)}, u32[]{:S(2)}) collective-permute-start(bf16[584,128]{1,0:T(8,128)(2,1)S(1)} %collective-permute-done.5.refs_6_), channel_id=1, source_target_pairs={{8,1},{9,0},{0,5},{1,4},{4,13},{5,12},{12,9},{13,8},{10,3},{11,2},... | collective-permute-start | bytes 448520 | tf_op jit(solution)/shard_map/ppermute | solution.py:287
  20.2 1.0 %collective-permute-start.13 = (bf16[584,128]{1,0:T(8,128)(2,1)S(1)}, bf16[584,128]{1,0:T(8,128)(2,1)S(1)}, u32[]{:S(2)}, u32[]{:S(2)}) collective-permute-start(bf16[584,128]{1,0:T(8,128)(2,1)S(1)} %collective-permute-done.5.refs_6_), channel_id=1, source_target_pairs={{0,3},{1,2},{2,1},{3,0},{4,7},{5,6},{6,5},{7,4},{8,11},{9,10},{10,... | collective-permute-start | bytes 448520 | tf_op jit(solution)/shard_map/ppermute | solution.py:290
  21.2 0.9 %collective-permute-done.7.refs_7_ = bf16[584,128]{1,0:T(8,128)(2,1)S(1)} collective-permute-done((bf16[584,128]{1,0:T(8,128)(2,1)S(1)}, bf16[584,128]{1,0:T(8,128)(2,1)S(1)}, u32[]{:S(2)}, u32[]{:S(2)}) %collective-permute-start.7) | collective-permute-done | bytes 149536 | tf_op jit(solution)/shard_map/ppermute | solution.py:287
  22.1 0.9 %collective-permute-done.8.refs_3_ = bf16[584,128]{1,0:T(8,128)(2,1)S(1)} collective-permute-done((bf16[584,128]{1,0:T(8,128)(2,1)S(1)}, bf16[584,128]{1,0:T(8,128)(2,1)S(1)}, u32[]{:S(2)}, u32[]{:S(2)}) %collective-permute-start.8) | collective-permute-done | bytes 149536 | tf_op jit(solution)/shard_map/ppermute | solution.py:290
  22.9 0.2 collective-permute-start.10
  23.2 1.2 %collective-permute-start.9 = (bf16[584,128]{1,0:T(8,128)(2,1)S(1)}, bf16[584,128]{1,0:T(8,128)(2,1)S(1)}, u32[]{:S(2)}, u32[]{:S(2)}) collective-permute-start(bf16[584,128]{1,0:T(8,128)(2,1)S(1)} %collective-permute-done.7.refs_7_), channel_id=1, source_target_pairs={{8,1},{9,0},{0,5},{1,4},{4,13},{5,12},{12,9},{13,8},{10,3},{11,2},... | collective-permute-start | bytes 448520 | tf_op jit(solution)/shard_map/ppermute | solution.py:287
  24.3 0.0 collective-permute-done.other
  24.3 2.7 %shard_map.38 = (f32[192,896]{1,0:T(8,128)S(1)}, f32[192,896]{1,0:T(8,128)S(1)}, f32[384,128]{1,0:T(8,128)S(1)}) custom-call(bf16[1160,128]{1,0:T(8,128)(2,1)S(1)} %get-tuple-element.36.own, bf16[1160,128]{1,0:T(8,128)(2,1)S(1)} %collective-permute-done.other, bf16[584,128]{1,0:T(8,128)(2,1)S(1)} %collective-permute-done.2.refs_0_, ...), custom_call_target="tpu_custom_call" | custom-call | tf_op jit(solution)/shard_map/pallas_call | solution.py:233
  27.1 0.0 collective-permute-done.12.refs_2_
  27.1 0.0 collective-permute-done.13.refs_0_
  27.1 1.2 %collective-permute-start.14 = (bf16[584,128]{1,0:T(8,128)(2,1)S(1)}, bf16[584,128]{1,0:T(8,128)(2,1)S(1)}, u32[]{:S(2)}, u32[]{:S(2)}) collective-permute-start(bf16[584,128]{1,0:T(8,128)(2,1)S(1)} %collective-permute-done.13.refs_0_), channel_id=1, source_target_pairs={{8,1},{9,0},{0,5},{1,4},{4,13},{5,12},{12,9},{13,8},{10,3},{11,2},... | collective-permute-start | bytes 448520 | tf_op jit(solution)/shard_map/ppermute | solution.py:287
  28.2 1.2 %collective-permute-done.10.refs_1_ = bf16[584,128]{1,0:T(8,128)(2,1)S(1)} collective-permute-done((bf16[584,128]{1,0:T(8,128)(2,1)S(1)}, bf16[584,128]{1,0:T(8,128)(2,1)S(1)}, u32[]{:S(2)}, u32[]{:S(2)}) %collective-permute-start.10) | collective-permute-done | bytes 149536 | tf_op jit(solution)/shard_map/ppermute | solution.py:290
  29.5 0.2 collective-permute-done.9.refs_3_
  29.6 1.9 %collective-permute-start.11 = (bf16[584,128]{1,0:T(8,128)(2,1)S(1)}, bf16[584,128]{1,0:T(8,128)(2,1)S(1)}, u32[]{:S(2)}, u32[]{:S(2)}) collective-permute-start(bf16[584,128]{1,0:T(8,128)(2,1)S(1)} %collective-permute-done.9.refs_3_), channel_id=1, source_target_pairs={{0,3},{1,2},{2,1},{3,0},{4,7},{5,6},{6,5},{7,4},{8,11},{9,10},{10,... | collective-permute-start | bytes 448520 | tf_op jit(solution)/shard_map/ppermute | solution.py:290
  31.6 1.6 %shard_map.39 = (f32[192,896]{1,0:T(8,128)S(1)}, f32[192,896]{1,0:T(8,128)S(1)}) custom-call(bf16[1160,128]{1,0:T(8,128)(2,1)S(1)} %get-tuple-element.36.own, bf16[1160,128]{1,0:T(8,128)(2,1)S(1)} %collective-permute-done.other, f32[384,128]{1,0:T(8,128)S(1)} %get-tuple-element.47.info, ...), custom_call_target="tpu_custom_call", output_to_operand_aliasing={{0}: (7, {}), {1}: (8, {})} | custom-call | tf_op jit(solution)/shard_map/pallas_call | solution.py:233
  33.2 0.3 collective-permute-done.14.first
  33.4 0.8 %shard_map.40 = (f32[192,896]{1,0:T(8,128)S(1)}, bf16[64,896]{1,0:T(8,128)(2,1)S(1)}, bf16[64,896]{1,0:T(8,128)(2,1)S(1)}, bf16[64,896]{1,0:T(8,128)(2,1)S(1)}) custom-call(bf16[1160,128]{1,0:T(8,128)(2,1)S(1)} %get-tuple-element.36.own, bf16[1160,128]{1,0:T(8,128)(2,1)S(1)} %collective-permute-done.other, ...), custom_call_target="tpu_custom_call", output_to_operand_aliasing={{0}: (4, {})} | custom-call | tf_op jit(solution)/shard_map/pallas_call | solution.py:233
  34.3 0.7 %collective-permute-start.15 = (bf16[64,896]{1,0:T(8,128)(2,1)S(1)}, bf16[64,896]{1,0:T(8,128)(2,1)S(1)}, u32[]{:S(2)}, u32[]{:S(2)}) collective-permute-start(bf16[64,896]{1,0:T(8,128)(2,1)S(1)} %get-tuple-element.59), channel_id=1, source_target_pairs={{0,1},{1,0},{2,3},{3,2},{4,5},{5,4},{6,7},{7,6},{8,9},{9,8},{10,11... | collective-permute-start | bytes 344072 | tf_op jit(solution)/shard_map/ppermute | solution.py:293
  34.9 0.1 collective-permute-start.16
  35.0 0.4 %collective-permute-start.17 = (bf16[64,896]{1,0:T(8,128)(2,1)S(1)}, bf16[64,896]{1,0:T(8,128)(2,1)S(1)}, u32[]{:S(2)}, u32[]{:S(2)}) collective-permute-start(bf16[64,896]{1,0:T(8,128)(2,1)S(1)} %get-tuple-element.61), channel_id=1, source_target_pairs={{0,1},{1,0},{2,3},{3,2},{4,5},{5,4},{6,7},{7,6},{8,9},{9,8},{10,11... | collective-permute-start | bytes 344072 | tf_op jit(solution)/shard_map/ppermute | solution.py:293
  35.4 0.2 collective-permute-done.11.second
  35.6 0.3 collective-permute-done.15.refs_0_
  35.9 0.4 collective-permute-done.16.refs_1_
  36.3 0.2 collective-permute-done.17.refs_2_
  36.4 0.3 collective-permute-start.18
  36.8 1.0 %collective-permute-done.18.second_other = bf16[584,128]{1,0:T(8,128)(2,1)S(1)} collective-permute-done((bf16[584,128]{1,0:T(8,128)(2,1)S(1)}, bf16[584,128]{1,0:T(8,128)(2,1)S(1)}, u32[]{:S(2)}, u32[]{:S(2)}) %collective-permute-start.18) | collective-permute-done | bytes 149536 | tf_op jit(solution)/shard_map/ppermute | solution.py:293
  37.8 1.6 %shard_map.41 = bf16[192,768]{1,0:T(8,128)(2,1)} custom-call(bf16[1160,128]{1,0:T(8,128)(2,1)S(1)} %get-tuple-element.36.own, f32[384,128]{1,0:T(8,128)S(1)} %get-tuple-element.47.info, bf16[584,128]{1,0:T(8,128)(2,1)S(1)} %collective-permute-done.11.second, bf16[584,128]{1,0:T(8,128)(2,1)S(1)} %collective-permute-done.18.second_other, ...), custom_call_target="tpu_custom_call" | custom-call | tf_op jit(solution)/shard_map/pallas_call | solution.py:233
Async XLA Ops:
  0.0 0.7 %copy-start.2 = (s32[192]{0:T(256)S(1)}, s32[192]{0:T(256)}, u32[]{:S(2)}) copy-start(s32[192]{0:T(256)} %param.5) | copy-start | bytes 2308
  0.0 0.7 %copy-start.1 = (s32[192,1]{0,1:T(1,128)S(1)}, s32[192,1]{0,1:T(1,128)}, u32[]{:S(2)}) copy-start(s32[192,1]{0,1:T(1,128)} %param.4) | copy-start | bytes 2308
  0.7 1.0 %copy-start = (bf16[192,768]{1,0:T(8,128)(2,1)S(1)}, bf16[192,768]{1,0:T(8,128)(2,1)}, u32[]{:S(2)}) copy-start(bf16[192,768]{1,0:T(8,128)(2,1)} %rows.1) | copy-start | bytes 884740
  1.7 7.1 %collective-permute-start.1 = (bf16[584,128]{1,0:T(8,128)(2,1)S(1)}, bf16[584,128]{1,0:T(8,128)(2,1)S(1)}, u32[]{:S(2)}, u32[]{:S(2)}) collective-permute-start(bf16[584,128]{1,0:T(8,128)(2,1)S(1)} %get-tuple-element.37), channel_id=1, source_target_pairs={{8,1},{9,0},{0,5},{1,4},{4,13},{5,12},{12,9},{13,8},{10,3},{11,2},... | collective-permute-start | bytes 448520 | tf_op jit(solution)/shard_map/ppermute | solution.py:287
  4.3 5.5 %collective-permute-start.2 = (bf16[584,128]{1,0:T(8,128)(2,1)S(1)}, bf16[584,128]{1,0:T(8,128)(2,1)S(1)}, u32[]{:S(2)}, u32[]{:S(2)}) collective-permute-start(bf16[584,128]{1,0:T(8,128)(2,1)S(1)} %get-tuple-element.37), channel_id=1, source_target_pairs={{0,3},{1,2},{2,1},{3,0},{4,7},{5,6},{6,5},{7,4},{8,11},{9,10},{10,... | collective-permute-start | bytes 448520 | tf_op jit(solution)/shard_map/ppermute | solution.py:290
  6.0 9.2 %collective-permute-start.3 = (bf16[584,128]{1,0:T(8,128)(2,1)S(1)}, bf16[584,128]{1,0:T(8,128)(2,1)S(1)}, u32[]{:S(2)}, u32[]{:S(2)}) collective-permute-start(bf16[584,128]{1,0:T(8,128)(2,1)S(1)} %get-tuple-element.39), channel_id=1, source_target_pairs={{8,1},{9,0},{0,5},{1,4},{4,13},{5,12},{12,9},{13,8},{10,3},{11,2},... | collective-permute-start | bytes 448520 | tf_op jit(solution)/shard_map/ppermute | solution.py:287
  8.1 7.1 %collective-permute-start.4 = (bf16[584,128]{1,0:T(8,128)(2,1)S(1)}, bf16[584,128]{1,0:T(8,128)(2,1)S(1)}, u32[]{:S(2)}, u32[]{:S(2)}) collective-permute-start(bf16[584,128]{1,0:T(8,128)(2,1)S(1)} %get-tuple-element.39), channel_id=1, source_target_pairs={{0,3},{1,2},{2,1},{3,0},{4,7},{5,6},{6,5},{7,4},{8,11},{9,10},{10,... | collective-permute-start | bytes 448520 | tf_op jit(solution)/shard_map/ppermute | solution.py:290
  9.7 7.0 %collective-permute-start.5 = (bf16[584,128]{1,0:T(8,128)(2,1)S(1)}, bf16[584,128]{1,0:T(8,128)(2,1)S(1)}, u32[]{:S(2)}, u32[]{:S(2)}) collective-permute-start(bf16[584,128]{1,0:T(8,128)(2,1)S(1)} %collective-permute-done.1.refs_4_), channel_id=1, source_target_pairs={{8,1},{9,0},{0,5},{1,4},{4,13},{5,12},{12,9},{13,8},{10,3},{11,2},... | collective-permute-start | bytes 448520 | tf_op jit(solution)/shard_map/ppermute | solution.py:287
  13.6 6.1 %collective-permute-start.6 = (bf16[584,128]{1,0:T(8,128)(2,1)S(1)}, bf16[584,128]{1,0:T(8,128)(2,1)S(1)}, u32[]{:S(2)}, u32[]{:S(2)}) collective-permute-start(bf16[584,128]{1,0:T(8,128)(2,1)S(1)} %collective-permute-done.1.refs_4_), channel_id=1, source_target_pairs={{0,3},{1,2},{2,1},{3,0},{4,7},{5,6},{6,5},{7,4},{8,11},{9,10},{10,... | collective-permute-start | bytes 448520 | tf_op jit(solution)/shard_map/ppermute | solution.py:290
  13.6 10.8 %collective-permute-start = (bf16[1160,128]{1,0:T(8,128)(2,1)S(1)}, bf16[1160,128]{1,0:T(8,128)(2,1)S(1)}, u32[]{:S(2)}, u32[]{:S(2)}) collective-permute-start(bf16[1160,128]{1,0:T(8,128)(2,1)S(1)} %get-tuple-element.36.own), channel_id=1, source_target_pairs={{0,1},{1,0},{2,3},{3,2},{4,5},{5,4},{6,7},{7,6},{8,9},{9,8},{10,11... | collective-permute-start | bytes 890888 | tf_op jit(solution)/shard_map/ppermute | solution.py:293
  15.2 6.9 %collective-permute-start.7 = (bf16[584,128]{1,0:T(8,128)(2,1)S(1)}, bf16[584,128]{1,0:T(8,128)(2,1)S(1)}, u32[]{:S(2)}, u32[]{:S(2)}) collective-permute-start(bf16[584,128]{1,0:T(8,128)(2,1)S(1)} %collective-permute-done.3.refs_5_), channel_id=1, source_target_pairs={{8,1},{9,0},{0,5},{1,4},{4,13},{5,12},{12,9},{13,8},{10,3},{11,2},... | collective-permute-start | bytes 448520 | tf_op jit(solution)/shard_map/ppermute | solution.py:287
  16.0 6.9 %collective-permute-start.8 = (bf16[584,128]{1,0:T(8,128)(2,1)S(1)}, bf16[584,128]{1,0:T(8,128)(2,1)S(1)}, u32[]{:S(2)}, u32[]{:S(2)}) collective-permute-start(bf16[584,128]{1,0:T(8,128)(2,1)S(1)} %collective-permute-done.3.refs_5_), channel_id=1, source_target_pairs={{0,3},{1,2},{2,1},{3,0},{4,7},{5,6},{6,5},{7,4},{8,11},{9,10},{10,... | collective-permute-start | bytes 448520 | tf_op jit(solution)/shard_map/ppermute | solution.py:290
  19.7 7.3 %collective-permute-start.12 = (bf16[584,128]{1,0:T(8,128)(2,1)S(1)}, bf16[584,128]{1,0:T(8,128)(2,1)S(1)}, u32[]{:S(2)}, u32[]{:S(2)}) collective-permute-start(bf16[584,128]{1,0:T(8,128)(2,1)S(1)} %collective-permute-done.5.refs_6_), channel_id=1, source_target_pairs={{8,1},{9,0},{0,5},{1,4},{4,13},{5,12},{12,9},{13,8},{10,3},{11,2},... | collective-permute-start | bytes 448520 | tf_op jit(solution)/shard_map/ppermute | solution.py:287
  20.2 6.9 %collective-permute-start.13 = (bf16[584,128]{1,0:T(8,128)(2,1)S(1)}, bf16[584,128]{1,0:T(8,128)(2,1)S(1)}, u32[]{:S(2)}, u32[]{:S(2)}) collective-permute-start(bf16[584,128]{1,0:T(8,128)(2,1)S(1)} %collective-permute-done.5.refs_6_), channel_id=1, source_target_pairs={{0,3},{1,2},{2,1},{3,0},{4,7},{5,6},{6,5},{7,4},{8,11},{9,10},{10,... | collective-permute-start | bytes 448520 | tf_op jit(solution)/shard_map/ppermute | solution.py:290
  22.9 6.5 %collective-permute-start.10 = (bf16[584,128]{1,0:T(8,128)(2,1)S(1)}, bf16[584,128]{1,0:T(8,128)(2,1)S(1)}, u32[]{:S(2)}, u32[]{:S(2)}) collective-permute-start(bf16[584,128]{1,0:T(8,128)(2,1)S(1)} %collective-permute-done.7.refs_7_), channel_id=1, source_target_pairs={{0,3},{1,2},{2,1},{3,0},{4,7},{5,6},{6,5},{7,4},{8,11},{9,10},{10,... | collective-permute-start | bytes 448520 | tf_op jit(solution)/shard_map/ppermute | solution.py:290
  23.2 6.5 %collective-permute-start.9 = (bf16[584,128]{1,0:T(8,128)(2,1)S(1)}, bf16[584,128]{1,0:T(8,128)(2,1)S(1)}, u32[]{:S(2)}, u32[]{:S(2)}) collective-permute-start(bf16[584,128]{1,0:T(8,128)(2,1)S(1)} %collective-permute-done.7.refs_7_), channel_id=1, source_target_pairs={{8,1},{9,0},{0,5},{1,4},{4,13},{5,12},{12,9},{13,8},{10,3},{11,2},... | collective-permute-start | bytes 448520 | tf_op jit(solution)/shard_map/ppermute | solution.py:287
  27.1 6.4 %collective-permute-start.14 = (bf16[584,128]{1,0:T(8,128)(2,1)S(1)}, bf16[584,128]{1,0:T(8,128)(2,1)S(1)}, u32[]{:S(2)}, u32[]{:S(2)}) collective-permute-start(bf16[584,128]{1,0:T(8,128)(2,1)S(1)} %collective-permute-done.13.refs_0_), channel_id=1, source_target_pairs={{8,1},{9,0},{0,5},{1,4},{4,13},{5,12},{12,9},{13,8},{10,3},{11,2},... | collective-permute-start | bytes 448520 | tf_op jit(solution)/shard_map/ppermute | solution.py:287
  29.6 6.0 %collective-permute-start.11 = (bf16[584,128]{1,0:T(8,128)(2,1)S(1)}, bf16[584,128]{1,0:T(8,128)(2,1)S(1)}, u32[]{:S(2)}, u32[]{:S(2)}) collective-permute-start(bf16[584,128]{1,0:T(8,128)(2,1)S(1)} %collective-permute-done.9.refs_3_), channel_id=1, source_target_pairs={{0,3},{1,2},{2,1},{3,0},{4,7},{5,6},{6,5},{7,4},{8,11},{9,10},{10,... | collective-permute-start | bytes 448520 | tf_op jit(solution)/shard_map/ppermute | solution.py:290
  34.3 1.6 %collective-permute-start.15 = (bf16[64,896]{1,0:T(8,128)(2,1)S(1)}, bf16[64,896]{1,0:T(8,128)(2,1)S(1)}, u32[]{:S(2)}, u32[]{:S(2)}) collective-permute-start(bf16[64,896]{1,0:T(8,128)(2,1)S(1)} %get-tuple-element.59), channel_id=1, source_target_pairs={{0,1},{1,0},{2,3},{3,2},{4,5},{5,4},{6,7},{7,6},{8,9},{9,8},{10,11... | collective-permute-start | bytes 344072 | tf_op jit(solution)/shard_map/ppermute | solution.py:293
  34.9 1.3 %collective-permute-start.16 = (bf16[64,896]{1,0:T(8,128)(2,1)S(1)}, bf16[64,896]{1,0:T(8,128)(2,1)S(1)}, u32[]{:S(2)}, u32[]{:S(2)}) collective-permute-start(bf16[64,896]{1,0:T(8,128)(2,1)S(1)} %get-tuple-element.60), channel_id=1, source_target_pairs={{0,1},{1,0},{2,3},{3,2},{4,5},{5,4},{6,7},{7,6},{8,9},{9,8},{10,11... | collective-permute-start | bytes 344072 | tf_op jit(solution)/shard_map/ppermute | solution.py:293
  35.0 1.4 %collective-permute-start.17 = (bf16[64,896]{1,0:T(8,128)(2,1)S(1)}, bf16[64,896]{1,0:T(8,128)(2,1)S(1)}, u32[]{:S(2)}, u32[]{:S(2)}) collective-permute-start(bf16[64,896]{1,0:T(8,128)(2,1)S(1)} %get-tuple-element.61), channel_id=1, source_target_pairs={{0,1},{1,0},{2,3},{3,2},{4,5},{5,4},{6,7},{7,6},{8,9},{9,8},{10,11... | collective-permute-start | bytes 344072 | tf_op jit(solution)/shard_map/ppermute | solution.py:293
  36.4 1.4 %collective-permute-start.18 = (bf16[584,128]{1,0:T(8,128)(2,1)S(1)}, bf16[584,128]{1,0:T(8,128)(2,1)S(1)}, u32[]{:S(2)}, u32[]{:S(2)}) collective-permute-start(bf16[584,128]{1,0:T(8,128)(2,1)S(1)} %collective-permute-done.11.second), channel_id=1, source_target_pairs={{0,1},{1,0},{2,3},{3,2},{4,5},{5,4},{6,7},{7,6},{8,9},{9,8},{10,11... | collective-permute-start | bytes 448520 | tf_op jit(solution)/shard_map/ppermute | solution.py:293

commit v14 on v13

--- a/solution.py
+++ b/solution.py
@@ -77,32 +77,33 @@
     return lax.rsqrt(jnp.sum(wide * wide, axis=1, keepdims=True) + 1e-06)
 
 
-def name_lines(rows_here):
-    return -(-rows_here // 128)
-
-
-def pack_kernel(rows, group, cluster, whole, first, second):
+def first_pack_kernel(rows, first):
+    width = rows.shape[1]
+    slabs = width // 128
+    half = rows.shape[0] // 2
+    for slab in range(slabs):
+        first[slab * half : (slab + 1) * half, :] = rows[:half, slab * 128 : (slab + 1) * 128]
+    first[slabs * half :, :] = jnp.zeros((8, 128), BF16)
+
+
+def pack_kernel(rows, group, cluster, whole, second):
     rows_here, width = rows.shape
     slabs = width // 128
     half = rows_here // 2
     for slab in range(slabs):
         columns = rows[:, slab * 128 : (slab + 1) * 128]
         whole[slab * rows_here : (slab + 1) * rows_here, :] = columns
-        first[slab * half : (slab + 1) * half, :] = columns[:half]
         second[slab * half : (slab + 1) * half, :] = columns[half:]
     line_at = lax.broadcasted_iota(jnp.int32, (8, 128), 0)
-    lines = name_lines(rows_here)
     named = jnp.zeros((8, 128), jnp.int32)
-    for kind, ref in enumerate((group, cluster)):
-        for line in range(lines):
-            part = ref[:, line * 128 : (line + 1) * 128]
-            if part.shape[1] < 128:
-                rest = jnp.zeros((1, 128 - part.shape[1]), jnp.int32)
-                part = jnp.concatenate([part, rest], axis=1)
-            named = jnp.where(line_at == kind * lines + line, part, named)
+    for line in range(4):
+        top = line % 2 * half
+        part = (group, cluster)[line // 2][:, top : top + half]
+        if half < 128:
+            part = jnp.concatenate([part, jnp.zeros((1, 128 - half), jnp.int32)], axis=1)
+        named = jnp.where(line_at == line, part, named)
     named = named.astype(F32).astype(BF16)
     whole[slabs * rows_here :, :] = named
-    first[slabs * half :, :] = named
     second[slabs * half :, :] = named
 
 
@@ -111,20 +112,19 @@
     return jnp.concatenate(slabs, axis=1)
 
 
+def key_rows(ref, half):
+    wide = ref[ref.shape[0] - 8 :, :].astype(F32)
+    return [wide[side : side + 1, :half] * 256.0 + wide[side + 2 : side + 3, :half] for side in range(2)]
+
+
 def key_row(ref, rows_here):
-    wide = ref[ref.shape[0] - 8 :, :].astype(F32)
-    lines = name_lines(rows_here)
-    kinds = []
-    for kind in range(2):
-        parts = [wide[kind * lines + line : kind * lines + line + 1, :] for line in range(lines)]
-        kinds.append(jnp.concatenate(parts, axis=1)[:, :rows_here])
-    return kinds[0] * 256.0 + kinds[1]
+    return jnp.concatenate(key_rows(ref, rows_here // 2), axis=1)
 
 
 def from_halves(first, second, rows_here):
     half = rows_here // 2
     rows = jnp.concatenate([from_slabs(first, half), from_slabs(second, half)], axis=0)
-    return rows, key_row(first, rows_here)
+    return rows, key_row(second, rows_here)
 
 
 def add_blocks(left, info, blocks, numer, denom):
@@ -187,17 +187,12 @@
     store_sides(*add_blocks(left, info, blocks, numer, denom), refs[2:])
 
 
-def half_of(piece, top, rows_here):
-    rows = from_slabs(piece, rows_here // 2)
-    key = to_column(key_row(piece, rows_here))[top : top + rows_here // 2]
-    return rows, to_row(key), to_row(scale_column(rows))
-
-
-def first_half_kernel(own, other, info, first, mine_in, theirs_in, mine, *theirs):
+def first_half_kernel(own, other, info, first, names, mine_in, theirs_in, mine, *theirs):
     rows_here, wide = mine.shape
     width = wide - 128
     left = left_rows((own, other), rows_here)
-    blocks = [half_of(first, 0, rows_here)]
+    rows = from_slabs(first, rows_here // 2)
+    blocks = [(rows, key_rows(names, rows_here // 2)[0], to_row(scale_column(rows)))]
     numer = jnp.concatenate([ref[:, :width] for ref in (mine_in, theirs_in)], axis=0)
     denom = jnp.concatenate([ref[:, width : width + 1] for ref in (mine_in, theirs_in)], axis=0)
     numer, denom = add_blocks(left, info, blocks, numer, denom)
@@ -217,12 +212,16 @@
     out = refs[-1]
     rows_here, width = out.shape
     theirs = jnp.concatenate([ref[...] for ref in refs[:-1]], axis=0)
-    blocks = [half_of(ref, rows_here // 2, rows_here) for ref in (second, second_other)]
+    half = rows_here // 2
+    pieces = (second, second_other)
+    rows = jnp.concatenate([from_slabs(ref, half) for ref in pieces], axis=0)
+    key = jnp.concatenate([key_rows(ref, half)[1] for ref in pieces], axis=1)
+    blocks = [(rows, key, to_row(scale_column(rows)))]
     parts = theirs[:, width:].astype(F32)
     numer = mine[:, :width] + theirs[:, :width].astype(F32)
     denom = mine[:, width : width + 1] + (parts[:, 0:1] + parts[:, 1:2])
     numer, denom = add_blocks(left_rows((own,), rows_here), info, blocks, numer, denom)
-    out[...] = (numer / denom).astype(BF16)
+    out[...] = (numer * (1.0 / denom)).astype(BF16)
 
 
 def whole_in_vmem(count):
@@ -256,10 +255,10 @@
     )
 
 
-def add_first_half(left, first, before):
+def add_first_half(left, first, names, before):
     rows_here, wide = before[0].shape
     shapes = [((rows_here, wide), F32)] + [((rows_here // PARTS, wide), BF16)] * PARTS
-    return call(first_half_kernel, shapes, [*left, first, *before], {4: 0})
+    return call(first_half_kernel, shapes, [*left, first, names, *before], {5: 0})
 
 
 def folded_ring(size):
@@ -292,13 +291,11 @@
     def other_core(rows):
         return lax.ppermute(rows, "pair", [(0, 1), (1, 0)])
 
-    whole, first, second = call(
+    half_shape = ((slabs * half + 8, 128), BF16)
+    (first,) = call(first_pack_kernel, [half_shape], [embeddings])
+    whole, second = call(
         pack_kernel,
-        [
-            ((slabs * rows_here + 8, 128), BF16),
-            ((slabs * half + 8, 128), BF16),
-            ((slabs * half + 8, 128), BF16),
-        ],
+        [((slabs * rows_here + 8, 128), BF16), half_shape],
         [embeddings, group_of.reshape(line), cluster_id.reshape(line)],
     )
     along_by = [(first, second)]
@@ -314,10 +311,12 @@
         left, across_by[:-1] + along_by[1:-1], (rows_here, width + 128)
     )
     left = (*left, info)
-    near_first, _, mine, theirs = together(across_by[-1][0], along_by[-1][0], mine, theirs)
-    last_first, last_second = along(near_first), across(along_by[-1][1])
+    near_first, _ = together(across_by[-1][0], along_by[-1][0])
+    far_second, mine, theirs = together(along_by[-1][1], mine, theirs)
+    last_first, last_second = along(near_first), across(far_second)
     mine, theirs = add_both(left, [across_by[-1], along_by[-1]], (mine, theirs))
-    mine, *theirs = add_first_half(left, last_first, (mine, theirs))
+    names = along(across_by[-1][1][slabs * half :])
+    mine, *theirs = add_first_half(left, last_first, names, (mine, theirs))
     last_second, *back = together(last_second, *[other_core(part) for part in theirs])
     (out,) = call(
         last_kernel,
@@ -331,7 +330,7 @@
     rows_here, width = embeddings.shape
     devices = lax.axis_size("blk") * lax.axis_size("sub") * lax.axis_size("pair")
     small = devices * rows_here * width * 2 <= GATHER_LIMIT
-    fits = width % 128 == 0 and rows_here % (32 * PARTS) == 0 and rows_here <= 512
+    fits = width % 128 == 0 and rows_here % (32 * PARTS) == 0 and rows_here <= 256
     if small and fits and lax.axis_size("sub") == 2 and lax.axis_size("pair") == 2:
         return by_block(embeddings, group_of, cluster_id)
     return by_group(embeddings, group_of, cluster_id)

time: 39.5 us -> 40.2 us (1.018)
  starting transfers between devices: 21.5 us -> 23.1 us
  waiting for transfers between devices: 9.38 us -> 8.75 us
    ppermute x7 -> x8, starting transfers between devices: 12 us -> 14.7 us  [along(): return lax.ppermute(rows, ('blk', 'pair'), hops)]
    ppermute x7, waiting for transfers between devices: 6.11 us -> 4.03 us  [across(): return lax.ppermute(rows, ('sub', 'pair'), [(0, 3), (1, 2), (2, 1), (3, 0)])]
    ppermute x7 -> x8, waiting for transfers between devices: 1.46 us -> 2.72 us  [along(): return lax.ppermute(rows, ('blk', 'pair'), hops)]
    ppermute x7, starting transfers between devices: 6.41 us -> 5.48 us  [across(): return lax.ppermute(rows, ('sub', 'pair'), [(0, 3), (1, 2), (2, 1), (3, 0)])]
    pallas_call x5 -> x6, Pallas kernels: 6.78 us -> 6.55 us  [call(): pl.pallas_call(kernel, out_shape=[jax.ShapeDtypeStruct(shape, dtype) for...]
  transfers between devices with their start and end apart: 19 -> 20, of which waited for: 13 -> 11; matrix products, arithmetic and copies ran while one was open for 0% -> 0% of each run, Pallas kernels for 13% -> 13%
where the time goes in v14:
time: 40.2 us; the launch traced here: 40.1 us
  starting transfers between devices  23.1 us (57%)
  waiting for transfers between devices  8.75 us (22%)
  Pallas kernels  6.55 us (16%)
  local copies, waits for them, and re-layouts  1.64 us (4%)
    ppermute x8, starting transfers between devices, along(): return lax.ppermute(rows, ('blk', 'pair'), hops)  14.7 us
    pallas_call x6, Pallas kernels, call(): pl.pallas_call(kernel, out_shape=[jax.ShapeDtypeStruct(shape, dtype) for...  6.55 us
    ppermute x7, starting transfers between devices, across(): return lax.ppermute(rows, ('sub', 'pair'), [(0, 3), (1, 2), (2, 1), (3, 0)])  5.48 us
    ppermute x7, waiting for transfers between devices, across(): return lax.ppermute(rows, ('sub', 'pair'), [(0, 3), (1, 2), (2, 1), (3, 0)])  4.03 us
    ppermute x5, starting transfers between devices, other_core(): return lax.ppermute(rows, 'pair', [(0, 1), (1, 0)])  2.92 us
    ppermute x8, waiting for transfers between devices, along(): return lax.ppermute(rows, ('blk', 'pair'), hops)  2.72 us
    ppermute x5, waiting for transfers between devices, other_core(): return lax.ppermute(rows, 'pair', [(0, 1), (1, 0)])  2 us
    unnamed x6, local copies, waits for them, and re-layouts  1.64 us
  transfers between devices with their start and end apart: 20, of which 11 were waited for; matrix products, arithmetic and copies ran while one was open for 0% of the time, Pallas kernels for 13%

profile of v14, /device:TPU:0, one launch (start us, length us, event | category | flops | bytes accessed | tf_op | source)
XLA Modules:
  0.0 40.1 jit_solution(16832745023296265440)
XLA Ops:
  0.0 0.0 copy-start
  0.0 1.0 %copy-done = bf16[192,768]{1,0:T(8,128)(2,1)S(1)} copy-done((bf16[192,768]{1,0:T(8,128)(2,1)S(1)}, bf16[192,768]{1,0:T(8,128)(2,1)}, u32[]{:S(2)}) %copy-start) | copy-done | bytes 294936
  1.0 0.0 copy-start.2
  1.0 2.5 %collective-permute-start.1 = (bf16[584,128]{1,0:T(8,128)(2,1)S(1)}, bf16[584,128]{1,0:T(8,128)(2,1)S(1)}, u32[]{:S(2)}, u32[]{:S(2)}) collective-permute-start(bf16[584,128]{1,0:T(8,128)(2,1)S(1)} %shard_map.38), channel_id=1, source_target_pairs={{8,1},{9,0},{0,5},{1,4},{4,13},{5,12},{12,9},{13,8},{10,3},{11,2},... | collective-permute-start | bytes 448520 | tf_op jit(solution)/shard_map/ppermute | solution.py:286
  3.5 1.8 %collective-permute-start.2 = (bf16[584,128]{1,0:T(8,128)(2,1)S(1)}, bf16[584,128]{1,0:T(8,128)(2,1)S(1)}, u32[]{:S(2)}, u32[]{:S(2)}) collective-permute-start(bf16[584,128]{1,0:T(8,128)(2,1)S(1)} %shard_map.38), channel_id=1, source_target_pairs={{0,3},{1,2},{2,1},{3,0},{4,7},{5,6},{6,5},{7,4},{8,11},{9,10},{10,... | collective-permute-start | bytes 448520 | tf_op jit(solution)/shard_map/ppermute | solution.py:289
  5.3 0.0 copy-start.1
  5.3 0.0 copy-done.2
  5.3 0.7 %copy-done.1 = s32[192,1]{0,1:T(1,128)S(1)} copy-done((s32[192,1]{0,1:T(1,128)S(1)}, s32[192,1]{0,1:T(1,128)}, u32[]{:S(2)}) %copy-start.1) | copy-done | bytes 792
  6.0 0.1 shard_map.37
  6.0 2.1 %collective-permute-start.3 = (bf16[584,128]{1,0:T(8,128)(2,1)S(1)}, bf16[584,128]{1,0:T(8,128)(2,1)S(1)}, u32[]{:S(2)}, u32[]{:S(2)}) collective-permute-start(bf16[584,128]{1,0:T(8,128)(2,1)S(1)} %get-tuple-element.38), channel_id=1, source_target_pairs={{8,1},{9,0},{0,5},{1,4},{4,13},{5,12},{12,9},{13,8},{10,3},{11,2},... | collective-permute-start | bytes 448520 | tf_op jit(solution)/shard_map/ppermute | solution.py:286
  8.1 0.8 %collective-permute-start.4 = (bf16[584,128]{1,0:T(8,128)(2,1)S(1)}, bf16[584,128]{1,0:T(8,128)(2,1)S(1)}, u32[]{:S(2)}, u32[]{:S(2)}) collective-permute-start(bf16[584,128]{1,0:T(8,128)(2,1)S(1)} %get-tuple-element.38), channel_id=1, source_target_pairs={{0,3},{1,2},{2,1},{3,0},{4,7},{5,6},{6,5},{7,4},{8,11},{9,10},{10,... | collective-permute-start | bytes 448520 | tf_op jit(solution)/shard_map/ppermute | solution.py:289
  8.9 0.0 collective-permute-done.1.refs_4_
  8.9 0.0 collective-permute-done.2.refs_0_
  8.9 3.6 %collective-permute-start.5 = (bf16[584,128]{1,0:T(8,128)(2,1)S(1)}, bf16[584,128]{1,0:T(8,128)(2,1)S(1)}, u32[]{:S(2)}, u32[]{:S(2)}) collective-permute-start(bf16[584,128]{1,0:T(8,128)(2,1)S(1)} %collective-permute-done.1.refs_4_), channel_id=1, source_target_pairs={{8,1},{9,0},{0,5},{1,4},{4,13},{5,12},{12,9},{13,8},{10,3},{11,2},... | collective-permute-start | bytes 448520 | tf_op jit(solution)/shard_map/ppermute | solution.py:286
  12.5 0.1 collective-permute-start.6
  12.7 0.5 %collective-permute-done.3.refs_5_ = bf16[584,128]{1,0:T(8,128)(2,1)S(1)} collective-permute-done((bf16[584,128]{1,0:T(8,128)(2,1)S(1)}, bf16[584,128]{1,0:T(8,128)(2,1)S(1)}, u32[]{:S(2)}, u32[]{:S(2)}) %collective-permute-start.3) | collective-permute-done | bytes 149536 | tf_op jit(solution)/shard_map/ppermute | solution.py:286
  13.2 0.3 collective-permute-done.4.refs_1_
  13.5 1.8 %collective-permute-start.7 = (bf16[584,128]{1,0:T(8,128)(2,1)S(1)}, bf16[584,128]{1,0:T(8,128)(2,1)S(1)}, u32[]{:S(2)}, u32[]{:S(2)}) collective-permute-start(bf16[584,128]{1,0:T(8,128)(2,1)S(1)} %collective-permute-done.3.refs_5_), channel_id=1, source_target_pairs={{8,1},{9,0},{0,5},{1,4},{4,13},{5,12},{12,9},{13,8},{10,3},{11,2},... | collective-permute-start | bytes 448520 | tf_op jit(solution)/shard_map/ppermute | solution.py:286
  15.2 0.6 %collective-permute-start.8 = (bf16[584,128]{1,0:T(8,128)(2,1)S(1)}, bf16[584,128]{1,0:T(8,128)(2,1)S(1)}, u32[]{:S(2)}, u32[]{:S(2)}) collective-permute-start(bf16[584,128]{1,0:T(8,128)(2,1)S(1)} %collective-permute-done.3.refs_5_), channel_id=1, source_target_pairs={{0,3},{1,2},{2,1},{3,0},{4,7},{5,6},{6,5},{7,4},{8,11},{9,10},{10,... | collective-permute-start | bytes 448520 | tf_op jit(solution)/shard_map/ppermute | solution.py:289
  15.9 0.9 %collective-permute-start = (bf16[1160,128]{1,0:T(8,128)(2,1)S(1)}, bf16[1160,128]{1,0:T(8,128)(2,1)S(1)}, u32[]{:S(2)}, u32[]{:S(2)}) collective-permute-start(bf16[1160,128]{1,0:T(8,128)(2,1)S(1)} %get-tuple-element.36.own), channel_id=1, source_target_pairs={{0,1},{1,0},{2,3},{3,2},{4,5},{5,4},{6,7},{7,6},{8,9},{9,8},{10,11... | collective-permute-start | bytes 890888 | tf_op jit(solution)/shard_map/ppermute | solution.py:292
  16.8 0.0 collective-permute-done.5.refs_6_
  16.8 1.6 %collective-permute-done.6.refs_2_ = bf16[584,128]{1,0:T(8,128)(2,1)S(1)} collective-permute-done((bf16[584,128]{1,0:T(8,128)(2,1)S(1)}, bf16[584,128]{1,0:T(8,128)(2,1)S(1)}, u32[]{:S(2)}, u32[]{:S(2)}) %collective-permute-start.6) | collective-permute-done | bytes 149536 | tf_op jit(solution)/shard_map/ppermute | solution.py:289
  18.4 1.0 %collective-permute-start.12 = (bf16[584,128]{1,0:T(8,128)(2,1)S(1)}, bf16[584,128]{1,0:T(8,128)(2,1)S(1)}, u32[]{:S(2)}, u32[]{:S(2)}) collective-permute-start(bf16[584,128]{1,0:T(8,128)(2,1)S(1)} %collective-permute-done.5.refs_6_), channel_id=1, source_target_pairs={{8,1},{9,0},{0,5},{1,4},{4,13},{5,12},{12,9},{13,8},{10,3},{11,2},... | collective-permute-start | bytes 448520 | tf_op jit(solution)/shard_map/ppermute | solution.py:286
  19.4 1.0 %collective-permute-start.13 = (bf16[584,128]{1,0:T(8,128)(2,1)S(1)}, bf16[584,128]{1,0:T(8,128)(2,1)S(1)}, u32[]{:S(2)}, u32[]{:S(2)}) collective-permute-start(bf16[584,128]{1,0:T(8,128)(2,1)S(1)} %collective-permute-done.5.refs_6_), channel_id=1, source_target_pairs={{0,3},{1,2},{2,1},{3,0},{4,7},{5,6},{6,5},{7,4},{8,11},{9,10},{10,... | collective-permute-start | bytes 448520 | tf_op jit(solution)/shard_map/ppermute | solution.py:289
  20.4 0.0 collective-permute-done.7.refs_7_
  20.4 1.2 %collective-permute-done.8.refs_3_ = bf16[584,128]{1,0:T(8,128)(2,1)S(1)} collective-permute-done((bf16[584,128]{1,0:T(8,128)(2,1)S(1)}, bf16[584,128]{1,0:T(8,128)(2,1)S(1)}, u32[]{:S(2)}, u32[]{:S(2)}) %collective-permute-start.8) | collective-permute-done | bytes 149536 | tf_op jit(solution)/shard_map/ppermute | solution.py:289
  21.6 0.5 %collective-permute-start.10 = (bf16[584,128]{1,0:T(8,128)(2,1)S(1)}, bf16[584,128]{1,0:T(8,128)(2,1)S(1)}, u32[]{:S(2)}, u32[]{:S(2)}) collective-permute-start(bf16[584,128]{1,0:T(8,128)(2,1)S(1)} %collective-permute-done.7.refs_7_), channel_id=1, source_target_pairs={{0,3},{1,2},{2,1},{3,0},{4,7},{5,6},{6,5},{7,4},{8,11},{9,10},{10,... | collective-permute-start | bytes 448520 | tf_op jit(solution)/shard_map/ppermute | solution.py:289
  22.1 1.5 %collective-permute-start.9 = (bf16[584,128]{1,0:T(8,128)(2,1)S(1)}, bf16[584,128]{1,0:T(8,128)(2,1)S(1)}, u32[]{:S(2)}, u32[]{:S(2)}) collective-permute-start(bf16[584,128]{1,0:T(8,128)(2,1)S(1)} %collective-permute-done.7.refs_7_), channel_id=1, source_target_pairs={{8,1},{9,0},{0,5},{1,4},{4,13},{5,12},{12,9},{13,8},{10,3},{11,2},... | collective-permute-start | bytes 448520 | tf_op jit(solution)/shard_map/ppermute | solution.py:286
  23.6 0.9 %collective-permute-done.12.refs_2_ = bf16[584,128]{1,0:T(8,128)(2,1)S(1)} collective-permute-done((bf16[584,128]{1,0:T(8,128)(2,1)S(1)}, bf16[584,128]{1,0:T(8,128)(2,1)S(1)}, u32[]{:S(2)}, u32[]{:S(2)}) %collective-permute-start.12) | collective-permute-done | bytes 149536 | tf_op jit(solution)/shard_map/ppermute | solution.py:286
  24.5 1.0 %collective-permute-done.13.refs_0_ = bf16[584,128]{1,0:T(8,128)(2,1)S(1)} collective-permute-done((bf16[584,128]{1,0:T(8,128)(2,1)S(1)}, bf16[584,128]{1,0:T(8,128)(2,1)S(1)}, u32[]{:S(2)}, u32[]{:S(2)}) %collective-permute-start.13) | collective-permute-done | bytes 149536 | tf_op jit(solution)/shard_map/ppermute | solution.py:289
  25.5 1.1 %collective-permute-start.14 = (bf16[584,128]{1,0:T(8,128)(2,1)S(1)}, bf16[584,128]{1,0:T(8,128)(2,1)S(1)}, u32[]{:S(2)}, u32[]{:S(2)}) collective-permute-start(bf16[584,128]{1,0:T(8,128)(2,1)S(1)} %collective-permute-done.13.refs_0_), channel_id=1, source_target_pairs={{8,1},{9,0},{0,5},{1,4},{4,13},{5,12},{12,9},{13,8},{10,3},{11,2},... | collective-permute-start | bytes 448520 | tf_op jit(solution)/shard_map/ppermute | solution.py:286
  26.7 0.0 collective-permute-done.other
  26.7 2.7 %shard_map.39 = (f32[192,896]{1,0:T(8,128)S(1)}, f32[192,896]{1,0:T(8,128)S(1)}, f32[384,128]{1,0:T(8,128)S(1)}) custom-call(bf16[1160,128]{1,0:T(8,128)(2,1)S(1)} %get-tuple-element.36.own, bf16[1160,128]{1,0:T(8,128)(2,1)S(1)} %collective-permute-done.other, bf16[584,128]{1,0:T(8,128)(2,1)S(1)} %collective-permute-done.2.refs_0_, ...), custom_call_target="tpu_custom_call" | custom-call | tf_op jit(solution)/shard_map/pallas_call | solution.py:232
  29.4 0.0 collective-permute-done.10.refs_1_
  29.4 0.0 collective-permute-done.9.refs_3_
  29.4 0.6 %collective-permute-start.11 = (bf16[584,128]{1,0:T(8,128)(2,1)S(1)}, bf16[584,128]{1,0:T(8,128)(2,1)S(1)}, u32[]{:S(2)}, u32[]{:S(2)}) collective-permute-start(bf16[584,128]{1,0:T(8,128)(2,1)S(1)} %collective-permute-done.9.refs_3_), channel_id=1, source_target_pairs={{0,3},{1,2},{2,1},{3,0},{4,7},{5,6},{6,5},{7,4},{8,11},{9,10},{10,... | collective-permute-start | bytes 448520 | tf_op jit(solution)/shard_map/ppermute | solution.py:289
  30.0 1.0 %collective-permute-start.15 = (bf16[8,128]{1,0:T(8,128)(2,1)S(1)}, bf16[8,128]{1,0:T(8,128)(2,1)S(1)}, u32[]{:S(2)}, u32[]{:S(2)}) collective-permute-start(bf16[8,128]{1,0:T(8,128)(2,1)S(1)} %slice.3), channel_id=1, source_target_pairs={{8,1},{9,0},{0,5},{1,4},{4,13},{5,12},{12,9},{13,8},{10,3},{11,2},... | collective-permute-start | bytes 6152 | tf_op jit(solution)/shard_map/ppermute | solution.py:286
  31.1 1.6 %shard_map.40 = (f32[192,896]{1,0:T(8,128)S(1)}, f32[192,896]{1,0:T(8,128)S(1)}) custom-call(bf16[1160,128]{1,0:T(8,128)(2,1)S(1)} %get-tuple-element.36.own, bf16[1160,128]{1,0:T(8,128)(2,1)S(1)} %collective-permute-done.other, f32[384,128]{1,0:T(8,128)S(1)} %get-tuple-element.46.info, ...), custom_call_target="tpu_custom_call", output_to_operand_aliasing={{0}: (7, {}), {1}: (8, {})} | custom-call | tf_op jit(solution)/shard_map/pallas_call | solution.py:232
  32.7 1.3 %collective-permute-done.15.names = bf16[8,128]{1,0:T(8,128)(2,1)S(1)} collective-permute-done((bf16[8,128]{1,0:T(8,128)(2,1)S(1)}, bf16[8,128]{1,0:T(8,128)(2,1)S(1)}, u32[]{:S(2)}, u32[]{:S(2)}) %collective-permute-start.15) | collective-permute-done | bytes 2080 | tf_op jit(solution)/shard_map/ppermute | solution.py:286
  34.0 0.0 collective-permute-done.14.first
  34.0 0.8 %shard_map.41 = (f32[192,896]{1,0:T(8,128)S(1)}, bf16[64,896]{1,0:T(8,128)(2,1)S(1)}, bf16[64,896]{1,0:T(8,128)(2,1)S(1)}, bf16[64,896]{1,0:T(8,128)(2,1)S(1)}) custom-call(bf16[1160,128]{1,0:T(8,128)(2,1)S(1)} %get-tuple-element.36.own, bf16[1160,128]{1,0:T(8,128)(2,1)S(1)} %collective-permute-done.other, ...), custom_call_target="tpu_custom_call", output_to_operand_aliasing={{0}: (5, {})} | custom-call | tf_op jit(solution)/shard_map/pallas_call | solution.py:232
  34.8 1.1 %collective-permute-start.16 = (bf16[64,896]{1,0:T(8,128)(2,1)S(1)}, bf16[64,896]{1,0:T(8,128)(2,1)S(1)}, u32[]{:S(2)}, u32[]{:S(2)}) collective-permute-start(bf16[64,896]{1,0:T(8,128)(2,1)S(1)} %get-tuple-element.59), channel_id=1, source_target_pairs={{0,1},{1,0},{2,3},{3,2},{4,5},{5,4},{6,7},{7,6},{8,9},{9,8},{10,11... | collective-permute-start | bytes 344072 | tf_op jit(solution)/shard_map/ppermute | solution.py:292
  35.9 0.1 collective-permute-start.17
  36.0 0.4 %collective-permute-start.18 = (bf16[64,896]{1,0:T(8,128)(2,1)S(1)}, bf16[64,896]{1,0:T(8,128)(2,1)S(1)}, u32[]{:S(2)}, u32[]{:S(2)}) collective-permute-start(bf16[64,896]{1,0:T(8,128)(2,1)S(1)} %get-tuple-element.61), channel_id=1, source_target_pairs={{0,1},{1,0},{2,3},{3,2},{4,5},{5,4},{6,7},{7,6},{8,9},{9,8},{10,11... | collective-permute-start | bytes 344072 | tf_op jit(solution)/shard_map/ppermute | solution.py:292
  36.4 0.0 collective-permute-done.11.second
  36.4 0.5 %collective-permute-done.16.refs_0_ = bf16[64,896]{1,0:T(8,128)(2,1)S(1)} collective-permute-done((bf16[64,896]{1,0:T(8,128)(2,1)S(1)}, bf16[64,896]{1,0:T(8,128)(2,1)S(1)}, u32[]{:S(2)}, u32[]{:S(2)}) %collective-permute-start.16) | collective-permute-done | bytes 114720 | tf_op jit(solution)/shard_map/ppermute | solution.py:292
  36.9 0.4 collective-permute-done.17.refs_1_
  37.2 0.2 collective-permute-done.18.refs_2_
  37.4 0.3 collective-permute-start.19
  37.7 1.0 %collective-permute-done.19.second_other = bf16[584,128]{1,0:T(8,128)(2,1)S(1)} collective-permute-done((bf16[584,128]{1,0:T(8,128)(2,1)S(1)}, bf16[584,128]{1,0:T(8,128)(2,1)S(1)}, u32[]{:S(2)}, u32[]{:S(2)}) %collective-permute-start.19) | collective-permute-done | bytes 149536 | tf_op jit(solution)/shard_map/ppermute | solution.py:292
  38.8 1.3 %shard_map.42 = bf16[192,768]{1,0:T(8,128)(2,1)} custom-call(bf16[1160,128]{1,0:T(8,128)(2,1)S(1)} %get-tuple-element.36.own, f32[384,128]{1,0:T(8,128)S(1)} %get-tuple-element.46.info, bf16[584,128]{1,0:T(8,128)(2,1)S(1)} %collective-permute-done.11.second, bf16[584,128]{1,0:T(8,128)(2,1)S(1)} %collective-permute-done.19.second_other, ...), custom_call_target="tpu_custom_call" | custom-call | tf_op jit(solution)/shard_map/pallas_call | solution.py:232
  (2 shorter events, 0.0 us)
Async XLA Ops:
  0.0 1.0 %copy-start = (bf16[192,768]{1,0:T(8,128)(2,1)S(1)}, bf16[192,768]{1,0:T(8,128)(2,1)}, u32[]{:S(2)}) copy-start(bf16[192,768]{1,0:T(8,128)(2,1)} %rows.3) | copy-start | bytes 884740
  1.0 4.3 %copy-start.2 = (s32[192]{0:T(256)S(1)}, s32[192]{0:T(256)}, u32[]{:S(2)}) copy-start(s32[192]{0:T(256)} %param.5) | copy-start | bytes 2308
  1.0 7.9 %collective-permute-start.1 = (bf16[584,128]{1,0:T(8,128)(2,1)S(1)}, bf16[584,128]{1,0:T(8,128)(2,1)S(1)}, u32[]{:S(2)}, u32[]{:S(2)}) collective-permute-start(bf16[584,128]{1,0:T(8,128)(2,1)S(1)} %shard_map.38), channel_id=1, source_target_pairs={{8,1},{9,0},{0,5},{1,4},{4,13},{5,12},{12,9},{13,8},{10,3},{11,2},... | collective-permute-start | bytes 448520 | tf_op jit(solution)/shard_map/ppermute | solution.py:286
  3.5 5.4 %collective-permute-start.2 = (bf16[584,128]{1,0:T(8,128)(2,1)S(1)}, bf16[584,128]{1,0:T(8,128)(2,1)S(1)}, u32[]{:S(2)}, u32[]{:S(2)}) collective-permute-start(bf16[584,128]{1,0:T(8,128)(2,1)S(1)} %shard_map.38), channel_id=1, source_target_pairs={{0,3},{1,2},{2,1},{3,0},{4,7},{5,6},{6,5},{7,4},{8,11},{9,10},{10,... | collective-permute-start | bytes 448520 | tf_op jit(solution)/shard_map/ppermute | solution.py:289
  5.3 0.7 %copy-start.1 = (s32[192,1]{0,1:T(1,128)S(1)}, s32[192,1]{0,1:T(1,128)}, u32[]{:S(2)}) copy-start(s32[192,1]{0,1:T(1,128)} %param.4) | copy-start | bytes 2308
  6.0 7.1 %collective-permute-start.3 = (bf16[584,128]{1,0:T(8,128)(2,1)S(1)}, bf16[584,128]{1,0:T(8,128)(2,1)S(1)}, u32[]{:S(2)}, u32[]{:S(2)}) collective-permute-start(bf16[584,128]{1,0:T(8,128)(2,1)S(1)} %get-tuple-element.38), channel_id=1, source_target_pairs={{8,1},{9,0},{0,5},{1,4},{4,13},{5,12},{12,9},{13,8},{10,3},{11,2},... | collective-permute-start | bytes 448520 | tf_op jit(solution)/shard_map/ppermute | solution.py:286
  8.1 5.4 %collective-permute-start.4 = (bf16[584,128]{1,0:T(8,128)(2,1)S(1)}, bf16[584,128]{1,0:T(8,128)(2,1)S(1)}, u32[]{:S(2)}, u32[]{:S(2)}) collective-permute-start(bf16[584,128]{1,0:T(8,128)(2,1)S(1)} %get-tuple-element.38), channel_id=1, source_target_pairs={{0,3},{1,2},{2,1},{3,0},{4,7},{5,6},{6,5},{7,4},{8,11},{9,10},{10,... | collective-permute-start | bytes 448520 | tf_op jit(solution)/shard_map/ppermute | solution.py:289
  8.9 7.9 %collective-permute-start.5 = (bf16[584,128]{1,0:T(8,128)(2,1)S(1)}, bf16[584,128]{1,0:T(8,128)(2,1)S(1)}, u32[]{:S(2)}, u32[]{:S(2)}) collective-permute-start(bf16[584,128]{1,0:T(8,128)(2,1)S(1)} %collective-permute-done.1.refs_4_), channel_id=1, source_target_pairs={{8,1},{9,0},{0,5},{1,4},{4,13},{5,12},{12,9},{13,8},{10,3},{11,2},... | collective-permute-start | bytes 448520 | tf_op jit(solution)/shard_map/ppermute | solution.py:286
  12.5 5.9 %collective-permute-start.6 = (bf16[584,128]{1,0:T(8,128)(2,1)S(1)}, bf16[584,128]{1,0:T(8,128)(2,1)S(1)}, u32[]{:S(2)}, u32[]{:S(2)}) collective-permute-start(bf16[584,128]{1,0:T(8,128)(2,1)S(1)} %collective-permute-done.1.refs_4_), channel_id=1, source_target_pairs={{0,3},{1,2},{2,1},{3,0},{4,7},{5,6},{6,5},{7,4},{8,11},{9,10},{10,... | collective-permute-start | bytes 448520 | tf_op jit(solution)/shard_map/ppermute | solution.py:289
  13.5 7.0 %collective-permute-start.7 = (bf16[584,128]{1,0:T(8,128)(2,1)S(1)}, bf16[584,128]{1,0:T(8,128)(2,1)S(1)}, u32[]{:S(2)}, u32[]{:S(2)}) collective-permute-start(bf16[584,128]{1,0:T(8,128)(2,1)S(1)} %collective-permute-done.3.refs_5_), channel_id=1, source_target_pairs={{8,1},{9,0},{0,5},{1,4},{4,13},{5,12},{12,9},{13,8},{10,3},{11,2},... | collective-permute-start | bytes 448520 | tf_op jit(solution)/shard_map/ppermute | solution.py:286
  15.2 6.4 %collective-permute-start.8 = (bf16[584,128]{1,0:T(8,128)(2,1)S(1)}, bf16[584,128]{1,0:T(8,128)(2,1)S(1)}, u32[]{:S(2)}, u32[]{:S(2)}) collective-permute-start(bf16[584,128]{1,0:T(8,128)(2,1)S(1)} %collective-permute-done.3.refs_5_), channel_id=1, source_target_pairs={{0,3},{1,2},{2,1},{3,0},{4,7},{5,6},{6,5},{7,4},{8,11},{9,10},{10,... | collective-permute-start | bytes 448520 | tf_op jit(solution)/shard_map/ppermute | solution.py:289
  15.9 10.8 %collective-permute-start = (bf16[1160,128]{1,0:T(8,128)(2,1)S(1)}, bf16[1160,128]{1,0:T(8,128)(2,1)S(1)}, u32[]{:S(2)}, u32[]{:S(2)}) collective-permute-start(bf16[1160,128]{1,0:T(8,128)(2,1)S(1)} %get-tuple-element.36.own), channel_id=1, source_target_pairs={{0,1},{1,0},{2,3},{3,2},{4,5},{5,4},{6,7},{7,6},{8,9},{9,8},{10,11... | collective-permute-start | bytes 890888 | tf_op jit(solution)/shard_map/ppermute | solution.py:292
  18.4 6.1 %collective-permute-start.12 = (bf16[584,128]{1,0:T(8,128)(2,1)S(1)}, bf16[584,128]{1,0:T(8,128)(2,1)S(1)}, u32[]{:S(2)}, u32[]{:S(2)}) collective-permute-start(bf16[584,128]{1,0:T(8,128)(2,1)S(1)} %collective-permute-done.5.refs_6_), channel_id=1, source_target_pairs={{8,1},{9,0},{0,5},{1,4},{4,13},{5,12},{12,9},{13,8},{10,3},{11,2},... | collective-permute-start | bytes 448520 | tf_op jit(solution)/shard_map/ppermute | solution.py:286
  19.4 6.1 %collective-permute-start.13 = (bf16[584,128]{1,0:T(8,128)(2,1)S(1)}, bf16[584,128]{1,0:T(8,128)(2,1)S(1)}, u32[]{:S(2)}, u32[]{:S(2)}) collective-permute-start(bf16[584,128]{1,0:T(8,128)(2,1)S(1)} %collective-permute-done.5.refs_6_), channel_id=1, source_target_pairs={{0,3},{1,2},{2,1},{3,0},{4,7},{5,6},{6,5},{7,4},{8,11},{9,10},{10,... | collective-permute-start | bytes 448520 | tf_op jit(solution)/shard_map/ppermute | solution.py:289
  21.6 7.8 %collective-permute-start.10 = (bf16[584,128]{1,0:T(8,128)(2,1)S(1)}, bf16[584,128]{1,0:T(8,128)(2,1)S(1)}, u32[]{:S(2)}, u32[]{:S(2)}) collective-permute-start(bf16[584,128]{1,0:T(8,128)(2,1)S(1)} %collective-permute-done.7.refs_7_), channel_id=1, source_target_pairs={{0,3},{1,2},{2,1},{3,0},{4,7},{5,6},{6,5},{7,4},{8,11},{9,10},{10,... | collective-permute-start | bytes 448520 | tf_op jit(solution)/shard_map/ppermute | solution.py:289
  22.1 7.3 %collective-permute-start.9 = (bf16[584,128]{1,0:T(8,128)(2,1)S(1)}, bf16[584,128]{1,0:T(8,128)(2,1)S(1)}, u32[]{:S(2)}, u32[]{:S(2)}) collective-permute-start(bf16[584,128]{1,0:T(8,128)(2,1)S(1)} %collective-permute-done.7.refs_7_), channel_id=1, source_target_pairs={{8,1},{9,0},{0,5},{1,4},{4,13},{5,12},{12,9},{13,8},{10,3},{11,2},... | collective-permute-start | bytes 448520 | tf_op jit(solution)/shard_map/ppermute | solution.py:286
  25.5 8.5 %collective-permute-start.14 = (bf16[584,128]{1,0:T(8,128)(2,1)S(1)}, bf16[584,128]{1,0:T(8,128)(2,1)S(1)}, u32[]{:S(2)}, u32[]{:S(2)}) collective-permute-start(bf16[584,128]{1,0:T(8,128)(2,1)S(1)} %collective-permute-done.13.refs_0_), channel_id=1, source_target_pairs={{8,1},{9,0},{0,5},{1,4},{4,13},{5,12},{12,9},{13,8},{10,3},{11,2},... | collective-permute-start | bytes 448520 | tf_op jit(solution)/shard_map/ppermute | solution.py:286
  29.4 7.0 %collective-permute-start.11 = (bf16[584,128]{1,0:T(8,128)(2,1)S(1)}, bf16[584,128]{1,0:T(8,128)(2,1)S(1)}, u32[]{:S(2)}, u32[]{:S(2)}) collective-permute-start(bf16[584,128]{1,0:T(8,128)(2,1)S(1)} %collective-permute-done.9.refs_3_), channel_id=1, source_target_pairs={{0,3},{1,2},{2,1},{3,0},{4,7},{5,6},{6,5},{7,4},{8,11},{9,10},{10,... | collective-permute-start | bytes 448520 | tf_op jit(solution)/shard_map/ppermute | solution.py:289
  30.0 3.9 %collective-permute-start.15 = (bf16[8,128]{1,0:T(8,128)(2,1)S(1)}, bf16[8,128]{1,0:T(8,128)(2,1)S(1)}, u32[]{:S(2)}, u32[]{:S(2)}) collective-permute-start(bf16[8,128]{1,0:T(8,128)(2,1)S(1)} %slice.3), channel_id=1, source_target_pairs={{8,1},{9,0},{0,5},{1,4},{4,13},{5,12},{12,9},{13,8},{10,3},{11,2},... | collective-permute-start | bytes 6152 | tf_op jit(solution)/shard_map/ppermute | solution.py:286
  34.8 2.1 %collective-permute-start.16 = (bf16[64,896]{1,0:T(8,128)(2,1)S(1)}, bf16[64,896]{1,0:T(8,128)(2,1)S(1)}, u32[]{:S(2)}, u32[]{:S(2)}) collective-permute-start(bf16[64,896]{1,0:T(8,128)(2,1)S(1)} %get-tuple-element.59), channel_id=1, source_target_pairs={{0,1},{1,0},{2,3},{3,2},{4,5},{5,4},{6,7},{7,6},{8,9},{9,8},{10,11... | collective-permute-start | bytes 344072 | tf_op jit(solution)/shard_map/ppermute | solution.py:292
  35.9 1.3 %collective-permute-start.17 = (bf16[64,896]{1,0:T(8,128)(2,1)S(1)}, bf16[64,896]{1,0:T(8,128)(2,1)S(1)}, u32[]{:S(2)}, u32[]{:S(2)}) collective-permute-start(bf16[64,896]{1,0:T(8,128)(2,1)S(1)} %get-tuple-element.60), channel_id=1, source_target_pairs={{0,1},{1,0},{2,3},{3,2},{4,5},{5,4},{6,7},{7,6},{8,9},{9,8},{10,11... | collective-permute-start | bytes 344072 | tf_op jit(solution)/shard_map/ppermute | solution.py:292
  36.0 1.4 %collective-permute-start.18 = (bf16[64,896]{1,0:T(8,128)(2,1)S(1)}, bf16[64,896]{1,0:T(8,128)(2,1)S(1)}, u32[]{:S(2)}, u32[]{:S(2)}) collective-permute-start(bf16[64,896]{1,0:T(8,128)(2,1)S(1)} %get-tuple-element.61), channel_id=1, source_target_pairs={{0,1},{1,0},{2,3},{3,2},{4,5},{5,4},{6,7},{7,6},{8,9},{9,8},{10,11... | collective-permute-start | bytes 344072 | tf_op jit(solution)/shard_map/ppermute | solution.py:292
  37.4 1.4 %collective-permute-start.19 = (bf16[584,128]{1,0:T(8,128)(2,1)S(1)}, bf16[584,128]{1,0:T(8,128)(2,1)S(1)}, u32[]{:S(2)}, u32[]{:S(2)}) collective-permute-start(bf16[584,128]{1,0:T(8,128)(2,1)S(1)} %collective-permute-done.11.second), channel_id=1, source_target_pairs={{0,1},{1,0},{2,3},{3,2},{4,5},{5,4},{6,7},{7,6},{8,9},{9,8},{10,11... | collective-permute-start | bytes 448520 | tf_op jit(solution)/shard_map/ppermute | solution.py:292

commit v15 on v14

--- a/solution.py
+++ b/solution.py
@@ -179,20 +179,12 @@
 
 def both_kernel(n_blocks, own, other, info, *refs):
     refs = list(refs)
-    rows_here, wide = refs[-1].shape
-    left = left_rows((own, other), rows_here)
+    rows_here = refs[2 * n_blocks].shape[0]
     blocks = take_blocks(refs, n_blocks, rows_here)
-    numer = jnp.concatenate([ref[:, : wide - 128] for ref in refs[:2]], axis=0)
-    denom = jnp.concatenate([ref[:, wide - 128 : wide - 127] for ref in refs[:2]], axis=0)
-    store_sides(*add_blocks(left, info, blocks, numer, denom), refs[2:])
-
-
-def first_half_kernel(own, other, info, first, names, mine_in, theirs_in, mine, *theirs):
-    rows_here, wide = mine.shape
+    mine_in, theirs_in, mine, *theirs = refs
+    wide = mine.shape[1]
     width = wide - 128
     left = left_rows((own, other), rows_here)
-    rows = from_slabs(first, rows_here // 2)
-    blocks = [(rows, key_rows(names, rows_here // 2)[0], to_row(scale_column(rows)))]
     numer = jnp.concatenate([ref[:, :width] for ref in (mine_in, theirs_in)], axis=0)
     denom = jnp.concatenate([ref[:, width : width + 1] for ref in (mine_in, theirs_in)], axis=0)
     numer, denom = add_blocks(left, info, blocks, numer, denom)
@@ -208,15 +200,11 @@
         out[:, width:] = pair[top : top + count]
 
 
-def last_kernel(own, info, second, second_other, mine, *refs):
+def last_kernel(own, info, first, second, first_other, second_other, mine, *refs):
     out = refs[-1]
     rows_here, width = out.shape
     theirs = jnp.concatenate([ref[...] for ref in refs[:-1]], axis=0)
-    half = rows_here // 2
-    pieces = (second, second_other)
-    rows = jnp.concatenate([from_slabs(ref, half) for ref in pieces], axis=0)
-    key = jnp.concatenate([key_rows(ref, half)[1] for ref in pieces], axis=1)
-    blocks = [(rows, key, to_row(scale_column(rows)))]
+    blocks = take_blocks([first, second, first_other, second_other], 2, rows_here)
     parts = theirs[:, width:].astype(F32)
     numer = mine[:, :width] + theirs[:, :width].astype(F32)
     denom = mine[:, width : width + 1] + (parts[:, 0:1] + parts[:, 1:2])
@@ -248,17 +236,10 @@
 
 def add_both(left, right, before):
     args = list(left) + [half for block in right for half in block] + list(before)
-    at = len(args) - 2
-    shapes = [(total.shape, F32) for total in before]
-    return call(
-        functools.partial(both_kernel, len(right)), shapes, args, {at: 0, at + 1: 1}
-    )
-
-
-def add_first_half(left, first, names, before):
     rows_here, wide = before[0].shape
     shapes = [((rows_here, wide), F32)] + [((rows_here // PARTS, wide), BF16)] * PARTS
-    return call(first_half_kernel, shapes, [*left, first, names, *before], {5: 0})
+    kernel = functools.partial(both_kernel, len(right))
+    return call(kernel, shapes, args, {len(args) - 2: 0})
 
 
 def folded_ring(size):
@@ -303,25 +284,26 @@
     for s in range(1, n_blk):
         moved = [along(piece) for piece in along_by[-1]]
         swapped = [across(piece) for piece in along_by[-1]]
-        pairs = [together(m, w) for m, w in zip(moved, swapped)]
-        along_by.append(tuple(pair[0] for pair in pairs))
-        across_by.append(tuple(pair[1] for pair in pairs))
+        moved[0], swapped[0] = together(moved[0], swapped[0])
+        moved[1], swapped[1], _ = together(moved[1], swapped[1], moved[0])
+        along_by.append(tuple(moved))
+        across_by.append(tuple(swapped))
     left = (whole, other_core(whole))
-    mine, theirs, info = start_both(
-        left, across_by[:-1] + along_by[1:-1], (rows_here, width + 128)
-    )
+    early = across_by[:-1] + along_by[1:-2]
+    mine, theirs, info = start_both(left, early, (rows_here, width + 128))
     left = (*left, info)
     near_first, _ = together(across_by[-1][0], along_by[-1][0])
-    far_second, mine, theirs = together(along_by[-1][1], mine, theirs)
+    far_second, mine, theirs, _ = together(along_by[-1][1], mine, theirs, near_first)
     last_first, last_second = along(near_first), across(far_second)
-    mine, theirs = add_both(left, [across_by[-1], along_by[-1]], (mine, theirs))
-    names = along(across_by[-1][1][slabs * half :])
-    mine, *theirs = add_first_half(left, last_first, names, (mine, theirs))
+    late = [along_by[-2], across_by[-1], along_by[-1]]
+    mine, *theirs = add_both(left, late, (mine, theirs))
+    last_first, *theirs = together(last_first, *theirs)
     last_second, *back = together(last_second, *[other_core(part) for part in theirs])
+    last = (last_first, last_second)
     (out,) = call(
         last_kernel,
         [((rows_here, width), BF16)],
-        [whole, info, last_second, other_core(last_second), mine, *back],
+        [whole, info, *last, *[other_core(half) for half in last], mine, *back],
     )
     return out
 

time: 40.2 us -> 38.4 us (0.955)
  waiting for transfers between devices: 8.75 us -> 7.68 us
  Pallas kernels: 6.55 us -> 5.71 us
    ppermute x8 -> x7, waiting for transfers between devices: 2.72 us -> 0.56 us  [along(): return lax.ppermute(rows, ('blk', 'pair'), hops)]
    ppermute x7, waiting for transfers between devices: 4.03 us -> 5.84 us  [across(): return lax.ppermute(rows, ('sub', 'pair'), [(0, 3), (1, 2), (2, 1), (3, 0)])]
    ppermute x8 -> x7, starting transfers between devices: 14.7 us -> 15.7 us  [along(): return lax.ppermute(rows, ('blk', 'pair'), hops)]
    pallas_call x6 -> x5, Pallas kernels: 6.55 us -> 5.71 us  [call(): pl.pallas_call(kernel, out_shape=[jax.ShapeDtypeStruct(shape, dtype) for...]
    ppermute x5 -> x6, waiting for transfers between devices: 2 us -> 1.27 us  [other_core(): return lax.ppermute(rows, 'pair', [(0, 1), (1, 0)])]
    ppermute x5 -> x6, starting transfers between devices: 2.92 us -> 2.28 us  [other_core(): return lax.ppermute(rows, 'pair', [(0, 1), (1, 0)])]
  transfers between devices with their start and end apart: 20 -> 20, of which waited for: 11 -> 8; matrix products, arithmetic and copies ran while one was open for 0% -> 0% of each run, Pallas kernels for 13% -> 11%
where the time goes in v15:
time: 38.4 us; the launch traced here: 38.3 us
  starting transfers between devices  23.2 us (60%)
  waiting for transfers between devices  7.68 us (20%)
  Pallas kernels  5.71 us (15%)
  local copies, waits for them, and re-layouts  1.64 us (4%)
    ppermute x7, starting transfers between devices, along(): return lax.ppermute(rows, ('blk', 'pair'), hops)  15.7 us
    ppermute x7, waiting for transfers between devices, across(): return lax.ppermute(rows, ('sub', 'pair'), [(0, 3), (1, 2), (2, 1), (3, 0)])  5.84 us
    pallas_call x5, Pallas kernels, call(): pl.pallas_call(kernel, out_shape=[jax.ShapeDtypeStruct(shape, dtype) for...  5.71 us
    ppermute x7, starting transfers between devices, across(): return lax.ppermute(rows, ('sub', 'pair'), [(0, 3), (1, 2), (2, 1), (3, 0)])  5.17 us
    ppermute x6, starting transfers between devices, other_core(): return lax.ppermute(rows, 'pair', [(0, 1), (1, 0)])  2.28 us
    unnamed x6, local copies, waits for them, and re-layouts  1.64 us
    ppermute x6, waiting for transfers between devices, other_core(): return lax.ppermute(rows, 'pair', [(0, 1), (1, 0)])  1.27 us
  transfers between devices with their start and end apart: 20, of which 8 were waited for; matrix products, arithmetic and copies ran while one was open for 0% of the time, Pallas kernels for 11%

profile of v15, /device:TPU:0, one launch (start us, length us, event | category | flops | bytes accessed | tf_op | source)
XLA Modules:
  0.0 38.3 jit_solution(8923311833733586437)
XLA Ops:
  0.0 0.0 copy-start
  0.0 1.0 %copy-done = bf16[192,768]{1,0:T(8,128)(2,1)S(1)} copy-done((bf16[192,768]{1,0:T(8,128)(2,1)S(1)}, bf16[192,768]{1,0:T(8,128)(2,1)}, u32[]{:S(2)}) %copy-start) | copy-done | bytes 294936
  1.0 0.0 copy-start.2
  1.0 2.5 %collective-permute-start.1 = (bf16[584,128]{1,0:T(8,128)(2,1)S(1)}, bf16[584,128]{1,0:T(8,128)(2,1)S(1)}, u32[]{:S(2)}, u32[]{:S(2)}) collective-permute-start(bf16[584,128]{1,0:T(8,128)(2,1)S(1)} %shard_map.38), channel_id=1, source_target_pairs={{8,1},{9,0},{0,5},{1,4},{4,13},{5,12},{12,9},{13,8},{10,3},{11,2},... | collective-permute-start | bytes 448520 | tf_op jit(solution)/shard_map/ppermute | solution.py:267
  3.5 1.8 %collective-permute-start.2 = (bf16[584,128]{1,0:T(8,128)(2,1)S(1)}, bf16[584,128]{1,0:T(8,128)(2,1)S(1)}, u32[]{:S(2)}, u32[]{:S(2)}) collective-permute-start(bf16[584,128]{1,0:T(8,128)(2,1)S(1)} %shard_map.38), channel_id=1, source_target_pairs={{0,3},{1,2},{2,1},{3,0},{4,7},{5,6},{6,5},{7,4},{8,11},{9,10},{10,... | collective-permute-start | bytes 448520 | tf_op jit(solution)/shard_map/ppermute | solution.py:270
  5.3 0.0 copy-start.1
  5.3 0.0 copy-done.2
  5.3 0.7 %copy-done.1 = s32[192,1]{0,1:T(1,128)S(1)} copy-done((s32[192,1]{0,1:T(1,128)S(1)}, s32[192,1]{0,1:T(1,128)}, u32[]{:S(2)}) %copy-start.1) | copy-done | bytes 792
  6.0 0.1 shard_map.37
  6.0 2.1 %collective-permute-start.3 = (bf16[584,128]{1,0:T(8,128)(2,1)S(1)}, bf16[584,128]{1,0:T(8,128)(2,1)S(1)}, u32[]{:S(2)}, u32[]{:S(2)}) collective-permute-start(bf16[584,128]{1,0:T(8,128)(2,1)S(1)} %get-tuple-element.40), channel_id=1, source_target_pairs={{8,1},{9,0},{0,5},{1,4},{4,13},{5,12},{12,9},{13,8},{10,3},{11,2},... | collective-permute-start | bytes 448520 | tf_op jit(solution)/shard_map/ppermute | solution.py:267
  8.1 0.8 %collective-permute-start.4 = (bf16[584,128]{1,0:T(8,128)(2,1)S(1)}, bf16[584,128]{1,0:T(8,128)(2,1)S(1)}, u32[]{:S(2)}, u32[]{:S(2)}) collective-permute-start(bf16[584,128]{1,0:T(8,128)(2,1)S(1)} %get-tuple-element.40), channel_id=1, source_target_pairs={{0,3},{1,2},{2,1},{3,0},{4,7},{5,6},{6,5},{7,4},{8,11},{9,10},{10,... | collective-permute-start | bytes 448520 | tf_op jit(solution)/shard_map/ppermute | solution.py:270
  8.9 0.0 collective-permute-done.1.refs_4_
  8.9 0.0 collective-permute-done.2.refs_0_
  8.9 3.6 %collective-permute-start.5 = (bf16[584,128]{1,0:T(8,128)(2,1)S(1)}, bf16[584,128]{1,0:T(8,128)(2,1)S(1)}, u32[]{:S(2)}, u32[]{:S(2)}) collective-permute-start(bf16[584,128]{1,0:T(8,128)(2,1)S(1)} %collective-permute-done.1.refs_4_), channel_id=1, source_target_pairs={{8,1},{9,0},{0,5},{1,4},{4,13},{5,12},{12,9},{13,8},{10,3},{11,2},... | collective-permute-start | bytes 448520 | tf_op jit(solution)/shard_map/ppermute | solution.py:267
  12.5 0.1 collective-permute-start.6
  12.7 0.5 %collective-permute-done.3.refs_5_ = bf16[584,128]{1,0:T(8,128)(2,1)S(1)} collective-permute-done((bf16[584,128]{1,0:T(8,128)(2,1)S(1)}, bf16[584,128]{1,0:T(8,128)(2,1)S(1)}, u32[]{:S(2)}, u32[]{:S(2)}) %collective-permute-start.3) | collective-permute-done | bytes 149536 | tf_op jit(solution)/shard_map/ppermute | solution.py:267
  13.2 0.3 collective-permute-done.4.refs_1_
  13.5 1.8 %collective-permute-start.7 = (bf16[584,128]{1,0:T(8,128)(2,1)S(1)}, bf16[584,128]{1,0:T(8,128)(2,1)S(1)}, u32[]{:S(2)}, u32[]{:S(2)}) collective-permute-start(bf16[584,128]{1,0:T(8,128)(2,1)S(1)} %collective-permute-done.3.refs_5_), channel_id=1, source_target_pairs={{8,1},{9,0},{0,5},{1,4},{4,13},{5,12},{12,9},{13,8},{10,3},{11,2},... | collective-permute-start | bytes 448520 | tf_op jit(solution)/shard_map/ppermute | solution.py:267
  15.2 0.6 %collective-permute-start.8 = (bf16[584,128]{1,0:T(8,128)(2,1)S(1)}, bf16[584,128]{1,0:T(8,128)(2,1)S(1)}, u32[]{:S(2)}, u32[]{:S(2)}) collective-permute-start(bf16[584,128]{1,0:T(8,128)(2,1)S(1)} %collective-permute-done.3.refs_5_), channel_id=1, source_target_pairs={{0,3},{1,2},{2,1},{3,0},{4,7},{5,6},{6,5},{7,4},{8,11},{9,10},{10,... | collective-permute-start | bytes 448520 | tf_op jit(solution)/shard_map/ppermute | solution.py:270
  15.9 0.9 %collective-permute-start = (bf16[1160,128]{1,0:T(8,128)(2,1)S(1)}, bf16[1160,128]{1,0:T(8,128)(2,1)S(1)}, u32[]{:S(2)}, u32[]{:S(2)}) collective-permute-start(bf16[1160,128]{1,0:T(8,128)(2,1)S(1)} %get-tuple-element.38.own), channel_id=1, source_target_pairs={{0,1},{1,0},{2,3},{3,2},{4,5},{5,4},{6,7},{7,6},{8,9},{9,8},{10,11... | collective-permute-start | bytes 890888 | tf_op jit(solution)/shard_map/ppermute | solution.py:273
  16.8 0.0 collective-permute-done.5.refs_0_
  16.8 1.6 %collective-permute-done.6.refs_2_ = bf16[584,128]{1,0:T(8,128)(2,1)S(1)} collective-permute-done((bf16[584,128]{1,0:T(8,128)(2,1)S(1)}, bf16[584,128]{1,0:T(8,128)(2,1)S(1)}, u32[]{:S(2)}, u32[]{:S(2)}) %collective-permute-start.6) | collective-permute-done | bytes 149536 | tf_op jit(solution)/shard_map/ppermute | solution.py:270
  18.4 0.0 collective-permute-start.10
  18.4 2.0 %collective-permute-start.9 = (bf16[584,128]{1,0:T(8,128)(2,1)S(1)}, bf16[584,128]{1,0:T(8,128)(2,1)S(1)}, u32[]{:S(2)}, u32[]{:S(2)}) collective-permute-start(bf16[584,128]{1,0:T(8,128)(2,1)S(1)} %collective-permute-done.5.refs_0_), channel_id=1, source_target_pairs={{8,1},{9,0},{0,5},{1,4},{4,13},{5,12},{12,9},{13,8},{10,3},{11,2},... | collective-permute-start | bytes 448520 | tf_op jit(solution)/shard_map/ppermute | solution.py:267
  20.4 0.0 collective-permute-done.7.refs_1_
  20.4 1.2 %collective-permute-done.8.refs_3_ = bf16[584,128]{1,0:T(8,128)(2,1)S(1)} collective-permute-done((bf16[584,128]{1,0:T(8,128)(2,1)S(1)}, bf16[584,128]{1,0:T(8,128)(2,1)S(1)}, u32[]{:S(2)}, u32[]{:S(2)}) %collective-permute-start.8) | collective-permute-done | bytes 149536 | tf_op jit(solution)/shard_map/ppermute | solution.py:270
  21.6 1.5 %collective-permute-start.12 = (bf16[584,128]{1,0:T(8,128)(2,1)S(1)}, bf16[584,128]{1,0:T(8,128)(2,1)S(1)}, u32[]{:S(2)}, u32[]{:S(2)}) collective-permute-start(bf16[584,128]{1,0:T(8,128)(2,1)S(1)} %collective-permute-done.7.refs_1_), channel_id=1, source_target_pairs={{8,1},{9,0},{0,5},{1,4},{4,13},{5,12},{12,9},{13,8},{10,3},{11,2},... | collective-permute-start | bytes 448520 | tf_op jit(solution)/shard_map/ppermute | solution.py:267
  23.1 0.5 %collective-permute-start.13 = (bf16[584,128]{1,0:T(8,128)(2,1)S(1)}, bf16[584,128]{1,0:T(8,128)(2,1)S(1)}, u32[]{:S(2)}, u32[]{:S(2)}) collective-permute-start(bf16[584,128]{1,0:T(8,128)(2,1)S(1)} %collective-permute-done.7.refs_1_), channel_id=1, source_target_pairs={{0,3},{1,2},{2,1},{3,0},{4,7},{5,6},{6,5},{7,4},{8,11},{9,10},{10,... | collective-permute-start | bytes 448520 | tf_op jit(solution)/shard_map/ppermute | solution.py:270
  23.6 1.1 %collective-permute-done.10.refs_2_ = bf16[584,128]{1,0:T(8,128)(2,1)S(1)} collective-permute-done((bf16[584,128]{1,0:T(8,128)(2,1)S(1)}, bf16[584,128]{1,0:T(8,128)(2,1)S(1)}, u32[]{:S(2)}, u32[]{:S(2)}) %collective-permute-start.10) | collective-permute-done | bytes 149536 | tf_op jit(solution)/shard_map/ppermute | solution.py:270
  24.7 0.1 collective-permute-done.9.refs_4_
  24.7 2.2 %collective-permute-start.11 = (bf16[584,128]{1,0:T(8,128)(2,1)S(1)}, bf16[584,128]{1,0:T(8,128)(2,1)S(1)}, u32[]{:S(2)}, u32[]{:S(2)}) collective-permute-start(bf16[584,128]{1,0:T(8,128)(2,1)S(1)} %collective-permute-done.10.refs_2_), channel_id=1, source_target_pairs={{8,1},{9,0},{0,5},{1,4},{4,13},{5,12},{12,9},{13,8},{10,3},{11,2},... | collective-permute-start | bytes 448520 | tf_op jit(solution)/shard_map/ppermute | solution.py:267
  26.9 0.0 collective-permute-done.other
  26.9 2.3 %shard_map.39 = (f32[192,896]{1,0:T(8,128)S(1)}, f32[192,896]{1,0:T(8,128)S(1)}, f32[384,128]{1,0:T(8,128)S(1)}) custom-call(bf16[1160,128]{1,0:T(8,128)(2,1)S(1)} %get-tuple-element.38.own, bf16[1160,128]{1,0:T(8,128)(2,1)S(1)} %collective-permute-done.other, bf16[584,128]{1,0:T(8,128)(2,1)S(1)} %collective-permute-done.2.refs_0_, ...), custom_call_target="tpu_custom_call" | custom-call | tf_op jit(solution)/shard_map/pallas_call | solution.py:220
  29.2 0.0 collective-permute-done.12.refs_5_
  29.2 0.0 collective-permute-done.13.refs_3_
  29.3 1.4 %collective-permute-start.14 = (bf16[584,128]{1,0:T(8,128)(2,1)S(1)}, bf16[584,128]{1,0:T(8,128)(2,1)S(1)}, u32[]{:S(2)}, u32[]{:S(2)}) collective-permute-start(bf16[584,128]{1,0:T(8,128)(2,1)S(1)} %collective-permute-done.12.refs_5_), channel_id=1, source_target_pairs={{0,3},{1,2},{2,1},{3,0},{4,7},{5,6},{6,5},{7,4},{8,11},{9,10},{10,... | collective-permute-start | bytes 448520 | tf_op jit(solution)/shard_map/ppermute | solution.py:270
  30.6 1.7 %shard_map.40 = (f32[192,896]{1,0:T(8,128)S(1)}, bf16[64,896]{1,0:T(8,128)(2,1)S(1)}, bf16[64,896]{1,0:T(8,128)(2,1)S(1)}, bf16[64,896]{1,0:T(8,128)(2,1)S(1)}) custom-call(bf16[1160,128]{1,0:T(8,128)(2,1)S(1)} %get-tuple-element.38.own, bf16[1160,128]{1,0:T(8,128)(2,1)S(1)} %collective-permute-done.other, ...), custom_call_target="tpu_custom_call", output_to_operand_aliasing={{0}: (9, {})} | custom-call | tf_op jit(solution)/shard_map/pallas_call | solution.py:220
  32.4 0.0 collective-permute-done.11.first
  32.4 0.6 %collective-permute-start.15 = (bf16[64,896]{1,0:T(8,128)(2,1)S(1)}, bf16[64,896]{1,0:T(8,128)(2,1)S(1)}, u32[]{:S(2)}, u32[]{:S(2)}) collective-permute-start(bf16[64,896]{1,0:T(8,128)(2,1)S(1)} %get-tuple-element.63), channel_id=1, source_target_pairs={{0,1},{1,0},{2,3},{3,2},{4,5},{5,4},{6,7},{7,6},{8,9},{9,8},{10,11... | collective-permute-start | bytes 344072 | tf_op jit(solution)/shard_map/ppermute | solution.py:273
  32.9 0.1 collective-permute-start.16
  33.0 0.4 %collective-permute-start.17 = (bf16[64,896]{1,0:T(8,128)(2,1)S(1)}, bf16[64,896]{1,0:T(8,128)(2,1)S(1)}, u32[]{:S(2)}, u32[]{:S(2)}) collective-permute-start(bf16[64,896]{1,0:T(8,128)(2,1)S(1)} %get-tuple-element.65), channel_id=1, source_target_pairs={{0,1},{1,0},{2,3},{3,2},{4,5},{5,4},{6,7},{7,6},{8,9},{9,8},{10,11... | collective-permute-start | bytes 344072 | tf_op jit(solution)/shard_map/ppermute | solution.py:273
  33.5 0.1 collective-permute-start.18
  33.5 1.7 %collective-permute-done.14.second = bf16[584,128]{1,0:T(8,128)(2,1)S(1)} collective-permute-done((bf16[584,128]{1,0:T(8,128)(2,1)S(1)}, bf16[584,128]{1,0:T(8,128)(2,1)S(1)}, u32[]{:S(2)}, u32[]{:S(2)}) %collective-permute-start.14) | collective-permute-done | bytes 149536 | tf_op jit(solution)/shard_map/ppermute | solution.py:270
  35.2 0.0 collective-permute-done.15.refs_0_
  35.2 0.0 collective-permute-done.16.refs_1_
  35.2 0.0 collective-permute-done.17.refs_2_
  35.2 0.2 collective-permute-start.19
  35.4 0.0 collective-permute-done.18.first_other
  35.4 1.3 %collective-permute-done.19.second_other = bf16[584,128]{1,0:T(8,128)(2,1)S(1)} collective-permute-done((bf16[584,128]{1,0:T(8,128)(2,1)S(1)}, bf16[584,128]{1,0:T(8,128)(2,1)S(1)}, u32[]{:S(2)}, u32[]{:S(2)}) %collective-permute-start.19) | collective-permute-done | bytes 149536 | tf_op jit(solution)/shard_map/ppermute | solution.py:273
  36.7 1.6 %shard_map.41 = bf16[192,768]{1,0:T(8,128)(2,1)} custom-call(bf16[1160,128]{1,0:T(8,128)(2,1)S(1)} %get-tuple-element.38.own, f32[384,128]{1,0:T(8,128)S(1)} %get-tuple-element.47.info, bf16[584,128]{1,0:T(8,128)(2,1)S(1)} %collective-permute-done.11.first, bf16[584,128]{1,0:T(8,128)(2,1)S(1)} %collective-permute-done.14.second, ...), custom_call_target="tpu_custom_call" | custom-call | tf_op jit(solution)/shard_map/pallas_call | solution.py:220
  (1 shorter events, 0.0 us)
Async XLA Ops:
  0.0 1.0 %copy-start = (bf16[192,768]{1,0:T(8,128)(2,1)S(1)}, bf16[192,768]{1,0:T(8,128)(2,1)}, u32[]{:S(2)}) copy-start(bf16[192,768]{1,0:T(8,128)(2,1)} %rows.3) | copy-start | bytes 884740
  1.0 4.3 %copy-start.2 = (s32[192]{0:T(256)S(1)}, s32[192]{0:T(256)}, u32[]{:S(2)}) copy-start(s32[192]{0:T(256)} %param.5) | copy-start | bytes 2308
  1.0 7.9 %collective-permute-start.1 = (bf16[584,128]{1,0:T(8,128)(2,1)S(1)}, bf16[584,128]{1,0:T(8,128)(2,1)S(1)}, u32[]{:S(2)}, u32[]{:S(2)}) collective-permute-start(bf16[584,128]{1,0:T(8,128)(2,1)S(1)} %shard_map.38), channel_id=1, source_target_pairs={{8,1},{9,0},{0,5},{1,4},{4,13},{5,12},{12,9},{13,8},{10,3},{11,2},... | collective-permute-start | bytes 448520 | tf_op jit(solution)/shard_map/ppermute | solution.py:267
  3.5 5.4 %collective-permute-start.2 = (bf16[584,128]{1,0:T(8,128)(2,1)S(1)}, bf16[584,128]{1,0:T(8,128)(2,1)S(1)}, u32[]{:S(2)}, u32[]{:S(2)}) collective-permute-start(bf16[584,128]{1,0:T(8,128)(2,1)S(1)} %shard_map.38), channel_id=1, source_target_pairs={{0,3},{1,2},{2,1},{3,0},{4,7},{5,6},{6,5},{7,4},{8,11},{9,10},{10,... | collective-permute-start | bytes 448520 | tf_op jit(solution)/shard_map/ppermute | solution.py:270
  5.3 0.7 %copy-start.1 = (s32[192,1]{0,1:T(1,128)S(1)}, s32[192,1]{0,1:T(1,128)}, u32[]{:S(2)}) copy-start(s32[192,1]{0,1:T(1,128)} %param.4) | copy-start | bytes 2308
  6.0 7.1 %collective-permute-start.3 = (bf16[584,128]{1,0:T(8,128)(2,1)S(1)}, bf16[584,128]{1,0:T(8,128)(2,1)S(1)}, u32[]{:S(2)}, u32[]{:S(2)}) collective-permute-start(bf16[584,128]{1,0:T(8,128)(2,1)S(1)} %get-tuple-element.40), channel_id=1, source_target_pairs={{8,1},{9,0},{0,5},{1,4},{4,13},{5,12},{12,9},{13,8},{10,3},{11,2},... | collective-permute-start | bytes 448520 | tf_op jit(solution)/shard_map/ppermute | solution.py:267
  8.1 5.4 %collective-permute-start.4 = (bf16[584,128]{1,0:T(8,128)(2,1)S(1)}, bf16[584,128]{1,0:T(8,128)(2,1)S(1)}, u32[]{:S(2)}, u32[]{:S(2)}) collective-permute-start(bf16[584,128]{1,0:T(8,128)(2,1)S(1)} %get-tuple-element.40), channel_id=1, source_target_pairs={{0,3},{1,2},{2,1},{3,0},{4,7},{5,6},{6,5},{7,4},{8,11},{9,10},{10,... | collective-permute-start | bytes 448520 | tf_op jit(solution)/shard_map/ppermute | solution.py:270
  8.9 7.9 %collective-permute-start.5 = (bf16[584,128]{1,0:T(8,128)(2,1)S(1)}, bf16[584,128]{1,0:T(8,128)(2,1)S(1)}, u32[]{:S(2)}, u32[]{:S(2)}) collective-permute-start(bf16[584,128]{1,0:T(8,128)(2,1)S(1)} %collective-permute-done.1.refs_4_), channel_id=1, source_target_pairs={{8,1},{9,0},{0,5},{1,4},{4,13},{5,12},{12,9},{13,8},{10,3},{11,2},... | collective-permute-start | bytes 448520 | tf_op jit(solution)/shard_map/ppermute | solution.py:267
  12.5 5.9 %collective-permute-start.6 = (bf16[584,128]{1,0:T(8,128)(2,1)S(1)}, bf16[584,128]{1,0:T(8,128)(2,1)S(1)}, u32[]{:S(2)}, u32[]{:S(2)}) collective-permute-start(bf16[584,128]{1,0:T(8,128)(2,1)S(1)} %collective-permute-done.1.refs_4_), channel_id=1, source_target_pairs={{0,3},{1,2},{2,1},{3,0},{4,7},{5,6},{6,5},{7,4},{8,11},{9,10},{10,... | collective-permute-start | bytes 448520 | tf_op jit(solution)/shard_map/ppermute | solution.py:270
  13.5 7.0 %collective-permute-start.7 = (bf16[584,128]{1,0:T(8,128)(2,1)S(1)}, bf16[584,128]{1,0:T(8,128)(2,1)S(1)}, u32[]{:S(2)}, u32[]{:S(2)}) collective-permute-start(bf16[584,128]{1,0:T(8,128)(2,1)S(1)} %collective-permute-done.3.refs_5_), channel_id=1, source_target_pairs={{8,1},{9,0},{0,5},{1,4},{4,13},{5,12},{12,9},{13,8},{10,3},{11,2},... | collective-permute-start | bytes 448520 | tf_op jit(solution)/shard_map/ppermute | solution.py:267
  15.2 6.4 %collective-permute-start.8 = (bf16[584,128]{1,0:T(8,128)(2,1)S(1)}, bf16[584,128]{1,0:T(8,128)(2,1)S(1)}, u32[]{:S(2)}, u32[]{:S(2)}) collective-permute-start(bf16[584,128]{1,0:T(8,128)(2,1)S(1)} %collective-permute-done.3.refs_5_), channel_id=1, source_target_pairs={{0,3},{1,2},{2,1},{3,0},{4,7},{5,6},{6,5},{7,4},{8,11},{9,10},{10,... | collective-permute-start | bytes 448520 | tf_op jit(solution)/shard_map/ppermute | solution.py:270
  15.9 11.0 %collective-permute-start = (bf16[1160,128]{1,0:T(8,128)(2,1)S(1)}, bf16[1160,128]{1,0:T(8,128)(2,1)S(1)}, u32[]{:S(2)}, u32[]{:S(2)}) collective-permute-start(bf16[1160,128]{1,0:T(8,128)(2,1)S(1)} %get-tuple-element.38.own), channel_id=1, source_target_pairs={{0,1},{1,0},{2,3},{3,2},{4,5},{5,4},{6,7},{7,6},{8,9},{9,8},{10,11... | collective-permute-start | bytes 890888 | tf_op jit(solution)/shard_map/ppermute | solution.py:273
  18.4 6.3 %collective-permute-start.10 = (bf16[584,128]{1,0:T(8,128)(2,1)S(1)}, bf16[584,128]{1,0:T(8,128)(2,1)S(1)}, u32[]{:S(2)}, u32[]{:S(2)}) collective-permute-start(bf16[584,128]{1,0:T(8,128)(2,1)S(1)} %collective-permute-done.5.refs_0_), channel_id=1, source_target_pairs={{0,3},{1,2},{2,1},{3,0},{4,7},{5,6},{6,5},{7,4},{8,11},{9,10},{10,... | collective-permute-start | bytes 448520 | tf_op jit(solution)/shard_map/ppermute | solution.py:270
  18.4 6.3 %collective-permute-start.9 = (bf16[584,128]{1,0:T(8,128)(2,1)S(1)}, bf16[584,128]{1,0:T(8,128)(2,1)S(1)}, u32[]{:S(2)}, u32[]{:S(2)}) collective-permute-start(bf16[584,128]{1,0:T(8,128)(2,1)S(1)} %collective-permute-done.5.refs_0_), channel_id=1, source_target_pairs={{8,1},{9,0},{0,5},{1,4},{4,13},{5,12},{12,9},{13,8},{10,3},{11,2},... | collective-permute-start | bytes 448520 | tf_op jit(solution)/shard_map/ppermute | solution.py:267
  21.6 7.6 %collective-permute-start.12 = (bf16[584,128]{1,0:T(8,128)(2,1)S(1)}, bf16[584,128]{1,0:T(8,128)(2,1)S(1)}, u32[]{:S(2)}, u32[]{:S(2)}) collective-permute-start(bf16[584,128]{1,0:T(8,128)(2,1)S(1)} %collective-permute-done.7.refs_1_), channel_id=1, source_target_pairs={{8,1},{9,0},{0,5},{1,4},{4,13},{5,12},{12,9},{13,8},{10,3},{11,2},... | collective-permute-start | bytes 448520 | tf_op jit(solution)/shard_map/ppermute | solution.py:267
  23.1 6.1 %collective-permute-start.13 = (bf16[584,128]{1,0:T(8,128)(2,1)S(1)}, bf16[584,128]{1,0:T(8,128)(2,1)S(1)}, u32[]{:S(2)}, u32[]{:S(2)}) collective-permute-start(bf16[584,128]{1,0:T(8,128)(2,1)S(1)} %collective-permute-done.7.refs_1_), channel_id=1, source_target_pairs={{0,3},{1,2},{2,1},{3,0},{4,7},{5,6},{6,5},{7,4},{8,11},{9,10},{10,... | collective-permute-start | bytes 448520 | tf_op jit(solution)/shard_map/ppermute | solution.py:270
  24.7 7.7 %collective-permute-start.11 = (bf16[584,128]{1,0:T(8,128)(2,1)S(1)}, bf16[584,128]{1,0:T(8,128)(2,1)S(1)}, u32[]{:S(2)}, u32[]{:S(2)}) collective-permute-start(bf16[584,128]{1,0:T(8,128)(2,1)S(1)} %collective-permute-done.10.refs_2_), channel_id=1, source_target_pairs={{8,1},{9,0},{0,5},{1,4},{4,13},{5,12},{12,9},{13,8},{10,3},{11,2},... | collective-permute-start | bytes 448520 | tf_op jit(solution)/shard_map/ppermute | solution.py:267
  29.3 5.9 %collective-permute-start.14 = (bf16[584,128]{1,0:T(8,128)(2,1)S(1)}, bf16[584,128]{1,0:T(8,128)(2,1)S(1)}, u32[]{:S(2)}, u32[]{:S(2)}) collective-permute-start(bf16[584,128]{1,0:T(8,128)(2,1)S(1)} %collective-permute-done.12.refs_5_), channel_id=1, source_target_pairs={{0,3},{1,2},{2,1},{3,0},{4,7},{5,6},{6,5},{7,4},{8,11},{9,10},{10,... | collective-permute-start | bytes 448520 | tf_op jit(solution)/shard_map/ppermute | solution.py:270
  32.4 2.8 %collective-permute-start.15 = (bf16[64,896]{1,0:T(8,128)(2,1)S(1)}, bf16[64,896]{1,0:T(8,128)(2,1)S(1)}, u32[]{:S(2)}, u32[]{:S(2)}) collective-permute-start(bf16[64,896]{1,0:T(8,128)(2,1)S(1)} %get-tuple-element.63), channel_id=1, source_target_pairs={{0,1},{1,0},{2,3},{3,2},{4,5},{5,4},{6,7},{7,6},{8,9},{9,8},{10,11... | collective-permute-start | bytes 344072 | tf_op jit(solution)/shard_map/ppermute | solution.py:273
  32.9 2.3 %collective-permute-start.16 = (bf16[64,896]{1,0:T(8,128)(2,1)S(1)}, bf16[64,896]{1,0:T(8,128)(2,1)S(1)}, u32[]{:S(2)}, u32[]{:S(2)}) collective-permute-start(bf16[64,896]{1,0:T(8,128)(2,1)S(1)} %get-tuple-element.64), channel_id=1, source_target_pairs={{0,1},{1,0},{2,3},{3,2},{4,5},{5,4},{6,7},{7,6},{8,9},{9,8},{10,11... | collective-permute-start | bytes 344072 | tf_op jit(solution)/shard_map/ppermute | solution.py:273
  33.0 2.2 %collective-permute-start.17 = (bf16[64,896]{1,0:T(8,128)(2,1)S(1)}, bf16[64,896]{1,0:T(8,128)(2,1)S(1)}, u32[]{:S(2)}, u32[]{:S(2)}) collective-permute-start(bf16[64,896]{1,0:T(8,128)(2,1)S(1)} %get-tuple-element.65), channel_id=1, source_target_pairs={{0,1},{1,0},{2,3},{3,2},{4,5},{5,4},{6,7},{7,6},{8,9},{9,8},{10,11... | collective-permute-start | bytes 344072 | tf_op jit(solution)/shard_map/ppermute | solution.py:273
  33.5 2.0 %collective-permute-start.18 = (bf16[584,128]{1,0:T(8,128)(2,1)S(1)}, bf16[584,128]{1,0:T(8,128)(2,1)S(1)}, u32[]{:S(2)}, u32[]{:S(2)}) collective-permute-start(bf16[584,128]{1,0:T(8,128)(2,1)S(1)} %collective-permute-done.11.first), channel_id=1, source_target_pairs={{0,1},{1,0},{2,3},{3,2},{4,5},{5,4},{6,7},{7,6},{8,9},{9,8},{10,11... | collective-permute-start | bytes 448520 | tf_op jit(solution)/shard_map/ppermute | solution.py:273
  35.2 1.4 %collective-permute-start.19 = (bf16[584,128]{1,0:T(8,128)(2,1)S(1)}, bf16[584,128]{1,0:T(8,128)(2,1)S(1)}, u32[]{:S(2)}, u32[]{:S(2)}) collective-permute-start(bf16[584,128]{1,0:T(8,128)(2,1)S(1)} %collective-permute-done.14.second), channel_id=1, source_target_pairs={{0,1},{1,0},{2,3},{3,2},{4,5},{5,4},{6,7},{7,6},{8,9},{9,8},{10,11... | collective-permute-start | bytes 448520 | tf_op jit(solution)/shard_map/ppermute | solution.py:273

commit v16 on v15

--- a/solution.py
+++ b/solution.py
@@ -292,8 +292,8 @@
     early = across_by[:-1] + along_by[1:-2]
     mine, theirs, info = start_both(left, early, (rows_here, width + 128))
     left = (*left, info)
-    near_first, _ = together(across_by[-1][0], along_by[-1][0])
-    far_second, mine, theirs, _ = together(along_by[-1][1], mine, theirs, near_first)
+    near_first, _, mine, theirs = together(across_by[-1][0], along_by[-1][0], mine, theirs)
+    far_second, _ = together(along_by[-1][1], near_first)
     last_first, last_second = along(near_first), across(far_second)
     late = [along_by[-2], across_by[-1], along_by[-1]]
     mine, *theirs = add_both(left, late, (mine, theirs))

time: 38.4 us -> 38 us (0.990)
  starting transfers between devices: 23.2 us -> 21.5 us
  waiting for transfers between devices: 7.68 us -> 8.92 us
    ppermute x7, waiting for transfers between devices: 0.56 us -> 6.94 us  [along(): return lax.ppermute(rows, ('blk', 'pair'), hops)]
    ppermute x7, waiting for transfers between devices: 5.84 us -> 0.78 us  [across(): return lax.ppermute(rows, ('sub', 'pair'), [(0, 3), (1, 2), (2, 1), (3, 0)])]
    ppermute x7, starting transfers between devices: 15.7 us -> 12.8 us  [along(): return lax.ppermute(rows, ('blk', 'pair'), hops)]
    ppermute x7, starting transfers between devices: 5.17 us -> 7.35 us  [across(): return lax.ppermute(rows, ('sub', 'pair'), [(0, 3), (1, 2), (2, 1), (3, 0)])]
    ppermute x6, starting transfers between devices: 2.28 us -> 1.37 us  [other_core(): return lax.ppermute(rows, 'pair', [(0, 1), (1, 0)])]
  transfers between devices with their start and end apart: 20 -> 20, of which waited for: 8 -> 10; matrix products, arithmetic and copies ran while one was open for 0% -> 0% of each run, Pallas kernels for 11% -> 11%
where the time goes in v16:
time: 38 us; the launch traced here: 37.8 us
  starting transfers between devices  21.5 us (57%)
  waiting for transfers between devices  8.92 us (23%)
  Pallas kernels  5.72 us (15%)
  local copies, waits for them, and re-layouts  1.64 us (4%)
    ppermute x7, starting transfers between devices, along(): return lax.ppermute(rows, ('blk', 'pair'), hops)  12.8 us
    ppermute x7, starting transfers between devices, across(): return lax.ppermute(rows, ('sub', 'pair'), [(0, 3), (1, 2), (2, 1), (3, 0)])  7.35 us
    ppermute x7, waiting for transfers between devices, along(): return lax.ppermute(rows, ('blk', 'pair'), hops)  6.94 us
    pallas_call x5, Pallas kernels, call(): pl.pallas_call(kernel, out_shape=[jax.ShapeDtypeStruct(shape, dtype) for...  5.72 us
    unnamed x6, local copies, waits for them, and re-layouts  1.64 us
    ppermute x6, starting transfers between devices, other_core(): return lax.ppermute(rows, 'pair', [(0, 1), (1, 0)])  1.37 us
    ppermute x6, waiting for transfers between devices, other_core(): return lax.ppermute(rows, 'pair', [(0, 1), (1, 0)])  1.19 us
    ppermute x7, waiting for transfers between devices, across(): return lax.ppermute(rows, ('sub', 'pair'), [(0, 3), (1, 2), (2, 1), (3, 0)])  0.78 us
  transfers between devices with their start and end apart: 20, of which 10 were waited for; matrix products, arithmetic and copies ran while one was open for 0% of the time, Pallas kernels for 11%

profile of v16, /device:TPU:0, one launch (start us, length us, event | category | flops | bytes accessed | tf_op | source)
XLA Modules:
  0.0 37.8 jit_solution(2690237814313538030)
XLA Ops:
  0.0 0.0 copy-start
  0.0 1.0 %copy-done = bf16[192,768]{1,0:T(8,128)(2,1)S(1)} copy-done((bf16[192,768]{1,0:T(8,128)(2,1)S(1)}, bf16[192,768]{1,0:T(8,128)(2,1)}, u32[]{:S(2)}) %copy-start) | copy-done | bytes 294936
  1.0 0.0 copy-start.2
  1.0 2.4 %collective-permute-start.2 = (bf16[584,128]{1,0:T(8,128)(2,1)S(1)}, bf16[584,128]{1,0:T(8,128)(2,1)S(1)}, u32[]{:S(2)}, u32[]{:S(2)}) collective-permute-start(bf16[584,128]{1,0:T(8,128)(2,1)S(1)} %shard_map.38), channel_id=1, source_target_pairs={{0,3},{1,2},{2,1},{3,0},{4,7},{5,6},{6,5},{7,4},{8,11},{9,10},{10,... | collective-permute-start | bytes 448520 | tf_op jit(solution)/shard_map/ppermute | solution.py:270
  3.4 1.9 %collective-permute-start.1 = (bf16[584,128]{1,0:T(8,128)(2,1)S(1)}, bf16[584,128]{1,0:T(8,128)(2,1)S(1)}, u32[]{:S(2)}, u32[]{:S(2)}) collective-permute-start(bf16[584,128]{1,0:T(8,128)(2,1)S(1)} %shard_map.38), channel_id=1, source_target_pairs={{8,1},{9,0},{0,5},{1,4},{4,13},{5,12},{12,9},{13,8},{10,3},{11,2},... | collective-permute-start | bytes 448520 | tf_op jit(solution)/shard_map/ppermute | solution.py:267
  5.3 0.0 copy-start.1
  5.3 0.0 copy-done.2
  5.3 0.7 %copy-done.1 = s32[192,1]{0,1:T(1,128)S(1)} copy-done((s32[192,1]{0,1:T(1,128)S(1)}, s32[192,1]{0,1:T(1,128)}, u32[]{:S(2)}) %copy-start.1) | copy-done | bytes 792
  6.0 0.1 shard_map.37
  6.1 0.1 collective-permute-start.4
  6.2 2.8 %collective-permute-start.3 = (bf16[584,128]{1,0:T(8,128)(2,1)S(1)}, bf16[584,128]{1,0:T(8,128)(2,1)S(1)}, u32[]{:S(2)}, u32[]{:S(2)}) collective-permute-start(bf16[584,128]{1,0:T(8,128)(2,1)S(1)} %get-tuple-element.40), channel_id=1, source_target_pairs={{8,1},{9,0},{0,5},{1,4},{4,13},{5,12},{12,9},{13,8},{10,3},{11,2},... | collective-permute-start | bytes 448520 | tf_op jit(solution)/shard_map/ppermute | solution.py:267
  9.0 0.0 collective-permute-done.2.refs_0_
  9.0 1.2 %collective-permute-done.1.refs_4_ = bf16[584,128]{1,0:T(8,128)(2,1)S(1)} collective-permute-done((bf16[584,128]{1,0:T(8,128)(2,1)S(1)}, bf16[584,128]{1,0:T(8,128)(2,1)S(1)}, u32[]{:S(2)}, u32[]{:S(2)}) %collective-permute-start.1) | collective-permute-done | bytes 149536 | tf_op jit(solution)/shard_map/ppermute | solution.py:267
  10.2 0.7 %collective-permute-start.6 = (bf16[584,128]{1,0:T(8,128)(2,1)S(1)}, bf16[584,128]{1,0:T(8,128)(2,1)S(1)}, u32[]{:S(2)}, u32[]{:S(2)}) collective-permute-start(bf16[584,128]{1,0:T(8,128)(2,1)S(1)} %collective-permute-done.1.refs_4_), channel_id=1, source_target_pairs={{0,3},{1,2},{2,1},{3,0},{4,7},{5,6},{6,5},{7,4},{8,11},{9,10},{10,... | collective-permute-start | bytes 448520 | tf_op jit(solution)/shard_map/ppermute | solution.py:270
  10.9 1.4 %collective-permute-start.5 = (bf16[584,128]{1,0:T(8,128)(2,1)S(1)}, bf16[584,128]{1,0:T(8,128)(2,1)S(1)}, u32[]{:S(2)}, u32[]{:S(2)}) collective-permute-start(bf16[584,128]{1,0:T(8,128)(2,1)S(1)} %collective-permute-done.1.refs_4_), channel_id=1, source_target_pairs={{8,1},{9,0},{0,5},{1,4},{4,13},{5,12},{12,9},{13,8},{10,3},{11,2},... | collective-permute-start | bytes 448520 | tf_op jit(solution)/shard_map/ppermute | solution.py:267
  12.3 0.0 collective-permute-start
  12.3 0.0 collective-permute-done.4.refs_1_
  12.3 1.1 %collective-permute-done.3.refs_5_ = bf16[584,128]{1,0:T(8,128)(2,1)S(1)} collective-permute-done((bf16[584,128]{1,0:T(8,128)(2,1)S(1)}, bf16[584,128]{1,0:T(8,128)(2,1)S(1)}, u32[]{:S(2)}, u32[]{:S(2)}) %collective-permute-start.3) | collective-permute-done | bytes 149536 | tf_op jit(solution)/shard_map/ppermute | solution.py:267
  13.4 0.7 %collective-permute-start.8 = (bf16[584,128]{1,0:T(8,128)(2,1)S(1)}, bf16[584,128]{1,0:T(8,128)(2,1)S(1)}, u32[]{:S(2)}, u32[]{:S(2)}) collective-permute-start(bf16[584,128]{1,0:T(8,128)(2,1)S(1)} %collective-permute-done.3.refs_5_), channel_id=1, source_target_pairs={{0,3},{1,2},{2,1},{3,0},{4,7},{5,6},{6,5},{7,4},{8,11},{9,10},{10,... | collective-permute-start | bytes 448520 | tf_op jit(solution)/shard_map/ppermute | solution.py:270
  14.1 3.0 %collective-permute-start.7 = (bf16[584,128]{1,0:T(8,128)(2,1)S(1)}, bf16[584,128]{1,0:T(8,128)(2,1)S(1)}, u32[]{:S(2)}, u32[]{:S(2)}) collective-permute-start(bf16[584,128]{1,0:T(8,128)(2,1)S(1)} %collective-permute-done.3.refs_5_), channel_id=1, source_target_pairs={{8,1},{9,0},{0,5},{1,4},{4,13},{5,12},{12,9},{13,8},{10,3},{11,2},... | collective-permute-start | bytes 448520 | tf_op jit(solution)/shard_map/ppermute | solution.py:267
  17.1 0.0 collective-permute-done.6.refs_2_
  17.1 0.2 collective-permute-done.5.refs_0_
  17.3 1.5 %collective-permute-start.10 = (bf16[584,128]{1,0:T(8,128)(2,1)S(1)}, bf16[584,128]{1,0:T(8,128)(2,1)S(1)}, u32[]{:S(2)}, u32[]{:S(2)}) collective-permute-start(bf16[584,128]{1,0:T(8,128)(2,1)S(1)} %collective-permute-done.5.refs_0_), channel_id=1, source_target_pairs={{0,3},{1,2},{2,1},{3,0},{4,7},{5,6},{6,5},{7,4},{8,11},{9,10},{10,... | collective-permute-start | bytes 448520 | tf_op jit(solution)/shard_map/ppermute | solution.py:270
  18.8 0.2 collective-permute-start.9
  19.0 0.1 collective-permute-done.8.refs_3_
  19.0 2.3 %collective-permute-done.7.refs_1_ = bf16[584,128]{1,0:T(8,128)(2,1)S(1)} collective-permute-done((bf16[584,128]{1,0:T(8,128)(2,1)S(1)}, bf16[584,128]{1,0:T(8,128)(2,1)S(1)}, u32[]{:S(2)}, u32[]{:S(2)}) %collective-permute-start.7) | collective-permute-done | bytes 149536 | tf_op jit(solution)/shard_map/ppermute | solution.py:267
  21.3 1.1 %collective-permute-start.13 = (bf16[584,128]{1,0:T(8,128)(2,1)S(1)}, bf16[584,128]{1,0:T(8,128)(2,1)S(1)}, u32[]{:S(2)}, u32[]{:S(2)}) collective-permute-start(bf16[584,128]{1,0:T(8,128)(2,1)S(1)} %collective-permute-done.7.refs_1_), channel_id=1, source_target_pairs={{0,3},{1,2},{2,1},{3,0},{4,7},{5,6},{6,5},{7,4},{8,11},{9,10},{10,... | collective-permute-start | bytes 448520 | tf_op jit(solution)/shard_map/ppermute | solution.py:270
  22.4 1.6 %collective-permute-start.12 = (bf16[584,128]{1,0:T(8,128)(2,1)S(1)}, bf16[584,128]{1,0:T(8,128)(2,1)S(1)}, u32[]{:S(2)}, u32[]{:S(2)}) collective-permute-start(bf16[584,128]{1,0:T(8,128)(2,1)S(1)} %collective-permute-done.7.refs_1_), channel_id=1, source_target_pairs={{8,1},{9,0},{0,5},{1,4},{4,13},{5,12},{12,9},{13,8},{10,3},{11,2},... | collective-permute-start | bytes 448520 | tf_op jit(solution)/shard_map/ppermute | solution.py:267
  24.1 0.0 collective-permute-done.other
  24.1 2.3 %shard_map.39 = (f32[192,896]{1,0:T(8,128)S(1)}, f32[192,896]{1,0:T(8,128)S(1)}, f32[384,128]{1,0:T(8,128)S(1)}) custom-call(bf16[1160,128]{1,0:T(8,128)(2,1)S(1)} %get-tuple-element.38.own, bf16[1160,128]{1,0:T(8,128)(2,1)S(1)} %collective-permute-done.other, bf16[584,128]{1,0:T(8,128)(2,1)S(1)} %collective-permute-done.2.refs_0_, ...), custom_call_target="tpu_custom_call" | custom-call | tf_op jit(solution)/shard_map/pallas_call | solution.py:220
  26.4 0.0 collective-permute-done.10.refs_2_
  26.4 0.0 collective-permute-done.9.refs_4_
  26.4 2.0 %collective-permute-start.11 = (bf16[584,128]{1,0:T(8,128)(2,1)S(1)}, bf16[584,128]{1,0:T(8,128)(2,1)S(1)}, u32[]{:S(2)}, u32[]{:S(2)}) collective-permute-start(bf16[584,128]{1,0:T(8,128)(2,1)S(1)} %collective-permute-done.10.refs_2_), channel_id=1, source_target_pairs={{8,1},{9,0},{0,5},{1,4},{4,13},{5,12},{12,9},{13,8},{10,3},{11,2},... | collective-permute-start | bytes 448520 | tf_op jit(solution)/shard_map/ppermute | solution.py:267
  28.4 0.0 collective-permute-done.13.refs_3_
  28.4 0.6 %collective-permute-done.12.refs_5_ = bf16[584,128]{1,0:T(8,128)(2,1)S(1)} collective-permute-done((bf16[584,128]{1,0:T(8,128)(2,1)S(1)}, bf16[584,128]{1,0:T(8,128)(2,1)S(1)}, u32[]{:S(2)}, u32[]{:S(2)}) %collective-permute-start.12) | collective-permute-done | bytes 149536 | tf_op jit(solution)/shard_map/ppermute | solution.py:267
  29.0 0.7 %collective-permute-start.14 = (bf16[584,128]{1,0:T(8,128)(2,1)S(1)}, bf16[584,128]{1,0:T(8,128)(2,1)S(1)}, u32[]{:S(2)}, u32[]{:S(2)}) collective-permute-start(bf16[584,128]{1,0:T(8,128)(2,1)S(1)} %collective-permute-done.12.refs_5_), channel_id=1, source_target_pairs={{0,3},{1,2},{2,1},{3,0},{4,7},{5,6},{6,5},{7,4},{8,11},{9,10},{10,... | collective-permute-start | bytes 448520 | tf_op jit(solution)/shard_map/ppermute | solution.py:270
  29.7 1.7 %shard_map.40 = (f32[192,896]{1,0:T(8,128)S(1)}, bf16[64,896]{1,0:T(8,128)(2,1)S(1)}, bf16[64,896]{1,0:T(8,128)(2,1)S(1)}, bf16[64,896]{1,0:T(8,128)(2,1)S(1)}) custom-call(bf16[1160,128]{1,0:T(8,128)(2,1)S(1)} %get-tuple-element.38.own, bf16[1160,128]{1,0:T(8,128)(2,1)S(1)} %collective-permute-done.other, ...), custom_call_target="tpu_custom_call", output_to_operand_aliasing={{0}: (9, {})} | custom-call | tf_op jit(solution)/shard_map/pallas_call | solution.py:220
  31.5 1.5 %collective-permute-done.11.first = bf16[584,128]{1,0:T(8,128)(2,1)S(1)} collective-permute-done((bf16[584,128]{1,0:T(8,128)(2,1)S(1)}, bf16[584,128]{1,0:T(8,128)(2,1)S(1)}, u32[]{:S(2)}, u32[]{:S(2)}) %collective-permute-start.11) | collective-permute-done | bytes 149536 | tf_op jit(solution)/shard_map/ppermute | solution.py:267
  33.0 0.4 %collective-permute-start.15 = (bf16[64,896]{1,0:T(8,128)(2,1)S(1)}, bf16[64,896]{1,0:T(8,128)(2,1)S(1)}, u32[]{:S(2)}, u32[]{:S(2)}) collective-permute-start(bf16[64,896]{1,0:T(8,128)(2,1)S(1)} %get-tuple-element.63), channel_id=1, source_target_pairs={{0,1},{1,0},{2,3},{3,2},{4,5},{5,4},{6,7},{7,6},{8,9},{9,8},{10,11... | collective-permute-start | bytes 344072 | tf_op jit(solution)/shard_map/ppermute | solution.py:273
  33.4 0.1 collective-permute-start.16
  33.5 0.4 %collective-permute-start.17 = (bf16[64,896]{1,0:T(8,128)(2,1)S(1)}, bf16[64,896]{1,0:T(8,128)(2,1)S(1)}, u32[]{:S(2)}, u32[]{:S(2)}) collective-permute-start(bf16[64,896]{1,0:T(8,128)(2,1)S(1)} %get-tuple-element.65), channel_id=1, source_target_pairs={{0,1},{1,0},{2,3},{3,2},{4,5},{5,4},{6,7},{7,6},{8,9},{9,8},{10,11... | collective-permute-start | bytes 344072 | tf_op jit(solution)/shard_map/ppermute | solution.py:273
  33.9 0.1 collective-permute-start.18
  34.0 0.7 %collective-permute-done.14.second = bf16[584,128]{1,0:T(8,128)(2,1)S(1)} collective-permute-done((bf16[584,128]{1,0:T(8,128)(2,1)S(1)}, bf16[584,128]{1,0:T(8,128)(2,1)S(1)}, u32[]{:S(2)}, u32[]{:S(2)}) %collective-permute-start.14) | collective-permute-done | bytes 149536 | tf_op jit(solution)/shard_map/ppermute | solution.py:270
  34.7 0.0 collective-permute-done.15.refs_0_
  34.7 0.0 collective-permute-done.16.refs_1_
  34.7 0.2 collective-permute-done.17.refs_2_
  34.9 0.3 collective-permute-start.19
  35.2 0.0 collective-permute-done.18.first_other
  35.3 1.0 %collective-permute-done.19.second_other = bf16[584,128]{1,0:T(8,128)(2,1)S(1)} collective-permute-done((bf16[584,128]{1,0:T(8,128)(2,1)S(1)}, bf16[584,128]{1,0:T(8,128)(2,1)S(1)}, u32[]{:S(2)}, u32[]{:S(2)}) %collective-permute-start.19) | collective-permute-done | bytes 149536 | tf_op jit(solution)/shard_map/ppermute | solution.py:273
  36.3 1.6 %shard_map.41 = bf16[192,768]{1,0:T(8,128)(2,1)} custom-call(bf16[1160,128]{1,0:T(8,128)(2,1)S(1)} %get-tuple-element.38.own, f32[384,128]{1,0:T(8,128)S(1)} %get-tuple-element.47.info, bf16[584,128]{1,0:T(8,128)(2,1)S(1)} %collective-permute-done.11.first, bf16[584,128]{1,0:T(8,128)(2,1)S(1)} %collective-permute-done.14.second, ...), custom_call_target="tpu_custom_call" | custom-call | tf_op jit(solution)/shard_map/pallas_call | solution.py:220
  (1 shorter events, 0.0 us)
Async XLA Ops:
  0.0 1.0 %copy-start = (bf16[192,768]{1,0:T(8,128)(2,1)S(1)}, bf16[192,768]{1,0:T(8,128)(2,1)}, u32[]{:S(2)}) copy-start(bf16[192,768]{1,0:T(8,128)(2,1)} %rows.3) | copy-start | bytes 884740
  1.0 4.3 %copy-start.2 = (s32[192]{0:T(256)S(1)}, s32[192]{0:T(256)}, u32[]{:S(2)}) copy-start(s32[192]{0:T(256)} %param.5) | copy-start | bytes 2308
  1.0 8.0 %collective-permute-start.2 = (bf16[584,128]{1,0:T(8,128)(2,1)S(1)}, bf16[584,128]{1,0:T(8,128)(2,1)S(1)}, u32[]{:S(2)}, u32[]{:S(2)}) collective-permute-start(bf16[584,128]{1,0:T(8,128)(2,1)S(1)} %shard_map.38), channel_id=1, source_target_pairs={{0,3},{1,2},{2,1},{3,0},{4,7},{5,6},{6,5},{7,4},{8,11},{9,10},{10,... | collective-permute-start | bytes 448520 | tf_op jit(solution)/shard_map/ppermute | solution.py:270
  3.4 6.7 %collective-permute-start.1 = (bf16[584,128]{1,0:T(8,128)(2,1)S(1)}, bf16[584,128]{1,0:T(8,128)(2,1)S(1)}, u32[]{:S(2)}, u32[]{:S(2)}) collective-permute-start(bf16[584,128]{1,0:T(8,128)(2,1)S(1)} %shard_map.38), channel_id=1, source_target_pairs={{8,1},{9,0},{0,5},{1,4},{4,13},{5,12},{12,9},{13,8},{10,3},{11,2},... | collective-permute-start | bytes 448520 | tf_op jit(solution)/shard_map/ppermute | solution.py:267
  5.3 0.7 %copy-start.1 = (s32[192,1]{0,1:T(1,128)S(1)}, s32[192,1]{0,1:T(1,128)}, u32[]{:S(2)}) copy-start(s32[192,1]{0,1:T(1,128)} %param.4) | copy-start | bytes 2308
  6.1 6.2 %collective-permute-start.4 = (bf16[584,128]{1,0:T(8,128)(2,1)S(1)}, bf16[584,128]{1,0:T(8,128)(2,1)S(1)}, u32[]{:S(2)}, u32[]{:S(2)}) collective-permute-start(bf16[584,128]{1,0:T(8,128)(2,1)S(1)} %get-tuple-element.40), channel_id=1, source_target_pairs={{0,3},{1,2},{2,1},{3,0},{4,7},{5,6},{6,5},{7,4},{8,11},{9,10},{10,... | collective-permute-start | bytes 448520 | tf_op jit(solution)/shard_map/ppermute | solution.py:270
  6.2 7.2 %collective-permute-start.3 = (bf16[584,128]{1,0:T(8,128)(2,1)S(1)}, bf16[584,128]{1,0:T(8,128)(2,1)S(1)}, u32[]{:S(2)}, u32[]{:S(2)}) collective-permute-start(bf16[584,128]{1,0:T(8,128)(2,1)S(1)} %get-tuple-element.40), channel_id=1, source_target_pairs={{8,1},{9,0},{0,5},{1,4},{4,13},{5,12},{12,9},{13,8},{10,3},{11,2},... | collective-permute-start | bytes 448520 | tf_op jit(solution)/shard_map/ppermute | solution.py:267
  10.2 6.9 %collective-permute-start.6 = (bf16[584,128]{1,0:T(8,128)(2,1)S(1)}, bf16[584,128]{1,0:T(8,128)(2,1)S(1)}, u32[]{:S(2)}, u32[]{:S(2)}) collective-permute-start(bf16[584,128]{1,0:T(8,128)(2,1)S(1)} %collective-permute-done.1.refs_4_), channel_id=1, source_target_pairs={{0,3},{1,2},{2,1},{3,0},{4,7},{5,6},{6,5},{7,4},{8,11},{9,10},{10,... | collective-permute-start | bytes 448520 | tf_op jit(solution)/shard_map/ppermute | solution.py:270
  10.9 6.4 %collective-permute-start.5 = (bf16[584,128]{1,0:T(8,128)(2,1)S(1)}, bf16[584,128]{1,0:T(8,128)(2,1)S(1)}, u32[]{:S(2)}, u32[]{:S(2)}) collective-permute-start(bf16[584,128]{1,0:T(8,128)(2,1)S(1)} %collective-permute-done.1.refs_4_), channel_id=1, source_target_pairs={{8,1},{9,0},{0,5},{1,4},{4,13},{5,12},{12,9},{13,8},{10,3},{11,2},... | collective-permute-start | bytes 448520 | tf_op jit(solution)/shard_map/ppermute | solution.py:267
  12.3 11.8 %collective-permute-start = (bf16[1160,128]{1,0:T(8,128)(2,1)S(1)}, bf16[1160,128]{1,0:T(8,128)(2,1)S(1)}, u32[]{:S(2)}, u32[]{:S(2)}) collective-permute-start(bf16[1160,128]{1,0:T(8,128)(2,1)S(1)} %get-tuple-element.38.own), channel_id=1, source_target_pairs={{0,1},{1,0},{2,3},{3,2},{4,5},{5,4},{6,7},{7,6},{8,9},{9,8},{10,11... | collective-permute-start | bytes 890888 | tf_op jit(solution)/shard_map/ppermute | solution.py:273
  13.4 5.6 %collective-permute-start.8 = (bf16[584,128]{1,0:T(8,128)(2,1)S(1)}, bf16[584,128]{1,0:T(8,128)(2,1)S(1)}, u32[]{:S(2)}, u32[]{:S(2)}) collective-permute-start(bf16[584,128]{1,0:T(8,128)(2,1)S(1)} %collective-permute-done.3.refs_5_), channel_id=1, source_target_pairs={{0,3},{1,2},{2,1},{3,0},{4,7},{5,6},{6,5},{7,4},{8,11},{9,10},{10,... | collective-permute-start | bytes 448520 | tf_op jit(solution)/shard_map/ppermute | solution.py:270
  14.1 7.2 %collective-permute-start.7 = (bf16[584,128]{1,0:T(8,128)(2,1)S(1)}, bf16[584,128]{1,0:T(8,128)(2,1)S(1)}, u32[]{:S(2)}, u32[]{:S(2)}) collective-permute-start(bf16[584,128]{1,0:T(8,128)(2,1)S(1)} %collective-permute-done.3.refs_5_), channel_id=1, source_target_pairs={{8,1},{9,0},{0,5},{1,4},{4,13},{5,12},{12,9},{13,8},{10,3},{11,2},... | collective-permute-start | bytes 448520 | tf_op jit(solution)/shard_map/ppermute | solution.py:267
  17.3 9.1 %collective-permute-start.10 = (bf16[584,128]{1,0:T(8,128)(2,1)S(1)}, bf16[584,128]{1,0:T(8,128)(2,1)S(1)}, u32[]{:S(2)}, u32[]{:S(2)}) collective-permute-start(bf16[584,128]{1,0:T(8,128)(2,1)S(1)} %collective-permute-done.5.refs_0_), channel_id=1, source_target_pairs={{0,3},{1,2},{2,1},{3,0},{4,7},{5,6},{6,5},{7,4},{8,11},{9,10},{10,... | collective-permute-start | bytes 448520 | tf_op jit(solution)/shard_map/ppermute | solution.py:270
  18.8 7.6 %collective-permute-start.9 = (bf16[584,128]{1,0:T(8,128)(2,1)S(1)}, bf16[584,128]{1,0:T(8,128)(2,1)S(1)}, u32[]{:S(2)}, u32[]{:S(2)}) collective-permute-start(bf16[584,128]{1,0:T(8,128)(2,1)S(1)} %collective-permute-done.5.refs_0_), channel_id=1, source_target_pairs={{8,1},{9,0},{0,5},{1,4},{4,13},{5,12},{12,9},{13,8},{10,3},{11,2},... | collective-permute-start | bytes 448520 | tf_op jit(solution)/shard_map/ppermute | solution.py:267
  21.3 7.0 %collective-permute-start.13 = (bf16[584,128]{1,0:T(8,128)(2,1)S(1)}, bf16[584,128]{1,0:T(8,128)(2,1)S(1)}, u32[]{:S(2)}, u32[]{:S(2)}) collective-permute-start(bf16[584,128]{1,0:T(8,128)(2,1)S(1)} %collective-permute-done.7.refs_1_), channel_id=1, source_target_pairs={{0,3},{1,2},{2,1},{3,0},{4,7},{5,6},{6,5},{7,4},{8,11},{9,10},{10,... | collective-permute-start | bytes 448520 | tf_op jit(solution)/shard_map/ppermute | solution.py:270
  22.4 6.5 %collective-permute-start.12 = (bf16[584,128]{1,0:T(8,128)(2,1)S(1)}, bf16[584,128]{1,0:T(8,128)(2,1)S(1)}, u32[]{:S(2)}, u32[]{:S(2)}) collective-permute-start(bf16[584,128]{1,0:T(8,128)(2,1)S(1)} %collective-permute-done.7.refs_1_), channel_id=1, source_target_pairs={{8,1},{9,0},{0,5},{1,4},{4,13},{5,12},{12,9},{13,8},{10,3},{11,2},... | collective-permute-start | bytes 448520 | tf_op jit(solution)/shard_map/ppermute | solution.py:267
  26.4 6.6 %collective-permute-start.11 = (bf16[584,128]{1,0:T(8,128)(2,1)S(1)}, bf16[584,128]{1,0:T(8,128)(2,1)S(1)}, u32[]{:S(2)}, u32[]{:S(2)}) collective-permute-start(bf16[584,128]{1,0:T(8,128)(2,1)S(1)} %collective-permute-done.10.refs_2_), channel_id=1, source_target_pairs={{8,1},{9,0},{0,5},{1,4},{4,13},{5,12},{12,9},{13,8},{10,3},{11,2},... | collective-permute-start | bytes 448520 | tf_op jit(solution)/shard_map/ppermute | solution.py:267
  29.0 5.7 %collective-permute-start.14 = (bf16[584,128]{1,0:T(8,128)(2,1)S(1)}, bf16[584,128]{1,0:T(8,128)(2,1)S(1)}, u32[]{:S(2)}, u32[]{:S(2)}) collective-permute-start(bf16[584,128]{1,0:T(8,128)(2,1)S(1)} %collective-permute-done.12.refs_5_), channel_id=1, source_target_pairs={{0,3},{1,2},{2,1},{3,0},{4,7},{5,6},{6,5},{7,4},{8,11},{9,10},{10,... | collective-permute-start | bytes 448520 | tf_op jit(solution)/shard_map/ppermute | solution.py:270
  33.0 1.7 %collective-permute-start.15 = (bf16[64,896]{1,0:T(8,128)(2,1)S(1)}, bf16[64,896]{1,0:T(8,128)(2,1)S(1)}, u32[]{:S(2)}, u32[]{:S(2)}) collective-permute-start(bf16[64,896]{1,0:T(8,128)(2,1)S(1)} %get-tuple-element.63), channel_id=1, source_target_pairs={{0,1},{1,0},{2,3},{3,2},{4,5},{5,4},{6,7},{7,6},{8,9},{9,8},{10,11... | collective-permute-start | bytes 344072 | tf_op jit(solution)/shard_map/ppermute | solution.py:273
  33.4 1.3 %collective-permute-start.16 = (bf16[64,896]{1,0:T(8,128)(2,1)S(1)}, bf16[64,896]{1,0:T(8,128)(2,1)S(1)}, u32[]{:S(2)}, u32[]{:S(2)}) collective-permute-start(bf16[64,896]{1,0:T(8,128)(2,1)S(1)} %get-tuple-element.64), channel_id=1, source_target_pairs={{0,1},{1,0},{2,3},{3,2},{4,5},{5,4},{6,7},{7,6},{8,9},{9,8},{10,11... | collective-permute-start | bytes 344072 | tf_op jit(solution)/shard_map/ppermute | solution.py:273
  33.5 1.4 %collective-permute-start.17 = (bf16[64,896]{1,0:T(8,128)(2,1)S(1)}, bf16[64,896]{1,0:T(8,128)(2,1)S(1)}, u32[]{:S(2)}, u32[]{:S(2)}) collective-permute-start(bf16[64,896]{1,0:T(8,128)(2,1)S(1)} %get-tuple-element.65), channel_id=1, source_target_pairs={{0,1},{1,0},{2,3},{3,2},{4,5},{5,4},{6,7},{7,6},{8,9},{9,8},{10,11... | collective-permute-start | bytes 344072 | tf_op jit(solution)/shard_map/ppermute | solution.py:273
  33.9 1.4 %collective-permute-start.18 = (bf16[584,128]{1,0:T(8,128)(2,1)S(1)}, bf16[584,128]{1,0:T(8,128)(2,1)S(1)}, u32[]{:S(2)}, u32[]{:S(2)}) collective-permute-start(bf16[584,128]{1,0:T(8,128)(2,1)S(1)} %collective-permute-done.11.first), channel_id=1, source_target_pairs={{0,1},{1,0},{2,3},{3,2},{4,5},{5,4},{6,7},{7,6},{8,9},{9,8},{10,11... | collective-permute-start | bytes 448520 | tf_op jit(solution)/shard_map/ppermute | solution.py:273
  34.9 1.4 %collective-permute-start.19 = (bf16[584,128]{1,0:T(8,128)(2,1)S(1)}, bf16[584,128]{1,0:T(8,128)(2,1)S(1)}, u32[]{:S(2)}, u32[]{:S(2)}) collective-permute-start(bf16[584,128]{1,0:T(8,128)(2,1)S(1)} %collective-permute-done.14.second), channel_id=1, source_target_pairs={{0,1},{1,0},{2,3},{3,2},{4,5},{5,4},{6,7},{7,6},{8,9},{9,8},{10,11... | collective-permute-start | bytes 448520 | tf_op jit(solution)/shard_map/ppermute | solution.py:273

commit v17 on v16

--- a/solution.py
+++ b/solution.py
@@ -243,7 +243,7 @@
 
 
 def folded_ring(size):
-    return [0] + list(range(1, size, 2)) + list(range(2, size, 2))[::-1]
+    return list(range(0, size, 2)) + list(range(1, size, 2))[::-1]
 
 
 def together(*arrays):

time: 38 us -> 37.4 us (0.984)
  waiting for transfers between devices: 8.92 us -> 6.2 us
  starting transfers between devices: 21.5 us -> 23.6 us
    ppermute x7, waiting for transfers between devices: 6.94 us -> 3.7 us  [along(): return lax.ppermute(rows, ('blk', 'pair'), hops)]
    ppermute x7, starting transfers between devices: 12.8 us -> 15.7 us  [along(): return lax.ppermute(rows, ('blk', 'pair'), hops)]
    ppermute x7, starting transfers between devices: 7.35 us -> 6.46 us  [across(): return lax.ppermute(rows, ('sub', 'pair'), [(0, 3), (1, 2), (2, 1), (3, 0)])]
    ppermute x7, waiting for transfers between devices: 0.78 us -> 1.23 us  [across(): return lax.ppermute(rows, ('sub', 'pair'), [(0, 3), (1, 2), (2, 1), (3, 0)])]
where the time goes in v17:
time: 37.4 us; the launch traced here: 37.3 us
  starting transfers between devices  23.6 us (63%)
  waiting for transfers between devices  6.2 us (17%)
  Pallas kernels  5.72 us (15%)
  local copies, waits for them, and re-layouts  1.64 us (4%)
    ppermute x7, starting transfers between devices, along(): return lax.ppermute(rows, ('blk', 'pair'), hops)  15.7 us
    ppermute x7, starting transfers between devices, across(): return lax.ppermute(rows, ('sub', 'pair'), [(0, 3), (1, 2), (2, 1), (3, 0)])  6.46 us
    pallas_call x5, Pallas kernels, call(): pl.pallas_call(kernel, out_shape=[jax.ShapeDtypeStruct(shape, dtype) for...  5.72 us
    ppermute x7, waiting for transfers between devices, along(): return lax.ppermute(rows, ('blk', 'pair'), hops)  3.7 us
    unnamed x6, local copies, waits for them, and re-layouts  1.64 us
    ppermute x6, starting transfers between devices, other_core(): return lax.ppermute(rows, 'pair', [(0, 1), (1, 0)])  1.47 us
    ppermute x6, waiting for transfers between devices, other_core(): return lax.ppermute(rows, 'pair', [(0, 1), (1, 0)])  1.26 us
    ppermute x7, waiting for transfers between devices, across(): return lax.ppermute(rows, ('sub', 'pair'), [(0, 3), (1, 2), (2, 1), (3, 0)])  1.23 us
  transfers between devices with their start and end apart: 20, of which 10 were waited for; matrix products, arithmetic and copies ran while one was open for 0% of the time, Pallas kernels for 11%

profile of v17, /device:TPU:0, one launch (start us, length us, event | category | flops | bytes accessed | tf_op | source)
XLA Modules:
  0.0 37.3 jit_solution(16942700216504604923)
XLA Ops:
  0.0 0.0 copy-start
  0.0 1.0 %copy-done = bf16[192,768]{1,0:T(8,128)(2,1)S(1)} copy-done((bf16[192,768]{1,0:T(8,128)(2,1)S(1)}, bf16[192,768]{1,0:T(8,128)(2,1)}, u32[]{:S(2)}) %copy-start) | copy-done | bytes 294936
  1.0 0.0 copy-start.2
  1.0 2.4 %collective-permute-start.2 = (bf16[584,128]{1,0:T(8,128)(2,1)S(1)}, bf16[584,128]{1,0:T(8,128)(2,1)S(1)}, u32[]{:S(2)}, u32[]{:S(2)}) collective-permute-start(bf16[584,128]{1,0:T(8,128)(2,1)S(1)} %shard_map.38), channel_id=1, source_target_pairs={{0,3},{1,2},{2,1},{3,0},{4,7},{5,6},{6,5},{7,4},{8,11},{9,10},{10,... | collective-permute-start | bytes 448520 | tf_op jit(solution)/shard_map/ppermute | solution.py:270
  3.4 2.9 %collective-permute-start.1 = (bf16[584,128]{1,0:T(8,128)(2,1)S(1)}, bf16[584,128]{1,0:T(8,128)(2,1)S(1)}, u32[]{:S(2)}, u32[]{:S(2)}) collective-permute-start(bf16[584,128]{1,0:T(8,128)(2,1)S(1)} %shard_map.38), channel_id=1, source_target_pairs={{4,1},{5,0},{0,9},{1,8},{8,13},{9,12},{12,5},{13,4},{6,3},{7,2},{2... | collective-permute-start | bytes 448520 | tf_op jit(solution)/shard_map/ppermute | solution.py:267
  6.3 0.0 copy-start.1
  6.3 0.0 copy-done.2
  6.3 0.7 %copy-done.1 = s32[192,1]{0,1:T(1,128)S(1)} copy-done((s32[192,1]{0,1:T(1,128)S(1)}, s32[192,1]{0,1:T(1,128)}, u32[]{:S(2)}) %copy-start.1) | copy-done | bytes 792
  7.0 0.1 shard_map.37
  7.1 0.1 collective-permute-start.4
  7.2 1.8 %collective-permute-start.3 = (bf16[584,128]{1,0:T(8,128)(2,1)S(1)}, bf16[584,128]{1,0:T(8,128)(2,1)S(1)}, u32[]{:S(2)}, u32[]{:S(2)}) collective-permute-start(bf16[584,128]{1,0:T(8,128)(2,1)S(1)} %get-tuple-element.40), channel_id=1, source_target_pairs={{4,1},{5,0},{0,9},{1,8},{8,13},{9,12},{12,5},{13,4},{6,3},{7,2},{2... | collective-permute-start | bytes 448520 | tf_op jit(solution)/shard_map/ppermute | solution.py:267
  9.0 0.0 collective-permute-done.2.refs_0_
  9.0 1.2 %collective-permute-done.1.refs_4_ = bf16[584,128]{1,0:T(8,128)(2,1)S(1)} collective-permute-done((bf16[584,128]{1,0:T(8,128)(2,1)S(1)}, bf16[584,128]{1,0:T(8,128)(2,1)S(1)}, u32[]{:S(2)}, u32[]{:S(2)}) %collective-permute-start.1) | collective-permute-done | bytes 149536 | tf_op jit(solution)/shard_map/ppermute | solution.py:267
  10.1 0.0 collective-permute-start.6
  10.1 3.1 %collective-permute-start.5 = (bf16[584,128]{1,0:T(8,128)(2,1)S(1)}, bf16[584,128]{1,0:T(8,128)(2,1)S(1)}, u32[]{:S(2)}, u32[]{:S(2)}) collective-permute-start(bf16[584,128]{1,0:T(8,128)(2,1)S(1)} %collective-permute-done.1.refs_4_), channel_id=1, source_target_pairs={{4,1},{5,0},{0,9},{1,8},{8,13},{9,12},{12,5},{13,4},{6,3},{7,2},{2... | collective-permute-start | bytes 448520 | tf_op jit(solution)/shard_map/ppermute | solution.py:267
  13.2 0.1 collective-permute-start
  13.3 0.0 collective-permute-done.4.refs_1_
  13.3 0.0 collective-permute-done.3.refs_5_
  13.3 1.7 %collective-permute-start.8 = (bf16[584,128]{1,0:T(8,128)(2,1)S(1)}, bf16[584,128]{1,0:T(8,128)(2,1)S(1)}, u32[]{:S(2)}, u32[]{:S(2)}) collective-permute-start(bf16[584,128]{1,0:T(8,128)(2,1)S(1)} %collective-permute-done.3.refs_5_), channel_id=1, source_target_pairs={{0,3},{1,2},{2,1},{3,0},{4,7},{5,6},{6,5},{7,4},{8,11},{9,10},{10,... | collective-permute-start | bytes 448520 | tf_op jit(solution)/shard_map/ppermute | solution.py:270
  15.1 1.2 %collective-permute-start.7 = (bf16[584,128]{1,0:T(8,128)(2,1)S(1)}, bf16[584,128]{1,0:T(8,128)(2,1)S(1)}, u32[]{:S(2)}, u32[]{:S(2)}) collective-permute-start(bf16[584,128]{1,0:T(8,128)(2,1)S(1)} %collective-permute-done.3.refs_5_), channel_id=1, source_target_pairs={{4,1},{5,0},{0,9},{1,8},{8,13},{9,12},{12,5},{13,4},{6,3},{7,2},{2... | collective-permute-start | bytes 448520 | tf_op jit(solution)/shard_map/ppermute | solution.py:267
  16.2 0.3 collective-permute-done.6.refs_2_
  16.5 0.4 collective-permute-done.5.refs_0_
  16.9 1.2 %collective-permute-start.10 = (bf16[584,128]{1,0:T(8,128)(2,1)S(1)}, bf16[584,128]{1,0:T(8,128)(2,1)S(1)}, u32[]{:S(2)}, u32[]{:S(2)}) collective-permute-start(bf16[584,128]{1,0:T(8,128)(2,1)S(1)} %collective-permute-done.5.refs_0_), channel_id=1, source_target_pairs={{0,3},{1,2},{2,1},{3,0},{4,7},{5,6},{6,5},{7,4},{8,11},{9,10},{10,... | collective-permute-start | bytes 448520 | tf_op jit(solution)/shard_map/ppermute | solution.py:270
  18.0 3.4 %collective-permute-start.9 = (bf16[584,128]{1,0:T(8,128)(2,1)S(1)}, bf16[584,128]{1,0:T(8,128)(2,1)S(1)}, u32[]{:S(2)}, u32[]{:S(2)}) collective-permute-start(bf16[584,128]{1,0:T(8,128)(2,1)S(1)} %collective-permute-done.5.refs_0_), channel_id=1, source_target_pairs={{4,1},{5,0},{0,9},{1,8},{8,13},{9,12},{12,5},{13,4},{6,3},{7,2},{2... | collective-permute-start | bytes 448520 | tf_op jit(solution)/shard_map/ppermute | solution.py:267
  21.4 0.0 collective-permute-done.8.refs_3_
  21.4 0.0 collective-permute-done.7.refs_1_
  21.4 0.1 collective-permute-start.13
  21.6 2.6 %collective-permute-start.12 = (bf16[584,128]{1,0:T(8,128)(2,1)S(1)}, bf16[584,128]{1,0:T(8,128)(2,1)S(1)}, u32[]{:S(2)}, u32[]{:S(2)}) collective-permute-start(bf16[584,128]{1,0:T(8,128)(2,1)S(1)} %collective-permute-done.7.refs_1_), channel_id=1, source_target_pairs={{4,1},{5,0},{0,9},{1,8},{8,13},{9,12},{12,5},{13,4},{6,3},{7,2},{2... | collective-permute-start | bytes 448520 | tf_op jit(solution)/shard_map/ppermute | solution.py:267
  24.1 0.0 collective-permute-done.other
  24.1 2.3 %shard_map.39 = (f32[192,896]{1,0:T(8,128)S(1)}, f32[192,896]{1,0:T(8,128)S(1)}, f32[384,128]{1,0:T(8,128)S(1)}) custom-call(bf16[1160,128]{1,0:T(8,128)(2,1)S(1)} %get-tuple-element.38.own, bf16[1160,128]{1,0:T(8,128)(2,1)S(1)} %collective-permute-done.other, bf16[584,128]{1,0:T(8,128)(2,1)S(1)} %collective-permute-done.2.refs_0_, ...), custom_call_target="tpu_custom_call" | custom-call | tf_op jit(solution)/shard_map/pallas_call | solution.py:220
  26.4 0.0 collective-permute-done.10.refs_2_
  26.4 0.0 collective-permute-done.9.refs_4_
  26.5 0.9 %collective-permute-start.11 = (bf16[584,128]{1,0:T(8,128)(2,1)S(1)}, bf16[584,128]{1,0:T(8,128)(2,1)S(1)}, u32[]{:S(2)}, u32[]{:S(2)}) collective-permute-start(bf16[584,128]{1,0:T(8,128)(2,1)S(1)} %collective-permute-done.10.refs_2_), channel_id=1, source_target_pairs={{4,1},{5,0},{0,9},{1,8},{8,13},{9,12},{12,5},{13,4},{6,3},{7,2},{2... | collective-permute-start | bytes 448520 | tf_op jit(solution)/shard_map/ppermute | solution.py:267
  27.3 0.2 collective-permute-done.13.refs_3_
  27.5 0.7 %collective-permute-done.12.refs_5_ = bf16[584,128]{1,0:T(8,128)(2,1)S(1)} collective-permute-done((bf16[584,128]{1,0:T(8,128)(2,1)S(1)}, bf16[584,128]{1,0:T(8,128)(2,1)S(1)}, u32[]{:S(2)}, u32[]{:S(2)}) %collective-permute-start.12) | collective-permute-done | bytes 149536 | tf_op jit(solution)/shard_map/ppermute | solution.py:267
  28.2 0.9 %collective-permute-start.14 = (bf16[584,128]{1,0:T(8,128)(2,1)S(1)}, bf16[584,128]{1,0:T(8,128)(2,1)S(1)}, u32[]{:S(2)}, u32[]{:S(2)}) collective-permute-start(bf16[584,128]{1,0:T(8,128)(2,1)S(1)} %collective-permute-done.12.refs_5_), channel_id=1, source_target_pairs={{0,3},{1,2},{2,1},{3,0},{4,7},{5,6},{6,5},{7,4},{8,11},{9,10},{10,... | collective-permute-start | bytes 448520 | tf_op jit(solution)/shard_map/ppermute | solution.py:270
  29.0 1.7 %shard_map.40 = (f32[192,896]{1,0:T(8,128)S(1)}, bf16[64,896]{1,0:T(8,128)(2,1)S(1)}, bf16[64,896]{1,0:T(8,128)(2,1)S(1)}, bf16[64,896]{1,0:T(8,128)(2,1)S(1)}) custom-call(bf16[1160,128]{1,0:T(8,128)(2,1)S(1)} %get-tuple-element.38.own, bf16[1160,128]{1,0:T(8,128)(2,1)S(1)} %collective-permute-done.other, ...), custom_call_target="tpu_custom_call", output_to_operand_aliasing={{0}: (9, {})} | custom-call | tf_op jit(solution)/shard_map/pallas_call | solution.py:220
  30.8 1.5 %collective-permute-done.11.first = bf16[584,128]{1,0:T(8,128)(2,1)S(1)} collective-permute-done((bf16[584,128]{1,0:T(8,128)(2,1)S(1)}, bf16[584,128]{1,0:T(8,128)(2,1)S(1)}, u32[]{:S(2)}, u32[]{:S(2)}) %collective-permute-start.11) | collective-permute-done | bytes 149536 | tf_op jit(solution)/shard_map/ppermute | solution.py:267
  32.3 0.6 %collective-permute-start.15 = (bf16[64,896]{1,0:T(8,128)(2,1)S(1)}, bf16[64,896]{1,0:T(8,128)(2,1)S(1)}, u32[]{:S(2)}, u32[]{:S(2)}) collective-permute-start(bf16[64,896]{1,0:T(8,128)(2,1)S(1)} %get-tuple-element.63), channel_id=1, source_target_pairs={{0,1},{1,0},{2,3},{3,2},{4,5},{5,4},{6,7},{7,6},{8,9},{9,8},{10,11... | collective-permute-start | bytes 344072 | tf_op jit(solution)/shard_map/ppermute | solution.py:273
  32.8 0.0 collective-permute-start.16
  32.8 0.5 %collective-permute-start.17 = (bf16[64,896]{1,0:T(8,128)(2,1)S(1)}, bf16[64,896]{1,0:T(8,128)(2,1)S(1)}, u32[]{:S(2)}, u32[]{:S(2)}) collective-permute-start(bf16[64,896]{1,0:T(8,128)(2,1)S(1)} %get-tuple-element.65), channel_id=1, source_target_pairs={{0,1},{1,0},{2,3},{3,2},{4,5},{5,4},{6,7},{7,6},{8,9},{9,8},{10,11... | collective-permute-start | bytes 344072 | tf_op jit(solution)/shard_map/ppermute | solution.py:273
  33.3 0.0 collective-permute-start.18
  33.3 0.7 %collective-permute-done.14.second = bf16[584,128]{1,0:T(8,128)(2,1)S(1)} collective-permute-done((bf16[584,128]{1,0:T(8,128)(2,1)S(1)}, bf16[584,128]{1,0:T(8,128)(2,1)S(1)}, u32[]{:S(2)}, u32[]{:S(2)}) %collective-permute-start.14) | collective-permute-done | bytes 149536 | tf_op jit(solution)/shard_map/ppermute | solution.py:270
  34.1 0.0 collective-permute-done.15.refs_0_
  34.1 0.1 collective-permute-done.16.refs_1_
  34.1 0.2 collective-permute-done.17.refs_2_
  34.3 0.3 collective-permute-start.19
  34.6 0.0 collective-permute-done.18.first_other
  34.7 1.0 %collective-permute-done.19.second_other = bf16[584,128]{1,0:T(8,128)(2,1)S(1)} collective-permute-done((bf16[584,128]{1,0:T(8,128)(2,1)S(1)}, bf16[584,128]{1,0:T(8,128)(2,1)S(1)}, u32[]{:S(2)}, u32[]{:S(2)}) %collective-permute-start.19) | collective-permute-done | bytes 149536 | tf_op jit(solution)/shard_map/ppermute | solution.py:273
  35.7 1.6 %shard_map.41 = bf16[192,768]{1,0:T(8,128)(2,1)} custom-call(bf16[1160,128]{1,0:T(8,128)(2,1)S(1)} %get-tuple-element.38.own, f32[384,128]{1,0:T(8,128)S(1)} %get-tuple-element.47.info, bf16[584,128]{1,0:T(8,128)(2,1)S(1)} %collective-permute-done.11.first, bf16[584,128]{1,0:T(8,128)(2,1)S(1)} %collective-permute-done.14.second, ...), custom_call_target="tpu_custom_call" | custom-call | tf_op jit(solution)/shard_map/pallas_call | solution.py:220
  (1 shorter events, 0.0 us)
Async XLA Ops:
  0.0 1.0 %copy-start = (bf16[192,768]{1,0:T(8,128)(2,1)S(1)}, bf16[192,768]{1,0:T(8,128)(2,1)}, u32[]{:S(2)}) copy-start(bf16[192,768]{1,0:T(8,128)(2,1)} %rows.3) | copy-start | bytes 884740
  1.0 5.3 %copy-start.2 = (s32[192]{0:T(256)S(1)}, s32[192]{0:T(256)}, u32[]{:S(2)}) copy-start(s32[192]{0:T(256)} %param.5) | copy-start | bytes 2308
  1.0 8.0 %collective-permute-start.2 = (bf16[584,128]{1,0:T(8,128)(2,1)S(1)}, bf16[584,128]{1,0:T(8,128)(2,1)S(1)}, u32[]{:S(2)}, u32[]{:S(2)}) collective-permute-start(bf16[584,128]{1,0:T(8,128)(2,1)S(1)} %shard_map.38), channel_id=1, source_target_pairs={{0,3},{1,2},{2,1},{3,0},{4,7},{5,6},{6,5},{7,4},{8,11},{9,10},{10,... | collective-permute-start | bytes 448520 | tf_op jit(solution)/shard_map/ppermute | solution.py:270
  3.4 6.7 %collective-permute-start.1 = (bf16[584,128]{1,0:T(8,128)(2,1)S(1)}, bf16[584,128]{1,0:T(8,128)(2,1)S(1)}, u32[]{:S(2)}, u32[]{:S(2)}) collective-permute-start(bf16[584,128]{1,0:T(8,128)(2,1)S(1)} %shard_map.38), channel_id=1, source_target_pairs={{4,1},{5,0},{0,9},{1,8},{8,13},{9,12},{12,5},{13,4},{6,3},{7,2},{2... | collective-permute-start | bytes 448520 | tf_op jit(solution)/shard_map/ppermute | solution.py:267
  6.3 0.7 %copy-start.1 = (s32[192,1]{0,1:T(1,128)S(1)}, s32[192,1]{0,1:T(1,128)}, u32[]{:S(2)}) copy-start(s32[192,1]{0,1:T(1,128)} %param.4) | copy-start | bytes 2308
  7.1 6.2 %collective-permute-start.4 = (bf16[584,128]{1,0:T(8,128)(2,1)S(1)}, bf16[584,128]{1,0:T(8,128)(2,1)S(1)}, u32[]{:S(2)}, u32[]{:S(2)}) collective-permute-start(bf16[584,128]{1,0:T(8,128)(2,1)S(1)} %get-tuple-element.40), channel_id=1, source_target_pairs={{0,3},{1,2},{2,1},{3,0},{4,7},{5,6},{6,5},{7,4},{8,11},{9,10},{10,... | collective-permute-start | bytes 448520 | tf_op jit(solution)/shard_map/ppermute | solution.py:270
  7.2 6.1 %collective-permute-start.3 = (bf16[584,128]{1,0:T(8,128)(2,1)S(1)}, bf16[584,128]{1,0:T(8,128)(2,1)S(1)}, u32[]{:S(2)}, u32[]{:S(2)}) collective-permute-start(bf16[584,128]{1,0:T(8,128)(2,1)S(1)} %get-tuple-element.40), channel_id=1, source_target_pairs={{4,1},{5,0},{0,9},{1,8},{8,13},{9,12},{12,5},{13,4},{6,3},{7,2},{2... | collective-permute-start | bytes 448520 | tf_op jit(solution)/shard_map/ppermute | solution.py:267
  10.1 6.4 %collective-permute-start.6 = (bf16[584,128]{1,0:T(8,128)(2,1)S(1)}, bf16[584,128]{1,0:T(8,128)(2,1)S(1)}, u32[]{:S(2)}, u32[]{:S(2)}) collective-permute-start(bf16[584,128]{1,0:T(8,128)(2,1)S(1)} %collective-permute-done.1.refs_4_), channel_id=1, source_target_pairs={{0,3},{1,2},{2,1},{3,0},{4,7},{5,6},{6,5},{7,4},{8,11},{9,10},{10,... | collective-permute-start | bytes 448520 | tf_op jit(solution)/shard_map/ppermute | solution.py:270
  10.1 6.8 %collective-permute-start.5 = (bf16[584,128]{1,0:T(8,128)(2,1)S(1)}, bf16[584,128]{1,0:T(8,128)(2,1)S(1)}, u32[]{:S(2)}, u32[]{:S(2)}) collective-permute-start(bf16[584,128]{1,0:T(8,128)(2,1)S(1)} %collective-permute-done.1.refs_4_), channel_id=1, source_target_pairs={{4,1},{5,0},{0,9},{1,8},{8,13},{9,12},{12,5},{13,4},{6,3},{7,2},{2... | collective-permute-start | bytes 448520 | tf_op jit(solution)/shard_map/ppermute | solution.py:267
  13.2 10.9 %collective-permute-start = (bf16[1160,128]{1,0:T(8,128)(2,1)S(1)}, bf16[1160,128]{1,0:T(8,128)(2,1)S(1)}, u32[]{:S(2)}, u32[]{:S(2)}) collective-permute-start(bf16[1160,128]{1,0:T(8,128)(2,1)S(1)} %get-tuple-element.38.own), channel_id=1, source_target_pairs={{0,1},{1,0},{2,3},{3,2},{4,5},{5,4},{6,7},{7,6},{8,9},{9,8},{10,11... | collective-permute-start | bytes 890888 | tf_op jit(solution)/shard_map/ppermute | solution.py:273
  13.3 8.1 %collective-permute-start.8 = (bf16[584,128]{1,0:T(8,128)(2,1)S(1)}, bf16[584,128]{1,0:T(8,128)(2,1)S(1)}, u32[]{:S(2)}, u32[]{:S(2)}) collective-permute-start(bf16[584,128]{1,0:T(8,128)(2,1)S(1)} %collective-permute-done.3.refs_5_), channel_id=1, source_target_pairs={{0,3},{1,2},{2,1},{3,0},{4,7},{5,6},{6,5},{7,4},{8,11},{9,10},{10,... | collective-permute-start | bytes 448520 | tf_op jit(solution)/shard_map/ppermute | solution.py:270
  15.1 6.4 %collective-permute-start.7 = (bf16[584,128]{1,0:T(8,128)(2,1)S(1)}, bf16[584,128]{1,0:T(8,128)(2,1)S(1)}, u32[]{:S(2)}, u32[]{:S(2)}) collective-permute-start(bf16[584,128]{1,0:T(8,128)(2,1)S(1)} %collective-permute-done.3.refs_5_), channel_id=1, source_target_pairs={{4,1},{5,0},{0,9},{1,8},{8,13},{9,12},{12,5},{13,4},{6,3},{7,2},{2... | collective-permute-start | bytes 448520 | tf_op jit(solution)/shard_map/ppermute | solution.py:267
  16.9 9.5 %collective-permute-start.10 = (bf16[584,128]{1,0:T(8,128)(2,1)S(1)}, bf16[584,128]{1,0:T(8,128)(2,1)S(1)}, u32[]{:S(2)}, u32[]{:S(2)}) collective-permute-start(bf16[584,128]{1,0:T(8,128)(2,1)S(1)} %collective-permute-done.5.refs_0_), channel_id=1, source_target_pairs={{0,3},{1,2},{2,1},{3,0},{4,7},{5,6},{6,5},{7,4},{8,11},{9,10},{10,... | collective-permute-start | bytes 448520 | tf_op jit(solution)/shard_map/ppermute | solution.py:270
  18.0 8.4 %collective-permute-start.9 = (bf16[584,128]{1,0:T(8,128)(2,1)S(1)}, bf16[584,128]{1,0:T(8,128)(2,1)S(1)}, u32[]{:S(2)}, u32[]{:S(2)}) collective-permute-start(bf16[584,128]{1,0:T(8,128)(2,1)S(1)} %collective-permute-done.5.refs_0_), channel_id=1, source_target_pairs={{4,1},{5,0},{0,9},{1,8},{8,13},{9,12},{12,5},{13,4},{6,3},{7,2},{2... | collective-permute-start | bytes 448520 | tf_op jit(solution)/shard_map/ppermute | solution.py:267
  21.4 6.1 %collective-permute-start.13 = (bf16[584,128]{1,0:T(8,128)(2,1)S(1)}, bf16[584,128]{1,0:T(8,128)(2,1)S(1)}, u32[]{:S(2)}, u32[]{:S(2)}) collective-permute-start(bf16[584,128]{1,0:T(8,128)(2,1)S(1)} %collective-permute-done.7.refs_1_), channel_id=1, source_target_pairs={{0,3},{1,2},{2,1},{3,0},{4,7},{5,6},{6,5},{7,4},{8,11},{9,10},{10,... | collective-permute-start | bytes 448520 | tf_op jit(solution)/shard_map/ppermute | solution.py:270
  21.6 6.6 %collective-permute-start.12 = (bf16[584,128]{1,0:T(8,128)(2,1)S(1)}, bf16[584,128]{1,0:T(8,128)(2,1)S(1)}, u32[]{:S(2)}, u32[]{:S(2)}) collective-permute-start(bf16[584,128]{1,0:T(8,128)(2,1)S(1)} %collective-permute-done.7.refs_1_), channel_id=1, source_target_pairs={{4,1},{5,0},{0,9},{1,8},{8,13},{9,12},{12,5},{13,4},{6,3},{7,2},{2... | collective-permute-start | bytes 448520 | tf_op jit(solution)/shard_map/ppermute | solution.py:267
  26.5 5.8 %collective-permute-start.11 = (bf16[584,128]{1,0:T(8,128)(2,1)S(1)}, bf16[584,128]{1,0:T(8,128)(2,1)S(1)}, u32[]{:S(2)}, u32[]{:S(2)}) collective-permute-start(bf16[584,128]{1,0:T(8,128)(2,1)S(1)} %collective-permute-done.10.refs_2_), channel_id=1, source_target_pairs={{4,1},{5,0},{0,9},{1,8},{8,13},{9,12},{12,5},{13,4},{6,3},{7,2},{2... | collective-permute-start | bytes 448520 | tf_op jit(solution)/shard_map/ppermute | solution.py:267
  28.2 5.9 %collective-permute-start.14 = (bf16[584,128]{1,0:T(8,128)(2,1)S(1)}, bf16[584,128]{1,0:T(8,128)(2,1)S(1)}, u32[]{:S(2)}, u32[]{:S(2)}) collective-permute-start(bf16[584,128]{1,0:T(8,128)(2,1)S(1)} %collective-permute-done.12.refs_5_), channel_id=1, source_target_pairs={{0,3},{1,2},{2,1},{3,0},{4,7},{5,6},{6,5},{7,4},{8,11},{9,10},{10,... | collective-permute-start | bytes 448520 | tf_op jit(solution)/shard_map/ppermute | solution.py:270
  32.3 1.8 %collective-permute-start.15 = (bf16[64,896]{1,0:T(8,128)(2,1)S(1)}, bf16[64,896]{1,0:T(8,128)(2,1)S(1)}, u32[]{:S(2)}, u32[]{:S(2)}) collective-permute-start(bf16[64,896]{1,0:T(8,128)(2,1)S(1)} %get-tuple-element.63), channel_id=1, source_target_pairs={{0,1},{1,0},{2,3},{3,2},{4,5},{5,4},{6,7},{7,6},{8,9},{9,8},{10,11... | collective-permute-start | bytes 344072 | tf_op jit(solution)/shard_map/ppermute | solution.py:273
  32.8 1.3 %collective-permute-start.16 = (bf16[64,896]{1,0:T(8,128)(2,1)S(1)}, bf16[64,896]{1,0:T(8,128)(2,1)S(1)}, u32[]{:S(2)}, u32[]{:S(2)}) collective-permute-start(bf16[64,896]{1,0:T(8,128)(2,1)S(1)} %get-tuple-element.64), channel_id=1, source_target_pairs={{0,1},{1,0},{2,3},{3,2},{4,5},{5,4},{6,7},{7,6},{8,9},{9,8},{10,11... | collective-permute-start | bytes 344072 | tf_op jit(solution)/shard_map/ppermute | solution.py:273
  32.8 1.5 %collective-permute-start.17 = (bf16[64,896]{1,0:T(8,128)(2,1)S(1)}, bf16[64,896]{1,0:T(8,128)(2,1)S(1)}, u32[]{:S(2)}, u32[]{:S(2)}) collective-permute-start(bf16[64,896]{1,0:T(8,128)(2,1)S(1)} %get-tuple-element.65), channel_id=1, source_target_pairs={{0,1},{1,0},{2,3},{3,2},{4,5},{5,4},{6,7},{7,6},{8,9},{9,8},{10,11... | collective-permute-start | bytes 344072 | tf_op jit(solution)/shard_map/ppermute | solution.py:273
  33.3 1.4 %collective-permute-start.18 = (bf16[584,128]{1,0:T(8,128)(2,1)S(1)}, bf16[584,128]{1,0:T(8,128)(2,1)S(1)}, u32[]{:S(2)}, u32[]{:S(2)}) collective-permute-start(bf16[584,128]{1,0:T(8,128)(2,1)S(1)} %collective-permute-done.11.first), channel_id=1, source_target_pairs={{0,1},{1,0},{2,3},{3,2},{4,5},{5,4},{6,7},{7,6},{8,9},{9,8},{10,11... | collective-permute-start | bytes 448520 | tf_op jit(solution)/shard_map/ppermute | solution.py:273
  34.3 1.4 %collective-permute-start.19 = (bf16[584,128]{1,0:T(8,128)(2,1)S(1)}, bf16[584,128]{1,0:T(8,128)(2,1)S(1)}, u32[]{:S(2)}, u32[]{:S(2)}) collective-permute-start(bf16[584,128]{1,0:T(8,128)(2,1)S(1)} %collective-permute-done.14.second), channel_id=1, source_target_pairs={{0,1},{1,0},{2,3},{3,2},{4,5},{5,4},{6,7},{7,6},{8,9},{9,8},{10,11... | collective-permute-start | bytes 448520 | tf_op jit(solution)/shard_map/ppermute | solution.py:273

commit v18 on v17

--- a/solution.py
+++ b/solution.py
@@ -130,17 +130,19 @@
 def add_blocks(left, info, blocks, numer, denom):
     key = info[: left.shape[0], 0:1]
     scale = info[: left.shape[0], 1:2]
-    for right_rows, right_key, right_scale in blocks:
-        grams = lax.dot_general(
-            left, right_rows, (((1,), (1,)), ((), ())), preferred_element_type=F32
-        )
-        half = jnp.tanh(grams * scale * right_scale - 1.0)
-        weight = jnp.where(key == right_key, 0.5 + 0.5 * half, 0.0)
-        add = jnp.dot(weight.astype(BF16), right_rows, preferred_element_type=F32)
-        add_denom = jnp.sum(weight, axis=1, keepdims=True)
-        numer = add if numer is None else numer + add
-        denom = add_denom if denom is None else denom + add_denom
-    return numer, denom
+    right_rows = jnp.concatenate([block[0] for block in blocks], axis=0)
+    right_key = jnp.concatenate([block[1] for block in blocks], axis=1)
+    right_scale = jnp.concatenate([block[2] for block in blocks], axis=1)
+    grams = lax.dot_general(
+        left, right_rows, (((1,), (1,)), ((), ())), preferred_element_type=F32
+    )
+    half = jnp.tanh(grams * scale * right_scale - 1.0)
+    weight = jnp.where(key == right_key, 0.5 + 0.5 * half, 0.0)
+    add = jnp.dot(weight.astype(BF16), right_rows, preferred_element_type=F32)
+    add_denom = jnp.sum(weight, axis=1, keepdims=True)
+    if numer is None:
+        return add, add_denom
+    return numer + add, denom + add_denom
 
 
 def left_rows(refs, rows_here):
@@ -297,8 +299,9 @@
     last_first, last_second = along(near_first), across(far_second)
     late = [along_by[-2], across_by[-1], along_by[-1]]
     mine, *theirs = add_both(left, late, (mine, theirs))
-    last_first, *theirs = together(last_first, *theirs)
-    last_second, *back = together(last_second, *[other_core(part) for part in theirs])
+    back = [other_core(part) for part in theirs[:-1]]
+    last_first, theirs[-1] = together(last_first, theirs[-1])
+    last_second, *back = together(last_second, *back, other_core(theirs[-1]))
     last = (last_first, last_second)
     (out,) = call(
         last_kernel,

time: 37.4 us -> 37.3 us (level)
  Pallas kernels: 5.72 us -> 4.51 us
  waiting for transfers between devices: 6.2 us -> 6.83 us
  starting transfers between devices: 23.6 us -> 24.1 us
    ppermute x7, waiting for transfers between devices: 1.23 us -> 2.62 us  [across(): return lax.ppermute(rows, ('sub', 'pair'), [(0, 3), (1, 2), (2, 1), (3, 0)])]
    pallas_call x5, Pallas kernels: 5.72 us -> 4.51 us  [call(): pl.pallas_call(kernel, out_shape=[jax.ShapeDtypeStruct(shape, dtype) for...]
    ppermute x7, waiting for transfers between devices: 3.7 us -> 2.78 us  [along(): return lax.ppermute(rows, ('blk', 'pair'), hops)]
    ppermute x7, starting transfers between devices: 15.7 us -> 16.5 us  [along(): return lax.ppermute(rows, ('blk', 'pair'), hops)]
  transfers between devices with their start and end apart: 20 -> 20, of which waited for: 10 -> 9; matrix products, arithmetic and copies ran while one was open for 0% -> 0% of each run, Pallas kernels for 11% -> 8%
where the time goes in v18:
time: 37.3 us; the launch traced here: 37.2 us
  starting transfers between devices  24.1 us (65%)
  waiting for transfers between devices  6.83 us (18%)
  Pallas kernels  4.51 us (12%)
  local copies, waits for them, and re-layouts  1.64 us (4%)
    ppermute x7, starting transfers between devices, along(): return lax.ppermute(rows, ('blk', 'pair'), hops)  16.5 us
    ppermute x7, starting transfers between devices, across(): return lax.ppermute(rows, ('sub', 'pair'), [(0, 3), (1, 2), (2, 1), (3, 0)])  6.34 us
    pallas_call x5, Pallas kernels, call(): pl.pallas_call(kernel, out_shape=[jax.ShapeDtypeStruct(shape, dtype) for...  4.51 us
    ppermute x7, waiting for transfers between devices, along(): return lax.ppermute(rows, ('blk', 'pair'), hops)  2.78 us
    ppermute x7, waiting for transfers between devices, across(): return lax.ppermute(rows, ('sub', 'pair'), [(0, 3), (1, 2), (2, 1), (3, 0)])  2.62 us
    unnamed x6, local copies, waits for them, and re-layouts  1.64 us
    ppermute x6, waiting for transfers between devices, other_core(): return lax.ppermute(rows, 'pair', [(0, 1), (1, 0)])  1.43 us
    ppermute x6, starting transfers between devices, other_core(): return lax.ppermute(rows, 'pair', [(0, 1), (1, 0)])  1.3 us
  transfers between devices with their start and end apart: 20, of which 9 were waited for; matrix products, arithmetic and copies ran while one was open for 0% of the time, Pallas kernels for 8%

profile of v18, /device:TPU:0, one launch (start us, length us, event | category | flops | bytes accessed | tf_op | source)
XLA Modules:
  0.0 37.2 jit_solution(16361184115185168402)
XLA Ops:
  0.0 0.0 copy-start
  0.0 1.0 %copy-done = bf16[192,768]{1,0:T(8,128)(2,1)S(1)} copy-done((bf16[192,768]{1,0:T(8,128)(2,1)S(1)}, bf16[192,768]{1,0:T(8,128)(2,1)}, u32[]{:S(2)}) %copy-start) | copy-done | bytes 294936
  1.0 0.0 copy-start.2
  1.0 2.4 %collective-permute-start.2 = (bf16[584,128]{1,0:T(8,128)(2,1)S(1)}, bf16[584,128]{1,0:T(8,128)(2,1)S(1)}, u32[]{:S(2)}, u32[]{:S(2)}) collective-permute-start(bf16[584,128]{1,0:T(8,128)(2,1)S(1)} %shard_map.38), channel_id=1, source_target_pairs={{0,3},{1,2},{2,1},{3,0},{4,7},{5,6},{6,5},{7,4},{8,11},{9,10},{10,... | collective-permute-start | bytes 448520 | tf_op jit(solution)/shard_map/ppermute | solution.py:272
  3.4 2.9 %collective-permute-start.1 = (bf16[584,128]{1,0:T(8,128)(2,1)S(1)}, bf16[584,128]{1,0:T(8,128)(2,1)S(1)}, u32[]{:S(2)}, u32[]{:S(2)}) collective-permute-start(bf16[584,128]{1,0:T(8,128)(2,1)S(1)} %shard_map.38), channel_id=1, source_target_pairs={{4,1},{5,0},{0,9},{1,8},{8,13},{9,12},{12,5},{13,4},{6,3},{7,2},{2... | collective-permute-start | bytes 448520 | tf_op jit(solution)/shard_map/ppermute | solution.py:269
  6.3 0.0 copy-start.1
  6.3 0.0 copy-done.2
  6.3 0.7 %copy-done.1 = s32[192,1]{0,1:T(1,128)S(1)} copy-done((s32[192,1]{0,1:T(1,128)S(1)}, s32[192,1]{0,1:T(1,128)}, u32[]{:S(2)}) %copy-start.1) | copy-done | bytes 792
  7.0 0.1 shard_map.37
  7.1 0.1 collective-permute-start.4
  7.2 1.8 %collective-permute-start.3 = (bf16[584,128]{1,0:T(8,128)(2,1)S(1)}, bf16[584,128]{1,0:T(8,128)(2,1)S(1)}, u32[]{:S(2)}, u32[]{:S(2)}) collective-permute-start(bf16[584,128]{1,0:T(8,128)(2,1)S(1)} %get-tuple-element.38), channel_id=1, source_target_pairs={{4,1},{5,0},{0,9},{1,8},{8,13},{9,12},{12,5},{13,4},{6,3},{7,2},{2... | collective-permute-start | bytes 448520 | tf_op jit(solution)/shard_map/ppermute | solution.py:269
  9.0 0.0 collective-permute-done.2.refs_0_
  9.0 1.2 %collective-permute-done.1.refs_4_ = bf16[584,128]{1,0:T(8,128)(2,1)S(1)} collective-permute-done((bf16[584,128]{1,0:T(8,128)(2,1)S(1)}, bf16[584,128]{1,0:T(8,128)(2,1)S(1)}, u32[]{:S(2)}, u32[]{:S(2)}) %collective-permute-start.1) | collective-permute-done | bytes 149536 | tf_op jit(solution)/shard_map/ppermute | solution.py:269
  10.1 0.0 collective-permute-start.6
  10.1 3.1 %collective-permute-start.5 = (bf16[584,128]{1,0:T(8,128)(2,1)S(1)}, bf16[584,128]{1,0:T(8,128)(2,1)S(1)}, u32[]{:S(2)}, u32[]{:S(2)}) collective-permute-start(bf16[584,128]{1,0:T(8,128)(2,1)S(1)} %collective-permute-done.1.refs_4_), channel_id=1, source_target_pairs={{4,1},{5,0},{0,9},{1,8},{8,13},{9,12},{12,5},{13,4},{6,3},{7,2},{2... | collective-permute-start | bytes 448520 | tf_op jit(solution)/shard_map/ppermute | solution.py:269
  13.2 0.1 collective-permute-start
  13.3 0.0 collective-permute-done.4.refs_1_
  13.3 0.0 collective-permute-done.3.refs_5_
  13.3 1.7 %collective-permute-start.8 = (bf16[584,128]{1,0:T(8,128)(2,1)S(1)}, bf16[584,128]{1,0:T(8,128)(2,1)S(1)}, u32[]{:S(2)}, u32[]{:S(2)}) collective-permute-start(bf16[584,128]{1,0:T(8,128)(2,1)S(1)} %collective-permute-done.3.refs_5_), channel_id=1, source_target_pairs={{0,3},{1,2},{2,1},{3,0},{4,7},{5,6},{6,5},{7,4},{8,11},{9,10},{10,... | collective-permute-start | bytes 448520 | tf_op jit(solution)/shard_map/ppermute | solution.py:272
  15.1 1.2 %collective-permute-start.7 = (bf16[584,128]{1,0:T(8,128)(2,1)S(1)}, bf16[584,128]{1,0:T(8,128)(2,1)S(1)}, u32[]{:S(2)}, u32[]{:S(2)}) collective-permute-start(bf16[584,128]{1,0:T(8,128)(2,1)S(1)} %collective-permute-done.3.refs_5_), channel_id=1, source_target_pairs={{4,1},{5,0},{0,9},{1,8},{8,13},{9,12},{12,5},{13,4},{6,3},{7,2},{2... | collective-permute-start | bytes 448520 | tf_op jit(solution)/shard_map/ppermute | solution.py:269
  16.2 0.3 collective-permute-done.6.refs_2_
  16.5 0.4 %collective-permute-done.5.refs_0_ = bf16[584,128]{1,0:T(8,128)(2,1)S(1)} collective-permute-done((bf16[584,128]{1,0:T(8,128)(2,1)S(1)}, bf16[584,128]{1,0:T(8,128)(2,1)S(1)}, u32[]{:S(2)}, u32[]{:S(2)}) %collective-permute-start.5) | collective-permute-done | bytes 149536 | tf_op jit(solution)/shard_map/ppermute | solution.py:269
  16.9 1.2 %collective-permute-start.10 = (bf16[584,128]{1,0:T(8,128)(2,1)S(1)}, bf16[584,128]{1,0:T(8,128)(2,1)S(1)}, u32[]{:S(2)}, u32[]{:S(2)}) collective-permute-start(bf16[584,128]{1,0:T(8,128)(2,1)S(1)} %collective-permute-done.5.refs_0_), channel_id=1, source_target_pairs={{0,3},{1,2},{2,1},{3,0},{4,7},{5,6},{6,5},{7,4},{8,11},{9,10},{10,... | collective-permute-start | bytes 448520 | tf_op jit(solution)/shard_map/ppermute | solution.py:272
  18.0 3.4 %collective-permute-start.9 = (bf16[584,128]{1,0:T(8,128)(2,1)S(1)}, bf16[584,128]{1,0:T(8,128)(2,1)S(1)}, u32[]{:S(2)}, u32[]{:S(2)}) collective-permute-start(bf16[584,128]{1,0:T(8,128)(2,1)S(1)} %collective-permute-done.5.refs_0_), channel_id=1, source_target_pairs={{4,1},{5,0},{0,9},{1,8},{8,13},{9,12},{12,5},{13,4},{6,3},{7,2},{2... | collective-permute-start | bytes 448520 | tf_op jit(solution)/shard_map/ppermute | solution.py:269
  21.4 0.0 collective-permute-done.8.refs_3_
  21.4 0.0 collective-permute-done.7.refs_1_
  21.4 0.1 collective-permute-start.13
  21.6 2.6 %collective-permute-start.12 = (bf16[584,128]{1,0:T(8,128)(2,1)S(1)}, bf16[584,128]{1,0:T(8,128)(2,1)S(1)}, u32[]{:S(2)}, u32[]{:S(2)}) collective-permute-start(bf16[584,128]{1,0:T(8,128)(2,1)S(1)} %collective-permute-done.7.refs_1_), channel_id=1, source_target_pairs={{4,1},{5,0},{0,9},{1,8},{8,13},{9,12},{12,5},{13,4},{6,3},{7,2},{2... | collective-permute-start | bytes 448520 | tf_op jit(solution)/shard_map/ppermute | solution.py:269
  24.1 0.0 collective-permute-done.other
  24.1 1.5 %shard_map.39 = (f32[192,896]{1,0:T(8,128)S(1)}, f32[192,896]{1,0:T(8,128)S(1)}, f32[384,128]{1,0:T(8,128)S(1)}) custom-call(bf16[1160,128]{1,0:T(8,128)(2,1)S(1)} %get-tuple-element.36.own, bf16[1160,128]{1,0:T(8,128)(2,1)S(1)} %collective-permute-done.other, bf16[584,128]{1,0:T(8,128)(2,1)S(1)} %collective-permute-done.2.refs_0_, ...), custom_call_target="tpu_custom_call" | custom-call | tf_op jit(solution)/shard_map/pallas_call | solution.py:222
  25.6 0.0 collective-permute-done.10.refs_2_
  25.7 0.0 collective-permute-done.9.refs_4_
  25.7 1.7 %collective-permute-start.11 = (bf16[584,128]{1,0:T(8,128)(2,1)S(1)}, bf16[584,128]{1,0:T(8,128)(2,1)S(1)}, u32[]{:S(2)}, u32[]{:S(2)}) collective-permute-start(bf16[584,128]{1,0:T(8,128)(2,1)S(1)} %collective-permute-done.10.refs_2_), channel_id=1, source_target_pairs={{4,1},{5,0},{0,9},{1,8},{8,13},{9,12},{12,5},{13,4},{6,3},{7,2},{2... | collective-permute-start | bytes 448520 | tf_op jit(solution)/shard_map/ppermute | solution.py:269
  27.3 0.2 collective-permute-done.13.refs_3_
  27.5 0.8 %collective-permute-done.12.refs_5_ = bf16[584,128]{1,0:T(8,128)(2,1)S(1)} collective-permute-done((bf16[584,128]{1,0:T(8,128)(2,1)S(1)}, bf16[584,128]{1,0:T(8,128)(2,1)S(1)}, u32[]{:S(2)}, u32[]{:S(2)}) %collective-permute-start.12) | collective-permute-done | bytes 149536 | tf_op jit(solution)/shard_map/ppermute | solution.py:269
  28.3 0.7 %collective-permute-start.14 = (bf16[584,128]{1,0:T(8,128)(2,1)S(1)}, bf16[584,128]{1,0:T(8,128)(2,1)S(1)}, u32[]{:S(2)}, u32[]{:S(2)}) collective-permute-start(bf16[584,128]{1,0:T(8,128)(2,1)S(1)} %collective-permute-done.12.refs_5_), channel_id=1, source_target_pairs={{0,3},{1,2},{2,1},{3,0},{4,7},{5,6},{6,5},{7,4},{8,11},{9,10},{10,... | collective-permute-start | bytes 448520 | tf_op jit(solution)/shard_map/ppermute | solution.py:272
  29.0 1.4 %shard_map.40 = (f32[192,896]{1,0:T(8,128)S(1)}, bf16[64,896]{1,0:T(8,128)(2,1)S(1)}, bf16[64,896]{1,0:T(8,128)(2,1)S(1)}, bf16[64,896]{1,0:T(8,128)(2,1)S(1)}) custom-call(bf16[1160,128]{1,0:T(8,128)(2,1)S(1)} %get-tuple-element.36.own, bf16[1160,128]{1,0:T(8,128)(2,1)S(1)} %collective-permute-done.other, ...), custom_call_target="tpu_custom_call", output_to_operand_aliasing={{0}: (9, {})} | custom-call | tf_op jit(solution)/shard_map/pallas_call | solution.py:222
  30.5 0.4 %collective-permute-start.15 = (bf16[64,896]{1,0:T(8,128)(2,1)S(1)}, bf16[64,896]{1,0:T(8,128)(2,1)S(1)}, u32[]{:S(2)}, u32[]{:S(2)}) collective-permute-start(bf16[64,896]{1,0:T(8,128)(2,1)S(1)} %get-tuple-element.59), channel_id=1, source_target_pairs={{0,1},{1,0},{2,3},{3,2},{4,5},{5,4},{6,7},{7,6},{8,9},{9,8},{10,11... | collective-permute-start | bytes 344072 | tf_op jit(solution)/shard_map/ppermute | solution.py:275
  30.9 0.2 collective-permute-start.16
  31.0 0.4 %collective-permute-done.11.first = bf16[584,128]{1,0:T(8,128)(2,1)S(1)} collective-permute-done((bf16[584,128]{1,0:T(8,128)(2,1)S(1)}, bf16[584,128]{1,0:T(8,128)(2,1)S(1)}, u32[]{:S(2)}, u32[]{:S(2)}) %collective-permute-start.11) | collective-permute-done | bytes 149536 | tf_op jit(solution)/shard_map/ppermute | solution.py:269
  31.5 0.6 %collective-permute-start.17 = (bf16[64,896]{1,0:T(8,128)(2,1)S(1)}, bf16[64,896]{1,0:T(8,128)(2,1)S(1)}, u32[]{:S(2)}, u32[]{:S(2)}) collective-permute-start(bf16[64,896]{1,0:T(8,128)(2,1)S(1)} %get-tuple-element.61), channel_id=1, source_target_pairs={{0,1},{1,0},{2,3},{3,2},{4,5},{5,4},{6,7},{7,6},{8,9},{9,8},{10,11... | collective-permute-start | bytes 344072 | tf_op jit(solution)/shard_map/ppermute | solution.py:275
  32.0 0.0 collective-permute-start.18
  32.0 0.0 collective-permute-done.15.refs_0_
  32.0 0.2 collective-permute-done.16.refs_1_
  32.2 2.1 %collective-permute-done.14.second = bf16[584,128]{1,0:T(8,128)(2,1)S(1)} collective-permute-done((bf16[584,128]{1,0:T(8,128)(2,1)S(1)}, bf16[584,128]{1,0:T(8,128)(2,1)S(1)}, u32[]{:S(2)}, u32[]{:S(2)}) %collective-permute-start.14) | collective-permute-done | bytes 149536 | tf_op jit(solution)/shard_map/ppermute | solution.py:272
  34.3 0.0 collective-permute-done.17.refs_2_
  34.3 0.1 collective-permute-start.19
  34.4 0.0 collective-permute-done.18.first_other
  34.4 1.3 %collective-permute-done.19.second_other = bf16[584,128]{1,0:T(8,128)(2,1)S(1)} collective-permute-done((bf16[584,128]{1,0:T(8,128)(2,1)S(1)}, bf16[584,128]{1,0:T(8,128)(2,1)S(1)}, u32[]{:S(2)}, u32[]{:S(2)}) %collective-permute-start.19) | collective-permute-done | bytes 149536 | tf_op jit(solution)/shard_map/ppermute | solution.py:275
  35.7 1.5 %shard_map.41 = bf16[192,768]{1,0:T(8,128)(2,1)} custom-call(bf16[1160,128]{1,0:T(8,128)(2,1)S(1)} %get-tuple-element.36.own, f32[384,128]{1,0:T(8,128)S(1)} %get-tuple-element.45.info, bf16[584,128]{1,0:T(8,128)(2,1)S(1)} %collective-permute-done.11.first, bf16[584,128]{1,0:T(8,128)(2,1)S(1)} %collective-permute-done.14.second, ...), custom_call_target="tpu_custom_call" | custom-call | tf_op jit(solution)/shard_map/pallas_call | solution.py:222
  (1 shorter events, 0.0 us)
Async XLA Ops:
  0.0 1.0 %copy-start = (bf16[192,768]{1,0:T(8,128)(2,1)S(1)}, bf16[192,768]{1,0:T(8,128)(2,1)}, u32[]{:S(2)}) copy-start(bf16[192,768]{1,0:T(8,128)(2,1)} %rows.3) | copy-start | bytes 884740
  1.0 5.3 %copy-start.2 = (s32[192]{0:T(256)S(1)}, s32[192]{0:T(256)}, u32[]{:S(2)}) copy-start(s32[192]{0:T(256)} %param.5) | copy-start | bytes 2308
  1.0 8.0 %collective-permute-start.2 = (bf16[584,128]{1,0:T(8,128)(2,1)S(1)}, bf16[584,128]{1,0:T(8,128)(2,1)S(1)}, u32[]{:S(2)}, u32[]{:S(2)}) collective-permute-start(bf16[584,128]{1,0:T(8,128)(2,1)S(1)} %shard_map.38), channel_id=1, source_target_pairs={{0,3},{1,2},{2,1},{3,0},{4,7},{5,6},{6,5},{7,4},{8,11},{9,10},{10,... | collective-permute-start | bytes 448520 | tf_op jit(solution)/shard_map/ppermute | solution.py:272
  3.4 6.7 %collective-permute-start.1 = (bf16[584,128]{1,0:T(8,128)(2,1)S(1)}, bf16[584,128]{1,0:T(8,128)(2,1)S(1)}, u32[]{:S(2)}, u32[]{:S(2)}) collective-permute-start(bf16[584,128]{1,0:T(8,128)(2,1)S(1)} %shard_map.38), channel_id=1, source_target_pairs={{4,1},{5,0},{0,9},{1,8},{8,13},{9,12},{12,5},{13,4},{6,3},{7,2},{2... | collective-permute-start | bytes 448520 | tf_op jit(solution)/shard_map/ppermute | solution.py:269
  6.3 0.7 %copy-start.1 = (s32[192,1]{0,1:T(1,128)S(1)}, s32[192,1]{0,1:T(1,128)}, u32[]{:S(2)}) copy-start(s32[192,1]{0,1:T(1,128)} %param.4) | copy-start | bytes 2308
  7.1 6.2 %collective-permute-start.4 = (bf16[584,128]{1,0:T(8,128)(2,1)S(1)}, bf16[584,128]{1,0:T(8,128)(2,1)S(1)}, u32[]{:S(2)}, u32[]{:S(2)}) collective-permute-start(bf16[584,128]{1,0:T(8,128)(2,1)S(1)} %get-tuple-element.38), channel_id=1, source_target_pairs={{0,3},{1,2},{2,1},{3,0},{4,7},{5,6},{6,5},{7,4},{8,11},{9,10},{10,... | collective-permute-start | bytes 448520 | tf_op jit(solution)/shard_map/ppermute | solution.py:272
  7.2 6.1 %collective-permute-start.3 = (bf16[584,128]{1,0:T(8,128)(2,1)S(1)}, bf16[584,128]{1,0:T(8,128)(2,1)S(1)}, u32[]{:S(2)}, u32[]{:S(2)}) collective-permute-start(bf16[584,128]{1,0:T(8,128)(2,1)S(1)} %get-tuple-element.38), channel_id=1, source_target_pairs={{4,1},{5,0},{0,9},{1,8},{8,13},{9,12},{12,5},{13,4},{6,3},{7,2},{2... | collective-permute-start | bytes 448520 | tf_op jit(solution)/shard_map/ppermute | solution.py:269
  10.1 6.4 %collective-permute-start.6 = (bf16[584,128]{1,0:T(8,128)(2,1)S(1)}, bf16[584,128]{1,0:T(8,128)(2,1)S(1)}, u32[]{:S(2)}, u32[]{:S(2)}) collective-permute-start(bf16[584,128]{1,0:T(8,128)(2,1)S(1)} %collective-permute-done.1.refs_4_), channel_id=1, source_target_pairs={{0,3},{1,2},{2,1},{3,0},{4,7},{5,6},{6,5},{7,4},{8,11},{9,10},{10,... | collective-permute-start | bytes 448520 | tf_op jit(solution)/shard_map/ppermute | solution.py:272
  10.1 6.8 %collective-permute-start.5 = (bf16[584,128]{1,0:T(8,128)(2,1)S(1)}, bf16[584,128]{1,0:T(8,128)(2,1)S(1)}, u32[]{:S(2)}, u32[]{:S(2)}) collective-permute-start(bf16[584,128]{1,0:T(8,128)(2,1)S(1)} %collective-permute-done.1.refs_4_), channel_id=1, source_target_pairs={{4,1},{5,0},{0,9},{1,8},{8,13},{9,12},{12,5},{13,4},{6,3},{7,2},{2... | collective-permute-start | bytes 448520 | tf_op jit(solution)/shard_map/ppermute | solution.py:269
  13.2 10.9 %collective-permute-start = (bf16[1160,128]{1,0:T(8,128)(2,1)S(1)}, bf16[1160,128]{1,0:T(8,128)(2,1)S(1)}, u32[]{:S(2)}, u32[]{:S(2)}) collective-permute-start(bf16[1160,128]{1,0:T(8,128)(2,1)S(1)} %get-tuple-element.36.own), channel_id=1, source_target_pairs={{0,1},{1,0},{2,3},{3,2},{4,5},{5,4},{6,7},{7,6},{8,9},{9,8},{10,11... | collective-permute-start | bytes 890888 | tf_op jit(solution)/shard_map/ppermute | solution.py:275
  13.3 8.1 %collective-permute-start.8 = (bf16[584,128]{1,0:T(8,128)(2,1)S(1)}, bf16[584,128]{1,0:T(8,128)(2,1)S(1)}, u32[]{:S(2)}, u32[]{:S(2)}) collective-permute-start(bf16[584,128]{1,0:T(8,128)(2,1)S(1)} %collective-permute-done.3.refs_5_), channel_id=1, source_target_pairs={{0,3},{1,2},{2,1},{3,0},{4,7},{5,6},{6,5},{7,4},{8,11},{9,10},{10,... | collective-permute-start | bytes 448520 | tf_op jit(solution)/shard_map/ppermute | solution.py:272
  15.1 6.4 %collective-permute-start.7 = (bf16[584,128]{1,0:T(8,128)(2,1)S(1)}, bf16[584,128]{1,0:T(8,128)(2,1)S(1)}, u32[]{:S(2)}, u32[]{:S(2)}) collective-permute-start(bf16[584,128]{1,0:T(8,128)(2,1)S(1)} %collective-permute-done.3.refs_5_), channel_id=1, source_target_pairs={{4,1},{5,0},{0,9},{1,8},{8,13},{9,12},{12,5},{13,4},{6,3},{7,2},{2... | collective-permute-start | bytes 448520 | tf_op jit(solution)/shard_map/ppermute | solution.py:269
  16.9 8.8 %collective-permute-start.10 = (bf16[584,128]{1,0:T(8,128)(2,1)S(1)}, bf16[584,128]{1,0:T(8,128)(2,1)S(1)}, u32[]{:S(2)}, u32[]{:S(2)}) collective-permute-start(bf16[584,128]{1,0:T(8,128)(2,1)S(1)} %collective-permute-done.5.refs_0_), channel_id=1, source_target_pairs={{0,3},{1,2},{2,1},{3,0},{4,7},{5,6},{6,5},{7,4},{8,11},{9,10},{10,... | collective-permute-start | bytes 448520 | tf_op jit(solution)/shard_map/ppermute | solution.py:272
  18.0 7.6 %collective-permute-start.9 = (bf16[584,128]{1,0:T(8,128)(2,1)S(1)}, bf16[584,128]{1,0:T(8,128)(2,1)S(1)}, u32[]{:S(2)}, u32[]{:S(2)}) collective-permute-start(bf16[584,128]{1,0:T(8,128)(2,1)S(1)} %collective-permute-done.5.refs_0_), channel_id=1, source_target_pairs={{4,1},{5,0},{0,9},{1,8},{8,13},{9,12},{12,5},{13,4},{6,3},{7,2},{2... | collective-permute-start | bytes 448520 | tf_op jit(solution)/shard_map/ppermute | solution.py:269
  21.4 6.1 %collective-permute-start.13 = (bf16[584,128]{1,0:T(8,128)(2,1)S(1)}, bf16[584,128]{1,0:T(8,128)(2,1)S(1)}, u32[]{:S(2)}, u32[]{:S(2)}) collective-permute-start(bf16[584,128]{1,0:T(8,128)(2,1)S(1)} %collective-permute-done.7.refs_1_), channel_id=1, source_target_pairs={{0,3},{1,2},{2,1},{3,0},{4,7},{5,6},{6,5},{7,4},{8,11},{9,10},{10,... | collective-permute-start | bytes 448520 | tf_op jit(solution)/shard_map/ppermute | solution.py:272
  21.6 6.7 %collective-permute-start.12 = (bf16[584,128]{1,0:T(8,128)(2,1)S(1)}, bf16[584,128]{1,0:T(8,128)(2,1)S(1)}, u32[]{:S(2)}, u32[]{:S(2)}) collective-permute-start(bf16[584,128]{1,0:T(8,128)(2,1)S(1)} %collective-permute-done.7.refs_1_), channel_id=1, source_target_pairs={{4,1},{5,0},{0,9},{1,8},{8,13},{9,12},{12,5},{13,4},{6,3},{7,2},{2... | collective-permute-start | bytes 448520 | tf_op jit(solution)/shard_map/ppermute | solution.py:269
  25.7 5.8 %collective-permute-start.11 = (bf16[584,128]{1,0:T(8,128)(2,1)S(1)}, bf16[584,128]{1,0:T(8,128)(2,1)S(1)}, u32[]{:S(2)}, u32[]{:S(2)}) collective-permute-start(bf16[584,128]{1,0:T(8,128)(2,1)S(1)} %collective-permute-done.10.refs_2_), channel_id=1, source_target_pairs={{4,1},{5,0},{0,9},{1,8},{8,13},{9,12},{12,5},{13,4},{6,3},{7,2},{2... | collective-permute-start | bytes 448520 | tf_op jit(solution)/shard_map/ppermute | solution.py:269
  28.3 6.0 %collective-permute-start.14 = (bf16[584,128]{1,0:T(8,128)(2,1)S(1)}, bf16[584,128]{1,0:T(8,128)(2,1)S(1)}, u32[]{:S(2)}, u32[]{:S(2)}) collective-permute-start(bf16[584,128]{1,0:T(8,128)(2,1)S(1)} %collective-permute-done.12.refs_5_), channel_id=1, source_target_pairs={{0,3},{1,2},{2,1},{3,0},{4,7},{5,6},{6,5},{7,4},{8,11},{9,10},{10,... | collective-permute-start | bytes 448520 | tf_op jit(solution)/shard_map/ppermute | solution.py:272
  30.5 1.6 %collective-permute-start.15 = (bf16[64,896]{1,0:T(8,128)(2,1)S(1)}, bf16[64,896]{1,0:T(8,128)(2,1)S(1)}, u32[]{:S(2)}, u32[]{:S(2)}) collective-permute-start(bf16[64,896]{1,0:T(8,128)(2,1)S(1)} %get-tuple-element.59), channel_id=1, source_target_pairs={{0,1},{1,0},{2,3},{3,2},{4,5},{5,4},{6,7},{7,6},{8,9},{9,8},{10,11... | collective-permute-start | bytes 344072 | tf_op jit(solution)/shard_map/ppermute | solution.py:275
  30.9 1.3 %collective-permute-start.16 = (bf16[64,896]{1,0:T(8,128)(2,1)S(1)}, bf16[64,896]{1,0:T(8,128)(2,1)S(1)}, u32[]{:S(2)}, u32[]{:S(2)}) collective-permute-start(bf16[64,896]{1,0:T(8,128)(2,1)S(1)} %get-tuple-element.60), channel_id=1, source_target_pairs={{0,1},{1,0},{2,3},{3,2},{4,5},{5,4},{6,7},{7,6},{8,9},{9,8},{10,11... | collective-permute-start | bytes 344072 | tf_op jit(solution)/shard_map/ppermute | solution.py:275
  31.5 2.9 %collective-permute-start.17 = (bf16[64,896]{1,0:T(8,128)(2,1)S(1)}, bf16[64,896]{1,0:T(8,128)(2,1)S(1)}, u32[]{:S(2)}, u32[]{:S(2)}) collective-permute-start(bf16[64,896]{1,0:T(8,128)(2,1)S(1)} %get-tuple-element.61), channel_id=1, source_target_pairs={{0,1},{1,0},{2,3},{3,2},{4,5},{5,4},{6,7},{7,6},{8,9},{9,8},{10,11... | collective-permute-start | bytes 344072 | tf_op jit(solution)/shard_map/ppermute | solution.py:275
  32.0 2.4 %collective-permute-start.18 = (bf16[584,128]{1,0:T(8,128)(2,1)S(1)}, bf16[584,128]{1,0:T(8,128)(2,1)S(1)}, u32[]{:S(2)}, u32[]{:S(2)}) collective-permute-start(bf16[584,128]{1,0:T(8,128)(2,1)S(1)} %collective-permute-done.11.first), channel_id=1, source_target_pairs={{0,1},{1,0},{2,3},{3,2},{4,5},{5,4},{6,7},{7,6},{8,9},{9,8},{10,11... | collective-permute-start | bytes 448520 | tf_op jit(solution)/shard_map/ppermute | solution.py:275
  34.3 1.4 %collective-permute-start.19 = (bf16[584,128]{1,0:T(8,128)(2,1)S(1)}, bf16[584,128]{1,0:T(8,128)(2,1)S(1)}, u32[]{:S(2)}, u32[]{:S(2)}) collective-permute-start(bf16[584,128]{1,0:T(8,128)(2,1)S(1)} %collective-permute-done.14.second), channel_id=1, source_target_pairs={{0,1},{1,0},{2,3},{3,2},{4,5},{5,4},{6,7},{7,6},{8,9},{9,8},{10,11... | collective-permute-start | bytes 448520 | tf_op jit(solution)/shard_map/ppermute | solution.py:275

commit v19 on v18

--- a/solution.py
+++ b/solution.py
@@ -77,34 +77,37 @@
     return lax.rsqrt(jnp.sum(wide * wide, axis=1, keepdims=True) + 1e-06)
 
 
+def first_rows(rows_here):
+    return rows_here * 7 // 192 * 16
+
+
 def first_pack_kernel(rows, first):
-    width = rows.shape[1]
-    slabs = width // 128
-    half = rows.shape[0] // 2
-    for slab in range(slabs):
-        first[slab * half : (slab + 1) * half, :] = rows[:half, slab * 128 : (slab + 1) * 128]
-    first[slabs * half :, :] = jnp.zeros((8, 128), BF16)
+    cut = first_rows(rows.shape[0])
+    for slab in range(rows.shape[1] // 128):
+        first[slab * cut : (slab + 1) * cut, :] = rows[:cut, slab * 128 : (slab + 1) * 128]
 
 
 def pack_kernel(rows, group, cluster, whole, second):
     rows_here, width = rows.shape
     slabs = width // 128
-    half = rows_here // 2
+    cut = first_rows(rows_here)
+    rest = rows_here - cut
     for slab in range(slabs):
         columns = rows[:, slab * 128 : (slab + 1) * 128]
         whole[slab * rows_here : (slab + 1) * rows_here, :] = columns
-        second[slab * half : (slab + 1) * half, :] = columns[half:]
+        second[slab * rest : (slab + 1) * rest, :] = columns[cut:]
     line_at = lax.broadcasted_iota(jnp.int32, (8, 128), 0)
     named = jnp.zeros((8, 128), jnp.int32)
     for line in range(4):
-        top = line % 2 * half
-        part = (group, cluster)[line // 2][:, top : top + half]
-        if half < 128:
-            part = jnp.concatenate([part, jnp.zeros((1, 128 - half), jnp.int32)], axis=1)
+        top = line % 2 * 128
+        part = (group, cluster)[line // 2][:, top : top + 128]
+        gap = 128 - part.shape[1]
+        if gap:
+            part = jnp.concatenate([part, jnp.zeros((1, gap), jnp.int32)], axis=1)
         named = jnp.where(line_at == line, part, named)
     named = named.astype(F32).astype(BF16)
     whole[slabs * rows_here :, :] = named
-    second[slabs * half :, :] = named
+    second[slabs * rest :, :] = named
 
 
 def from_slabs(ref, count):
@@ -112,18 +115,16 @@
     return jnp.concatenate(slabs, axis=1)
 
 
-def key_rows(ref, half):
+def key_row(ref, rows_here):
     wide = ref[ref.shape[0] - 8 :, :].astype(F32)
-    return [wide[side : side + 1, :half] * 256.0 + wide[side + 2 : side + 3, :half] for side in range(2)]
-
-
-def key_row(ref, rows_here):
-    return jnp.concatenate(key_rows(ref, rows_here // 2), axis=1)
-
-
-def from_halves(first, second, rows_here):
-    half = rows_here // 2
-    rows = jnp.concatenate([from_slabs(first, half), from_slabs(second, half)], axis=0)
+    kinds = [jnp.concatenate([wide[at : at + 1], wide[at + 1 : at + 2]], axis=1) for at in (0, 2)]
+    return (kinds[0] * 256.0 + kinds[1])[:, :rows_here]
+
+
+def from_pieces(first, second, rows_here):
+    cut = first_rows(rows_here)
+    pieces = [from_slabs(first, cut), from_slabs(second, rows_here - cut)]
+    rows = jnp.concatenate(pieces, axis=0)
     return rows, key_row(second, rows_here)
 
 
@@ -152,7 +153,7 @@
 def take_blocks(refs, count, rows_here):
     blocks = []
     for _ in range(count):
-        rows, key = from_halves(refs.pop(0), refs.pop(0), rows_here)
+        rows, key = from_pieces(refs.pop(0), refs.pop(0), rows_here)
         blocks.append((rows, key, to_row(scale_column(rows))))
     return blocks
 
@@ -218,7 +219,7 @@
     return [pl.BlockSpec(memory_space=pltpu.VMEM)] * count
 
 
-def call(kernel, shapes, args, aliases={}):
+def call(kernel, shapes, args, aliases={}, products=0):
     return pl.pallas_call(
         kernel,
         out_shape=[jax.ShapeDtypeStruct(shape, dtype) for shape, dtype in shapes],
@@ -226,22 +227,29 @@
         out_specs=whole_in_vmem(len(shapes)),
         input_output_aliases=aliases,
         compiler_params=pltpu.CompilerParams(vmem_limit_bytes=VMEM_BYTES),
+        cost_estimate=pl.CostEstimate(
+            flops=3 * products, transcendentals=0, bytes_accessed=0
+        ),
     )(*args)
 
 
 def start_both(left, right, shape):
     rows_here = shape[0]
-    args = list(left) + [half for block in right for half in block]
+    args = list(left) + [piece for block in right for piece in block]
     shapes = [(shape, F32), (shape, F32), ((2 * rows_here, 128), F32)]
-    return call(functools.partial(start_kernel, len(right)), shapes, args)
+    products = 4 * rows_here * (len(right) + 1) * rows_here * (shape[1] - 128)
+    return call(
+        functools.partial(start_kernel, len(right)), shapes, args, products=products
+    )
 
 
 def add_both(left, right, before):
-    args = list(left) + [half for block in right for half in block] + list(before)
+    args = list(left) + [piece for block in right for piece in block] + list(before)
     rows_here, wide = before[0].shape
     shapes = [((rows_here, wide), F32)] + [((rows_here // PARTS, wide), BF16)] * PARTS
     kernel = functools.partial(both_kernel, len(right))
-    return call(kernel, shapes, args, {len(args) - 2: 0})
+    products = 4 * rows_here * len(right) * rows_here * (wide - 128)
+    return call(kernel, shapes, args, {len(args) - 2: 0}, products)
 
 
 def folded_ring(size):
@@ -254,7 +262,7 @@
 
 def by_block(embeddings, group_of, cluster_id):
     rows_here, width = embeddings.shape
-    half = rows_here // 2
+    cut = first_rows(rows_here)
     slabs = width // 128
     n_blk = lax.axis_size("blk")
     order = folded_ring(n_blk)
@@ -274,11 +282,13 @@
     def other_core(rows):
         return lax.ppermute(rows, "pair", [(0, 1), (1, 0)])
 
-    half_shape = ((slabs * half + 8, 128), BF16)
-    (first,) = call(first_pack_kernel, [half_shape], [embeddings])
+    (first,) = call(first_pack_kernel, [((slabs * cut, 128), BF16)], [embeddings])
     whole, second = call(
         pack_kernel,
-        [((slabs * rows_here + 8, 128), BF16), half_shape],
+        [
+            ((slabs * rows_here + 8, 128), BF16),
+            ((slabs * (rows_here - cut) + 8, 128), BF16),
+        ],
         [embeddings, group_of.reshape(line), cluster_id.reshape(line)],
     )
     along_by = [(first, second)]
@@ -306,7 +316,8 @@
     (out,) = call(
         last_kernel,
         [((rows_here, width), BF16)],
-        [whole, info, *last, *[other_core(half) for half in last], mine, *back],
+        [whole, info, *last, *[other_core(piece) for piece in last], mine, *back],
+        products=4 * rows_here * rows_here * width,
     )
     return out
 

time: 37.3 us -> 37.6 us (level)
  starting transfers between devices: 24.1 us -> 25.1 us
  waiting for transfers between devices: 6.83 us -> 6.07 us
    ppermute x7, waiting for transfers between devices: 2.62 us -> 0.9 us  [across(): return lax.ppermute(rows, ('sub', 'pair'), [(0, 3), (1, 2), (2, 1), (3, 0)])]
    ppermute x7, waiting for transfers between devices: 2.78 us -> 3.83 us  [along(): return lax.ppermute(rows, ('blk', 'pair'), hops)]
    ppermute x7, starting transfers between devices: 6.34 us -> 7 us  [across(): return lax.ppermute(rows, ('sub', 'pair'), [(0, 3), (1, 2), (2, 1), (3, 0)])]
where the time goes in v19:
time: 37.6 us; the launch traced here: 37.5 us
  starting transfers between devices  25.1 us (67%)
  waiting for transfers between devices  6.07 us (16%)
  Pallas kernels  4.55 us (12%)
  local copies, waits for them, and re-layouts  1.64 us (4%)
    ppermute x7, starting transfers between devices, along(): return lax.ppermute(rows, ('blk', 'pair'), hops)  16.8 us
    ppermute x7, starting transfers between devices, across(): return lax.ppermute(rows, ('sub', 'pair'), [(0, 3), (1, 2), (2, 1), (3, 0)])  7 us
    pallas_call x5, Pallas kernels, call(): pl.pallas_call(kernel, out_shape=[jax.ShapeDtypeStruct(shape, dtype) for...  4.55 us
    ppermute x7, waiting for transfers between devices, along(): return lax.ppermute(rows, ('blk', 'pair'), hops)  3.83 us
    unnamed x6, local copies, waits for them, and re-layouts  1.64 us
    ppermute x6, waiting for transfers between devices, other_core(): return lax.ppermute(rows, 'pair', [(0, 1), (1, 0)])  1.34 us
    ppermute x6, starting transfers between devices, other_core(): return lax.ppermute(rows, 'pair', [(0, 1), (1, 0)])  1.3 us
    ppermute x7, waiting for transfers between devices, across(): return lax.ppermute(rows, ('sub', 'pair'), [(0, 3), (1, 2), (2, 1), (3, 0)])  0.9 us
  transfers between devices with their start and end apart: 20, of which 9 were waited for; matrix products, arithmetic and copies ran while one was open for 0% of the time, Pallas kernels for 8%

profile of v19, /device:TPU:0, one launch (start us, length us, event | category | flops | bytes accessed | tf_op | source)
XLA Modules:
  0.0 37.5 jit_solution(8022136708753709988)
XLA Ops:
  0.0 0.0 copy-start
  0.0 1.0 %copy-done = bf16[192,768]{1,0:T(8,128)(2,1)S(1)} copy-done((bf16[192,768]{1,0:T(8,128)(2,1)S(1)}, bf16[192,768]{1,0:T(8,128)(2,1)}, u32[]{:S(2)}) %copy-start) | copy-done | bytes 294936
  1.0 0.0 copy-start.2
  1.0 2.4 %collective-permute-start.2 = (bf16[672,128]{1,0:T(8,128)(2,1)S(1)}, bf16[672,128]{1,0:T(8,128)(2,1)S(1)}, u32[]{:S(2)}, u32[]{:S(2)}) collective-permute-start(bf16[672,128]{1,0:T(8,128)(2,1)S(1)} %shard_map.38), channel_id=1, source_target_pairs={{0,3},{1,2},{2,1},{3,0},{4,7},{5,6},{6,5},{7,4},{8,11},{9,10},{10,... | collective-permute-start | bytes 516104 | tf_op jit(solution)/shard_map/ppermute | solution.py:280
  3.4 2.9 %collective-permute-start.1 = (bf16[672,128]{1,0:T(8,128)(2,1)S(1)}, bf16[672,128]{1,0:T(8,128)(2,1)S(1)}, u32[]{:S(2)}, u32[]{:S(2)}) collective-permute-start(bf16[672,128]{1,0:T(8,128)(2,1)S(1)} %shard_map.38), channel_id=1, source_target_pairs={{4,1},{5,0},{0,9},{1,8},{8,13},{9,12},{12,5},{13,4},{6,3},{7,2},{2... | collective-permute-start | bytes 516104 | tf_op jit(solution)/shard_map/ppermute | solution.py:277
  6.3 0.0 copy-start.1
  6.3 0.0 copy-done.2
  6.3 0.7 %copy-done.1 = s32[192,1]{0,1:T(1,128)S(1)} copy-done((s32[192,1]{0,1:T(1,128)S(1)}, s32[192,1]{0,1:T(1,128)}, u32[]{:S(2)}) %copy-start.1) | copy-done | bytes 792
  7.0 0.1 shard_map.37
  7.1 0.1 collective-permute-start
  7.1 0.7 %collective-permute-start.4 = (bf16[488,128]{1,0:T(8,128)(2,1)S(1)}, bf16[488,128]{1,0:T(8,128)(2,1)S(1)}, u32[]{:S(2)}, u32[]{:S(2)}) collective-permute-start(bf16[488,128]{1,0:T(8,128)(2,1)S(1)} %get-tuple-element.38), channel_id=1, source_target_pairs={{0,3},{1,2},{2,1},{3,0},{4,7},{5,6},{6,5},{7,4},{8,11},{9,10},{10,... | collective-permute-start | bytes 374792 | tf_op jit(solution)/shard_map/ppermute | solution.py:280
  7.8 1.2 %collective-permute-start.3 = (bf16[488,128]{1,0:T(8,128)(2,1)S(1)}, bf16[488,128]{1,0:T(8,128)(2,1)S(1)}, u32[]{:S(2)}, u32[]{:S(2)}) collective-permute-start(bf16[488,128]{1,0:T(8,128)(2,1)S(1)} %get-tuple-element.38), channel_id=1, source_target_pairs={{4,1},{5,0},{0,9},{1,8},{8,13},{9,12},{12,5},{13,4},{6,3},{7,2},{2... | collective-permute-start | bytes 374792 | tf_op jit(solution)/shard_map/ppermute | solution.py:277
  9.0 0.0 collective-permute-done.2.refs_0_
  9.0 1.5 %collective-permute-done.1.refs_4_ = bf16[672,128]{1,0:T(8,128)(2,1)S(1)} collective-permute-done((bf16[672,128]{1,0:T(8,128)(2,1)S(1)}, bf16[672,128]{1,0:T(8,128)(2,1)S(1)}, u32[]{:S(2)}, u32[]{:S(2)}) %collective-permute-start.1) | collective-permute-done | bytes 172064 | tf_op jit(solution)/shard_map/ppermute | solution.py:277
  10.5 0.1 collective-permute-start.6
  10.6 3.0 %collective-permute-start.5 = (bf16[672,128]{1,0:T(8,128)(2,1)S(1)}, bf16[672,128]{1,0:T(8,128)(2,1)S(1)}, u32[]{:S(2)}, u32[]{:S(2)}) collective-permute-start(bf16[672,128]{1,0:T(8,128)(2,1)S(1)} %collective-permute-done.1.refs_4_), channel_id=1, source_target_pairs={{4,1},{5,0},{0,9},{1,8},{8,13},{9,12},{12,5},{13,4},{6,3},{7,2},{2... | collective-permute-start | bytes 516104 | tf_op jit(solution)/shard_map/ppermute | solution.py:277
  13.6 0.0 collective-permute-done.4.refs_1_
  13.6 0.0 collective-permute-done.3.refs_5_
  13.6 1.7 %collective-permute-start.8 = (bf16[488,128]{1,0:T(8,128)(2,1)S(1)}, bf16[488,128]{1,0:T(8,128)(2,1)S(1)}, u32[]{:S(2)}, u32[]{:S(2)}) collective-permute-start(bf16[488,128]{1,0:T(8,128)(2,1)S(1)} %collective-permute-done.3.refs_5_), channel_id=1, source_target_pairs={{0,3},{1,2},{2,1},{3,0},{4,7},{5,6},{6,5},{7,4},{8,11},{9,10},{10,... | collective-permute-start | bytes 374792 | tf_op jit(solution)/shard_map/ppermute | solution.py:280
  15.4 1.6 %collective-permute-start.7 = (bf16[488,128]{1,0:T(8,128)(2,1)S(1)}, bf16[488,128]{1,0:T(8,128)(2,1)S(1)}, u32[]{:S(2)}, u32[]{:S(2)}) collective-permute-start(bf16[488,128]{1,0:T(8,128)(2,1)S(1)} %collective-permute-done.3.refs_5_), channel_id=1, source_target_pairs={{4,1},{5,0},{0,9},{1,8},{8,13},{9,12},{12,5},{13,4},{6,3},{7,2},{2... | collective-permute-start | bytes 374792 | tf_op jit(solution)/shard_map/ppermute | solution.py:277
  16.9 0.2 collective-permute-done.6.refs_2_
  17.2 1.1 %collective-permute-done.5.refs_0_ = bf16[672,128]{1,0:T(8,128)(2,1)S(1)} collective-permute-done((bf16[672,128]{1,0:T(8,128)(2,1)S(1)}, bf16[672,128]{1,0:T(8,128)(2,1)S(1)}, u32[]{:S(2)}, u32[]{:S(2)}) %collective-permute-start.5) | collective-permute-done | bytes 172064 | tf_op jit(solution)/shard_map/ppermute | solution.py:277
  18.2 1.1 %collective-permute-start.10 = (bf16[672,128]{1,0:T(8,128)(2,1)S(1)}, bf16[672,128]{1,0:T(8,128)(2,1)S(1)}, u32[]{:S(2)}, u32[]{:S(2)}) collective-permute-start(bf16[672,128]{1,0:T(8,128)(2,1)S(1)} %collective-permute-done.5.refs_0_), channel_id=1, source_target_pairs={{0,3},{1,2},{2,1},{3,0},{4,7},{5,6},{6,5},{7,4},{8,11},{9,10},{10,... | collective-permute-start | bytes 516104 | tf_op jit(solution)/shard_map/ppermute | solution.py:280
  19.4 3.4 %collective-permute-start.9 = (bf16[672,128]{1,0:T(8,128)(2,1)S(1)}, bf16[672,128]{1,0:T(8,128)(2,1)S(1)}, u32[]{:S(2)}, u32[]{:S(2)}) collective-permute-start(bf16[672,128]{1,0:T(8,128)(2,1)S(1)} %collective-permute-done.5.refs_0_), channel_id=1, source_target_pairs={{4,1},{5,0},{0,9},{1,8},{8,13},{9,12},{12,5},{13,4},{6,3},{7,2},{2... | collective-permute-start | bytes 516104 | tf_op jit(solution)/shard_map/ppermute | solution.py:277
  22.7 0.0 collective-permute-done.8.refs_3_
  22.7 0.0 collective-permute-done.7.refs_1_
  22.8 0.3 collective-permute-start.13
  23.1 2.0 %collective-permute-start.12 = (bf16[488,128]{1,0:T(8,128)(2,1)S(1)}, bf16[488,128]{1,0:T(8,128)(2,1)S(1)}, u32[]{:S(2)}, u32[]{:S(2)}) collective-permute-start(bf16[488,128]{1,0:T(8,128)(2,1)S(1)} %collective-permute-done.7.refs_1_), channel_id=1, source_target_pairs={{4,1},{5,0},{0,9},{1,8},{8,13},{9,12},{12,5},{13,4},{6,3},{7,2},{2... | collective-permute-start | bytes 374792 | tf_op jit(solution)/shard_map/ppermute | solution.py:277
  25.1 0.0 collective-permute-done.other
  25.1 1.6 %shard_map.39 = (f32[192,896]{1,0:T(8,128)S(1)}, f32[192,896]{1,0:T(8,128)S(1)}, f32[384,128]{1,0:T(8,128)S(1)}) custom-call(bf16[1160,128]{1,0:T(8,128)(2,1)S(1)} %get-tuple-element.36.own, bf16[1160,128]{1,0:T(8,128)(2,1)S(1)} %collective-permute-done.other, bf16[672,128]{1,0:T(8,128)(2,1)S(1)} %collective-permute-done.2.refs_0_, ...), custom_call_target="tpu_custom_call" | custom-call | flops 1358954496 | tf_op jit(solution)/shard_map/pallas_call | solution.py:223
  26.7 0.0 collective-permute-done.10.refs_2_
  26.7 0.6 %collective-permute-done.9.refs_4_ = bf16[672,128]{1,0:T(8,128)(2,1)S(1)} collective-permute-done((bf16[672,128]{1,0:T(8,128)(2,1)S(1)}, bf16[672,128]{1,0:T(8,128)(2,1)S(1)}, u32[]{:S(2)}, u32[]{:S(2)}) %collective-permute-start.9) | collective-permute-done | bytes 172064 | tf_op jit(solution)/shard_map/ppermute | solution.py:277
  27.3 2.8 %collective-permute-start.11 = (bf16[672,128]{1,0:T(8,128)(2,1)S(1)}, bf16[672,128]{1,0:T(8,128)(2,1)S(1)}, u32[]{:S(2)}, u32[]{:S(2)}) collective-permute-start(bf16[672,128]{1,0:T(8,128)(2,1)S(1)} %collective-permute-done.10.refs_2_), channel_id=1, source_target_pairs={{4,1},{5,0},{0,9},{1,8},{8,13},{9,12},{12,5},{13,4},{6,3},{7,2},{2... | collective-permute-start | bytes 516104 | tf_op jit(solution)/shard_map/ppermute | solution.py:277
  30.0 0.0 collective-permute-done.13.refs_3_
  30.0 0.0 collective-permute-done.12.refs_5_
  30.1 0.6 %collective-permute-start.14 = (bf16[488,128]{1,0:T(8,128)(2,1)S(1)}, bf16[488,128]{1,0:T(8,128)(2,1)S(1)}, u32[]{:S(2)}, u32[]{:S(2)}) collective-permute-start(bf16[488,128]{1,0:T(8,128)(2,1)S(1)} %collective-permute-done.12.refs_5_), channel_id=1, source_target_pairs={{0,3},{1,2},{2,1},{3,0},{4,7},{5,6},{6,5},{7,4},{8,11},{9,10},{10,... | collective-permute-start | bytes 374792 | tf_op jit(solution)/shard_map/ppermute | solution.py:280
  30.7 1.4 %shard_map.40 = (f32[192,896]{1,0:T(8,128)S(1)}, bf16[64,896]{1,0:T(8,128)(2,1)S(1)}, bf16[64,896]{1,0:T(8,128)(2,1)S(1)}, bf16[64,896]{1,0:T(8,128)(2,1)S(1)}) custom-call(bf16[1160,128]{1,0:T(8,128)(2,1)S(1)} %get-tuple-element.36.own, bf16[1160,128]{1,0:T(8,128)(2,1)S(1)} %collective-permute-done.other, ...), custom_call_target="tpu_custom_call", output_to_operand_aliasing={{0}: (9, {})} | custom-call | flops 1019215872 | tf_op jit(solution)/shard_map/pallas_call | solution.py:223
  32.1 0.1 collective-permute-start.15
  32.1 0.5 %collective-permute-start.16 = (bf16[64,896]{1,0:T(8,128)(2,1)S(1)}, bf16[64,896]{1,0:T(8,128)(2,1)S(1)}, u32[]{:S(2)}, u32[]{:S(2)}) collective-permute-start(bf16[64,896]{1,0:T(8,128)(2,1)S(1)} %get-tuple-element.60), channel_id=1, source_target_pairs={{0,1},{1,0},{2,3},{3,2},{4,5},{5,4},{6,7},{7,6},{8,9},{9,8},{10,11... | collective-permute-start | bytes 344072 | tf_op jit(solution)/shard_map/ppermute | solution.py:283
  32.6 0.7 %collective-permute-done.11.first = bf16[672,128]{1,0:T(8,128)(2,1)S(1)} collective-permute-done((bf16[672,128]{1,0:T(8,128)(2,1)S(1)}, bf16[672,128]{1,0:T(8,128)(2,1)S(1)}, u32[]{:S(2)}, u32[]{:S(2)}) %collective-permute-start.11) | collective-permute-done | bytes 172064 | tf_op jit(solution)/shard_map/ppermute | solution.py:277
  33.3 0.0 collective-permute-start.17
  33.3 0.5 %collective-permute-start.18 = (bf16[672,128]{1,0:T(8,128)(2,1)S(1)}, bf16[672,128]{1,0:T(8,128)(2,1)S(1)}, u32[]{:S(2)}, u32[]{:S(2)}) collective-permute-start(bf16[672,128]{1,0:T(8,128)(2,1)S(1)} %collective-permute-done.11.first), channel_id=1, source_target_pairs={{0,1},{1,0},{2,3},{3,2},{4,5},{5,4},{6,7},{7,6},{8,9},{9,8},{10,11... | collective-permute-start | bytes 516104 | tf_op jit(solution)/shard_map/ppermute | solution.py:283
  33.8 0.0 collective-permute-done.15.refs_0_
  33.8 0.0 collective-permute-done.16.refs_1_
  33.9 0.7 %collective-permute-done.14.second = bf16[488,128]{1,0:T(8,128)(2,1)S(1)} collective-permute-done((bf16[488,128]{1,0:T(8,128)(2,1)S(1)}, bf16[488,128]{1,0:T(8,128)(2,1)S(1)}, u32[]{:S(2)}, u32[]{:S(2)}) %collective-permute-start.14) | collective-permute-done | bytes 124960 | tf_op jit(solution)/shard_map/ppermute | solution.py:280
  34.5 0.1 collective-permute-done.17.refs_2_
  34.7 0.2 collective-permute-start.19
  34.8 0.1 collective-permute-done.18.first_other
  34.9 1.1 %collective-permute-done.19.second_other = bf16[488,128]{1,0:T(8,128)(2,1)S(1)} collective-permute-done((bf16[488,128]{1,0:T(8,128)(2,1)S(1)}, bf16[488,128]{1,0:T(8,128)(2,1)S(1)}, u32[]{:S(2)}, u32[]{:S(2)}) %collective-permute-start.19) | collective-permute-done | bytes 124960 | tf_op jit(solution)/shard_map/ppermute | solution.py:283
  36.0 1.5 %shard_map.41 = bf16[192,768]{1,0:T(8,128)(2,1)} custom-call(bf16[1160,128]{1,0:T(8,128)(2,1)S(1)} %get-tuple-element.36.own, f32[384,128]{1,0:T(8,128)S(1)} %get-tuple-element.45.info, bf16[672,128]{1,0:T(8,128)(2,1)S(1)} %collective-permute-done.11.first, bf16[488,128]{1,0:T(8,128)(2,1)S(1)} %collective-permute-done.14.second, ...), custom_call_target="tpu_custom_call" | custom-call | flops 339738624 | tf_op jit(solution)/shard_map/pallas_call | solution.py:223
  (1 shorter events, 0.0 us)
Async XLA Ops:
  0.0 1.0 %copy-start = (bf16[192,768]{1,0:T(8,128)(2,1)S(1)}, bf16[192,768]{1,0:T(8,128)(2,1)}, u32[]{:S(2)}) copy-start(bf16[192,768]{1,0:T(8,128)(2,1)} %rows.3) | copy-start | bytes 884740
  1.0 5.4 %copy-start.2 = (s32[192]{0:T(256)S(1)}, s32[192]{0:T(256)}, u32[]{:S(2)}) copy-start(s32[192]{0:T(256)} %param.5) | copy-start | bytes 2308
  1.0 8.0 %collective-permute-start.2 = (bf16[672,128]{1,0:T(8,128)(2,1)S(1)}, bf16[672,128]{1,0:T(8,128)(2,1)S(1)}, u32[]{:S(2)}, u32[]{:S(2)}) collective-permute-start(bf16[672,128]{1,0:T(8,128)(2,1)S(1)} %shard_map.38), channel_id=1, source_target_pairs={{0,3},{1,2},{2,1},{3,0},{4,7},{5,6},{6,5},{7,4},{8,11},{9,10},{10,... | collective-permute-start | bytes 516104 | tf_op jit(solution)/shard_map/ppermute | solution.py:280
  3.4 7.1 %collective-permute-start.1 = (bf16[672,128]{1,0:T(8,128)(2,1)S(1)}, bf16[672,128]{1,0:T(8,128)(2,1)S(1)}, u32[]{:S(2)}, u32[]{:S(2)}) collective-permute-start(bf16[672,128]{1,0:T(8,128)(2,1)S(1)} %shard_map.38), channel_id=1, source_target_pairs={{4,1},{5,0},{0,9},{1,8},{8,13},{9,12},{12,5},{13,4},{6,3},{7,2},{2... | collective-permute-start | bytes 516104 | tf_op jit(solution)/shard_map/ppermute | solution.py:277
  6.3 0.7 %copy-start.1 = (s32[192,1]{0,1:T(1,128)S(1)}, s32[192,1]{0,1:T(1,128)}, u32[]{:S(2)}) copy-start(s32[192,1]{0,1:T(1,128)} %param.4) | copy-start | bytes 2308
  7.1 18.0 %collective-permute-start = (bf16[1160,128]{1,0:T(8,128)(2,1)S(1)}, bf16[1160,128]{1,0:T(8,128)(2,1)S(1)}, u32[]{:S(2)}, u32[]{:S(2)}) collective-permute-start(bf16[1160,128]{1,0:T(8,128)(2,1)S(1)} %get-tuple-element.36.own), channel_id=1, source_target_pairs={{0,1},{1,0},{2,3},{3,2},{4,5},{5,4},{6,7},{7,6},{8,9},{9,8},{10,11... | collective-permute-start | bytes 890888 | tf_op jit(solution)/shard_map/ppermute | solution.py:283
  7.1 6.5 %collective-permute-start.4 = (bf16[488,128]{1,0:T(8,128)(2,1)S(1)}, bf16[488,128]{1,0:T(8,128)(2,1)S(1)}, u32[]{:S(2)}, u32[]{:S(2)}) collective-permute-start(bf16[488,128]{1,0:T(8,128)(2,1)S(1)} %get-tuple-element.38), channel_id=1, source_target_pairs={{0,3},{1,2},{2,1},{3,0},{4,7},{5,6},{6,5},{7,4},{8,11},{9,10},{10,... | collective-permute-start | bytes 374792 | tf_op jit(solution)/shard_map/ppermute | solution.py:280
  7.8 5.8 %collective-permute-start.3 = (bf16[488,128]{1,0:T(8,128)(2,1)S(1)}, bf16[488,128]{1,0:T(8,128)(2,1)S(1)}, u32[]{:S(2)}, u32[]{:S(2)}) collective-permute-start(bf16[488,128]{1,0:T(8,128)(2,1)S(1)} %get-tuple-element.38), channel_id=1, source_target_pairs={{4,1},{5,0},{0,9},{1,8},{8,13},{9,12},{12,5},{13,4},{6,3},{7,2},{2... | collective-permute-start | bytes 374792 | tf_op jit(solution)/shard_map/ppermute | solution.py:277
  10.5 6.7 %collective-permute-start.6 = (bf16[672,128]{1,0:T(8,128)(2,1)S(1)}, bf16[672,128]{1,0:T(8,128)(2,1)S(1)}, u32[]{:S(2)}, u32[]{:S(2)}) collective-permute-start(bf16[672,128]{1,0:T(8,128)(2,1)S(1)} %collective-permute-done.1.refs_4_), channel_id=1, source_target_pairs={{0,3},{1,2},{2,1},{3,0},{4,7},{5,6},{6,5},{7,4},{8,11},{9,10},{10,... | collective-permute-start | bytes 516104 | tf_op jit(solution)/shard_map/ppermute | solution.py:280
  10.6 7.6 %collective-permute-start.5 = (bf16[672,128]{1,0:T(8,128)(2,1)S(1)}, bf16[672,128]{1,0:T(8,128)(2,1)S(1)}, u32[]{:S(2)}, u32[]{:S(2)}) collective-permute-start(bf16[672,128]{1,0:T(8,128)(2,1)S(1)} %collective-permute-done.1.refs_4_), channel_id=1, source_target_pairs={{4,1},{5,0},{0,9},{1,8},{8,13},{9,12},{12,5},{13,4},{6,3},{7,2},{2... | collective-permute-start | bytes 516104 | tf_op jit(solution)/shard_map/ppermute | solution.py:277
  13.6 9.1 %collective-permute-start.8 = (bf16[488,128]{1,0:T(8,128)(2,1)S(1)}, bf16[488,128]{1,0:T(8,128)(2,1)S(1)}, u32[]{:S(2)}, u32[]{:S(2)}) collective-permute-start(bf16[488,128]{1,0:T(8,128)(2,1)S(1)} %collective-permute-done.3.refs_5_), channel_id=1, source_target_pairs={{0,3},{1,2},{2,1},{3,0},{4,7},{5,6},{6,5},{7,4},{8,11},{9,10},{10,... | collective-permute-start | bytes 374792 | tf_op jit(solution)/shard_map/ppermute | solution.py:280
  15.4 7.4 %collective-permute-start.7 = (bf16[488,128]{1,0:T(8,128)(2,1)S(1)}, bf16[488,128]{1,0:T(8,128)(2,1)S(1)}, u32[]{:S(2)}, u32[]{:S(2)}) collective-permute-start(bf16[488,128]{1,0:T(8,128)(2,1)S(1)} %collective-permute-done.3.refs_5_), channel_id=1, source_target_pairs={{4,1},{5,0},{0,9},{1,8},{8,13},{9,12},{12,5},{13,4},{6,3},{7,2},{2... | collective-permute-start | bytes 374792 | tf_op jit(solution)/shard_map/ppermute | solution.py:277
  18.2 8.4 %collective-permute-start.10 = (bf16[672,128]{1,0:T(8,128)(2,1)S(1)}, bf16[672,128]{1,0:T(8,128)(2,1)S(1)}, u32[]{:S(2)}, u32[]{:S(2)}) collective-permute-start(bf16[672,128]{1,0:T(8,128)(2,1)S(1)} %collective-permute-done.5.refs_0_), channel_id=1, source_target_pairs={{0,3},{1,2},{2,1},{3,0},{4,7},{5,6},{6,5},{7,4},{8,11},{9,10},{10,... | collective-permute-start | bytes 516104 | tf_op jit(solution)/shard_map/ppermute | solution.py:280
  19.4 7.9 %collective-permute-start.9 = (bf16[672,128]{1,0:T(8,128)(2,1)S(1)}, bf16[672,128]{1,0:T(8,128)(2,1)S(1)}, u32[]{:S(2)}, u32[]{:S(2)}) collective-permute-start(bf16[672,128]{1,0:T(8,128)(2,1)S(1)} %collective-permute-done.5.refs_0_), channel_id=1, source_target_pairs={{4,1},{5,0},{0,9},{1,8},{8,13},{9,12},{12,5},{13,4},{6,3},{7,2},{2... | collective-permute-start | bytes 516104 | tf_op jit(solution)/shard_map/ppermute | solution.py:277
  22.8 7.3 %collective-permute-start.13 = (bf16[488,128]{1,0:T(8,128)(2,1)S(1)}, bf16[488,128]{1,0:T(8,128)(2,1)S(1)}, u32[]{:S(2)}, u32[]{:S(2)}) collective-permute-start(bf16[488,128]{1,0:T(8,128)(2,1)S(1)} %collective-permute-done.7.refs_1_), channel_id=1, source_target_pairs={{0,3},{1,2},{2,1},{3,0},{4,7},{5,6},{6,5},{7,4},{8,11},{9,10},{10,... | collective-permute-start | bytes 374792 | tf_op jit(solution)/shard_map/ppermute | solution.py:280
  23.1 7.0 %collective-permute-start.12 = (bf16[488,128]{1,0:T(8,128)(2,1)S(1)}, bf16[488,128]{1,0:T(8,128)(2,1)S(1)}, u32[]{:S(2)}, u32[]{:S(2)}) collective-permute-start(bf16[488,128]{1,0:T(8,128)(2,1)S(1)} %collective-permute-done.7.refs_1_), channel_id=1, source_target_pairs={{4,1},{5,0},{0,9},{1,8},{8,13},{9,12},{12,5},{13,4},{6,3},{7,2},{2... | collective-permute-start | bytes 374792 | tf_op jit(solution)/shard_map/ppermute | solution.py:277
  27.3 6.1 %collective-permute-start.11 = (bf16[672,128]{1,0:T(8,128)(2,1)S(1)}, bf16[672,128]{1,0:T(8,128)(2,1)S(1)}, u32[]{:S(2)}, u32[]{:S(2)}) collective-permute-start(bf16[672,128]{1,0:T(8,128)(2,1)S(1)} %collective-permute-done.10.refs_2_), channel_id=1, source_target_pairs={{4,1},{5,0},{0,9},{1,8},{8,13},{9,12},{12,5},{13,4},{6,3},{7,2},{2... | collective-permute-start | bytes 516104 | tf_op jit(solution)/shard_map/ppermute | solution.py:277
  30.1 4.5 %collective-permute-start.14 = (bf16[488,128]{1,0:T(8,128)(2,1)S(1)}, bf16[488,128]{1,0:T(8,128)(2,1)S(1)}, u32[]{:S(2)}, u32[]{:S(2)}) collective-permute-start(bf16[488,128]{1,0:T(8,128)(2,1)S(1)} %collective-permute-done.12.refs_5_), channel_id=1, source_target_pairs={{0,3},{1,2},{2,1},{3,0},{4,7},{5,6},{6,5},{7,4},{8,11},{9,10},{10,... | collective-permute-start | bytes 374792 | tf_op jit(solution)/shard_map/ppermute | solution.py:280
  32.1 1.8 %collective-permute-start.15 = (bf16[64,896]{1,0:T(8,128)(2,1)S(1)}, bf16[64,896]{1,0:T(8,128)(2,1)S(1)}, u32[]{:S(2)}, u32[]{:S(2)}) collective-permute-start(bf16[64,896]{1,0:T(8,128)(2,1)S(1)} %get-tuple-element.59), channel_id=1, source_target_pairs={{0,1},{1,0},{2,3},{3,2},{4,5},{5,4},{6,7},{7,6},{8,9},{9,8},{10,11... | collective-permute-start | bytes 344072 | tf_op jit(solution)/shard_map/ppermute | solution.py:283
  32.1 1.7 %collective-permute-start.16 = (bf16[64,896]{1,0:T(8,128)(2,1)S(1)}, bf16[64,896]{1,0:T(8,128)(2,1)S(1)}, u32[]{:S(2)}, u32[]{:S(2)}) collective-permute-start(bf16[64,896]{1,0:T(8,128)(2,1)S(1)} %get-tuple-element.60), channel_id=1, source_target_pairs={{0,1},{1,0},{2,3},{3,2},{4,5},{5,4},{6,7},{7,6},{8,9},{9,8},{10,11... | collective-permute-start | bytes 344072 | tf_op jit(solution)/shard_map/ppermute | solution.py:283
  33.3 1.3 %collective-permute-start.17 = (bf16[64,896]{1,0:T(8,128)(2,1)S(1)}, bf16[64,896]{1,0:T(8,128)(2,1)S(1)}, u32[]{:S(2)}, u32[]{:S(2)}) collective-permute-start(bf16[64,896]{1,0:T(8,128)(2,1)S(1)} %get-tuple-element.61), channel_id=1, source_target_pairs={{0,1},{1,0},{2,3},{3,2},{4,5},{5,4},{6,7},{7,6},{8,9},{9,8},{10,11... | collective-permute-start | bytes 344072 | tf_op jit(solution)/shard_map/ppermute | solution.py:283
  33.3 1.6 %collective-permute-start.18 = (bf16[672,128]{1,0:T(8,128)(2,1)S(1)}, bf16[672,128]{1,0:T(8,128)(2,1)S(1)}, u32[]{:S(2)}, u32[]{:S(2)}) collective-permute-start(bf16[672,128]{1,0:T(8,128)(2,1)S(1)} %collective-permute-done.11.first), channel_id=1, source_target_pairs={{0,1},{1,0},{2,3},{3,2},{4,5},{5,4},{6,7},{7,6},{8,9},{9,8},{10,11... | collective-permute-start | bytes 516104 | tf_op jit(solution)/shard_map/ppermute | solution.py:283
  34.7 1.3 %collective-permute-start.19 = (bf16[488,128]{1,0:T(8,128)(2,1)S(1)}, bf16[488,128]{1,0:T(8,128)(2,1)S(1)}, u32[]{:S(2)}, u32[]{:S(2)}) collective-permute-start(bf16[488,128]{1,0:T(8,128)(2,1)S(1)} %collective-permute-done.14.second), channel_id=1, source_target_pairs={{0,1},{1,0},{2,3},{3,2},{4,5},{5,4},{6,7},{7,6},{8,9},{9,8},{10,11... | collective-permute-start | bytes 374792 | tf_op jit(solution)/shard_map/ppermute | solution.py:283

commit v20 on v18

--- a/solution.py
+++ b/solution.py
@@ -287,16 +287,17 @@
         moved = [along(piece) for piece in along_by[-1]]
         swapped = [across(piece) for piece in along_by[-1]]
         moved[0], swapped[0] = together(moved[0], swapped[0])
-        moved[1], swapped[1], _ = together(moved[1], swapped[1], moved[0])
+        if s < n_blk - 1:
+            moved[1], swapped[1], _ = together(moved[1], swapped[1], moved[0])
         along_by.append(tuple(moved))
         across_by.append(tuple(swapped))
     left = (whole, other_core(whole))
     early = across_by[:-1] + along_by[1:-2]
     mine, theirs, info = start_both(left, early, (rows_here, width + 128))
     left = (*left, info)
-    near_first, _, mine, theirs = together(across_by[-1][0], along_by[-1][0], mine, theirs)
-    far_second, _ = together(along_by[-1][1], near_first)
-    last_first, last_second = along(near_first), across(far_second)
+    far_first, _, mine, theirs = together(along_by[-1][0], across_by[-1][0], mine, theirs)
+    near_second, _ = together(across_by[-1][1], far_first)
+    last_first, last_second = across(far_first), along(near_second)
     late = [along_by[-2], across_by[-1], along_by[-1]]
     mine, *theirs = add_both(left, late, (mine, theirs))
     back = [other_core(part) for part in theirs[:-1]]

time: 37.3 us -> 36.5 us (0.979)
  waiting for transfers between devices: 6.83 us -> 5.04 us
  starting transfers between devices: 24.1 us -> 25 us
    ppermute x7, waiting for transfers between devices: 2.62 us -> 1.07 us  [across(): return lax.ppermute(rows, ('sub', 'pair'), [(0, 3), (1, 2), (2, 1), (3, 0)])]
    ppermute x7, starting transfers between devices: 16.5 us -> 17 us  [along(): return lax.ppermute(rows, ('blk', 'pair'), hops)]
    ppermute x7, waiting for transfers between devices: 2.78 us -> 2.29 us  [along(): return lax.ppermute(rows, ('blk', 'pair'), hops)]
  transfers between devices with their start and end apart: 20 -> 20, of which waited for: 9 -> 8; matrix products, arithmetic and copies ran while one was open for 0% -> 0% of each run, Pallas kernels for 8% -> 8%
where the time goes in v20:
time: 36.5 us; the launch traced here: 36.3 us
  starting transfers between devices  25 us (68%)
  waiting for transfers between devices  5.04 us (14%)
  Pallas kernels  4.52 us (12%)
  local copies, waits for them, and re-layouts  1.64 us (4%)
    ppermute x7, starting transfers between devices, along(): return lax.ppermute(rows, ('blk', 'pair'), hops)  17 us
    ppermute x7, starting transfers between devices, across(): return lax.ppermute(rows, ('sub', 'pair'), [(0, 3), (1, 2), (2, 1), (3, 0)])  6.7 us
    pallas_call x5, Pallas kernels, call(): pl.pallas_call(kernel, out_shape=[jax.ShapeDtypeStruct(shape, dtype) for...  4.52 us
    ppermute x7, waiting for transfers between devices, along(): return lax.ppermute(rows, ('blk', 'pair'), hops)  2.29 us
    ppermute x6, waiting for transfers between devices, other_core(): return lax.ppermute(rows, 'pair', [(0, 1), (1, 0)])  1.69 us
    unnamed x6, local copies, waits for them, and re-layouts  1.64 us
    ppermute x6, starting transfers between devices, other_core(): return lax.ppermute(rows, 'pair', [(0, 1), (1, 0)])  1.29 us
    ppermute x7, waiting for transfers between devices, across(): return lax.ppermute(rows, ('sub', 'pair'), [(0, 3), (1, 2), (2, 1), (3, 0)])  1.07 us
  transfers between devices with their start and end apart: 20, of which 8 were waited for; matrix products, arithmetic and copies ran while one was open for 0% of the time, Pallas kernels for 8%

profile of v20, /device:TPU:0, one launch (start us, length us, event | category | flops | bytes accessed | tf_op | source)
XLA Modules:
  0.0 36.3 jit_solution(3218588355875285755)
XLA Ops:
  0.0 0.0 copy-start
  0.0 1.0 %copy-done = bf16[192,768]{1,0:T(8,128)(2,1)S(1)} copy-done((bf16[192,768]{1,0:T(8,128)(2,1)S(1)}, bf16[192,768]{1,0:T(8,128)(2,1)}, u32[]{:S(2)}) %copy-start) | copy-done | bytes 294936
  1.0 0.0 copy-start.2
  1.0 2.4 %collective-permute-start.2 = (bf16[584,128]{1,0:T(8,128)(2,1)S(1)}, bf16[584,128]{1,0:T(8,128)(2,1)S(1)}, u32[]{:S(2)}, u32[]{:S(2)}) collective-permute-start(bf16[584,128]{1,0:T(8,128)(2,1)S(1)} %shard_map.38), channel_id=1, source_target_pairs={{0,3},{1,2},{2,1},{3,0},{4,7},{5,6},{6,5},{7,4},{8,11},{9,10},{10,... | collective-permute-start | bytes 448520 | tf_op jit(solution)/shard_map/ppermute | solution.py:272
  3.4 2.9 %collective-permute-start.1 = (bf16[584,128]{1,0:T(8,128)(2,1)S(1)}, bf16[584,128]{1,0:T(8,128)(2,1)S(1)}, u32[]{:S(2)}, u32[]{:S(2)}) collective-permute-start(bf16[584,128]{1,0:T(8,128)(2,1)S(1)} %shard_map.38), channel_id=1, source_target_pairs={{4,1},{5,0},{0,9},{1,8},{8,13},{9,12},{12,5},{13,4},{6,3},{7,2},{2... | collective-permute-start | bytes 448520 | tf_op jit(solution)/shard_map/ppermute | solution.py:269
  6.3 0.0 copy-start.1
  6.3 0.0 copy-done.2
  6.3 0.7 %copy-done.1 = s32[192,1]{0,1:T(1,128)S(1)} copy-done((s32[192,1]{0,1:T(1,128)S(1)}, s32[192,1]{0,1:T(1,128)}, u32[]{:S(2)}) %copy-start.1) | copy-done | bytes 792
  7.0 0.1 shard_map.37
  7.1 0.1 collective-permute-start.4
  7.2 1.8 %collective-permute-start.3 = (bf16[584,128]{1,0:T(8,128)(2,1)S(1)}, bf16[584,128]{1,0:T(8,128)(2,1)S(1)}, u32[]{:S(2)}, u32[]{:S(2)}) collective-permute-start(bf16[584,128]{1,0:T(8,128)(2,1)S(1)} %get-tuple-element.36), channel_id=1, source_target_pairs={{4,1},{5,0},{0,9},{1,8},{8,13},{9,12},{12,5},{13,4},{6,3},{7,2},{2... | collective-permute-start | bytes 448520 | tf_op jit(solution)/shard_map/ppermute | solution.py:269
  9.0 0.0 collective-permute-done.2.refs_0_
  9.0 1.2 %collective-permute-done.1.refs_4_ = bf16[584,128]{1,0:T(8,128)(2,1)S(1)} collective-permute-done((bf16[584,128]{1,0:T(8,128)(2,1)S(1)}, bf16[584,128]{1,0:T(8,128)(2,1)S(1)}, u32[]{:S(2)}, u32[]{:S(2)}) %collective-permute-start.1) | collective-permute-done | bytes 149536 | tf_op jit(solution)/shard_map/ppermute | solution.py:269
  10.1 0.0 collective-permute-start.6
  10.1 3.1 %collective-permute-start.5 = (bf16[584,128]{1,0:T(8,128)(2,1)S(1)}, bf16[584,128]{1,0:T(8,128)(2,1)S(1)}, u32[]{:S(2)}, u32[]{:S(2)}) collective-permute-start(bf16[584,128]{1,0:T(8,128)(2,1)S(1)} %collective-permute-done.1.refs_4_), channel_id=1, source_target_pairs={{4,1},{5,0},{0,9},{1,8},{8,13},{9,12},{12,5},{13,4},{6,3},{7,2},{2... | collective-permute-start | bytes 448520 | tf_op jit(solution)/shard_map/ppermute | solution.py:269
  13.2 0.1 collective-permute-start
  13.3 0.0 collective-permute-done.4.refs_1_
  13.3 0.0 collective-permute-done.3.refs_5_
  13.3 1.7 %collective-permute-start.8 = (bf16[584,128]{1,0:T(8,128)(2,1)S(1)}, bf16[584,128]{1,0:T(8,128)(2,1)S(1)}, u32[]{:S(2)}, u32[]{:S(2)}) collective-permute-start(bf16[584,128]{1,0:T(8,128)(2,1)S(1)} %collective-permute-done.3.refs_5_), channel_id=1, source_target_pairs={{0,3},{1,2},{2,1},{3,0},{4,7},{5,6},{6,5},{7,4},{8,11},{9,10},{10,... | collective-permute-start | bytes 448520 | tf_op jit(solution)/shard_map/ppermute | solution.py:272
  15.1 1.2 %collective-permute-start.7 = (bf16[584,128]{1,0:T(8,128)(2,1)S(1)}, bf16[584,128]{1,0:T(8,128)(2,1)S(1)}, u32[]{:S(2)}, u32[]{:S(2)}) collective-permute-start(bf16[584,128]{1,0:T(8,128)(2,1)S(1)} %collective-permute-done.3.refs_5_), channel_id=1, source_target_pairs={{4,1},{5,0},{0,9},{1,8},{8,13},{9,12},{12,5},{13,4},{6,3},{7,2},{2... | collective-permute-start | bytes 448520 | tf_op jit(solution)/shard_map/ppermute | solution.py:269
  16.2 0.3 collective-permute-done.6.refs_2_
  16.5 0.4 %collective-permute-done.5.refs_0_ = bf16[584,128]{1,0:T(8,128)(2,1)S(1)} collective-permute-done((bf16[584,128]{1,0:T(8,128)(2,1)S(1)}, bf16[584,128]{1,0:T(8,128)(2,1)S(1)}, u32[]{:S(2)}, u32[]{:S(2)}) %collective-permute-start.5) | collective-permute-done | bytes 149536 | tf_op jit(solution)/shard_map/ppermute | solution.py:269
  16.9 1.2 %collective-permute-start.10 = (bf16[584,128]{1,0:T(8,128)(2,1)S(1)}, bf16[584,128]{1,0:T(8,128)(2,1)S(1)}, u32[]{:S(2)}, u32[]{:S(2)}) collective-permute-start(bf16[584,128]{1,0:T(8,128)(2,1)S(1)} %collective-permute-done.5.refs_0_), channel_id=1, source_target_pairs={{0,3},{1,2},{2,1},{3,0},{4,7},{5,6},{6,5},{7,4},{8,11},{9,10},{10,... | collective-permute-start | bytes 448520 | tf_op jit(solution)/shard_map/ppermute | solution.py:272
  18.0 3.4 %collective-permute-start.9 = (bf16[584,128]{1,0:T(8,128)(2,1)S(1)}, bf16[584,128]{1,0:T(8,128)(2,1)S(1)}, u32[]{:S(2)}, u32[]{:S(2)}) collective-permute-start(bf16[584,128]{1,0:T(8,128)(2,1)S(1)} %collective-permute-done.5.refs_0_), channel_id=1, source_target_pairs={{4,1},{5,0},{0,9},{1,8},{8,13},{9,12},{12,5},{13,4},{6,3},{7,2},{2... | collective-permute-start | bytes 448520 | tf_op jit(solution)/shard_map/ppermute | solution.py:269
  21.4 0.0 collective-permute-done.8.refs_3_
  21.4 0.0 collective-permute-done.7.refs_1_
  21.4 0.1 collective-permute-start.12
  21.6 2.6 %collective-permute-start.13 = (bf16[584,128]{1,0:T(8,128)(2,1)S(1)}, bf16[584,128]{1,0:T(8,128)(2,1)S(1)}, u32[]{:S(2)}, u32[]{:S(2)}) collective-permute-start(bf16[584,128]{1,0:T(8,128)(2,1)S(1)} %collective-permute-done.7.refs_1_), channel_id=1, source_target_pairs={{4,1},{5,0},{0,9},{1,8},{8,13},{9,12},{12,5},{13,4},{6,3},{7,2},{2... | collective-permute-start | bytes 448520 | tf_op jit(solution)/shard_map/ppermute | solution.py:269
  24.1 0.0 collective-permute-done.other
  24.1 1.5 %shard_map.39 = (f32[192,896]{1,0:T(8,128)S(1)}, f32[192,896]{1,0:T(8,128)S(1)}, f32[384,128]{1,0:T(8,128)S(1)}) custom-call(bf16[1160,128]{1,0:T(8,128)(2,1)S(1)} %get-tuple-element.34.own, bf16[1160,128]{1,0:T(8,128)(2,1)S(1)} %collective-permute-done.other, bf16[584,128]{1,0:T(8,128)(2,1)S(1)} %collective-permute-done.2.refs_0_, ...), custom_call_target="tpu_custom_call" | custom-call | tf_op jit(solution)/shard_map/pallas_call | solution.py:222
  25.6 0.0 collective-permute-done.10.refs_2_
  25.7 0.0 collective-permute-done.9.refs_4_
  25.7 1.1 %collective-permute-start.11 = (bf16[584,128]{1,0:T(8,128)(2,1)S(1)}, bf16[584,128]{1,0:T(8,128)(2,1)S(1)}, u32[]{:S(2)}, u32[]{:S(2)}) collective-permute-start(bf16[584,128]{1,0:T(8,128)(2,1)S(1)} %collective-permute-done.9.refs_4_), channel_id=1, source_target_pairs={{0,3},{1,2},{2,1},{3,0},{4,7},{5,6},{6,5},{7,4},{8,11},{9,10},{10,... | collective-permute-start | bytes 448520 | tf_op jit(solution)/shard_map/ppermute | solution.py:272
  26.8 0.7 %collective-permute-done.12.refs_3_ = bf16[584,128]{1,0:T(8,128)(2,1)S(1)} collective-permute-done((bf16[584,128]{1,0:T(8,128)(2,1)S(1)}, bf16[584,128]{1,0:T(8,128)(2,1)S(1)}, u32[]{:S(2)}, u32[]{:S(2)}) %collective-permute-start.12) | collective-permute-done | bytes 149536 | tf_op jit(solution)/shard_map/ppermute | solution.py:272
  27.5 2.2 %collective-permute-start.14 = (bf16[584,128]{1,0:T(8,128)(2,1)S(1)}, bf16[584,128]{1,0:T(8,128)(2,1)S(1)}, u32[]{:S(2)}, u32[]{:S(2)}) collective-permute-start(bf16[584,128]{1,0:T(8,128)(2,1)S(1)} %collective-permute-done.12.refs_3_), channel_id=1, source_target_pairs={{4,1},{5,0},{0,9},{1,8},{8,13},{9,12},{12,5},{13,4},{6,3},{7,2},{2... | collective-permute-start | bytes 448520 | tf_op jit(solution)/shard_map/ppermute | solution.py:269
  29.7 0.0 collective-permute-done.13.refs_5_
  29.7 1.4 %shard_map.40 = (f32[192,896]{1,0:T(8,128)S(1)}, bf16[64,896]{1,0:T(8,128)(2,1)S(1)}, bf16[64,896]{1,0:T(8,128)(2,1)S(1)}, bf16[64,896]{1,0:T(8,128)(2,1)S(1)}) custom-call(bf16[1160,128]{1,0:T(8,128)(2,1)S(1)} %get-tuple-element.34.own, bf16[1160,128]{1,0:T(8,128)(2,1)S(1)} %collective-permute-done.other, ...), custom_call_target="tpu_custom_call", output_to_operand_aliasing={{0}: (9, {})} | custom-call | tf_op jit(solution)/shard_map/pallas_call | solution.py:222
  31.1 0.1 collective-permute-start.15
  31.2 0.5 %collective-permute-start.16 = (bf16[64,896]{1,0:T(8,128)(2,1)S(1)}, bf16[64,896]{1,0:T(8,128)(2,1)S(1)}, u32[]{:S(2)}, u32[]{:S(2)}) collective-permute-start(bf16[64,896]{1,0:T(8,128)(2,1)S(1)} %get-tuple-element.56), channel_id=1, source_target_pairs={{0,1},{1,0},{2,3},{3,2},{4,5},{5,4},{6,7},{7,6},{8,9},{9,8},{10,11... | collective-permute-start | bytes 344072 | tf_op jit(solution)/shard_map/ppermute | solution.py:275
  31.7 0.0 collective-permute-done.11.first
  31.7 0.3 collective-permute-start.17
  32.0 0.2 collective-permute-start.18
  32.2 0.3 collective-permute-done.15.refs_0_
  32.5 0.2 collective-permute-done.16.refs_1_
  32.7 0.7 %collective-permute-done.14.second = bf16[584,128]{1,0:T(8,128)(2,1)S(1)} collective-permute-done((bf16[584,128]{1,0:T(8,128)(2,1)S(1)}, bf16[584,128]{1,0:T(8,128)(2,1)S(1)}, u32[]{:S(2)}, u32[]{:S(2)}) %collective-permute-start.14) | collective-permute-done | bytes 149536 | tf_op jit(solution)/shard_map/ppermute | solution.py:269
  33.4 0.0 collective-permute-done.17.refs_2_
  33.4 0.2 collective-permute-start.19
  33.6 0.0 collective-permute-done.18.first_other
  33.6 1.2 %collective-permute-done.19.second_other = bf16[584,128]{1,0:T(8,128)(2,1)S(1)} collective-permute-done((bf16[584,128]{1,0:T(8,128)(2,1)S(1)}, bf16[584,128]{1,0:T(8,128)(2,1)S(1)}, u32[]{:S(2)}, u32[]{:S(2)}) %collective-permute-start.19) | collective-permute-done | bytes 149536 | tf_op jit(solution)/shard_map/ppermute | solution.py:275
  34.8 1.5 %shard_map.41 = bf16[192,768]{1,0:T(8,128)(2,1)} custom-call(bf16[1160,128]{1,0:T(8,128)(2,1)S(1)} %get-tuple-element.34.own, f32[384,128]{1,0:T(8,128)S(1)} %get-tuple-element.43.info, bf16[584,128]{1,0:T(8,128)(2,1)S(1)} %collective-permute-done.11.first, bf16[584,128]{1,0:T(8,128)(2,1)S(1)} %collective-permute-done.14.second, ...), custom_call_target="tpu_custom_call" | custom-call | tf_op jit(solution)/shard_map/pallas_call | solution.py:222
  (1 shorter events, 0.0 us)
Async XLA Ops:
  0.0 1.0 %copy-start = (bf16[192,768]{1,0:T(8,128)(2,1)S(1)}, bf16[192,768]{1,0:T(8,128)(2,1)}, u32[]{:S(2)}) copy-start(bf16[192,768]{1,0:T(8,128)(2,1)} %rows.3) | copy-start | bytes 884740
  1.0 5.3 %copy-start.2 = (s32[192]{0:T(256)S(1)}, s32[192]{0:T(256)}, u32[]{:S(2)}) copy-start(s32[192]{0:T(256)} %param.5) | copy-start | bytes 2308
  1.0 8.0 %collective-permute-start.2 = (bf16[584,128]{1,0:T(8,128)(2,1)S(1)}, bf16[584,128]{1,0:T(8,128)(2,1)S(1)}, u32[]{:S(2)}, u32[]{:S(2)}) collective-permute-start(bf16[584,128]{1,0:T(8,128)(2,1)S(1)} %shard_map.38), channel_id=1, source_target_pairs={{0,3},{1,2},{2,1},{3,0},{4,7},{5,6},{6,5},{7,4},{8,11},{9,10},{10,... | collective-permute-start | bytes 448520 | tf_op jit(solution)/shard_map/ppermute | solution.py:272
  3.4 6.7 %collective-permute-start.1 = (bf16[584,128]{1,0:T(8,128)(2,1)S(1)}, bf16[584,128]{1,0:T(8,128)(2,1)S(1)}, u32[]{:S(2)}, u32[]{:S(2)}) collective-permute-start(bf16[584,128]{1,0:T(8,128)(2,1)S(1)} %shard_map.38), channel_id=1, source_target_pairs={{4,1},{5,0},{0,9},{1,8},{8,13},{9,12},{12,5},{13,4},{6,3},{7,2},{2... | collective-permute-start | bytes 448520 | tf_op jit(solution)/shard_map/ppermute | solution.py:269
  6.3 0.7 %copy-start.1 = (s32[192,1]{0,1:T(1,128)S(1)}, s32[192,1]{0,1:T(1,128)}, u32[]{:S(2)}) copy-start(s32[192,1]{0,1:T(1,128)} %param.4) | copy-start | bytes 2308
  7.1 6.2 %collective-permute-start.4 = (bf16[584,128]{1,0:T(8,128)(2,1)S(1)}, bf16[584,128]{1,0:T(8,128)(2,1)S(1)}, u32[]{:S(2)}, u32[]{:S(2)}) collective-permute-start(bf16[584,128]{1,0:T(8,128)(2,1)S(1)} %get-tuple-element.36), channel_id=1, source_target_pairs={{0,3},{1,2},{2,1},{3,0},{4,7},{5,6},{6,5},{7,4},{8,11},{9,10},{10,... | collective-permute-start | bytes 448520 | tf_op jit(solution)/shard_map/ppermute | solution.py:272
  7.2 6.1 %collective-permute-start.3 = (bf16[584,128]{1,0:T(8,128)(2,1)S(1)}, bf16[584,128]{1,0:T(8,128)(2,1)S(1)}, u32[]{:S(2)}, u32[]{:S(2)}) collective-permute-start(bf16[584,128]{1,0:T(8,128)(2,1)S(1)} %get-tuple-element.36), channel_id=1, source_target_pairs={{4,1},{5,0},{0,9},{1,8},{8,13},{9,12},{12,5},{13,4},{6,3},{7,2},{2... | collective-permute-start | bytes 448520 | tf_op jit(solution)/shard_map/ppermute | solution.py:269
  10.1 6.4 %collective-permute-start.6 = (bf16[584,128]{1,0:T(8,128)(2,1)S(1)}, bf16[584,128]{1,0:T(8,128)(2,1)S(1)}, u32[]{:S(2)}, u32[]{:S(2)}) collective-permute-start(bf16[584,128]{1,0:T(8,128)(2,1)S(1)} %collective-permute-done.1.refs_4_), channel_id=1, source_target_pairs={{0,3},{1,2},{2,1},{3,0},{4,7},{5,6},{6,5},{7,4},{8,11},{9,10},{10,... | collective-permute-start | bytes 448520 | tf_op jit(solution)/shard_map/ppermute | solution.py:272
  10.1 6.8 %collective-permute-start.5 = (bf16[584,128]{1,0:T(8,128)(2,1)S(1)}, bf16[584,128]{1,0:T(8,128)(2,1)S(1)}, u32[]{:S(2)}, u32[]{:S(2)}) collective-permute-start(bf16[584,128]{1,0:T(8,128)(2,1)S(1)} %collective-permute-done.1.refs_4_), channel_id=1, source_target_pairs={{4,1},{5,0},{0,9},{1,8},{8,13},{9,12},{12,5},{13,4},{6,3},{7,2},{2... | collective-permute-start | bytes 448520 | tf_op jit(solution)/shard_map/ppermute | solution.py:269
  13.2 10.9 %collective-permute-start = (bf16[1160,128]{1,0:T(8,128)(2,1)S(1)}, bf16[1160,128]{1,0:T(8,128)(2,1)S(1)}, u32[]{:S(2)}, u32[]{:S(2)}) collective-permute-start(bf16[1160,128]{1,0:T(8,128)(2,1)S(1)} %get-tuple-element.34.own), channel_id=1, source_target_pairs={{0,1},{1,0},{2,3},{3,2},{4,5},{5,4},{6,7},{7,6},{8,9},{9,8},{10,11... | collective-permute-start | bytes 890888 | tf_op jit(solution)/shard_map/ppermute | solution.py:275
  13.3 8.1 %collective-permute-start.8 = (bf16[584,128]{1,0:T(8,128)(2,1)S(1)}, bf16[584,128]{1,0:T(8,128)(2,1)S(1)}, u32[]{:S(2)}, u32[]{:S(2)}) collective-permute-start(bf16[584,128]{1,0:T(8,128)(2,1)S(1)} %collective-permute-done.3.refs_5_), channel_id=1, source_target_pairs={{0,3},{1,2},{2,1},{3,0},{4,7},{5,6},{6,5},{7,4},{8,11},{9,10},{10,... | collective-permute-start | bytes 448520 | tf_op jit(solution)/shard_map/ppermute | solution.py:272
  15.1 6.4 %collective-permute-start.7 = (bf16[584,128]{1,0:T(8,128)(2,1)S(1)}, bf16[584,128]{1,0:T(8,128)(2,1)S(1)}, u32[]{:S(2)}, u32[]{:S(2)}) collective-permute-start(bf16[584,128]{1,0:T(8,128)(2,1)S(1)} %collective-permute-done.3.refs_5_), channel_id=1, source_target_pairs={{4,1},{5,0},{0,9},{1,8},{8,13},{9,12},{12,5},{13,4},{6,3},{7,2},{2... | collective-permute-start | bytes 448520 | tf_op jit(solution)/shard_map/ppermute | solution.py:269
  16.9 8.8 %collective-permute-start.10 = (bf16[584,128]{1,0:T(8,128)(2,1)S(1)}, bf16[584,128]{1,0:T(8,128)(2,1)S(1)}, u32[]{:S(2)}, u32[]{:S(2)}) collective-permute-start(bf16[584,128]{1,0:T(8,128)(2,1)S(1)} %collective-permute-done.5.refs_0_), channel_id=1, source_target_pairs={{0,3},{1,2},{2,1},{3,0},{4,7},{5,6},{6,5},{7,4},{8,11},{9,10},{10,... | collective-permute-start | bytes 448520 | tf_op jit(solution)/shard_map/ppermute | solution.py:272
  18.0 7.6 %collective-permute-start.9 = (bf16[584,128]{1,0:T(8,128)(2,1)S(1)}, bf16[584,128]{1,0:T(8,128)(2,1)S(1)}, u32[]{:S(2)}, u32[]{:S(2)}) collective-permute-start(bf16[584,128]{1,0:T(8,128)(2,1)S(1)} %collective-permute-done.5.refs_0_), channel_id=1, source_target_pairs={{4,1},{5,0},{0,9},{1,8},{8,13},{9,12},{12,5},{13,4},{6,3},{7,2},{2... | collective-permute-start | bytes 448520 | tf_op jit(solution)/shard_map/ppermute | solution.py:269
  21.4 6.1 %collective-permute-start.12 = (bf16[584,128]{1,0:T(8,128)(2,1)S(1)}, bf16[584,128]{1,0:T(8,128)(2,1)S(1)}, u32[]{:S(2)}, u32[]{:S(2)}) collective-permute-start(bf16[584,128]{1,0:T(8,128)(2,1)S(1)} %collective-permute-done.7.refs_1_), channel_id=1, source_target_pairs={{0,3},{1,2},{2,1},{3,0},{4,7},{5,6},{6,5},{7,4},{8,11},{9,10},{10,... | collective-permute-start | bytes 448520 | tf_op jit(solution)/shard_map/ppermute | solution.py:272
  21.6 8.1 %collective-permute-start.13 = (bf16[584,128]{1,0:T(8,128)(2,1)S(1)}, bf16[584,128]{1,0:T(8,128)(2,1)S(1)}, u32[]{:S(2)}, u32[]{:S(2)}) collective-permute-start(bf16[584,128]{1,0:T(8,128)(2,1)S(1)} %collective-permute-done.7.refs_1_), channel_id=1, source_target_pairs={{4,1},{5,0},{0,9},{1,8},{8,13},{9,12},{12,5},{13,4},{6,3},{7,2},{2... | collective-permute-start | bytes 448520 | tf_op jit(solution)/shard_map/ppermute | solution.py:269
  25.7 6.1 %collective-permute-start.11 = (bf16[584,128]{1,0:T(8,128)(2,1)S(1)}, bf16[584,128]{1,0:T(8,128)(2,1)S(1)}, u32[]{:S(2)}, u32[]{:S(2)}) collective-permute-start(bf16[584,128]{1,0:T(8,128)(2,1)S(1)} %collective-permute-done.9.refs_4_), channel_id=1, source_target_pairs={{0,3},{1,2},{2,1},{3,0},{4,7},{5,6},{6,5},{7,4},{8,11},{9,10},{10,... | collective-permute-start | bytes 448520 | tf_op jit(solution)/shard_map/ppermute | solution.py:272
  27.5 5.9 %collective-permute-start.14 = (bf16[584,128]{1,0:T(8,128)(2,1)S(1)}, bf16[584,128]{1,0:T(8,128)(2,1)S(1)}, u32[]{:S(2)}, u32[]{:S(2)}) collective-permute-start(bf16[584,128]{1,0:T(8,128)(2,1)S(1)} %collective-permute-done.12.refs_3_), channel_id=1, source_target_pairs={{4,1},{5,0},{0,9},{1,8},{8,13},{9,12},{12,5},{13,4},{6,3},{7,2},{2... | collective-permute-start | bytes 448520 | tf_op jit(solution)/shard_map/ppermute | solution.py:269
  31.1 1.4 %collective-permute-start.15 = (bf16[64,896]{1,0:T(8,128)(2,1)S(1)}, bf16[64,896]{1,0:T(8,128)(2,1)S(1)}, u32[]{:S(2)}, u32[]{:S(2)}) collective-permute-start(bf16[64,896]{1,0:T(8,128)(2,1)S(1)} %get-tuple-element.55), channel_id=1, source_target_pairs={{0,1},{1,0},{2,3},{3,2},{4,5},{5,4},{6,7},{7,6},{8,9},{9,8},{10,11... | collective-permute-start | bytes 344072 | tf_op jit(solution)/shard_map/ppermute | solution.py:275
  31.2 1.5 %collective-permute-start.16 = (bf16[64,896]{1,0:T(8,128)(2,1)S(1)}, bf16[64,896]{1,0:T(8,128)(2,1)S(1)}, u32[]{:S(2)}, u32[]{:S(2)}) collective-permute-start(bf16[64,896]{1,0:T(8,128)(2,1)S(1)} %get-tuple-element.56), channel_id=1, source_target_pairs={{0,1},{1,0},{2,3},{3,2},{4,5},{5,4},{6,7},{7,6},{8,9},{9,8},{10,11... | collective-permute-start | bytes 344072 | tf_op jit(solution)/shard_map/ppermute | solution.py:275
  31.7 1.7 %collective-permute-start.17 = (bf16[64,896]{1,0:T(8,128)(2,1)S(1)}, bf16[64,896]{1,0:T(8,128)(2,1)S(1)}, u32[]{:S(2)}, u32[]{:S(2)}) collective-permute-start(bf16[64,896]{1,0:T(8,128)(2,1)S(1)} %get-tuple-element.57), channel_id=1, source_target_pairs={{0,1},{1,0},{2,3},{3,2},{4,5},{5,4},{6,7},{7,6},{8,9},{9,8},{10,11... | collective-permute-start | bytes 344072 | tf_op jit(solution)/shard_map/ppermute | solution.py:275
  32.0 1.6 %collective-permute-start.18 = (bf16[584,128]{1,0:T(8,128)(2,1)S(1)}, bf16[584,128]{1,0:T(8,128)(2,1)S(1)}, u32[]{:S(2)}, u32[]{:S(2)}) collective-permute-start(bf16[584,128]{1,0:T(8,128)(2,1)S(1)} %collective-permute-done.11.first), channel_id=1, source_target_pairs={{0,1},{1,0},{2,3},{3,2},{4,5},{5,4},{6,7},{7,6},{8,9},{9,8},{10,11... | collective-permute-start | bytes 448520 | tf_op jit(solution)/shard_map/ppermute | solution.py:275
  33.4 1.4 %collective-permute-start.19 = (bf16[584,128]{1,0:T(8,128)(2,1)S(1)}, bf16[584,128]{1,0:T(8,128)(2,1)S(1)}, u32[]{:S(2)}, u32[]{:S(2)}) collective-permute-start(bf16[584,128]{1,0:T(8,128)(2,1)S(1)} %collective-permute-done.14.second), channel_id=1, source_target_pairs={{0,1},{1,0},{2,3},{3,2},{4,5},{5,4},{6,7},{7,6},{8,9},{9,8},{10,11... | collective-permute-start | bytes 448520 | tf_op jit(solution)/shard_map/ppermute | solution.py:275

commit v21 on v20

--- a/solution.py
+++ b/solution.py
@@ -112,13 +112,18 @@
     return jnp.concatenate(slabs, axis=1)
 
 
-def key_rows(ref, half):
-    wide = ref[ref.shape[0] - 8 :, :].astype(F32)
-    return [wide[side : side + 1, :half] * 256.0 + wide[side + 2 : side + 3, :half] for side in range(2)]
-
-
-def key_row(ref, rows_here):
-    return jnp.concatenate(key_rows(ref, rows_here // 2), axis=1)
+def key_row(ref, rows_here, line=0):
+    half = rows_here // 2
+    wide = ref[ref.shape[0] - 8 :, :].astype(F32)[line : line + 4, :half]
+    return jnp.concatenate([wide[0:1] * 256.0 + wide[2:3], wide[1:2] * 256.0 + wide[3:4]], axis=1)
+
+
+def add_names_kernel(piece, whole, out):
+    top = piece.shape[0] - 8
+    out[:top, :] = piece[:top, :]
+    lines = piece[top:, :].astype(F32)
+    own = whole[whole.shape[0] - 8 :, :].astype(F32)
+    out[top:, :] = jnp.concatenate([lines[:4], own[:4]], axis=0).astype(BF16)
 
 
 def from_halves(first, second, rows_here):
@@ -165,9 +170,11 @@
         out[:, wide - 128 :] = jnp.broadcast_to(denom[top : top + rows_here], (rows_here, 128))
 
 
-def start_kernel(n_blocks, own, other, *refs):
+def start_kernel(n_blocks, own, other, crossed, *refs):
     refs = list(refs)
     rows_here = refs[-1].shape[0] // 2
+    raw = crossed[...]
+    crossed = (raw, key_row(refs[1], rows_here, 4), to_row(scale_column(raw)))
     left = left_rows((own, other), rows_here)
     key = jnp.concatenate([to_column(key_row(ref, rows_here)) for ref in (own, other)], axis=0)
     scale = scale_column(left)
@@ -175,7 +182,7 @@
     lane = lax.broadcasted_iota(jnp.int32, info.shape, 1)
     info[...] = jnp.where(lane == 0, key, 4.0 * scale)
     first = (left[:rows_here], key_row(own, rows_here), to_row(scale[:rows_here]))
-    blocks = [first] + take_blocks(refs, n_blocks, rows_here)
+    blocks = [first, crossed] + take_blocks(refs, n_blocks, rows_here)
     store_sides(*add_blocks(left, info, blocks, None, None), refs)
 
 
@@ -229,9 +236,9 @@
     )(*args)
 
 
-def start_both(left, right, shape):
+def start_both(left, crossed, right, shape):
     rows_here = shape[0]
-    args = list(left) + [half for block in right for half in block]
+    args = [*left, crossed] + [half for block in right for half in block]
     shapes = [(shape, F32), (shape, F32), ((2 * rows_here, 128), F32)]
     return call(functools.partial(start_kernel, len(right)), shapes, args)
 
@@ -281,9 +288,13 @@
         [((slabs * rows_here + 8, 128), BF16), half_shape],
         [embeddings, group_of.reshape(line), cluster_id.reshape(line)],
     )
-    along_by = [(first, second)]
-    across_by = []
-    for s in range(1, n_blk):
+    crossed = across(embeddings)
+    moved = [along(first), along(second)]
+    moved[1], crossed, _ = together(moved[1], crossed, moved[0])
+    (named,) = call(add_names_kernel, [half_shape], [moved[1], whole])
+    along_by = [(first, second), (moved[0], named)]
+    across_by = [crossed]
+    for s in range(2, n_blk):
         moved = [along(piece) for piece in along_by[-1]]
         swapped = [across(piece) for piece in along_by[-1]]
         moved[0], swapped[0] = together(moved[0], swapped[0])
@@ -292,8 +303,8 @@
         along_by.append(tuple(moved))
         across_by.append(tuple(swapped))
     left = (whole, other_core(whole))
-    early = across_by[:-1] + along_by[1:-2]
-    mine, theirs, info = start_both(left, early, (rows_here, width + 128))
+    early = across_by[1:-1] + along_by[1:-2]
+    mine, theirs, info = start_both(left, crossed, early, (rows_here, width + 128))
     left = (*left, info)
     far_first, _, mine, theirs = together(along_by[-1][0], across_by[-1][0], mine, theirs)
     near_second, _ = together(across_by[-1][1], far_first)
@@ -315,7 +326,7 @@
 def per_device(embeddings, group_of, cluster_id):
     rows_here, width = embeddings.shape
     devices = lax.axis_size("blk") * lax.axis_size("sub") * lax.axis_size("pair")
-    small = devices * rows_here * width * 2 <= GATHER_LIMIT
+    small = devices * rows_here * width * 2 <= GATHER_LIMIT and lax.axis_size("blk") > 3
     fits = width % 128 == 0 and rows_here % (32 * PARTS) == 0 and rows_here <= 256
     if small and fits and lax.axis_size("sub") == 2 and lax.axis_size("pair") == 2:
         return by_block(embeddings, group_of, cluster_id)

time: 36.5 us -> 36.9 us (1.011)
  waiting for transfers between devices: 5.04 us -> 6.08 us
  starting transfers between devices: 25 us -> 24.3 us
    ppermute x7, waiting for transfers between devices: 2.29 us -> 3.74 us  [along(): return lax.ppermute(rows, ('blk', 'pair'), hops)]
    ppermute x7 -> x6, waiting for transfers between devices: 1.07 us -> 0.15 us  [across(): return lax.ppermute(rows, ('sub', 'pair'), [(0, 3), (1, 2), (2, 1), (3, 0)])]
    ppermute x7, starting transfers between devices: 17 us -> 16.3 us  [along(): return lax.ppermute(rows, ('blk', 'pair'), hops)]
    ppermute x6, starting transfers between devices: 1.29 us -> 1.8 us  [other_core(): return lax.ppermute(rows, 'pair', [(0, 1), (1, 0)])]
    ppermute x6, waiting for transfers between devices: 1.69 us -> 2.19 us  [other_core(): return lax.ppermute(rows, 'pair', [(0, 1), (1, 0)])]
    ppermute x7 -> x6, starting transfers between devices: 6.7 us -> 6.29 us  [across(): return lax.ppermute(rows, ('sub', 'pair'), [(0, 3), (1, 2), (2, 1), (3, 0)])]
    pallas_call x5 -> x6, Pallas kernels: 4.52 us -> 4.57 us  [call(): pl.pallas_call(kernel, out_shape=[jax.ShapeDtypeStruct(shape, dtype) for...]
  transfers between devices with their start and end apart: 20 -> 19, of which waited for: 8 -> 8; matrix products, arithmetic and copies ran while one was open for 0% -> 0% of each run, Pallas kernels for 8% -> 8%
where the time goes in v21:
time: 36.9 us; the launch traced here: 36.7 us
  starting transfers between devices  24.3 us (66%)
  waiting for transfers between devices  6.08 us (16%)
  Pallas kernels  4.57 us (12%)
  local copies, waits for them, and re-layouts  1.67 us (5%)
    ppermute x7, starting transfers between devices, along(): return lax.ppermute(rows, ('blk', 'pair'), hops)  16.3 us
    ppermute x6, starting transfers between devices, across(): return lax.ppermute(rows, ('sub', 'pair'), [(0, 3), (1, 2), (2, 1), (3, 0)])  6.29 us
    pallas_call x6, Pallas kernels, call(): pl.pallas_call(kernel, out_shape=[jax.ShapeDtypeStruct(shape, dtype) for...  4.57 us
    ppermute x7, waiting for transfers between devices, along(): return lax.ppermute(rows, ('blk', 'pair'), hops)  3.74 us
    ppermute x6, waiting for transfers between devices, other_core(): return lax.ppermute(rows, 'pair', [(0, 1), (1, 0)])  2.19 us
    ppermute x6, starting transfers between devices, other_core(): return lax.ppermute(rows, 'pair', [(0, 1), (1, 0)])  1.8 us
    unnamed x6, local copies, waits for them, and re-layouts  1.67 us
  transfers between devices with their start and end apart: 19, of which 8 were waited for; matrix products, arithmetic and copies ran while one was open for 0% of the time, Pallas kernels for 8%

profile of v21, /device:TPU:0, one launch (start us, length us, event | category | flops | bytes accessed | tf_op | source)
XLA Modules:
  0.0 36.7 jit_solution(11598699883236222955)
XLA Ops:
  0.0 2.4 %collective-permute-start.2 = (bf16[192,768]{1,0:T(8,128)(2,1)}, bf16[192,768]{1,0:T(8,128)(2,1)S(1)}, u32[]{:S(2)}, u32[]{:S(2)}) collective-permute-start(bf16[192,768]{1,0:T(8,128)(2,1)} %rows.3), channel_id=1, source_target_pairs={{0,3},{1,2},{2,1},{3,0},{4,7},{5,6},{6,5},{7,4},{8,11},{9,10},{10,... | collective-permute-start | bytes 884744 | tf_op jit(solution)/shard_map/ppermute | solution.py:279
  2.4 0.0 copy-start
  2.4 1.0 %copy-done = bf16[192,768]{1,0:T(8,128)(2,1)S(1)} copy-done((bf16[192,768]{1,0:T(8,128)(2,1)S(1)}, bf16[192,768]{1,0:T(8,128)(2,1)}, u32[]{:S(2)}) %copy-start) | copy-done | bytes 294936
  3.4 0.0 copy-start.2
  3.4 2.9 %collective-permute-start.3 = (bf16[584,128]{1,0:T(8,128)(2,1)S(1)}, bf16[584,128]{1,0:T(8,128)(2,1)S(1)}, u32[]{:S(2)}, u32[]{:S(2)}) collective-permute-start(bf16[584,128]{1,0:T(8,128)(2,1)S(1)} %shard_map.38), channel_id=1, source_target_pairs={{4,1},{5,0},{0,9},{1,8},{8,13},{9,12},{12,5},{13,4},{6,3},{7,2},{2... | collective-permute-start | bytes 448520 | tf_op jit(solution)/shard_map/ppermute | solution.py:276
  6.3 0.0 copy-start.1
  6.3 0.0 copy-done.2
  6.3 0.7 %copy-done.1 = s32[192,1]{0,1:T(1,128)S(1)} copy-done((s32[192,1]{0,1:T(1,128)S(1)}, s32[192,1]{0,1:T(1,128)}, u32[]{:S(2)}) %copy-start.1) | copy-done | bytes 792
  7.0 0.1 shard_map.37
  7.1 1.1 %collective-permute-start.1 = (bf16[584,128]{1,0:T(8,128)(2,1)S(1)}, bf16[584,128]{1,0:T(8,128)(2,1)S(1)}, u32[]{:S(2)}, u32[]{:S(2)}) collective-permute-start(bf16[584,128]{1,0:T(8,128)(2,1)S(1)} %get-tuple-element.33), channel_id=1, source_target_pairs={{4,1},{5,0},{0,9},{1,8},{8,13},{9,12},{12,5},{13,4},{6,3},{7,2},{2... | collective-permute-start | bytes 448520 | tf_op jit(solution)/shard_map/ppermute | solution.py:276
  8.2 2.1 %collective-permute-done.3.refs_2_ = bf16[584,128]{1,0:T(8,128)(2,1)S(1)} collective-permute-done((bf16[584,128]{1,0:T(8,128)(2,1)S(1)}, bf16[584,128]{1,0:T(8,128)(2,1)S(1)}, u32[]{:S(2)}, u32[]{:S(2)}) %collective-permute-start.3) | collective-permute-done | bytes 149536 | tf_op jit(solution)/shard_map/ppermute | solution.py:276
  10.2 0.0 collective-permute-start.5
  10.2 3.1 %collective-permute-start.4 = (bf16[584,128]{1,0:T(8,128)(2,1)S(1)}, bf16[584,128]{1,0:T(8,128)(2,1)S(1)}, u32[]{:S(2)}, u32[]{:S(2)}) collective-permute-start(bf16[584,128]{1,0:T(8,128)(2,1)S(1)} %collective-permute-done.3.refs_2_), channel_id=1, source_target_pairs={{4,1},{5,0},{0,9},{1,8},{8,13},{9,12},{12,5},{13,4},{6,3},{7,2},{2... | collective-permute-start | bytes 448520 | tf_op jit(solution)/shard_map/ppermute | solution.py:276
  13.3 0.7 %collective-permute-start = (bf16[1160,128]{1,0:T(8,128)(2,1)S(1)}, bf16[1160,128]{1,0:T(8,128)(2,1)S(1)}, u32[]{:S(2)}, u32[]{:S(2)}) collective-permute-start(bf16[1160,128]{1,0:T(8,128)(2,1)S(1)} %get-tuple-element.32.whole.own), channel_id=1, source_target_pairs={{0,1},{1,0},{2,3},{3,2},{4,5},{5,4},{6,7},{7,6},{8,9},{9,8},{10,11... | collective-permute-start | bytes 890888 | tf_op jit(solution)/shard_map/ppermute | solution.py:282
  14.0 0.0 collective-permute-done.1.piece
  14.0 0.0 collective-permute-done.2.crossed
  14.1 1.1 %collective-permute-start.7 = (bf16[584,128]{1,0:T(8,128)(2,1)S(1)}, bf16[584,128]{1,0:T(8,128)(2,1)S(1)}, u32[]{:S(2)}, u32[]{:S(2)}) collective-permute-start(bf16[584,128]{1,0:T(8,128)(2,1)S(1)} %shard_map.39.refs_3_), channel_id=1, source_target_pairs={{0,3},{1,2},{2,1},{3,0},{4,7},{5,6},{6,5},{7,4},{8,11},{9,10},{10,... | collective-permute-start | bytes 448520 | tf_op jit(solution)/shard_map/ppermute | solution.py:279
  15.2 1.1 %collective-permute-start.6 = (bf16[584,128]{1,0:T(8,128)(2,1)S(1)}, bf16[584,128]{1,0:T(8,128)(2,1)S(1)}, u32[]{:S(2)}, u32[]{:S(2)}) collective-permute-start(bf16[584,128]{1,0:T(8,128)(2,1)S(1)} %shard_map.39.refs_3_), channel_id=1, source_target_pairs={{4,1},{5,0},{0,9},{1,8},{8,13},{9,12},{12,5},{13,4},{6,3},{7,2},{2... | collective-permute-start | bytes 448520 | tf_op jit(solution)/shard_map/ppermute | solution.py:276
  16.3 0.0 collective-permute-done.5.refs_0_
  16.3 1.3 %collective-permute-done.4.refs_0_ = bf16[584,128]{1,0:T(8,128)(2,1)S(1)} collective-permute-done((bf16[584,128]{1,0:T(8,128)(2,1)S(1)}, bf16[584,128]{1,0:T(8,128)(2,1)S(1)}, u32[]{:S(2)}, u32[]{:S(2)}) %collective-permute-start.4) | collective-permute-done | bytes 149536 | tf_op jit(solution)/shard_map/ppermute | solution.py:276
  17.6 0.5 %collective-permute-start.9 = (bf16[584,128]{1,0:T(8,128)(2,1)S(1)}, bf16[584,128]{1,0:T(8,128)(2,1)S(1)}, u32[]{:S(2)}, u32[]{:S(2)}) collective-permute-start(bf16[584,128]{1,0:T(8,128)(2,1)S(1)} %collective-permute-done.4.refs_0_), channel_id=1, source_target_pairs={{0,3},{1,2},{2,1},{3,0},{4,7},{5,6},{6,5},{7,4},{8,11},{9,10},{10,... | collective-permute-start | bytes 448520 | tf_op jit(solution)/shard_map/ppermute | solution.py:279
  18.1 3.4 %collective-permute-start.8 = (bf16[584,128]{1,0:T(8,128)(2,1)S(1)}, bf16[584,128]{1,0:T(8,128)(2,1)S(1)}, u32[]{:S(2)}, u32[]{:S(2)}) collective-permute-start(bf16[584,128]{1,0:T(8,128)(2,1)S(1)} %collective-permute-done.4.refs_0_), channel_id=1, source_target_pairs={{4,1},{5,0},{0,9},{1,8},{8,13},{9,12},{12,5},{13,4},{6,3},{7,2},{2... | collective-permute-start | bytes 448520 | tf_op jit(solution)/shard_map/ppermute | solution.py:276
  21.4 0.0 collective-permute-done.7.refs_1_
  21.4 0.0 collective-permute-done.6.refs_1_
  21.4 1.0 %collective-permute-start.11 = (bf16[584,128]{1,0:T(8,128)(2,1)S(1)}, bf16[584,128]{1,0:T(8,128)(2,1)S(1)}, u32[]{:S(2)}, u32[]{:S(2)}) collective-permute-start(bf16[584,128]{1,0:T(8,128)(2,1)S(1)} %collective-permute-done.6.refs_1_), channel_id=1, source_target_pairs={{0,3},{1,2},{2,1},{3,0},{4,7},{5,6},{6,5},{7,4},{8,11},{9,10},{10,... | collective-permute-start | bytes 448520 | tf_op jit(solution)/shard_map/ppermute | solution.py:279
  22.5 1.9 %collective-permute-start.12 = (bf16[584,128]{1,0:T(8,128)(2,1)S(1)}, bf16[584,128]{1,0:T(8,128)(2,1)S(1)}, u32[]{:S(2)}, u32[]{:S(2)}) collective-permute-start(bf16[584,128]{1,0:T(8,128)(2,1)S(1)} %collective-permute-done.6.refs_1_), channel_id=1, source_target_pairs={{4,1},{5,0},{0,9},{1,8},{8,13},{9,12},{12,5},{13,4},{6,3},{7,2},{2... | collective-permute-start | bytes 448520 | tf_op jit(solution)/shard_map/ppermute | solution.py:276
  24.4 0.0 collective-permute-done.other
  24.4 1.5 %shard_map.40 = (f32[192,896]{1,0:T(8,128)S(1)}, f32[192,896]{1,0:T(8,128)S(1)}, f32[384,128]{1,0:T(8,128)S(1)}) custom-call(bf16[1160,128]{1,0:T(8,128)(2,1)S(1)} %get-tuple-element.32.whole.own, bf16[1160,128]{1,0:T(8,128)(2,1)S(1)} %collective-permute-done.other, bf16[192,768]{1,0:T(8,128)(2,1)S(1)} %collective-permute-done.2.crossed, ...), custom_call_target="tpu_custom_call" | custom-call | tf_op jit(solution)/shard_map/pallas_call | solution.py:229
  25.9 0.0 collective-permute-done.9.refs_2_
  25.9 0.0 collective-permute-done.8.refs_4_
  26.0 1.3 %collective-permute-start.10 = (bf16[584,128]{1,0:T(8,128)(2,1)S(1)}, bf16[584,128]{1,0:T(8,128)(2,1)S(1)}, u32[]{:S(2)}, u32[]{:S(2)}) collective-permute-start(bf16[584,128]{1,0:T(8,128)(2,1)S(1)} %collective-permute-done.8.refs_4_), channel_id=1, source_target_pairs={{0,3},{1,2},{2,1},{3,0},{4,7},{5,6},{6,5},{7,4},{8,11},{9,10},{10,... | collective-permute-start | bytes 448520 | tf_op jit(solution)/shard_map/ppermute | solution.py:279
  27.3 0.1 collective-permute-done.11.refs_3_
  27.4 2.7 %collective-permute-start.13 = (bf16[584,128]{1,0:T(8,128)(2,1)S(1)}, bf16[584,128]{1,0:T(8,128)(2,1)S(1)}, u32[]{:S(2)}, u32[]{:S(2)}) collective-permute-start(bf16[584,128]{1,0:T(8,128)(2,1)S(1)} %collective-permute-done.11.refs_3_), channel_id=1, source_target_pairs={{4,1},{5,0},{0,9},{1,8},{8,13},{9,12},{12,5},{13,4},{6,3},{7,2},{2... | collective-permute-start | bytes 448520 | tf_op jit(solution)/shard_map/ppermute | solution.py:276
  30.1 0.0 collective-permute-done.12.refs_5_
  30.1 1.4 %shard_map.41 = (f32[192,896]{1,0:T(8,128)S(1)}, bf16[64,896]{1,0:T(8,128)(2,1)S(1)}, bf16[64,896]{1,0:T(8,128)(2,1)S(1)}, bf16[64,896]{1,0:T(8,128)(2,1)S(1)}) custom-call(bf16[1160,128]{1,0:T(8,128)(2,1)S(1)} %get-tuple-element.32.whole.own, bf16[1160,128]{1,0:T(8,128)(2,1)S(1)} %collective-permute-done.other, ...), custom_call_target="tpu_custom_call", output_to_operand_aliasing={{0}: (9, {})} | custom-call | tf_op jit(solution)/shard_map/pallas_call | solution.py:229
  31.6 0.2 collective-permute-start.14
  31.8 0.4 collective-permute-start.15
  32.2 0.0 collective-permute-done.10.first
  32.2 0.2 collective-permute-start.16
  32.3 0.3 collective-permute-start.17
  32.7 0.3 collective-permute-done.14.refs_0_
  33.0 0.2 collective-permute-done.15.refs_1_
  33.1 0.3 collective-permute-done.16.refs_2_
  33.5 0.4 %collective-permute-done.13.second = bf16[584,128]{1,0:T(8,128)(2,1)S(1)} collective-permute-done((bf16[584,128]{1,0:T(8,128)(2,1)S(1)}, bf16[584,128]{1,0:T(8,128)(2,1)S(1)}, u32[]{:S(2)}, u32[]{:S(2)}) %collective-permute-start.13) | collective-permute-done | bytes 149536 | tf_op jit(solution)/shard_map/ppermute | solution.py:276
  33.9 0.0 collective-permute-start.18
  33.9 0.0 collective-permute-done.17.first_other
  33.9 1.4 %collective-permute-done.18.second_other = bf16[584,128]{1,0:T(8,128)(2,1)S(1)} collective-permute-done((bf16[584,128]{1,0:T(8,128)(2,1)S(1)}, bf16[584,128]{1,0:T(8,128)(2,1)S(1)}, u32[]{:S(2)}, u32[]{:S(2)}) %collective-permute-start.18) | collective-permute-done | bytes 149536 | tf_op jit(solution)/shard_map/ppermute | solution.py:282
  35.3 1.5 %shard_map.42 = bf16[192,768]{1,0:T(8,128)(2,1)} custom-call(bf16[1160,128]{1,0:T(8,128)(2,1)S(1)} %get-tuple-element.32.whole.own, f32[384,128]{1,0:T(8,128)S(1)} %get-tuple-element.39.info, bf16[584,128]{1,0:T(8,128)(2,1)S(1)} %collective-permute-done.10.first, bf16[584,128]{1,0:T(8,128)(2,1)S(1)} %collective-permute-done.13.second, ...), custom_call_target="tpu_custom_call" | custom-call | tf_op jit(solution)/shard_map/pallas_call | solution.py:229
  (2 shorter events, 0.0 us)
Async XLA Ops:
  0.0 14.0 %collective-permute-start.2 = (bf16[192,768]{1,0:T(8,128)(2,1)}, bf16[192,768]{1,0:T(8,128)(2,1)S(1)}, u32[]{:S(2)}, u32[]{:S(2)}) collective-permute-start(bf16[192,768]{1,0:T(8,128)(2,1)} %rows.3), channel_id=1, source_target_pairs={{0,3},{1,2},{2,1},{3,0},{4,7},{5,6},{6,5},{7,4},{8,11},{9,10},{10,... | collective-permute-start | bytes 884744 | tf_op jit(solution)/shard_map/ppermute | solution.py:279
  2.4 1.0 %copy-start = (bf16[192,768]{1,0:T(8,128)(2,1)S(1)}, bf16[192,768]{1,0:T(8,128)(2,1)}, u32[]{:S(2)}) copy-start(bf16[192,768]{1,0:T(8,128)(2,1)} %rows.3) | copy-start | bytes 884740
  3.4 3.0 %copy-start.2 = (s32[192]{0:T(256)S(1)}, s32[192]{0:T(256)}, u32[]{:S(2)}) copy-start(s32[192]{0:T(256)} %param.5) | copy-start | bytes 2308
  3.4 6.8 %collective-permute-start.3 = (bf16[584,128]{1,0:T(8,128)(2,1)S(1)}, bf16[584,128]{1,0:T(8,128)(2,1)S(1)}, u32[]{:S(2)}, u32[]{:S(2)}) collective-permute-start(bf16[584,128]{1,0:T(8,128)(2,1)S(1)} %shard_map.38), channel_id=1, source_target_pairs={{4,1},{5,0},{0,9},{1,8},{8,13},{9,12},{12,5},{13,4},{6,3},{7,2},{2... | collective-permute-start | bytes 448520 | tf_op jit(solution)/shard_map/ppermute | solution.py:276
  6.3 0.7 %copy-start.1 = (s32[192,1]{0,1:T(1,128)S(1)}, s32[192,1]{0,1:T(1,128)}, u32[]{:S(2)}) copy-start(s32[192,1]{0,1:T(1,128)} %param.4) | copy-start | bytes 2308
  7.1 7.0 %collective-permute-start.1 = (bf16[584,128]{1,0:T(8,128)(2,1)S(1)}, bf16[584,128]{1,0:T(8,128)(2,1)S(1)}, u32[]{:S(2)}, u32[]{:S(2)}) collective-permute-start(bf16[584,128]{1,0:T(8,128)(2,1)S(1)} %get-tuple-element.33), channel_id=1, source_target_pairs={{4,1},{5,0},{0,9},{1,8},{8,13},{9,12},{12,5},{13,4},{6,3},{7,2},{2... | collective-permute-start | bytes 448520 | tf_op jit(solution)/shard_map/ppermute | solution.py:276
  10.2 6.1 %collective-permute-start.5 = (bf16[584,128]{1,0:T(8,128)(2,1)S(1)}, bf16[584,128]{1,0:T(8,128)(2,1)S(1)}, u32[]{:S(2)}, u32[]{:S(2)}) collective-permute-start(bf16[584,128]{1,0:T(8,128)(2,1)S(1)} %collective-permute-done.3.refs_2_), channel_id=1, source_target_pairs={{0,3},{1,2},{2,1},{3,0},{4,7},{5,6},{6,5},{7,4},{8,11},{9,10},{10,... | collective-permute-start | bytes 448520 | tf_op jit(solution)/shard_map/ppermute | solution.py:279
  10.2 7.4 %collective-permute-start.4 = (bf16[584,128]{1,0:T(8,128)(2,1)S(1)}, bf16[584,128]{1,0:T(8,128)(2,1)S(1)}, u32[]{:S(2)}, u32[]{:S(2)}) collective-permute-start(bf16[584,128]{1,0:T(8,128)(2,1)S(1)} %collective-permute-done.3.refs_2_), channel_id=1, source_target_pairs={{4,1},{5,0},{0,9},{1,8},{8,13},{9,12},{12,5},{13,4},{6,3},{7,2},{2... | collective-permute-start | bytes 448520 | tf_op jit(solution)/shard_map/ppermute | solution.py:276
  13.3 11.1 %collective-permute-start = (bf16[1160,128]{1,0:T(8,128)(2,1)S(1)}, bf16[1160,128]{1,0:T(8,128)(2,1)S(1)}, u32[]{:S(2)}, u32[]{:S(2)}) collective-permute-start(bf16[1160,128]{1,0:T(8,128)(2,1)S(1)} %get-tuple-element.32.whole.own), channel_id=1, source_target_pairs={{0,1},{1,0},{2,3},{3,2},{4,5},{5,4},{6,7},{7,6},{8,9},{9,8},{10,11... | collective-permute-start | bytes 890888 | tf_op jit(solution)/shard_map/ppermute | solution.py:282
  14.1 7.4 %collective-permute-start.7 = (bf16[584,128]{1,0:T(8,128)(2,1)S(1)}, bf16[584,128]{1,0:T(8,128)(2,1)S(1)}, u32[]{:S(2)}, u32[]{:S(2)}) collective-permute-start(bf16[584,128]{1,0:T(8,128)(2,1)S(1)} %shard_map.39.refs_3_), channel_id=1, source_target_pairs={{0,3},{1,2},{2,1},{3,0},{4,7},{5,6},{6,5},{7,4},{8,11},{9,10},{10,... | collective-permute-start | bytes 448520 | tf_op jit(solution)/shard_map/ppermute | solution.py:279
  15.2 6.3 %collective-permute-start.6 = (bf16[584,128]{1,0:T(8,128)(2,1)S(1)}, bf16[584,128]{1,0:T(8,128)(2,1)S(1)}, u32[]{:S(2)}, u32[]{:S(2)}) collective-permute-start(bf16[584,128]{1,0:T(8,128)(2,1)S(1)} %shard_map.39.refs_3_), channel_id=1, source_target_pairs={{4,1},{5,0},{0,9},{1,8},{8,13},{9,12},{12,5},{13,4},{6,3},{7,2},{2... | collective-permute-start | bytes 448520 | tf_op jit(solution)/shard_map/ppermute | solution.py:276
  17.6 8.3 %collective-permute-start.9 = (bf16[584,128]{1,0:T(8,128)(2,1)S(1)}, bf16[584,128]{1,0:T(8,128)(2,1)S(1)}, u32[]{:S(2)}, u32[]{:S(2)}) collective-permute-start(bf16[584,128]{1,0:T(8,128)(2,1)S(1)} %collective-permute-done.4.refs_0_), channel_id=1, source_target_pairs={{0,3},{1,2},{2,1},{3,0},{4,7},{5,6},{6,5},{7,4},{8,11},{9,10},{10,... | collective-permute-start | bytes 448520 | tf_op jit(solution)/shard_map/ppermute | solution.py:279
  18.1 7.9 %collective-permute-start.8 = (bf16[584,128]{1,0:T(8,128)(2,1)S(1)}, bf16[584,128]{1,0:T(8,128)(2,1)S(1)}, u32[]{:S(2)}, u32[]{:S(2)}) collective-permute-start(bf16[584,128]{1,0:T(8,128)(2,1)S(1)} %collective-permute-done.4.refs_0_), channel_id=1, source_target_pairs={{4,1},{5,0},{0,9},{1,8},{8,13},{9,12},{12,5},{13,4},{6,3},{7,2},{2... | collective-permute-start | bytes 448520 | tf_op jit(solution)/shard_map/ppermute | solution.py:276
  21.4 6.0 %collective-permute-start.11 = (bf16[584,128]{1,0:T(8,128)(2,1)S(1)}, bf16[584,128]{1,0:T(8,128)(2,1)S(1)}, u32[]{:S(2)}, u32[]{:S(2)}) collective-permute-start(bf16[584,128]{1,0:T(8,128)(2,1)S(1)} %collective-permute-done.6.refs_1_), channel_id=1, source_target_pairs={{0,3},{1,2},{2,1},{3,0},{4,7},{5,6},{6,5},{7,4},{8,11},{9,10},{10,... | collective-permute-start | bytes 448520 | tf_op jit(solution)/shard_map/ppermute | solution.py:279
  22.5 7.7 %collective-permute-start.12 = (bf16[584,128]{1,0:T(8,128)(2,1)S(1)}, bf16[584,128]{1,0:T(8,128)(2,1)S(1)}, u32[]{:S(2)}, u32[]{:S(2)}) collective-permute-start(bf16[584,128]{1,0:T(8,128)(2,1)S(1)} %collective-permute-done.6.refs_1_), channel_id=1, source_target_pairs={{4,1},{5,0},{0,9},{1,8},{8,13},{9,12},{12,5},{13,4},{6,3},{7,2},{2... | collective-permute-start | bytes 448520 | tf_op jit(solution)/shard_map/ppermute | solution.py:276
  26.0 6.2 %collective-permute-start.10 = (bf16[584,128]{1,0:T(8,128)(2,1)S(1)}, bf16[584,128]{1,0:T(8,128)(2,1)S(1)}, u32[]{:S(2)}, u32[]{:S(2)}) collective-permute-start(bf16[584,128]{1,0:T(8,128)(2,1)S(1)} %collective-permute-done.8.refs_4_), channel_id=1, source_target_pairs={{0,3},{1,2},{2,1},{3,0},{4,7},{5,6},{6,5},{7,4},{8,11},{9,10},{10,... | collective-permute-start | bytes 448520 | tf_op jit(solution)/shard_map/ppermute | solution.py:279
  27.4 6.5 %collective-permute-start.13 = (bf16[584,128]{1,0:T(8,128)(2,1)S(1)}, bf16[584,128]{1,0:T(8,128)(2,1)S(1)}, u32[]{:S(2)}, u32[]{:S(2)}) collective-permute-start(bf16[584,128]{1,0:T(8,128)(2,1)S(1)} %collective-permute-done.11.refs_3_), channel_id=1, source_target_pairs={{4,1},{5,0},{0,9},{1,8},{8,13},{9,12},{12,5},{13,4},{6,3},{7,2},{2... | collective-permute-start | bytes 448520 | tf_op jit(solution)/shard_map/ppermute | solution.py:276
  31.6 1.4 %collective-permute-start.14 = (bf16[64,896]{1,0:T(8,128)(2,1)S(1)}, bf16[64,896]{1,0:T(8,128)(2,1)S(1)}, u32[]{:S(2)}, u32[]{:S(2)}) collective-permute-start(bf16[64,896]{1,0:T(8,128)(2,1)S(1)} %get-tuple-element.51), channel_id=1, source_target_pairs={{0,1},{1,0},{2,3},{3,2},{4,5},{5,4},{6,7},{7,6},{8,9},{9,8},{10,11... | collective-permute-start | bytes 344072 | tf_op jit(solution)/shard_map/ppermute | solution.py:282
  31.8 1.3 %collective-permute-start.15 = (bf16[64,896]{1,0:T(8,128)(2,1)S(1)}, bf16[64,896]{1,0:T(8,128)(2,1)S(1)}, u32[]{:S(2)}, u32[]{:S(2)}) collective-permute-start(bf16[64,896]{1,0:T(8,128)(2,1)S(1)} %get-tuple-element.52), channel_id=1, source_target_pairs={{0,1},{1,0},{2,3},{3,2},{4,5},{5,4},{6,7},{7,6},{8,9},{9,8},{10,11... | collective-permute-start | bytes 344072 | tf_op jit(solution)/shard_map/ppermute | solution.py:282
  32.2 1.3 %collective-permute-start.16 = (bf16[64,896]{1,0:T(8,128)(2,1)S(1)}, bf16[64,896]{1,0:T(8,128)(2,1)S(1)}, u32[]{:S(2)}, u32[]{:S(2)}) collective-permute-start(bf16[64,896]{1,0:T(8,128)(2,1)S(1)} %get-tuple-element.53), channel_id=1, source_target_pairs={{0,1},{1,0},{2,3},{3,2},{4,5},{5,4},{6,7},{7,6},{8,9},{9,8},{10,11... | collective-permute-start | bytes 344072 | tf_op jit(solution)/shard_map/ppermute | solution.py:282
  32.3 1.6 %collective-permute-start.17 = (bf16[584,128]{1,0:T(8,128)(2,1)S(1)}, bf16[584,128]{1,0:T(8,128)(2,1)S(1)}, u32[]{:S(2)}, u32[]{:S(2)}) collective-permute-start(bf16[584,128]{1,0:T(8,128)(2,1)S(1)} %collective-permute-done.10.first), channel_id=1, source_target_pairs={{0,1},{1,0},{2,3},{3,2},{4,5},{5,4},{6,7},{7,6},{8,9},{9,8},{10,11... | collective-permute-start | bytes 448520 | tf_op jit(solution)/shard_map/ppermute | solution.py:282
  33.9 1.4 %collective-permute-start.18 = (bf16[584,128]{1,0:T(8,128)(2,1)S(1)}, bf16[584,128]{1,0:T(8,128)(2,1)S(1)}, u32[]{:S(2)}, u32[]{:S(2)}) collective-permute-start(bf16[584,128]{1,0:T(8,128)(2,1)S(1)} %collective-permute-done.13.second), channel_id=1, source_target_pairs={{0,1},{1,0},{2,3},{3,2},{4,5},{5,4},{6,7},{7,6},{8,9},{9,8},{10,11... | collective-permute-start | bytes 448520 | tf_op jit(solution)/shard_map/ppermute | solution.py:282

commit v22 on v20

--- a/solution.py
+++ b/solution.py
@@ -285,7 +285,7 @@
     across_by = []
     for s in range(1, n_blk):
         moved = [along(piece) for piece in along_by[-1]]
-        swapped = [across(piece) for piece in along_by[-1]]
+        swapped = [across(piece) for piece in (along_by[-1] if s > 1 else together(first, second))]
         moved[0], swapped[0] = together(moved[0], swapped[0])
         if s < n_blk - 1:
             moved[1], swapped[1], _ = together(moved[1], swapped[1], moved[0])

time: 36.5 us -> 37.5 us (1.027)
  waiting for transfers between devices: 5.04 us -> 8.25 us
  starting transfers between devices: 25 us -> 22.9 us
    ppermute x7, starting transfers between devices: 17 us -> 11.9 us  [along(): return lax.ppermute(rows, ('blk', 'pair'), hops)]
    ppermute x7, waiting for transfers between devices: 1.07 us -> 5.06 us  [across(): return lax.ppermute(rows, ('sub', 'pair'), [(0, 3), (1, 2), (2, 1), (3, 0)])]
    ppermute x6, starting transfers between devices: 1.29 us -> 3.08 us  [other_core(): return lax.ppermute(rows, 'pair', [(0, 1), (1, 0)])]
    ppermute x7, starting transfers between devices: 6.7 us -> 7.87 us  [across(): return lax.ppermute(rows, ('sub', 'pair'), [(0, 3), (1, 2), (2, 1), (3, 0)])]
    ppermute x6, waiting for transfers between devices: 1.69 us -> 1.16 us  [other_core(): return lax.ppermute(rows, 'pair', [(0, 1), (1, 0)])]
where the time goes in v22:
time: 37.5 us; the launch traced here: 37.4 us
  starting transfers between devices  22.9 us (61%)
  waiting for transfers between devices  8.25 us (22%)
  Pallas kernels  4.53 us (12%)
  local copies, waits for them, and re-layouts  1.64 us (4%)
    ppermute x7, starting transfers between devices, along(): return lax.ppermute(rows, ('blk', 'pair'), hops)  11.9 us
    ppermute x7, starting transfers between devices, across(): return lax.ppermute(rows, ('sub', 'pair'), [(0, 3), (1, 2), (2, 1), (3, 0)])  7.87 us
    ppermute x7, waiting for transfers between devices, across(): return lax.ppermute(rows, ('sub', 'pair'), [(0, 3), (1, 2), (2, 1), (3, 0)])  5.06 us
    pallas_call x5, Pallas kernels, call(): pl.pallas_call(kernel, out_shape=[jax.ShapeDtypeStruct(shape, dtype) for...  4.53 us
    ppermute x6, starting transfers between devices, other_core(): return lax.ppermute(rows, 'pair', [(0, 1), (1, 0)])  3.08 us
    ppermute x7, waiting for transfers between devices, along(): return lax.ppermute(rows, ('blk', 'pair'), hops)  2.04 us
    unnamed x6, local copies, waits for them, and re-layouts  1.64 us
    ppermute x6, waiting for transfers between devices, other_core(): return lax.ppermute(rows, 'pair', [(0, 1), (1, 0)])  1.16 us
  transfers between devices with their start and end apart: 20, of which 8 were waited for; matrix products, arithmetic and copies ran while one was open for 0% of the time, Pallas kernels for 8%

profile of v22, /device:TPU:0, one launch (start us, length us, event | category | flops | bytes accessed | tf_op | source)
XLA Modules:
  0.0 37.4 jit_solution(11845061063504304858)
XLA Ops:
  0.0 0.0 copy-start
  0.0 1.0 %copy-done = bf16[192,768]{1,0:T(8,128)(2,1)S(1)} copy-done((bf16[192,768]{1,0:T(8,128)(2,1)S(1)}, bf16[192,768]{1,0:T(8,128)(2,1)}, u32[]{:S(2)}) %copy-start) | copy-done | bytes 294936
  1.0 0.0 copy-start.2
  1.0 3.5 %collective-permute-start.1 = (bf16[584,128]{1,0:T(8,128)(2,1)S(1)}, bf16[584,128]{1,0:T(8,128)(2,1)S(1)}, u32[]{:S(2)}, u32[]{:S(2)}) collective-permute-start(bf16[584,128]{1,0:T(8,128)(2,1)S(1)} %shard_map.38), channel_id=1, source_target_pairs={{4,1},{5,0},{0,9},{1,8},{8,13},{9,12},{12,5},{13,4},{6,3},{7,2},{2... | collective-permute-start | bytes 448520 | tf_op jit(solution)/shard_map/ppermute | solution.py:269
  4.5 0.0 copy-start.1
  4.5 0.0 copy-done.2
  4.5 0.7 %copy-done.1 = s32[192,1]{0,1:T(1,128)S(1)} copy-done((s32[192,1]{0,1:T(1,128)S(1)}, s32[192,1]{0,1:T(1,128)}, u32[]{:S(2)}) %copy-start.1) | copy-done | bytes 792
  5.2 0.1 shard_map.37
  5.3 1.8 %collective-permute-start.2 = (bf16[584,128]{1,0:T(8,128)(2,1)S(1)}, bf16[584,128]{1,0:T(8,128)(2,1)S(1)}, u32[]{:S(2)}, u32[]{:S(2)}) collective-permute-start(bf16[584,128]{1,0:T(8,128)(2,1)S(1)} %shard_map.38), channel_id=1, source_target_pairs={{0,3},{1,2},{2,1},{3,0},{4,7},{5,6},{6,5},{7,4},{8,11},{9,10},{10,... | collective-permute-start | bytes 448520 | tf_op jit(solution)/shard_map/ppermute | solution.py:272
  7.1 0.1 collective-permute-start.4
  7.2 1.8 %collective-permute-start.3 = (bf16[584,128]{1,0:T(8,128)(2,1)S(1)}, bf16[584,128]{1,0:T(8,128)(2,1)S(1)}, u32[]{:S(2)}, u32[]{:S(2)}) collective-permute-start(bf16[584,128]{1,0:T(8,128)(2,1)S(1)} %get-tuple-element.40), channel_id=1, source_target_pairs={{4,1},{5,0},{0,9},{1,8},{8,13},{9,12},{12,5},{13,4},{6,3},{7,2},{2... | collective-permute-start | bytes 448520 | tf_op jit(solution)/shard_map/ppermute | solution.py:269
  8.9 0.0 collective-permute-done.1.refs_4_
  9.0 2.4 %collective-permute-done.2.refs_0_ = bf16[584,128]{1,0:T(8,128)(2,1)S(1)} collective-permute-done((bf16[584,128]{1,0:T(8,128)(2,1)S(1)}, bf16[584,128]{1,0:T(8,128)(2,1)S(1)}, u32[]{:S(2)}, u32[]{:S(2)}) %collective-permute-start.2) | collective-permute-done | bytes 149536 | tf_op jit(solution)/shard_map/ppermute | solution.py:272
  11.4 2.2 %collective-permute-start.6 = (bf16[584,128]{1,0:T(8,128)(2,1)S(1)}, bf16[584,128]{1,0:T(8,128)(2,1)S(1)}, u32[]{:S(2)}, u32[]{:S(2)}) collective-permute-start(bf16[584,128]{1,0:T(8,128)(2,1)S(1)} %collective-permute-done.1.refs_4_), channel_id=1, source_target_pairs={{0,3},{1,2},{2,1},{3,0},{4,7},{5,6},{6,5},{7,4},{8,11},{9,10},{10,... | collective-permute-start | bytes 448520 | tf_op jit(solution)/shard_map/ppermute | solution.py:272
  13.6 0.1 collective-permute-start.5
  13.7 1.6 %collective-permute-start = (bf16[1160,128]{1,0:T(8,128)(2,1)S(1)}, bf16[1160,128]{1,0:T(8,128)(2,1)S(1)}, u32[]{:S(2)}, u32[]{:S(2)}) collective-permute-start(bf16[1160,128]{1,0:T(8,128)(2,1)S(1)} %get-tuple-element.36.own), channel_id=1, source_target_pairs={{0,1},{1,0},{2,3},{3,2},{4,5},{5,4},{6,7},{7,6},{8,9},{9,8},{10,11... | collective-permute-start | bytes 890888 | tf_op jit(solution)/shard_map/ppermute | solution.py:275
  15.3 0.0 collective-permute-done.4.refs_1_
  15.3 0.0 collective-permute-done.3.refs_5_
  15.3 1.5 %collective-permute-start.8 = (bf16[584,128]{1,0:T(8,128)(2,1)S(1)}, bf16[584,128]{1,0:T(8,128)(2,1)S(1)}, u32[]{:S(2)}, u32[]{:S(2)}) collective-permute-start(bf16[584,128]{1,0:T(8,128)(2,1)S(1)} %collective-permute-done.3.refs_5_), channel_id=1, source_target_pairs={{0,3},{1,2},{2,1},{3,0},{4,7},{5,6},{6,5},{7,4},{8,11},{9,10},{10,... | collective-permute-start | bytes 448520 | tf_op jit(solution)/shard_map/ppermute | solution.py:272
  16.8 0.0 collective-permute-start.7
  16.8 0.7 %collective-permute-done.6.refs_2_ = bf16[584,128]{1,0:T(8,128)(2,1)S(1)} collective-permute-done((bf16[584,128]{1,0:T(8,128)(2,1)S(1)}, bf16[584,128]{1,0:T(8,128)(2,1)S(1)}, u32[]{:S(2)}, u32[]{:S(2)}) %collective-permute-start.6) | collective-permute-done | bytes 149536 | tf_op jit(solution)/shard_map/ppermute | solution.py:272
  17.5 1.3 %collective-permute-done.5.refs_0_ = bf16[584,128]{1,0:T(8,128)(2,1)S(1)} collective-permute-done((bf16[584,128]{1,0:T(8,128)(2,1)S(1)}, bf16[584,128]{1,0:T(8,128)(2,1)S(1)}, u32[]{:S(2)}, u32[]{:S(2)}) %collective-permute-start.5) | collective-permute-done | bytes 149536 | tf_op jit(solution)/shard_map/ppermute | solution.py:269
  18.9 1.2 %collective-permute-start.10 = (bf16[584,128]{1,0:T(8,128)(2,1)S(1)}, bf16[584,128]{1,0:T(8,128)(2,1)S(1)}, u32[]{:S(2)}, u32[]{:S(2)}) collective-permute-start(bf16[584,128]{1,0:T(8,128)(2,1)S(1)} %collective-permute-done.5.refs_0_), channel_id=1, source_target_pairs={{0,3},{1,2},{2,1},{3,0},{4,7},{5,6},{6,5},{7,4},{8,11},{9,10},{10,... | collective-permute-start | bytes 448520 | tf_op jit(solution)/shard_map/ppermute | solution.py:272
  20.1 2.4 %collective-permute-start.9 = (bf16[584,128]{1,0:T(8,128)(2,1)S(1)}, bf16[584,128]{1,0:T(8,128)(2,1)S(1)}, u32[]{:S(2)}, u32[]{:S(2)}) collective-permute-start(bf16[584,128]{1,0:T(8,128)(2,1)S(1)} %collective-permute-done.5.refs_0_), channel_id=1, source_target_pairs={{4,1},{5,0},{0,9},{1,8},{8,13},{9,12},{12,5},{13,4},{6,3},{7,2},{2... | collective-permute-start | bytes 448520 | tf_op jit(solution)/shard_map/ppermute | solution.py:269
  22.5 0.0 collective-permute-done.8.refs_3_
  22.5 0.0 collective-permute-done.7.refs_1_
  22.5 1.0 %collective-permute-start.12 = (bf16[584,128]{1,0:T(8,128)(2,1)S(1)}, bf16[584,128]{1,0:T(8,128)(2,1)S(1)}, u32[]{:S(2)}, u32[]{:S(2)}) collective-permute-start(bf16[584,128]{1,0:T(8,128)(2,1)S(1)} %collective-permute-done.7.refs_1_), channel_id=1, source_target_pairs={{0,3},{1,2},{2,1},{3,0},{4,7},{5,6},{6,5},{7,4},{8,11},{9,10},{10,... | collective-permute-start | bytes 448520 | tf_op jit(solution)/shard_map/ppermute | solution.py:272
  23.4 2.2 %collective-permute-start.13 = (bf16[584,128]{1,0:T(8,128)(2,1)S(1)}, bf16[584,128]{1,0:T(8,128)(2,1)S(1)}, u32[]{:S(2)}, u32[]{:S(2)}) collective-permute-start(bf16[584,128]{1,0:T(8,128)(2,1)S(1)} %collective-permute-done.7.refs_1_), channel_id=1, source_target_pairs={{4,1},{5,0},{0,9},{1,8},{8,13},{9,12},{12,5},{13,4},{6,3},{7,2},{2... | collective-permute-start | bytes 448520 | tf_op jit(solution)/shard_map/ppermute | solution.py:269
  25.6 0.0 collective-permute-done.other
  25.6 1.5 %shard_map.39 = (f32[192,896]{1,0:T(8,128)S(1)}, f32[192,896]{1,0:T(8,128)S(1)}, f32[384,128]{1,0:T(8,128)S(1)}) custom-call(bf16[1160,128]{1,0:T(8,128)(2,1)S(1)} %get-tuple-element.36.own, bf16[1160,128]{1,0:T(8,128)(2,1)S(1)} %collective-permute-done.other, bf16[584,128]{1,0:T(8,128)(2,1)S(1)} %collective-permute-done.2.refs_0_, ...), custom_call_target="tpu_custom_call" | custom-call | tf_op jit(solution)/shard_map/pallas_call | solution.py:222
  27.2 0.0 collective-permute-done.10.refs_2_
  27.2 0.0 collective-permute-done.9.refs_4_
  27.2 0.1 collective-permute-start.11
  27.3 1.1 %collective-permute-done.12.refs_3_ = bf16[584,128]{1,0:T(8,128)(2,1)S(1)} collective-permute-done((bf16[584,128]{1,0:T(8,128)(2,1)S(1)}, bf16[584,128]{1,0:T(8,128)(2,1)S(1)}, u32[]{:S(2)}, u32[]{:S(2)}) %collective-permute-start.12) | collective-permute-done | bytes 149536 | tf_op jit(solution)/shard_map/ppermute | solution.py:272
  28.4 2.0 %collective-permute-start.14 = (bf16[584,128]{1,0:T(8,128)(2,1)S(1)}, bf16[584,128]{1,0:T(8,128)(2,1)S(1)}, u32[]{:S(2)}, u32[]{:S(2)}) collective-permute-start(bf16[584,128]{1,0:T(8,128)(2,1)S(1)} %collective-permute-done.12.refs_3_), channel_id=1, source_target_pairs={{4,1},{5,0},{0,9},{1,8},{8,13},{9,12},{12,5},{13,4},{6,3},{7,2},{2... | collective-permute-start | bytes 448520 | tf_op jit(solution)/shard_map/ppermute | solution.py:269
  30.3 0.0 collective-permute-done.13.refs_5_
  30.3 1.4 %shard_map.40 = (f32[192,896]{1,0:T(8,128)S(1)}, bf16[64,896]{1,0:T(8,128)(2,1)S(1)}, bf16[64,896]{1,0:T(8,128)(2,1)S(1)}, bf16[64,896]{1,0:T(8,128)(2,1)S(1)}) custom-call(bf16[1160,128]{1,0:T(8,128)(2,1)S(1)} %get-tuple-element.36.own, bf16[1160,128]{1,0:T(8,128)(2,1)S(1)} %collective-permute-done.other, ...), custom_call_target="tpu_custom_call", output_to_operand_aliasing={{0}: (9, {})} | custom-call | tf_op jit(solution)/shard_map/pallas_call | solution.py:222
  31.8 0.5 %collective-permute-start.15 = (bf16[64,896]{1,0:T(8,128)(2,1)S(1)}, bf16[64,896]{1,0:T(8,128)(2,1)S(1)}, u32[]{:S(2)}, u32[]{:S(2)}) collective-permute-start(bf16[64,896]{1,0:T(8,128)(2,1)S(1)} %get-tuple-element.59), channel_id=1, source_target_pairs={{0,1},{1,0},{2,3},{3,2},{4,5},{5,4},{6,7},{7,6},{8,9},{9,8},{10,11... | collective-permute-start | bytes 344072 | tf_op jit(solution)/shard_map/ppermute | solution.py:275
  32.3 0.1 collective-permute-start.16
  32.4 0.8 %collective-permute-done.11.first = bf16[584,128]{1,0:T(8,128)(2,1)S(1)} collective-permute-done((bf16[584,128]{1,0:T(8,128)(2,1)S(1)}, bf16[584,128]{1,0:T(8,128)(2,1)S(1)}, u32[]{:S(2)}, u32[]{:S(2)}) %collective-permute-start.11) | collective-permute-done | bytes 149536 | tf_op jit(solution)/shard_map/ppermute | solution.py:272
  33.2 0.4 collective-permute-start.17
  33.6 0.1 collective-permute-start.18
  33.7 0.0 collective-permute-done.15.refs_0_
  33.7 0.0 collective-permute-done.16.refs_1_
  33.7 0.7 %collective-permute-done.14.second = bf16[584,128]{1,0:T(8,128)(2,1)S(1)} collective-permute-done((bf16[584,128]{1,0:T(8,128)(2,1)S(1)}, bf16[584,128]{1,0:T(8,128)(2,1)S(1)}, u32[]{:S(2)}, u32[]{:S(2)}) %collective-permute-start.14) | collective-permute-done | bytes 149536 | tf_op jit(solution)/shard_map/ppermute | solution.py:269
  34.4 0.1 collective-permute-done.17.refs_2_
  34.5 0.4 collective-permute-start.19
  34.9 0.0 collective-permute-done.18.first_other
  34.9 1.0 %collective-permute-done.19.second_other = bf16[584,128]{1,0:T(8,128)(2,1)S(1)} collective-permute-done((bf16[584,128]{1,0:T(8,128)(2,1)S(1)}, bf16[584,128]{1,0:T(8,128)(2,1)S(1)}, u32[]{:S(2)}, u32[]{:S(2)}) %collective-permute-start.19) | collective-permute-done | bytes 149536 | tf_op jit(solution)/shard_map/ppermute | solution.py:275
  35.9 1.5 %shard_map.41 = bf16[192,768]{1,0:T(8,128)(2,1)} custom-call(bf16[1160,128]{1,0:T(8,128)(2,1)S(1)} %get-tuple-element.36.own, f32[384,128]{1,0:T(8,128)S(1)} %get-tuple-element.47.info, bf16[584,128]{1,0:T(8,128)(2,1)S(1)} %collective-permute-done.11.first, bf16[584,128]{1,0:T(8,128)(2,1)S(1)} %collective-permute-done.14.second, ...), custom_call_target="tpu_custom_call" | custom-call | tf_op jit(solution)/shard_map/pallas_call | solution.py:222
  (1 shorter events, 0.0 us)
Async XLA Ops:
  0.0 1.0 %copy-start = (bf16[192,768]{1,0:T(8,128)(2,1)S(1)}, bf16[192,768]{1,0:T(8,128)(2,1)}, u32[]{:S(2)}) copy-start(bf16[192,768]{1,0:T(8,128)(2,1)} %rows.3) | copy-start | bytes 884740
  1.0 3.6 %copy-start.2 = (s32[192]{0:T(256)S(1)}, s32[192]{0:T(256)}, u32[]{:S(2)}) copy-start(s32[192]{0:T(256)} %param.5) | copy-start | bytes 2308
  1.0 8.0 %collective-permute-start.1 = (bf16[584,128]{1,0:T(8,128)(2,1)S(1)}, bf16[584,128]{1,0:T(8,128)(2,1)S(1)}, u32[]{:S(2)}, u32[]{:S(2)}) collective-permute-start(bf16[584,128]{1,0:T(8,128)(2,1)S(1)} %shard_map.38), channel_id=1, source_target_pairs={{4,1},{5,0},{0,9},{1,8},{8,13},{9,12},{12,5},{13,4},{6,3},{7,2},{2... | collective-permute-start | bytes 448520 | tf_op jit(solution)/shard_map/ppermute | solution.py:269
  4.5 0.7 %copy-start.1 = (s32[192,1]{0,1:T(1,128)S(1)}, s32[192,1]{0,1:T(1,128)}, u32[]{:S(2)}) copy-start(s32[192,1]{0,1:T(1,128)} %param.4) | copy-start | bytes 2308
  5.3 6.1 %collective-permute-start.2 = (bf16[584,128]{1,0:T(8,128)(2,1)S(1)}, bf16[584,128]{1,0:T(8,128)(2,1)S(1)}, u32[]{:S(2)}, u32[]{:S(2)}) collective-permute-start(bf16[584,128]{1,0:T(8,128)(2,1)S(1)} %shard_map.38), channel_id=1, source_target_pairs={{0,3},{1,2},{2,1},{3,0},{4,7},{5,6},{6,5},{7,4},{8,11},{9,10},{10,... | collective-permute-start | bytes 448520 | tf_op jit(solution)/shard_map/ppermute | solution.py:272
  7.1 8.2 %collective-permute-start.4 = (bf16[584,128]{1,0:T(8,128)(2,1)S(1)}, bf16[584,128]{1,0:T(8,128)(2,1)S(1)}, u32[]{:S(2)}, u32[]{:S(2)}) collective-permute-start(bf16[584,128]{1,0:T(8,128)(2,1)S(1)} %get-tuple-element.40), channel_id=1, source_target_pairs={{0,3},{1,2},{2,1},{3,0},{4,7},{5,6},{6,5},{7,4},{8,11},{9,10},{10,... | collective-permute-start | bytes 448520 | tf_op jit(solution)/shard_map/ppermute | solution.py:272
  7.2 8.1 %collective-permute-start.3 = (bf16[584,128]{1,0:T(8,128)(2,1)S(1)}, bf16[584,128]{1,0:T(8,128)(2,1)S(1)}, u32[]{:S(2)}, u32[]{:S(2)}) collective-permute-start(bf16[584,128]{1,0:T(8,128)(2,1)S(1)} %get-tuple-element.40), channel_id=1, source_target_pairs={{4,1},{5,0},{0,9},{1,8},{8,13},{9,12},{12,5},{13,4},{6,3},{7,2},{2... | collective-permute-start | bytes 448520 | tf_op jit(solution)/shard_map/ppermute | solution.py:269
  11.4 6.1 %collective-permute-start.6 = (bf16[584,128]{1,0:T(8,128)(2,1)S(1)}, bf16[584,128]{1,0:T(8,128)(2,1)S(1)}, u32[]{:S(2)}, u32[]{:S(2)}) collective-permute-start(bf16[584,128]{1,0:T(8,128)(2,1)S(1)} %collective-permute-done.1.refs_4_), channel_id=1, source_target_pairs={{0,3},{1,2},{2,1},{3,0},{4,7},{5,6},{6,5},{7,4},{8,11},{9,10},{10,... | collective-permute-start | bytes 448520 | tf_op jit(solution)/shard_map/ppermute | solution.py:272
  13.6 5.3 %collective-permute-start.5 = (bf16[584,128]{1,0:T(8,128)(2,1)S(1)}, bf16[584,128]{1,0:T(8,128)(2,1)S(1)}, u32[]{:S(2)}, u32[]{:S(2)}) collective-permute-start(bf16[584,128]{1,0:T(8,128)(2,1)S(1)} %collective-permute-done.1.refs_4_), channel_id=1, source_target_pairs={{4,1},{5,0},{0,9},{1,8},{8,13},{9,12},{12,5},{13,4},{6,3},{7,2},{2... | collective-permute-start | bytes 448520 | tf_op jit(solution)/shard_map/ppermute | solution.py:269
  13.7 12.0 %collective-permute-start = (bf16[1160,128]{1,0:T(8,128)(2,1)S(1)}, bf16[1160,128]{1,0:T(8,128)(2,1)S(1)}, u32[]{:S(2)}, u32[]{:S(2)}) collective-permute-start(bf16[1160,128]{1,0:T(8,128)(2,1)S(1)} %get-tuple-element.36.own), channel_id=1, source_target_pairs={{0,1},{1,0},{2,3},{3,2},{4,5},{5,4},{6,7},{7,6},{8,9},{9,8},{10,11... | collective-permute-start | bytes 890888 | tf_op jit(solution)/shard_map/ppermute | solution.py:275
  15.3 7.2 %collective-permute-start.8 = (bf16[584,128]{1,0:T(8,128)(2,1)S(1)}, bf16[584,128]{1,0:T(8,128)(2,1)S(1)}, u32[]{:S(2)}, u32[]{:S(2)}) collective-permute-start(bf16[584,128]{1,0:T(8,128)(2,1)S(1)} %collective-permute-done.3.refs_5_), channel_id=1, source_target_pairs={{0,3},{1,2},{2,1},{3,0},{4,7},{5,6},{6,5},{7,4},{8,11},{9,10},{10,... | collective-permute-start | bytes 448520 | tf_op jit(solution)/shard_map/ppermute | solution.py:272
  16.8 5.7 %collective-permute-start.7 = (bf16[584,128]{1,0:T(8,128)(2,1)S(1)}, bf16[584,128]{1,0:T(8,128)(2,1)S(1)}, u32[]{:S(2)}, u32[]{:S(2)}) collective-permute-start(bf16[584,128]{1,0:T(8,128)(2,1)S(1)} %collective-permute-done.3.refs_5_), channel_id=1, source_target_pairs={{4,1},{5,0},{0,9},{1,8},{8,13},{9,12},{12,5},{13,4},{6,3},{7,2},{2... | collective-permute-start | bytes 448520 | tf_op jit(solution)/shard_map/ppermute | solution.py:269
  18.9 8.3 %collective-permute-start.10 = (bf16[584,128]{1,0:T(8,128)(2,1)S(1)}, bf16[584,128]{1,0:T(8,128)(2,1)S(1)}, u32[]{:S(2)}, u32[]{:S(2)}) collective-permute-start(bf16[584,128]{1,0:T(8,128)(2,1)S(1)} %collective-permute-done.5.refs_0_), channel_id=1, source_target_pairs={{0,3},{1,2},{2,1},{3,0},{4,7},{5,6},{6,5},{7,4},{8,11},{9,10},{10,... | collective-permute-start | bytes 448520 | tf_op jit(solution)/shard_map/ppermute | solution.py:272
  20.1 7.1 %collective-permute-start.9 = (bf16[584,128]{1,0:T(8,128)(2,1)S(1)}, bf16[584,128]{1,0:T(8,128)(2,1)S(1)}, u32[]{:S(2)}, u32[]{:S(2)}) collective-permute-start(bf16[584,128]{1,0:T(8,128)(2,1)S(1)} %collective-permute-done.5.refs_0_), channel_id=1, source_target_pairs={{4,1},{5,0},{0,9},{1,8},{8,13},{9,12},{12,5},{13,4},{6,3},{7,2},{2... | collective-permute-start | bytes 448520 | tf_op jit(solution)/shard_map/ppermute | solution.py:269
  22.5 5.9 %collective-permute-start.12 = (bf16[584,128]{1,0:T(8,128)(2,1)S(1)}, bf16[584,128]{1,0:T(8,128)(2,1)S(1)}, u32[]{:S(2)}, u32[]{:S(2)}) collective-permute-start(bf16[584,128]{1,0:T(8,128)(2,1)S(1)} %collective-permute-done.7.refs_1_), channel_id=1, source_target_pairs={{0,3},{1,2},{2,1},{3,0},{4,7},{5,6},{6,5},{7,4},{8,11},{9,10},{10,... | collective-permute-start | bytes 448520 | tf_op jit(solution)/shard_map/ppermute | solution.py:272
  23.4 6.9 %collective-permute-start.13 = (bf16[584,128]{1,0:T(8,128)(2,1)S(1)}, bf16[584,128]{1,0:T(8,128)(2,1)S(1)}, u32[]{:S(2)}, u32[]{:S(2)}) collective-permute-start(bf16[584,128]{1,0:T(8,128)(2,1)S(1)} %collective-permute-done.7.refs_1_), channel_id=1, source_target_pairs={{4,1},{5,0},{0,9},{1,8},{8,13},{9,12},{12,5},{13,4},{6,3},{7,2},{2... | collective-permute-start | bytes 448520 | tf_op jit(solution)/shard_map/ppermute | solution.py:269
  27.2 6.0 %collective-permute-start.11 = (bf16[584,128]{1,0:T(8,128)(2,1)S(1)}, bf16[584,128]{1,0:T(8,128)(2,1)S(1)}, u32[]{:S(2)}, u32[]{:S(2)}) collective-permute-start(bf16[584,128]{1,0:T(8,128)(2,1)S(1)} %collective-permute-done.9.refs_4_), channel_id=1, source_target_pairs={{0,3},{1,2},{2,1},{3,0},{4,7},{5,6},{6,5},{7,4},{8,11},{9,10},{10,... | collective-permute-start | bytes 448520 | tf_op jit(solution)/shard_map/ppermute | solution.py:272
  28.4 6.0 %collective-permute-start.14 = (bf16[584,128]{1,0:T(8,128)(2,1)S(1)}, bf16[584,128]{1,0:T(8,128)(2,1)S(1)}, u32[]{:S(2)}, u32[]{:S(2)}) collective-permute-start(bf16[584,128]{1,0:T(8,128)(2,1)S(1)} %collective-permute-done.12.refs_3_), channel_id=1, source_target_pairs={{4,1},{5,0},{0,9},{1,8},{8,13},{9,12},{12,5},{13,4},{6,3},{7,2},{2... | collective-permute-start | bytes 448520 | tf_op jit(solution)/shard_map/ppermute | solution.py:269
  31.8 1.9 %collective-permute-start.15 = (bf16[64,896]{1,0:T(8,128)(2,1)S(1)}, bf16[64,896]{1,0:T(8,128)(2,1)S(1)}, u32[]{:S(2)}, u32[]{:S(2)}) collective-permute-start(bf16[64,896]{1,0:T(8,128)(2,1)S(1)} %get-tuple-element.59), channel_id=1, source_target_pairs={{0,1},{1,0},{2,3},{3,2},{4,5},{5,4},{6,7},{7,6},{8,9},{9,8},{10,11... | collective-permute-start | bytes 344072 | tf_op jit(solution)/shard_map/ppermute | solution.py:275
  32.3 1.4 %collective-permute-start.16 = (bf16[64,896]{1,0:T(8,128)(2,1)S(1)}, bf16[64,896]{1,0:T(8,128)(2,1)S(1)}, u32[]{:S(2)}, u32[]{:S(2)}) collective-permute-start(bf16[64,896]{1,0:T(8,128)(2,1)S(1)} %get-tuple-element.60), channel_id=1, source_target_pairs={{0,1},{1,0},{2,3},{3,2},{4,5},{5,4},{6,7},{7,6},{8,9},{9,8},{10,11... | collective-permute-start | bytes 344072 | tf_op jit(solution)/shard_map/ppermute | solution.py:275
  33.2 1.3 %collective-permute-start.17 = (bf16[64,896]{1,0:T(8,128)(2,1)S(1)}, bf16[64,896]{1,0:T(8,128)(2,1)S(1)}, u32[]{:S(2)}, u32[]{:S(2)}) collective-permute-start(bf16[64,896]{1,0:T(8,128)(2,1)S(1)} %get-tuple-element.61), channel_id=1, source_target_pairs={{0,1},{1,0},{2,3},{3,2},{4,5},{5,4},{6,7},{7,6},{8,9},{9,8},{10,11... | collective-permute-start | bytes 344072 | tf_op jit(solution)/shard_map/ppermute | solution.py:275
  33.6 1.4 %collective-permute-start.18 = (bf16[584,128]{1,0:T(8,128)(2,1)S(1)}, bf16[584,128]{1,0:T(8,128)(2,1)S(1)}, u32[]{:S(2)}, u32[]{:S(2)}) collective-permute-start(bf16[584,128]{1,0:T(8,128)(2,1)S(1)} %collective-permute-done.11.first), channel_id=1, source_target_pairs={{0,1},{1,0},{2,3},{3,2},{4,5},{5,4},{6,7},{7,6},{8,9},{9,8},{10,11... | collective-permute-start | bytes 448520 | tf_op jit(solution)/shard_map/ppermute | solution.py:275
  34.5 1.4 %collective-permute-start.19 = (bf16[584,128]{1,0:T(8,128)(2,1)S(1)}, bf16[584,128]{1,0:T(8,128)(2,1)S(1)}, u32[]{:S(2)}, u32[]{:S(2)}) collective-permute-start(bf16[584,128]{1,0:T(8,128)(2,1)S(1)} %collective-permute-done.14.second), channel_id=1, source_target_pairs={{0,1},{1,0},{2,3},{3,2},{4,5},{5,4},{6,7},{7,6},{8,9},{9,8},{10,11... | collective-permute-start | bytes 448520 | tf_op jit(solution)/shard_map/ppermute | solution.py:275

commit v23 on v20

--- a/solution.py
+++ b/solution.py
@@ -202,16 +202,35 @@
         out[:, width:] = pair[top : top + count]
 
 
-def last_kernel(own, info, first, second, first_other, second_other, mine, *refs):
-    out = refs[-1]
+def join_kernel(own, info, first, second, mine, *refs):
+    *parts, out = refs
+    rows_here, wide = out.shape
+    width = wide - 128
+    theirs = jnp.concatenate([ref[...] for ref in parts], axis=0)
+    pair = theirs[:, width:].astype(F32)
+    numer = mine[:, :width] + theirs[:, :width].astype(F32)
+    denom = mine[:, width : width + 1] + (pair[:, 0:1] + pair[:, 1:2])
+    blocks = take_blocks([first, second], 1, rows_here)
+    left = left_rows((own,), rows_here)
+    store_sides(*add_blocks(left, info, blocks, numer, denom), [out])
+
+
+def last_kernel(own, info, first, second, total, out, staged, sems):
     rows_here, width = out.shape
-    theirs = jnp.concatenate([ref[...] for ref in refs[:-1]], axis=0)
-    blocks = take_blocks([first, second, first_other, second_other], 2, rows_here)
-    parts = theirs[:, width:].astype(F32)
-    numer = mine[:, :width] + theirs[:, :width].astype(F32)
-    denom = mine[:, width : width + 1] + (parts[:, 0:1] + parts[:, 1:2])
-    numer, denom = add_blocks(left_rows((own,), rows_here), info, blocks, numer, denom)
-    out[...] = (numer * (1.0 / denom)).astype(BF16)
+    blocks = take_blocks([first, second], 1, rows_here)
+    left = left_rows((own,), rows_here)
+    numer, denom = total[:, :width], total[:, width : width + 1]
+    numer, denom = add_blocks(left, info, blocks, numer, denom)
+    share = 1.0 / denom
+    count = rows_here // 4
+    copies = []
+    for part in range(4):
+        rows = slice(part * count, (part + 1) * count)
+        staged[rows, :] = (numer[rows] * share[rows]).astype(BF16)
+        copies.append(pltpu.make_async_copy(staged.at[rows, :], out.at[rows, :], sems.at[part]))
+        copies[-1].start()
+    for copy in copies:
+        copy.wait()
 
 
 def whole_in_vmem(count):
@@ -242,6 +261,17 @@
     shapes = [((rows_here, wide), F32)] + [((rows_here // PARTS, wide), BF16)] * PARTS
     kernel = functools.partial(both_kernel, len(right))
     return call(kernel, shapes, args, {len(args) - 2: 0})
+
+
+def finish(shape, args):
+    return pl.pallas_call(
+        last_kernel,
+        out_shape=jax.ShapeDtypeStruct(shape, BF16),
+        in_specs=whole_in_vmem(len(args)),
+        out_specs=pl.BlockSpec(memory_space=pl.ANY),
+        scratch_shapes=[pltpu.VMEM(shape, BF16), pltpu.SemaphoreType.DMA((4,))],
+        compiler_params=pltpu.CompilerParams(vmem_limit_bytes=VMEM_BYTES),
+    )(*args)
 
 
 def folded_ring(size):
@@ -303,12 +333,14 @@
     back = [other_core(part) for part in theirs[:-1]]
     last_first, theirs[-1] = together(last_first, theirs[-1])
     last_second, *back = together(last_second, *back, other_core(theirs[-1]))
-    last = (last_first, last_second)
-    (out,) = call(
-        last_kernel,
-        [((rows_here, width), BF16)],
-        [whole, info, *last, *[other_core(half) for half in last], mine, *back],
-    )
+    last = [other_core(last_first), other_core(last_second)]
+    (total,) = call(
+        join_kernel,
+        [((rows_here, width + 128), F32)],
+        [whole, info, last_first, last_second, mine, *back],
+        {4: 0},
+    )
+    out = finish((rows_here, width), [whole, info, *last, total])
     return out
 
 
@@ -316,7 +348,7 @@
     rows_here, width = embeddings.shape
     devices = lax.axis_size("blk") * lax.axis_size("sub") * lax.axis_size("pair")
     small = devices * rows_here * width * 2 <= GATHER_LIMIT
-    fits = width % 128 == 0 and rows_here % (32 * PARTS) == 0 and rows_here <= 256
+    fits = width % 128 == 0 and rows_here % (64 * PARTS) == 0 and rows_here <= 256
     if small and fits and lax.axis_size("sub") == 2 and lax.axis_size("pair") == 2:
         return by_block(embeddings, group_of, cluster_id)
     return by_group(embeddings, group_of, cluster_id)

time: 36.5 us -> 36.3 us (level)
  waiting for transfers between devices: 5.04 us -> 4.29 us
  Pallas kernels: 4.52 us -> 5.09 us
    pallas_call x0 -> x1, Pallas kernels: none -> 1.29 us  [finish(): pl.pallas_call(last_kernel, out_shape=jax.ShapeDtypeStruct(shape, BF16),...]
    ppermute x6, waiting for transfers between devices: 1.69 us -> 0.92 us  [other_core(): return lax.ppermute(rows, 'pair', [(0, 1), (1, 0)])]
    pallas_call x5, Pallas kernels: 4.52 us -> 3.8 us  [call(): pl.pallas_call(kernel, out_shape=[jax.ShapeDtypeStruct(shape, dtype) for...]
  transfers between devices with their start and end apart: 20 -> 20, of which waited for: 8 -> 8; matrix products, arithmetic and copies ran while one was open for 0% -> 0% of each run, Pallas kernels for 8% -> 10%
where the time goes in v23:
time: 36.3 us; the launch traced here: 36.1 us
  starting transfers between devices  25 us (69%)
  Pallas kernels  5.09 us (14%)
  waiting for transfers between devices  4.29 us (12%)
  local copies, waits for them, and re-layouts  1.64 us (5%)
    ppermute x7, starting transfers between devices, along(): return lax.ppermute(rows, ('blk', 'pair'), hops)  17 us
    ppermute x7, starting transfers between devices, across(): return lax.ppermute(rows, ('sub', 'pair'), [(0, 3), (1, 2), (2, 1), (3, 0)])  6.7 us
    pallas_call x5, Pallas kernels, call(): pl.pallas_call(kernel, out_shape=[jax.ShapeDtypeStruct(shape, dtype) for...  3.8 us
    ppermute x7, waiting for transfers between devices, along(): return lax.ppermute(rows, ('blk', 'pair'), hops)  2.3 us
    unnamed x6, local copies, waits for them, and re-layouts  1.64 us
    pallas_call x1, Pallas kernels, finish(): pl.pallas_call(last_kernel, out_shape=jax.ShapeDtypeStruct(shape, BF16),...  1.29 us
    ppermute x6, starting transfers between devices, other_core(): return lax.ppermute(rows, 'pair', [(0, 1), (1, 0)])  1.29 us
    ppermute x7, waiting for transfers between devices, across(): return lax.ppermute(rows, ('sub', 'pair'), [(0, 3), (1, 2), (2, 1), (3, 0)])  1.06 us
  transfers between devices with their start and end apart: 20, of which 8 were waited for; matrix products, arithmetic and copies ran while one was open for 0% of the time, Pallas kernels for 10%

profile of v23, /device:TPU:0, one launch (start us, length us, event | category | flops | bytes accessed | tf_op | source)
XLA Modules:
  0.0 36.1 jit_solution(18439500098518449506)
XLA Ops:
  0.0 0.0 copy-start
  0.0 1.0 %copy-done = bf16[192,768]{1,0:T(8,128)(2,1)S(1)} copy-done((bf16[192,768]{1,0:T(8,128)(2,1)S(1)}, bf16[192,768]{1,0:T(8,128)(2,1)}, u32[]{:S(2)}) %copy-start) | copy-done | bytes 294936
  1.0 0.0 copy-start.2
  1.0 2.4 %collective-permute-start.2 = (bf16[584,128]{1,0:T(8,128)(2,1)S(1)}, bf16[584,128]{1,0:T(8,128)(2,1)S(1)}, u32[]{:S(2)}, u32[]{:S(2)}) collective-permute-start(bf16[584,128]{1,0:T(8,128)(2,1)S(1)} %shard_map.38), channel_id=1, source_target_pairs={{0,3},{1,2},{2,1},{3,0},{4,7},{5,6},{6,5},{7,4},{8,11},{9,10},{10,... | collective-permute-start | bytes 448520 | tf_op jit(solution)/shard_map/ppermute | solution.py:302
  3.4 2.9 %collective-permute-start.1 = (bf16[584,128]{1,0:T(8,128)(2,1)S(1)}, bf16[584,128]{1,0:T(8,128)(2,1)S(1)}, u32[]{:S(2)}, u32[]{:S(2)}) collective-permute-start(bf16[584,128]{1,0:T(8,128)(2,1)S(1)} %shard_map.38), channel_id=1, source_target_pairs={{4,1},{5,0},{0,9},{1,8},{8,13},{9,12},{12,5},{13,4},{6,3},{7,2},{2... | collective-permute-start | bytes 448520 | tf_op jit(solution)/shard_map/ppermute | solution.py:299
  6.3 0.0 copy-start.1
  6.3 0.0 copy-done.2
  6.3 0.7 %copy-done.1 = s32[192,1]{0,1:T(1,128)S(1)} copy-done((s32[192,1]{0,1:T(1,128)S(1)}, s32[192,1]{0,1:T(1,128)}, u32[]{:S(2)}) %copy-start.1) | copy-done | bytes 792
  7.0 0.1 shard_map.37
  7.1 0.1 collective-permute-start.4
  7.2 1.8 %collective-permute-start.3 = (bf16[584,128]{1,0:T(8,128)(2,1)S(1)}, bf16[584,128]{1,0:T(8,128)(2,1)S(1)}, u32[]{:S(2)}, u32[]{:S(2)}) collective-permute-start(bf16[584,128]{1,0:T(8,128)(2,1)S(1)} %get-tuple-element.36), channel_id=1, source_target_pairs={{4,1},{5,0},{0,9},{1,8},{8,13},{9,12},{12,5},{13,4},{6,3},{7,2},{2... | collective-permute-start | bytes 448520 | tf_op jit(solution)/shard_map/ppermute | solution.py:299
  9.0 0.0 collective-permute-done.2.refs_0_
  9.0 1.2 %collective-permute-done.1.refs_4_ = bf16[584,128]{1,0:T(8,128)(2,1)S(1)} collective-permute-done((bf16[584,128]{1,0:T(8,128)(2,1)S(1)}, bf16[584,128]{1,0:T(8,128)(2,1)S(1)}, u32[]{:S(2)}, u32[]{:S(2)}) %collective-permute-start.1) | collective-permute-done | bytes 149536 | tf_op jit(solution)/shard_map/ppermute | solution.py:299
  10.1 0.0 collective-permute-start.6
  10.1 3.1 %collective-permute-start.5 = (bf16[584,128]{1,0:T(8,128)(2,1)S(1)}, bf16[584,128]{1,0:T(8,128)(2,1)S(1)}, u32[]{:S(2)}, u32[]{:S(2)}) collective-permute-start(bf16[584,128]{1,0:T(8,128)(2,1)S(1)} %collective-permute-done.1.refs_4_), channel_id=1, source_target_pairs={{4,1},{5,0},{0,9},{1,8},{8,13},{9,12},{12,5},{13,4},{6,3},{7,2},{2... | collective-permute-start | bytes 448520 | tf_op jit(solution)/shard_map/ppermute | solution.py:299
  13.2 0.1 collective-permute-start
  13.3 0.0 collective-permute-done.4.refs_1_
  13.3 0.0 collective-permute-done.3.refs_5_
  13.3 1.7 %collective-permute-start.8 = (bf16[584,128]{1,0:T(8,128)(2,1)S(1)}, bf16[584,128]{1,0:T(8,128)(2,1)S(1)}, u32[]{:S(2)}, u32[]{:S(2)}) collective-permute-start(bf16[584,128]{1,0:T(8,128)(2,1)S(1)} %collective-permute-done.3.refs_5_), channel_id=1, source_target_pairs={{0,3},{1,2},{2,1},{3,0},{4,7},{5,6},{6,5},{7,4},{8,11},{9,10},{10,... | collective-permute-start | bytes 448520 | tf_op jit(solution)/shard_map/ppermute | solution.py:302
  15.1 1.2 %collective-permute-start.7 = (bf16[584,128]{1,0:T(8,128)(2,1)S(1)}, bf16[584,128]{1,0:T(8,128)(2,1)S(1)}, u32[]{:S(2)}, u32[]{:S(2)}) collective-permute-start(bf16[584,128]{1,0:T(8,128)(2,1)S(1)} %collective-permute-done.3.refs_5_), channel_id=1, source_target_pairs={{4,1},{5,0},{0,9},{1,8},{8,13},{9,12},{12,5},{13,4},{6,3},{7,2},{2... | collective-permute-start | bytes 448520 | tf_op jit(solution)/shard_map/ppermute | solution.py:299
  16.2 0.3 collective-permute-done.6.refs_2_
  16.5 0.4 %collective-permute-done.5.refs_0_ = bf16[584,128]{1,0:T(8,128)(2,1)S(1)} collective-permute-done((bf16[584,128]{1,0:T(8,128)(2,1)S(1)}, bf16[584,128]{1,0:T(8,128)(2,1)S(1)}, u32[]{:S(2)}, u32[]{:S(2)}) %collective-permute-start.5) | collective-permute-done | bytes 149536 | tf_op jit(solution)/shard_map/ppermute | solution.py:299
  16.9 1.2 %collective-permute-start.10 = (bf16[584,128]{1,0:T(8,128)(2,1)S(1)}, bf16[584,128]{1,0:T(8,128)(2,1)S(1)}, u32[]{:S(2)}, u32[]{:S(2)}) collective-permute-start(bf16[584,128]{1,0:T(8,128)(2,1)S(1)} %collective-permute-done.5.refs_0_), channel_id=1, source_target_pairs={{0,3},{1,2},{2,1},{3,0},{4,7},{5,6},{6,5},{7,4},{8,11},{9,10},{10,... | collective-permute-start | bytes 448520 | tf_op jit(solution)/shard_map/ppermute | solution.py:302
  18.0 3.4 %collective-permute-start.9 = (bf16[584,128]{1,0:T(8,128)(2,1)S(1)}, bf16[584,128]{1,0:T(8,128)(2,1)S(1)}, u32[]{:S(2)}, u32[]{:S(2)}) collective-permute-start(bf16[584,128]{1,0:T(8,128)(2,1)S(1)} %collective-permute-done.5.refs_0_), channel_id=1, source_target_pairs={{4,1},{5,0},{0,9},{1,8},{8,13},{9,12},{12,5},{13,4},{6,3},{7,2},{2... | collective-permute-start | bytes 448520 | tf_op jit(solution)/shard_map/ppermute | solution.py:299
  21.4 0.0 collective-permute-done.8.refs_3_
  21.4 0.0 collective-permute-done.7.refs_1_
  21.4 0.1 collective-permute-start.12
  21.6 2.6 %collective-permute-start.13 = (bf16[584,128]{1,0:T(8,128)(2,1)S(1)}, bf16[584,128]{1,0:T(8,128)(2,1)S(1)}, u32[]{:S(2)}, u32[]{:S(2)}) collective-permute-start(bf16[584,128]{1,0:T(8,128)(2,1)S(1)} %collective-permute-done.7.refs_1_), channel_id=1, source_target_pairs={{4,1},{5,0},{0,9},{1,8},{8,13},{9,12},{12,5},{13,4},{6,3},{7,2},{2... | collective-permute-start | bytes 448520 | tf_op jit(solution)/shard_map/ppermute | solution.py:299
  24.1 0.0 collective-permute-done.other
  24.1 1.5 %shard_map.39 = (f32[192,896]{1,0:T(8,128)S(1)}, f32[192,896]{1,0:T(8,128)S(1)}, f32[384,128]{1,0:T(8,128)S(1)}) custom-call(bf16[1160,128]{1,0:T(8,128)(2,1)S(1)} %get-tuple-element.34.own, bf16[1160,128]{1,0:T(8,128)(2,1)S(1)} %collective-permute-done.other, bf16[584,128]{1,0:T(8,128)(2,1)S(1)} %collective-permute-done.2.refs_0_, ...), custom_call_target="tpu_custom_call" | custom-call | tf_op jit(solution)/shard_map/pallas_call | solution.py:241
  25.6 0.0 collective-permute-done.10.refs_2_
  25.7 0.0 collective-permute-done.9.refs_4_
  25.7 1.1 %collective-permute-start.11 = (bf16[584,128]{1,0:T(8,128)(2,1)S(1)}, bf16[584,128]{1,0:T(8,128)(2,1)S(1)}, u32[]{:S(2)}, u32[]{:S(2)}) collective-permute-start(bf16[584,128]{1,0:T(8,128)(2,1)S(1)} %collective-permute-done.9.refs_4_), channel_id=1, source_target_pairs={{0,3},{1,2},{2,1},{3,0},{4,7},{5,6},{6,5},{7,4},{8,11},{9,10},{10,... | collective-permute-start | bytes 448520 | tf_op jit(solution)/shard_map/ppermute | solution.py:302
  26.8 0.7 %collective-permute-done.12.refs_3_ = bf16[584,128]{1,0:T(8,128)(2,1)S(1)} collective-permute-done((bf16[584,128]{1,0:T(8,128)(2,1)S(1)}, bf16[584,128]{1,0:T(8,128)(2,1)S(1)}, u32[]{:S(2)}, u32[]{:S(2)}) %collective-permute-start.12) | collective-permute-done | bytes 149536 | tf_op jit(solution)/shard_map/ppermute | solution.py:302
  27.5 2.2 %collective-permute-start.15 = (bf16[584,128]{1,0:T(8,128)(2,1)S(1)}, bf16[584,128]{1,0:T(8,128)(2,1)S(1)}, u32[]{:S(2)}, u32[]{:S(2)}) collective-permute-start(bf16[584,128]{1,0:T(8,128)(2,1)S(1)} %collective-permute-done.12.refs_3_), channel_id=1, source_target_pairs={{4,1},{5,0},{0,9},{1,8},{8,13},{9,12},{12,5},{13,4},{6,3},{7,2},{2... | collective-permute-start | bytes 448520 | tf_op jit(solution)/shard_map/ppermute | solution.py:299
  29.7 0.0 collective-permute-done.13.refs_5_
  29.7 1.4 %shard_map.40 = (f32[192,896]{1,0:T(8,128)S(1)}, bf16[64,896]{1,0:T(8,128)(2,1)S(1)}, bf16[64,896]{1,0:T(8,128)(2,1)S(1)}, bf16[64,896]{1,0:T(8,128)(2,1)S(1)}) custom-call(bf16[1160,128]{1,0:T(8,128)(2,1)S(1)} %get-tuple-element.34.own, bf16[1160,128]{1,0:T(8,128)(2,1)S(1)} %collective-permute-done.other, ...), custom_call_target="tpu_custom_call", output_to_operand_aliasing={{0}: (9, {})} | custom-call | tf_op jit(solution)/shard_map/pallas_call | solution.py:241
  31.1 0.1 collective-permute-start.16
  31.2 0.5 %collective-permute-start.17 = (bf16[64,896]{1,0:T(8,128)(2,1)S(1)}, bf16[64,896]{1,0:T(8,128)(2,1)S(1)}, u32[]{:S(2)}, u32[]{:S(2)}) collective-permute-start(bf16[64,896]{1,0:T(8,128)(2,1)S(1)} %get-tuple-element.56), channel_id=1, source_target_pairs={{0,1},{1,0},{2,3},{3,2},{4,5},{5,4},{6,7},{7,6},{8,9},{9,8},{10,11... | collective-permute-start | bytes 344072 | tf_op jit(solution)/shard_map/ppermute | solution.py:305
  31.7 0.0 collective-permute-done.11.first
  31.7 0.3 collective-permute-start.18
  32.0 0.2 collective-permute-start.14
  32.2 0.3 collective-permute-done.16.refs_0_
  32.5 0.2 collective-permute-done.17.refs_1_
  32.7 0.8 %collective-permute-done.15.second = bf16[584,128]{1,0:T(8,128)(2,1)S(1)} collective-permute-done((bf16[584,128]{1,0:T(8,128)(2,1)S(1)}, bf16[584,128]{1,0:T(8,128)(2,1)S(1)}, u32[]{:S(2)}, u32[]{:S(2)}) %collective-permute-start.15) | collective-permute-done | bytes 149536 | tf_op jit(solution)/shard_map/ppermute | solution.py:299
  33.4 0.0 collective-permute-done.18.refs_2_
  33.4 0.2 collective-permute-start.19
  33.6 0.7 %shard_map.41.total = f32[192,896]{1,0:T(8,128)S(1)} custom-call(bf16[1160,128]{1,0:T(8,128)(2,1)S(1)} %get-tuple-element.34.own, f32[384,128]{1,0:T(8,128)S(1)} %get-tuple-element.43.info, bf16[584,128]{1,0:T(8,128)(2,1)S(1)} %collective-permute-done.11.first, bf16[584,128]{1,0:T(8,128)(2,1)S(1)} %collective-permute-done.15.second, ...), custom_call_target="tpu_custom_call", output_to_operand_aliasing={{}: (4, {})} | custom-call | tf_op jit(solution)/shard_map/pallas_call | solution.py:241
  34.4 0.0 collective-permute-done.14.first
  34.4 0.5 %collective-permute-done.19.second = bf16[584,128]{1,0:T(8,128)(2,1)S(1)} collective-permute-done((bf16[584,128]{1,0:T(8,128)(2,1)S(1)}, bf16[584,128]{1,0:T(8,128)(2,1)S(1)}, u32[]{:S(2)}, u32[]{:S(2)}) %collective-permute-start.19) | collective-permute-done | bytes 149536 | tf_op jit(solution)/shard_map/ppermute | solution.py:305
  34.8 1.3 %shard_map.42 = bf16[192,768]{1,0:T(8,128)(2,1)} custom-call(bf16[1160,128]{1,0:T(8,128)(2,1)S(1)} %get-tuple-element.34.own, f32[384,128]{1,0:T(8,128)S(1)} %get-tuple-element.43.info, bf16[584,128]{1,0:T(8,128)(2,1)S(1)} %collective-permute-done.14.first, bf16[584,128]{1,0:T(8,128)(2,1)S(1)} %collective-permute-done.19.second, f32[192,896]{1,0:T(8,128)S(1)} %shard_map.41.total), custom_call_target="tpu_custom_call" | custom-call | tf_op jit(solution)/shard_map/pallas_call | solution.py:267
  (1 shorter events, 0.0 us)
Async XLA Ops:
  0.0 1.0 %copy-start = (bf16[192,768]{1,0:T(8,128)(2,1)S(1)}, bf16[192,768]{1,0:T(8,128)(2,1)}, u32[]{:S(2)}) copy-start(bf16[192,768]{1,0:T(8,128)(2,1)} %rows.3) | copy-start | bytes 884740
  1.0 5.3 %copy-start.2 = (s32[192]{0:T(256)S(1)}, s32[192]{0:T(256)}, u32[]{:S(2)}) copy-start(s32[192]{0:T(256)} %param.5) | copy-start | bytes 2308
  1.0 8.0 %collective-permute-start.2 = (bf16[584,128]{1,0:T(8,128)(2,1)S(1)}, bf16[584,128]{1,0:T(8,128)(2,1)S(1)}, u32[]{:S(2)}, u32[]{:S(2)}) collective-permute-start(bf16[584,128]{1,0:T(8,128)(2,1)S(1)} %shard_map.38), channel_id=1, source_target_pairs={{0,3},{1,2},{2,1},{3,0},{4,7},{5,6},{6,5},{7,4},{8,11},{9,10},{10,... | collective-permute-start | bytes 448520 | tf_op jit(solution)/shard_map/ppermute | solution.py:302
  3.4 6.7 %collective-permute-start.1 = (bf16[584,128]{1,0:T(8,128)(2,1)S(1)}, bf16[584,128]{1,0:T(8,128)(2,1)S(1)}, u32[]{:S(2)}, u32[]{:S(2)}) collective-permute-start(bf16[584,128]{1,0:T(8,128)(2,1)S(1)} %shard_map.38), channel_id=1, source_target_pairs={{4,1},{5,0},{0,9},{1,8},{8,13},{9,12},{12,5},{13,4},{6,3},{7,2},{2... | collective-permute-start | bytes 448520 | tf_op jit(solution)/shard_map/ppermute | solution.py:299
  6.3 0.7 %copy-start.1 = (s32[192,1]{0,1:T(1,128)S(1)}, s32[192,1]{0,1:T(1,128)}, u32[]{:S(2)}) copy-start(s32[192,1]{0,1:T(1,128)} %param.4) | copy-start | bytes 2308
  7.1 6.2 %collective-permute-start.4 = (bf16[584,128]{1,0:T(8,128)(2,1)S(1)}, bf16[584,128]{1,0:T(8,128)(2,1)S(1)}, u32[]{:S(2)}, u32[]{:S(2)}) collective-permute-start(bf16[584,128]{1,0:T(8,128)(2,1)S(1)} %get-tuple-element.36), channel_id=1, source_target_pairs={{0,3},{1,2},{2,1},{3,0},{4,7},{5,6},{6,5},{7,4},{8,11},{9,10},{10,... | collective-permute-start | bytes 448520 | tf_op jit(solution)/shard_map/ppermute | solution.py:302
  7.2 6.1 %collective-permute-start.3 = (bf16[584,128]{1,0:T(8,128)(2,1)S(1)}, bf16[584,128]{1,0:T(8,128)(2,1)S(1)}, u32[]{:S(2)}, u32[]{:S(2)}) collective-permute-start(bf16[584,128]{1,0:T(8,128)(2,1)S(1)} %get-tuple-element.36), channel_id=1, source_target_pairs={{4,1},{5,0},{0,9},{1,8},{8,13},{9,12},{12,5},{13,4},{6,3},{7,2},{2... | collective-permute-start | bytes 448520 | tf_op jit(solution)/shard_map/ppermute | solution.py:299
  10.1 6.4 %collective-permute-start.6 = (bf16[584,128]{1,0:T(8,128)(2,1)S(1)}, bf16[584,128]{1,0:T(8,128)(2,1)S(1)}, u32[]{:S(2)}, u32[]{:S(2)}) collective-permute-start(bf16[584,128]{1,0:T(8,128)(2,1)S(1)} %collective-permute-done.1.refs_4_), channel_id=1, source_target_pairs={{0,3},{1,2},{2,1},{3,0},{4,7},{5,6},{6,5},{7,4},{8,11},{9,10},{10,... | collective-permute-start | bytes 448520 | tf_op jit(solution)/shard_map/ppermute | solution.py:302
  10.1 6.8 %collective-permute-start.5 = (bf16[584,128]{1,0:T(8,128)(2,1)S(1)}, bf16[584,128]{1,0:T(8,128)(2,1)S(1)}, u32[]{:S(2)}, u32[]{:S(2)}) collective-permute-start(bf16[584,128]{1,0:T(8,128)(2,1)S(1)} %collective-permute-done.1.refs_4_), channel_id=1, source_target_pairs={{4,1},{5,0},{0,9},{1,8},{8,13},{9,12},{12,5},{13,4},{6,3},{7,2},{2... | collective-permute-start | bytes 448520 | tf_op jit(solution)/shard_map/ppermute | solution.py:299
  13.2 10.9 %collective-permute-start = (bf16[1160,128]{1,0:T(8,128)(2,1)S(1)}, bf16[1160,128]{1,0:T(8,128)(2,1)S(1)}, u32[]{:S(2)}, u32[]{:S(2)}) collective-permute-start(bf16[1160,128]{1,0:T(8,128)(2,1)S(1)} %get-tuple-element.34.own), channel_id=1, source_target_pairs={{0,1},{1,0},{2,3},{3,2},{4,5},{5,4},{6,7},{7,6},{8,9},{9,8},{10,11... | collective-permute-start | bytes 890888 | tf_op jit(solution)/shard_map/ppermute | solution.py:305
  13.3 8.1 %collective-permute-start.8 = (bf16[584,128]{1,0:T(8,128)(2,1)S(1)}, bf16[584,128]{1,0:T(8,128)(2,1)S(1)}, u32[]{:S(2)}, u32[]{:S(2)}) collective-permute-start(bf16[584,128]{1,0:T(8,128)(2,1)S(1)} %collective-permute-done.3.refs_5_), channel_id=1, source_target_pairs={{0,3},{1,2},{2,1},{3,0},{4,7},{5,6},{6,5},{7,4},{8,11},{9,10},{10,... | collective-permute-start | bytes 448520 | tf_op jit(solution)/shard_map/ppermute | solution.py:302
  15.1 6.4 %collective-permute-start.7 = (bf16[584,128]{1,0:T(8,128)(2,1)S(1)}, bf16[584,128]{1,0:T(8,128)(2,1)S(1)}, u32[]{:S(2)}, u32[]{:S(2)}) collective-permute-start(bf16[584,128]{1,0:T(8,128)(2,1)S(1)} %collective-permute-done.3.refs_5_), channel_id=1, source_target_pairs={{4,1},{5,0},{0,9},{1,8},{8,13},{9,12},{12,5},{13,4},{6,3},{7,2},{2... | collective-permute-start | bytes 448520 | tf_op jit(solution)/shard_map/ppermute | solution.py:299
  16.9 8.8 %collective-permute-start.10 = (bf16[584,128]{1,0:T(8,128)(2,1)S(1)}, bf16[584,128]{1,0:T(8,128)(2,1)S(1)}, u32[]{:S(2)}, u32[]{:S(2)}) collective-permute-start(bf16[584,128]{1,0:T(8,128)(2,1)S(1)} %collective-permute-done.5.refs_0_), channel_id=1, source_target_pairs={{0,3},{1,2},{2,1},{3,0},{4,7},{5,6},{6,5},{7,4},{8,11},{9,10},{10,... | collective-permute-start | bytes 448520 | tf_op jit(solution)/shard_map/ppermute | solution.py:302
  18.0 7.6 %collective-permute-start.9 = (bf16[584,128]{1,0:T(8,128)(2,1)S(1)}, bf16[584,128]{1,0:T(8,128)(2,1)S(1)}, u32[]{:S(2)}, u32[]{:S(2)}) collective-permute-start(bf16[584,128]{1,0:T(8,128)(2,1)S(1)} %collective-permute-done.5.refs_0_), channel_id=1, source_target_pairs={{4,1},{5,0},{0,9},{1,8},{8,13},{9,12},{12,5},{13,4},{6,3},{7,2},{2... | collective-permute-start | bytes 448520 | tf_op jit(solution)/shard_map/ppermute | solution.py:299
  21.4 6.1 %collective-permute-start.12 = (bf16[584,128]{1,0:T(8,128)(2,1)S(1)}, bf16[584,128]{1,0:T(8,128)(2,1)S(1)}, u32[]{:S(2)}, u32[]{:S(2)}) collective-permute-start(bf16[584,128]{1,0:T(8,128)(2,1)S(1)} %collective-permute-done.7.refs_1_), channel_id=1, source_target_pairs={{0,3},{1,2},{2,1},{3,0},{4,7},{5,6},{6,5},{7,4},{8,11},{9,10},{10,... | collective-permute-start | bytes 448520 | tf_op jit(solution)/shard_map/ppermute | solution.py:302
  21.6 8.1 %collective-permute-start.13 = (bf16[584,128]{1,0:T(8,128)(2,1)S(1)}, bf16[584,128]{1,0:T(8,128)(2,1)S(1)}, u32[]{:S(2)}, u32[]{:S(2)}) collective-permute-start(bf16[584,128]{1,0:T(8,128)(2,1)S(1)} %collective-permute-done.7.refs_1_), channel_id=1, source_target_pairs={{4,1},{5,0},{0,9},{1,8},{8,13},{9,12},{12,5},{13,4},{6,3},{7,2},{2... | collective-permute-start | bytes 448520 | tf_op jit(solution)/shard_map/ppermute | solution.py:299
  25.7 6.0 %collective-permute-start.11 = (bf16[584,128]{1,0:T(8,128)(2,1)S(1)}, bf16[584,128]{1,0:T(8,128)(2,1)S(1)}, u32[]{:S(2)}, u32[]{:S(2)}) collective-permute-start(bf16[584,128]{1,0:T(8,128)(2,1)S(1)} %collective-permute-done.9.refs_4_), channel_id=1, source_target_pairs={{0,3},{1,2},{2,1},{3,0},{4,7},{5,6},{6,5},{7,4},{8,11},{9,10},{10,... | collective-permute-start | bytes 448520 | tf_op jit(solution)/shard_map/ppermute | solution.py:302
  27.5 5.9 %collective-permute-start.15 = (bf16[584,128]{1,0:T(8,128)(2,1)S(1)}, bf16[584,128]{1,0:T(8,128)(2,1)S(1)}, u32[]{:S(2)}, u32[]{:S(2)}) collective-permute-start(bf16[584,128]{1,0:T(8,128)(2,1)S(1)} %collective-permute-done.12.refs_3_), channel_id=1, source_target_pairs={{4,1},{5,0},{0,9},{1,8},{8,13},{9,12},{12,5},{13,4},{6,3},{7,2},{2... | collective-permute-start | bytes 448520 | tf_op jit(solution)/shard_map/ppermute | solution.py:299
  31.1 1.4 %collective-permute-start.16 = (bf16[64,896]{1,0:T(8,128)(2,1)S(1)}, bf16[64,896]{1,0:T(8,128)(2,1)S(1)}, u32[]{:S(2)}, u32[]{:S(2)}) collective-permute-start(bf16[64,896]{1,0:T(8,128)(2,1)S(1)} %get-tuple-element.55), channel_id=1, source_target_pairs={{0,1},{1,0},{2,3},{3,2},{4,5},{5,4},{6,7},{7,6},{8,9},{9,8},{10,11... | collective-permute-start | bytes 344072 | tf_op jit(solution)/shard_map/ppermute | solution.py:305
  31.2 1.5 %collective-permute-start.17 = (bf16[64,896]{1,0:T(8,128)(2,1)S(1)}, bf16[64,896]{1,0:T(8,128)(2,1)S(1)}, u32[]{:S(2)}, u32[]{:S(2)}) collective-permute-start(bf16[64,896]{1,0:T(8,128)(2,1)S(1)} %get-tuple-element.56), channel_id=1, source_target_pairs={{0,1},{1,0},{2,3},{3,2},{4,5},{5,4},{6,7},{7,6},{8,9},{9,8},{10,11... | collective-permute-start | bytes 344072 | tf_op jit(solution)/shard_map/ppermute | solution.py:305
  31.7 1.7 %collective-permute-start.18 = (bf16[64,896]{1,0:T(8,128)(2,1)S(1)}, bf16[64,896]{1,0:T(8,128)(2,1)S(1)}, u32[]{:S(2)}, u32[]{:S(2)}) collective-permute-start(bf16[64,896]{1,0:T(8,128)(2,1)S(1)} %get-tuple-element.57), channel_id=1, source_target_pairs={{0,1},{1,0},{2,3},{3,2},{4,5},{5,4},{6,7},{7,6},{8,9},{9,8},{10,11... | collective-permute-start | bytes 344072 | tf_op jit(solution)/shard_map/ppermute | solution.py:305
  32.0 2.3 %collective-permute-start.14 = (bf16[584,128]{1,0:T(8,128)(2,1)S(1)}, bf16[584,128]{1,0:T(8,128)(2,1)S(1)}, u32[]{:S(2)}, u32[]{:S(2)}) collective-permute-start(bf16[584,128]{1,0:T(8,128)(2,1)S(1)} %collective-permute-done.11.first), channel_id=1, source_target_pairs={{0,1},{1,0},{2,3},{3,2},{4,5},{5,4},{6,7},{7,6},{8,9},{9,8},{10,11... | collective-permute-start | bytes 448520 | tf_op jit(solution)/shard_map/ppermute | solution.py:305
  33.4 1.4 %collective-permute-start.19 = (bf16[584,128]{1,0:T(8,128)(2,1)S(1)}, bf16[584,128]{1,0:T(8,128)(2,1)S(1)}, u32[]{:S(2)}, u32[]{:S(2)}) collective-permute-start(bf16[584,128]{1,0:T(8,128)(2,1)S(1)} %collective-permute-done.15.second), channel_id=1, source_target_pairs={{0,1},{1,0},{2,3},{3,2},{4,5},{5,4},{6,7},{7,6},{8,9},{9,8},{10,11... | collective-permute-start | bytes 448520 | tf_op jit(solution)/shard_map/ppermute | solution.py:305

commit v24 on v23

--- a/solution.py
+++ b/solution.py
@@ -315,10 +315,14 @@
     across_by = []
     for s in range(1, n_blk):
         moved = [along(piece) for piece in along_by[-1]]
-        swapped = [across(piece) for piece in along_by[-1]]
-        moved[0], swapped[0] = together(moved[0], swapped[0])
-        if s < n_blk - 1:
-            moved[1], swapped[1], _ = together(moved[1], swapped[1], moved[0])
+        if s == 1:
+            swapped = [across(piece) for piece in together(first, second)]
+            moved[1], *swapped, _ = together(moved[1], *swapped, moved[0])
+        else:
+            swapped = [across(piece) for piece in along_by[-1]]
+            moved[0], swapped[0] = together(moved[0], swapped[0])
+            if s < n_blk - 1:
+                moved[1], swapped[1], _ = together(moved[1], swapped[1], moved[0])
         along_by.append(tuple(moved))
         across_by.append(tuple(swapped))
     left = (whole, other_core(whole))

time: 36.3 us -> 37.4 us (1.030)
  waiting for transfers between devices: 4.29 us -> 6.86 us
  starting transfers between devices: 25 us -> 23.6 us
    ppermute x7, waiting for transfers between devices: 1.06 us -> 4.69 us  [across(): return lax.ppermute(rows, ('sub', 'pair'), [(0, 3), (1, 2), (2, 1), (3, 0)])]
    ppermute x7, starting transfers between devices: 17 us -> 13.4 us  [along(): return lax.ppermute(rows, ('blk', 'pair'), hops)]
    ppermute x7, starting transfers between devices: 6.7 us -> 8.6 us  [across(): return lax.ppermute(rows, ('sub', 'pair'), [(0, 3), (1, 2), (2, 1), (3, 0)])]
    ppermute x7, waiting for transfers between devices: 2.3 us -> 1.75 us  [along(): return lax.ppermute(rows, ('blk', 'pair'), hops)]
    ppermute x6, waiting for transfers between devices: 0.92 us -> 0.42 us  [other_core(): return lax.ppermute(rows, 'pair', [(0, 1), (1, 0)])]
  transfers between devices with their start and end apart: 20 -> 20, of which waited for: 8 -> 9; matrix products, arithmetic and copies ran while one was open for 0% -> 0% of each run, Pallas kernels for 10% -> 10%
where the time goes in v24:
time: 37.4 us; the launch traced here: 37.2 us
  starting transfers between devices  23.6 us (63%)
  waiting for transfers between devices  6.86 us (18%)
  Pallas kernels  5.09 us (14%)
  local copies, waits for them, and re-layouts  1.64 us (4%)
    ppermute x7, starting transfers between devices, along(): return lax.ppermute(rows, ('blk', 'pair'), hops)  13.4 us
    ppermute x7, starting transfers between devices, across(): return lax.ppermute(rows, ('sub', 'pair'), [(0, 3), (1, 2), (2, 1), (3, 0)])  8.6 us
    ppermute x7, waiting for transfers between devices, across(): return lax.ppermute(rows, ('sub', 'pair'), [(0, 3), (1, 2), (2, 1), (3, 0)])  4.69 us
    pallas_call x5, Pallas kernels, call(): pl.pallas_call(kernel, out_shape=[jax.ShapeDtypeStruct(shape, dtype) for...  3.79 us
    ppermute x7, waiting for transfers between devices, along(): return lax.ppermute(rows, ('blk', 'pair'), hops)  1.75 us
    unnamed x6, local copies, waits for them, and re-layouts  1.64 us
    ppermute x6, starting transfers between devices, other_core(): return lax.ppermute(rows, 'pair', [(0, 1), (1, 0)])  1.55 us
    pallas_call x1, Pallas kernels, finish(): pl.pallas_call(last_kernel, out_shape=jax.ShapeDtypeStruct(shape, BF16),...  1.29 us
  transfers between devices with their start and end apart: 20, of which 9 were waited for; matrix products, arithmetic and copies ran while one was open for 0% of the time, Pallas kernels for 10%

profile of v24, /device:TPU:0, one launch (start us, length us, event | category | flops | bytes accessed | tf_op | source)
XLA Modules:
  0.0 37.2 jit_solution(9071847404401835984)
XLA Ops:
  0.0 0.0 copy-start
  0.0 1.0 %copy-done = bf16[192,768]{1,0:T(8,128)(2,1)S(1)} copy-done((bf16[192,768]{1,0:T(8,128)(2,1)S(1)}, bf16[192,768]{1,0:T(8,128)(2,1)}, u32[]{:S(2)}) %copy-start) | copy-done | bytes 294936
  1.0 0.0 copy-start.2
  1.0 3.5 %collective-permute-start.4 = (bf16[584,128]{1,0:T(8,128)(2,1)S(1)}, bf16[584,128]{1,0:T(8,128)(2,1)S(1)}, u32[]{:S(2)}, u32[]{:S(2)}) collective-permute-start(bf16[584,128]{1,0:T(8,128)(2,1)S(1)} %shard_map.38), channel_id=1, source_target_pairs={{4,1},{5,0},{0,9},{1,8},{8,13},{9,12},{12,5},{13,4},{6,3},{7,2},{2... | collective-permute-start | bytes 448520 | tf_op jit(solution)/shard_map/ppermute | solution.py:299
  4.5 0.0 copy-start.1
  4.5 0.0 copy-done.2
  4.5 0.7 %copy-done.1 = s32[192,1]{0,1:T(1,128)S(1)} copy-done((s32[192,1]{0,1:T(1,128)S(1)}, s32[192,1]{0,1:T(1,128)}, u32[]{:S(2)}) %copy-start.1) | copy-done | bytes 792
  5.2 0.1 shard_map.37
  5.3 1.8 %collective-permute-start.2 = (bf16[584,128]{1,0:T(8,128)(2,1)S(1)}, bf16[584,128]{1,0:T(8,128)(2,1)S(1)}, u32[]{:S(2)}, u32[]{:S(2)}) collective-permute-start(bf16[584,128]{1,0:T(8,128)(2,1)S(1)} %shard_map.38), channel_id=1, source_target_pairs={{0,3},{1,2},{2,1},{3,0},{4,7},{5,6},{6,5},{7,4},{8,11},{9,10},{10,... | collective-permute-start | bytes 448520 | tf_op jit(solution)/shard_map/ppermute | solution.py:302
  7.1 0.1 collective-permute-start.3
  7.2 1.8 %collective-permute-start.1 = (bf16[584,128]{1,0:T(8,128)(2,1)S(1)}, bf16[584,128]{1,0:T(8,128)(2,1)S(1)}, u32[]{:S(2)}, u32[]{:S(2)}) collective-permute-start(bf16[584,128]{1,0:T(8,128)(2,1)S(1)} %get-tuple-element.38), channel_id=1, source_target_pairs={{4,1},{5,0},{0,9},{1,8},{8,13},{9,12},{12,5},{13,4},{6,3},{7,2},{2... | collective-permute-start | bytes 448520 | tf_op jit(solution)/shard_map/ppermute | solution.py:299
  8.9 0.0 collective-permute-done.4.refs_4_
  9.0 1.0 %collective-permute-start.6 = (bf16[584,128]{1,0:T(8,128)(2,1)S(1)}, bf16[584,128]{1,0:T(8,128)(2,1)S(1)}, u32[]{:S(2)}, u32[]{:S(2)}) collective-permute-start(bf16[584,128]{1,0:T(8,128)(2,1)S(1)} %collective-permute-done.4.refs_4_), channel_id=1, source_target_pairs={{0,3},{1,2},{2,1},{3,0},{4,7},{5,6},{6,5},{7,4},{8,11},{9,10},{10,... | collective-permute-start | bytes 448520 | tf_op jit(solution)/shard_map/ppermute | solution.py:302
  10.0 3.4 %collective-permute-start.5 = (bf16[584,128]{1,0:T(8,128)(2,1)S(1)}, bf16[584,128]{1,0:T(8,128)(2,1)S(1)}, u32[]{:S(2)}, u32[]{:S(2)}) collective-permute-start(bf16[584,128]{1,0:T(8,128)(2,1)S(1)} %collective-permute-done.4.refs_4_), channel_id=1, source_target_pairs={{4,1},{5,0},{0,9},{1,8},{8,13},{9,12},{12,5},{13,4},{6,3},{7,2},{2... | collective-permute-start | bytes 448520 | tf_op jit(solution)/shard_map/ppermute | solution.py:299
  13.4 0.0 collective-permute-done.2.refs_0_
  13.4 0.1 collective-permute-start
  13.5 1.1 %collective-permute-done.3.refs_1_ = bf16[584,128]{1,0:T(8,128)(2,1)S(1)} collective-permute-done((bf16[584,128]{1,0:T(8,128)(2,1)S(1)}, bf16[584,128]{1,0:T(8,128)(2,1)S(1)}, u32[]{:S(2)}, u32[]{:S(2)}) %collective-permute-start.3) | collective-permute-done | bytes 149536 | tf_op jit(solution)/shard_map/ppermute | solution.py:302
  14.6 0.0 collective-permute-done.1.refs_5_
  14.6 2.2 %collective-permute-start.8 = (bf16[584,128]{1,0:T(8,128)(2,1)S(1)}, bf16[584,128]{1,0:T(8,128)(2,1)S(1)}, u32[]{:S(2)}, u32[]{:S(2)}) collective-permute-start(bf16[584,128]{1,0:T(8,128)(2,1)S(1)} %collective-permute-done.1.refs_5_), channel_id=1, source_target_pairs={{0,3},{1,2},{2,1},{3,0},{4,7},{5,6},{6,5},{7,4},{8,11},{9,10},{10,... | collective-permute-start | bytes 448520 | tf_op jit(solution)/shard_map/ppermute | solution.py:302
  16.8 0.1 collective-permute-start.7
  16.9 0.9 %collective-permute-done.6.refs_2_ = bf16[584,128]{1,0:T(8,128)(2,1)S(1)} collective-permute-done((bf16[584,128]{1,0:T(8,128)(2,1)S(1)}, bf16[584,128]{1,0:T(8,128)(2,1)S(1)}, u32[]{:S(2)}, u32[]{:S(2)}) %collective-permute-start.6) | collective-permute-done | bytes 149536 | tf_op jit(solution)/shard_map/ppermute | solution.py:302
  17.8 0.0 collective-permute-done.5.refs_0_
  17.8 2.2 %collective-permute-start.10 = (bf16[584,128]{1,0:T(8,128)(2,1)S(1)}, bf16[584,128]{1,0:T(8,128)(2,1)S(1)}, u32[]{:S(2)}, u32[]{:S(2)}) collective-permute-start(bf16[584,128]{1,0:T(8,128)(2,1)S(1)} %collective-permute-done.5.refs_0_), channel_id=1, source_target_pairs={{0,3},{1,2},{2,1},{3,0},{4,7},{5,6},{6,5},{7,4},{8,11},{9,10},{10,... | collective-permute-start | bytes 448520 | tf_op jit(solution)/shard_map/ppermute | solution.py:302
  20.0 0.2 collective-permute-start.9
  20.2 1.0 %collective-permute-done.8.refs_3_ = bf16[584,128]{1,0:T(8,128)(2,1)S(1)} collective-permute-done((bf16[584,128]{1,0:T(8,128)(2,1)S(1)}, bf16[584,128]{1,0:T(8,128)(2,1)S(1)}, u32[]{:S(2)}, u32[]{:S(2)}) %collective-permute-start.8) | collective-permute-done | bytes 149536 | tf_op jit(solution)/shard_map/ppermute | solution.py:302
  21.1 1.0 %collective-permute-done.7.refs_1_ = bf16[584,128]{1,0:T(8,128)(2,1)S(1)} collective-permute-done((bf16[584,128]{1,0:T(8,128)(2,1)S(1)}, bf16[584,128]{1,0:T(8,128)(2,1)S(1)}, u32[]{:S(2)}, u32[]{:S(2)}) %collective-permute-start.7) | collective-permute-done | bytes 149536 | tf_op jit(solution)/shard_map/ppermute | solution.py:299
  22.2 1.2 %collective-permute-start.12 = (bf16[584,128]{1,0:T(8,128)(2,1)S(1)}, bf16[584,128]{1,0:T(8,128)(2,1)S(1)}, u32[]{:S(2)}, u32[]{:S(2)}) collective-permute-start(bf16[584,128]{1,0:T(8,128)(2,1)S(1)} %collective-permute-done.7.refs_1_), channel_id=1, source_target_pairs={{0,3},{1,2},{2,1},{3,0},{4,7},{5,6},{6,5},{7,4},{8,11},{9,10},{10,... | collective-permute-start | bytes 448520 | tf_op jit(solution)/shard_map/ppermute | solution.py:302
  23.3 2.3 %collective-permute-start.13 = (bf16[584,128]{1,0:T(8,128)(2,1)S(1)}, bf16[584,128]{1,0:T(8,128)(2,1)S(1)}, u32[]{:S(2)}, u32[]{:S(2)}) collective-permute-start(bf16[584,128]{1,0:T(8,128)(2,1)S(1)} %collective-permute-done.7.refs_1_), channel_id=1, source_target_pairs={{4,1},{5,0},{0,9},{1,8},{8,13},{9,12},{12,5},{13,4},{6,3},{7,2},{2... | collective-permute-start | bytes 448520 | tf_op jit(solution)/shard_map/ppermute | solution.py:299
  25.7 0.0 collective-permute-done.other
  25.7 1.5 %shard_map.39 = (f32[192,896]{1,0:T(8,128)S(1)}, f32[192,896]{1,0:T(8,128)S(1)}, f32[384,128]{1,0:T(8,128)S(1)}) custom-call(bf16[1160,128]{1,0:T(8,128)(2,1)S(1)} %get-tuple-element.35.own, bf16[1160,128]{1,0:T(8,128)(2,1)S(1)} %collective-permute-done.other, bf16[584,128]{1,0:T(8,128)(2,1)S(1)} %collective-permute-done.2.refs_0_, ...), custom_call_target="tpu_custom_call" | custom-call | tf_op jit(solution)/shard_map/pallas_call | solution.py:241
  27.2 0.0 collective-permute-done.10.refs_2_
  27.2 0.0 collective-permute-done.9.refs_4_
  27.2 0.1 collective-permute-start.11
  27.3 0.9 %collective-permute-done.12.refs_3_ = bf16[584,128]{1,0:T(8,128)(2,1)S(1)} collective-permute-done((bf16[584,128]{1,0:T(8,128)(2,1)S(1)}, bf16[584,128]{1,0:T(8,128)(2,1)S(1)}, u32[]{:S(2)}, u32[]{:S(2)}) %collective-permute-start.12) | collective-permute-done | bytes 149536 | tf_op jit(solution)/shard_map/ppermute | solution.py:302
  28.2 2.1 %collective-permute-start.15 = (bf16[584,128]{1,0:T(8,128)(2,1)S(1)}, bf16[584,128]{1,0:T(8,128)(2,1)S(1)}, u32[]{:S(2)}, u32[]{:S(2)}) collective-permute-start(bf16[584,128]{1,0:T(8,128)(2,1)S(1)} %collective-permute-done.12.refs_3_), channel_id=1, source_target_pairs={{4,1},{5,0},{0,9},{1,8},{8,13},{9,12},{12,5},{13,4},{6,3},{7,2},{2... | collective-permute-start | bytes 448520 | tf_op jit(solution)/shard_map/ppermute | solution.py:299
  30.4 0.0 collective-permute-done.13.refs_5_
  30.4 1.4 %shard_map.40 = (f32[192,896]{1,0:T(8,128)S(1)}, bf16[64,896]{1,0:T(8,128)(2,1)S(1)}, bf16[64,896]{1,0:T(8,128)(2,1)S(1)}, bf16[64,896]{1,0:T(8,128)(2,1)S(1)}) custom-call(bf16[1160,128]{1,0:T(8,128)(2,1)S(1)} %get-tuple-element.35.own, bf16[1160,128]{1,0:T(8,128)(2,1)S(1)} %collective-permute-done.other, ...), custom_call_target="tpu_custom_call", output_to_operand_aliasing={{0}: (9, {})} | custom-call | tf_op jit(solution)/shard_map/pallas_call | solution.py:241
  31.8 0.5 %collective-permute-start.16 = (bf16[64,896]{1,0:T(8,128)(2,1)S(1)}, bf16[64,896]{1,0:T(8,128)(2,1)S(1)}, u32[]{:S(2)}, u32[]{:S(2)}) collective-permute-start(bf16[64,896]{1,0:T(8,128)(2,1)S(1)} %get-tuple-element.57), channel_id=1, source_target_pairs={{0,1},{1,0},{2,3},{3,2},{4,5},{5,4},{6,7},{7,6},{8,9},{9,8},{10,11... | collective-permute-start | bytes 344072 | tf_op jit(solution)/shard_map/ppermute | solution.py:305
  32.3 0.1 collective-permute-start.17
  32.4 0.8 %collective-permute-done.11.first = bf16[584,128]{1,0:T(8,128)(2,1)S(1)} collective-permute-done((bf16[584,128]{1,0:T(8,128)(2,1)S(1)}, bf16[584,128]{1,0:T(8,128)(2,1)S(1)}, u32[]{:S(2)}, u32[]{:S(2)}) %collective-permute-start.11) | collective-permute-done | bytes 149536 | tf_op jit(solution)/shard_map/ppermute | solution.py:302
  33.2 0.4 %collective-permute-start.18 = (bf16[64,896]{1,0:T(8,128)(2,1)S(1)}, bf16[64,896]{1,0:T(8,128)(2,1)S(1)}, u32[]{:S(2)}, u32[]{:S(2)}) collective-permute-start(bf16[64,896]{1,0:T(8,128)(2,1)S(1)} %get-tuple-element.59), channel_id=1, source_target_pairs={{0,1},{1,0},{2,3},{3,2},{4,5},{5,4},{6,7},{7,6},{8,9},{9,8},{10,11... | collective-permute-start | bytes 344072 | tf_op jit(solution)/shard_map/ppermute | solution.py:305
  33.6 0.1 collective-permute-start.14
  33.7 0.0 collective-permute-done.16.refs_0_
  33.7 0.0 collective-permute-done.17.refs_1_
  33.7 0.7 %collective-permute-done.15.second = bf16[584,128]{1,0:T(8,128)(2,1)S(1)} collective-permute-done((bf16[584,128]{1,0:T(8,128)(2,1)S(1)}, bf16[584,128]{1,0:T(8,128)(2,1)S(1)}, u32[]{:S(2)}, u32[]{:S(2)}) %collective-permute-start.15) | collective-permute-done | bytes 149536 | tf_op jit(solution)/shard_map/ppermute | solution.py:299
  34.4 0.2 collective-permute-done.18.refs_2_
  34.6 0.4 collective-permute-start.19
  34.9 0.8 %shard_map.41.total = f32[192,896]{1,0:T(8,128)S(1)} custom-call(bf16[1160,128]{1,0:T(8,128)(2,1)S(1)} %get-tuple-element.35.own, f32[384,128]{1,0:T(8,128)S(1)} %get-tuple-element.45.info, bf16[584,128]{1,0:T(8,128)(2,1)S(1)} %collective-permute-done.11.first, bf16[584,128]{1,0:T(8,128)(2,1)S(1)} %collective-permute-done.15.second, ...), custom_call_target="tpu_custom_call", output_to_operand_aliasing={{}: (4, {})} | custom-call | tf_op jit(solution)/shard_map/pallas_call | solution.py:241
  35.7 0.0 collective-permute-done.14.first
  35.7 0.2 collective-permute-done.19.second
  35.9 1.3 %shard_map.42 = bf16[192,768]{1,0:T(8,128)(2,1)} custom-call(bf16[1160,128]{1,0:T(8,128)(2,1)S(1)} %get-tuple-element.35.own, f32[384,128]{1,0:T(8,128)S(1)} %get-tuple-element.45.info, bf16[584,128]{1,0:T(8,128)(2,1)S(1)} %collective-permute-done.14.first, bf16[584,128]{1,0:T(8,128)(2,1)S(1)} %collective-permute-done.19.second, f32[192,896]{1,0:T(8,128)S(1)} %shard_map.41.total), custom_call_target="tpu_custom_call" | custom-call | tf_op jit(solution)/shard_map/pallas_call | solution.py:267
  (1 shorter events, 0.0 us)
Async XLA Ops:
  0.0 1.0 %copy-start = (bf16[192,768]{1,0:T(8,128)(2,1)S(1)}, bf16[192,768]{1,0:T(8,128)(2,1)}, u32[]{:S(2)}) copy-start(bf16[192,768]{1,0:T(8,128)(2,1)} %rows.3) | copy-start | bytes 884740
  1.0 3.6 %copy-start.2 = (s32[192]{0:T(256)S(1)}, s32[192]{0:T(256)}, u32[]{:S(2)}) copy-start(s32[192]{0:T(256)} %param.5) | copy-start | bytes 2308
  1.0 8.0 %collective-permute-start.4 = (bf16[584,128]{1,0:T(8,128)(2,1)S(1)}, bf16[584,128]{1,0:T(8,128)(2,1)S(1)}, u32[]{:S(2)}, u32[]{:S(2)}) collective-permute-start(bf16[584,128]{1,0:T(8,128)(2,1)S(1)} %shard_map.38), channel_id=1, source_target_pairs={{4,1},{5,0},{0,9},{1,8},{8,13},{9,12},{12,5},{13,4},{6,3},{7,2},{2... | collective-permute-start | bytes 448520 | tf_op jit(solution)/shard_map/ppermute | solution.py:299
  4.5 0.7 %copy-start.1 = (s32[192,1]{0,1:T(1,128)S(1)}, s32[192,1]{0,1:T(1,128)}, u32[]{:S(2)}) copy-start(s32[192,1]{0,1:T(1,128)} %param.4) | copy-start | bytes 2308
  5.3 8.1 %collective-permute-start.2 = (bf16[584,128]{1,0:T(8,128)(2,1)S(1)}, bf16[584,128]{1,0:T(8,128)(2,1)S(1)}, u32[]{:S(2)}, u32[]{:S(2)}) collective-permute-start(bf16[584,128]{1,0:T(8,128)(2,1)S(1)} %shard_map.38), channel_id=1, source_target_pairs={{0,3},{1,2},{2,1},{3,0},{4,7},{5,6},{6,5},{7,4},{8,11},{9,10},{10,... | collective-permute-start | bytes 448520 | tf_op jit(solution)/shard_map/ppermute | solution.py:302
  7.1 7.5 %collective-permute-start.3 = (bf16[584,128]{1,0:T(8,128)(2,1)S(1)}, bf16[584,128]{1,0:T(8,128)(2,1)S(1)}, u32[]{:S(2)}, u32[]{:S(2)}) collective-permute-start(bf16[584,128]{1,0:T(8,128)(2,1)S(1)} %get-tuple-element.38), channel_id=1, source_target_pairs={{0,3},{1,2},{2,1},{3,0},{4,7},{5,6},{6,5},{7,4},{8,11},{9,10},{10,... | collective-permute-start | bytes 448520 | tf_op jit(solution)/shard_map/ppermute | solution.py:302
  7.2 7.4 %collective-permute-start.1 = (bf16[584,128]{1,0:T(8,128)(2,1)S(1)}, bf16[584,128]{1,0:T(8,128)(2,1)S(1)}, u32[]{:S(2)}, u32[]{:S(2)}) collective-permute-start(bf16[584,128]{1,0:T(8,128)(2,1)S(1)} %get-tuple-element.38), channel_id=1, source_target_pairs={{4,1},{5,0},{0,9},{1,8},{8,13},{9,12},{12,5},{13,4},{6,3},{7,2},{2... | collective-permute-start | bytes 448520 | tf_op jit(solution)/shard_map/ppermute | solution.py:299
  9.0 8.8 %collective-permute-start.6 = (bf16[584,128]{1,0:T(8,128)(2,1)S(1)}, bf16[584,128]{1,0:T(8,128)(2,1)S(1)}, u32[]{:S(2)}, u32[]{:S(2)}) collective-permute-start(bf16[584,128]{1,0:T(8,128)(2,1)S(1)} %collective-permute-done.4.refs_4_), channel_id=1, source_target_pairs={{0,3},{1,2},{2,1},{3,0},{4,7},{5,6},{6,5},{7,4},{8,11},{9,10},{10,... | collective-permute-start | bytes 448520 | tf_op jit(solution)/shard_map/ppermute | solution.py:302
  10.0 7.8 %collective-permute-start.5 = (bf16[584,128]{1,0:T(8,128)(2,1)S(1)}, bf16[584,128]{1,0:T(8,128)(2,1)S(1)}, u32[]{:S(2)}, u32[]{:S(2)}) collective-permute-start(bf16[584,128]{1,0:T(8,128)(2,1)S(1)} %collective-permute-done.4.refs_4_), channel_id=1, source_target_pairs={{4,1},{5,0},{0,9},{1,8},{8,13},{9,12},{12,5},{13,4},{6,3},{7,2},{2... | collective-permute-start | bytes 448520 | tf_op jit(solution)/shard_map/ppermute | solution.py:299
  13.4 12.3 %collective-permute-start = (bf16[1160,128]{1,0:T(8,128)(2,1)S(1)}, bf16[1160,128]{1,0:T(8,128)(2,1)S(1)}, u32[]{:S(2)}, u32[]{:S(2)}) collective-permute-start(bf16[1160,128]{1,0:T(8,128)(2,1)S(1)} %get-tuple-element.35.own), channel_id=1, source_target_pairs={{0,1},{1,0},{2,3},{3,2},{4,5},{5,4},{6,7},{7,6},{8,9},{9,8},{10,11... | collective-permute-start | bytes 890888 | tf_op jit(solution)/shard_map/ppermute | solution.py:305
  14.6 6.6 %collective-permute-start.8 = (bf16[584,128]{1,0:T(8,128)(2,1)S(1)}, bf16[584,128]{1,0:T(8,128)(2,1)S(1)}, u32[]{:S(2)}, u32[]{:S(2)}) collective-permute-start(bf16[584,128]{1,0:T(8,128)(2,1)S(1)} %collective-permute-done.1.refs_5_), channel_id=1, source_target_pairs={{0,3},{1,2},{2,1},{3,0},{4,7},{5,6},{6,5},{7,4},{8,11},{9,10},{10,... | collective-permute-start | bytes 448520 | tf_op jit(solution)/shard_map/ppermute | solution.py:302
  16.8 5.4 %collective-permute-start.7 = (bf16[584,128]{1,0:T(8,128)(2,1)S(1)}, bf16[584,128]{1,0:T(8,128)(2,1)S(1)}, u32[]{:S(2)}, u32[]{:S(2)}) collective-permute-start(bf16[584,128]{1,0:T(8,128)(2,1)S(1)} %collective-permute-done.1.refs_5_), channel_id=1, source_target_pairs={{4,1},{5,0},{0,9},{1,8},{8,13},{9,12},{12,5},{13,4},{6,3},{7,2},{2... | collective-permute-start | bytes 448520 | tf_op jit(solution)/shard_map/ppermute | solution.py:299
  17.8 9.4 %collective-permute-start.10 = (bf16[584,128]{1,0:T(8,128)(2,1)S(1)}, bf16[584,128]{1,0:T(8,128)(2,1)S(1)}, u32[]{:S(2)}, u32[]{:S(2)}) collective-permute-start(bf16[584,128]{1,0:T(8,128)(2,1)S(1)} %collective-permute-done.5.refs_0_), channel_id=1, source_target_pairs={{0,3},{1,2},{2,1},{3,0},{4,7},{5,6},{6,5},{7,4},{8,11},{9,10},{10,... | collective-permute-start | bytes 448520 | tf_op jit(solution)/shard_map/ppermute | solution.py:302
  20.0 7.2 %collective-permute-start.9 = (bf16[584,128]{1,0:T(8,128)(2,1)S(1)}, bf16[584,128]{1,0:T(8,128)(2,1)S(1)}, u32[]{:S(2)}, u32[]{:S(2)}) collective-permute-start(bf16[584,128]{1,0:T(8,128)(2,1)S(1)} %collective-permute-done.5.refs_0_), channel_id=1, source_target_pairs={{4,1},{5,0},{0,9},{1,8},{8,13},{9,12},{12,5},{13,4},{6,3},{7,2},{2... | collective-permute-start | bytes 448520 | tf_op jit(solution)/shard_map/ppermute | solution.py:299
  22.2 6.0 %collective-permute-start.12 = (bf16[584,128]{1,0:T(8,128)(2,1)S(1)}, bf16[584,128]{1,0:T(8,128)(2,1)S(1)}, u32[]{:S(2)}, u32[]{:S(2)}) collective-permute-start(bf16[584,128]{1,0:T(8,128)(2,1)S(1)} %collective-permute-done.7.refs_1_), channel_id=1, source_target_pairs={{0,3},{1,2},{2,1},{3,0},{4,7},{5,6},{6,5},{7,4},{8,11},{9,10},{10,... | collective-permute-start | bytes 448520 | tf_op jit(solution)/shard_map/ppermute | solution.py:302
  23.3 7.0 %collective-permute-start.13 = (bf16[584,128]{1,0:T(8,128)(2,1)S(1)}, bf16[584,128]{1,0:T(8,128)(2,1)S(1)}, u32[]{:S(2)}, u32[]{:S(2)}) collective-permute-start(bf16[584,128]{1,0:T(8,128)(2,1)S(1)} %collective-permute-done.7.refs_1_), channel_id=1, source_target_pairs={{4,1},{5,0},{0,9},{1,8},{8,13},{9,12},{12,5},{13,4},{6,3},{7,2},{2... | collective-permute-start | bytes 448520 | tf_op jit(solution)/shard_map/ppermute | solution.py:299
  27.2 6.0 %collective-permute-start.11 = (bf16[584,128]{1,0:T(8,128)(2,1)S(1)}, bf16[584,128]{1,0:T(8,128)(2,1)S(1)}, u32[]{:S(2)}, u32[]{:S(2)}) collective-permute-start(bf16[584,128]{1,0:T(8,128)(2,1)S(1)} %collective-permute-done.9.refs_4_), channel_id=1, source_target_pairs={{0,3},{1,2},{2,1},{3,0},{4,7},{5,6},{6,5},{7,4},{8,11},{9,10},{10,... | collective-permute-start | bytes 448520 | tf_op jit(solution)/shard_map/ppermute | solution.py:302
  28.2 6.2 %collective-permute-start.15 = (bf16[584,128]{1,0:T(8,128)(2,1)S(1)}, bf16[584,128]{1,0:T(8,128)(2,1)S(1)}, u32[]{:S(2)}, u32[]{:S(2)}) collective-permute-start(bf16[584,128]{1,0:T(8,128)(2,1)S(1)} %collective-permute-done.12.refs_3_), channel_id=1, source_target_pairs={{4,1},{5,0},{0,9},{1,8},{8,13},{9,12},{12,5},{13,4},{6,3},{7,2},{2... | collective-permute-start | bytes 448520 | tf_op jit(solution)/shard_map/ppermute | solution.py:299
  31.8 1.9 %collective-permute-start.16 = (bf16[64,896]{1,0:T(8,128)(2,1)S(1)}, bf16[64,896]{1,0:T(8,128)(2,1)S(1)}, u32[]{:S(2)}, u32[]{:S(2)}) collective-permute-start(bf16[64,896]{1,0:T(8,128)(2,1)S(1)} %get-tuple-element.57), channel_id=1, source_target_pairs={{0,1},{1,0},{2,3},{3,2},{4,5},{5,4},{6,7},{7,6},{8,9},{9,8},{10,11... | collective-permute-start | bytes 344072 | tf_op jit(solution)/shard_map/ppermute | solution.py:305
  32.3 1.4 %collective-permute-start.17 = (bf16[64,896]{1,0:T(8,128)(2,1)S(1)}, bf16[64,896]{1,0:T(8,128)(2,1)S(1)}, u32[]{:S(2)}, u32[]{:S(2)}) collective-permute-start(bf16[64,896]{1,0:T(8,128)(2,1)S(1)} %get-tuple-element.58), channel_id=1, source_target_pairs={{0,1},{1,0},{2,3},{3,2},{4,5},{5,4},{6,7},{7,6},{8,9},{9,8},{10,11... | collective-permute-start | bytes 344072 | tf_op jit(solution)/shard_map/ppermute | solution.py:305
  33.2 1.4 %collective-permute-start.18 = (bf16[64,896]{1,0:T(8,128)(2,1)S(1)}, bf16[64,896]{1,0:T(8,128)(2,1)S(1)}, u32[]{:S(2)}, u32[]{:S(2)}) collective-permute-start(bf16[64,896]{1,0:T(8,128)(2,1)S(1)} %get-tuple-element.59), channel_id=1, source_target_pairs={{0,1},{1,0},{2,3},{3,2},{4,5},{5,4},{6,7},{7,6},{8,9},{9,8},{10,11... | collective-permute-start | bytes 344072 | tf_op jit(solution)/shard_map/ppermute | solution.py:305
  33.6 2.1 %collective-permute-start.14 = (bf16[584,128]{1,0:T(8,128)(2,1)S(1)}, bf16[584,128]{1,0:T(8,128)(2,1)S(1)}, u32[]{:S(2)}, u32[]{:S(2)}) collective-permute-start(bf16[584,128]{1,0:T(8,128)(2,1)S(1)} %collective-permute-done.11.first), channel_id=1, source_target_pairs={{0,1},{1,0},{2,3},{3,2},{4,5},{5,4},{6,7},{7,6},{8,9},{9,8},{10,11... | collective-permute-start | bytes 448520 | tf_op jit(solution)/shard_map/ppermute | solution.py:305
  34.6 1.4 %collective-permute-start.19 = (bf16[584,128]{1,0:T(8,128)(2,1)S(1)}, bf16[584,128]{1,0:T(8,128)(2,1)S(1)}, u32[]{:S(2)}, u32[]{:S(2)}) collective-permute-start(bf16[584,128]{1,0:T(8,128)(2,1)S(1)} %collective-permute-done.15.second), channel_id=1, source_target_pairs={{0,1},{1,0},{2,3},{3,2},{4,5},{5,4},{6,7},{7,6},{8,9},{9,8},{10,11... | collective-permute-start | bytes 448520 | tf_op jit(solution)/shard_map/ppermute | solution.py:305

commit v25 on v19

--- a/solution.py
+++ b/solution.py
@@ -203,16 +203,35 @@
         out[:, width:] = pair[top : top + count]
 
 
-def last_kernel(own, info, first, second, first_other, second_other, mine, *refs):
-    out = refs[-1]
+def join_kernel(own, info, first, second, mine, *refs):
+    *parts, out = refs
+    rows_here, wide = out.shape
+    width = wide - 128
+    theirs = jnp.concatenate([ref[...] for ref in parts], axis=0)
+    pair = theirs[:, width:].astype(F32)
+    numer = mine[:, :width] + theirs[:, :width].astype(F32)
+    denom = mine[:, width : width + 1] + (pair[:, 0:1] + pair[:, 1:2])
+    blocks = take_blocks([first, second], 1, rows_here)
+    left = left_rows((own,), rows_here)
+    store_sides(*add_blocks(left, info, blocks, numer, denom), [out])
+
+
+def last_kernel(own, info, first, second, total, out, staged, sems):
     rows_here, width = out.shape
-    theirs = jnp.concatenate([ref[...] for ref in refs[:-1]], axis=0)
-    blocks = take_blocks([first, second, first_other, second_other], 2, rows_here)
-    parts = theirs[:, width:].astype(F32)
-    numer = mine[:, :width] + theirs[:, :width].astype(F32)
-    denom = mine[:, width : width + 1] + (parts[:, 0:1] + parts[:, 1:2])
-    numer, denom = add_blocks(left_rows((own,), rows_here), info, blocks, numer, denom)
-    out[...] = (numer * (1.0 / denom)).astype(BF16)
+    blocks = take_blocks([first, second], 1, rows_here)
+    left = left_rows((own,), rows_here)
+    numer, denom = total[:, :width], total[:, width : width + 1]
+    numer, denom = add_blocks(left, info, blocks, numer, denom)
+    share = 1.0 / denom
+    count = rows_here // 4
+    copies = []
+    for part in range(4):
+        rows = slice(part * count, (part + 1) * count)
+        staged[rows, :] = (numer[rows] * share[rows]).astype(BF16)
+        copies.append(pltpu.make_async_copy(staged.at[rows, :], out.at[rows, :], sems.at[part]))
+        copies[-1].start()
+    for copy in copies:
+        copy.wait()
 
 
 def whole_in_vmem(count):
@@ -252,6 +271,17 @@
     return call(kernel, shapes, args, {len(args) - 2: 0}, products)
 
 
+def finish(shape, args):
+    return pl.pallas_call(
+        last_kernel,
+        out_shape=jax.ShapeDtypeStruct(shape, BF16),
+        in_specs=whole_in_vmem(len(args)),
+        out_specs=pl.BlockSpec(memory_space=pl.ANY),
+        scratch_shapes=[pltpu.VMEM(shape, BF16), pltpu.SemaphoreType.DMA((4,))],
+        compiler_params=pltpu.CompilerParams(vmem_limit_bytes=VMEM_BYTES),
+    )(*args)
+
+
 def folded_ring(size):
     return list(range(0, size, 2)) + list(range(1, size, 2))[::-1]
 
@@ -297,28 +327,30 @@
         moved = [along(piece) for piece in along_by[-1]]
         swapped = [across(piece) for piece in along_by[-1]]
         moved[0], swapped[0] = together(moved[0], swapped[0])
-        moved[1], swapped[1], _ = together(moved[1], swapped[1], moved[0])
+        if s < n_blk - 1:
+            moved[1], swapped[1], _ = together(moved[1], swapped[1], moved[0])
         along_by.append(tuple(moved))
         across_by.append(tuple(swapped))
     left = (whole, other_core(whole))
     early = across_by[:-1] + along_by[1:-2]
     mine, theirs, info = start_both(left, early, (rows_here, width + 128))
     left = (*left, info)
-    near_first, _, mine, theirs = together(across_by[-1][0], along_by[-1][0], mine, theirs)
-    far_second, _ = together(along_by[-1][1], near_first)
-    last_first, last_second = along(near_first), across(far_second)
+    far_first, _, mine, theirs = together(along_by[-1][0], across_by[-1][0], mine, theirs)
+    near_second, _ = together(across_by[-1][1], far_first)
+    last_first, last_second = across(far_first), along(near_second)
     late = [along_by[-2], across_by[-1], along_by[-1]]
     mine, *theirs = add_both(left, late, (mine, theirs))
     back = [other_core(part) for part in theirs[:-1]]
     last_first, theirs[-1] = together(last_first, theirs[-1])
     last_second, *back = together(last_second, *back, other_core(theirs[-1]))
-    last = (last_first, last_second)
-    (out,) = call(
-        last_kernel,
-        [((rows_here, width), BF16)],
-        [whole, info, *last, *[other_core(piece) for piece in last], mine, *back],
-        products=4 * rows_here * rows_here * width,
-    )
+    last = [other_core(last_first), other_core(last_second)]
+    (total,) = call(
+        join_kernel,
+        [((rows_here, width + 128), F32)],
+        [whole, info, last_first, last_second, mine, *back],
+        {4: 0},
+    )
+    out = finish((rows_here, width), [whole, info, *last, total])
     return out
 
 
@@ -326,7 +358,7 @@
     rows_here, width = embeddings.shape
     devices = lax.axis_size("blk") * lax.axis_size("sub") * lax.axis_size("pair")
     small = devices * rows_here * width * 2 <= GATHER_LIMIT
-    fits = width % 128 == 0 and rows_here % (32 * PARTS) == 0 and rows_here <= 256
+    fits = width % 128 == 0 and rows_here % (64 * PARTS) == 0 and rows_here <= 256
     if small and fits and lax.axis_size("sub") == 2 and lax.axis_size("pair") == 2:
         return by_block(embeddings, group_of, cluster_id)
     return by_group(embeddings, group_of, cluster_id)

time: 37.6 us -> 37.5 us (level)
  starting transfers between devices: 25.1 us -> 24.2 us
  Pallas kernels: 4.55 us -> 5.12 us
    ppermute x7, starting transfers between devices: 16.8 us -> 14.7 us  [along(): return lax.ppermute(rows, ('blk', 'pair'), hops)]
    pallas_call x0 -> x1, Pallas kernels: none -> 1.3 us  [finish(): pl.pallas_call(last_kernel, out_shape=jax.ShapeDtypeStruct(shape, BF16),...]
    ppermute x7, starting transfers between devices: 7 us -> 8.2 us  [across(): return lax.ppermute(rows, ('sub', 'pair'), [(0, 3), (1, 2), (2, 1), (3, 0)])]
    ppermute x7, waiting for transfers between devices: 0.9 us -> 1.67 us  [across(): return lax.ppermute(rows, ('sub', 'pair'), [(0, 3), (1, 2), (2, 1), (3, 0)])]
    pallas_call x5, Pallas kernels: 4.55 us -> 3.83 us  [call(): pl.pallas_call(kernel, out_shape=[jax.ShapeDtypeStruct(shape, dtype) for...]
    ppermute x7, waiting for transfers between devices: 3.83 us -> 3.32 us  [along(): return lax.ppermute(rows, ('blk', 'pair'), hops)]
  transfers between devices with their start and end apart: 20 -> 20, of which waited for: 9 -> 8; matrix products, arithmetic and copies ran while one was open for 0% -> 0% of each run, Pallas kernels for 8% -> 10%
where the time goes in v25:
time: 37.5 us; the launch traced here: 37.3 us
  starting transfers between devices  24.2 us (65%)
  waiting for transfers between devices  6.23 us (17%)
  Pallas kernels  5.12 us (14%)
  local copies, waits for them, and re-layouts  1.64 us (4%)
    ppermute x7, starting transfers between devices, along(): return lax.ppermute(rows, ('blk', 'pair'), hops)  14.7 us
    ppermute x7, starting transfers between devices, across(): return lax.ppermute(rows, ('sub', 'pair'), [(0, 3), (1, 2), (2, 1), (3, 0)])  8.2 us
    pallas_call x5, Pallas kernels, call(): pl.pallas_call(kernel, out_shape=[jax.ShapeDtypeStruct(shape, dtype) for...  3.83 us
    ppermute x7, waiting for transfers between devices, along(): return lax.ppermute(rows, ('blk', 'pair'), hops)  3.32 us
    ppermute x7, waiting for transfers between devices, across(): return lax.ppermute(rows, ('sub', 'pair'), [(0, 3), (1, 2), (2, 1), (3, 0)])  1.67 us
    unnamed x6, local copies, waits for them, and re-layouts  1.64 us
    ppermute x6, starting transfers between devices, other_core(): return lax.ppermute(rows, 'pair', [(0, 1), (1, 0)])  1.3 us
    pallas_call x1, Pallas kernels, finish(): pl.pallas_call(last_kernel, out_shape=jax.ShapeDtypeStruct(shape, BF16),...  1.3 us
  transfers between devices with their start and end apart: 20, of which 8 were waited for; matrix products, arithmetic and copies ran while one was open for 0% of the time, Pallas kernels for 10%

profile of v25, /device:TPU:0, one launch (start us, length us, event | category | flops | bytes accessed | tf_op | source)
XLA Modules:
  0.0 37.3 jit_solution(947474786021423950)
XLA Ops:
  0.0 0.0 copy-start
  0.0 1.0 %copy-done = bf16[192,768]{1,0:T(8,128)(2,1)S(1)} copy-done((bf16[192,768]{1,0:T(8,128)(2,1)S(1)}, bf16[192,768]{1,0:T(8,128)(2,1)}, u32[]{:S(2)}) %copy-start) | copy-done | bytes 294936
  1.0 0.0 copy-start.2
  1.0 2.4 %collective-permute-start.2 = (bf16[672,128]{1,0:T(8,128)(2,1)S(1)}, bf16[672,128]{1,0:T(8,128)(2,1)S(1)}, u32[]{:S(2)}, u32[]{:S(2)}) collective-permute-start(bf16[672,128]{1,0:T(8,128)(2,1)S(1)} %shard_map.38), channel_id=1, source_target_pairs={{0,3},{1,2},{2,1},{3,0},{4,7},{5,6},{6,5},{7,4},{8,11},{9,10},{10,... | collective-permute-start | bytes 516104 | tf_op jit(solution)/shard_map/ppermute | solution.py:310
  3.4 2.9 %collective-permute-start.1 = (bf16[672,128]{1,0:T(8,128)(2,1)S(1)}, bf16[672,128]{1,0:T(8,128)(2,1)S(1)}, u32[]{:S(2)}, u32[]{:S(2)}) collective-permute-start(bf16[672,128]{1,0:T(8,128)(2,1)S(1)} %shard_map.38), channel_id=1, source_target_pairs={{4,1},{5,0},{0,9},{1,8},{8,13},{9,12},{12,5},{13,4},{6,3},{7,2},{2... | collective-permute-start | bytes 516104 | tf_op jit(solution)/shard_map/ppermute | solution.py:307
  6.3 0.0 copy-start.1
  6.3 0.0 copy-done.2
  6.3 0.7 %copy-done.1 = s32[192,1]{0,1:T(1,128)S(1)} copy-done((s32[192,1]{0,1:T(1,128)S(1)}, s32[192,1]{0,1:T(1,128)}, u32[]{:S(2)}) %copy-start.1) | copy-done | bytes 792
  7.0 0.1 shard_map.37
  7.1 0.1 collective-permute-start
  7.1 0.7 %collective-permute-start.4 = (bf16[488,128]{1,0:T(8,128)(2,1)S(1)}, bf16[488,128]{1,0:T(8,128)(2,1)S(1)}, u32[]{:S(2)}, u32[]{:S(2)}) collective-permute-start(bf16[488,128]{1,0:T(8,128)(2,1)S(1)} %get-tuple-element.36), channel_id=1, source_target_pairs={{0,3},{1,2},{2,1},{3,0},{4,7},{5,6},{6,5},{7,4},{8,11},{9,10},{10,... | collective-permute-start | bytes 374792 | tf_op jit(solution)/shard_map/ppermute | solution.py:310
  7.8 1.2 %collective-permute-start.3 = (bf16[488,128]{1,0:T(8,128)(2,1)S(1)}, bf16[488,128]{1,0:T(8,128)(2,1)S(1)}, u32[]{:S(2)}, u32[]{:S(2)}) collective-permute-start(bf16[488,128]{1,0:T(8,128)(2,1)S(1)} %get-tuple-element.36), channel_id=1, source_target_pairs={{4,1},{5,0},{0,9},{1,8},{8,13},{9,12},{12,5},{13,4},{6,3},{7,2},{2... | collective-permute-start | bytes 374792 | tf_op jit(solution)/shard_map/ppermute | solution.py:307
  9.0 0.0 collective-permute-done.2.refs_0_
  9.0 1.5 %collective-permute-done.1.refs_4_ = bf16[672,128]{1,0:T(8,128)(2,1)S(1)} collective-permute-done((bf16[672,128]{1,0:T(8,128)(2,1)S(1)}, bf16[672,128]{1,0:T(8,128)(2,1)S(1)}, u32[]{:S(2)}, u32[]{:S(2)}) %collective-permute-start.1) | collective-permute-done | bytes 172064 | tf_op jit(solution)/shard_map/ppermute | solution.py:307
  10.5 0.1 collective-permute-start.6
  10.6 3.0 %collective-permute-start.5 = (bf16[672,128]{1,0:T(8,128)(2,1)S(1)}, bf16[672,128]{1,0:T(8,128)(2,1)S(1)}, u32[]{:S(2)}, u32[]{:S(2)}) collective-permute-start(bf16[672,128]{1,0:T(8,128)(2,1)S(1)} %collective-permute-done.1.refs_4_), channel_id=1, source_target_pairs={{4,1},{5,0},{0,9},{1,8},{8,13},{9,12},{12,5},{13,4},{6,3},{7,2},{2... | collective-permute-start | bytes 516104 | tf_op jit(solution)/shard_map/ppermute | solution.py:307
  13.6 0.0 collective-permute-done.4.refs_1_
  13.6 0.0 collective-permute-done.3.refs_5_
  13.6 1.7 %collective-permute-start.8 = (bf16[488,128]{1,0:T(8,128)(2,1)S(1)}, bf16[488,128]{1,0:T(8,128)(2,1)S(1)}, u32[]{:S(2)}, u32[]{:S(2)}) collective-permute-start(bf16[488,128]{1,0:T(8,128)(2,1)S(1)} %collective-permute-done.3.refs_5_), channel_id=1, source_target_pairs={{0,3},{1,2},{2,1},{3,0},{4,7},{5,6},{6,5},{7,4},{8,11},{9,10},{10,... | collective-permute-start | bytes 374792 | tf_op jit(solution)/shard_map/ppermute | solution.py:310
  15.4 1.6 %collective-permute-start.7 = (bf16[488,128]{1,0:T(8,128)(2,1)S(1)}, bf16[488,128]{1,0:T(8,128)(2,1)S(1)}, u32[]{:S(2)}, u32[]{:S(2)}) collective-permute-start(bf16[488,128]{1,0:T(8,128)(2,1)S(1)} %collective-permute-done.3.refs_5_), channel_id=1, source_target_pairs={{4,1},{5,0},{0,9},{1,8},{8,13},{9,12},{12,5},{13,4},{6,3},{7,2},{2... | collective-permute-start | bytes 374792 | tf_op jit(solution)/shard_map/ppermute | solution.py:307
  16.9 0.2 collective-permute-done.6.refs_2_
  17.2 1.1 %collective-permute-done.5.refs_0_ = bf16[672,128]{1,0:T(8,128)(2,1)S(1)} collective-permute-done((bf16[672,128]{1,0:T(8,128)(2,1)S(1)}, bf16[672,128]{1,0:T(8,128)(2,1)S(1)}, u32[]{:S(2)}, u32[]{:S(2)}) %collective-permute-start.5) | collective-permute-done | bytes 172064 | tf_op jit(solution)/shard_map/ppermute | solution.py:307
  18.2 1.1 %collective-permute-start.10 = (bf16[672,128]{1,0:T(8,128)(2,1)S(1)}, bf16[672,128]{1,0:T(8,128)(2,1)S(1)}, u32[]{:S(2)}, u32[]{:S(2)}) collective-permute-start(bf16[672,128]{1,0:T(8,128)(2,1)S(1)} %collective-permute-done.5.refs_0_), channel_id=1, source_target_pairs={{0,3},{1,2},{2,1},{3,0},{4,7},{5,6},{6,5},{7,4},{8,11},{9,10},{10,... | collective-permute-start | bytes 516104 | tf_op jit(solution)/shard_map/ppermute | solution.py:310
  19.4 3.4 %collective-permute-start.9 = (bf16[672,128]{1,0:T(8,128)(2,1)S(1)}, bf16[672,128]{1,0:T(8,128)(2,1)S(1)}, u32[]{:S(2)}, u32[]{:S(2)}) collective-permute-start(bf16[672,128]{1,0:T(8,128)(2,1)S(1)} %collective-permute-done.5.refs_0_), channel_id=1, source_target_pairs={{4,1},{5,0},{0,9},{1,8},{8,13},{9,12},{12,5},{13,4},{6,3},{7,2},{2... | collective-permute-start | bytes 516104 | tf_op jit(solution)/shard_map/ppermute | solution.py:307
  22.7 0.0 collective-permute-done.8.refs_3_
  22.7 0.0 collective-permute-done.7.refs_1_
  22.8 0.6 %collective-permute-start.13 = (bf16[488,128]{1,0:T(8,128)(2,1)S(1)}, bf16[488,128]{1,0:T(8,128)(2,1)S(1)}, u32[]{:S(2)}, u32[]{:S(2)}) collective-permute-start(bf16[488,128]{1,0:T(8,128)(2,1)S(1)} %collective-permute-done.7.refs_1_), channel_id=1, source_target_pairs={{4,1},{5,0},{0,9},{1,8},{8,13},{9,12},{12,5},{13,4},{6,3},{7,2},{2... | collective-permute-start | bytes 374792 | tf_op jit(solution)/shard_map/ppermute | solution.py:307
  23.3 1.7 %collective-permute-start.12 = (bf16[488,128]{1,0:T(8,128)(2,1)S(1)}, bf16[488,128]{1,0:T(8,128)(2,1)S(1)}, u32[]{:S(2)}, u32[]{:S(2)}) collective-permute-start(bf16[488,128]{1,0:T(8,128)(2,1)S(1)} %collective-permute-done.7.refs_1_), channel_id=1, source_target_pairs={{0,3},{1,2},{2,1},{3,0},{4,7},{5,6},{6,5},{7,4},{8,11},{9,10},{10,... | collective-permute-start | bytes 374792 | tf_op jit(solution)/shard_map/ppermute | solution.py:310
  25.1 0.0 collective-permute-done.other
  25.1 1.6 %shard_map.39 = (f32[192,896]{1,0:T(8,128)S(1)}, f32[192,896]{1,0:T(8,128)S(1)}, f32[384,128]{1,0:T(8,128)S(1)}) custom-call(bf16[1160,128]{1,0:T(8,128)(2,1)S(1)} %get-tuple-element.34.own, bf16[1160,128]{1,0:T(8,128)(2,1)S(1)} %collective-permute-done.other, bf16[672,128]{1,0:T(8,128)(2,1)S(1)} %collective-permute-done.2.refs_0_, ...), custom_call_target="tpu_custom_call" | custom-call | flops 1358954496 | tf_op jit(solution)/shard_map/pallas_call | solution.py:242
  26.7 0.0 collective-permute-done.10.refs_2_
  26.7 0.8 %collective-permute-done.9.refs_4_ = bf16[672,128]{1,0:T(8,128)(2,1)S(1)} collective-permute-done((bf16[672,128]{1,0:T(8,128)(2,1)S(1)}, bf16[672,128]{1,0:T(8,128)(2,1)S(1)}, u32[]{:S(2)}, u32[]{:S(2)}) %collective-permute-start.9) | collective-permute-done | bytes 172064 | tf_op jit(solution)/shard_map/ppermute | solution.py:307
  27.4 0.4 %collective-permute-start.11 = (bf16[672,128]{1,0:T(8,128)(2,1)S(1)}, bf16[672,128]{1,0:T(8,128)(2,1)S(1)}, u32[]{:S(2)}, u32[]{:S(2)}) collective-permute-start(bf16[672,128]{1,0:T(8,128)(2,1)S(1)} %collective-permute-done.9.refs_4_), channel_id=1, source_target_pairs={{0,3},{1,2},{2,1},{3,0},{4,7},{5,6},{6,5},{7,4},{8,11},{9,10},{10,... | collective-permute-start | bytes 516104 | tf_op jit(solution)/shard_map/ppermute | solution.py:310
  27.9 0.7 %collective-permute-done.12.refs_3_ = bf16[488,128]{1,0:T(8,128)(2,1)S(1)} collective-permute-done((bf16[488,128]{1,0:T(8,128)(2,1)S(1)}, bf16[488,128]{1,0:T(8,128)(2,1)S(1)}, u32[]{:S(2)}, u32[]{:S(2)}) %collective-permute-start.12) | collective-permute-done | bytes 124960 | tf_op jit(solution)/shard_map/ppermute | solution.py:310
  28.6 2.1 %collective-permute-start.15 = (bf16[488,128]{1,0:T(8,128)(2,1)S(1)}, bf16[488,128]{1,0:T(8,128)(2,1)S(1)}, u32[]{:S(2)}, u32[]{:S(2)}) collective-permute-start(bf16[488,128]{1,0:T(8,128)(2,1)S(1)} %collective-permute-done.12.refs_3_), channel_id=1, source_target_pairs={{4,1},{5,0},{0,9},{1,8},{8,13},{9,12},{12,5},{13,4},{6,3},{7,2},{2... | collective-permute-start | bytes 374792 | tf_op jit(solution)/shard_map/ppermute | solution.py:307
  30.7 0.0 collective-permute-done.13.refs_5_
  30.7 1.4 %shard_map.40 = (f32[192,896]{1,0:T(8,128)S(1)}, bf16[64,896]{1,0:T(8,128)(2,1)S(1)}, bf16[64,896]{1,0:T(8,128)(2,1)S(1)}, bf16[64,896]{1,0:T(8,128)(2,1)S(1)}) custom-call(bf16[1160,128]{1,0:T(8,128)(2,1)S(1)} %get-tuple-element.34.own, bf16[1160,128]{1,0:T(8,128)(2,1)S(1)} %collective-permute-done.other, ...), custom_call_target="tpu_custom_call", output_to_operand_aliasing={{0}: (9, {})} | custom-call | flops 1019215872 | tf_op jit(solution)/shard_map/pallas_call | solution.py:242
  32.1 0.1 collective-permute-start.16
  32.1 0.5 %collective-permute-start.17 = (bf16[64,896]{1,0:T(8,128)(2,1)S(1)}, bf16[64,896]{1,0:T(8,128)(2,1)S(1)}, u32[]{:S(2)}, u32[]{:S(2)}) collective-permute-start(bf16[64,896]{1,0:T(8,128)(2,1)S(1)} %get-tuple-element.56), channel_id=1, source_target_pairs={{0,1},{1,0},{2,3},{3,2},{4,5},{5,4},{6,7},{7,6},{8,9},{9,8},{10,11... | collective-permute-start | bytes 344072 | tf_op jit(solution)/shard_map/ppermute | solution.py:313
  32.6 0.7 %collective-permute-done.11.first = bf16[672,128]{1,0:T(8,128)(2,1)S(1)} collective-permute-done((bf16[672,128]{1,0:T(8,128)(2,1)S(1)}, bf16[672,128]{1,0:T(8,128)(2,1)S(1)}, u32[]{:S(2)}, u32[]{:S(2)}) %collective-permute-start.11) | collective-permute-done | bytes 172064 | tf_op jit(solution)/shard_map/ppermute | solution.py:310
  33.3 0.0 collective-permute-start.18
  33.4 0.5 %collective-permute-start.14 = (bf16[672,128]{1,0:T(8,128)(2,1)S(1)}, bf16[672,128]{1,0:T(8,128)(2,1)S(1)}, u32[]{:S(2)}, u32[]{:S(2)}) collective-permute-start(bf16[672,128]{1,0:T(8,128)(2,1)S(1)} %collective-permute-done.11.first), channel_id=1, source_target_pairs={{0,1},{1,0},{2,3},{3,2},{4,5},{5,4},{6,7},{7,6},{8,9},{9,8},{10,11... | collective-permute-start | bytes 516104 | tf_op jit(solution)/shard_map/ppermute | solution.py:313
  33.9 0.0 collective-permute-done.16.refs_0_
  33.9 0.0 collective-permute-done.17.refs_1_
  33.9 0.0 collective-permute-done.15.second
  33.9 0.8 %collective-permute-done.18.refs_2_ = bf16[64,896]{1,0:T(8,128)(2,1)S(1)} collective-permute-done((bf16[64,896]{1,0:T(8,128)(2,1)S(1)}, bf16[64,896]{1,0:T(8,128)(2,1)S(1)}, u32[]{:S(2)}, u32[]{:S(2)}) %collective-permute-start.18) | collective-permute-done | bytes 114720 | tf_op jit(solution)/shard_map/ppermute | solution.py:313
  34.7 0.2 collective-permute-start.19
  34.8 0.7 %shard_map.41.total = f32[192,896]{1,0:T(8,128)S(1)} custom-call(bf16[1160,128]{1,0:T(8,128)(2,1)S(1)} %get-tuple-element.34.own, f32[384,128]{1,0:T(8,128)S(1)} %get-tuple-element.43.info, bf16[672,128]{1,0:T(8,128)(2,1)S(1)} %collective-permute-done.11.first, bf16[488,128]{1,0:T(8,128)(2,1)S(1)} %collective-permute-done.15.second, ...), custom_call_target="tpu_custom_call", output_to_operand_aliasing={{}: (4, {})} | custom-call | tf_op jit(solution)/shard_map/pallas_call | solution.py:242
  35.6 0.0 collective-permute-done.14.first
  35.6 0.4 %collective-permute-done.19.second = bf16[488,128]{1,0:T(8,128)(2,1)S(1)} collective-permute-done((bf16[488,128]{1,0:T(8,128)(2,1)S(1)}, bf16[488,128]{1,0:T(8,128)(2,1)S(1)}, u32[]{:S(2)}, u32[]{:S(2)}) %collective-permute-start.19) | collective-permute-done | bytes 124960 | tf_op jit(solution)/shard_map/ppermute | solution.py:313
  36.0 1.3 %shard_map.42 = bf16[192,768]{1,0:T(8,128)(2,1)} custom-call(bf16[1160,128]{1,0:T(8,128)(2,1)S(1)} %get-tuple-element.34.own, f32[384,128]{1,0:T(8,128)S(1)} %get-tuple-element.43.info, bf16[672,128]{1,0:T(8,128)(2,1)S(1)} %collective-permute-done.14.first, bf16[488,128]{1,0:T(8,128)(2,1)S(1)} %collective-permute-done.19.second, f32[192,896]{1,0:T(8,128)S(1)} %shard_map.41.total), custom_call_target="tpu_custom_call" | custom-call | tf_op jit(solution)/shard_map/pallas_call | solution.py:275
  (1 shorter events, 0.0 us)
Async XLA Ops:
  0.0 1.0 %copy-start = (bf16[192,768]{1,0:T(8,128)(2,1)S(1)}, bf16[192,768]{1,0:T(8,128)(2,1)}, u32[]{:S(2)}) copy-start(bf16[192,768]{1,0:T(8,128)(2,1)} %rows.3) | copy-start | bytes 884740
  1.0 5.4 %copy-start.2 = (s32[192]{0:T(256)S(1)}, s32[192]{0:T(256)}, u32[]{:S(2)}) copy-start(s32[192]{0:T(256)} %param.5) | copy-start | bytes 2308
  1.0 8.0 %collective-permute-start.2 = (bf16[672,128]{1,0:T(8,128)(2,1)S(1)}, bf16[672,128]{1,0:T(8,128)(2,1)S(1)}, u32[]{:S(2)}, u32[]{:S(2)}) collective-permute-start(bf16[672,128]{1,0:T(8,128)(2,1)S(1)} %shard_map.38), channel_id=1, source_target_pairs={{0,3},{1,2},{2,1},{3,0},{4,7},{5,6},{6,5},{7,4},{8,11},{9,10},{10,... | collective-permute-start | bytes 516104 | tf_op jit(solution)/shard_map/ppermute | solution.py:310
  3.4 7.1 %collective-permute-start.1 = (bf16[672,128]{1,0:T(8,128)(2,1)S(1)}, bf16[672,128]{1,0:T(8,128)(2,1)S(1)}, u32[]{:S(2)}, u32[]{:S(2)}) collective-permute-start(bf16[672,128]{1,0:T(8,128)(2,1)S(1)} %shard_map.38), channel_id=1, source_target_pairs={{4,1},{5,0},{0,9},{1,8},{8,13},{9,12},{12,5},{13,4},{6,3},{7,2},{2... | collective-permute-start | bytes 516104 | tf_op jit(solution)/shard_map/ppermute | solution.py:307
  6.3 0.7 %copy-start.1 = (s32[192,1]{0,1:T(1,128)S(1)}, s32[192,1]{0,1:T(1,128)}, u32[]{:S(2)}) copy-start(s32[192,1]{0,1:T(1,128)} %param.4) | copy-start | bytes 2308
  7.1 18.0 %collective-permute-start = (bf16[1160,128]{1,0:T(8,128)(2,1)S(1)}, bf16[1160,128]{1,0:T(8,128)(2,1)S(1)}, u32[]{:S(2)}, u32[]{:S(2)}) collective-permute-start(bf16[1160,128]{1,0:T(8,128)(2,1)S(1)} %get-tuple-element.34.own), channel_id=1, source_target_pairs={{0,1},{1,0},{2,3},{3,2},{4,5},{5,4},{6,7},{7,6},{8,9},{9,8},{10,11... | collective-permute-start | bytes 890888 | tf_op jit(solution)/shard_map/ppermute | solution.py:313
  7.1 6.5 %collective-permute-start.4 = (bf16[488,128]{1,0:T(8,128)(2,1)S(1)}, bf16[488,128]{1,0:T(8,128)(2,1)S(1)}, u32[]{:S(2)}, u32[]{:S(2)}) collective-permute-start(bf16[488,128]{1,0:T(8,128)(2,1)S(1)} %get-tuple-element.36), channel_id=1, source_target_pairs={{0,3},{1,2},{2,1},{3,0},{4,7},{5,6},{6,5},{7,4},{8,11},{9,10},{10,... | collective-permute-start | bytes 374792 | tf_op jit(solution)/shard_map/ppermute | solution.py:310
  7.8 5.8 %collective-permute-start.3 = (bf16[488,128]{1,0:T(8,128)(2,1)S(1)}, bf16[488,128]{1,0:T(8,128)(2,1)S(1)}, u32[]{:S(2)}, u32[]{:S(2)}) collective-permute-start(bf16[488,128]{1,0:T(8,128)(2,1)S(1)} %get-tuple-element.36), channel_id=1, source_target_pairs={{4,1},{5,0},{0,9},{1,8},{8,13},{9,12},{12,5},{13,4},{6,3},{7,2},{2... | collective-permute-start | bytes 374792 | tf_op jit(solution)/shard_map/ppermute | solution.py:307
  10.5 6.7 %collective-permute-start.6 = (bf16[672,128]{1,0:T(8,128)(2,1)S(1)}, bf16[672,128]{1,0:T(8,128)(2,1)S(1)}, u32[]{:S(2)}, u32[]{:S(2)}) collective-permute-start(bf16[672,128]{1,0:T(8,128)(2,1)S(1)} %collective-permute-done.1.refs_4_), channel_id=1, source_target_pairs={{0,3},{1,2},{2,1},{3,0},{4,7},{5,6},{6,5},{7,4},{8,11},{9,10},{10,... | collective-permute-start | bytes 516104 | tf_op jit(solution)/shard_map/ppermute | solution.py:310
  10.6 7.6 %collective-permute-start.5 = (bf16[672,128]{1,0:T(8,128)(2,1)S(1)}, bf16[672,128]{1,0:T(8,128)(2,1)S(1)}, u32[]{:S(2)}, u32[]{:S(2)}) collective-permute-start(bf16[672,128]{1,0:T(8,128)(2,1)S(1)} %collective-permute-done.1.refs_4_), channel_id=1, source_target_pairs={{4,1},{5,0},{0,9},{1,8},{8,13},{9,12},{12,5},{13,4},{6,3},{7,2},{2... | collective-permute-start | bytes 516104 | tf_op jit(solution)/shard_map/ppermute | solution.py:307
  13.6 9.1 %collective-permute-start.8 = (bf16[488,128]{1,0:T(8,128)(2,1)S(1)}, bf16[488,128]{1,0:T(8,128)(2,1)S(1)}, u32[]{:S(2)}, u32[]{:S(2)}) collective-permute-start(bf16[488,128]{1,0:T(8,128)(2,1)S(1)} %collective-permute-done.3.refs_5_), channel_id=1, source_target_pairs={{0,3},{1,2},{2,1},{3,0},{4,7},{5,6},{6,5},{7,4},{8,11},{9,10},{10,... | collective-permute-start | bytes 374792 | tf_op jit(solution)/shard_map/ppermute | solution.py:310
  15.4 7.4 %collective-permute-start.7 = (bf16[488,128]{1,0:T(8,128)(2,1)S(1)}, bf16[488,128]{1,0:T(8,128)(2,1)S(1)}, u32[]{:S(2)}, u32[]{:S(2)}) collective-permute-start(bf16[488,128]{1,0:T(8,128)(2,1)S(1)} %collective-permute-done.3.refs_5_), channel_id=1, source_target_pairs={{4,1},{5,0},{0,9},{1,8},{8,13},{9,12},{12,5},{13,4},{6,3},{7,2},{2... | collective-permute-start | bytes 374792 | tf_op jit(solution)/shard_map/ppermute | solution.py:307
  18.2 8.4 %collective-permute-start.10 = (bf16[672,128]{1,0:T(8,128)(2,1)S(1)}, bf16[672,128]{1,0:T(8,128)(2,1)S(1)}, u32[]{:S(2)}, u32[]{:S(2)}) collective-permute-start(bf16[672,128]{1,0:T(8,128)(2,1)S(1)} %collective-permute-done.5.refs_0_), channel_id=1, source_target_pairs={{0,3},{1,2},{2,1},{3,0},{4,7},{5,6},{6,5},{7,4},{8,11},{9,10},{10,... | collective-permute-start | bytes 516104 | tf_op jit(solution)/shard_map/ppermute | solution.py:310
  19.4 8.1 %collective-permute-start.9 = (bf16[672,128]{1,0:T(8,128)(2,1)S(1)}, bf16[672,128]{1,0:T(8,128)(2,1)S(1)}, u32[]{:S(2)}, u32[]{:S(2)}) collective-permute-start(bf16[672,128]{1,0:T(8,128)(2,1)S(1)} %collective-permute-done.5.refs_0_), channel_id=1, source_target_pairs={{4,1},{5,0},{0,9},{1,8},{8,13},{9,12},{12,5},{13,4},{6,3},{7,2},{2... | collective-permute-start | bytes 516104 | tf_op jit(solution)/shard_map/ppermute | solution.py:307
  22.8 7.9 %collective-permute-start.13 = (bf16[488,128]{1,0:T(8,128)(2,1)S(1)}, bf16[488,128]{1,0:T(8,128)(2,1)S(1)}, u32[]{:S(2)}, u32[]{:S(2)}) collective-permute-start(bf16[488,128]{1,0:T(8,128)(2,1)S(1)} %collective-permute-done.7.refs_1_), channel_id=1, source_target_pairs={{4,1},{5,0},{0,9},{1,8},{8,13},{9,12},{12,5},{13,4},{6,3},{7,2},{2... | collective-permute-start | bytes 374792 | tf_op jit(solution)/shard_map/ppermute | solution.py:307
  23.3 5.3 %collective-permute-start.12 = (bf16[488,128]{1,0:T(8,128)(2,1)S(1)}, bf16[488,128]{1,0:T(8,128)(2,1)S(1)}, u32[]{:S(2)}, u32[]{:S(2)}) collective-permute-start(bf16[488,128]{1,0:T(8,128)(2,1)S(1)} %collective-permute-done.7.refs_1_), channel_id=1, source_target_pairs={{0,3},{1,2},{2,1},{3,0},{4,7},{5,6},{6,5},{7,4},{8,11},{9,10},{10,... | collective-permute-start | bytes 374792 | tf_op jit(solution)/shard_map/ppermute | solution.py:310
  27.4 5.9 %collective-permute-start.11 = (bf16[672,128]{1,0:T(8,128)(2,1)S(1)}, bf16[672,128]{1,0:T(8,128)(2,1)S(1)}, u32[]{:S(2)}, u32[]{:S(2)}) collective-permute-start(bf16[672,128]{1,0:T(8,128)(2,1)S(1)} %collective-permute-done.9.refs_4_), channel_id=1, source_target_pairs={{0,3},{1,2},{2,1},{3,0},{4,7},{5,6},{6,5},{7,4},{8,11},{9,10},{10,... | collective-permute-start | bytes 516104 | tf_op jit(solution)/shard_map/ppermute | solution.py:310
  28.6 5.3 %collective-permute-start.15 = (bf16[488,128]{1,0:T(8,128)(2,1)S(1)}, bf16[488,128]{1,0:T(8,128)(2,1)S(1)}, u32[]{:S(2)}, u32[]{:S(2)}) collective-permute-start(bf16[488,128]{1,0:T(8,128)(2,1)S(1)} %collective-permute-done.12.refs_3_), channel_id=1, source_target_pairs={{4,1},{5,0},{0,9},{1,8},{8,13},{9,12},{12,5},{13,4},{6,3},{7,2},{2... | collective-permute-start | bytes 374792 | tf_op jit(solution)/shard_map/ppermute | solution.py:307
  32.1 1.8 %collective-permute-start.16 = (bf16[64,896]{1,0:T(8,128)(2,1)S(1)}, bf16[64,896]{1,0:T(8,128)(2,1)S(1)}, u32[]{:S(2)}, u32[]{:S(2)}) collective-permute-start(bf16[64,896]{1,0:T(8,128)(2,1)S(1)} %get-tuple-element.55), channel_id=1, source_target_pairs={{0,1},{1,0},{2,3},{3,2},{4,5},{5,4},{6,7},{7,6},{8,9},{9,8},{10,11... | collective-permute-start | bytes 344072 | tf_op jit(solution)/shard_map/ppermute | solution.py:313
  32.1 1.7 %collective-permute-start.17 = (bf16[64,896]{1,0:T(8,128)(2,1)S(1)}, bf16[64,896]{1,0:T(8,128)(2,1)S(1)}, u32[]{:S(2)}, u32[]{:S(2)}) collective-permute-start(bf16[64,896]{1,0:T(8,128)(2,1)S(1)} %get-tuple-element.56), channel_id=1, source_target_pairs={{0,1},{1,0},{2,3},{3,2},{4,5},{5,4},{6,7},{7,6},{8,9},{9,8},{10,11... | collective-permute-start | bytes 344072 | tf_op jit(solution)/shard_map/ppermute | solution.py:313
  33.3 1.3 %collective-permute-start.18 = (bf16[64,896]{1,0:T(8,128)(2,1)S(1)}, bf16[64,896]{1,0:T(8,128)(2,1)S(1)}, u32[]{:S(2)}, u32[]{:S(2)}) collective-permute-start(bf16[64,896]{1,0:T(8,128)(2,1)S(1)} %get-tuple-element.57), channel_id=1, source_target_pairs={{0,1},{1,0},{2,3},{3,2},{4,5},{5,4},{6,7},{7,6},{8,9},{9,8},{10,11... | collective-permute-start | bytes 344072 | tf_op jit(solution)/shard_map/ppermute | solution.py:313
  33.4 2.2 %collective-permute-start.14 = (bf16[672,128]{1,0:T(8,128)(2,1)S(1)}, bf16[672,128]{1,0:T(8,128)(2,1)S(1)}, u32[]{:S(2)}, u32[]{:S(2)}) collective-permute-start(bf16[672,128]{1,0:T(8,128)(2,1)S(1)} %collective-permute-done.11.first), channel_id=1, source_target_pairs={{0,1},{1,0},{2,3},{3,2},{4,5},{5,4},{6,7},{7,6},{8,9},{9,8},{10,11... | collective-permute-start | bytes 516104 | tf_op jit(solution)/shard_map/ppermute | solution.py:313
  34.7 1.3 %collective-permute-start.19 = (bf16[488,128]{1,0:T(8,128)(2,1)S(1)}, bf16[488,128]{1,0:T(8,128)(2,1)S(1)}, u32[]{:S(2)}, u32[]{:S(2)}) collective-permute-start(bf16[488,128]{1,0:T(8,128)(2,1)S(1)} %collective-permute-done.15.second), channel_id=1, source_target_pairs={{0,1},{1,0},{2,3},{3,2},{4,5},{5,4},{6,7},{7,6},{8,9},{9,8},{10,11... | collective-permute-start | bytes 374792 | tf_op jit(solution)/shard_map/ppermute | solution.py:313

commit v26 on v23

--- a/solution.py
+++ b/solution.py
@@ -11,6 +11,7 @@
 BF16 = jnp.bfloat16
 VMEM_BYTES = 24 * 1024 * 1024
 PARTS = 3
+LINES = 16
 GATHER_LIMIT = 8 * 1024 * 1024
 
 
@@ -83,7 +84,7 @@
     half = rows.shape[0] // 2
     for slab in range(slabs):
         first[slab * half : (slab + 1) * half, :] = rows[:half, slab * 128 : (slab + 1) * 128]
-    first[slabs * half :, :] = jnp.zeros((8, 128), BF16)
+    first[slabs * half :, :] = jnp.zeros((LINES, 128), BF16)
 
 
 def pack_kernel(rows, group, cluster, whole, second):
@@ -94,8 +95,8 @@
         columns = rows[:, slab * 128 : (slab + 1) * 128]
         whole[slab * rows_here : (slab + 1) * rows_here, :] = columns
         second[slab * half : (slab + 1) * half, :] = columns[half:]
-    line_at = lax.broadcasted_iota(jnp.int32, (8, 128), 0)
-    named = jnp.zeros((8, 128), jnp.int32)
+    line_at = lax.broadcasted_iota(jnp.int32, (LINES, 128), 0)
+    named = jnp.zeros((LINES, 128), jnp.int32)
     for line in range(4):
         top = line % 2 * half
         part = (group, cluster)[line // 2][:, top : top + half]
@@ -113,8 +114,11 @@
 
 
 def key_rows(ref, half):
-    wide = ref[ref.shape[0] - 8 :, :].astype(F32)
-    return [wide[side : side + 1, :half] * 256.0 + wide[side + 2 : side + 3, :half] for side in range(2)]
+    wide = ref[ref.shape[0] - LINES :, :].astype(F32)
+    return [
+        wide[side : side + 1, :half] * 256.0 + wide[side + 2 : side + 3, :half]
+        for side in range(2)
+    ]
 
 
 def key_row(ref, rows_here):
@@ -304,11 +308,11 @@
     def other_core(rows):
         return lax.ppermute(rows, "pair", [(0, 1), (1, 0)])
 
-    half_shape = ((slabs * half + 8, 128), BF16)
+    half_shape = ((slabs * half + LINES, 128), BF16)
     (first,) = call(first_pack_kernel, [half_shape], [embeddings])
     whole, second = call(
         pack_kernel,
-        [((slabs * rows_here + 8, 128), BF16), half_shape],
+        [((slabs * rows_here + LINES, 128), BF16), half_shape],
         [embeddings, group_of.reshape(line), cluster_id.reshape(line)],
     )
     along_by = [(first, second)]

time: 36.3 us -> 36.5 us (level)
  no operation moved by 1% of the time
where the time goes in v26:
time: 36.5 us; the launch traced here: 36.4 us
  starting transfers between devices  25.1 us (69%)
  Pallas kernels  5.09 us (14%)
  waiting for transfers between devices  4.5 us (12%)
  local copies, waits for them, and re-layouts  1.64 us (4%)
    ppermute x7, starting transfers between devices, along(): return lax.ppermute(rows, ('blk', 'pair'), hops)  17.2 us
    ppermute x7, starting transfers between devices, across(): return lax.ppermute(rows, ('sub', 'pair'), [(0, 3), (1, 2), (2, 1), (3, 0)])  6.7 us
    pallas_call x5, Pallas kernels, call(): pl.pallas_call(kernel, out_shape=[jax.ShapeDtypeStruct(shape, dtype) for...  3.79 us
    ppermute x7, waiting for transfers between devices, along(): return lax.ppermute(rows, ('blk', 'pair'), hops)  2.41 us
    unnamed x6, local copies, waits for them, and re-layouts  1.64 us
    pallas_call x1, Pallas kernels, finish(): pl.pallas_call(last_kernel, out_shape=jax.ShapeDtypeStruct(shape, BF16),...  1.29 us
    ppermute x6, starting transfers between devices, other_core(): return lax.ppermute(rows, 'pair', [(0, 1), (1, 0)])  1.2 us
    ppermute x7, waiting for transfers between devices, across(): return lax.ppermute(rows, ('sub', 'pair'), [(0, 3), (1, 2), (2, 1), (3, 0)])  1.12 us
  transfers between devices with their start and end apart: 20, of which 8 were waited for; matrix products, arithmetic and copies ran while one was open for 0% of the time, Pallas kernels for 10%

profile of v26, /device:TPU:0, one launch (start us, length us, event | category | flops | bytes accessed | tf_op | source)
XLA Modules:
  0.0 36.4 jit_solution(15116723265465145166)
XLA Ops:
  0.0 0.0 copy-start
  0.0 1.0 %copy-done = bf16[192,768]{1,0:T(8,128)(2,1)S(1)} copy-done((bf16[192,768]{1,0:T(8,128)(2,1)S(1)}, bf16[192,768]{1,0:T(8,128)(2,1)}, u32[]{:S(2)}) %copy-start) | copy-done | bytes 294936
  1.0 0.0 copy-start.2
  1.0 2.4 %collective-permute-start.2 = (bf16[592,128]{1,0:T(8,128)(2,1)S(1)}, bf16[592,128]{1,0:T(8,128)(2,1)S(1)}, u32[]{:S(2)}, u32[]{:S(2)}) collective-permute-start(bf16[592,128]{1,0:T(8,128)(2,1)S(1)} %shard_map.38), channel_id=1, source_target_pairs={{0,3},{1,2},{2,1},{3,0},{4,7},{5,6},{6,5},{7,4},{8,11},{9,10},{10,... | collective-permute-start | bytes 454664 | tf_op jit(solution)/shard_map/ppermute | solution.py:306
  3.4 2.9 %collective-permute-start.1 = (bf16[592,128]{1,0:T(8,128)(2,1)S(1)}, bf16[592,128]{1,0:T(8,128)(2,1)S(1)}, u32[]{:S(2)}, u32[]{:S(2)}) collective-permute-start(bf16[592,128]{1,0:T(8,128)(2,1)S(1)} %shard_map.38), channel_id=1, source_target_pairs={{4,1},{5,0},{0,9},{1,8},{8,13},{9,12},{12,5},{13,4},{6,3},{7,2},{2... | collective-permute-start | bytes 454664 | tf_op jit(solution)/shard_map/ppermute | solution.py:303
  6.3 0.0 copy-start.1
  6.3 0.0 copy-done.2
  6.3 0.7 %copy-done.1 = s32[192,1]{0,1:T(1,128)S(1)} copy-done((s32[192,1]{0,1:T(1,128)S(1)}, s32[192,1]{0,1:T(1,128)}, u32[]{:S(2)}) %copy-start.1) | copy-done | bytes 792
  7.0 0.1 shard_map.37
  7.1 0.1 collective-permute-start.4
  7.2 1.8 %collective-permute-start.3 = (bf16[592,128]{1,0:T(8,128)(2,1)S(1)}, bf16[592,128]{1,0:T(8,128)(2,1)S(1)}, u32[]{:S(2)}, u32[]{:S(2)}) collective-permute-start(bf16[592,128]{1,0:T(8,128)(2,1)S(1)} %get-tuple-element.36), channel_id=1, source_target_pairs={{4,1},{5,0},{0,9},{1,8},{8,13},{9,12},{12,5},{13,4},{6,3},{7,2},{2... | collective-permute-start | bytes 454664 | tf_op jit(solution)/shard_map/ppermute | solution.py:303
  9.0 0.0 collective-permute-done.2.refs_0_
  9.0 1.3 %collective-permute-done.1.refs_4_ = bf16[592,128]{1,0:T(8,128)(2,1)S(1)} collective-permute-done((bf16[592,128]{1,0:T(8,128)(2,1)S(1)}, bf16[592,128]{1,0:T(8,128)(2,1)S(1)}, u32[]{:S(2)}, u32[]{:S(2)}) %collective-permute-start.1) | collective-permute-done | bytes 151584 | tf_op jit(solution)/shard_map/ppermute | solution.py:303
  10.2 0.0 collective-permute-start.6
  10.2 3.1 %collective-permute-start.5 = (bf16[592,128]{1,0:T(8,128)(2,1)S(1)}, bf16[592,128]{1,0:T(8,128)(2,1)S(1)}, u32[]{:S(2)}, u32[]{:S(2)}) collective-permute-start(bf16[592,128]{1,0:T(8,128)(2,1)S(1)} %collective-permute-done.1.refs_4_), channel_id=1, source_target_pairs={{4,1},{5,0},{0,9},{1,8},{8,13},{9,12},{12,5},{13,4},{6,3},{7,2},{2... | collective-permute-start | bytes 454664 | tf_op jit(solution)/shard_map/ppermute | solution.py:303
  13.3 0.0 collective-permute-start
  13.3 0.0 collective-permute-done.4.refs_1_
  13.4 0.0 collective-permute-done.3.refs_5_
  13.4 1.8 %collective-permute-start.8 = (bf16[592,128]{1,0:T(8,128)(2,1)S(1)}, bf16[592,128]{1,0:T(8,128)(2,1)S(1)}, u32[]{:S(2)}, u32[]{:S(2)}) collective-permute-start(bf16[592,128]{1,0:T(8,128)(2,1)S(1)} %collective-permute-done.3.refs_5_), channel_id=1, source_target_pairs={{0,3},{1,2},{2,1},{3,0},{4,7},{5,6},{6,5},{7,4},{8,11},{9,10},{10,... | collective-permute-start | bytes 454664 | tf_op jit(solution)/shard_map/ppermute | solution.py:306
  15.1 1.1 %collective-permute-start.7 = (bf16[592,128]{1,0:T(8,128)(2,1)S(1)}, bf16[592,128]{1,0:T(8,128)(2,1)S(1)}, u32[]{:S(2)}, u32[]{:S(2)}) collective-permute-start(bf16[592,128]{1,0:T(8,128)(2,1)S(1)} %collective-permute-done.3.refs_5_), channel_id=1, source_target_pairs={{4,1},{5,0},{0,9},{1,8},{8,13},{9,12},{12,5},{13,4},{6,3},{7,2},{2... | collective-permute-start | bytes 454664 | tf_op jit(solution)/shard_map/ppermute | solution.py:303
  16.3 0.3 collective-permute-done.6.refs_2_
  16.6 0.4 %collective-permute-done.5.refs_0_ = bf16[592,128]{1,0:T(8,128)(2,1)S(1)} collective-permute-done((bf16[592,128]{1,0:T(8,128)(2,1)S(1)}, bf16[592,128]{1,0:T(8,128)(2,1)S(1)}, u32[]{:S(2)}, u32[]{:S(2)}) %collective-permute-start.5) | collective-permute-done | bytes 151584 | tf_op jit(solution)/shard_map/ppermute | solution.py:303
  17.0 1.2 %collective-permute-start.10 = (bf16[592,128]{1,0:T(8,128)(2,1)S(1)}, bf16[592,128]{1,0:T(8,128)(2,1)S(1)}, u32[]{:S(2)}, u32[]{:S(2)}) collective-permute-start(bf16[592,128]{1,0:T(8,128)(2,1)S(1)} %collective-permute-done.5.refs_0_), channel_id=1, source_target_pairs={{0,3},{1,2},{2,1},{3,0},{4,7},{5,6},{6,5},{7,4},{8,11},{9,10},{10,... | collective-permute-start | bytes 454664 | tf_op jit(solution)/shard_map/ppermute | solution.py:306
  18.1 3.4 %collective-permute-start.9 = (bf16[592,128]{1,0:T(8,128)(2,1)S(1)}, bf16[592,128]{1,0:T(8,128)(2,1)S(1)}, u32[]{:S(2)}, u32[]{:S(2)}) collective-permute-start(bf16[592,128]{1,0:T(8,128)(2,1)S(1)} %collective-permute-done.5.refs_0_), channel_id=1, source_target_pairs={{4,1},{5,0},{0,9},{1,8},{8,13},{9,12},{12,5},{13,4},{6,3},{7,2},{2... | collective-permute-start | bytes 454664 | tf_op jit(solution)/shard_map/ppermute | solution.py:303
  21.5 0.0 collective-permute-done.8.refs_3_
  21.5 0.0 collective-permute-done.7.refs_1_
  21.5 0.2 collective-permute-start.12
  21.7 2.6 %collective-permute-start.13 = (bf16[592,128]{1,0:T(8,128)(2,1)S(1)}, bf16[592,128]{1,0:T(8,128)(2,1)S(1)}, u32[]{:S(2)}, u32[]{:S(2)}) collective-permute-start(bf16[592,128]{1,0:T(8,128)(2,1)S(1)} %collective-permute-done.7.refs_1_), channel_id=1, source_target_pairs={{4,1},{5,0},{0,9},{1,8},{8,13},{9,12},{12,5},{13,4},{6,3},{7,2},{2... | collective-permute-start | bytes 454664 | tf_op jit(solution)/shard_map/ppermute | solution.py:303
  24.3 0.0 collective-permute-done.other
  24.3 1.5 %shard_map.39 = (f32[192,896]{1,0:T(8,128)S(1)}, f32[192,896]{1,0:T(8,128)S(1)}, f32[384,128]{1,0:T(8,128)S(1)}) custom-call(bf16[1168,128]{1,0:T(8,128)(2,1)S(1)} %get-tuple-element.34.own, bf16[1168,128]{1,0:T(8,128)(2,1)S(1)} %collective-permute-done.other, bf16[592,128]{1,0:T(8,128)(2,1)S(1)} %collective-permute-done.2.refs_0_, ...), custom_call_target="tpu_custom_call" | custom-call | tf_op jit(solution)/shard_map/pallas_call | solution.py:245
  25.8 0.0 collective-permute-done.10.refs_2_
  25.8 0.0 collective-permute-done.9.refs_4_
  25.8 1.0 %collective-permute-start.11 = (bf16[592,128]{1,0:T(8,128)(2,1)S(1)}, bf16[592,128]{1,0:T(8,128)(2,1)S(1)}, u32[]{:S(2)}, u32[]{:S(2)}) collective-permute-start(bf16[592,128]{1,0:T(8,128)(2,1)S(1)} %collective-permute-done.9.refs_4_), channel_id=1, source_target_pairs={{0,3},{1,2},{2,1},{3,0},{4,7},{5,6},{6,5},{7,4},{8,11},{9,10},{10,... | collective-permute-start | bytes 454664 | tf_op jit(solution)/shard_map/ppermute | solution.py:306
  26.8 0.8 %collective-permute-done.12.refs_3_ = bf16[592,128]{1,0:T(8,128)(2,1)S(1)} collective-permute-done((bf16[592,128]{1,0:T(8,128)(2,1)S(1)}, bf16[592,128]{1,0:T(8,128)(2,1)S(1)}, u32[]{:S(2)}, u32[]{:S(2)}) %collective-permute-start.12) | collective-permute-done | bytes 151584 | tf_op jit(solution)/shard_map/ppermute | solution.py:306
  27.6 2.3 %collective-permute-start.15 = (bf16[592,128]{1,0:T(8,128)(2,1)S(1)}, bf16[592,128]{1,0:T(8,128)(2,1)S(1)}, u32[]{:S(2)}, u32[]{:S(2)}) collective-permute-start(bf16[592,128]{1,0:T(8,128)(2,1)S(1)} %collective-permute-done.12.refs_3_), channel_id=1, source_target_pairs={{4,1},{5,0},{0,9},{1,8},{8,13},{9,12},{12,5},{13,4},{6,3},{7,2},{2... | collective-permute-start | bytes 454664 | tf_op jit(solution)/shard_map/ppermute | solution.py:303
  29.9 0.0 collective-permute-done.13.refs_5_
  29.9 1.4 %shard_map.40 = (f32[192,896]{1,0:T(8,128)S(1)}, bf16[64,896]{1,0:T(8,128)(2,1)S(1)}, bf16[64,896]{1,0:T(8,128)(2,1)S(1)}, bf16[64,896]{1,0:T(8,128)(2,1)S(1)}) custom-call(bf16[1168,128]{1,0:T(8,128)(2,1)S(1)} %get-tuple-element.34.own, bf16[1168,128]{1,0:T(8,128)(2,1)S(1)} %collective-permute-done.other, ...), custom_call_target="tpu_custom_call", output_to_operand_aliasing={{0}: (9, {})} | custom-call | tf_op jit(solution)/shard_map/pallas_call | solution.py:245
  31.4 0.1 collective-permute-start.16
  31.4 0.5 %collective-permute-start.17 = (bf16[64,896]{1,0:T(8,128)(2,1)S(1)}, bf16[64,896]{1,0:T(8,128)(2,1)S(1)}, u32[]{:S(2)}, u32[]{:S(2)}) collective-permute-start(bf16[64,896]{1,0:T(8,128)(2,1)S(1)} %get-tuple-element.56), channel_id=1, source_target_pairs={{0,1},{1,0},{2,3},{3,2},{4,5},{5,4},{6,7},{7,6},{8,9},{9,8},{10,11... | collective-permute-start | bytes 344072 | tf_op jit(solution)/shard_map/ppermute | solution.py:309
  31.9 0.0 collective-permute-done.11.first
  31.9 0.3 collective-permute-start.18
  32.3 0.2 collective-permute-start.14
  32.5 0.3 collective-permute-done.16.refs_0_
  32.8 0.2 collective-permute-done.17.refs_1_
  32.9 0.8 %collective-permute-done.15.second = bf16[592,128]{1,0:T(8,128)(2,1)S(1)} collective-permute-done((bf16[592,128]{1,0:T(8,128)(2,1)S(1)}, bf16[592,128]{1,0:T(8,128)(2,1)S(1)}, u32[]{:S(2)}, u32[]{:S(2)}) %collective-permute-start.15) | collective-permute-done | bytes 151584 | tf_op jit(solution)/shard_map/ppermute | solution.py:303
  33.7 0.0 collective-permute-done.18.refs_2_
  33.7 0.1 collective-permute-start.19
  33.8 0.8 %shard_map.41.total = f32[192,896]{1,0:T(8,128)S(1)} custom-call(bf16[1168,128]{1,0:T(8,128)(2,1)S(1)} %get-tuple-element.34.own, f32[384,128]{1,0:T(8,128)S(1)} %get-tuple-element.43.info, bf16[592,128]{1,0:T(8,128)(2,1)S(1)} %collective-permute-done.11.first, bf16[592,128]{1,0:T(8,128)(2,1)S(1)} %collective-permute-done.15.second, ...), custom_call_target="tpu_custom_call", output_to_operand_aliasing={{}: (4, {})} | custom-call | tf_op jit(solution)/shard_map/pallas_call | solution.py:245
  34.6 0.0 collective-permute-done.14.first
  34.6 0.5 %collective-permute-done.19.second = bf16[592,128]{1,0:T(8,128)(2,1)S(1)} collective-permute-done((bf16[592,128]{1,0:T(8,128)(2,1)S(1)}, bf16[592,128]{1,0:T(8,128)(2,1)S(1)}, u32[]{:S(2)}, u32[]{:S(2)}) %collective-permute-start.19) | collective-permute-done | bytes 151584 | tf_op jit(solution)/shard_map/ppermute | solution.py:309
  35.1 1.3 %shard_map.42 = bf16[192,768]{1,0:T(8,128)(2,1)} custom-call(bf16[1168,128]{1,0:T(8,128)(2,1)S(1)} %get-tuple-element.34.own, f32[384,128]{1,0:T(8,128)S(1)} %get-tuple-element.43.info, bf16[592,128]{1,0:T(8,128)(2,1)S(1)} %collective-permute-done.14.first, bf16[592,128]{1,0:T(8,128)(2,1)S(1)} %collective-permute-done.19.second, f32[192,896]{1,0:T(8,128)S(1)} %shard_map.41.total), custom_call_target="tpu_custom_call" | custom-call | tf_op jit(solution)/shard_map/pallas_call | solution.py:271
  (1 shorter events, 0.0 us)
Async XLA Ops:
  0.0 1.0 %copy-start = (bf16[192,768]{1,0:T(8,128)(2,1)S(1)}, bf16[192,768]{1,0:T(8,128)(2,1)}, u32[]{:S(2)}) copy-start(bf16[192,768]{1,0:T(8,128)(2,1)} %rows.3) | copy-start | bytes 884740
  1.0 5.3 %copy-start.2 = (s32[192]{0:T(256)S(1)}, s32[192]{0:T(256)}, u32[]{:S(2)}) copy-start(s32[192]{0:T(256)} %param.5) | copy-start | bytes 2308
  1.0 8.0 %collective-permute-start.2 = (bf16[592,128]{1,0:T(8,128)(2,1)S(1)}, bf16[592,128]{1,0:T(8,128)(2,1)S(1)}, u32[]{:S(2)}, u32[]{:S(2)}) collective-permute-start(bf16[592,128]{1,0:T(8,128)(2,1)S(1)} %shard_map.38), channel_id=1, source_target_pairs={{0,3},{1,2},{2,1},{3,0},{4,7},{5,6},{6,5},{7,4},{8,11},{9,10},{10,... | collective-permute-start | bytes 454664 | tf_op jit(solution)/shard_map/ppermute | solution.py:306
  3.4 6.8 %collective-permute-start.1 = (bf16[592,128]{1,0:T(8,128)(2,1)S(1)}, bf16[592,128]{1,0:T(8,128)(2,1)S(1)}, u32[]{:S(2)}, u32[]{:S(2)}) collective-permute-start(bf16[592,128]{1,0:T(8,128)(2,1)S(1)} %shard_map.38), channel_id=1, source_target_pairs={{4,1},{5,0},{0,9},{1,8},{8,13},{9,12},{12,5},{13,4},{6,3},{7,2},{2... | collective-permute-start | bytes 454664 | tf_op jit(solution)/shard_map/ppermute | solution.py:303
  6.3 0.7 %copy-start.1 = (s32[192,1]{0,1:T(1,128)S(1)}, s32[192,1]{0,1:T(1,128)}, u32[]{:S(2)}) copy-start(s32[192,1]{0,1:T(1,128)} %param.4) | copy-start | bytes 2308
  7.1 6.3 %collective-permute-start.4 = (bf16[592,128]{1,0:T(8,128)(2,1)S(1)}, bf16[592,128]{1,0:T(8,128)(2,1)S(1)}, u32[]{:S(2)}, u32[]{:S(2)}) collective-permute-start(bf16[592,128]{1,0:T(8,128)(2,1)S(1)} %get-tuple-element.36), channel_id=1, source_target_pairs={{0,3},{1,2},{2,1},{3,0},{4,7},{5,6},{6,5},{7,4},{8,11},{9,10},{10,... | collective-permute-start | bytes 454664 | tf_op jit(solution)/shard_map/ppermute | solution.py:306
  7.2 6.2 %collective-permute-start.3 = (bf16[592,128]{1,0:T(8,128)(2,1)S(1)}, bf16[592,128]{1,0:T(8,128)(2,1)S(1)}, u32[]{:S(2)}, u32[]{:S(2)}) collective-permute-start(bf16[592,128]{1,0:T(8,128)(2,1)S(1)} %get-tuple-element.36), channel_id=1, source_target_pairs={{4,1},{5,0},{0,9},{1,8},{8,13},{9,12},{12,5},{13,4},{6,3},{7,2},{2... | collective-permute-start | bytes 454664 | tf_op jit(solution)/shard_map/ppermute | solution.py:303
  10.2 6.4 %collective-permute-start.6 = (bf16[592,128]{1,0:T(8,128)(2,1)S(1)}, bf16[592,128]{1,0:T(8,128)(2,1)S(1)}, u32[]{:S(2)}, u32[]{:S(2)}) collective-permute-start(bf16[592,128]{1,0:T(8,128)(2,1)S(1)} %collective-permute-done.1.refs_4_), channel_id=1, source_target_pairs={{0,3},{1,2},{2,1},{3,0},{4,7},{5,6},{6,5},{7,4},{8,11},{9,10},{10,... | collective-permute-start | bytes 454664 | tf_op jit(solution)/shard_map/ppermute | solution.py:306
  10.2 6.8 %collective-permute-start.5 = (bf16[592,128]{1,0:T(8,128)(2,1)S(1)}, bf16[592,128]{1,0:T(8,128)(2,1)S(1)}, u32[]{:S(2)}, u32[]{:S(2)}) collective-permute-start(bf16[592,128]{1,0:T(8,128)(2,1)S(1)} %collective-permute-done.1.refs_4_), channel_id=1, source_target_pairs={{4,1},{5,0},{0,9},{1,8},{8,13},{9,12},{12,5},{13,4},{6,3},{7,2},{2... | collective-permute-start | bytes 454664 | tf_op jit(solution)/shard_map/ppermute | solution.py:303
  13.3 11.0 %collective-permute-start = (bf16[1168,128]{1,0:T(8,128)(2,1)S(1)}, bf16[1168,128]{1,0:T(8,128)(2,1)S(1)}, u32[]{:S(2)}, u32[]{:S(2)}) collective-permute-start(bf16[1168,128]{1,0:T(8,128)(2,1)S(1)} %get-tuple-element.34.own), channel_id=1, source_target_pairs={{0,1},{1,0},{2,3},{3,2},{4,5},{5,4},{6,7},{7,6},{8,9},{9,8},{10,11... | collective-permute-start | bytes 897032 | tf_op jit(solution)/shard_map/ppermute | solution.py:309
  13.4 8.2 %collective-permute-start.8 = (bf16[592,128]{1,0:T(8,128)(2,1)S(1)}, bf16[592,128]{1,0:T(8,128)(2,1)S(1)}, u32[]{:S(2)}, u32[]{:S(2)}) collective-permute-start(bf16[592,128]{1,0:T(8,128)(2,1)S(1)} %collective-permute-done.3.refs_5_), channel_id=1, source_target_pairs={{0,3},{1,2},{2,1},{3,0},{4,7},{5,6},{6,5},{7,4},{8,11},{9,10},{10,... | collective-permute-start | bytes 454664 | tf_op jit(solution)/shard_map/ppermute | solution.py:306
  15.1 6.4 %collective-permute-start.7 = (bf16[592,128]{1,0:T(8,128)(2,1)S(1)}, bf16[592,128]{1,0:T(8,128)(2,1)S(1)}, u32[]{:S(2)}, u32[]{:S(2)}) collective-permute-start(bf16[592,128]{1,0:T(8,128)(2,1)S(1)} %collective-permute-done.3.refs_5_), channel_id=1, source_target_pairs={{4,1},{5,0},{0,9},{1,8},{8,13},{9,12},{12,5},{13,4},{6,3},{7,2},{2... | collective-permute-start | bytes 454664 | tf_op jit(solution)/shard_map/ppermute | solution.py:303
  17.0 8.8 %collective-permute-start.10 = (bf16[592,128]{1,0:T(8,128)(2,1)S(1)}, bf16[592,128]{1,0:T(8,128)(2,1)S(1)}, u32[]{:S(2)}, u32[]{:S(2)}) collective-permute-start(bf16[592,128]{1,0:T(8,128)(2,1)S(1)} %collective-permute-done.5.refs_0_), channel_id=1, source_target_pairs={{0,3},{1,2},{2,1},{3,0},{4,7},{5,6},{6,5},{7,4},{8,11},{9,10},{10,... | collective-permute-start | bytes 454664 | tf_op jit(solution)/shard_map/ppermute | solution.py:306
  18.1 7.7 %collective-permute-start.9 = (bf16[592,128]{1,0:T(8,128)(2,1)S(1)}, bf16[592,128]{1,0:T(8,128)(2,1)S(1)}, u32[]{:S(2)}, u32[]{:S(2)}) collective-permute-start(bf16[592,128]{1,0:T(8,128)(2,1)S(1)} %collective-permute-done.5.refs_0_), channel_id=1, source_target_pairs={{4,1},{5,0},{0,9},{1,8},{8,13},{9,12},{12,5},{13,4},{6,3},{7,2},{2... | collective-permute-start | bytes 454664 | tf_op jit(solution)/shard_map/ppermute | solution.py:303
  21.5 6.1 %collective-permute-start.12 = (bf16[592,128]{1,0:T(8,128)(2,1)S(1)}, bf16[592,128]{1,0:T(8,128)(2,1)S(1)}, u32[]{:S(2)}, u32[]{:S(2)}) collective-permute-start(bf16[592,128]{1,0:T(8,128)(2,1)S(1)} %collective-permute-done.7.refs_1_), channel_id=1, source_target_pairs={{0,3},{1,2},{2,1},{3,0},{4,7},{5,6},{6,5},{7,4},{8,11},{9,10},{10,... | collective-permute-start | bytes 454664 | tf_op jit(solution)/shard_map/ppermute | solution.py:306
  21.7 8.2 %collective-permute-start.13 = (bf16[592,128]{1,0:T(8,128)(2,1)S(1)}, bf16[592,128]{1,0:T(8,128)(2,1)S(1)}, u32[]{:S(2)}, u32[]{:S(2)}) collective-permute-start(bf16[592,128]{1,0:T(8,128)(2,1)S(1)} %collective-permute-done.7.refs_1_), channel_id=1, source_target_pairs={{4,1},{5,0},{0,9},{1,8},{8,13},{9,12},{12,5},{13,4},{6,3},{7,2},{2... | collective-permute-start | bytes 454664 | tf_op jit(solution)/shard_map/ppermute | solution.py:303
  25.8 6.1 %collective-permute-start.11 = (bf16[592,128]{1,0:T(8,128)(2,1)S(1)}, bf16[592,128]{1,0:T(8,128)(2,1)S(1)}, u32[]{:S(2)}, u32[]{:S(2)}) collective-permute-start(bf16[592,128]{1,0:T(8,128)(2,1)S(1)} %collective-permute-done.9.refs_4_), channel_id=1, source_target_pairs={{0,3},{1,2},{2,1},{3,0},{4,7},{5,6},{6,5},{7,4},{8,11},{9,10},{10,... | collective-permute-start | bytes 454664 | tf_op jit(solution)/shard_map/ppermute | solution.py:306
  27.6 6.1 %collective-permute-start.15 = (bf16[592,128]{1,0:T(8,128)(2,1)S(1)}, bf16[592,128]{1,0:T(8,128)(2,1)S(1)}, u32[]{:S(2)}, u32[]{:S(2)}) collective-permute-start(bf16[592,128]{1,0:T(8,128)(2,1)S(1)} %collective-permute-done.12.refs_3_), channel_id=1, source_target_pairs={{4,1},{5,0},{0,9},{1,8},{8,13},{9,12},{12,5},{13,4},{6,3},{7,2},{2... | collective-permute-start | bytes 454664 | tf_op jit(solution)/shard_map/ppermute | solution.py:303
  31.4 1.4 %collective-permute-start.16 = (bf16[64,896]{1,0:T(8,128)(2,1)S(1)}, bf16[64,896]{1,0:T(8,128)(2,1)S(1)}, u32[]{:S(2)}, u32[]{:S(2)}) collective-permute-start(bf16[64,896]{1,0:T(8,128)(2,1)S(1)} %get-tuple-element.55), channel_id=1, source_target_pairs={{0,1},{1,0},{2,3},{3,2},{4,5},{5,4},{6,7},{7,6},{8,9},{9,8},{10,11... | collective-permute-start | bytes 344072 | tf_op jit(solution)/shard_map/ppermute | solution.py:309
  31.4 1.5 %collective-permute-start.17 = (bf16[64,896]{1,0:T(8,128)(2,1)S(1)}, bf16[64,896]{1,0:T(8,128)(2,1)S(1)}, u32[]{:S(2)}, u32[]{:S(2)}) collective-permute-start(bf16[64,896]{1,0:T(8,128)(2,1)S(1)} %get-tuple-element.56), channel_id=1, source_target_pairs={{0,1},{1,0},{2,3},{3,2},{4,5},{5,4},{6,7},{7,6},{8,9},{9,8},{10,11... | collective-permute-start | bytes 344072 | tf_op jit(solution)/shard_map/ppermute | solution.py:309
  31.9 1.8 %collective-permute-start.18 = (bf16[64,896]{1,0:T(8,128)(2,1)S(1)}, bf16[64,896]{1,0:T(8,128)(2,1)S(1)}, u32[]{:S(2)}, u32[]{:S(2)}) collective-permute-start(bf16[64,896]{1,0:T(8,128)(2,1)S(1)} %get-tuple-element.57), channel_id=1, source_target_pairs={{0,1},{1,0},{2,3},{3,2},{4,5},{5,4},{6,7},{7,6},{8,9},{9,8},{10,11... | collective-permute-start | bytes 344072 | tf_op jit(solution)/shard_map/ppermute | solution.py:309
  32.3 2.3 %collective-permute-start.14 = (bf16[592,128]{1,0:T(8,128)(2,1)S(1)}, bf16[592,128]{1,0:T(8,128)(2,1)S(1)}, u32[]{:S(2)}, u32[]{:S(2)}) collective-permute-start(bf16[592,128]{1,0:T(8,128)(2,1)S(1)} %collective-permute-done.11.first), channel_id=1, source_target_pairs={{0,1},{1,0},{2,3},{3,2},{4,5},{5,4},{6,7},{7,6},{8,9},{9,8},{10,11... | collective-permute-start | bytes 454664 | tf_op jit(solution)/shard_map/ppermute | solution.py:309
  33.7 1.4 %collective-permute-start.19 = (bf16[592,128]{1,0:T(8,128)(2,1)S(1)}, bf16[592,128]{1,0:T(8,128)(2,1)S(1)}, u32[]{:S(2)}, u32[]{:S(2)}) collective-permute-start(bf16[592,128]{1,0:T(8,128)(2,1)S(1)} %collective-permute-done.15.second), channel_id=1, source_target_pairs={{0,1},{1,0},{2,3},{3,2},{4,5},{5,4},{6,7},{7,6},{8,9},{9,8},{10,11... | collective-permute-start | bytes 454664 | tf_op jit(solution)/shard_map/ppermute | solution.py:309

commit v27 on v26

--- a/solution.py
+++ b/solution.py
@@ -79,12 +79,9 @@
 
 
 def first_pack_kernel(rows, first):
-    width = rows.shape[1]
-    slabs = width // 128
     half = rows.shape[0] // 2
-    for slab in range(slabs):
+    for slab in range(rows.shape[1] // 128):
         first[slab * half : (slab + 1) * half, :] = rows[:half, slab * 128 : (slab + 1) * 128]
-    first[slabs * half :, :] = jnp.zeros((LINES, 128), BF16)
 
 
 def pack_kernel(rows, group, cluster, whole, second):
@@ -308,11 +305,10 @@
     def other_core(rows):
         return lax.ppermute(rows, "pair", [(0, 1), (1, 0)])
 
-    half_shape = ((slabs * half + LINES, 128), BF16)
-    (first,) = call(first_pack_kernel, [half_shape], [embeddings])
+    (first,) = call(first_pack_kernel, [((slabs * half, 128), BF16)], [embeddings])
     whole, second = call(
         pack_kernel,
-        [((slabs * rows_here + LINES, 128), BF16), half_shape],
+        [((slabs * count + LINES, 128), BF16) for count in (rows_here, half)],
         [embeddings, group_of.reshape(line), cluster_id.reshape(line)],
     )
     along_by = [(first, second)]

time: 36.5 us -> 36.6 us (level)
  waiting for transfers between devices: 4.5 us -> 3.96 us
  starting transfers between devices: 25.1 us -> 25.6 us
    ppermute x7, waiting for transfers between devices: 2.41 us -> 1.83 us  [along(): return lax.ppermute(rows, ('blk', 'pair'), hops)]
  transfers between devices with their start and end apart: 20 -> 20, of which waited for: 8 -> 9; matrix products, arithmetic and copies ran while one was open for 0% -> 0% of each run, Pallas kernels for 10% -> 10%
where the time goes in v27:
time: 36.6 us; the launch traced here: 36.4 us
  starting transfers between devices  25.6 us (70%)
  Pallas kernels  5.11 us (14%)
  waiting for transfers between devices  3.96 us (11%)
  local copies, waits for them, and re-layouts  1.64 us (4%)
    ppermute x7, starting transfers between devices, along(): return lax.ppermute(rows, ('blk', 'pair'), hops)  17.5 us
    ppermute x7, starting transfers between devices, across(): return lax.ppermute(rows, ('sub', 'pair'), [(0, 3), (1, 2), (2, 1), (3, 0)])  7.01 us
    pallas_call x5, Pallas kernels, call(): pl.pallas_call(kernel, out_shape=[jax.ShapeDtypeStruct(shape, dtype) for...  3.82 us
    ppermute x7, waiting for transfers between devices, along(): return lax.ppermute(rows, ('blk', 'pair'), hops)  1.83 us
    unnamed x6, local copies, waits for them, and re-layouts  1.64 us
    pallas_call x1, Pallas kernels, finish(): pl.pallas_call(last_kernel, out_shape=jax.ShapeDtypeStruct(shape, BF16),...  1.29 us
    ppermute x6, waiting for transfers between devices, other_core(): return lax.ppermute(rows, 'pair', [(0, 1), (1, 0)])  1.22 us
    ppermute x6, starting transfers between devices, other_core(): return lax.ppermute(rows, 'pair', [(0, 1), (1, 0)])  1.16 us
  transfers between devices with their start and end apart: 20, of which 9 were waited for; matrix products, arithmetic and copies ran while one was open for 0% of the time, Pallas kernels for 10%

profile of v27, /device:TPU:0, one launch (start us, length us, event | category | flops | bytes accessed | tf_op | source)
XLA Modules:
  0.0 36.4 jit_solution(13497518184392980824)
XLA Ops:
  0.0 0.0 copy-start
  0.0 1.0 %copy-done = bf16[192,768]{1,0:T(8,128)(2,1)S(1)} copy-done((bf16[192,768]{1,0:T(8,128)(2,1)S(1)}, bf16[192,768]{1,0:T(8,128)(2,1)}, u32[]{:S(2)}) %copy-start) | copy-done | bytes 294936
  1.0 0.0 copy-start.2
  1.0 2.4 %collective-permute-start.2 = (bf16[576,128]{1,0:T(8,128)(2,1)S(1)}, bf16[576,128]{1,0:T(8,128)(2,1)S(1)}, u32[]{:S(2)}, u32[]{:S(2)}) collective-permute-start(bf16[576,128]{1,0:T(8,128)(2,1)S(1)} %shard_map.38), channel_id=1, source_target_pairs={{0,3},{1,2},{2,1},{3,0},{4,7},{5,6},{6,5},{7,4},{8,11},{9,10},{10,... | collective-permute-start | bytes 442376 | tf_op jit(solution)/shard_map/ppermute | solution.py:303
  3.4 2.9 %collective-permute-start.1 = (bf16[576,128]{1,0:T(8,128)(2,1)S(1)}, bf16[576,128]{1,0:T(8,128)(2,1)S(1)}, u32[]{:S(2)}, u32[]{:S(2)}) collective-permute-start(bf16[576,128]{1,0:T(8,128)(2,1)S(1)} %shard_map.38), channel_id=1, source_target_pairs={{4,1},{5,0},{0,9},{1,8},{8,13},{9,12},{12,5},{13,4},{6,3},{7,2},{2... | collective-permute-start | bytes 442376 | tf_op jit(solution)/shard_map/ppermute | solution.py:300
  6.3 0.0 copy-start.1
  6.3 0.0 copy-done.2
  6.3 0.7 %copy-done.1 = s32[192,1]{0,1:T(1,128)S(1)} copy-done((s32[192,1]{0,1:T(1,128)S(1)}, s32[192,1]{0,1:T(1,128)}, u32[]{:S(2)}) %copy-start.1) | copy-done | bytes 792
  7.0 0.1 shard_map.37
  7.1 0.1 collective-permute-start.4
  7.2 1.8 %collective-permute-start.3 = (bf16[592,128]{1,0:T(8,128)(2,1)S(1)}, bf16[592,128]{1,0:T(8,128)(2,1)S(1)}, u32[]{:S(2)}, u32[]{:S(2)}) collective-permute-start(bf16[592,128]{1,0:T(8,128)(2,1)S(1)} %get-tuple-element.36), channel_id=1, source_target_pairs={{4,1},{5,0},{0,9},{1,8},{8,13},{9,12},{12,5},{13,4},{6,3},{7,2},{2... | collective-permute-start | bytes 454664 | tf_op jit(solution)/shard_map/ppermute | solution.py:300
  9.0 0.0 collective-permute-start
  9.0 0.0 collective-permute-done.2.refs_0_
  9.0 1.1 %collective-permute-done.1.refs_4_ = bf16[576,128]{1,0:T(8,128)(2,1)S(1)} collective-permute-done((bf16[576,128]{1,0:T(8,128)(2,1)S(1)}, bf16[576,128]{1,0:T(8,128)(2,1)S(1)}, u32[]{:S(2)}, u32[]{:S(2)}) %collective-permute-start.1) | collective-permute-done | bytes 147488 | tf_op jit(solution)/shard_map/ppermute | solution.py:300
  10.0 0.5 %collective-permute-start.6 = (bf16[576,128]{1,0:T(8,128)(2,1)S(1)}, bf16[576,128]{1,0:T(8,128)(2,1)S(1)}, u32[]{:S(2)}, u32[]{:S(2)}) collective-permute-start(bf16[576,128]{1,0:T(8,128)(2,1)S(1)} %collective-permute-done.1.refs_4_), channel_id=1, source_target_pairs={{0,3},{1,2},{2,1},{3,0},{4,7},{5,6},{6,5},{7,4},{8,11},{9,10},{10,... | collective-permute-start | bytes 442376 | tf_op jit(solution)/shard_map/ppermute | solution.py:303
  10.6 2.6 %collective-permute-start.5 = (bf16[576,128]{1,0:T(8,128)(2,1)S(1)}, bf16[576,128]{1,0:T(8,128)(2,1)S(1)}, u32[]{:S(2)}, u32[]{:S(2)}) collective-permute-start(bf16[576,128]{1,0:T(8,128)(2,1)S(1)} %collective-permute-done.1.refs_4_), channel_id=1, source_target_pairs={{4,1},{5,0},{0,9},{1,8},{8,13},{9,12},{12,5},{13,4},{6,3},{7,2},{2... | collective-permute-start | bytes 442376 | tf_op jit(solution)/shard_map/ppermute | solution.py:300
  13.2 0.2 collective-permute-done.4.refs_1_
  13.4 0.0 collective-permute-done.3.refs_5_
  13.4 1.5 %collective-permute-start.8 = (bf16[592,128]{1,0:T(8,128)(2,1)S(1)}, bf16[592,128]{1,0:T(8,128)(2,1)S(1)}, u32[]{:S(2)}, u32[]{:S(2)}) collective-permute-start(bf16[592,128]{1,0:T(8,128)(2,1)S(1)} %collective-permute-done.3.refs_5_), channel_id=1, source_target_pairs={{0,3},{1,2},{2,1},{3,0},{4,7},{5,6},{6,5},{7,4},{8,11},{9,10},{10,... | collective-permute-start | bytes 454664 | tf_op jit(solution)/shard_map/ppermute | solution.py:303
  14.9 1.3 %collective-permute-start.7 = (bf16[592,128]{1,0:T(8,128)(2,1)S(1)}, bf16[592,128]{1,0:T(8,128)(2,1)S(1)}, u32[]{:S(2)}, u32[]{:S(2)}) collective-permute-start(bf16[592,128]{1,0:T(8,128)(2,1)S(1)} %collective-permute-done.3.refs_5_), channel_id=1, source_target_pairs={{4,1},{5,0},{0,9},{1,8},{8,13},{9,12},{12,5},{13,4},{6,3},{7,2},{2... | collective-permute-start | bytes 454664 | tf_op jit(solution)/shard_map/ppermute | solution.py:300
  16.2 0.3 collective-permute-done.6.refs_2_
  16.5 0.3 collective-permute-done.5.refs_0_
  16.8 1.2 %collective-permute-start.10 = (bf16[576,128]{1,0:T(8,128)(2,1)S(1)}, bf16[576,128]{1,0:T(8,128)(2,1)S(1)}, u32[]{:S(2)}, u32[]{:S(2)}) collective-permute-start(bf16[576,128]{1,0:T(8,128)(2,1)S(1)} %collective-permute-done.5.refs_0_), channel_id=1, source_target_pairs={{0,3},{1,2},{2,1},{3,0},{4,7},{5,6},{6,5},{7,4},{8,11},{9,10},{10,... | collective-permute-start | bytes 442376 | tf_op jit(solution)/shard_map/ppermute | solution.py:303
  18.0 3.4 %collective-permute-start.9 = (bf16[576,128]{1,0:T(8,128)(2,1)S(1)}, bf16[576,128]{1,0:T(8,128)(2,1)S(1)}, u32[]{:S(2)}, u32[]{:S(2)}) collective-permute-start(bf16[576,128]{1,0:T(8,128)(2,1)S(1)} %collective-permute-done.5.refs_0_), channel_id=1, source_target_pairs={{4,1},{5,0},{0,9},{1,8},{8,13},{9,12},{12,5},{13,4},{6,3},{7,2},{2... | collective-permute-start | bytes 442376 | tf_op jit(solution)/shard_map/ppermute | solution.py:300
  21.3 0.0 collective-permute-done.8.refs_3_
  21.3 0.0 collective-permute-done.7.refs_1_
  21.3 0.0 collective-permute-start.12
  21.4 2.8 %collective-permute-start.13 = (bf16[592,128]{1,0:T(8,128)(2,1)S(1)}, bf16[592,128]{1,0:T(8,128)(2,1)S(1)}, u32[]{:S(2)}, u32[]{:S(2)}) collective-permute-start(bf16[592,128]{1,0:T(8,128)(2,1)S(1)} %collective-permute-done.7.refs_1_), channel_id=1, source_target_pairs={{4,1},{5,0},{0,9},{1,8},{8,13},{9,12},{12,5},{13,4},{6,3},{7,2},{2... | collective-permute-start | bytes 454664 | tf_op jit(solution)/shard_map/ppermute | solution.py:300
  24.2 0.0 collective-permute-done.other
  24.2 1.5 %shard_map.39 = (f32[192,896]{1,0:T(8,128)S(1)}, f32[192,896]{1,0:T(8,128)S(1)}, f32[384,128]{1,0:T(8,128)S(1)}) custom-call(bf16[1168,128]{1,0:T(8,128)(2,1)S(1)} %get-tuple-element.34.own, bf16[1168,128]{1,0:T(8,128)(2,1)S(1)} %collective-permute-done.other, bf16[576,128]{1,0:T(8,128)(2,1)S(1)} %collective-permute-done.2.refs_0_, ...), custom_call_target="tpu_custom_call" | custom-call | tf_op jit(solution)/shard_map/pallas_call | solution.py:242
  25.7 0.0 collective-permute-done.10.refs_2_
  25.7 0.0 collective-permute-done.9.refs_4_
  25.7 1.2 %collective-permute-start.11 = (bf16[576,128]{1,0:T(8,128)(2,1)S(1)}, bf16[576,128]{1,0:T(8,128)(2,1)S(1)}, u32[]{:S(2)}, u32[]{:S(2)}) collective-permute-start(bf16[576,128]{1,0:T(8,128)(2,1)S(1)} %collective-permute-done.9.refs_4_), channel_id=1, source_target_pairs={{0,3},{1,2},{2,1},{3,0},{4,7},{5,6},{6,5},{7,4},{8,11},{9,10},{10,... | collective-permute-start | bytes 442376 | tf_op jit(solution)/shard_map/ppermute | solution.py:303
  26.9 0.4 %collective-permute-done.12.refs_3_ = bf16[592,128]{1,0:T(8,128)(2,1)S(1)} collective-permute-done((bf16[592,128]{1,0:T(8,128)(2,1)S(1)}, bf16[592,128]{1,0:T(8,128)(2,1)S(1)}, u32[]{:S(2)}, u32[]{:S(2)}) %collective-permute-start.12) | collective-permute-done | bytes 151584 | tf_op jit(solution)/shard_map/ppermute | solution.py:303
  27.3 2.8 %collective-permute-start.15 = (bf16[592,128]{1,0:T(8,128)(2,1)S(1)}, bf16[592,128]{1,0:T(8,128)(2,1)S(1)}, u32[]{:S(2)}, u32[]{:S(2)}) collective-permute-start(bf16[592,128]{1,0:T(8,128)(2,1)S(1)} %collective-permute-done.12.refs_3_), channel_id=1, source_target_pairs={{4,1},{5,0},{0,9},{1,8},{8,13},{9,12},{12,5},{13,4},{6,3},{7,2},{2... | collective-permute-start | bytes 454664 | tf_op jit(solution)/shard_map/ppermute | solution.py:300
  30.1 0.0 collective-permute-done.13.refs_5_
  30.1 1.4 %shard_map.40 = (f32[192,896]{1,0:T(8,128)S(1)}, bf16[64,896]{1,0:T(8,128)(2,1)S(1)}, bf16[64,896]{1,0:T(8,128)(2,1)S(1)}, bf16[64,896]{1,0:T(8,128)(2,1)S(1)}) custom-call(bf16[1168,128]{1,0:T(8,128)(2,1)S(1)} %get-tuple-element.34.own, bf16[1168,128]{1,0:T(8,128)(2,1)S(1)} %collective-permute-done.other, ...), custom_call_target="tpu_custom_call", output_to_operand_aliasing={{0}: (9, {})} | custom-call | tf_op jit(solution)/shard_map/pallas_call | solution.py:242
  31.5 0.1 collective-permute-start.16
  31.6 0.5 %collective-permute-start.17 = (bf16[64,896]{1,0:T(8,128)(2,1)S(1)}, bf16[64,896]{1,0:T(8,128)(2,1)S(1)}, u32[]{:S(2)}, u32[]{:S(2)}) collective-permute-start(bf16[64,896]{1,0:T(8,128)(2,1)S(1)} %get-tuple-element.56), channel_id=1, source_target_pairs={{0,1},{1,0},{2,3},{3,2},{4,5},{5,4},{6,7},{7,6},{8,9},{9,8},{10,11... | collective-permute-start | bytes 344072 | tf_op jit(solution)/shard_map/ppermute | solution.py:306
  32.1 0.0 collective-permute-done.11.first
  32.1 0.1 collective-permute-start.18
  32.2 0.7 %collective-permute-done.16.refs_0_ = bf16[64,896]{1,0:T(8,128)(2,1)S(1)} collective-permute-done((bf16[64,896]{1,0:T(8,128)(2,1)S(1)}, bf16[64,896]{1,0:T(8,128)(2,1)S(1)}, u32[]{:S(2)}, u32[]{:S(2)}) %collective-permute-start.16) | collective-permute-done | bytes 114720 | tf_op jit(solution)/shard_map/ppermute | solution.py:306
  32.9 0.2 collective-permute-done.17.refs_1_
  33.1 0.5 %collective-permute-done.15.second = bf16[592,128]{1,0:T(8,128)(2,1)S(1)} collective-permute-done((bf16[592,128]{1,0:T(8,128)(2,1)S(1)}, bf16[592,128]{1,0:T(8,128)(2,1)S(1)}, u32[]{:S(2)}, u32[]{:S(2)}) %collective-permute-start.15) | collective-permute-done | bytes 151584 | tf_op jit(solution)/shard_map/ppermute | solution.py:300
  33.5 0.0 collective-permute-done.18.refs_2_
  33.5 0.1 collective-permute-start.19
  33.7 0.4 %collective-permute-start.14 = (bf16[576,128]{1,0:T(8,128)(2,1)S(1)}, bf16[576,128]{1,0:T(8,128)(2,1)S(1)}, u32[]{:S(2)}, u32[]{:S(2)}) collective-permute-start(bf16[576,128]{1,0:T(8,128)(2,1)S(1)} %collective-permute-done.11.first), channel_id=1, source_target_pairs={{0,1},{1,0},{2,3},{3,2},{4,5},{5,4},{6,7},{7,6},{8,9},{9,8},{10,11... | collective-permute-start | bytes 442376 | tf_op jit(solution)/shard_map/ppermute | solution.py:306
  34.1 0.8 %shard_map.41.total = f32[192,896]{1,0:T(8,128)S(1)} custom-call(bf16[1168,128]{1,0:T(8,128)(2,1)S(1)} %get-tuple-element.34.own, f32[384,128]{1,0:T(8,128)S(1)} %get-tuple-element.43.info, bf16[576,128]{1,0:T(8,128)(2,1)S(1)} %collective-permute-done.11.first, bf16[592,128]{1,0:T(8,128)(2,1)S(1)} %collective-permute-done.15.second, ...), custom_call_target="tpu_custom_call", output_to_operand_aliasing={{}: (4, {})} | custom-call | tf_op jit(solution)/shard_map/pallas_call | solution.py:242
  34.8 0.3 collective-permute-done.14.first
  35.1 0.0 collective-permute-done.19.second
  35.1 1.3 %shard_map.42 = bf16[192,768]{1,0:T(8,128)(2,1)} custom-call(bf16[1168,128]{1,0:T(8,128)(2,1)S(1)} %get-tuple-element.34.own, f32[384,128]{1,0:T(8,128)S(1)} %get-tuple-element.43.info, bf16[576,128]{1,0:T(8,128)(2,1)S(1)} %collective-permute-done.14.first, bf16[592,128]{1,0:T(8,128)(2,1)S(1)} %collective-permute-done.19.second, f32[192,896]{1,0:T(8,128)S(1)} %shard_map.41.total), custom_call_target="tpu_custom_call" | custom-call | tf_op jit(solution)/shard_map/pallas_call | solution.py:268
  (1 shorter events, 0.0 us)
Async XLA Ops:
  0.0 1.0 %copy-start = (bf16[192,768]{1,0:T(8,128)(2,1)S(1)}, bf16[192,768]{1,0:T(8,128)(2,1)}, u32[]{:S(2)}) copy-start(bf16[192,768]{1,0:T(8,128)(2,1)} %rows.3) | copy-start | bytes 884740
  1.0 5.3 %copy-start.2 = (s32[192]{0:T(256)S(1)}, s32[192]{0:T(256)}, u32[]{:S(2)}) copy-start(s32[192]{0:T(256)} %param.5) | copy-start | bytes 2308
  1.0 8.0 %collective-permute-start.2 = (bf16[576,128]{1,0:T(8,128)(2,1)S(1)}, bf16[576,128]{1,0:T(8,128)(2,1)S(1)}, u32[]{:S(2)}, u32[]{:S(2)}) collective-permute-start(bf16[576,128]{1,0:T(8,128)(2,1)S(1)} %shard_map.38), channel_id=1, source_target_pairs={{0,3},{1,2},{2,1},{3,0},{4,7},{5,6},{6,5},{7,4},{8,11},{9,10},{10,... | collective-permute-start | bytes 442376 | tf_op jit(solution)/shard_map/ppermute | solution.py:303
  3.4 6.6 %collective-permute-start.1 = (bf16[576,128]{1,0:T(8,128)(2,1)S(1)}, bf16[576,128]{1,0:T(8,128)(2,1)S(1)}, u32[]{:S(2)}, u32[]{:S(2)}) collective-permute-start(bf16[576,128]{1,0:T(8,128)(2,1)S(1)} %shard_map.38), channel_id=1, source_target_pairs={{4,1},{5,0},{0,9},{1,8},{8,13},{9,12},{12,5},{13,4},{6,3},{7,2},{2... | collective-permute-start | bytes 442376 | tf_op jit(solution)/shard_map/ppermute | solution.py:300
  6.3 0.7 %copy-start.1 = (s32[192,1]{0,1:T(1,128)S(1)}, s32[192,1]{0,1:T(1,128)}, u32[]{:S(2)}) copy-start(s32[192,1]{0,1:T(1,128)} %param.4) | copy-start | bytes 2308
  7.1 6.3 %collective-permute-start.4 = (bf16[592,128]{1,0:T(8,128)(2,1)S(1)}, bf16[592,128]{1,0:T(8,128)(2,1)S(1)}, u32[]{:S(2)}, u32[]{:S(2)}) collective-permute-start(bf16[592,128]{1,0:T(8,128)(2,1)S(1)} %get-tuple-element.36), channel_id=1, source_target_pairs={{0,3},{1,2},{2,1},{3,0},{4,7},{5,6},{6,5},{7,4},{8,11},{9,10},{10,... | collective-permute-start | bytes 454664 | tf_op jit(solution)/shard_map/ppermute | solution.py:303
  7.2 6.2 %collective-permute-start.3 = (bf16[592,128]{1,0:T(8,128)(2,1)S(1)}, bf16[592,128]{1,0:T(8,128)(2,1)S(1)}, u32[]{:S(2)}, u32[]{:S(2)}) collective-permute-start(bf16[592,128]{1,0:T(8,128)(2,1)S(1)} %get-tuple-element.36), channel_id=1, source_target_pairs={{4,1},{5,0},{0,9},{1,8},{8,13},{9,12},{12,5},{13,4},{6,3},{7,2},{2... | collective-permute-start | bytes 454664 | tf_op jit(solution)/shard_map/ppermute | solution.py:300
  9.0 15.2 %collective-permute-start = (bf16[1168,128]{1,0:T(8,128)(2,1)S(1)}, bf16[1168,128]{1,0:T(8,128)(2,1)S(1)}, u32[]{:S(2)}, u32[]{:S(2)}) collective-permute-start(bf16[1168,128]{1,0:T(8,128)(2,1)S(1)} %get-tuple-element.34.own), channel_id=1, source_target_pairs={{0,1},{1,0},{2,3},{3,2},{4,5},{5,4},{6,7},{7,6},{8,9},{9,8},{10,11... | collective-permute-start | bytes 897032 | tf_op jit(solution)/shard_map/ppermute | solution.py:306
  10.0 6.5 %collective-permute-start.6 = (bf16[576,128]{1,0:T(8,128)(2,1)S(1)}, bf16[576,128]{1,0:T(8,128)(2,1)S(1)}, u32[]{:S(2)}, u32[]{:S(2)}) collective-permute-start(bf16[576,128]{1,0:T(8,128)(2,1)S(1)} %collective-permute-done.1.refs_4_), channel_id=1, source_target_pairs={{0,3},{1,2},{2,1},{3,0},{4,7},{5,6},{6,5},{7,4},{8,11},{9,10},{10,... | collective-permute-start | bytes 442376 | tf_op jit(solution)/shard_map/ppermute | solution.py:303
  10.6 6.2 %collective-permute-start.5 = (bf16[576,128]{1,0:T(8,128)(2,1)S(1)}, bf16[576,128]{1,0:T(8,128)(2,1)S(1)}, u32[]{:S(2)}, u32[]{:S(2)}) collective-permute-start(bf16[576,128]{1,0:T(8,128)(2,1)S(1)} %collective-permute-done.1.refs_4_), channel_id=1, source_target_pairs={{4,1},{5,0},{0,9},{1,8},{8,13},{9,12},{12,5},{13,4},{6,3},{7,2},{2... | collective-permute-start | bytes 442376 | tf_op jit(solution)/shard_map/ppermute | solution.py:300
  13.4 8.0 %collective-permute-start.8 = (bf16[592,128]{1,0:T(8,128)(2,1)S(1)}, bf16[592,128]{1,0:T(8,128)(2,1)S(1)}, u32[]{:S(2)}, u32[]{:S(2)}) collective-permute-start(bf16[592,128]{1,0:T(8,128)(2,1)S(1)} %collective-permute-done.3.refs_5_), channel_id=1, source_target_pairs={{0,3},{1,2},{2,1},{3,0},{4,7},{5,6},{6,5},{7,4},{8,11},{9,10},{10,... | collective-permute-start | bytes 454664 | tf_op jit(solution)/shard_map/ppermute | solution.py:303
  14.9 6.4 %collective-permute-start.7 = (bf16[592,128]{1,0:T(8,128)(2,1)S(1)}, bf16[592,128]{1,0:T(8,128)(2,1)S(1)}, u32[]{:S(2)}, u32[]{:S(2)}) collective-permute-start(bf16[592,128]{1,0:T(8,128)(2,1)S(1)} %collective-permute-done.3.refs_5_), channel_id=1, source_target_pairs={{4,1},{5,0},{0,9},{1,8},{8,13},{9,12},{12,5},{13,4},{6,3},{7,2},{2... | collective-permute-start | bytes 454664 | tf_op jit(solution)/shard_map/ppermute | solution.py:300
  16.8 8.9 %collective-permute-start.10 = (bf16[576,128]{1,0:T(8,128)(2,1)S(1)}, bf16[576,128]{1,0:T(8,128)(2,1)S(1)}, u32[]{:S(2)}, u32[]{:S(2)}) collective-permute-start(bf16[576,128]{1,0:T(8,128)(2,1)S(1)} %collective-permute-done.5.refs_0_), channel_id=1, source_target_pairs={{0,3},{1,2},{2,1},{3,0},{4,7},{5,6},{6,5},{7,4},{8,11},{9,10},{10,... | collective-permute-start | bytes 442376 | tf_op jit(solution)/shard_map/ppermute | solution.py:303
  18.0 7.8 %collective-permute-start.9 = (bf16[576,128]{1,0:T(8,128)(2,1)S(1)}, bf16[576,128]{1,0:T(8,128)(2,1)S(1)}, u32[]{:S(2)}, u32[]{:S(2)}) collective-permute-start(bf16[576,128]{1,0:T(8,128)(2,1)S(1)} %collective-permute-done.5.refs_0_), channel_id=1, source_target_pairs={{4,1},{5,0},{0,9},{1,8},{8,13},{9,12},{12,5},{13,4},{6,3},{7,2},{2... | collective-permute-start | bytes 442376 | tf_op jit(solution)/shard_map/ppermute | solution.py:300
  21.3 6.0 %collective-permute-start.12 = (bf16[592,128]{1,0:T(8,128)(2,1)S(1)}, bf16[592,128]{1,0:T(8,128)(2,1)S(1)}, u32[]{:S(2)}, u32[]{:S(2)}) collective-permute-start(bf16[592,128]{1,0:T(8,128)(2,1)S(1)} %collective-permute-done.7.refs_1_), channel_id=1, source_target_pairs={{0,3},{1,2},{2,1},{3,0},{4,7},{5,6},{6,5},{7,4},{8,11},{9,10},{10,... | collective-permute-start | bytes 454664 | tf_op jit(solution)/shard_map/ppermute | solution.py:303
  21.4 8.7 %collective-permute-start.13 = (bf16[592,128]{1,0:T(8,128)(2,1)S(1)}, bf16[592,128]{1,0:T(8,128)(2,1)S(1)}, u32[]{:S(2)}, u32[]{:S(2)}) collective-permute-start(bf16[592,128]{1,0:T(8,128)(2,1)S(1)} %collective-permute-done.7.refs_1_), channel_id=1, source_target_pairs={{4,1},{5,0},{0,9},{1,8},{8,13},{9,12},{12,5},{13,4},{6,3},{7,2},{2... | collective-permute-start | bytes 454664 | tf_op jit(solution)/shard_map/ppermute | solution.py:300
  25.7 6.4 %collective-permute-start.11 = (bf16[576,128]{1,0:T(8,128)(2,1)S(1)}, bf16[576,128]{1,0:T(8,128)(2,1)S(1)}, u32[]{:S(2)}, u32[]{:S(2)}) collective-permute-start(bf16[576,128]{1,0:T(8,128)(2,1)S(1)} %collective-permute-done.9.refs_4_), channel_id=1, source_target_pairs={{0,3},{1,2},{2,1},{3,0},{4,7},{5,6},{6,5},{7,4},{8,11},{9,10},{10,... | collective-permute-start | bytes 442376 | tf_op jit(solution)/shard_map/ppermute | solution.py:303
  27.3 6.2 %collective-permute-start.15 = (bf16[592,128]{1,0:T(8,128)(2,1)S(1)}, bf16[592,128]{1,0:T(8,128)(2,1)S(1)}, u32[]{:S(2)}, u32[]{:S(2)}) collective-permute-start(bf16[592,128]{1,0:T(8,128)(2,1)S(1)} %collective-permute-done.12.refs_3_), channel_id=1, source_target_pairs={{4,1},{5,0},{0,9},{1,8},{8,13},{9,12},{12,5},{13,4},{6,3},{7,2},{2... | collective-permute-start | bytes 454664 | tf_op jit(solution)/shard_map/ppermute | solution.py:300
  31.5 1.4 %collective-permute-start.16 = (bf16[64,896]{1,0:T(8,128)(2,1)S(1)}, bf16[64,896]{1,0:T(8,128)(2,1)S(1)}, u32[]{:S(2)}, u32[]{:S(2)}) collective-permute-start(bf16[64,896]{1,0:T(8,128)(2,1)S(1)} %get-tuple-element.55), channel_id=1, source_target_pairs={{0,1},{1,0},{2,3},{3,2},{4,5},{5,4},{6,7},{7,6},{8,9},{9,8},{10,11... | collective-permute-start | bytes 344072 | tf_op jit(solution)/shard_map/ppermute | solution.py:306
  31.6 1.5 %collective-permute-start.17 = (bf16[64,896]{1,0:T(8,128)(2,1)S(1)}, bf16[64,896]{1,0:T(8,128)(2,1)S(1)}, u32[]{:S(2)}, u32[]{:S(2)}) collective-permute-start(bf16[64,896]{1,0:T(8,128)(2,1)S(1)} %get-tuple-element.56), channel_id=1, source_target_pairs={{0,1},{1,0},{2,3},{3,2},{4,5},{5,4},{6,7},{7,6},{8,9},{9,8},{10,11... | collective-permute-start | bytes 344072 | tf_op jit(solution)/shard_map/ppermute | solution.py:306
  32.1 1.4 %collective-permute-start.18 = (bf16[64,896]{1,0:T(8,128)(2,1)S(1)}, bf16[64,896]{1,0:T(8,128)(2,1)S(1)}, u32[]{:S(2)}, u32[]{:S(2)}) collective-permute-start(bf16[64,896]{1,0:T(8,128)(2,1)S(1)} %get-tuple-element.57), channel_id=1, source_target_pairs={{0,1},{1,0},{2,3},{3,2},{4,5},{5,4},{6,7},{7,6},{8,9},{9,8},{10,11... | collective-permute-start | bytes 344072 | tf_op jit(solution)/shard_map/ppermute | solution.py:306
  33.5 1.6 %collective-permute-start.19 = (bf16[592,128]{1,0:T(8,128)(2,1)S(1)}, bf16[592,128]{1,0:T(8,128)(2,1)S(1)}, u32[]{:S(2)}, u32[]{:S(2)}) collective-permute-start(bf16[592,128]{1,0:T(8,128)(2,1)S(1)} %collective-permute-done.15.second), channel_id=1, source_target_pairs={{0,1},{1,0},{2,3},{3,2},{4,5},{5,4},{6,7},{7,6},{8,9},{9,8},{10,11... | collective-permute-start | bytes 454664 | tf_op jit(solution)/shard_map/ppermute | solution.py:306
  33.7 1.5 %collective-permute-start.14 = (bf16[576,128]{1,0:T(8,128)(2,1)S(1)}, bf16[576,128]{1,0:T(8,128)(2,1)S(1)}, u32[]{:S(2)}, u32[]{:S(2)}) collective-permute-start(bf16[576,128]{1,0:T(8,128)(2,1)S(1)} %collective-permute-done.11.first), channel_id=1, source_target_pairs={{0,1},{1,0},{2,3},{3,2},{4,5},{5,4},{6,7},{7,6},{8,9},{9,8},{10,11... | collective-permute-start | bytes 442376 | tf_op jit(solution)/shard_map/ppermute | solution.py:306

commit v28 on v27

--- a/solution.py
+++ b/solution.py
@@ -103,6 +103,12 @@
     named = named.astype(F32).astype(BF16)
     whole[slabs * rows_here :, :] = named
     second[slabs * half :, :] = named
+
+
+def pad_kernel(first, out):
+    top = first.shape[0]
+    out[:top, :] = first[...]
+    out[top:, :] = jnp.zeros((out.shape[0] - top, 128), BF16)
 
 
 def from_slabs(ref, count):
@@ -333,7 +339,8 @@
     back = [other_core(part) for part in theirs[:-1]]
     last_first, theirs[-1] = together(last_first, theirs[-1])
     last_second, *back = together(last_second, *back, other_core(theirs[-1]))
-    last = [other_core(last_first), other_core(last_second)]
+    (padded,) = call(pad_kernel, [(last_second.shape, BF16)], [last_first])
+    last = [other_core(padded), other_core(last_second)]
     (total,) = call(
         join_kernel,
         [((rows_here, width + 128), F32)],

time: 36.6 us -> 36.4 us (level)
    pallas_call x5 -> x6, Pallas kernels: 3.82 us -> 3.84 us  [call(): pl.pallas_call(kernel, out_shape=[jax.ShapeDtypeStruct(shape, dtype) for...]
  transfers between devices with their start and end apart: 20 -> 20, of which waited for: 9 -> 9; matrix products, arithmetic and copies ran while one was open for 0% -> 0% of each run, Pallas kernels for 10% -> 11%
where the time goes in v28:
time: 36.4 us; the launch traced here: 36.2 us
  starting transfers between devices  25.7 us (71%)
  Pallas kernels  5.13 us (14%)
  waiting for transfers between devices  3.61 us (10%)
  local copies, waits for them, and re-layouts  1.64 us (5%)
    ppermute x7, starting transfers between devices, along(): return lax.ppermute(rows, ('blk', 'pair'), hops)  17.5 us
    ppermute x7, starting transfers between devices, across(): return lax.ppermute(rows, ('sub', 'pair'), [(0, 3), (1, 2), (2, 1), (3, 0)])  7.01 us
    pallas_call x6, Pallas kernels, call(): pl.pallas_call(kernel, out_shape=[jax.ShapeDtypeStruct(shape, dtype) for...  3.84 us
    ppermute x7, waiting for transfers between devices, along(): return lax.ppermute(rows, ('blk', 'pair'), hops)  1.82 us
    unnamed x6, local copies, waits for them, and re-layouts  1.64 us
    pallas_call x1, Pallas kernels, finish(): pl.pallas_call(last_kernel, out_shape=jax.ShapeDtypeStruct(shape, BF16),...  1.29 us
    ppermute x6, starting transfers between devices, other_core(): return lax.ppermute(rows, 'pair', [(0, 1), (1, 0)])  1.26 us
    ppermute x7, waiting for transfers between devices, across(): return lax.ppermute(rows, ('sub', 'pair'), [(0, 3), (1, 2), (2, 1), (3, 0)])  0.9 us
  transfers between devices with their start and end apart: 20, of which 9 were waited for; matrix products, arithmetic and copies ran while one was open for 0% of the time, Pallas kernels for 11%

profile of v28, /device:TPU:0, one launch (start us, length us, event | category | flops | bytes accessed | tf_op | source)
XLA Modules:
  0.0 36.2 jit_solution(10625982407691382122)
XLA Ops:
  0.0 0.0 copy-start
  0.0 1.0 %copy-done = bf16[192,768]{1,0:T(8,128)(2,1)S(1)} copy-done((bf16[192,768]{1,0:T(8,128)(2,1)S(1)}, bf16[192,768]{1,0:T(8,128)(2,1)}, u32[]{:S(2)}) %copy-start) | copy-done | bytes 294936
  1.0 0.0 copy-start.2
  1.0 2.4 %collective-permute-start.2 = (bf16[576,128]{1,0:T(8,128)(2,1)S(1)}, bf16[576,128]{1,0:T(8,128)(2,1)S(1)}, u32[]{:S(2)}, u32[]{:S(2)}) collective-permute-start(bf16[576,128]{1,0:T(8,128)(2,1)S(1)} %shard_map.38), channel_id=1, source_target_pairs={{0,3},{1,2},{2,1},{3,0},{4,7},{5,6},{6,5},{7,4},{8,11},{9,10},{10,... | collective-permute-start | bytes 442376 | tf_op jit(solution)/shard_map/ppermute | solution.py:309
  3.4 2.9 %collective-permute-start.1 = (bf16[576,128]{1,0:T(8,128)(2,1)S(1)}, bf16[576,128]{1,0:T(8,128)(2,1)S(1)}, u32[]{:S(2)}, u32[]{:S(2)}) collective-permute-start(bf16[576,128]{1,0:T(8,128)(2,1)S(1)} %shard_map.38), channel_id=1, source_target_pairs={{4,1},{5,0},{0,9},{1,8},{8,13},{9,12},{12,5},{13,4},{6,3},{7,2},{2... | collective-permute-start | bytes 442376 | tf_op jit(solution)/shard_map/ppermute | solution.py:306
  6.3 0.0 copy-start.1
  6.3 0.0 copy-done.2
  6.3 0.7 %copy-done.1 = s32[192,1]{0,1:T(1,128)S(1)} copy-done((s32[192,1]{0,1:T(1,128)S(1)}, s32[192,1]{0,1:T(1,128)}, u32[]{:S(2)}) %copy-start.1) | copy-done | bytes 792
  7.0 0.1 shard_map.37
  7.1 0.1 collective-permute-start.4
  7.2 1.8 %collective-permute-start.3 = (bf16[592,128]{1,0:T(8,128)(2,1)S(1)}, bf16[592,128]{1,0:T(8,128)(2,1)S(1)}, u32[]{:S(2)}, u32[]{:S(2)}) collective-permute-start(bf16[592,128]{1,0:T(8,128)(2,1)S(1)} %get-tuple-element.36), channel_id=1, source_target_pairs={{4,1},{5,0},{0,9},{1,8},{8,13},{9,12},{12,5},{13,4},{6,3},{7,2},{2... | collective-permute-start | bytes 454664 | tf_op jit(solution)/shard_map/ppermute | solution.py:306
  9.0 0.0 collective-permute-start
  9.0 0.0 collective-permute-done.2.refs_0_
  9.0 1.1 %collective-permute-done.1.refs_4_ = bf16[576,128]{1,0:T(8,128)(2,1)S(1)} collective-permute-done((bf16[576,128]{1,0:T(8,128)(2,1)S(1)}, bf16[576,128]{1,0:T(8,128)(2,1)S(1)}, u32[]{:S(2)}, u32[]{:S(2)}) %collective-permute-start.1) | collective-permute-done | bytes 147488 | tf_op jit(solution)/shard_map/ppermute | solution.py:306
  10.0 0.5 %collective-permute-start.6 = (bf16[576,128]{1,0:T(8,128)(2,1)S(1)}, bf16[576,128]{1,0:T(8,128)(2,1)S(1)}, u32[]{:S(2)}, u32[]{:S(2)}) collective-permute-start(bf16[576,128]{1,0:T(8,128)(2,1)S(1)} %collective-permute-done.1.refs_4_), channel_id=1, source_target_pairs={{0,3},{1,2},{2,1},{3,0},{4,7},{5,6},{6,5},{7,4},{8,11},{9,10},{10,... | collective-permute-start | bytes 442376 | tf_op jit(solution)/shard_map/ppermute | solution.py:309
  10.6 2.6 %collective-permute-start.5 = (bf16[576,128]{1,0:T(8,128)(2,1)S(1)}, bf16[576,128]{1,0:T(8,128)(2,1)S(1)}, u32[]{:S(2)}, u32[]{:S(2)}) collective-permute-start(bf16[576,128]{1,0:T(8,128)(2,1)S(1)} %collective-permute-done.1.refs_4_), channel_id=1, source_target_pairs={{4,1},{5,0},{0,9},{1,8},{8,13},{9,12},{12,5},{13,4},{6,3},{7,2},{2... | collective-permute-start | bytes 442376 | tf_op jit(solution)/shard_map/ppermute | solution.py:306
  13.2 0.2 collective-permute-done.4.refs_1_
  13.4 0.0 collective-permute-done.3.refs_5_
  13.4 1.5 %collective-permute-start.8 = (bf16[592,128]{1,0:T(8,128)(2,1)S(1)}, bf16[592,128]{1,0:T(8,128)(2,1)S(1)}, u32[]{:S(2)}, u32[]{:S(2)}) collective-permute-start(bf16[592,128]{1,0:T(8,128)(2,1)S(1)} %collective-permute-done.3.refs_5_), channel_id=1, source_target_pairs={{0,3},{1,2},{2,1},{3,0},{4,7},{5,6},{6,5},{7,4},{8,11},{9,10},{10,... | collective-permute-start | bytes 454664 | tf_op jit(solution)/shard_map/ppermute | solution.py:309
  14.9 1.3 %collective-permute-start.7 = (bf16[592,128]{1,0:T(8,128)(2,1)S(1)}, bf16[592,128]{1,0:T(8,128)(2,1)S(1)}, u32[]{:S(2)}, u32[]{:S(2)}) collective-permute-start(bf16[592,128]{1,0:T(8,128)(2,1)S(1)} %collective-permute-done.3.refs_5_), channel_id=1, source_target_pairs={{4,1},{5,0},{0,9},{1,8},{8,13},{9,12},{12,5},{13,4},{6,3},{7,2},{2... | collective-permute-start | bytes 454664 | tf_op jit(solution)/shard_map/ppermute | solution.py:306
  16.2 0.3 collective-permute-done.6.refs_2_
  16.5 0.3 collective-permute-done.5.refs_0_
  16.8 1.2 %collective-permute-start.10 = (bf16[576,128]{1,0:T(8,128)(2,1)S(1)}, bf16[576,128]{1,0:T(8,128)(2,1)S(1)}, u32[]{:S(2)}, u32[]{:S(2)}) collective-permute-start(bf16[576,128]{1,0:T(8,128)(2,1)S(1)} %collective-permute-done.5.refs_0_), channel_id=1, source_target_pairs={{0,3},{1,2},{2,1},{3,0},{4,7},{5,6},{6,5},{7,4},{8,11},{9,10},{10,... | collective-permute-start | bytes 442376 | tf_op jit(solution)/shard_map/ppermute | solution.py:309
  18.0 3.4 %collective-permute-start.9 = (bf16[576,128]{1,0:T(8,128)(2,1)S(1)}, bf16[576,128]{1,0:T(8,128)(2,1)S(1)}, u32[]{:S(2)}, u32[]{:S(2)}) collective-permute-start(bf16[576,128]{1,0:T(8,128)(2,1)S(1)} %collective-permute-done.5.refs_0_), channel_id=1, source_target_pairs={{4,1},{5,0},{0,9},{1,8},{8,13},{9,12},{12,5},{13,4},{6,3},{7,2},{2... | collective-permute-start | bytes 442376 | tf_op jit(solution)/shard_map/ppermute | solution.py:306
  21.3 0.0 collective-permute-done.8.refs_3_
  21.3 0.0 collective-permute-done.7.refs_1_
  21.3 0.0 collective-permute-start.12
  21.4 2.8 %collective-permute-start.13 = (bf16[592,128]{1,0:T(8,128)(2,1)S(1)}, bf16[592,128]{1,0:T(8,128)(2,1)S(1)}, u32[]{:S(2)}, u32[]{:S(2)}) collective-permute-start(bf16[592,128]{1,0:T(8,128)(2,1)S(1)} %collective-permute-done.7.refs_1_), channel_id=1, source_target_pairs={{4,1},{5,0},{0,9},{1,8},{8,13},{9,12},{12,5},{13,4},{6,3},{7,2},{2... | collective-permute-start | bytes 454664 | tf_op jit(solution)/shard_map/ppermute | solution.py:306
  24.2 0.0 collective-permute-done.other
  24.2 1.5 %shard_map.39 = (f32[192,896]{1,0:T(8,128)S(1)}, f32[192,896]{1,0:T(8,128)S(1)}, f32[384,128]{1,0:T(8,128)S(1)}) custom-call(bf16[1168,128]{1,0:T(8,128)(2,1)S(1)} %get-tuple-element.34.own, bf16[1168,128]{1,0:T(8,128)(2,1)S(1)} %collective-permute-done.other, bf16[576,128]{1,0:T(8,128)(2,1)S(1)} %collective-permute-done.2.refs_0_, ...), custom_call_target="tpu_custom_call" | custom-call | tf_op jit(solution)/shard_map/pallas_call | solution.py:248
  25.7 0.0 collective-permute-done.10.refs_2_
  25.7 0.0 collective-permute-done.9.refs_4_
  25.7 1.2 %collective-permute-start.11 = (bf16[576,128]{1,0:T(8,128)(2,1)S(1)}, bf16[576,128]{1,0:T(8,128)(2,1)S(1)}, u32[]{:S(2)}, u32[]{:S(2)}) collective-permute-start(bf16[576,128]{1,0:T(8,128)(2,1)S(1)} %collective-permute-done.9.refs_4_), channel_id=1, source_target_pairs={{0,3},{1,2},{2,1},{3,0},{4,7},{5,6},{6,5},{7,4},{8,11},{9,10},{10,... | collective-permute-start | bytes 442376 | tf_op jit(solution)/shard_map/ppermute | solution.py:309
  26.9 0.4 %collective-permute-done.12.refs_3_ = bf16[592,128]{1,0:T(8,128)(2,1)S(1)} collective-permute-done((bf16[592,128]{1,0:T(8,128)(2,1)S(1)}, bf16[592,128]{1,0:T(8,128)(2,1)S(1)}, u32[]{:S(2)}, u32[]{:S(2)}) %collective-permute-start.12) | collective-permute-done | bytes 151584 | tf_op jit(solution)/shard_map/ppermute | solution.py:309
  27.3 2.8 %collective-permute-start.15 = (bf16[592,128]{1,0:T(8,128)(2,1)S(1)}, bf16[592,128]{1,0:T(8,128)(2,1)S(1)}, u32[]{:S(2)}, u32[]{:S(2)}) collective-permute-start(bf16[592,128]{1,0:T(8,128)(2,1)S(1)} %collective-permute-done.12.refs_3_), channel_id=1, source_target_pairs={{4,1},{5,0},{0,9},{1,8},{8,13},{9,12},{12,5},{13,4},{6,3},{7,2},{2... | collective-permute-start | bytes 454664 | tf_op jit(solution)/shard_map/ppermute | solution.py:306
  30.1 0.0 collective-permute-done.13.refs_5_
  30.1 1.4 %shard_map.40 = (f32[192,896]{1,0:T(8,128)S(1)}, bf16[64,896]{1,0:T(8,128)(2,1)S(1)}, bf16[64,896]{1,0:T(8,128)(2,1)S(1)}, bf16[64,896]{1,0:T(8,128)(2,1)S(1)}) custom-call(bf16[1168,128]{1,0:T(8,128)(2,1)S(1)} %get-tuple-element.34.own, bf16[1168,128]{1,0:T(8,128)(2,1)S(1)} %collective-permute-done.other, ...), custom_call_target="tpu_custom_call", output_to_operand_aliasing={{0}: (9, {})} | custom-call | tf_op jit(solution)/shard_map/pallas_call | solution.py:248
  31.5 0.1 collective-permute-start.16
  31.6 0.5 %collective-permute-start.17 = (bf16[64,896]{1,0:T(8,128)(2,1)S(1)}, bf16[64,896]{1,0:T(8,128)(2,1)S(1)}, u32[]{:S(2)}, u32[]{:S(2)}) collective-permute-start(bf16[64,896]{1,0:T(8,128)(2,1)S(1)} %get-tuple-element.56), channel_id=1, source_target_pairs={{0,1},{1,0},{2,3},{3,2},{4,5},{5,4},{6,7},{7,6},{8,9},{9,8},{10,11... | collective-permute-start | bytes 344072 | tf_op jit(solution)/shard_map/ppermute | solution.py:312
  32.1 0.0 collective-permute-done.11.first
  32.1 0.1 collective-permute-start.18
  32.2 0.5 %collective-permute-start.14 = (bf16[592,128]{1,0:T(8,128)(2,1)S(1)}, bf16[592,128]{1,0:T(8,128)(2,1)S(1)}, u32[]{:S(2)}, u32[]{:S(2)}) collective-permute-start(bf16[592,128]{1,0:T(8,128)(2,1)S(1)} %shard_map.41), channel_id=1, source_target_pairs={{0,1},{1,0},{2,3},{3,2},{4,5},{5,4},{6,7},{7,6},{8,9},{9,8},{10,11... | collective-permute-start | bytes 454664 | tf_op jit(solution)/shard_map/ppermute | solution.py:312
  32.7 0.2 collective-permute-done.16.refs_0_
  32.9 0.2 collective-permute-done.17.refs_1_
  33.1 0.5 %collective-permute-done.15.second = bf16[592,128]{1,0:T(8,128)(2,1)S(1)} collective-permute-done((bf16[592,128]{1,0:T(8,128)(2,1)S(1)}, bf16[592,128]{1,0:T(8,128)(2,1)S(1)}, u32[]{:S(2)}, u32[]{:S(2)}) %collective-permute-start.15) | collective-permute-done | bytes 151584 | tf_op jit(solution)/shard_map/ppermute | solution.py:306
  33.5 0.0 collective-permute-done.18.refs_2_
  33.5 0.1 collective-permute-start.19
  33.7 0.7 %shard_map.42.total = f32[192,896]{1,0:T(8,128)S(1)} custom-call(bf16[1168,128]{1,0:T(8,128)(2,1)S(1)} %get-tuple-element.34.own, f32[384,128]{1,0:T(8,128)S(1)} %get-tuple-element.43.info, bf16[576,128]{1,0:T(8,128)(2,1)S(1)} %collective-permute-done.11.first, bf16[592,128]{1,0:T(8,128)(2,1)S(1)} %collective-permute-done.15.second, ...), custom_call_target="tpu_custom_call", output_to_operand_aliasing={{}: (4, {})} | custom-call | tf_op jit(solution)/shard_map/pallas_call | solution.py:248
  34.4 0.0 collective-permute-done.14.first
  34.4 0.5 %collective-permute-done.19.second = bf16[592,128]{1,0:T(8,128)(2,1)S(1)} collective-permute-done((bf16[592,128]{1,0:T(8,128)(2,1)S(1)}, bf16[592,128]{1,0:T(8,128)(2,1)S(1)}, u32[]{:S(2)}, u32[]{:S(2)}) %collective-permute-start.19) | collective-permute-done | bytes 151584 | tf_op jit(solution)/shard_map/ppermute | solution.py:312
  34.9 1.3 %shard_map.43 = bf16[192,768]{1,0:T(8,128)(2,1)} custom-call(bf16[1168,128]{1,0:T(8,128)(2,1)S(1)} %get-tuple-element.34.own, f32[384,128]{1,0:T(8,128)S(1)} %get-tuple-element.43.info, bf16[592,128]{1,0:T(8,128)(2,1)S(1)} %collective-permute-done.14.first, bf16[592,128]{1,0:T(8,128)(2,1)S(1)} %collective-permute-done.19.second, f32[192,896]{1,0:T(8,128)S(1)} %shard_map.42.total), custom_call_target="tpu_custom_call" | custom-call | tf_op jit(solution)/shard_map/pallas_call | solution.py:274
  (2 shorter events, 0.0 us)
Async XLA Ops:
  0.0 1.0 %copy-start = (bf16[192,768]{1,0:T(8,128)(2,1)S(1)}, bf16[192,768]{1,0:T(8,128)(2,1)}, u32[]{:S(2)}) copy-start(bf16[192,768]{1,0:T(8,128)(2,1)} %rows.3) | copy-start | bytes 884740
  1.0 5.3 %copy-start.2 = (s32[192]{0:T(256)S(1)}, s32[192]{0:T(256)}, u32[]{:S(2)}) copy-start(s32[192]{0:T(256)} %param.5) | copy-start | bytes 2308
  1.0 8.0 %collective-permute-start.2 = (bf16[576,128]{1,0:T(8,128)(2,1)S(1)}, bf16[576,128]{1,0:T(8,128)(2,1)S(1)}, u32[]{:S(2)}, u32[]{:S(2)}) collective-permute-start(bf16[576,128]{1,0:T(8,128)(2,1)S(1)} %shard_map.38), channel_id=1, source_target_pairs={{0,3},{1,2},{2,1},{3,0},{4,7},{5,6},{6,5},{7,4},{8,11},{9,10},{10,... | collective-permute-start | bytes 442376 | tf_op jit(solution)/shard_map/ppermute | solution.py:309
  3.4 6.6 %collective-permute-start.1 = (bf16[576,128]{1,0:T(8,128)(2,1)S(1)}, bf16[576,128]{1,0:T(8,128)(2,1)S(1)}, u32[]{:S(2)}, u32[]{:S(2)}) collective-permute-start(bf16[576,128]{1,0:T(8,128)(2,1)S(1)} %shard_map.38), channel_id=1, source_target_pairs={{4,1},{5,0},{0,9},{1,8},{8,13},{9,12},{12,5},{13,4},{6,3},{7,2},{2... | collective-permute-start | bytes 442376 | tf_op jit(solution)/shard_map/ppermute | solution.py:306
  6.3 0.7 %copy-start.1 = (s32[192,1]{0,1:T(1,128)S(1)}, s32[192,1]{0,1:T(1,128)}, u32[]{:S(2)}) copy-start(s32[192,1]{0,1:T(1,128)} %param.4) | copy-start | bytes 2308
  7.1 6.3 %collective-permute-start.4 = (bf16[592,128]{1,0:T(8,128)(2,1)S(1)}, bf16[592,128]{1,0:T(8,128)(2,1)S(1)}, u32[]{:S(2)}, u32[]{:S(2)}) collective-permute-start(bf16[592,128]{1,0:T(8,128)(2,1)S(1)} %get-tuple-element.36), channel_id=1, source_target_pairs={{0,3},{1,2},{2,1},{3,0},{4,7},{5,6},{6,5},{7,4},{8,11},{9,10},{10,... | collective-permute-start | bytes 454664 | tf_op jit(solution)/shard_map/ppermute | solution.py:309
  7.2 6.2 %collective-permute-start.3 = (bf16[592,128]{1,0:T(8,128)(2,1)S(1)}, bf16[592,128]{1,0:T(8,128)(2,1)S(1)}, u32[]{:S(2)}, u32[]{:S(2)}) collective-permute-start(bf16[592,128]{1,0:T(8,128)(2,1)S(1)} %get-tuple-element.36), channel_id=1, source_target_pairs={{4,1},{5,0},{0,9},{1,8},{8,13},{9,12},{12,5},{13,4},{6,3},{7,2},{2... | collective-permute-start | bytes 454664 | tf_op jit(solution)/shard_map/ppermute | solution.py:306
  9.0 15.2 %collective-permute-start = (bf16[1168,128]{1,0:T(8,128)(2,1)S(1)}, bf16[1168,128]{1,0:T(8,128)(2,1)S(1)}, u32[]{:S(2)}, u32[]{:S(2)}) collective-permute-start(bf16[1168,128]{1,0:T(8,128)(2,1)S(1)} %get-tuple-element.34.own), channel_id=1, source_target_pairs={{0,1},{1,0},{2,3},{3,2},{4,5},{5,4},{6,7},{7,6},{8,9},{9,8},{10,11... | collective-permute-start | bytes 897032 | tf_op jit(solution)/shard_map/ppermute | solution.py:312
  10.0 6.5 %collective-permute-start.6 = (bf16[576,128]{1,0:T(8,128)(2,1)S(1)}, bf16[576,128]{1,0:T(8,128)(2,1)S(1)}, u32[]{:S(2)}, u32[]{:S(2)}) collective-permute-start(bf16[576,128]{1,0:T(8,128)(2,1)S(1)} %collective-permute-done.1.refs_4_), channel_id=1, source_target_pairs={{0,3},{1,2},{2,1},{3,0},{4,7},{5,6},{6,5},{7,4},{8,11},{9,10},{10,... | collective-permute-start | bytes 442376 | tf_op jit(solution)/shard_map/ppermute | solution.py:309
  10.6 6.2 %collective-permute-start.5 = (bf16[576,128]{1,0:T(8,128)(2,1)S(1)}, bf16[576,128]{1,0:T(8,128)(2,1)S(1)}, u32[]{:S(2)}, u32[]{:S(2)}) collective-permute-start(bf16[576,128]{1,0:T(8,128)(2,1)S(1)} %collective-permute-done.1.refs_4_), channel_id=1, source_target_pairs={{4,1},{5,0},{0,9},{1,8},{8,13},{9,12},{12,5},{13,4},{6,3},{7,2},{2... | collective-permute-start | bytes 442376 | tf_op jit(solution)/shard_map/ppermute | solution.py:306
  13.4 8.0 %collective-permute-start.8 = (bf16[592,128]{1,0:T(8,128)(2,1)S(1)}, bf16[592,128]{1,0:T(8,128)(2,1)S(1)}, u32[]{:S(2)}, u32[]{:S(2)}) collective-permute-start(bf16[592,128]{1,0:T(8,128)(2,1)S(1)} %collective-permute-done.3.refs_5_), channel_id=1, source_target_pairs={{0,3},{1,2},{2,1},{3,0},{4,7},{5,6},{6,5},{7,4},{8,11},{9,10},{10,... | collective-permute-start | bytes 454664 | tf_op jit(solution)/shard_map/ppermute | solution.py:309
  14.9 6.4 %collective-permute-start.7 = (bf16[592,128]{1,0:T(8,128)(2,1)S(1)}, bf16[592,128]{1,0:T(8,128)(2,1)S(1)}, u32[]{:S(2)}, u32[]{:S(2)}) collective-permute-start(bf16[592,128]{1,0:T(8,128)(2,1)S(1)} %collective-permute-done.3.refs_5_), channel_id=1, source_target_pairs={{4,1},{5,0},{0,9},{1,8},{8,13},{9,12},{12,5},{13,4},{6,3},{7,2},{2... | collective-permute-start | bytes 454664 | tf_op jit(solution)/shard_map/ppermute | solution.py:306
  16.8 8.9 %collective-permute-start.10 = (bf16[576,128]{1,0:T(8,128)(2,1)S(1)}, bf16[576,128]{1,0:T(8,128)(2,1)S(1)}, u32[]{:S(2)}, u32[]{:S(2)}) collective-permute-start(bf16[576,128]{1,0:T(8,128)(2,1)S(1)} %collective-permute-done.5.refs_0_), channel_id=1, source_target_pairs={{0,3},{1,2},{2,1},{3,0},{4,7},{5,6},{6,5},{7,4},{8,11},{9,10},{10,... | collective-permute-start | bytes 442376 | tf_op jit(solution)/shard_map/ppermute | solution.py:309
  18.0 7.8 %collective-permute-start.9 = (bf16[576,128]{1,0:T(8,128)(2,1)S(1)}, bf16[576,128]{1,0:T(8,128)(2,1)S(1)}, u32[]{:S(2)}, u32[]{:S(2)}) collective-permute-start(bf16[576,128]{1,0:T(8,128)(2,1)S(1)} %collective-permute-done.5.refs_0_), channel_id=1, source_target_pairs={{4,1},{5,0},{0,9},{1,8},{8,13},{9,12},{12,5},{13,4},{6,3},{7,2},{2... | collective-permute-start | bytes 442376 | tf_op jit(solution)/shard_map/ppermute | solution.py:306
  21.3 6.0 %collective-permute-start.12 = (bf16[592,128]{1,0:T(8,128)(2,1)S(1)}, bf16[592,128]{1,0:T(8,128)(2,1)S(1)}, u32[]{:S(2)}, u32[]{:S(2)}) collective-permute-start(bf16[592,128]{1,0:T(8,128)(2,1)S(1)} %collective-permute-done.7.refs_1_), channel_id=1, source_target_pairs={{0,3},{1,2},{2,1},{3,0},{4,7},{5,6},{6,5},{7,4},{8,11},{9,10},{10,... | collective-permute-start | bytes 454664 | tf_op jit(solution)/shard_map/ppermute | solution.py:309
  21.4 8.7 %collective-permute-start.13 = (bf16[592,128]{1,0:T(8,128)(2,1)S(1)}, bf16[592,128]{1,0:T(8,128)(2,1)S(1)}, u32[]{:S(2)}, u32[]{:S(2)}) collective-permute-start(bf16[592,128]{1,0:T(8,128)(2,1)S(1)} %collective-permute-done.7.refs_1_), channel_id=1, source_target_pairs={{4,1},{5,0},{0,9},{1,8},{8,13},{9,12},{12,5},{13,4},{6,3},{7,2},{2... | collective-permute-start | bytes 454664 | tf_op jit(solution)/shard_map/ppermute | solution.py:306
  25.7 6.4 %collective-permute-start.11 = (bf16[576,128]{1,0:T(8,128)(2,1)S(1)}, bf16[576,128]{1,0:T(8,128)(2,1)S(1)}, u32[]{:S(2)}, u32[]{:S(2)}) collective-permute-start(bf16[576,128]{1,0:T(8,128)(2,1)S(1)} %collective-permute-done.9.refs_4_), channel_id=1, source_target_pairs={{0,3},{1,2},{2,1},{3,0},{4,7},{5,6},{6,5},{7,4},{8,11},{9,10},{10,... | collective-permute-start | bytes 442376 | tf_op jit(solution)/shard_map/ppermute | solution.py:309
  27.3 6.2 %collective-permute-start.15 = (bf16[592,128]{1,0:T(8,128)(2,1)S(1)}, bf16[592,128]{1,0:T(8,128)(2,1)S(1)}, u32[]{:S(2)}, u32[]{:S(2)}) collective-permute-start(bf16[592,128]{1,0:T(8,128)(2,1)S(1)} %collective-permute-done.12.refs_3_), channel_id=1, source_target_pairs={{4,1},{5,0},{0,9},{1,8},{8,13},{9,12},{12,5},{13,4},{6,3},{7,2},{2... | collective-permute-start | bytes 454664 | tf_op jit(solution)/shard_map/ppermute | solution.py:306
  31.5 1.4 %collective-permute-start.16 = (bf16[64,896]{1,0:T(8,128)(2,1)S(1)}, bf16[64,896]{1,0:T(8,128)(2,1)S(1)}, u32[]{:S(2)}, u32[]{:S(2)}) collective-permute-start(bf16[64,896]{1,0:T(8,128)(2,1)S(1)} %get-tuple-element.55), channel_id=1, source_target_pairs={{0,1},{1,0},{2,3},{3,2},{4,5},{5,4},{6,7},{7,6},{8,9},{9,8},{10,11... | collective-permute-start | bytes 344072 | tf_op jit(solution)/shard_map/ppermute | solution.py:312
  31.6 1.5 %collective-permute-start.17 = (bf16[64,896]{1,0:T(8,128)(2,1)S(1)}, bf16[64,896]{1,0:T(8,128)(2,1)S(1)}, u32[]{:S(2)}, u32[]{:S(2)}) collective-permute-start(bf16[64,896]{1,0:T(8,128)(2,1)S(1)} %get-tuple-element.56), channel_id=1, source_target_pairs={{0,1},{1,0},{2,3},{3,2},{4,5},{5,4},{6,7},{7,6},{8,9},{9,8},{10,11... | collective-permute-start | bytes 344072 | tf_op jit(solution)/shard_map/ppermute | solution.py:312
  32.1 1.4 %collective-permute-start.18 = (bf16[64,896]{1,0:T(8,128)(2,1)S(1)}, bf16[64,896]{1,0:T(8,128)(2,1)S(1)}, u32[]{:S(2)}, u32[]{:S(2)}) collective-permute-start(bf16[64,896]{1,0:T(8,128)(2,1)S(1)} %get-tuple-element.57), channel_id=1, source_target_pairs={{0,1},{1,0},{2,3},{3,2},{4,5},{5,4},{6,7},{7,6},{8,9},{9,8},{10,11... | collective-permute-start | bytes 344072 | tf_op jit(solution)/shard_map/ppermute | solution.py:312
  32.2 2.2 %collective-permute-start.14 = (bf16[592,128]{1,0:T(8,128)(2,1)S(1)}, bf16[592,128]{1,0:T(8,128)(2,1)S(1)}, u32[]{:S(2)}, u32[]{:S(2)}) collective-permute-start(bf16[592,128]{1,0:T(8,128)(2,1)S(1)} %shard_map.41), channel_id=1, source_target_pairs={{0,1},{1,0},{2,3},{3,2},{4,5},{5,4},{6,7},{7,6},{8,9},{9,8},{10,11... | collective-permute-start | bytes 454664 | tf_op jit(solution)/shard_map/ppermute | solution.py:312
  33.5 1.4 %collective-permute-start.19 = (bf16[592,128]{1,0:T(8,128)(2,1)S(1)}, bf16[592,128]{1,0:T(8,128)(2,1)S(1)}, u32[]{:S(2)}, u32[]{:S(2)}) collective-permute-start(bf16[592,128]{1,0:T(8,128)(2,1)S(1)} %collective-permute-done.15.second), channel_id=1, source_target_pairs={{0,1},{1,0},{2,3},{3,2},{4,5},{5,4},{6,7},{7,6},{8,9},{9,8},{10,11... | collective-permute-start | bytes 454664 | tf_op jit(solution)/shard_map/ppermute | solution.py:312

commit v29 on v28

--- a/solution.py
+++ b/solution.py
@@ -281,8 +281,8 @@
     )(*args)
 
 
-def folded_ring(size):
-    return list(range(0, size, 2)) + list(range(1, size, 2))[::-1]
+def ring(size):
+    return list(range(size))[::-1]
 
 
 def together(*arrays):
@@ -294,7 +294,7 @@
     half = rows_here // 2
     slabs = width // 128
     n_blk = lax.axis_size("blk")
-    order = folded_ring(n_blk)
+    order = ring(n_blk)
     line = (1, rows_here)
 
     def along(rows):

time: 36.4 us -> 40.2 us (1.10)
  waiting for transfers between devices: 3.61 us -> 6.75 us
  starting transfers between devices: 25.7 us -> 26.5 us
    ppermute x7, waiting for transfers between devices: 1.82 us -> 5.28 us  [along(): return lax.ppermute(rows, ('blk', 'pair'), hops)]
    ppermute x7, starting transfers between devices: 17.5 us -> 18.5 us  [along(): return lax.ppermute(rows, ('blk', 'pair'), hops)]
    ppermute x7, waiting for transfers between devices: 0.9 us -> 0.21 us  [across(): return lax.ppermute(rows, ('sub', 'pair'), [(0, 3), (1, 2), (2, 1), (3, 0)])]
  transfers between devices with their start and end apart: 20 -> 20, of which waited for: 9 -> 7; matrix products, arithmetic and copies ran while one was open for 0% -> 0% of each run, Pallas kernels for 11% -> 10%
where the time goes in v29:
time: 40.2 us; the launch traced here: 40.1 us
  starting transfers between devices  26.5 us (66%)
  waiting for transfers between devices  6.75 us (17%)
  Pallas kernels  5.14 us (13%)
  local copies, waits for them, and re-layouts  1.64 us (4%)
    ppermute x7, starting transfers between devices, along(): return lax.ppermute(rows, ('blk', 'pair'), hops)  18.5 us
    ppermute x7, starting transfers between devices, across(): return lax.ppermute(rows, ('sub', 'pair'), [(0, 3), (1, 2), (2, 1), (3, 0)])  6.8 us
    ppermute x7, waiting for transfers between devices, along(): return lax.ppermute(rows, ('blk', 'pair'), hops)  5.28 us
    pallas_call x6, Pallas kernels, call(): pl.pallas_call(kernel, out_shape=[jax.ShapeDtypeStruct(shape, dtype) for...  3.84 us
    unnamed x6, local copies, waits for them, and re-layouts  1.64 us
    pallas_call x1, Pallas kernels, finish(): pl.pallas_call(last_kernel, out_shape=jax.ShapeDtypeStruct(shape, BF16),...  1.29 us
    ppermute x6, waiting for transfers between devices, other_core(): return lax.ppermute(rows, 'pair', [(0, 1), (1, 0)])  1.27 us
    ppermute x6, starting transfers between devices, other_core(): return lax.ppermute(rows, 'pair', [(0, 1), (1, 0)])  1.21 us
  transfers between devices with their start and end apart: 20, of which 7 were waited for; matrix products, arithmetic and copies ran while one was open for 0% of the time, Pallas kernels for 10%

profile of v29, /device:TPU:0, one launch (start us, length us, event | category | flops | bytes accessed | tf_op | source)
XLA Modules:
  0.0 40.1 jit_solution(6494922055374659174)
XLA Ops:
  0.0 0.0 copy-start
  0.0 1.0 %copy-done = bf16[192,768]{1,0:T(8,128)(2,1)S(1)} copy-done((bf16[192,768]{1,0:T(8,128)(2,1)S(1)}, bf16[192,768]{1,0:T(8,128)(2,1)}, u32[]{:S(2)}) %copy-start) | copy-done | bytes 294936
  1.0 0.0 copy-start.2
  1.0 2.4 %collective-permute-start.2 = (bf16[576,128]{1,0:T(8,128)(2,1)S(1)}, bf16[576,128]{1,0:T(8,128)(2,1)S(1)}, u32[]{:S(2)}, u32[]{:S(2)}) collective-permute-start(bf16[576,128]{1,0:T(8,128)(2,1)S(1)} %shard_map.38), channel_id=1, source_target_pairs={{0,3},{1,2},{2,1},{3,0},{4,7},{5,6},{6,5},{7,4},{8,11},{9,10},{10,... | collective-permute-start | bytes 442376 | tf_op jit(solution)/shard_map/ppermute | solution.py:309
  3.4 3.9 %collective-permute-start.1 = (bf16[576,128]{1,0:T(8,128)(2,1)S(1)}, bf16[576,128]{1,0:T(8,128)(2,1)S(1)}, u32[]{:S(2)}, u32[]{:S(2)}) collective-permute-start(bf16[576,128]{1,0:T(8,128)(2,1)S(1)} %shard_map.38), channel_id=1, source_target_pairs={{0,13},{1,12},{12,9},{13,8},{8,5},{9,4},{4,1},{5,0},{2,15},{3,14},... | collective-permute-start | bytes 442376 | tf_op jit(solution)/shard_map/ppermute | solution.py:306
  7.3 0.0 copy-start.1
  7.3 0.0 copy-done.2
  7.3 0.7 %copy-done.1 = s32[192,1]{0,1:T(1,128)S(1)} copy-done((s32[192,1]{0,1:T(1,128)S(1)}, s32[192,1]{0,1:T(1,128)}, u32[]{:S(2)}) %copy-start.1) | copy-done | bytes 792
  8.0 0.1 shard_map.37
  8.1 0.1 collective-permute-start.4
  8.2 0.6 %collective-permute-start.3 = (bf16[592,128]{1,0:T(8,128)(2,1)S(1)}, bf16[592,128]{1,0:T(8,128)(2,1)S(1)}, u32[]{:S(2)}, u32[]{:S(2)}) collective-permute-start(bf16[592,128]{1,0:T(8,128)(2,1)S(1)} %get-tuple-element.36), channel_id=1, source_target_pairs={{0,13},{1,12},{12,9},{13,8},{8,5},{9,4},{4,1},{5,0},{2,15},{3,14},... | collective-permute-start | bytes 454664 | tf_op jit(solution)/shard_map/ppermute | solution.py:306
  8.8 0.0 collective-permute-start
  8.9 0.0 collective-permute-done.2.refs_0_
  8.9 2.7 %collective-permute-done.1.refs_4_ = bf16[576,128]{1,0:T(8,128)(2,1)S(1)} collective-permute-done((bf16[576,128]{1,0:T(8,128)(2,1)S(1)}, bf16[576,128]{1,0:T(8,128)(2,1)S(1)}, u32[]{:S(2)}, u32[]{:S(2)}) %collective-permute-start.1) | collective-permute-done | bytes 147488 | tf_op jit(solution)/shard_map/ppermute | solution.py:306
  11.5 0.0 collective-permute-start.6
  11.5 4.0 %collective-permute-start.5 = (bf16[576,128]{1,0:T(8,128)(2,1)S(1)}, bf16[576,128]{1,0:T(8,128)(2,1)S(1)}, u32[]{:S(2)}, u32[]{:S(2)}) collective-permute-start(bf16[576,128]{1,0:T(8,128)(2,1)S(1)} %collective-permute-done.1.refs_4_), channel_id=1, source_target_pairs={{0,13},{1,12},{12,9},{13,8},{8,5},{9,4},{4,1},{5,0},{2,15},{3,14},... | collective-permute-start | bytes 442376 | tf_op jit(solution)/shard_map/ppermute | solution.py:306
  15.5 0.0 collective-permute-done.4.refs_1_
  15.5 0.0 collective-permute-done.3.refs_5_
  15.5 1.7 %collective-permute-start.8 = (bf16[592,128]{1,0:T(8,128)(2,1)S(1)}, bf16[592,128]{1,0:T(8,128)(2,1)S(1)}, u32[]{:S(2)}, u32[]{:S(2)}) collective-permute-start(bf16[592,128]{1,0:T(8,128)(2,1)S(1)} %collective-permute-done.3.refs_5_), channel_id=1, source_target_pairs={{0,3},{1,2},{2,1},{3,0},{4,7},{5,6},{6,5},{7,4},{8,11},{9,10},{10,... | collective-permute-start | bytes 454664 | tf_op jit(solution)/shard_map/ppermute | solution.py:309
  17.3 0.7 %collective-permute-start.7 = (bf16[592,128]{1,0:T(8,128)(2,1)S(1)}, bf16[592,128]{1,0:T(8,128)(2,1)S(1)}, u32[]{:S(2)}, u32[]{:S(2)}) collective-permute-start(bf16[592,128]{1,0:T(8,128)(2,1)S(1)} %collective-permute-done.3.refs_5_), channel_id=1, source_target_pairs={{0,13},{1,12},{12,9},{13,8},{8,5},{9,4},{4,1},{5,0},{2,15},{3,14},... | collective-permute-start | bytes 454664 | tf_op jit(solution)/shard_map/ppermute | solution.py:306
  18.0 0.0 collective-permute-done.6.refs_2_
  18.0 1.8 %collective-permute-done.5.refs_0_ = bf16[576,128]{1,0:T(8,128)(2,1)S(1)} collective-permute-done((bf16[576,128]{1,0:T(8,128)(2,1)S(1)}, bf16[576,128]{1,0:T(8,128)(2,1)S(1)}, u32[]{:S(2)}, u32[]{:S(2)}) %collective-permute-start.5) | collective-permute-done | bytes 147488 | tf_op jit(solution)/shard_map/ppermute | solution.py:306
  19.8 0.1 collective-permute-start.10
  19.9 4.3 %collective-permute-start.9 = (bf16[576,128]{1,0:T(8,128)(2,1)S(1)}, bf16[576,128]{1,0:T(8,128)(2,1)S(1)}, u32[]{:S(2)}, u32[]{:S(2)}) collective-permute-start(bf16[576,128]{1,0:T(8,128)(2,1)S(1)} %collective-permute-done.5.refs_0_), channel_id=1, source_target_pairs={{0,13},{1,12},{12,9},{13,8},{8,5},{9,4},{4,1},{5,0},{2,15},{3,14},... | collective-permute-start | bytes 442376 | tf_op jit(solution)/shard_map/ppermute | solution.py:306
  24.2 0.0 collective-permute-done.8.refs_3_
  24.2 0.0 collective-permute-done.7.refs_1_
  24.2 1.4 %collective-permute-start.12 = (bf16[592,128]{1,0:T(8,128)(2,1)S(1)}, bf16[592,128]{1,0:T(8,128)(2,1)S(1)}, u32[]{:S(2)}, u32[]{:S(2)}) collective-permute-start(bf16[592,128]{1,0:T(8,128)(2,1)S(1)} %collective-permute-done.7.refs_1_), channel_id=1, source_target_pairs={{0,3},{1,2},{2,1},{3,0},{4,7},{5,6},{6,5},{7,4},{8,11},{9,10},{10,... | collective-permute-start | bytes 454664 | tf_op jit(solution)/shard_map/ppermute | solution.py:309
  25.5 1.9 %collective-permute-start.13 = (bf16[592,128]{1,0:T(8,128)(2,1)S(1)}, bf16[592,128]{1,0:T(8,128)(2,1)S(1)}, u32[]{:S(2)}, u32[]{:S(2)}) collective-permute-start(bf16[592,128]{1,0:T(8,128)(2,1)S(1)} %collective-permute-done.7.refs_1_), channel_id=1, source_target_pairs={{0,13},{1,12},{12,9},{13,8},{8,5},{9,4},{4,1},{5,0},{2,15},{3,14},... | collective-permute-start | bytes 454664 | tf_op jit(solution)/shard_map/ppermute | solution.py:306
  27.4 0.0 collective-permute-done.other
  27.4 1.5 %shard_map.39 = (f32[192,896]{1,0:T(8,128)S(1)}, f32[192,896]{1,0:T(8,128)S(1)}, f32[384,128]{1,0:T(8,128)S(1)}) custom-call(bf16[1168,128]{1,0:T(8,128)(2,1)S(1)} %get-tuple-element.34.own, bf16[1168,128]{1,0:T(8,128)(2,1)S(1)} %collective-permute-done.other, bf16[576,128]{1,0:T(8,128)(2,1)S(1)} %collective-permute-done.2.refs_0_, ...), custom_call_target="tpu_custom_call" | custom-call | tf_op jit(solution)/shard_map/pallas_call | solution.py:248
  29.0 0.0 collective-permute-done.10.refs_2_
  29.0 0.0 collective-permute-done.9.refs_4_
  29.0 1.0 %collective-permute-start.11 = (bf16[576,128]{1,0:T(8,128)(2,1)S(1)}, bf16[576,128]{1,0:T(8,128)(2,1)S(1)}, u32[]{:S(2)}, u32[]{:S(2)}) collective-permute-start(bf16[576,128]{1,0:T(8,128)(2,1)S(1)} %collective-permute-done.9.refs_4_), channel_id=1, source_target_pairs={{0,3},{1,2},{2,1},{3,0},{4,7},{5,6},{6,5},{7,4},{8,11},{9,10},{10,... | collective-permute-start | bytes 442376 | tf_op jit(solution)/shard_map/ppermute | solution.py:309
  30.0 0.2 collective-permute-done.12.refs_3_
  30.2 3.1 %collective-permute-start.15 = (bf16[592,128]{1,0:T(8,128)(2,1)S(1)}, bf16[592,128]{1,0:T(8,128)(2,1)S(1)}, u32[]{:S(2)}, u32[]{:S(2)}) collective-permute-start(bf16[592,128]{1,0:T(8,128)(2,1)S(1)} %collective-permute-done.12.refs_3_), channel_id=1, source_target_pairs={{0,13},{1,12},{12,9},{13,8},{8,5},{9,4},{4,1},{5,0},{2,15},{3,14},... | collective-permute-start | bytes 454664 | tf_op jit(solution)/shard_map/ppermute | solution.py:306
  33.3 0.0 collective-permute-done.13.refs_5_
  33.3 1.4 %shard_map.40 = (f32[192,896]{1,0:T(8,128)S(1)}, bf16[64,896]{1,0:T(8,128)(2,1)S(1)}, bf16[64,896]{1,0:T(8,128)(2,1)S(1)}, bf16[64,896]{1,0:T(8,128)(2,1)S(1)}) custom-call(bf16[1168,128]{1,0:T(8,128)(2,1)S(1)} %get-tuple-element.34.own, bf16[1168,128]{1,0:T(8,128)(2,1)S(1)} %collective-permute-done.other, ...), custom_call_target="tpu_custom_call", output_to_operand_aliasing={{0}: (9, {})} | custom-call | tf_op jit(solution)/shard_map/pallas_call | solution.py:248
  34.7 0.5 %collective-permute-start.16 = (bf16[64,896]{1,0:T(8,128)(2,1)S(1)}, bf16[64,896]{1,0:T(8,128)(2,1)S(1)}, u32[]{:S(2)}, u32[]{:S(2)}) collective-permute-start(bf16[64,896]{1,0:T(8,128)(2,1)S(1)} %get-tuple-element.55), channel_id=1, source_target_pairs={{0,1},{1,0},{2,3},{3,2},{4,5},{5,4},{6,7},{7,6},{8,9},{9,8},{10,11... | collective-permute-start | bytes 344072 | tf_op jit(solution)/shard_map/ppermute | solution.py:312
  35.3 0.1 collective-permute-start.17
  35.4 0.0 collective-permute-done.11.first
  35.4 0.4 %collective-permute-start.18 = (bf16[64,896]{1,0:T(8,128)(2,1)S(1)}, bf16[64,896]{1,0:T(8,128)(2,1)S(1)}, u32[]{:S(2)}, u32[]{:S(2)}) collective-permute-start(bf16[64,896]{1,0:T(8,128)(2,1)S(1)} %get-tuple-element.57), channel_id=1, source_target_pairs={{0,1},{1,0},{2,3},{3,2},{4,5},{5,4},{6,7},{7,6},{8,9},{9,8},{10,11... | collective-permute-start | bytes 344072 | tf_op jit(solution)/shard_map/ppermute | solution.py:312
  35.8 0.1 collective-permute-start.14
  36.0 0.3 collective-permute-done.16.refs_0_
  36.3 0.4 collective-permute-done.17.refs_1_
  36.6 0.8 %collective-permute-done.15.second = bf16[592,128]{1,0:T(8,128)(2,1)S(1)} collective-permute-done((bf16[592,128]{1,0:T(8,128)(2,1)S(1)}, bf16[592,128]{1,0:T(8,128)(2,1)S(1)}, u32[]{:S(2)}, u32[]{:S(2)}) %collective-permute-start.15) | collective-permute-done | bytes 151584 | tf_op jit(solution)/shard_map/ppermute | solution.py:306
  37.4 0.0 collective-permute-done.18.refs_2_
  37.4 0.0 collective-permute-start.19
  37.4 0.8 %shard_map.42.total = f32[192,896]{1,0:T(8,128)S(1)} custom-call(bf16[1168,128]{1,0:T(8,128)(2,1)S(1)} %get-tuple-element.34.own, f32[384,128]{1,0:T(8,128)S(1)} %get-tuple-element.43.info, bf16[576,128]{1,0:T(8,128)(2,1)S(1)} %collective-permute-done.11.first, bf16[592,128]{1,0:T(8,128)(2,1)S(1)} %collective-permute-done.15.second, ...), custom_call_target="tpu_custom_call", output_to_operand_aliasing={{}: (4, {})} | custom-call | tf_op jit(solution)/shard_map/pallas_call | solution.py:248
  38.2 0.0 collective-permute-done.14.first
  38.2 0.6 %collective-permute-done.19.second = bf16[592,128]{1,0:T(8,128)(2,1)S(1)} collective-permute-done((bf16[592,128]{1,0:T(8,128)(2,1)S(1)}, bf16[592,128]{1,0:T(8,128)(2,1)S(1)}, u32[]{:S(2)}, u32[]{:S(2)}) %collective-permute-start.19) | collective-permute-done | bytes 151584 | tf_op jit(solution)/shard_map/ppermute | solution.py:312
  38.8 1.3 %shard_map.43 = bf16[192,768]{1,0:T(8,128)(2,1)} custom-call(bf16[1168,128]{1,0:T(8,128)(2,1)S(1)} %get-tuple-element.34.own, f32[384,128]{1,0:T(8,128)S(1)} %get-tuple-element.43.info, bf16[592,128]{1,0:T(8,128)(2,1)S(1)} %collective-permute-done.14.first, bf16[592,128]{1,0:T(8,128)(2,1)S(1)} %collective-permute-done.19.second, f32[192,896]{1,0:T(8,128)S(1)} %shard_map.42.total), custom_call_target="tpu_custom_call" | custom-call | tf_op jit(solution)/shard_map/pallas_call | solution.py:274
  (2 shorter events, 0.0 us)
Async XLA Ops:
  0.0 1.0 %copy-start = (bf16[192,768]{1,0:T(8,128)(2,1)S(1)}, bf16[192,768]{1,0:T(8,128)(2,1)}, u32[]{:S(2)}) copy-start(bf16[192,768]{1,0:T(8,128)(2,1)} %rows.3) | copy-start | bytes 884740
  1.0 6.4 %copy-start.2 = (s32[192]{0:T(256)S(1)}, s32[192]{0:T(256)}, u32[]{:S(2)}) copy-start(s32[192]{0:T(256)} %param.5) | copy-start | bytes 2308
  1.0 7.9 %collective-permute-start.2 = (bf16[576,128]{1,0:T(8,128)(2,1)S(1)}, bf16[576,128]{1,0:T(8,128)(2,1)S(1)}, u32[]{:S(2)}, u32[]{:S(2)}) collective-permute-start(bf16[576,128]{1,0:T(8,128)(2,1)S(1)} %shard_map.38), channel_id=1, source_target_pairs={{0,3},{1,2},{2,1},{3,0},{4,7},{5,6},{6,5},{7,4},{8,11},{9,10},{10,... | collective-permute-start | bytes 442376 | tf_op jit(solution)/shard_map/ppermute | solution.py:309
  3.4 8.1 %collective-permute-start.1 = (bf16[576,128]{1,0:T(8,128)(2,1)S(1)}, bf16[576,128]{1,0:T(8,128)(2,1)S(1)}, u32[]{:S(2)}, u32[]{:S(2)}) collective-permute-start(bf16[576,128]{1,0:T(8,128)(2,1)S(1)} %shard_map.38), channel_id=1, source_target_pairs={{0,13},{1,12},{12,9},{13,8},{8,5},{9,4},{4,1},{5,0},{2,15},{3,14},... | collective-permute-start | bytes 442376 | tf_op jit(solution)/shard_map/ppermute | solution.py:306
  7.3 0.7 %copy-start.1 = (s32[192,1]{0,1:T(1,128)S(1)}, s32[192,1]{0,1:T(1,128)}, u32[]{:S(2)}) copy-start(s32[192,1]{0,1:T(1,128)} %param.4) | copy-start | bytes 2308
  8.1 7.5 %collective-permute-start.4 = (bf16[592,128]{1,0:T(8,128)(2,1)S(1)}, bf16[592,128]{1,0:T(8,128)(2,1)S(1)}, u32[]{:S(2)}, u32[]{:S(2)}) collective-permute-start(bf16[592,128]{1,0:T(8,128)(2,1)S(1)} %get-tuple-element.36), channel_id=1, source_target_pairs={{0,3},{1,2},{2,1},{3,0},{4,7},{5,6},{6,5},{7,4},{8,11},{9,10},{10,... | collective-permute-start | bytes 454664 | tf_op jit(solution)/shard_map/ppermute | solution.py:309
  8.2 7.3 %collective-permute-start.3 = (bf16[592,128]{1,0:T(8,128)(2,1)S(1)}, bf16[592,128]{1,0:T(8,128)(2,1)S(1)}, u32[]{:S(2)}, u32[]{:S(2)}) collective-permute-start(bf16[592,128]{1,0:T(8,128)(2,1)S(1)} %get-tuple-element.36), channel_id=1, source_target_pairs={{0,13},{1,12},{12,9},{13,8},{8,5},{9,4},{4,1},{5,0},{2,15},{3,14},... | collective-permute-start | bytes 454664 | tf_op jit(solution)/shard_map/ppermute | solution.py:306
  8.8 18.6 %collective-permute-start = (bf16[1168,128]{1,0:T(8,128)(2,1)S(1)}, bf16[1168,128]{1,0:T(8,128)(2,1)S(1)}, u32[]{:S(2)}, u32[]{:S(2)}) collective-permute-start(bf16[1168,128]{1,0:T(8,128)(2,1)S(1)} %get-tuple-element.34.own), channel_id=1, source_target_pairs={{0,1},{1,0},{2,3},{3,2},{4,5},{5,4},{6,7},{7,6},{8,9},{9,8},{10,11... | collective-permute-start | bytes 897032 | tf_op jit(solution)/shard_map/ppermute | solution.py:312
  11.5 6.5 %collective-permute-start.6 = (bf16[576,128]{1,0:T(8,128)(2,1)S(1)}, bf16[576,128]{1,0:T(8,128)(2,1)S(1)}, u32[]{:S(2)}, u32[]{:S(2)}) collective-permute-start(bf16[576,128]{1,0:T(8,128)(2,1)S(1)} %collective-permute-done.1.refs_4_), channel_id=1, source_target_pairs={{0,3},{1,2},{2,1},{3,0},{4,7},{5,6},{6,5},{7,4},{8,11},{9,10},{10,... | collective-permute-start | bytes 442376 | tf_op jit(solution)/shard_map/ppermute | solution.py:309
  11.5 8.2 %collective-permute-start.5 = (bf16[576,128]{1,0:T(8,128)(2,1)S(1)}, bf16[576,128]{1,0:T(8,128)(2,1)S(1)}, u32[]{:S(2)}, u32[]{:S(2)}) collective-permute-start(bf16[576,128]{1,0:T(8,128)(2,1)S(1)} %collective-permute-done.1.refs_4_), channel_id=1, source_target_pairs={{0,13},{1,12},{12,9},{13,8},{8,5},{9,4},{4,1},{5,0},{2,15},{3,14},... | collective-permute-start | bytes 442376 | tf_op jit(solution)/shard_map/ppermute | solution.py:306
  15.5 8.6 %collective-permute-start.8 = (bf16[592,128]{1,0:T(8,128)(2,1)S(1)}, bf16[592,128]{1,0:T(8,128)(2,1)S(1)}, u32[]{:S(2)}, u32[]{:S(2)}) collective-permute-start(bf16[592,128]{1,0:T(8,128)(2,1)S(1)} %collective-permute-done.3.refs_5_), channel_id=1, source_target_pairs={{0,3},{1,2},{2,1},{3,0},{4,7},{5,6},{6,5},{7,4},{8,11},{9,10},{10,... | collective-permute-start | bytes 454664 | tf_op jit(solution)/shard_map/ppermute | solution.py:309
  17.3 6.9 %collective-permute-start.7 = (bf16[592,128]{1,0:T(8,128)(2,1)S(1)}, bf16[592,128]{1,0:T(8,128)(2,1)S(1)}, u32[]{:S(2)}, u32[]{:S(2)}) collective-permute-start(bf16[592,128]{1,0:T(8,128)(2,1)S(1)} %collective-permute-done.3.refs_5_), channel_id=1, source_target_pairs={{0,13},{1,12},{12,9},{13,8},{8,5},{9,4},{4,1},{5,0},{2,15},{3,14},... | collective-permute-start | bytes 454664 | tf_op jit(solution)/shard_map/ppermute | solution.py:306
  19.8 9.2 %collective-permute-start.10 = (bf16[576,128]{1,0:T(8,128)(2,1)S(1)}, bf16[576,128]{1,0:T(8,128)(2,1)S(1)}, u32[]{:S(2)}, u32[]{:S(2)}) collective-permute-start(bf16[576,128]{1,0:T(8,128)(2,1)S(1)} %collective-permute-done.5.refs_0_), channel_id=1, source_target_pairs={{0,3},{1,2},{2,1},{3,0},{4,7},{5,6},{6,5},{7,4},{8,11},{9,10},{10,... | collective-permute-start | bytes 442376 | tf_op jit(solution)/shard_map/ppermute | solution.py:309
  19.9 9.1 %collective-permute-start.9 = (bf16[576,128]{1,0:T(8,128)(2,1)S(1)}, bf16[576,128]{1,0:T(8,128)(2,1)S(1)}, u32[]{:S(2)}, u32[]{:S(2)}) collective-permute-start(bf16[576,128]{1,0:T(8,128)(2,1)S(1)} %collective-permute-done.5.refs_0_), channel_id=1, source_target_pairs={{0,13},{1,12},{12,9},{13,8},{8,5},{9,4},{4,1},{5,0},{2,15},{3,14},... | collective-permute-start | bytes 442376 | tf_op jit(solution)/shard_map/ppermute | solution.py:306
  24.2 6.0 %collective-permute-start.12 = (bf16[592,128]{1,0:T(8,128)(2,1)S(1)}, bf16[592,128]{1,0:T(8,128)(2,1)S(1)}, u32[]{:S(2)}, u32[]{:S(2)}) collective-permute-start(bf16[592,128]{1,0:T(8,128)(2,1)S(1)} %collective-permute-done.7.refs_1_), channel_id=1, source_target_pairs={{0,3},{1,2},{2,1},{3,0},{4,7},{5,6},{6,5},{7,4},{8,11},{9,10},{10,... | collective-permute-start | bytes 454664 | tf_op jit(solution)/shard_map/ppermute | solution.py:309
  25.5 7.8 %collective-permute-start.13 = (bf16[592,128]{1,0:T(8,128)(2,1)S(1)}, bf16[592,128]{1,0:T(8,128)(2,1)S(1)}, u32[]{:S(2)}, u32[]{:S(2)}) collective-permute-start(bf16[592,128]{1,0:T(8,128)(2,1)S(1)} %collective-permute-done.7.refs_1_), channel_id=1, source_target_pairs={{0,13},{1,12},{12,9},{13,8},{8,5},{9,4},{4,1},{5,0},{2,15},{3,14},... | collective-permute-start | bytes 454664 | tf_op jit(solution)/shard_map/ppermute | solution.py:306
  29.0 6.4 %collective-permute-start.11 = (bf16[576,128]{1,0:T(8,128)(2,1)S(1)}, bf16[576,128]{1,0:T(8,128)(2,1)S(1)}, u32[]{:S(2)}, u32[]{:S(2)}) collective-permute-start(bf16[576,128]{1,0:T(8,128)(2,1)S(1)} %collective-permute-done.9.refs_4_), channel_id=1, source_target_pairs={{0,3},{1,2},{2,1},{3,0},{4,7},{5,6},{6,5},{7,4},{8,11},{9,10},{10,... | collective-permute-start | bytes 442376 | tf_op jit(solution)/shard_map/ppermute | solution.py:309
  30.2 7.2 %collective-permute-start.15 = (bf16[592,128]{1,0:T(8,128)(2,1)S(1)}, bf16[592,128]{1,0:T(8,128)(2,1)S(1)}, u32[]{:S(2)}, u32[]{:S(2)}) collective-permute-start(bf16[592,128]{1,0:T(8,128)(2,1)S(1)} %collective-permute-done.12.refs_3_), channel_id=1, source_target_pairs={{0,13},{1,12},{12,9},{13,8},{8,5},{9,4},{4,1},{5,0},{2,15},{3,14},... | collective-permute-start | bytes 454664 | tf_op jit(solution)/shard_map/ppermute | solution.py:306
  34.7 1.5 %collective-permute-start.16 = (bf16[64,896]{1,0:T(8,128)(2,1)S(1)}, bf16[64,896]{1,0:T(8,128)(2,1)S(1)}, u32[]{:S(2)}, u32[]{:S(2)}) collective-permute-start(bf16[64,896]{1,0:T(8,128)(2,1)S(1)} %get-tuple-element.55), channel_id=1, source_target_pairs={{0,1},{1,0},{2,3},{3,2},{4,5},{5,4},{6,7},{7,6},{8,9},{9,8},{10,11... | collective-permute-start | bytes 344072 | tf_op jit(solution)/shard_map/ppermute | solution.py:312
  35.3 1.3 %collective-permute-start.17 = (bf16[64,896]{1,0:T(8,128)(2,1)S(1)}, bf16[64,896]{1,0:T(8,128)(2,1)S(1)}, u32[]{:S(2)}, u32[]{:S(2)}) collective-permute-start(bf16[64,896]{1,0:T(8,128)(2,1)S(1)} %get-tuple-element.56), channel_id=1, source_target_pairs={{0,1},{1,0},{2,3},{3,2},{4,5},{5,4},{6,7},{7,6},{8,9},{9,8},{10,11... | collective-permute-start | bytes 344072 | tf_op jit(solution)/shard_map/ppermute | solution.py:312
  35.4 2.0 %collective-permute-start.18 = (bf16[64,896]{1,0:T(8,128)(2,1)S(1)}, bf16[64,896]{1,0:T(8,128)(2,1)S(1)}, u32[]{:S(2)}, u32[]{:S(2)}) collective-permute-start(bf16[64,896]{1,0:T(8,128)(2,1)S(1)} %get-tuple-element.57), channel_id=1, source_target_pairs={{0,1},{1,0},{2,3},{3,2},{4,5},{5,4},{6,7},{7,6},{8,9},{9,8},{10,11... | collective-permute-start | bytes 344072 | tf_op jit(solution)/shard_map/ppermute | solution.py:312
  35.8 2.4 %collective-permute-start.14 = (bf16[592,128]{1,0:T(8,128)(2,1)S(1)}, bf16[592,128]{1,0:T(8,128)(2,1)S(1)}, u32[]{:S(2)}, u32[]{:S(2)}) collective-permute-start(bf16[592,128]{1,0:T(8,128)(2,1)S(1)} %shard_map.41), channel_id=1, source_target_pairs={{0,1},{1,0},{2,3},{3,2},{4,5},{5,4},{6,7},{7,6},{8,9},{9,8},{10,11... | collective-permute-start | bytes 454664 | tf_op jit(solution)/shard_map/ppermute | solution.py:312
  37.4 1.4 %collective-permute-start.19 = (bf16[592,128]{1,0:T(8,128)(2,1)S(1)}, bf16[592,128]{1,0:T(8,128)(2,1)S(1)}, u32[]{:S(2)}, u32[]{:S(2)}) collective-permute-start(bf16[592,128]{1,0:T(8,128)(2,1)S(1)} %collective-permute-done.15.second), channel_id=1, source_target_pairs={{0,1},{1,0},{2,3},{3,2},{4,5},{5,4},{6,7},{7,6},{8,9},{9,8},{10,11... | collective-permute-start | bytes 454664 | tf_op jit(solution)/shard_map/ppermute | solution.py:312

commit v30 on v28

--- a/solution.py
+++ b/solution.py
@@ -116,16 +116,18 @@
     return jnp.concatenate(slabs, axis=1)
 
 
-def key_rows(ref, half):
-    wide = ref[ref.shape[0] - LINES :, :].astype(F32)
-    return [
-        wide[side : side + 1, :half] * 256.0 + wide[side + 2 : side + 3, :half]
-        for side in range(2)
-    ]
-
-
-def key_row(ref, rows_here):
-    return jnp.concatenate(key_rows(ref, rows_here // 2), axis=1)
+def key_row(ref, rows_here, line=0):
+    half = rows_here // 2
+    wide = ref[ref.shape[0] - LINES :, :].astype(F32)[line : line + 4, :half]
+    return jnp.concatenate([wide[0:1] * 256.0 + wide[2:3], wide[1:2] * 256.0 + wide[3:4]], axis=1)
+
+
+def add_names_kernel(piece, whole, out):
+    top = piece.shape[0] - LINES
+    out[:top, :] = piece[:top, :]
+    lines = piece[top:, :].astype(F32)
+    own = whole[whole.shape[0] - LINES :, :].astype(F32)
+    out[top:, :] = jnp.concatenate([lines[:4], own[:4], lines[8:]], axis=0).astype(BF16)
 
 
 def from_halves(first, second, rows_here):
@@ -172,9 +174,11 @@
         out[:, wide - 128 :] = jnp.broadcast_to(denom[top : top + rows_here], (rows_here, 128))
 
 
-def start_kernel(n_blocks, own, other, *refs):
+def start_kernel(n_blocks, own, other, crossed, *refs):
     refs = list(refs)
     rows_here = refs[-1].shape[0] // 2
+    raw = crossed[...]
+    crossed = (raw, key_row(refs[1], rows_here, 4), to_row(scale_column(raw)))
     left = left_rows((own, other), rows_here)
     key = jnp.concatenate([to_column(key_row(ref, rows_here)) for ref in (own, other)], axis=0)
     scale = scale_column(left)
@@ -182,7 +186,7 @@
     lane = lax.broadcasted_iota(jnp.int32, info.shape, 1)
     info[...] = jnp.where(lane == 0, key, 4.0 * scale)
     first = (left[:rows_here], key_row(own, rows_here), to_row(scale[:rows_here]))
-    blocks = [first] + take_blocks(refs, n_blocks, rows_here)
+    blocks = [first, crossed] + take_blocks(refs, n_blocks, rows_here)
     store_sides(*add_blocks(left, info, blocks, None, None), refs)
 
 
@@ -255,9 +259,9 @@
     )(*args)
 
 
-def start_both(left, right, shape):
+def start_both(left, crossed, right, shape):
     rows_here = shape[0]
-    args = list(left) + [half for block in right for half in block]
+    args = [*left, crossed] + [half for block in right for half in block]
     shapes = [(shape, F32), (shape, F32), ((2 * rows_here, 128), F32)]
     return call(functools.partial(start_kernel, len(right)), shapes, args)
 
@@ -317,9 +321,13 @@
         [((slabs * count + LINES, 128), BF16) for count in (rows_here, half)],
         [embeddings, group_of.reshape(line), cluster_id.reshape(line)],
     )
-    along_by = [(first, second)]
-    across_by = []
-    for s in range(1, n_blk):
+    crossed = across(embeddings)
+    moved = [along(first), along(second)]
+    moved[1], crossed, _ = together(moved[1], crossed, moved[0])
+    (named,) = call(add_names_kernel, [(second.shape, BF16)], [moved[1], whole])
+    along_by = [(first, second), (moved[0], named)]
+    across_by = [crossed]
+    for s in range(2, n_blk):
         moved = [along(piece) for piece in along_by[-1]]
         swapped = [across(piece) for piece in along_by[-1]]
         moved[0], swapped[0] = together(moved[0], swapped[0])
@@ -328,8 +336,8 @@
         along_by.append(tuple(moved))
         across_by.append(tuple(swapped))
     left = (whole, other_core(whole))
-    early = across_by[:-1] + along_by[1:-2]
-    mine, theirs, info = start_both(left, early, (rows_here, width + 128))
+    early = across_by[1:-1] + along_by[1:-2]
+    mine, theirs, info = start_both(left, crossed, early, (rows_here, width + 128))
     left = (*left, info)
     far_first, _, mine, theirs = together(along_by[-1][0], across_by[-1][0], mine, theirs)
     near_second, _ = together(across_by[-1][1], far_first)
@@ -354,7 +362,7 @@
 def per_device(embeddings, group_of, cluster_id):
     rows_here, width = embeddings.shape
     devices = lax.axis_size("blk") * lax.axis_size("sub") * lax.axis_size("pair")
-    small = devices * rows_here * width * 2 <= GATHER_LIMIT
+    small = devices * rows_here * width * 2 <= GATHER_LIMIT and lax.axis_size("blk") > 3
     fits = width % 128 == 0 and rows_here % (64 * PARTS) == 0 and rows_here <= 256
     if small and fits and lax.axis_size("sub") == 2 and lax.axis_size("pair") == 2:
         return by_block(embeddings, group_of, cluster_id)

time: 36.4 us -> 37.3 us (1.025)
  waiting for transfers between devices: 3.61 us -> 5.36 us
  starting transfers between devices: 25.7 us -> 24.9 us
    ppermute x7, waiting for transfers between devices: 1.82 us -> 3.73 us  [along(): return lax.ppermute(rows, ('blk', 'pair'), hops)]
    ppermute x7, starting transfers between devices: 17.5 us -> 16.5 us  [along(): return lax.ppermute(rows, ('blk', 'pair'), hops)]
    ppermute x7 -> x6, waiting for transfers between devices: 0.9 us -> 0.29 us  [across(): return lax.ppermute(rows, ('sub', 'pair'), [(0, 3), (1, 2), (2, 1), (3, 0)])]
    ppermute x6, starting transfers between devices: 1.26 us -> 1.83 us  [other_core(): return lax.ppermute(rows, 'pair', [(0, 1), (1, 0)])]
    ppermute x6, waiting for transfers between devices: 0.89 us -> 1.35 us  [other_core(): return lax.ppermute(rows, 'pair', [(0, 1), (1, 0)])]
    ppermute x7 -> x6, starting transfers between devices: 7.01 us -> 6.59 us  [across(): return lax.ppermute(rows, ('sub', 'pair'), [(0, 3), (1, 2), (2, 1), (3, 0)])]
    pallas_call x6 -> x7, Pallas kernels: 3.84 us -> 3.85 us  [call(): pl.pallas_call(kernel, out_shape=[jax.ShapeDtypeStruct(shape, dtype) for...]
  transfers between devices with their start and end apart: 20 -> 19, of which waited for: 9 -> 9; matrix products, arithmetic and copies ran while one was open for 0% -> 0% of each run, Pallas kernels for 11% -> 10%
where the time goes in v30:
time: 37.3 us; the launch traced here: 37.1 us
  starting transfers between devices  24.9 us (67%)
  waiting for transfers between devices  5.36 us (14%)
  Pallas kernels  5.14 us (14%)
  local copies, waits for them, and re-layouts  1.67 us (4%)
    ppermute x7, starting transfers between devices, along(): return lax.ppermute(rows, ('blk', 'pair'), hops)  16.5 us
    ppermute x6, starting transfers between devices, across(): return lax.ppermute(rows, ('sub', 'pair'), [(0, 3), (1, 2), (2, 1), (3, 0)])  6.59 us
    pallas_call x7, Pallas kernels, call(): pl.pallas_call(kernel, out_shape=[jax.ShapeDtypeStruct(shape, dtype) for...  3.85 us
    ppermute x7, waiting for transfers between devices, along(): return lax.ppermute(rows, ('blk', 'pair'), hops)  3.73 us
    ppermute x6, starting transfers between devices, other_core(): return lax.ppermute(rows, 'pair', [(0, 1), (1, 0)])  1.83 us
    unnamed x6, local copies, waits for them, and re-layouts  1.67 us
    ppermute x6, waiting for transfers between devices, other_core(): return lax.ppermute(rows, 'pair', [(0, 1), (1, 0)])  1.35 us
    pallas_call x1, Pallas kernels, finish(): pl.pallas_call(last_kernel, out_shape=jax.ShapeDtypeStruct(shape, BF16),...  1.29 us
  transfers between devices with their start and end apart: 19, of which 9 were waited for; matrix products, arithmetic and copies ran while one was open for 0% of the time, Pallas kernels for 10%

profile of v30, /device:TPU:0, one launch (start us, length us, event | category | flops | bytes accessed | tf_op | source)
XLA Modules:
  0.0 37.1 jit_solution(13860374431638868717)
XLA Ops:
  0.0 2.4 %collective-permute-start.2 = (bf16[192,768]{1,0:T(8,128)(2,1)}, bf16[192,768]{1,0:T(8,128)(2,1)S(1)}, u32[]{:S(2)}, u32[]{:S(2)}) collective-permute-start(bf16[192,768]{1,0:T(8,128)(2,1)} %rows.3), channel_id=1, source_target_pairs={{0,3},{1,2},{2,1},{3,0},{4,7},{5,6},{6,5},{7,4},{8,11},{9,10},{10,... | collective-permute-start | bytes 884744 | tf_op jit(solution)/shard_map/ppermute | solution.py:313
  2.4 0.0 copy-start
  2.4 1.0 %copy-done = bf16[192,768]{1,0:T(8,128)(2,1)S(1)} copy-done((bf16[192,768]{1,0:T(8,128)(2,1)S(1)}, bf16[192,768]{1,0:T(8,128)(2,1)}, u32[]{:S(2)}) %copy-start) | copy-done | bytes 294936
  3.4 0.0 copy-start.2
  3.4 2.9 %collective-permute-start.3 = (bf16[576,128]{1,0:T(8,128)(2,1)S(1)}, bf16[576,128]{1,0:T(8,128)(2,1)S(1)}, u32[]{:S(2)}, u32[]{:S(2)}) collective-permute-start(bf16[576,128]{1,0:T(8,128)(2,1)S(1)} %shard_map.38), channel_id=1, source_target_pairs={{4,1},{5,0},{0,9},{1,8},{8,13},{9,12},{12,5},{13,4},{6,3},{7,2},{2... | collective-permute-start | bytes 442376 | tf_op jit(solution)/shard_map/ppermute | solution.py:310
  6.3 0.0 copy-start.1
  6.3 0.0 copy-done.2
  6.3 0.7 %copy-done.1 = s32[192,1]{0,1:T(1,128)S(1)} copy-done((s32[192,1]{0,1:T(1,128)S(1)}, s32[192,1]{0,1:T(1,128)}, u32[]{:S(2)}) %copy-start.1) | copy-done | bytes 792
  7.0 0.1 shard_map.37
  7.1 1.1 %collective-permute-start.1 = (bf16[592,128]{1,0:T(8,128)(2,1)S(1)}, bf16[592,128]{1,0:T(8,128)(2,1)S(1)}, u32[]{:S(2)}, u32[]{:S(2)}) collective-permute-start(bf16[592,128]{1,0:T(8,128)(2,1)S(1)} %get-tuple-element.33), channel_id=1, source_target_pairs={{4,1},{5,0},{0,9},{1,8},{8,13},{9,12},{12,5},{13,4},{6,3},{7,2},{2... | collective-permute-start | bytes 454664 | tf_op jit(solution)/shard_map/ppermute | solution.py:310
  8.2 0.7 %collective-permute-start = (bf16[1168,128]{1,0:T(8,128)(2,1)S(1)}, bf16[1168,128]{1,0:T(8,128)(2,1)S(1)}, u32[]{:S(2)}, u32[]{:S(2)}) collective-permute-start(bf16[1168,128]{1,0:T(8,128)(2,1)S(1)} %get-tuple-element.32.whole.own), channel_id=1, source_target_pairs={{0,1},{1,0},{2,3},{3,2},{4,5},{5,4},{6,7},{7,6},{8,9},{9,8},{10,11... | collective-permute-start | bytes 897032 | tf_op jit(solution)/shard_map/ppermute | solution.py:316
  8.8 1.3 %collective-permute-done.3.refs_2_ = bf16[576,128]{1,0:T(8,128)(2,1)S(1)} collective-permute-done((bf16[576,128]{1,0:T(8,128)(2,1)S(1)}, bf16[576,128]{1,0:T(8,128)(2,1)S(1)}, u32[]{:S(2)}, u32[]{:S(2)}) %collective-permute-start.3) | collective-permute-done | bytes 147488 | tf_op jit(solution)/shard_map/ppermute | solution.py:310
  10.1 0.0 collective-permute-start.5
  10.1 3.1 %collective-permute-start.4 = (bf16[576,128]{1,0:T(8,128)(2,1)S(1)}, bf16[576,128]{1,0:T(8,128)(2,1)S(1)}, u32[]{:S(2)}, u32[]{:S(2)}) collective-permute-start(bf16[576,128]{1,0:T(8,128)(2,1)S(1)} %collective-permute-done.3.refs_2_), channel_id=1, source_target_pairs={{4,1},{5,0},{0,9},{1,8},{8,13},{9,12},{12,5},{13,4},{6,3},{7,2},{2... | collective-permute-start | bytes 442376 | tf_op jit(solution)/shard_map/ppermute | solution.py:310
  13.2 0.1 collective-permute-done.1.piece
  13.4 0.0 collective-permute-done.2.crossed
  13.4 1.7 %collective-permute-start.7 = (bf16[592,128]{1,0:T(8,128)(2,1)S(1)}, bf16[592,128]{1,0:T(8,128)(2,1)S(1)}, u32[]{:S(2)}, u32[]{:S(2)}) collective-permute-start(bf16[592,128]{1,0:T(8,128)(2,1)S(1)} %shard_map.39.refs_3_), channel_id=1, source_target_pairs={{0,3},{1,2},{2,1},{3,0},{4,7},{5,6},{6,5},{7,4},{8,11},{9,10},{10,... | collective-permute-start | bytes 454664 | tf_op jit(solution)/shard_map/ppermute | solution.py:313
  15.1 1.2 %collective-permute-start.6 = (bf16[592,128]{1,0:T(8,128)(2,1)S(1)}, bf16[592,128]{1,0:T(8,128)(2,1)S(1)}, u32[]{:S(2)}, u32[]{:S(2)}) collective-permute-start(bf16[592,128]{1,0:T(8,128)(2,1)S(1)} %shard_map.39.refs_3_), channel_id=1, source_target_pairs={{4,1},{5,0},{0,9},{1,8},{8,13},{9,12},{12,5},{13,4},{6,3},{7,2},{2... | collective-permute-start | bytes 454664 | tf_op jit(solution)/shard_map/ppermute | solution.py:310
  16.3 0.0 collective-permute-done.5.refs_0_
  16.3 1.2 %collective-permute-done.4.refs_0_ = bf16[576,128]{1,0:T(8,128)(2,1)S(1)} collective-permute-done((bf16[576,128]{1,0:T(8,128)(2,1)S(1)}, bf16[576,128]{1,0:T(8,128)(2,1)S(1)}, u32[]{:S(2)}, u32[]{:S(2)}) %collective-permute-start.4) | collective-permute-done | bytes 147488 | tf_op jit(solution)/shard_map/ppermute | solution.py:310
  17.5 0.5 %collective-permute-start.9 = (bf16[576,128]{1,0:T(8,128)(2,1)S(1)}, bf16[576,128]{1,0:T(8,128)(2,1)S(1)}, u32[]{:S(2)}, u32[]{:S(2)}) collective-permute-start(bf16[576,128]{1,0:T(8,128)(2,1)S(1)} %collective-permute-done.4.refs_0_), channel_id=1, source_target_pairs={{0,3},{1,2},{2,1},{3,0},{4,7},{5,6},{6,5},{7,4},{8,11},{9,10},{10,... | collective-permute-start | bytes 442376 | tf_op jit(solution)/shard_map/ppermute | solution.py:313
  18.0 3.4 %collective-permute-start.8 = (bf16[576,128]{1,0:T(8,128)(2,1)S(1)}, bf16[576,128]{1,0:T(8,128)(2,1)S(1)}, u32[]{:S(2)}, u32[]{:S(2)}) collective-permute-start(bf16[576,128]{1,0:T(8,128)(2,1)S(1)} %collective-permute-done.4.refs_0_), channel_id=1, source_target_pairs={{4,1},{5,0},{0,9},{1,8},{8,13},{9,12},{12,5},{13,4},{6,3},{7,2},{2... | collective-permute-start | bytes 442376 | tf_op jit(solution)/shard_map/ppermute | solution.py:310
  21.4 0.0 collective-permute-done.7.refs_1_
  21.4 0.0 collective-permute-done.6.refs_1_
  21.4 1.0 %collective-permute-start.11 = (bf16[592,128]{1,0:T(8,128)(2,1)S(1)}, bf16[592,128]{1,0:T(8,128)(2,1)S(1)}, u32[]{:S(2)}, u32[]{:S(2)}) collective-permute-start(bf16[592,128]{1,0:T(8,128)(2,1)S(1)} %collective-permute-done.6.refs_1_), channel_id=1, source_target_pairs={{0,3},{1,2},{2,1},{3,0},{4,7},{5,6},{6,5},{7,4},{8,11},{9,10},{10,... | collective-permute-start | bytes 454664 | tf_op jit(solution)/shard_map/ppermute | solution.py:313
  22.3 2.1 %collective-permute-start.12 = (bf16[592,128]{1,0:T(8,128)(2,1)S(1)}, bf16[592,128]{1,0:T(8,128)(2,1)S(1)}, u32[]{:S(2)}, u32[]{:S(2)}) collective-permute-start(bf16[592,128]{1,0:T(8,128)(2,1)S(1)} %collective-permute-done.6.refs_1_), channel_id=1, source_target_pairs={{4,1},{5,0},{0,9},{1,8},{8,13},{9,12},{12,5},{13,4},{6,3},{7,2},{2... | collective-permute-start | bytes 454664 | tf_op jit(solution)/shard_map/ppermute | solution.py:310
  24.4 0.0 collective-permute-done.9.refs_2_
  24.4 0.7 %collective-permute-done.8.refs_4_ = bf16[576,128]{1,0:T(8,128)(2,1)S(1)} collective-permute-done((bf16[576,128]{1,0:T(8,128)(2,1)S(1)}, bf16[576,128]{1,0:T(8,128)(2,1)S(1)}, u32[]{:S(2)}, u32[]{:S(2)}) %collective-permute-start.8) | collective-permute-done | bytes 147488 | tf_op jit(solution)/shard_map/ppermute | solution.py:310
  25.0 0.0 collective-permute-done.other
  25.0 1.5 %shard_map.40 = (f32[192,896]{1,0:T(8,128)S(1)}, f32[192,896]{1,0:T(8,128)S(1)}, f32[384,128]{1,0:T(8,128)S(1)}) custom-call(bf16[1168,128]{1,0:T(8,128)(2,1)S(1)} %get-tuple-element.32.whole.own, bf16[1168,128]{1,0:T(8,128)(2,1)S(1)} %collective-permute-done.other, bf16[192,768]{1,0:T(8,128)(2,1)S(1)} %collective-permute-done.2.crossed, ...), custom_call_target="tpu_custom_call" | custom-call | tf_op jit(solution)/shard_map/pallas_call | solution.py:252
  26.6 1.0 %collective-permute-start.10 = (bf16[576,128]{1,0:T(8,128)(2,1)S(1)}, bf16[576,128]{1,0:T(8,128)(2,1)S(1)}, u32[]{:S(2)}, u32[]{:S(2)}) collective-permute-start(bf16[576,128]{1,0:T(8,128)(2,1)S(1)} %collective-permute-done.8.refs_4_), channel_id=1, source_target_pairs={{0,3},{1,2},{2,1},{3,0},{4,7},{5,6},{6,5},{7,4},{8,11},{9,10},{10,... | collective-permute-start | bytes 442376 | tf_op jit(solution)/shard_map/ppermute | solution.py:313
  27.6 0.0 collective-permute-done.11.refs_3_
  27.6 2.8 %collective-permute-start.14 = (bf16[592,128]{1,0:T(8,128)(2,1)S(1)}, bf16[592,128]{1,0:T(8,128)(2,1)S(1)}, u32[]{:S(2)}, u32[]{:S(2)}) collective-permute-start(bf16[592,128]{1,0:T(8,128)(2,1)S(1)} %collective-permute-done.11.refs_3_), channel_id=1, source_target_pairs={{4,1},{5,0},{0,9},{1,8},{8,13},{9,12},{12,5},{13,4},{6,3},{7,2},{2... | collective-permute-start | bytes 454664 | tf_op jit(solution)/shard_map/ppermute | solution.py:310
  30.4 0.0 collective-permute-done.12.refs_5_
  30.4 1.4 %shard_map.41 = (f32[192,896]{1,0:T(8,128)S(1)}, bf16[64,896]{1,0:T(8,128)(2,1)S(1)}, bf16[64,896]{1,0:T(8,128)(2,1)S(1)}, bf16[64,896]{1,0:T(8,128)(2,1)S(1)}) custom-call(bf16[1168,128]{1,0:T(8,128)(2,1)S(1)} %get-tuple-element.32.whole.own, bf16[1168,128]{1,0:T(8,128)(2,1)S(1)} %collective-permute-done.other, ...), custom_call_target="tpu_custom_call", output_to_operand_aliasing={{0}: (9, {})} | custom-call | tf_op jit(solution)/shard_map/pallas_call | solution.py:252
  31.8 0.5 %collective-permute-start.15 = (bf16[64,896]{1,0:T(8,128)(2,1)S(1)}, bf16[64,896]{1,0:T(8,128)(2,1)S(1)}, u32[]{:S(2)}, u32[]{:S(2)}) collective-permute-start(bf16[64,896]{1,0:T(8,128)(2,1)S(1)} %get-tuple-element.51), channel_id=1, source_target_pairs={{0,1},{1,0},{2,3},{3,2},{4,5},{5,4},{6,7},{7,6},{8,9},{9,8},{10,11... | collective-permute-start | bytes 344072 | tf_op jit(solution)/shard_map/ppermute | solution.py:316
  32.3 0.1 collective-permute-start.16
  32.4 0.3 collective-permute-done.10.first
  32.7 0.2 collective-permute-start.17
  32.9 0.4 collective-permute-start.13
  33.3 0.0 collective-permute-done.15.refs_0_
  33.3 0.4 collective-permute-done.16.refs_1_
  33.7 0.4 collective-permute-done.17.refs_2_
  34.0 0.4 %collective-permute-done.14.second = bf16[592,128]{1,0:T(8,128)(2,1)S(1)} collective-permute-done((bf16[592,128]{1,0:T(8,128)(2,1)S(1)}, bf16[592,128]{1,0:T(8,128)(2,1)S(1)}, u32[]{:S(2)}, u32[]{:S(2)}) %collective-permute-start.14) | collective-permute-done | bytes 151584 | tf_op jit(solution)/shard_map/ppermute | solution.py:310
  34.5 0.0 collective-permute-start.18
  34.5 0.8 %shard_map.43.total = f32[192,896]{1,0:T(8,128)S(1)} custom-call(bf16[1168,128]{1,0:T(8,128)(2,1)S(1)} %get-tuple-element.32.whole.own, f32[384,128]{1,0:T(8,128)S(1)} %get-tuple-element.39.info, bf16[576,128]{1,0:T(8,128)(2,1)S(1)} %collective-permute-done.10.first, ...), custom_call_target="tpu_custom_call", output_to_operand_aliasing={{}: (4, {})} | custom-call | tf_op jit(solution)/shard_map/pallas_call | solution.py:252
  35.2 0.0 collective-permute-done.13.first
  35.2 0.6 %collective-permute-done.18.second = bf16[592,128]{1,0:T(8,128)(2,1)S(1)} collective-permute-done((bf16[592,128]{1,0:T(8,128)(2,1)S(1)}, bf16[592,128]{1,0:T(8,128)(2,1)S(1)}, u32[]{:S(2)}, u32[]{:S(2)}) %collective-permute-start.18) | collective-permute-done | bytes 151584 | tf_op jit(solution)/shard_map/ppermute | solution.py:316
  35.8 1.3 %shard_map.44 = bf16[192,768]{1,0:T(8,128)(2,1)} custom-call(bf16[1168,128]{1,0:T(8,128)(2,1)S(1)} %get-tuple-element.32.whole.own, f32[384,128]{1,0:T(8,128)S(1)} %get-tuple-element.39.info, bf16[592,128]{1,0:T(8,128)(2,1)S(1)} %collective-permute-done.13.first, bf16[592,128]{1,0:T(8,128)(2,1)S(1)} %collective-permute-done.18.second, ...), custom_call_target="tpu_custom_call" | custom-call | tf_op jit(solution)/shard_map/pallas_call | solution.py:278
  (3 shorter events, 0.1 us)
Async XLA Ops:
  0.0 13.4 %collective-permute-start.2 = (bf16[192,768]{1,0:T(8,128)(2,1)}, bf16[192,768]{1,0:T(8,128)(2,1)S(1)}, u32[]{:S(2)}, u32[]{:S(2)}) collective-permute-start(bf16[192,768]{1,0:T(8,128)(2,1)} %rows.3), channel_id=1, source_target_pairs={{0,3},{1,2},{2,1},{3,0},{4,7},{5,6},{6,5},{7,4},{8,11},{9,10},{10,... | collective-permute-start | bytes 884744 | tf_op jit(solution)/shard_map/ppermute | solution.py:313
  2.4 1.0 %copy-start = (bf16[192,768]{1,0:T(8,128)(2,1)S(1)}, bf16[192,768]{1,0:T(8,128)(2,1)}, u32[]{:S(2)}) copy-start(bf16[192,768]{1,0:T(8,128)(2,1)} %rows.3) | copy-start | bytes 884740
  3.4 3.0 %copy-start.2 = (s32[192]{0:T(256)S(1)}, s32[192]{0:T(256)}, u32[]{:S(2)}) copy-start(s32[192]{0:T(256)} %param.5) | copy-start | bytes 2308
  3.4 6.7 %collective-permute-start.3 = (bf16[576,128]{1,0:T(8,128)(2,1)S(1)}, bf16[576,128]{1,0:T(8,128)(2,1)S(1)}, u32[]{:S(2)}, u32[]{:S(2)}) collective-permute-start(bf16[576,128]{1,0:T(8,128)(2,1)S(1)} %shard_map.38), channel_id=1, source_target_pairs={{4,1},{5,0},{0,9},{1,8},{8,13},{9,12},{12,5},{13,4},{6,3},{7,2},{2... | collective-permute-start | bytes 442376 | tf_op jit(solution)/shard_map/ppermute | solution.py:310
  6.3 0.7 %copy-start.1 = (s32[192,1]{0,1:T(1,128)S(1)}, s32[192,1]{0,1:T(1,128)}, u32[]{:S(2)}) copy-start(s32[192,1]{0,1:T(1,128)} %param.4) | copy-start | bytes 2308
  7.1 6.3 %collective-permute-start.1 = (bf16[592,128]{1,0:T(8,128)(2,1)S(1)}, bf16[592,128]{1,0:T(8,128)(2,1)S(1)}, u32[]{:S(2)}, u32[]{:S(2)}) collective-permute-start(bf16[592,128]{1,0:T(8,128)(2,1)S(1)} %get-tuple-element.33), channel_id=1, source_target_pairs={{4,1},{5,0},{0,9},{1,8},{8,13},{9,12},{12,5},{13,4},{6,3},{7,2},{2... | collective-permute-start | bytes 454664 | tf_op jit(solution)/shard_map/ppermute | solution.py:310
  8.2 16.9 %collective-permute-start = (bf16[1168,128]{1,0:T(8,128)(2,1)S(1)}, bf16[1168,128]{1,0:T(8,128)(2,1)S(1)}, u32[]{:S(2)}, u32[]{:S(2)}) collective-permute-start(bf16[1168,128]{1,0:T(8,128)(2,1)S(1)} %get-tuple-element.32.whole.own), channel_id=1, source_target_pairs={{0,1},{1,0},{2,3},{3,2},{4,5},{5,4},{6,7},{7,6},{8,9},{9,8},{10,11... | collective-permute-start | bytes 897032 | tf_op jit(solution)/shard_map/ppermute | solution.py:316
  10.1 6.1 %collective-permute-start.5 = (bf16[576,128]{1,0:T(8,128)(2,1)S(1)}, bf16[576,128]{1,0:T(8,128)(2,1)S(1)}, u32[]{:S(2)}, u32[]{:S(2)}) collective-permute-start(bf16[576,128]{1,0:T(8,128)(2,1)S(1)} %collective-permute-done.3.refs_2_), channel_id=1, source_target_pairs={{0,3},{1,2},{2,1},{3,0},{4,7},{5,6},{6,5},{7,4},{8,11},{9,10},{10,... | collective-permute-start | bytes 442376 | tf_op jit(solution)/shard_map/ppermute | solution.py:313
  10.1 7.3 %collective-permute-start.4 = (bf16[576,128]{1,0:T(8,128)(2,1)S(1)}, bf16[576,128]{1,0:T(8,128)(2,1)S(1)}, u32[]{:S(2)}, u32[]{:S(2)}) collective-permute-start(bf16[576,128]{1,0:T(8,128)(2,1)S(1)} %collective-permute-done.3.refs_2_), channel_id=1, source_target_pairs={{4,1},{5,0},{0,9},{1,8},{8,13},{9,12},{12,5},{13,4},{6,3},{7,2},{2... | collective-permute-start | bytes 442376 | tf_op jit(solution)/shard_map/ppermute | solution.py:310
  13.4 8.0 %collective-permute-start.7 = (bf16[592,128]{1,0:T(8,128)(2,1)S(1)}, bf16[592,128]{1,0:T(8,128)(2,1)S(1)}, u32[]{:S(2)}, u32[]{:S(2)}) collective-permute-start(bf16[592,128]{1,0:T(8,128)(2,1)S(1)} %shard_map.39.refs_3_), channel_id=1, source_target_pairs={{0,3},{1,2},{2,1},{3,0},{4,7},{5,6},{6,5},{7,4},{8,11},{9,10},{10,... | collective-permute-start | bytes 454664 | tf_op jit(solution)/shard_map/ppermute | solution.py:313
  15.1 6.3 %collective-permute-start.6 = (bf16[592,128]{1,0:T(8,128)(2,1)S(1)}, bf16[592,128]{1,0:T(8,128)(2,1)S(1)}, u32[]{:S(2)}, u32[]{:S(2)}) collective-permute-start(bf16[592,128]{1,0:T(8,128)(2,1)S(1)} %shard_map.39.refs_3_), channel_id=1, source_target_pairs={{4,1},{5,0},{0,9},{1,8},{8,13},{9,12},{12,5},{13,4},{6,3},{7,2},{2... | collective-permute-start | bytes 454664 | tf_op jit(solution)/shard_map/ppermute | solution.py:310
  17.5 6.9 %collective-permute-start.9 = (bf16[576,128]{1,0:T(8,128)(2,1)S(1)}, bf16[576,128]{1,0:T(8,128)(2,1)S(1)}, u32[]{:S(2)}, u32[]{:S(2)}) collective-permute-start(bf16[576,128]{1,0:T(8,128)(2,1)S(1)} %collective-permute-done.4.refs_0_), channel_id=1, source_target_pairs={{0,3},{1,2},{2,1},{3,0},{4,7},{5,6},{6,5},{7,4},{8,11},{9,10},{10,... | collective-permute-start | bytes 442376 | tf_op jit(solution)/shard_map/ppermute | solution.py:313
  18.0 7.1 %collective-permute-start.8 = (bf16[576,128]{1,0:T(8,128)(2,1)S(1)}, bf16[576,128]{1,0:T(8,128)(2,1)S(1)}, u32[]{:S(2)}, u32[]{:S(2)}) collective-permute-start(bf16[576,128]{1,0:T(8,128)(2,1)S(1)} %collective-permute-done.4.refs_0_), channel_id=1, source_target_pairs={{4,1},{5,0},{0,9},{1,8},{8,13},{9,12},{12,5},{13,4},{6,3},{7,2},{2... | collective-permute-start | bytes 442376 | tf_op jit(solution)/shard_map/ppermute | solution.py:310
  21.4 6.3 %collective-permute-start.11 = (bf16[592,128]{1,0:T(8,128)(2,1)S(1)}, bf16[592,128]{1,0:T(8,128)(2,1)S(1)}, u32[]{:S(2)}, u32[]{:S(2)}) collective-permute-start(bf16[592,128]{1,0:T(8,128)(2,1)S(1)} %collective-permute-done.6.refs_1_), channel_id=1, source_target_pairs={{0,3},{1,2},{2,1},{3,0},{4,7},{5,6},{6,5},{7,4},{8,11},{9,10},{10,... | collective-permute-start | bytes 454664 | tf_op jit(solution)/shard_map/ppermute | solution.py:313
  22.3 8.1 %collective-permute-start.12 = (bf16[592,128]{1,0:T(8,128)(2,1)S(1)}, bf16[592,128]{1,0:T(8,128)(2,1)S(1)}, u32[]{:S(2)}, u32[]{:S(2)}) collective-permute-start(bf16[592,128]{1,0:T(8,128)(2,1)S(1)} %collective-permute-done.6.refs_1_), channel_id=1, source_target_pairs={{4,1},{5,0},{0,9},{1,8},{8,13},{9,12},{12,5},{13,4},{6,3},{7,2},{2... | collective-permute-start | bytes 454664 | tf_op jit(solution)/shard_map/ppermute | solution.py:310
  26.6 6.1 %collective-permute-start.10 = (bf16[576,128]{1,0:T(8,128)(2,1)S(1)}, bf16[576,128]{1,0:T(8,128)(2,1)S(1)}, u32[]{:S(2)}, u32[]{:S(2)}) collective-permute-start(bf16[576,128]{1,0:T(8,128)(2,1)S(1)} %collective-permute-done.8.refs_4_), channel_id=1, source_target_pairs={{0,3},{1,2},{2,1},{3,0},{4,7},{5,6},{6,5},{7,4},{8,11},{9,10},{10,... | collective-permute-start | bytes 442376 | tf_op jit(solution)/shard_map/ppermute | solution.py:313
  27.6 6.8 %collective-permute-start.14 = (bf16[592,128]{1,0:T(8,128)(2,1)S(1)}, bf16[592,128]{1,0:T(8,128)(2,1)S(1)}, u32[]{:S(2)}, u32[]{:S(2)}) collective-permute-start(bf16[592,128]{1,0:T(8,128)(2,1)S(1)} %collective-permute-done.11.refs_3_), channel_id=1, source_target_pairs={{4,1},{5,0},{0,9},{1,8},{8,13},{9,12},{12,5},{13,4},{6,3},{7,2},{2... | collective-permute-start | bytes 454664 | tf_op jit(solution)/shard_map/ppermute | solution.py:310
  31.8 1.5 %collective-permute-start.15 = (bf16[64,896]{1,0:T(8,128)(2,1)S(1)}, bf16[64,896]{1,0:T(8,128)(2,1)S(1)}, u32[]{:S(2)}, u32[]{:S(2)}) collective-permute-start(bf16[64,896]{1,0:T(8,128)(2,1)S(1)} %get-tuple-element.51), channel_id=1, source_target_pairs={{0,1},{1,0},{2,3},{3,2},{4,5},{5,4},{6,7},{7,6},{8,9},{9,8},{10,11... | collective-permute-start | bytes 344072 | tf_op jit(solution)/shard_map/ppermute | solution.py:316
  32.3 1.3 %collective-permute-start.16 = (bf16[64,896]{1,0:T(8,128)(2,1)S(1)}, bf16[64,896]{1,0:T(8,128)(2,1)S(1)}, u32[]{:S(2)}, u32[]{:S(2)}) collective-permute-start(bf16[64,896]{1,0:T(8,128)(2,1)S(1)} %get-tuple-element.52), channel_id=1, source_target_pairs={{0,1},{1,0},{2,3},{3,2},{4,5},{5,4},{6,7},{7,6},{8,9},{9,8},{10,11... | collective-permute-start | bytes 344072 | tf_op jit(solution)/shard_map/ppermute | solution.py:316
  32.7 1.3 %collective-permute-start.17 = (bf16[64,896]{1,0:T(8,128)(2,1)S(1)}, bf16[64,896]{1,0:T(8,128)(2,1)S(1)}, u32[]{:S(2)}, u32[]{:S(2)}) collective-permute-start(bf16[64,896]{1,0:T(8,128)(2,1)S(1)} %get-tuple-element.53), channel_id=1, source_target_pairs={{0,1},{1,0},{2,3},{3,2},{4,5},{5,4},{6,7},{7,6},{8,9},{9,8},{10,11... | collective-permute-start | bytes 344072 | tf_op jit(solution)/shard_map/ppermute | solution.py:316
  32.9 2.3 %collective-permute-start.13 = (bf16[592,128]{1,0:T(8,128)(2,1)S(1)}, bf16[592,128]{1,0:T(8,128)(2,1)S(1)}, u32[]{:S(2)}, u32[]{:S(2)}) collective-permute-start(bf16[592,128]{1,0:T(8,128)(2,1)S(1)} %shard_map.42), channel_id=1, source_target_pairs={{0,1},{1,0},{2,3},{3,2},{4,5},{5,4},{6,7},{7,6},{8,9},{9,8},{10,11... | collective-permute-start | bytes 454664 | tf_op jit(solution)/shard_map/ppermute | solution.py:316
  34.5 1.4 %collective-permute-start.18 = (bf16[592,128]{1,0:T(8,128)(2,1)S(1)}, bf16[592,128]{1,0:T(8,128)(2,1)S(1)}, u32[]{:S(2)}, u32[]{:S(2)}) collective-permute-start(bf16[592,128]{1,0:T(8,128)(2,1)S(1)} %collective-permute-done.14.second), channel_id=1, source_target_pairs={{0,1},{1,0},{2,3},{3,2},{4,5},{5,4},{6,7},{7,6},{8,9},{9,8},{10,11... | collective-permute-start | bytes 454664 | tf_op jit(solution)/shard_map/ppermute | solution.py:316

commit v31 on v27

--- a/solution.py
+++ b/solution.py
@@ -166,6 +166,66 @@
         out[:, wide - 128 :] = jnp.broadcast_to(denom[top : top + rows_here], (rows_here, 128))
 
 
+def store_theirs(numer, denom, outs):
+    high = denom.astype(BF16).astype(F32)
+    lane = lax.broadcasted_iota(jnp.int32, (denom.shape[0], 128), 1)
+    pair = jnp.where(lane == 0, high, denom - high).astype(BF16)
+    count, wide = outs[0].shape
+    for part, out in enumerate(outs):
+        rows = slice(part * count, (part + 1) * count)
+        out[:, : wide - 128] = numer[rows].astype(BF16)
+        out[:, wide - 128 :] = pair[rows]
+
+
+def add_theirs(mine, parts):
+    width = mine.shape[1] - 128
+    theirs = jnp.concatenate([ref[...] for ref in parts], axis=0)
+    pair = theirs[:, width:].astype(F32)
+    numer = mine[:, :width] + theirs[:, :width].astype(F32)
+    return numer, mine[:, width : width + 1] + (pair[:, 0:1] + pair[:, 1:2])
+
+
+def back_kernel(near_first, near_second, over_first, over_second, *refs):
+    refs = list(refs)
+    rows_here = refs[4].shape[0]
+    blocks = take_blocks(refs, 2, rows_here)
+    mine, *theirs = refs
+    sides = [
+        from_halves(near_first, near_second, rows_here),
+        from_halves(over_first, over_second, rows_here),
+    ]
+    left = jnp.concatenate([side[0] for side in sides], axis=0)
+    key = jnp.concatenate([to_column(side[1]) for side in sides], axis=0)
+    lane = lax.broadcasted_iota(jnp.int32, (2 * rows_here, 128), 1)
+    info = jnp.where(lane == 0, key, 4.0 * scale_column(left))
+    numer, denom = add_blocks(left, info, blocks, None, None)
+    store_sides(numer[:rows_here], denom[:rows_here], [mine])
+    store_theirs(numer[rows_here:], denom[rows_here:], theirs)
+
+
+def back_sum_kernel(mine, *refs):
+    *parts, out = refs
+    rows_here = mine.shape[0]
+    half = rows_here // 2
+    numer, denom = add_theirs(mine, parts)
+    slabs = numer.shape[1] // 128
+    for slab in range(slabs):
+        out[slab * rows_here : (slab + 1) * rows_here, :] = numer[
+            :, slab * 128 : (slab + 1) * 128
+        ].astype(BF16)
+    high = denom.astype(BF16).astype(F32)
+    line_at = lax.broadcasted_iota(jnp.int32, (LINES, 128), 0)
+    lines = jnp.zeros((LINES, 128), F32)
+    for kind, column in enumerate((high, denom - high)):
+        row = to_row(column)
+        for side in range(2):
+            part = row[:, side * half : (side + 1) * half]
+            if half < 128:
+                part = jnp.concatenate([part, jnp.zeros((1, 128 - half), F32)], axis=1)
+            lines = jnp.where(line_at == 2 * kind + side, part, lines)
+    out[slabs * rows_here :, :] = lines.astype(BF16)
+
+
 def start_kernel(n_blocks, own, other, *refs):
     refs = list(refs)
     rows_here = refs[-1].shape[0] // 2
@@ -192,36 +252,18 @@
     denom = jnp.concatenate([ref[:, width : width + 1] for ref in (mine_in, theirs_in)], axis=0)
     numer, denom = add_blocks(left, info, blocks, numer, denom)
     store_sides(numer[:rows_here], denom[:rows_here], [mine])
-    denom = denom[rows_here:]
-    high = denom.astype(BF16).astype(F32)
-    lane = lax.broadcasted_iota(jnp.int32, (rows_here, 128), 1)
-    pair = jnp.where(lane == 0, high, denom - high).astype(BF16)
-    count = rows_here // len(theirs)
-    for part, out in enumerate(theirs):
-        top = part * count
-        out[:, :width] = numer[rows_here + top : rows_here + top + count].astype(BF16)
-        out[:, width:] = pair[top : top + count]
-
-
-def join_kernel(own, info, first, second, mine, *refs):
-    *parts, out = refs
-    rows_here, wide = out.shape
-    width = wide - 128
-    theirs = jnp.concatenate([ref[...] for ref in parts], axis=0)
-    pair = theirs[:, width:].astype(F32)
-    numer = mine[:, :width] + theirs[:, :width].astype(F32)
-    denom = mine[:, width : width + 1] + (pair[:, 0:1] + pair[:, 1:2])
-    blocks = take_blocks([first, second], 1, rows_here)
-    left = left_rows((own,), rows_here)
-    store_sides(*add_blocks(left, info, blocks, numer, denom), [out])
-
-
-def last_kernel(own, info, first, second, total, out, staged, sems):
+    store_theirs(numer[rows_here:], denom[rows_here:], theirs)
+
+
+def last_kernel(mine, returned, *refs):
+    *parts, out, staged, sems = refs
     rows_here, width = out.shape
-    blocks = take_blocks([first, second], 1, rows_here)
-    left = left_rows((own,), rows_here)
-    numer, denom = total[:, :width], total[:, width : width + 1]
-    numer, denom = add_blocks(left, info, blocks, numer, denom)
+    half = rows_here // 2
+    numer, denom = add_theirs(mine, parts)
+    numer = numer + from_slabs(returned, rows_here).astype(F32)
+    lines = returned[returned.shape[0] - LINES :, :].astype(F32)[:4, :half]
+    total = lines[0:2] + lines[2:4]
+    denom = denom + to_column(jnp.concatenate([total[0:1], total[1:2]], axis=1))
     share = 1.0 / denom
     count = rows_here // 4
     copies = []
@@ -299,6 +341,14 @@
         ]
         return lax.ppermute(rows, ("blk", "pair"), hops)
 
+    def back_along(rows):
+        hops = [
+            (2 * order[i] + core, 2 * order[i - 1] + 1 - core)
+            for i in range(n_blk)
+            for core in range(2)
+        ]
+        return lax.ppermute(rows, ("blk", "pair"), hops)
+
     def across(rows):
         return lax.ppermute(rows, ("sub", "pair"), [(0, 3), (1, 2), (2, 1), (3, 0)])
 
@@ -313,41 +363,48 @@
     )
     along_by = [(first, second)]
     across_by = []
-    for s in range(1, n_blk):
+    for s in range(1, n_blk - 1):
         moved = [along(piece) for piece in along_by[-1]]
         swapped = [across(piece) for piece in along_by[-1]]
         moved[0], swapped[0] = together(moved[0], swapped[0])
-        if s < n_blk - 1:
+        if s != 2:
             moved[1], swapped[1], _ = together(moved[1], swapped[1], moved[0])
+        else:
+            moved[1], swapped[1], to_return, _ = together(
+                moved[1], swapped[1], to_return, moved[0]
+            )
+        if s == 1:
+            over = [other_core(piece) for piece in moved]
+            near_sum, *over_sum = call(
+                back_kernel,
+                [((rows_here, width + 128), F32)]
+                + [((rows_here // PARTS, width + 128), BF16)] * PARTS,
+                [*moved, *over, first, second, *swapped],
+            )
+            (to_return,) = call(
+                back_sum_kernel,
+                [((slabs * rows_here + LINES, 128), BF16)],
+                [near_sum, *[other_core(part) for part in over_sum]],
+            )
         along_by.append(tuple(moved))
         across_by.append(tuple(swapped))
+    returned = back_along(to_return)
+    across_by.append(tuple(across(piece) for piece in along_by[-1]))
     left = (whole, other_core(whole))
-    early = across_by[:-1] + along_by[1:-2]
+    early = across_by[:-1] + along_by[1:-1]
     mine, theirs, info = start_both(left, early, (rows_here, width + 128))
-    left = (*left, info)
-    far_first, _, mine, theirs = together(along_by[-1][0], across_by[-1][0], mine, theirs)
-    near_second, _ = together(across_by[-1][1], far_first)
-    last_first, last_second = across(far_first), along(near_second)
-    late = [along_by[-2], across_by[-1], along_by[-1]]
-    mine, *theirs = add_both(left, late, (mine, theirs))
-    back = [other_core(part) for part in theirs[:-1]]
-    last_first, theirs[-1] = together(last_first, theirs[-1])
-    last_second, *back = together(last_second, *back, other_core(theirs[-1]))
-    last = [other_core(last_first), other_core(last_second)]
-    (total,) = call(
-        join_kernel,
-        [((rows_here, width + 128), F32)],
-        [whole, info, last_first, last_second, mine, *back],
-        {4: 0},
-    )
-    out = finish((rows_here, width), [whole, info, *last, total])
+    late = [along_by[-1], across_by[-1]]
+    mine, *theirs = add_both((*left, info), late, (mine, theirs))
+    out = finish(
+        (rows_here, width), [mine, returned, *[other_core(part) for part in theirs]]
+    )
     return out
 
 
 def per_device(embeddings, group_of, cluster_id):
     rows_here, width = embeddings.shape
     devices = lax.axis_size("blk") * lax.axis_size("sub") * lax.axis_size("pair")
-    small = devices * rows_here * width * 2 <= GATHER_LIMIT
+    small = devices * rows_here * width * 2 <= GATHER_LIMIT and lax.axis_size("blk") > 3
     fits = width % 128 == 0 and rows_here % (64 * PARTS) == 0 and rows_here <= 256
     if small and fits and lax.axis_size("sub") == 2 and lax.axis_size("pair") == 2:
         return by_block(embeddings, group_of, cluster_id)

time: 36.6 us -> 39.6 us (1.082)
  waiting for transfers between devices: 3.96 us -> 15.3 us
  starting transfers between devices: 25.6 us -> 17.2 us
    ppermute x7 -> x6, waiting for transfers between devices: 0.91 us -> 11.5 us  [across(): return lax.ppermute(rows, ('sub', 'pair'), [(0, 3), (1, 2), (2, 1), (3, 0)])]
    ppermute x7 -> x4, starting transfers between devices: 17.5 us -> 8.22 us  [along(): return lax.ppermute(rows, ('blk', 'pair'), hops)]
    ppermute x6 -> x9, starting transfers between devices: 1.16 us -> 2.3 us  [other_core(): return lax.ppermute(rows, 'pair', [(0, 1), (1, 0)])]
    ppermute x7 -> x6, starting transfers between devices: 7.01 us -> 5.9 us  [across(): return lax.ppermute(rows, ('sub', 'pair'), [(0, 3), (1, 2), (2, 1), (3, 0)])]
    ppermute x0 -> x1, starting transfers between devices: none -> 0.83 us  [back_along(): return lax.ppermute(rows, ('blk', 'pair'), hops)]
    ppermute x6 -> x9, waiting for transfers between devices: 1.22 us -> 1.96 us  [other_core(): return lax.ppermute(rows, 'pair', [(0, 1), (1, 0)])]
    pallas_call x5 -> x6, Pallas kernels: 3.82 us -> 4.19 us  [call(): pl.pallas_call(kernel, out_shape=[jax.ShapeDtypeStruct(shape, dtype) for...]
    ppermute x7 -> x4, waiting for transfers between devices: 1.83 us -> 1.78 us  [along(): return lax.ppermute(rows, ('blk', 'pair'), hops)]
  transfers between devices with their start and end apart: 20 -> 20, of which waited for: 9 -> 11; matrix products, arithmetic and copies ran while one was open for 0% -> 0% of each run, Pallas kernels for 10% -> 10%
where the time goes in v31:
time: 39.6 us; the launch traced here: 39.4 us
  starting transfers between devices  17.2 us (43%)
  waiting for transfers between devices  15.3 us (39%)
  Pallas kernels  5.21 us (13%)
  local copies, waits for them, and re-layouts  1.65 us (4%)
    ppermute x6, waiting for transfers between devices, across(): return lax.ppermute(rows, ('sub', 'pair'), [(0, 3), (1, 2), (2, 1), (3, 0)])  11.5 us
    ppermute x4, starting transfers between devices, along(): return lax.ppermute(rows, ('blk', 'pair'), hops)  8.22 us
    ppermute x6, starting transfers between devices, across(): return lax.ppermute(rows, ('sub', 'pair'), [(0, 3), (1, 2), (2, 1), (3, 0)])  5.9 us
    pallas_call x6, Pallas kernels, call(): pl.pallas_call(kernel, out_shape=[jax.ShapeDtypeStruct(shape, dtype) for...  4.19 us
    ppermute x9, starting transfers between devices, other_core(): return lax.ppermute(rows, 'pair', [(0, 1), (1, 0)])  2.3 us
    ppermute x9, waiting for transfers between devices, other_core(): return lax.ppermute(rows, 'pair', [(0, 1), (1, 0)])  1.96 us
    ppermute x4, waiting for transfers between devices, along(): return lax.ppermute(rows, ('blk', 'pair'), hops)  1.78 us
    unnamed x6, local copies, waits for them, and re-layouts  1.65 us
  transfers between devices with their start and end apart: 20, of which 11 were waited for; matrix products, arithmetic and copies ran while one was open for 0% of the time, Pallas kernels for 10%

profile of v31, /device:TPU:0, one launch (start us, length us, event | category | flops | bytes accessed | tf_op | source)
XLA Modules:
  0.0 39.4 jit_solution(18274232835048354526)
XLA Ops:
  0.0 0.0 copy-start.2
  0.0 0.0 copy-start.1
  0.0 0.7 %copy-done.2 = s32[192]{0:T(256)S(1)} copy-done((s32[192]{0:T(256)S(1)}, s32[192]{0:T(256)}, u32[]{:S(2)}) %copy-start.2) | copy-done | bytes 792
  0.7 0.0 copy-done.1
  0.7 0.0 copy-start
  0.7 1.0 %copy-done = bf16[192,768]{1,0:T(8,128)(2,1)S(1)} copy-done((bf16[192,768]{1,0:T(8,128)(2,1)S(1)}, bf16[192,768]{1,0:T(8,128)(2,1)}, u32[]{:S(2)}) %copy-start) | copy-done | bytes 294936
  1.7 0.1 shard_map.37
  1.7 2.4 %collective-permute-start.4 = (bf16[592,128]{1,0:T(8,128)(2,1)S(1)}, bf16[592,128]{1,0:T(8,128)(2,1)S(1)}, u32[]{:S(2)}, u32[]{:S(2)}) collective-permute-start(bf16[592,128]{1,0:T(8,128)(2,1)S(1)} %get-tuple-element.29.refs_1_), channel_id=1, source_target_pairs={{0,3},{1,2},{2,1},{3,0},{4,7},{5,6},{6,5},{7,4},{8,11},{9,10},{10,... | collective-permute-start | bytes 454664 | tf_op jit(solution)/shard_map/ppermute | solution.py:353
  4.2 2.9 %collective-permute-start.3 = (bf16[592,128]{1,0:T(8,128)(2,1)S(1)}, bf16[592,128]{1,0:T(8,128)(2,1)S(1)}, u32[]{:S(2)}, u32[]{:S(2)}) collective-permute-start(bf16[592,128]{1,0:T(8,128)(2,1)S(1)} %get-tuple-element.29.refs_1_), channel_id=1, source_target_pairs={{4,1},{5,0},{0,9},{1,8},{8,13},{9,12},{12,5},{13,4},{6,3},{7,2},{2... | collective-permute-start | bytes 454664 | tf_op jit(solution)/shard_map/ppermute | solution.py:342
  7.1 0.1 collective-permute-start.2
  7.2 1.8 %collective-permute-start.1 = (bf16[576,128]{1,0:T(8,128)(2,1)S(1)}, bf16[576,128]{1,0:T(8,128)(2,1)S(1)}, u32[]{:S(2)}, u32[]{:S(2)}) collective-permute-start(bf16[576,128]{1,0:T(8,128)(2,1)S(1)} %shard_map.38.refs_0_), channel_id=1, source_target_pairs={{4,1},{5,0},{0,9},{1,8},{8,13},{9,12},{12,5},{13,4},{6,3},{7,2},{2... | collective-permute-start | bytes 442376 | tf_op jit(solution)/shard_map/ppermute | solution.py:342
  9.0 4.3 %collective-permute-done.2.refs_2_.refs_0_ = bf16[576,128]{1,0:T(8,128)(2,1)S(1)} collective-permute-done((bf16[576,128]{1,0:T(8,128)(2,1)S(1)}, bf16[576,128]{1,0:T(8,128)(2,1)S(1)}, u32[]{:S(2)}, u32[]{:S(2)}) %collective-permute-start.2) | collective-permute-done | bytes 147488 | tf_op jit(solution)/shard_map/ppermute | solution.py:353
  13.3 0.4 %collective-permute-done.1.near_first.refs_4_ = bf16[576,128]{1,0:T(8,128)(2,1)S(1)} collective-permute-done((bf16[576,128]{1,0:T(8,128)(2,1)S(1)}, bf16[576,128]{1,0:T(8,128)(2,1)S(1)}, u32[]{:S(2)}, u32[]{:S(2)}) %collective-permute-start.1) | collective-permute-done | bytes 147488 | tf_op jit(solution)/shard_map/ppermute | solution.py:342
  13.7 0.0 collective-permute-done.4.refs_3_.refs_1_
  13.7 0.0 collective-permute-done.3.near_second.refs_5_
  13.7 0.0 collective-permute-start.10
  13.7 0.5 %collective-permute-start.9 = (bf16[576,128]{1,0:T(8,128)(2,1)S(1)}, bf16[576,128]{1,0:T(8,128)(2,1)S(1)}, u32[]{:S(2)}, u32[]{:S(2)}) collective-permute-start(bf16[576,128]{1,0:T(8,128)(2,1)S(1)} %collective-permute-done.1.near_first.refs_4_), channel_id=1, source_target_pairs={{0,1},{1,0},{2,3},{3,2},{4,5},{5,4},{6,7},{7,6},{8,9},{9,8},{10,11... | collective-permute-start | bytes 442376 | tf_op jit(solution)/shard_map/ppermute | solution.py:356
  14.2 0.5 %collective-permute-start.6 = (bf16[576,128]{1,0:T(8,128)(2,1)S(1)}, bf16[576,128]{1,0:T(8,128)(2,1)S(1)}, u32[]{:S(2)}, u32[]{:S(2)}) collective-permute-start(bf16[576,128]{1,0:T(8,128)(2,1)S(1)} %collective-permute-done.1.near_first.refs_4_), channel_id=1, source_target_pairs={{0,3},{1,2},{2,1},{3,0},{4,7},{5,6},{6,5},{7,4},{8,11},{9,10},{10,... | collective-permute-start | bytes 442376 | tf_op jit(solution)/shard_map/ppermute | solution.py:353
  14.7 2.8 %collective-permute-start.5 = (bf16[576,128]{1,0:T(8,128)(2,1)S(1)}, bf16[576,128]{1,0:T(8,128)(2,1)S(1)}, u32[]{:S(2)}, u32[]{:S(2)}) collective-permute-start(bf16[576,128]{1,0:T(8,128)(2,1)S(1)} %collective-permute-done.1.near_first.refs_4_), channel_id=1, source_target_pairs={{4,1},{5,0},{0,9},{1,8},{8,13},{9,12},{12,5},{13,4},{6,3},{7,2},{2... | collective-permute-start | bytes 442376 | tf_op jit(solution)/shard_map/ppermute | solution.py:342
  17.6 0.0 collective-permute-done.9.over_first
  17.6 0.0 collective-permute-done.10.over_second
  17.6 1.1 %shard_map.39 = (f32[192,896]{1,0:T(8,128)S(1)}, bf16[64,896]{1,0:T(8,128)(2,1)S(1)}, bf16[64,896]{1,0:T(8,128)(2,1)S(1)}, bf16[64,896]{1,0:T(8,128)(2,1)S(1)}) custom-call(bf16[576,128]{1,0:T(8,128)(2,1)S(1)} %collective-permute-done.1.near_first.refs_4_, bf16[592,128]{1,0:T(8,128)(2,1)S(1)} %collective-permute-done.3.near_second.refs_5_, ...), custom_call_target="tpu_custom_call" | custom-call | tf_op jit(solution)/shard_map/pallas_call | solution.py:284
  18.7 0.3 collective-permute-start.11
  19.0 1.1 %collective-permute-start.8 = (bf16[592,128]{1,0:T(8,128)(2,1)S(1)}, bf16[592,128]{1,0:T(8,128)(2,1)S(1)}, u32[]{:S(2)}, u32[]{:S(2)}) collective-permute-start(bf16[592,128]{1,0:T(8,128)(2,1)S(1)} %collective-permute-done.3.near_second.refs_5_), channel_id=1, source_target_pairs={{0,3},{1,2},{2,1},{3,0},{4,7},{5,6},{6,5},{7,4},{8,11},{9,10},{10,... | collective-permute-start | bytes 454664 | tf_op jit(solution)/shard_map/ppermute | solution.py:353
  20.0 0.7 %collective-permute-start.7 = (bf16[592,128]{1,0:T(8,128)(2,1)S(1)}, bf16[592,128]{1,0:T(8,128)(2,1)S(1)}, u32[]{:S(2)}, u32[]{:S(2)}) collective-permute-start(bf16[592,128]{1,0:T(8,128)(2,1)S(1)} %collective-permute-done.3.near_second.refs_5_), channel_id=1, source_target_pairs={{4,1},{5,0},{0,9},{1,8},{8,13},{9,12},{12,5},{13,4},{6,3},{7,2},{2... | collective-permute-start | bytes 454664 | tf_op jit(solution)/shard_map/ppermute | solution.py:342
  20.8 0.0 collective-permute-done.6.refs_2_
  20.8 0.1 collective-permute-start
  20.9 0.5 %collective-permute-done.5.refs_0_ = bf16[576,128]{1,0:T(8,128)(2,1)S(1)} collective-permute-done((bf16[576,128]{1,0:T(8,128)(2,1)S(1)}, bf16[576,128]{1,0:T(8,128)(2,1)S(1)}, u32[]{:S(2)}, u32[]{:S(2)}) %collective-permute-start.5) | collective-permute-done | bytes 147488 | tf_op jit(solution)/shard_map/ppermute | solution.py:342
  21.3 0.0 collective-permute-start.12
  21.3 0.0 collective-permute-done.11.refs_0_
  21.3 0.5 %collective-permute-start.13 = (bf16[64,896]{1,0:T(8,128)(2,1)S(1)}, bf16[64,896]{1,0:T(8,128)(2,1)S(1)}, u32[]{:S(2)}, u32[]{:S(2)}) collective-permute-start(bf16[64,896]{1,0:T(8,128)(2,1)S(1)} %get-tuple-element.37), channel_id=1, source_target_pairs={{0,1},{1,0},{2,3},{3,2},{4,5},{5,4},{6,7},{7,6},{8,9},{9,8},{10,11... | collective-permute-start | bytes 344072 | tf_op jit(solution)/shard_map/ppermute | solution.py:356
  21.8 0.8 %collective-permute-done.12.refs_1_ = bf16[64,896]{1,0:T(8,128)(2,1)S(1)} collective-permute-done((bf16[64,896]{1,0:T(8,128)(2,1)S(1)}, bf16[64,896]{1,0:T(8,128)(2,1)S(1)}, u32[]{:S(2)}, u32[]{:S(2)}) %collective-permute-start.12) | collective-permute-done | bytes 114720 | tf_op jit(solution)/shard_map/ppermute | solution.py:356
  22.6 0.2 collective-permute-done.13.refs_2_
  22.8 0.3 shard_map.40
  23.1 1.7 %collective-permute-done.8.refs_3_ = bf16[592,128]{1,0:T(8,128)(2,1)S(1)} collective-permute-done((bf16[592,128]{1,0:T(8,128)(2,1)S(1)}, bf16[592,128]{1,0:T(8,128)(2,1)S(1)}, u32[]{:S(2)}, u32[]{:S(2)}) %collective-permute-start.8) | collective-permute-done | bytes 151584 | tf_op jit(solution)/shard_map/ppermute | solution.py:353
  24.8 0.9 %collective-permute-done.7.refs_1_ = bf16[592,128]{1,0:T(8,128)(2,1)S(1)} collective-permute-done((bf16[592,128]{1,0:T(8,128)(2,1)S(1)}, bf16[592,128]{1,0:T(8,128)(2,1)S(1)}, u32[]{:S(2)}, u32[]{:S(2)}) %collective-permute-start.7) | collective-permute-done | bytes 151584 | tf_op jit(solution)/shard_map/ppermute | solution.py:342
  25.7 0.8 %collective-permute-start.16 = (bf16[1168,128]{1,0:T(8,128)(2,1)S(1)}, bf16[1168,128]{1,0:T(8,128)(2,1)S(1)}, u32[]{:S(2)}, u32[]{:S(2)}) collective-permute-start(bf16[1168,128]{1,0:T(8,128)(2,1)S(1)} %shard_map.40), channel_id=1, source_target_pairs={{0,5},{1,4},{8,1},{9,0},{12,9},{13,8},{4,13},{5,12},{2,7},{3,6},{1... | collective-permute-start | bytes 897032 | tf_op jit(solution)/shard_map/ppermute | solution.py:350
  26.5 1.5 %collective-permute-start.15 = (bf16[592,128]{1,0:T(8,128)(2,1)S(1)}, bf16[592,128]{1,0:T(8,128)(2,1)S(1)}, u32[]{:S(2)}, u32[]{:S(2)}) collective-permute-start(bf16[592,128]{1,0:T(8,128)(2,1)S(1)} %collective-permute-done.7.refs_1_), channel_id=1, source_target_pairs={{0,3},{1,2},{2,1},{3,0},{4,7},{5,6},{6,5},{7,4},{8,11},{9,10},{10,... | collective-permute-start | bytes 454664 | tf_op jit(solution)/shard_map/ppermute | solution.py:353
  28.1 0.2 collective-permute-start.14
  28.3 0.0 collective-permute-done.other
  28.3 1.5 %shard_map.41 = (f32[192,896]{1,0:T(8,128)S(1)}, f32[192,896]{1,0:T(8,128)S(1)}, f32[384,128]{1,0:T(8,128)S(1)}) custom-call(bf16[1168,128]{1,0:T(8,128)(2,1)S(1)} %get-tuple-element.27.own, bf16[1168,128]{1,0:T(8,128)(2,1)S(1)} %collective-permute-done.other, bf16[576,128]{1,0:T(8,128)(2,1)S(1)} %collective-permute-done.2.refs_2_.refs_0_, ...), custom_call_target="tpu_custom_call" | custom-call | tf_op jit(solution)/shard_map/pallas_call | solution.py:284
  29.8 5.6 %collective-permute-done.14.refs_2_ = bf16[576,128]{1,0:T(8,128)(2,1)S(1)} collective-permute-done((bf16[576,128]{1,0:T(8,128)(2,1)S(1)}, bf16[576,128]{1,0:T(8,128)(2,1)S(1)}, u32[]{:S(2)}, u32[]{:S(2)}) %collective-permute-start.14) | collective-permute-done | bytes 147488 | tf_op jit(solution)/shard_map/ppermute | solution.py:353
  35.4 0.0 collective-permute-done.15.refs_3_
  35.4 1.1 %shard_map.42 = (f32[192,896]{1,0:T(8,128)S(1)}, bf16[64,896]{1,0:T(8,128)(2,1)S(1)}, bf16[64,896]{1,0:T(8,128)(2,1)S(1)}, bf16[64,896]{1,0:T(8,128)(2,1)S(1)}) custom-call(bf16[1168,128]{1,0:T(8,128)(2,1)S(1)} %get-tuple-element.27.own, bf16[1168,128]{1,0:T(8,128)(2,1)S(1)} %collective-permute-done.other, ...), custom_call_target="tpu_custom_call", output_to_operand_aliasing={{0}: (7, {})} | custom-call | tf_op jit(solution)/shard_map/pallas_call | solution.py:284
  36.5 0.4 %collective-permute-start.17 = (bf16[64,896]{1,0:T(8,128)(2,1)S(1)}, bf16[64,896]{1,0:T(8,128)(2,1)S(1)}, u32[]{:S(2)}, u32[]{:S(2)}) collective-permute-start(bf16[64,896]{1,0:T(8,128)(2,1)S(1)} %get-tuple-element.46), channel_id=1, source_target_pairs={{0,1},{1,0},{2,3},{3,2},{4,5},{5,4},{6,7},{7,6},{8,9},{9,8},{10,11... | collective-permute-start | bytes 344072 | tf_op jit(solution)/shard_map/ppermute | solution.py:356
  36.9 0.1 collective-permute-start.18
  37.1 0.4 collective-permute-start.19
  37.4 0.5 %collective-permute-done.17.refs_0_ = bf16[64,896]{1,0:T(8,128)(2,1)S(1)} collective-permute-done((bf16[64,896]{1,0:T(8,128)(2,1)S(1)}, bf16[64,896]{1,0:T(8,128)(2,1)S(1)}, u32[]{:S(2)}, u32[]{:S(2)}) %collective-permute-start.17) | collective-permute-done | bytes 114720 | tf_op jit(solution)/shard_map/ppermute | solution.py:356
  37.9 0.4 collective-permute-done.18.refs_1_
  38.3 0.2 collective-permute-done.19.refs_2_
  38.4 0.0 collective-permute-done.16.returned
  38.4 1.0 %shard_map.43 = bf16[192,768]{1,0:T(8,128)(2,1)} custom-call(f32[192,896]{1,0:T(8,128)S(1)} %get-tuple-element.44.mine, bf16[1168,128]{1,0:T(8,128)(2,1)S(1)} %collective-permute-done.16.returned, bf16[64,896]{1,0:T(8,128)(2,1)S(1)} %collective-permute-done.17.refs_0_, bf16[64,896]{1,0:T(8,128)(2,1)S(1)} %collective-permute-done.18.refs_1_, ...), custom_call_target="tpu_custom_call" | custom-call | tf_op jit(solution)/shard_map/pallas_call | solution.py:310
  (1 shorter events, 0.0 us)
Async XLA Ops:
  0.0 0.7 %copy-start.2 = (s32[192]{0:T(256)S(1)}, s32[192]{0:T(256)}, u32[]{:S(2)}) copy-start(s32[192]{0:T(256)} %param.5) | copy-start | bytes 2308
  0.0 0.7 %copy-start.1 = (s32[192,1]{0,1:T(1,128)S(1)}, s32[192,1]{0,1:T(1,128)}, u32[]{:S(2)}) copy-start(s32[192,1]{0,1:T(1,128)} %param.4) | copy-start | bytes 2308
  0.7 1.0 %copy-start = (bf16[192,768]{1,0:T(8,128)(2,1)S(1)}, bf16[192,768]{1,0:T(8,128)(2,1)}, u32[]{:S(2)}) copy-start(bf16[192,768]{1,0:T(8,128)(2,1)} %rows.3) | copy-start | bytes 884740
  1.7 12.0 %collective-permute-start.4 = (bf16[592,128]{1,0:T(8,128)(2,1)S(1)}, bf16[592,128]{1,0:T(8,128)(2,1)S(1)}, u32[]{:S(2)}, u32[]{:S(2)}) collective-permute-start(bf16[592,128]{1,0:T(8,128)(2,1)S(1)} %get-tuple-element.29.refs_1_), channel_id=1, source_target_pairs={{0,3},{1,2},{2,1},{3,0},{4,7},{5,6},{6,5},{7,4},{8,11},{9,10},{10,... | collective-permute-start | bytes 454664 | tf_op jit(solution)/shard_map/ppermute | solution.py:353
  4.2 9.5 %collective-permute-start.3 = (bf16[592,128]{1,0:T(8,128)(2,1)S(1)}, bf16[592,128]{1,0:T(8,128)(2,1)S(1)}, u32[]{:S(2)}, u32[]{:S(2)}) collective-permute-start(bf16[592,128]{1,0:T(8,128)(2,1)S(1)} %get-tuple-element.29.refs_1_), channel_id=1, source_target_pairs={{4,1},{5,0},{0,9},{1,8},{8,13},{9,12},{12,5},{13,4},{6,3},{7,2},{2... | collective-permute-start | bytes 454664 | tf_op jit(solution)/shard_map/ppermute | solution.py:342
  7.1 6.2 %collective-permute-start.2 = (bf16[576,128]{1,0:T(8,128)(2,1)S(1)}, bf16[576,128]{1,0:T(8,128)(2,1)S(1)}, u32[]{:S(2)}, u32[]{:S(2)}) collective-permute-start(bf16[576,128]{1,0:T(8,128)(2,1)S(1)} %shard_map.38.refs_0_), channel_id=1, source_target_pairs={{0,3},{1,2},{2,1},{3,0},{4,7},{5,6},{6,5},{7,4},{8,11},{9,10},{10,... | collective-permute-start | bytes 442376 | tf_op jit(solution)/shard_map/ppermute | solution.py:353
  7.2 6.5 %collective-permute-start.1 = (bf16[576,128]{1,0:T(8,128)(2,1)S(1)}, bf16[576,128]{1,0:T(8,128)(2,1)S(1)}, u32[]{:S(2)}, u32[]{:S(2)}) collective-permute-start(bf16[576,128]{1,0:T(8,128)(2,1)S(1)} %shard_map.38.refs_0_), channel_id=1, source_target_pairs={{4,1},{5,0},{0,9},{1,8},{8,13},{9,12},{12,5},{13,4},{6,3},{7,2},{2... | collective-permute-start | bytes 442376 | tf_op jit(solution)/shard_map/ppermute | solution.py:342
  13.7 3.9 %collective-permute-start.10 = (bf16[592,128]{1,0:T(8,128)(2,1)S(1)}, bf16[592,128]{1,0:T(8,128)(2,1)S(1)}, u32[]{:S(2)}, u32[]{:S(2)}) collective-permute-start(bf16[592,128]{1,0:T(8,128)(2,1)S(1)} %collective-permute-done.3.near_second.refs_5_), channel_id=1, source_target_pairs={{0,1},{1,0},{2,3},{3,2},{4,5},{5,4},{6,7},{7,6},{8,9},{9,8},{10,11... | collective-permute-start | bytes 454664 | tf_op jit(solution)/shard_map/ppermute | solution.py:356
  13.7 3.9 %collective-permute-start.9 = (bf16[576,128]{1,0:T(8,128)(2,1)S(1)}, bf16[576,128]{1,0:T(8,128)(2,1)S(1)}, u32[]{:S(2)}, u32[]{:S(2)}) collective-permute-start(bf16[576,128]{1,0:T(8,128)(2,1)S(1)} %collective-permute-done.1.near_first.refs_4_), channel_id=1, source_target_pairs={{0,1},{1,0},{2,3},{3,2},{4,5},{5,4},{6,7},{7,6},{8,9},{9,8},{10,11... | collective-permute-start | bytes 442376 | tf_op jit(solution)/shard_map/ppermute | solution.py:356
  14.2 6.6 %collective-permute-start.6 = (bf16[576,128]{1,0:T(8,128)(2,1)S(1)}, bf16[576,128]{1,0:T(8,128)(2,1)S(1)}, u32[]{:S(2)}, u32[]{:S(2)}) collective-permute-start(bf16[576,128]{1,0:T(8,128)(2,1)S(1)} %collective-permute-done.1.near_first.refs_4_), channel_id=1, source_target_pairs={{0,3},{1,2},{2,1},{3,0},{4,7},{5,6},{6,5},{7,4},{8,11},{9,10},{10,... | collective-permute-start | bytes 442376 | tf_op jit(solution)/shard_map/ppermute | solution.py:353
  14.7 6.6 %collective-permute-start.5 = (bf16[576,128]{1,0:T(8,128)(2,1)S(1)}, bf16[576,128]{1,0:T(8,128)(2,1)S(1)}, u32[]{:S(2)}, u32[]{:S(2)}) collective-permute-start(bf16[576,128]{1,0:T(8,128)(2,1)S(1)} %collective-permute-done.1.near_first.refs_4_), channel_id=1, source_target_pairs={{4,1},{5,0},{0,9},{1,8},{8,13},{9,12},{12,5},{13,4},{6,3},{7,2},{2... | collective-permute-start | bytes 442376 | tf_op jit(solution)/shard_map/ppermute | solution.py:342
  18.7 2.6 %collective-permute-start.11 = (bf16[64,896]{1,0:T(8,128)(2,1)S(1)}, bf16[64,896]{1,0:T(8,128)(2,1)S(1)}, u32[]{:S(2)}, u32[]{:S(2)}) collective-permute-start(bf16[64,896]{1,0:T(8,128)(2,1)S(1)} %get-tuple-element.35), channel_id=1, source_target_pairs={{0,1},{1,0},{2,3},{3,2},{4,5},{5,4},{6,7},{7,6},{8,9},{9,8},{10,11... | collective-permute-start | bytes 344072 | tf_op jit(solution)/shard_map/ppermute | solution.py:356
  19.0 5.8 %collective-permute-start.8 = (bf16[592,128]{1,0:T(8,128)(2,1)S(1)}, bf16[592,128]{1,0:T(8,128)(2,1)S(1)}, u32[]{:S(2)}, u32[]{:S(2)}) collective-permute-start(bf16[592,128]{1,0:T(8,128)(2,1)S(1)} %collective-permute-done.3.near_second.refs_5_), channel_id=1, source_target_pairs={{0,3},{1,2},{2,1},{3,0},{4,7},{5,6},{6,5},{7,4},{8,11},{9,10},{10,... | collective-permute-start | bytes 454664 | tf_op jit(solution)/shard_map/ppermute | solution.py:353
  20.0 5.7 %collective-permute-start.7 = (bf16[592,128]{1,0:T(8,128)(2,1)S(1)}, bf16[592,128]{1,0:T(8,128)(2,1)S(1)}, u32[]{:S(2)}, u32[]{:S(2)}) collective-permute-start(bf16[592,128]{1,0:T(8,128)(2,1)S(1)} %collective-permute-done.3.near_second.refs_5_), channel_id=1, source_target_pairs={{4,1},{5,0},{0,9},{1,8},{8,13},{9,12},{12,5},{13,4},{6,3},{7,2},{2... | collective-permute-start | bytes 454664 | tf_op jit(solution)/shard_map/ppermute | solution.py:342
  20.8 7.5 %collective-permute-start = (bf16[1168,128]{1,0:T(8,128)(2,1)S(1)}, bf16[1168,128]{1,0:T(8,128)(2,1)S(1)}, u32[]{:S(2)}, u32[]{:S(2)}) collective-permute-start(bf16[1168,128]{1,0:T(8,128)(2,1)S(1)} %get-tuple-element.27.own), channel_id=1, source_target_pairs={{0,1},{1,0},{2,3},{3,2},{4,5},{5,4},{6,7},{7,6},{8,9},{9,8},{10,11... | collective-permute-start | bytes 897032 | tf_op jit(solution)/shard_map/ppermute | solution.py:356
  21.3 1.3 %collective-permute-start.12 = (bf16[64,896]{1,0:T(8,128)(2,1)S(1)}, bf16[64,896]{1,0:T(8,128)(2,1)S(1)}, u32[]{:S(2)}, u32[]{:S(2)}) collective-permute-start(bf16[64,896]{1,0:T(8,128)(2,1)S(1)} %get-tuple-element.36), channel_id=1, source_target_pairs={{0,1},{1,0},{2,3},{3,2},{4,5},{5,4},{6,7},{7,6},{8,9},{9,8},{10,11... | collective-permute-start | bytes 344072 | tf_op jit(solution)/shard_map/ppermute | solution.py:356
  21.3 1.5 %collective-permute-start.13 = (bf16[64,896]{1,0:T(8,128)(2,1)S(1)}, bf16[64,896]{1,0:T(8,128)(2,1)S(1)}, u32[]{:S(2)}, u32[]{:S(2)}) collective-permute-start(bf16[64,896]{1,0:T(8,128)(2,1)S(1)} %get-tuple-element.37), channel_id=1, source_target_pairs={{0,1},{1,0},{2,3},{3,2},{4,5},{5,4},{6,7},{7,6},{8,9},{9,8},{10,11... | collective-permute-start | bytes 344072 | tf_op jit(solution)/shard_map/ppermute | solution.py:356
  25.7 12.7 %collective-permute-start.16 = (bf16[1168,128]{1,0:T(8,128)(2,1)S(1)}, bf16[1168,128]{1,0:T(8,128)(2,1)S(1)}, u32[]{:S(2)}, u32[]{:S(2)}) collective-permute-start(bf16[1168,128]{1,0:T(8,128)(2,1)S(1)} %shard_map.40), channel_id=1, source_target_pairs={{0,5},{1,4},{8,1},{9,0},{12,9},{13,8},{4,13},{5,12},{2,7},{3,6},{1... | collective-permute-start | bytes 897032 | tf_op jit(solution)/shard_map/ppermute | solution.py:350
  26.5 8.8 %collective-permute-start.15 = (bf16[592,128]{1,0:T(8,128)(2,1)S(1)}, bf16[592,128]{1,0:T(8,128)(2,1)S(1)}, u32[]{:S(2)}, u32[]{:S(2)}) collective-permute-start(bf16[592,128]{1,0:T(8,128)(2,1)S(1)} %collective-permute-done.7.refs_1_), channel_id=1, source_target_pairs={{0,3},{1,2},{2,1},{3,0},{4,7},{5,6},{6,5},{7,4},{8,11},{9,10},{10,... | collective-permute-start | bytes 454664 | tf_op jit(solution)/shard_map/ppermute | solution.py:353
  28.1 7.3 %collective-permute-start.14 = (bf16[576,128]{1,0:T(8,128)(2,1)S(1)}, bf16[576,128]{1,0:T(8,128)(2,1)S(1)}, u32[]{:S(2)}, u32[]{:S(2)}) collective-permute-start(bf16[576,128]{1,0:T(8,128)(2,1)S(1)} %collective-permute-done.5.refs_0_), channel_id=1, source_target_pairs={{0,3},{1,2},{2,1},{3,0},{4,7},{5,6},{6,5},{7,4},{8,11},{9,10},{10,... | collective-permute-start | bytes 442376 | tf_op jit(solution)/shard_map/ppermute | solution.py:353
  36.5 1.4 %collective-permute-start.17 = (bf16[64,896]{1,0:T(8,128)(2,1)S(1)}, bf16[64,896]{1,0:T(8,128)(2,1)S(1)}, u32[]{:S(2)}, u32[]{:S(2)}) collective-permute-start(bf16[64,896]{1,0:T(8,128)(2,1)S(1)} %get-tuple-element.46), channel_id=1, source_target_pairs={{0,1},{1,0},{2,3},{3,2},{4,5},{5,4},{6,7},{7,6},{8,9},{9,8},{10,11... | collective-permute-start | bytes 344072 | tf_op jit(solution)/shard_map/ppermute | solution.py:356
  36.9 1.3 %collective-permute-start.18 = (bf16[64,896]{1,0:T(8,128)(2,1)S(1)}, bf16[64,896]{1,0:T(8,128)(2,1)S(1)}, u32[]{:S(2)}, u32[]{:S(2)}) collective-permute-start(bf16[64,896]{1,0:T(8,128)(2,1)S(1)} %get-tuple-element.47), channel_id=1, source_target_pairs={{0,1},{1,0},{2,3},{3,2},{4,5},{5,4},{6,7},{7,6},{8,9},{9,8},{10,11... | collective-permute-start | bytes 344072 | tf_op jit(solution)/shard_map/ppermute | solution.py:356
  37.1 1.4 %collective-permute-start.19 = (bf16[64,896]{1,0:T(8,128)(2,1)S(1)}, bf16[64,896]{1,0:T(8,128)(2,1)S(1)}, u32[]{:S(2)}, u32[]{:S(2)}) collective-permute-start(bf16[64,896]{1,0:T(8,128)(2,1)S(1)} %get-tuple-element.48), channel_id=1, source_target_pairs={{0,1},{1,0},{2,3},{3,2},{4,5},{5,4},{6,7},{7,6},{8,9},{9,8},{10,11... | collective-permute-start | bytes 344072 | tf_op jit(solution)/shard_map/ppermute | solution.py:356

commit v32 on v31

--- a/solution.py
+++ b/solution.py
@@ -355,7 +355,7 @@
     def other_core(rows):
         return lax.ppermute(rows, "pair", [(0, 1), (1, 0)])
 
-    (first,) = call(first_pack_kernel, [((slabs * half, 128), BF16)], [embeddings])
+    (first,) = call(first_pack_kernel, [((slabs * half + LINES, 128), BF16)], [embeddings])
     whole, second = call(
         pack_kernel,
         [((slabs * count + LINES, 128), BF16) for count in (rows_here, half)],
@@ -367,29 +367,28 @@
         moved = [along(piece) for piece in along_by[-1]]
         swapped = [across(piece) for piece in along_by[-1]]
         moved[0], swapped[0] = together(moved[0], swapped[0])
-        if s != 2:
-            moved[1], swapped[1], _ = together(moved[1], swapped[1], moved[0])
-        else:
-            moved[1], swapped[1], to_return, _ = together(
-                moved[1], swapped[1], to_return, moved[0]
-            )
-        if s == 1:
-            over = [other_core(piece) for piece in moved]
-            near_sum, *over_sum = call(
-                back_kernel,
-                [((rows_here, width + 128), F32)]
-                + [((rows_here // PARTS, width + 128), BF16)] * PARTS,
-                [*moved, *over, first, second, *swapped],
-            )
-            (to_return,) = call(
-                back_sum_kernel,
-                [((slabs * rows_here + LINES, 128), BF16)],
-                [near_sum, *[other_core(part) for part in over_sum]],
-            )
+        moved[1], swapped[1], _ = together(moved[1], swapped[1], moved[0])
         along_by.append(tuple(moved))
         across_by.append(tuple(swapped))
+    near = along_by[1]
+    over = [other_core(piece) for piece in near]
+    over[0], _ = together(over[0], along_by[2][0])
+    near_sum, *over_sum = call(
+        back_kernel,
+        [((rows_here, width + 128), F32)]
+        + [((rows_here // PARTS, width + 128), BF16)] * PARTS,
+        [*near, *over, first, second, *across_by[0]],
+    )
+    near_sum, _ = together(near_sum, along_by[2][1])
+    (to_return,) = call(
+        back_sum_kernel,
+        [((slabs * rows_here + LINES, 128), BF16)],
+        [near_sum, *[other_core(part) for part in over_sum]],
+    )
     returned = back_along(to_return)
-    across_by.append(tuple(across(piece) for piece in along_by[-1]))
+    first_crossed = across(along_by[-1][0])
+    last_half, first_crossed = together(along_by[-1][1], first_crossed)
+    across_by.append((first_crossed, across(last_half)))
     left = (whole, other_core(whole))
     early = across_by[:-1] + along_by[1:-1]
     mine, theirs, info = start_both(left, early, (rows_here, width + 128))

time: 39.6 us -> 35.3 us (0.89)
  waiting for transfers between devices: 15.3 us -> 8.46 us
  starting transfers between devices: 17.2 us -> 19.8 us
    ppermute x6, waiting for transfers between devices: 11.5 us -> 4.09 us  [across(): return lax.ppermute(rows, ('sub', 'pair'), [(0, 3), (1, 2), (2, 1), (3, 0)])]
    ppermute x4, starting transfers between devices: 8.22 us -> 9.42 us  [along(): return lax.ppermute(rows, ('blk', 'pair'), hops)]
    ppermute x1, waiting for transfers between devices: 0.01 us -> 1 us  [back_along(): return lax.ppermute(rows, ('blk', 'pair'), hops)]
    ppermute x9, waiting for transfers between devices: 1.96 us -> 0.98 us  [other_core(): return lax.ppermute(rows, 'pair', [(0, 1), (1, 0)])]
    ppermute x6, starting transfers between devices: 5.9 us -> 6.7 us  [across(): return lax.ppermute(rows, ('sub', 'pair'), [(0, 3), (1, 2), (2, 1), (3, 0)])]
    ppermute x4, waiting for transfers between devices: 1.78 us -> 2.39 us  [along(): return lax.ppermute(rows, ('blk', 'pair'), hops)]
    ppermute x9, starting transfers between devices: 2.3 us -> 2.83 us  [other_core(): return lax.ppermute(rows, 'pair', [(0, 1), (1, 0)])]
  transfers between devices with their start and end apart: 20 -> 20, of which waited for: 11 -> 6; matrix products, arithmetic and copies ran while one was open for 0% -> 0% of each run, Pallas kernels for 10% -> 12%
where the time goes in v32:
time: 35.3 us; the launch traced here: 35.1 us
  starting transfers between devices  19.8 us (56%)
  waiting for transfers between devices  8.46 us (24%)
  Pallas kernels  5.19 us (15%)
  local copies, waits for them, and re-layouts  1.64 us (5%)
    ppermute x4, starting transfers between devices, along(): return lax.ppermute(rows, ('blk', 'pair'), hops)  9.42 us
    ppermute x6, starting transfers between devices, across(): return lax.ppermute(rows, ('sub', 'pair'), [(0, 3), (1, 2), (2, 1), (3, 0)])  6.7 us
    pallas_call x6, Pallas kernels, call(): pl.pallas_call(kernel, out_shape=[jax.ShapeDtypeStruct(shape, dtype) for...  4.16 us
    ppermute x6, waiting for transfers between devices, across(): return lax.ppermute(rows, ('sub', 'pair'), [(0, 3), (1, 2), (2, 1), (3, 0)])  4.09 us
    ppermute x9, starting transfers between devices, other_core(): return lax.ppermute(rows, 'pair', [(0, 1), (1, 0)])  2.83 us
    ppermute x4, waiting for transfers between devices, along(): return lax.ppermute(rows, ('blk', 'pair'), hops)  2.39 us
    unnamed x6, local copies, waits for them, and re-layouts  1.64 us
    pallas_call x1, Pallas kernels, finish(): pl.pallas_call(last_kernel, out_shape=jax.ShapeDtypeStruct(shape, BF16),...  1.03 us
  transfers between devices with their start and end apart: 20, of which 6 were waited for; matrix products, arithmetic and copies ran while one was open for 0% of the time, Pallas kernels for 12%

profile of v32, /device:TPU:0, one launch (start us, length us, event | category | flops | bytes accessed | tf_op | source)
XLA Modules:
  0.0 35.1 jit_solution(14124882569843210488)
XLA Ops:
  0.0 0.0 copy-start
  0.0 1.0 %copy-done = bf16[192,768]{1,0:T(8,128)(2,1)S(1)} copy-done((bf16[192,768]{1,0:T(8,128)(2,1)S(1)}, bf16[192,768]{1,0:T(8,128)(2,1)}, u32[]{:S(2)}) %copy-start) | copy-done | bytes 294936
  1.0 0.0 copy-start.2
  1.0 2.4 %collective-permute-start.2 = (bf16[592,128]{1,0:T(8,128)(2,1)S(1)}, bf16[592,128]{1,0:T(8,128)(2,1)S(1)}, u32[]{:S(2)}, u32[]{:S(2)}) collective-permute-start(bf16[592,128]{1,0:T(8,128)(2,1)S(1)} %shard_map.38.refs_0_), channel_id=1, source_target_pairs={{0,3},{1,2},{2,1},{3,0},{4,7},{5,6},{6,5},{7,4},{8,11},{9,10},{10,... | collective-permute-start | bytes 454664 | tf_op jit(solution)/shard_map/ppermute | solution.py:353
  3.4 2.9 %collective-permute-start.1 = (bf16[592,128]{1,0:T(8,128)(2,1)S(1)}, bf16[592,128]{1,0:T(8,128)(2,1)S(1)}, u32[]{:S(2)}, u32[]{:S(2)}) collective-permute-start(bf16[592,128]{1,0:T(8,128)(2,1)S(1)} %shard_map.38.refs_0_), channel_id=1, source_target_pairs={{4,1},{5,0},{0,9},{1,8},{8,13},{9,12},{12,5},{13,4},{6,3},{7,2},{2... | collective-permute-start | bytes 454664 | tf_op jit(solution)/shard_map/ppermute | solution.py:342
  6.3 0.0 copy-start.1
  6.3 0.0 copy-done.2
  6.3 0.7 %copy-done.1 = s32[192,1]{0,1:T(1,128)S(1)} copy-done((s32[192,1]{0,1:T(1,128)S(1)}, s32[192,1]{0,1:T(1,128)}, u32[]{:S(2)}) %copy-start.1) | copy-done | bytes 792
  7.0 0.1 shard_map.37
  7.1 0.1 collective-permute-start.4
  7.2 1.8 %collective-permute-start.3 = (bf16[592,128]{1,0:T(8,128)(2,1)S(1)}, bf16[592,128]{1,0:T(8,128)(2,1)S(1)}, u32[]{:S(2)}, u32[]{:S(2)}) collective-permute-start(bf16[592,128]{1,0:T(8,128)(2,1)S(1)} %get-tuple-element.32.refs_1_), channel_id=1, source_target_pairs={{4,1},{5,0},{0,9},{1,8},{8,13},{9,12},{12,5},{13,4},{6,3},{7,2},{2... | collective-permute-start | bytes 454664 | tf_op jit(solution)/shard_map/ppermute | solution.py:342
  9.0 0.0 collective-permute-done.2.refs_0_.refs_2_
  9.0 1.3 %collective-permute-done.1.refs_4_.near_first = bf16[592,128]{1,0:T(8,128)(2,1)S(1)} collective-permute-done((bf16[592,128]{1,0:T(8,128)(2,1)S(1)}, bf16[592,128]{1,0:T(8,128)(2,1)S(1)}, u32[]{:S(2)}, u32[]{:S(2)}) %collective-permute-start.1) | collective-permute-done | bytes 151584 | tf_op jit(solution)/shard_map/ppermute | solution.py:342
  10.2 0.0 collective-permute-start.6
  10.2 3.1 %collective-permute-start.5 = (bf16[592,128]{1,0:T(8,128)(2,1)S(1)}, bf16[592,128]{1,0:T(8,128)(2,1)S(1)}, u32[]{:S(2)}, u32[]{:S(2)}) collective-permute-start(bf16[592,128]{1,0:T(8,128)(2,1)S(1)} %collective-permute-done.1.refs_4_.near_first), channel_id=1, source_target_pairs={{4,1},{5,0},{0,9},{1,8},{8,13},{9,12},{12,5},{13,4},{6,3},{7,2},{2... | collective-permute-start | bytes 454664 | tf_op jit(solution)/shard_map/ppermute | solution.py:342
  13.3 0.0 collective-permute-start.11
  13.3 0.0 collective-permute-done.4.refs_1_.refs_3_
  13.4 0.0 collective-permute-done.3.refs_5_.near_second
  13.4 0.5 %collective-permute-start.12 = (bf16[592,128]{1,0:T(8,128)(2,1)S(1)}, bf16[592,128]{1,0:T(8,128)(2,1)S(1)}, u32[]{:S(2)}, u32[]{:S(2)}) collective-permute-start(bf16[592,128]{1,0:T(8,128)(2,1)S(1)} %collective-permute-done.3.refs_5_.near_second), channel_id=1, source_target_pairs={{0,1},{1,0},{2,3},{3,2},{4,5},{5,4},{6,7},{7,6},{8,9},{9,8},{10,11... | collective-permute-start | bytes 454664 | tf_op jit(solution)/shard_map/ppermute | solution.py:356
  13.8 1.7 %collective-permute-start.8 = (bf16[592,128]{1,0:T(8,128)(2,1)S(1)}, bf16[592,128]{1,0:T(8,128)(2,1)S(1)}, u32[]{:S(2)}, u32[]{:S(2)}) collective-permute-start(bf16[592,128]{1,0:T(8,128)(2,1)S(1)} %collective-permute-done.3.refs_5_.near_second), channel_id=1, source_target_pairs={{0,3},{1,2},{2,1},{3,0},{4,7},{5,6},{6,5},{7,4},{8,11},{9,10},{10,... | collective-permute-start | bytes 454664 | tf_op jit(solution)/shard_map/ppermute | solution.py:353
  15.6 1.0 %collective-permute-done.6.refs_2_ = bf16[592,128]{1,0:T(8,128)(2,1)S(1)} collective-permute-done((bf16[592,128]{1,0:T(8,128)(2,1)S(1)}, bf16[592,128]{1,0:T(8,128)(2,1)S(1)}, u32[]{:S(2)}, u32[]{:S(2)}) %collective-permute-start.6) | collective-permute-done | bytes 151584 | tf_op jit(solution)/shard_map/ppermute | solution.py:353
  16.6 1.7 %collective-permute-start.7 = (bf16[592,128]{1,0:T(8,128)(2,1)S(1)}, bf16[592,128]{1,0:T(8,128)(2,1)S(1)}, u32[]{:S(2)}, u32[]{:S(2)}) collective-permute-start(bf16[592,128]{1,0:T(8,128)(2,1)S(1)} %collective-permute-done.3.refs_5_.near_second), channel_id=1, source_target_pairs={{4,1},{5,0},{0,9},{1,8},{8,13},{9,12},{12,5},{13,4},{6,3},{7,2},{2... | collective-permute-start | bytes 454664 | tf_op jit(solution)/shard_map/ppermute | solution.py:342
  18.3 0.0 collective-permute-done.5.refs_0_
  18.3 1.1 %collective-permute-start.9 = (bf16[592,128]{1,0:T(8,128)(2,1)S(1)}, bf16[592,128]{1,0:T(8,128)(2,1)S(1)}, u32[]{:S(2)}, u32[]{:S(2)}) collective-permute-start(bf16[592,128]{1,0:T(8,128)(2,1)S(1)} %collective-permute-done.5.refs_0_), channel_id=1, source_target_pairs={{0,3},{1,2},{2,1},{3,0},{4,7},{5,6},{6,5},{7,4},{8,11},{9,10},{10,... | collective-permute-start | bytes 454664 | tf_op jit(solution)/shard_map/ppermute | solution.py:353
  19.4 0.0 collective-permute-done.11.over_first
  19.4 0.3 collective-permute-start
  19.7 0.0 collective-permute-done.12.over_second
  19.7 1.1 %shard_map.41 = (f32[192,896]{1,0:T(8,128)S(1)}, bf16[64,896]{1,0:T(8,128)(2,1)S(1)}, bf16[64,896]{1,0:T(8,128)(2,1)S(1)}, bf16[64,896]{1,0:T(8,128)(2,1)S(1)}) custom-call(bf16[592,128]{1,0:T(8,128)(2,1)S(1)} %collective-permute-done.1.refs_4_.near_first, bf16[592,128]{1,0:T(8,128)(2,1)S(1)} %collective-permute-done.3.refs_5_.near_second, ...), custom_call_target="tpu_custom_call" | custom-call | tf_op jit(solution)/shard_map/pallas_call | solution.py:284
  20.8 0.3 collective-permute-start.13
  21.1 0.0 collective-permute-done.8.refs_3_
  21.1 0.3 collective-permute-start.14
  21.4 1.1 %collective-permute-done.7.refs_1_ = bf16[592,128]{1,0:T(8,128)(2,1)S(1)} collective-permute-done((bf16[592,128]{1,0:T(8,128)(2,1)S(1)}, bf16[592,128]{1,0:T(8,128)(2,1)S(1)}, u32[]{:S(2)}, u32[]{:S(2)}) %collective-permute-start.7) | collective-permute-done | bytes 151584 | tf_op jit(solution)/shard_map/ppermute | solution.py:342
  22.5 0.4 %collective-permute-start.15 = (bf16[64,896]{1,0:T(8,128)(2,1)S(1)}, bf16[64,896]{1,0:T(8,128)(2,1)S(1)}, u32[]{:S(2)}, u32[]{:S(2)}) collective-permute-start(bf16[64,896]{1,0:T(8,128)(2,1)S(1)} %get-tuple-element.51), channel_id=1, source_target_pairs={{0,1},{1,0},{2,3},{3,2},{4,5},{5,4},{6,7},{7,6},{8,9},{9,8},{10,11... | collective-permute-start | bytes 344072 | tf_op jit(solution)/shard_map/ppermute | solution.py:356
  23.0 0.0 collective-permute-done.13.refs_0_
  23.0 0.0 collective-permute-done.14.refs_1_
  23.0 1.0 %collective-permute-done.15.refs_2_ = bf16[64,896]{1,0:T(8,128)(2,1)S(1)} collective-permute-done((bf16[64,896]{1,0:T(8,128)(2,1)S(1)}, bf16[64,896]{1,0:T(8,128)(2,1)S(1)}, u32[]{:S(2)}, u32[]{:S(2)}) %collective-permute-start.15) | collective-permute-done | bytes 114720 | tf_op jit(solution)/shard_map/ppermute | solution.py:356
  23.9 0.3 shard_map.42
  24.2 0.8 %collective-permute-start.16 = (bf16[1168,128]{1,0:T(8,128)(2,1)S(1)}, bf16[1168,128]{1,0:T(8,128)(2,1)S(1)}, u32[]{:S(2)}, u32[]{:S(2)}) collective-permute-start(bf16[1168,128]{1,0:T(8,128)(2,1)S(1)} %shard_map.42), channel_id=1, source_target_pairs={{0,5},{1,4},{8,1},{9,0},{12,9},{13,8},{4,13},{5,12},{2,7},{3,6},{1... | collective-permute-start | bytes 897032 | tf_op jit(solution)/shard_map/ppermute | solution.py:350
  25.1 0.0 collective-permute-done.9.refs_2_
  25.1 1.3 %collective-permute-start.10 = (bf16[592,128]{1,0:T(8,128)(2,1)S(1)}, bf16[592,128]{1,0:T(8,128)(2,1)S(1)}, u32[]{:S(2)}, u32[]{:S(2)}) collective-permute-start(bf16[592,128]{1,0:T(8,128)(2,1)S(1)} %collective-permute-done.7.refs_1_), channel_id=1, source_target_pairs={{0,3},{1,2},{2,1},{3,0},{4,7},{5,6},{6,5},{7,4},{8,11},{9,10},{10,... | collective-permute-start | bytes 454664 | tf_op jit(solution)/shard_map/ppermute | solution.py:353
  26.4 0.0 collective-permute-done.other
  26.4 1.5 %shard_map.39 = (f32[192,896]{1,0:T(8,128)S(1)}, f32[192,896]{1,0:T(8,128)S(1)}, f32[384,128]{1,0:T(8,128)S(1)}) custom-call(bf16[1168,128]{1,0:T(8,128)(2,1)S(1)} %get-tuple-element.30.own, bf16[1168,128]{1,0:T(8,128)(2,1)S(1)} %collective-permute-done.other, bf16[592,128]{1,0:T(8,128)(2,1)S(1)} %collective-permute-done.2.refs_0_.refs_2_, ...), custom_call_target="tpu_custom_call" | custom-call | tf_op jit(solution)/shard_map/pallas_call | solution.py:284
  27.9 3.0 %collective-permute-done.10.refs_3_ = bf16[592,128]{1,0:T(8,128)(2,1)S(1)} collective-permute-done((bf16[592,128]{1,0:T(8,128)(2,1)S(1)}, bf16[592,128]{1,0:T(8,128)(2,1)S(1)}, u32[]{:S(2)}, u32[]{:S(2)}) %collective-permute-start.10) | collective-permute-done | bytes 151584 | tf_op jit(solution)/shard_map/ppermute | solution.py:353
  30.9 1.1 %shard_map.40 = (f32[192,896]{1,0:T(8,128)S(1)}, bf16[64,896]{1,0:T(8,128)(2,1)S(1)}, bf16[64,896]{1,0:T(8,128)(2,1)S(1)}, bf16[64,896]{1,0:T(8,128)(2,1)S(1)}) custom-call(bf16[1168,128]{1,0:T(8,128)(2,1)S(1)} %get-tuple-element.30.own, bf16[1168,128]{1,0:T(8,128)(2,1)S(1)} %collective-permute-done.other, ...), custom_call_target="tpu_custom_call", output_to_operand_aliasing={{0}: (7, {})} | custom-call | tf_op jit(solution)/shard_map/pallas_call | solution.py:284
  32.0 0.5 %collective-permute-start.17 = (bf16[64,896]{1,0:T(8,128)(2,1)S(1)}, bf16[64,896]{1,0:T(8,128)(2,1)S(1)}, u32[]{:S(2)}, u32[]{:S(2)}) collective-permute-start(bf16[64,896]{1,0:T(8,128)(2,1)S(1)} %get-tuple-element.52), channel_id=1, source_target_pairs={{0,1},{1,0},{2,3},{3,2},{4,5},{5,4},{6,7},{7,6},{8,9},{9,8},{10,11... | collective-permute-start | bytes 344072 | tf_op jit(solution)/shard_map/ppermute | solution.py:356
  32.6 0.1 collective-permute-start.18
  32.6 0.4 %collective-permute-start.19 = (bf16[64,896]{1,0:T(8,128)(2,1)S(1)}, bf16[64,896]{1,0:T(8,128)(2,1)S(1)}, u32[]{:S(2)}, u32[]{:S(2)}) collective-permute-start(bf16[64,896]{1,0:T(8,128)(2,1)S(1)} %get-tuple-element.54), channel_id=1, source_target_pairs={{0,1},{1,0},{2,3},{3,2},{4,5},{5,4},{6,7},{7,6},{8,9},{9,8},{10,11... | collective-permute-start | bytes 344072 | tf_op jit(solution)/shard_map/ppermute | solution.py:356
  33.1 1.0 %collective-permute-done.16.returned = bf16[1168,128]{1,0:T(8,128)(2,1)S(1)} collective-permute-done((bf16[1168,128]{1,0:T(8,128)(2,1)S(1)}, bf16[1168,128]{1,0:T(8,128)(2,1)S(1)}, u32[]{:S(2)}, u32[]{:S(2)}) %collective-permute-start.16) | collective-permute-done | bytes 299040 | tf_op jit(solution)/shard_map/ppermute | solution.py:350
  34.1 0.0 collective-permute-done.17.refs_0_
  34.1 0.0 collective-permute-done.18.refs_1_
  34.1 0.0 collective-permute-done.19.refs_2_
  34.1 1.0 %shard_map.43 = bf16[192,768]{1,0:T(8,128)(2,1)} custom-call(f32[192,896]{1,0:T(8,128)S(1)} %get-tuple-element.45.mine, bf16[1168,128]{1,0:T(8,128)(2,1)S(1)} %collective-permute-done.16.returned, bf16[64,896]{1,0:T(8,128)(2,1)S(1)} %collective-permute-done.17.refs_0_, bf16[64,896]{1,0:T(8,128)(2,1)S(1)} %collective-permute-done.18.refs_1_, ...), custom_call_target="tpu_custom_call" | custom-call | tf_op jit(solution)/shard_map/pallas_call | solution.py:310
  (1 shorter events, 0.0 us)
Async XLA Ops:
  0.0 1.0 %copy-start = (bf16[192,768]{1,0:T(8,128)(2,1)S(1)}, bf16[192,768]{1,0:T(8,128)(2,1)}, u32[]{:S(2)}) copy-start(bf16[192,768]{1,0:T(8,128)(2,1)} %rows.3) | copy-start | bytes 884740
  1.0 5.3 %copy-start.2 = (s32[192]{0:T(256)S(1)}, s32[192]{0:T(256)}, u32[]{:S(2)}) copy-start(s32[192]{0:T(256)} %param.5) | copy-start | bytes 2308
  1.0 8.0 %collective-permute-start.2 = (bf16[592,128]{1,0:T(8,128)(2,1)S(1)}, bf16[592,128]{1,0:T(8,128)(2,1)S(1)}, u32[]{:S(2)}, u32[]{:S(2)}) collective-permute-start(bf16[592,128]{1,0:T(8,128)(2,1)S(1)} %shard_map.38.refs_0_), channel_id=1, source_target_pairs={{0,3},{1,2},{2,1},{3,0},{4,7},{5,6},{6,5},{7,4},{8,11},{9,10},{10,... | collective-permute-start | bytes 454664 | tf_op jit(solution)/shard_map/ppermute | solution.py:353
  3.4 6.8 %collective-permute-start.1 = (bf16[592,128]{1,0:T(8,128)(2,1)S(1)}, bf16[592,128]{1,0:T(8,128)(2,1)S(1)}, u32[]{:S(2)}, u32[]{:S(2)}) collective-permute-start(bf16[592,128]{1,0:T(8,128)(2,1)S(1)} %shard_map.38.refs_0_), channel_id=1, source_target_pairs={{4,1},{5,0},{0,9},{1,8},{8,13},{9,12},{12,5},{13,4},{6,3},{7,2},{2... | collective-permute-start | bytes 454664 | tf_op jit(solution)/shard_map/ppermute | solution.py:342
  6.3 0.7 %copy-start.1 = (s32[192,1]{0,1:T(1,128)S(1)}, s32[192,1]{0,1:T(1,128)}, u32[]{:S(2)}) copy-start(s32[192,1]{0,1:T(1,128)} %param.4) | copy-start | bytes 2308
  7.1 6.3 %collective-permute-start.4 = (bf16[592,128]{1,0:T(8,128)(2,1)S(1)}, bf16[592,128]{1,0:T(8,128)(2,1)S(1)}, u32[]{:S(2)}, u32[]{:S(2)}) collective-permute-start(bf16[592,128]{1,0:T(8,128)(2,1)S(1)} %get-tuple-element.32.refs_1_), channel_id=1, source_target_pairs={{0,3},{1,2},{2,1},{3,0},{4,7},{5,6},{6,5},{7,4},{8,11},{9,10},{10,... | collective-permute-start | bytes 454664 | tf_op jit(solution)/shard_map/ppermute | solution.py:353
  7.2 6.2 %collective-permute-start.3 = (bf16[592,128]{1,0:T(8,128)(2,1)S(1)}, bf16[592,128]{1,0:T(8,128)(2,1)S(1)}, u32[]{:S(2)}, u32[]{:S(2)}) collective-permute-start(bf16[592,128]{1,0:T(8,128)(2,1)S(1)} %get-tuple-element.32.refs_1_), channel_id=1, source_target_pairs={{4,1},{5,0},{0,9},{1,8},{8,13},{9,12},{12,5},{13,4},{6,3},{7,2},{2... | collective-permute-start | bytes 454664 | tf_op jit(solution)/shard_map/ppermute | solution.py:342
  10.2 6.4 %collective-permute-start.6 = (bf16[592,128]{1,0:T(8,128)(2,1)S(1)}, bf16[592,128]{1,0:T(8,128)(2,1)S(1)}, u32[]{:S(2)}, u32[]{:S(2)}) collective-permute-start(bf16[592,128]{1,0:T(8,128)(2,1)S(1)} %collective-permute-done.1.refs_4_.near_first), channel_id=1, source_target_pairs={{0,3},{1,2},{2,1},{3,0},{4,7},{5,6},{6,5},{7,4},{8,11},{9,10},{10,... | collective-permute-start | bytes 454664 | tf_op jit(solution)/shard_map/ppermute | solution.py:353
  10.2 8.1 %collective-permute-start.5 = (bf16[592,128]{1,0:T(8,128)(2,1)S(1)}, bf16[592,128]{1,0:T(8,128)(2,1)S(1)}, u32[]{:S(2)}, u32[]{:S(2)}) collective-permute-start(bf16[592,128]{1,0:T(8,128)(2,1)S(1)} %collective-permute-done.1.refs_4_.near_first), channel_id=1, source_target_pairs={{4,1},{5,0},{0,9},{1,8},{8,13},{9,12},{12,5},{13,4},{6,3},{7,2},{2... | collective-permute-start | bytes 454664 | tf_op jit(solution)/shard_map/ppermute | solution.py:342
  13.3 6.1 %collective-permute-start.11 = (bf16[592,128]{1,0:T(8,128)(2,1)S(1)}, bf16[592,128]{1,0:T(8,128)(2,1)S(1)}, u32[]{:S(2)}, u32[]{:S(2)}) collective-permute-start(bf16[592,128]{1,0:T(8,128)(2,1)S(1)} %collective-permute-done.1.refs_4_.near_first), channel_id=1, source_target_pairs={{0,1},{1,0},{2,3},{3,2},{4,5},{5,4},{6,7},{7,6},{8,9},{9,8},{10,11... | collective-permute-start | bytes 454664 | tf_op jit(solution)/shard_map/ppermute | solution.py:356
  13.4 6.3 %collective-permute-start.12 = (bf16[592,128]{1,0:T(8,128)(2,1)S(1)}, bf16[592,128]{1,0:T(8,128)(2,1)S(1)}, u32[]{:S(2)}, u32[]{:S(2)}) collective-permute-start(bf16[592,128]{1,0:T(8,128)(2,1)S(1)} %collective-permute-done.3.refs_5_.near_second), channel_id=1, source_target_pairs={{0,1},{1,0},{2,3},{3,2},{4,5},{5,4},{6,7},{7,6},{8,9},{9,8},{10,11... | collective-permute-start | bytes 454664 | tf_op jit(solution)/shard_map/ppermute | solution.py:356
  13.8 7.3 %collective-permute-start.8 = (bf16[592,128]{1,0:T(8,128)(2,1)S(1)}, bf16[592,128]{1,0:T(8,128)(2,1)S(1)}, u32[]{:S(2)}, u32[]{:S(2)}) collective-permute-start(bf16[592,128]{1,0:T(8,128)(2,1)S(1)} %collective-permute-done.3.refs_5_.near_second), channel_id=1, source_target_pairs={{0,3},{1,2},{2,1},{3,0},{4,7},{5,6},{6,5},{7,4},{8,11},{9,10},{10,... | collective-permute-start | bytes 454664 | tf_op jit(solution)/shard_map/ppermute | solution.py:353
  16.6 5.9 %collective-permute-start.7 = (bf16[592,128]{1,0:T(8,128)(2,1)S(1)}, bf16[592,128]{1,0:T(8,128)(2,1)S(1)}, u32[]{:S(2)}, u32[]{:S(2)}) collective-permute-start(bf16[592,128]{1,0:T(8,128)(2,1)S(1)} %collective-permute-done.3.refs_5_.near_second), channel_id=1, source_target_pairs={{4,1},{5,0},{0,9},{1,8},{8,13},{9,12},{12,5},{13,4},{6,3},{7,2},{2... | collective-permute-start | bytes 454664 | tf_op jit(solution)/shard_map/ppermute | solution.py:342
  18.3 6.8 %collective-permute-start.9 = (bf16[592,128]{1,0:T(8,128)(2,1)S(1)}, bf16[592,128]{1,0:T(8,128)(2,1)S(1)}, u32[]{:S(2)}, u32[]{:S(2)}) collective-permute-start(bf16[592,128]{1,0:T(8,128)(2,1)S(1)} %collective-permute-done.5.refs_0_), channel_id=1, source_target_pairs={{0,3},{1,2},{2,1},{3,0},{4,7},{5,6},{6,5},{7,4},{8,11},{9,10},{10,... | collective-permute-start | bytes 454664 | tf_op jit(solution)/shard_map/ppermute | solution.py:353
  19.4 7.0 %collective-permute-start = (bf16[1168,128]{1,0:T(8,128)(2,1)S(1)}, bf16[1168,128]{1,0:T(8,128)(2,1)S(1)}, u32[]{:S(2)}, u32[]{:S(2)}) collective-permute-start(bf16[1168,128]{1,0:T(8,128)(2,1)S(1)} %get-tuple-element.30.own), channel_id=1, source_target_pairs={{0,1},{1,0},{2,3},{3,2},{4,5},{5,4},{6,7},{7,6},{8,9},{9,8},{10,11... | collective-permute-start | bytes 897032 | tf_op jit(solution)/shard_map/ppermute | solution.py:356
  20.8 2.1 %collective-permute-start.13 = (bf16[64,896]{1,0:T(8,128)(2,1)S(1)}, bf16[64,896]{1,0:T(8,128)(2,1)S(1)}, u32[]{:S(2)}, u32[]{:S(2)}) collective-permute-start(bf16[64,896]{1,0:T(8,128)(2,1)S(1)} %get-tuple-element.49), channel_id=1, source_target_pairs={{0,1},{1,0},{2,3},{3,2},{4,5},{5,4},{6,7},{7,6},{8,9},{9,8},{10,11... | collective-permute-start | bytes 344072 | tf_op jit(solution)/shard_map/ppermute | solution.py:356
  21.1 1.9 %collective-permute-start.14 = (bf16[64,896]{1,0:T(8,128)(2,1)S(1)}, bf16[64,896]{1,0:T(8,128)(2,1)S(1)}, u32[]{:S(2)}, u32[]{:S(2)}) collective-permute-start(bf16[64,896]{1,0:T(8,128)(2,1)S(1)} %get-tuple-element.50), channel_id=1, source_target_pairs={{0,1},{1,0},{2,3},{3,2},{4,5},{5,4},{6,7},{7,6},{8,9},{9,8},{10,11... | collective-permute-start | bytes 344072 | tf_op jit(solution)/shard_map/ppermute | solution.py:356
  22.5 1.4 %collective-permute-start.15 = (bf16[64,896]{1,0:T(8,128)(2,1)S(1)}, bf16[64,896]{1,0:T(8,128)(2,1)S(1)}, u32[]{:S(2)}, u32[]{:S(2)}) collective-permute-start(bf16[64,896]{1,0:T(8,128)(2,1)S(1)} %get-tuple-element.51), channel_id=1, source_target_pairs={{0,1},{1,0},{2,3},{3,2},{4,5},{5,4},{6,7},{7,6},{8,9},{9,8},{10,11... | collective-permute-start | bytes 344072 | tf_op jit(solution)/shard_map/ppermute | solution.py:356
  24.2 9.9 %collective-permute-start.16 = (bf16[1168,128]{1,0:T(8,128)(2,1)S(1)}, bf16[1168,128]{1,0:T(8,128)(2,1)S(1)}, u32[]{:S(2)}, u32[]{:S(2)}) collective-permute-start(bf16[1168,128]{1,0:T(8,128)(2,1)S(1)} %shard_map.42), channel_id=1, source_target_pairs={{0,5},{1,4},{8,1},{9,0},{12,9},{13,8},{4,13},{5,12},{2,7},{3,6},{1... | collective-permute-start | bytes 897032 | tf_op jit(solution)/shard_map/ppermute | solution.py:350
  25.1 5.9 %collective-permute-start.10 = (bf16[592,128]{1,0:T(8,128)(2,1)S(1)}, bf16[592,128]{1,0:T(8,128)(2,1)S(1)}, u32[]{:S(2)}, u32[]{:S(2)}) collective-permute-start(bf16[592,128]{1,0:T(8,128)(2,1)S(1)} %collective-permute-done.7.refs_1_), channel_id=1, source_target_pairs={{0,3},{1,2},{2,1},{3,0},{4,7},{5,6},{6,5},{7,4},{8,11},{9,10},{10,... | collective-permute-start | bytes 454664 | tf_op jit(solution)/shard_map/ppermute | solution.py:353
  32.0 2.0 %collective-permute-start.17 = (bf16[64,896]{1,0:T(8,128)(2,1)S(1)}, bf16[64,896]{1,0:T(8,128)(2,1)S(1)}, u32[]{:S(2)}, u32[]{:S(2)}) collective-permute-start(bf16[64,896]{1,0:T(8,128)(2,1)S(1)} %get-tuple-element.52), channel_id=1, source_target_pairs={{0,1},{1,0},{2,3},{3,2},{4,5},{5,4},{6,7},{7,6},{8,9},{9,8},{10,11... | collective-permute-start | bytes 344072 | tf_op jit(solution)/shard_map/ppermute | solution.py:356
  32.6 1.5 %collective-permute-start.18 = (bf16[64,896]{1,0:T(8,128)(2,1)S(1)}, bf16[64,896]{1,0:T(8,128)(2,1)S(1)}, u32[]{:S(2)}, u32[]{:S(2)}) collective-permute-start(bf16[64,896]{1,0:T(8,128)(2,1)S(1)} %get-tuple-element.53), channel_id=1, source_target_pairs={{0,1},{1,0},{2,3},{3,2},{4,5},{5,4},{6,7},{7,6},{8,9},{9,8},{10,11... | collective-permute-start | bytes 344072 | tf_op jit(solution)/shard_map/ppermute | solution.py:356
  32.6 1.4 %collective-permute-start.19 = (bf16[64,896]{1,0:T(8,128)(2,1)S(1)}, bf16[64,896]{1,0:T(8,128)(2,1)S(1)}, u32[]{:S(2)}, u32[]{:S(2)}) collective-permute-start(bf16[64,896]{1,0:T(8,128)(2,1)S(1)} %get-tuple-element.54), channel_id=1, source_target_pairs={{0,1},{1,0},{2,3},{3,2},{4,5},{5,4},{6,7},{7,6},{8,9},{9,8},{10,11... | collective-permute-start | bytes 344072 | tf_op jit(solution)/shard_map/ppermute | solution.py:356

commit v33 on v32

--- a/solution.py
+++ b/solution.py
@@ -379,7 +379,7 @@
         + [((rows_here // PARTS, width + 128), BF16)] * PARTS,
         [*near, *over, first, second, *across_by[0]],
     )
-    near_sum, _ = together(near_sum, along_by[2][1])
+    over_sum[-1], _ = together(over_sum[-1], along_by[2][1])
     (to_return,) = call(
         back_sum_kernel,
         [((slabs * rows_here + LINES, 128), BF16)],

time: 35.3 us -> 36.9 us (1.045)
  waiting for transfers between devices: 8.46 us -> 9.75 us
    ppermute x1, starting transfers between devices: 0.83 us -> 2.17 us  [back_along(): return lax.ppermute(rows, ('blk', 'pair'), hops)]
    ppermute x1, waiting for transfers between devices: 1 us -> 0.01 us  [back_along(): return lax.ppermute(rows, ('blk', 'pair'), hops)]
    ppermute x6, waiting for transfers between devices: 4.09 us -> 5.08 us  [across(): return lax.ppermute(rows, ('sub', 'pair'), [(0, 3), (1, 2), (2, 1), (3, 0)])]
    ppermute x9, waiting for transfers between devices: 0.98 us -> 1.96 us  [other_core(): return lax.ppermute(rows, 'pair', [(0, 1), (1, 0)])]
    ppermute x4, starting transfers between devices: 9.42 us -> 8.85 us  [along(): return lax.ppermute(rows, ('blk', 'pair'), hops)]
  transfers between devices with their start and end apart: 20 -> 20, of which waited for: 6 -> 12; matrix products, arithmetic and copies ran while one was open for 0% -> 0% of each run, Pallas kernels for 12% -> 11%
where the time goes in v33:
time: 36.9 us; the launch traced here: 36.7 us
  starting transfers between devices  20.1 us (54%)
  waiting for transfers between devices  9.75 us (26%)
  Pallas kernels  5.19 us (14%)
  local copies, waits for them, and re-layouts  1.64 us (4%)
    ppermute x4, starting transfers between devices, along(): return lax.ppermute(rows, ('blk', 'pair'), hops)  8.85 us
    ppermute x6, starting transfers between devices, across(): return lax.ppermute(rows, ('sub', 'pair'), [(0, 3), (1, 2), (2, 1), (3, 0)])  6.37 us
    ppermute x6, waiting for transfers between devices, across(): return lax.ppermute(rows, ('sub', 'pair'), [(0, 3), (1, 2), (2, 1), (3, 0)])  5.08 us
    pallas_call x6, Pallas kernels, call(): pl.pallas_call(kernel, out_shape=[jax.ShapeDtypeStruct(shape, dtype) for...  4.17 us
    ppermute x4, waiting for transfers between devices, along(): return lax.ppermute(rows, ('blk', 'pair'), hops)  2.71 us
    ppermute x9, starting transfers between devices, other_core(): return lax.ppermute(rows, 'pair', [(0, 1), (1, 0)])  2.67 us
    ppermute x1, starting transfers between devices, back_along(): return lax.ppermute(rows, ('blk', 'pair'), hops)  2.17 us
    ppermute x9, waiting for transfers between devices, other_core(): return lax.ppermute(rows, 'pair', [(0, 1), (1, 0)])  1.96 us
  transfers between devices with their start and end apart: 20, of which 12 were waited for; matrix products, arithmetic and copies ran while one was open for 0% of the time, Pallas kernels for 11%

profile of v33, /device:TPU:0, one launch (start us, length us, event | category | flops | bytes accessed | tf_op | source)
XLA Modules:
  0.0 36.7 jit_solution(1763907597718621436)
XLA Ops:
  0.0 0.0 copy-start
  0.0 1.0 %copy-done = bf16[192,768]{1,0:T(8,128)(2,1)S(1)} copy-done((bf16[192,768]{1,0:T(8,128)(2,1)S(1)}, bf16[192,768]{1,0:T(8,128)(2,1)}, u32[]{:S(2)}) %copy-start) | copy-done | bytes 294936
  1.0 0.0 copy-start.2
  1.0 2.4 %collective-permute-start.2 = (bf16[592,128]{1,0:T(8,128)(2,1)S(1)}, bf16[592,128]{1,0:T(8,128)(2,1)S(1)}, u32[]{:S(2)}, u32[]{:S(2)}) collective-permute-start(bf16[592,128]{1,0:T(8,128)(2,1)S(1)} %shard_map.38.refs_0_), channel_id=1, source_target_pairs={{0,3},{1,2},{2,1},{3,0},{4,7},{5,6},{6,5},{7,4},{8,11},{9,10},{10,... | collective-permute-start | bytes 454664 | tf_op jit(solution)/shard_map/ppermute | solution.py:353
  3.4 2.9 %collective-permute-start.1 = (bf16[592,128]{1,0:T(8,128)(2,1)S(1)}, bf16[592,128]{1,0:T(8,128)(2,1)S(1)}, u32[]{:S(2)}, u32[]{:S(2)}) collective-permute-start(bf16[592,128]{1,0:T(8,128)(2,1)S(1)} %shard_map.38.refs_0_), channel_id=1, source_target_pairs={{4,1},{5,0},{0,9},{1,8},{8,13},{9,12},{12,5},{13,4},{6,3},{7,2},{2... | collective-permute-start | bytes 454664 | tf_op jit(solution)/shard_map/ppermute | solution.py:342
  6.3 0.0 copy-start.1
  6.3 0.0 copy-done.2
  6.3 0.7 %copy-done.1 = s32[192,1]{0,1:T(1,128)S(1)} copy-done((s32[192,1]{0,1:T(1,128)S(1)}, s32[192,1]{0,1:T(1,128)}, u32[]{:S(2)}) %copy-start.1) | copy-done | bytes 792
  7.0 0.1 shard_map.37
  7.1 0.1 collective-permute-start.4
  7.2 1.8 %collective-permute-start.3 = (bf16[592,128]{1,0:T(8,128)(2,1)S(1)}, bf16[592,128]{1,0:T(8,128)(2,1)S(1)}, u32[]{:S(2)}, u32[]{:S(2)}) collective-permute-start(bf16[592,128]{1,0:T(8,128)(2,1)S(1)} %get-tuple-element.32.refs_1_), channel_id=1, source_target_pairs={{4,1},{5,0},{0,9},{1,8},{8,13},{9,12},{12,5},{13,4},{6,3},{7,2},{2... | collective-permute-start | bytes 454664 | tf_op jit(solution)/shard_map/ppermute | solution.py:342
  9.0 0.0 collective-permute-done.2.refs_0_.refs_2_
  9.0 1.3 %collective-permute-done.1.refs_4_.near_first = bf16[592,128]{1,0:T(8,128)(2,1)S(1)} collective-permute-done((bf16[592,128]{1,0:T(8,128)(2,1)S(1)}, bf16[592,128]{1,0:T(8,128)(2,1)S(1)}, u32[]{:S(2)}, u32[]{:S(2)}) %collective-permute-start.1) | collective-permute-done | bytes 151584 | tf_op jit(solution)/shard_map/ppermute | solution.py:342
  10.2 0.0 collective-permute-start.6
  10.2 3.1 %collective-permute-start.5 = (bf16[592,128]{1,0:T(8,128)(2,1)S(1)}, bf16[592,128]{1,0:T(8,128)(2,1)S(1)}, u32[]{:S(2)}, u32[]{:S(2)}) collective-permute-start(bf16[592,128]{1,0:T(8,128)(2,1)S(1)} %collective-permute-done.1.refs_4_.near_first), channel_id=1, source_target_pairs={{4,1},{5,0},{0,9},{1,8},{8,13},{9,12},{12,5},{13,4},{6,3},{7,2},{2... | collective-permute-start | bytes 454664 | tf_op jit(solution)/shard_map/ppermute | solution.py:342
  13.3 0.0 collective-permute-start.11
  13.3 0.0 collective-permute-done.4.refs_1_.refs_3_
  13.4 0.0 collective-permute-done.3.refs_5_.near_second
  13.4 1.8 %collective-permute-start.8 = (bf16[592,128]{1,0:T(8,128)(2,1)S(1)}, bf16[592,128]{1,0:T(8,128)(2,1)S(1)}, u32[]{:S(2)}, u32[]{:S(2)}) collective-permute-start(bf16[592,128]{1,0:T(8,128)(2,1)S(1)} %collective-permute-done.3.refs_5_.near_second), channel_id=1, source_target_pairs={{0,3},{1,2},{2,1},{3,0},{4,7},{5,6},{6,5},{7,4},{8,11},{9,10},{10,... | collective-permute-start | bytes 454664 | tf_op jit(solution)/shard_map/ppermute | solution.py:353
  15.1 1.1 %collective-permute-start.7 = (bf16[592,128]{1,0:T(8,128)(2,1)S(1)}, bf16[592,128]{1,0:T(8,128)(2,1)S(1)}, u32[]{:S(2)}, u32[]{:S(2)}) collective-permute-start(bf16[592,128]{1,0:T(8,128)(2,1)S(1)} %collective-permute-done.3.refs_5_.near_second), channel_id=1, source_target_pairs={{4,1},{5,0},{0,9},{1,8},{8,13},{9,12},{12,5},{13,4},{6,3},{7,2},{2... | collective-permute-start | bytes 454664 | tf_op jit(solution)/shard_map/ppermute | solution.py:342
  16.3 0.3 collective-permute-done.6.refs_2_
  16.6 0.3 collective-permute-start.12
  16.9 0.1 collective-permute-done.5.refs_0_
  17.0 1.2 %collective-permute-start.9 = (bf16[592,128]{1,0:T(8,128)(2,1)S(1)}, bf16[592,128]{1,0:T(8,128)(2,1)S(1)}, u32[]{:S(2)}, u32[]{:S(2)}) collective-permute-start(bf16[592,128]{1,0:T(8,128)(2,1)S(1)} %collective-permute-done.5.refs_0_), channel_id=1, source_target_pairs={{0,3},{1,2},{2,1},{3,0},{4,7},{5,6},{6,5},{7,4},{8,11},{9,10},{10,... | collective-permute-start | bytes 454664 | tf_op jit(solution)/shard_map/ppermute | solution.py:353
  18.1 0.0 collective-permute-done.11.over_first
  18.1 0.0 collective-permute-start
  18.1 1.3 %collective-permute-done.8.refs_3_ = bf16[592,128]{1,0:T(8,128)(2,1)S(1)} collective-permute-done((bf16[592,128]{1,0:T(8,128)(2,1)S(1)}, bf16[592,128]{1,0:T(8,128)(2,1)S(1)}, u32[]{:S(2)}, u32[]{:S(2)}) %collective-permute-start.8) | collective-permute-done | bytes 151584 | tf_op jit(solution)/shard_map/ppermute | solution.py:353
  19.5 1.3 %collective-permute-done.7.refs_1_ = bf16[592,128]{1,0:T(8,128)(2,1)S(1)} collective-permute-done((bf16[592,128]{1,0:T(8,128)(2,1)S(1)}, bf16[592,128]{1,0:T(8,128)(2,1)S(1)}, u32[]{:S(2)}, u32[]{:S(2)}) %collective-permute-start.7) | collective-permute-done | bytes 151584 | tf_op jit(solution)/shard_map/ppermute | solution.py:342
  20.8 0.0 collective-permute-done.12.over_second
  20.8 1.1 %shard_map.41 = (f32[192,896]{1,0:T(8,128)S(1)}, bf16[64,896]{1,0:T(8,128)(2,1)S(1)}, bf16[64,896]{1,0:T(8,128)(2,1)S(1)}, bf16[64,896]{1,0:T(8,128)(2,1)S(1)}) custom-call(bf16[592,128]{1,0:T(8,128)(2,1)S(1)} %collective-permute-done.1.refs_4_.near_first, bf16[592,128]{1,0:T(8,128)(2,1)S(1)} %collective-permute-done.3.refs_5_.near_second, ...), custom_call_target="tpu_custom_call" | custom-call | tf_op jit(solution)/shard_map/pallas_call | solution.py:284
  22.0 0.8 %collective-permute-start.15 = (bf16[64,896]{1,0:T(8,128)(2,1)S(1)}, bf16[64,896]{1,0:T(8,128)(2,1)S(1)}, u32[]{:S(2)}, u32[]{:S(2)}) collective-permute-start(bf16[64,896]{1,0:T(8,128)(2,1)S(1)} %get-tuple-element.51), channel_id=1, source_target_pairs={{0,1},{1,0},{2,3},{3,2},{4,5},{5,4},{6,7},{7,6},{8,9},{9,8},{10,11... | collective-permute-start | bytes 344072 | tf_op jit(solution)/shard_map/ppermute | solution.py:356
  22.7 0.1 collective-permute-start.13
  22.8 0.4 %collective-permute-start.14 = (bf16[64,896]{1,0:T(8,128)(2,1)S(1)}, bf16[64,896]{1,0:T(8,128)(2,1)S(1)}, u32[]{:S(2)}, u32[]{:S(2)}) collective-permute-start(bf16[64,896]{1,0:T(8,128)(2,1)S(1)} %get-tuple-element.49), channel_id=1, source_target_pairs={{0,1},{1,0},{2,3},{3,2},{4,5},{5,4},{6,7},{7,6},{8,9},{9,8},{10,11... | collective-permute-start | bytes 344072 | tf_op jit(solution)/shard_map/ppermute | solution.py:356
  23.2 0.5 %collective-permute-done.15.refs_2_ = bf16[64,896]{1,0:T(8,128)(2,1)S(1)} collective-permute-done((bf16[64,896]{1,0:T(8,128)(2,1)S(1)}, bf16[64,896]{1,0:T(8,128)(2,1)S(1)}, u32[]{:S(2)}, u32[]{:S(2)}) %collective-permute-start.15) | collective-permute-done | bytes 114720 | tf_op jit(solution)/shard_map/ppermute | solution.py:356
  23.7 0.4 collective-permute-done.13.refs_0_
  24.0 0.2 collective-permute-done.14.refs_1_
  24.2 0.3 shard_map.42
  24.5 2.2 %collective-permute-start.16 = (bf16[1168,128]{1,0:T(8,128)(2,1)S(1)}, bf16[1168,128]{1,0:T(8,128)(2,1)S(1)}, u32[]{:S(2)}, u32[]{:S(2)}) collective-permute-start(bf16[1168,128]{1,0:T(8,128)(2,1)S(1)} %shard_map.42), channel_id=1, source_target_pairs={{0,5},{1,4},{8,1},{9,0},{12,9},{13,8},{4,13},{5,12},{2,7},{3,6},{1... | collective-permute-start | bytes 897032 | tf_op jit(solution)/shard_map/ppermute | solution.py:350
  26.7 0.0 collective-permute-done.9.refs_2_
  26.7 0.9 %collective-permute-start.10 = (bf16[592,128]{1,0:T(8,128)(2,1)S(1)}, bf16[592,128]{1,0:T(8,128)(2,1)S(1)}, u32[]{:S(2)}, u32[]{:S(2)}) collective-permute-start(bf16[592,128]{1,0:T(8,128)(2,1)S(1)} %collective-permute-done.7.refs_1_), channel_id=1, source_target_pairs={{0,3},{1,2},{2,1},{3,0},{4,7},{5,6},{6,5},{7,4},{8,11},{9,10},{10,... | collective-permute-start | bytes 454664 | tf_op jit(solution)/shard_map/ppermute | solution.py:353
  27.5 0.0 collective-permute-done.other
  27.5 1.5 %shard_map.39 = (f32[192,896]{1,0:T(8,128)S(1)}, f32[192,896]{1,0:T(8,128)S(1)}, f32[384,128]{1,0:T(8,128)S(1)}) custom-call(bf16[1168,128]{1,0:T(8,128)(2,1)S(1)} %get-tuple-element.30.own, bf16[1168,128]{1,0:T(8,128)(2,1)S(1)} %collective-permute-done.other, bf16[592,128]{1,0:T(8,128)(2,1)S(1)} %collective-permute-done.2.refs_0_.refs_2_, ...), custom_call_target="tpu_custom_call" | custom-call | tf_op jit(solution)/shard_map/pallas_call | solution.py:284
  29.1 3.4 %collective-permute-done.10.refs_3_ = bf16[592,128]{1,0:T(8,128)(2,1)S(1)} collective-permute-done((bf16[592,128]{1,0:T(8,128)(2,1)S(1)}, bf16[592,128]{1,0:T(8,128)(2,1)S(1)}, u32[]{:S(2)}, u32[]{:S(2)}) %collective-permute-start.10) | collective-permute-done | bytes 151584 | tf_op jit(solution)/shard_map/ppermute | solution.py:353
  32.5 1.1 %shard_map.40 = (f32[192,896]{1,0:T(8,128)S(1)}, bf16[64,896]{1,0:T(8,128)(2,1)S(1)}, bf16[64,896]{1,0:T(8,128)(2,1)S(1)}, bf16[64,896]{1,0:T(8,128)(2,1)S(1)}) custom-call(bf16[1168,128]{1,0:T(8,128)(2,1)S(1)} %get-tuple-element.30.own, bf16[1168,128]{1,0:T(8,128)(2,1)S(1)} %collective-permute-done.other, ...), custom_call_target="tpu_custom_call", output_to_operand_aliasing={{0}: (7, {})} | custom-call | tf_op jit(solution)/shard_map/pallas_call | solution.py:284
  33.5 0.6 %collective-permute-start.17 = (bf16[64,896]{1,0:T(8,128)(2,1)S(1)}, bf16[64,896]{1,0:T(8,128)(2,1)S(1)}, u32[]{:S(2)}, u32[]{:S(2)}) collective-permute-start(bf16[64,896]{1,0:T(8,128)(2,1)S(1)} %get-tuple-element.52), channel_id=1, source_target_pairs={{0,1},{1,0},{2,3},{3,2},{4,5},{5,4},{6,7},{7,6},{8,9},{9,8},{10,11... | collective-permute-start | bytes 344072 | tf_op jit(solution)/shard_map/ppermute | solution.py:356
  34.2 0.1 collective-permute-start.18
  34.3 0.4 %collective-permute-start.19 = (bf16[64,896]{1,0:T(8,128)(2,1)S(1)}, bf16[64,896]{1,0:T(8,128)(2,1)S(1)}, u32[]{:S(2)}, u32[]{:S(2)}) collective-permute-start(bf16[64,896]{1,0:T(8,128)(2,1)S(1)} %get-tuple-element.54), channel_id=1, source_target_pairs={{0,1},{1,0},{2,3},{3,2},{4,5},{5,4},{6,7},{7,6},{8,9},{9,8},{10,11... | collective-permute-start | bytes 344072 | tf_op jit(solution)/shard_map/ppermute | solution.py:356
  34.7 0.0 collective-permute-done.16.returned
  34.7 0.5 %collective-permute-done.17.refs_0_ = bf16[64,896]{1,0:T(8,128)(2,1)S(1)} collective-permute-done((bf16[64,896]{1,0:T(8,128)(2,1)S(1)}, bf16[64,896]{1,0:T(8,128)(2,1)S(1)}, u32[]{:S(2)}, u32[]{:S(2)}) %collective-permute-start.17) | collective-permute-done | bytes 114720 | tf_op jit(solution)/shard_map/ppermute | solution.py:356
  35.1 0.4 collective-permute-done.18.refs_1_
  35.5 0.2 collective-permute-done.19.refs_2_
  35.7 1.0 %shard_map.43 = bf16[192,768]{1,0:T(8,128)(2,1)} custom-call(f32[192,896]{1,0:T(8,128)S(1)} %get-tuple-element.45.mine, bf16[1168,128]{1,0:T(8,128)(2,1)S(1)} %collective-permute-done.16.returned, bf16[64,896]{1,0:T(8,128)(2,1)S(1)} %collective-permute-done.17.refs_0_, bf16[64,896]{1,0:T(8,128)(2,1)S(1)} %collective-permute-done.18.refs_1_, ...), custom_call_target="tpu_custom_call" | custom-call | tf_op jit(solution)/shard_map/pallas_call | solution.py:310
  (1 shorter events, 0.0 us)
Async XLA Ops:
  0.0 1.0 %copy-start = (bf16[192,768]{1,0:T(8,128)(2,1)S(1)}, bf16[192,768]{1,0:T(8,128)(2,1)}, u32[]{:S(2)}) copy-start(bf16[192,768]{1,0:T(8,128)(2,1)} %rows.3) | copy-start | bytes 884740
  1.0 5.3 %copy-start.2 = (s32[192]{0:T(256)S(1)}, s32[192]{0:T(256)}, u32[]{:S(2)}) copy-start(s32[192]{0:T(256)} %param.5) | copy-start | bytes 2308
  1.0 8.0 %collective-permute-start.2 = (bf16[592,128]{1,0:T(8,128)(2,1)S(1)}, bf16[592,128]{1,0:T(8,128)(2,1)S(1)}, u32[]{:S(2)}, u32[]{:S(2)}) collective-permute-start(bf16[592,128]{1,0:T(8,128)(2,1)S(1)} %shard_map.38.refs_0_), channel_id=1, source_target_pairs={{0,3},{1,2},{2,1},{3,0},{4,7},{5,6},{6,5},{7,4},{8,11},{9,10},{10,... | collective-permute-start | bytes 454664 | tf_op jit(solution)/shard_map/ppermute | solution.py:353
  3.4 6.8 %collective-permute-start.1 = (bf16[592,128]{1,0:T(8,128)(2,1)S(1)}, bf16[592,128]{1,0:T(8,128)(2,1)S(1)}, u32[]{:S(2)}, u32[]{:S(2)}) collective-permute-start(bf16[592,128]{1,0:T(8,128)(2,1)S(1)} %shard_map.38.refs_0_), channel_id=1, source_target_pairs={{4,1},{5,0},{0,9},{1,8},{8,13},{9,12},{12,5},{13,4},{6,3},{7,2},{2... | collective-permute-start | bytes 454664 | tf_op jit(solution)/shard_map/ppermute | solution.py:342
  6.3 0.7 %copy-start.1 = (s32[192,1]{0,1:T(1,128)S(1)}, s32[192,1]{0,1:T(1,128)}, u32[]{:S(2)}) copy-start(s32[192,1]{0,1:T(1,128)} %param.4) | copy-start | bytes 2308
  7.1 6.3 %collective-permute-start.4 = (bf16[592,128]{1,0:T(8,128)(2,1)S(1)}, bf16[592,128]{1,0:T(8,128)(2,1)S(1)}, u32[]{:S(2)}, u32[]{:S(2)}) collective-permute-start(bf16[592,128]{1,0:T(8,128)(2,1)S(1)} %get-tuple-element.32.refs_1_), channel_id=1, source_target_pairs={{0,3},{1,2},{2,1},{3,0},{4,7},{5,6},{6,5},{7,4},{8,11},{9,10},{10,... | collective-permute-start | bytes 454664 | tf_op jit(solution)/shard_map/ppermute | solution.py:353
  7.2 6.2 %collective-permute-start.3 = (bf16[592,128]{1,0:T(8,128)(2,1)S(1)}, bf16[592,128]{1,0:T(8,128)(2,1)S(1)}, u32[]{:S(2)}, u32[]{:S(2)}) collective-permute-start(bf16[592,128]{1,0:T(8,128)(2,1)S(1)} %get-tuple-element.32.refs_1_), channel_id=1, source_target_pairs={{4,1},{5,0},{0,9},{1,8},{8,13},{9,12},{12,5},{13,4},{6,3},{7,2},{2... | collective-permute-start | bytes 454664 | tf_op jit(solution)/shard_map/ppermute | solution.py:342
  10.2 6.4 %collective-permute-start.6 = (bf16[592,128]{1,0:T(8,128)(2,1)S(1)}, bf16[592,128]{1,0:T(8,128)(2,1)S(1)}, u32[]{:S(2)}, u32[]{:S(2)}) collective-permute-start(bf16[592,128]{1,0:T(8,128)(2,1)S(1)} %collective-permute-done.1.refs_4_.near_first), channel_id=1, source_target_pairs={{0,3},{1,2},{2,1},{3,0},{4,7},{5,6},{6,5},{7,4},{8,11},{9,10},{10,... | collective-permute-start | bytes 454664 | tf_op jit(solution)/shard_map/ppermute | solution.py:353
  10.2 6.8 %collective-permute-start.5 = (bf16[592,128]{1,0:T(8,128)(2,1)S(1)}, bf16[592,128]{1,0:T(8,128)(2,1)S(1)}, u32[]{:S(2)}, u32[]{:S(2)}) collective-permute-start(bf16[592,128]{1,0:T(8,128)(2,1)S(1)} %collective-permute-done.1.refs_4_.near_first), channel_id=1, source_target_pairs={{4,1},{5,0},{0,9},{1,8},{8,13},{9,12},{12,5},{13,4},{6,3},{7,2},{2... | collective-permute-start | bytes 454664 | tf_op jit(solution)/shard_map/ppermute | solution.py:342
  13.3 4.8 %collective-permute-start.11 = (bf16[592,128]{1,0:T(8,128)(2,1)S(1)}, bf16[592,128]{1,0:T(8,128)(2,1)S(1)}, u32[]{:S(2)}, u32[]{:S(2)}) collective-permute-start(bf16[592,128]{1,0:T(8,128)(2,1)S(1)} %collective-permute-done.1.refs_4_.near_first), channel_id=1, source_target_pairs={{0,1},{1,0},{2,3},{3,2},{4,5},{5,4},{6,7},{7,6},{8,9},{9,8},{10,11... | collective-permute-start | bytes 454664 | tf_op jit(solution)/shard_map/ppermute | solution.py:356
  13.4 6.1 %collective-permute-start.8 = (bf16[592,128]{1,0:T(8,128)(2,1)S(1)}, bf16[592,128]{1,0:T(8,128)(2,1)S(1)}, u32[]{:S(2)}, u32[]{:S(2)}) collective-permute-start(bf16[592,128]{1,0:T(8,128)(2,1)S(1)} %collective-permute-done.3.refs_5_.near_second), channel_id=1, source_target_pairs={{0,3},{1,2},{2,1},{3,0},{4,7},{5,6},{6,5},{7,4},{8,11},{9,10},{10,... | collective-permute-start | bytes 454664 | tf_op jit(solution)/shard_map/ppermute | solution.py:353
  15.1 5.7 %collective-permute-start.7 = (bf16[592,128]{1,0:T(8,128)(2,1)S(1)}, bf16[592,128]{1,0:T(8,128)(2,1)S(1)}, u32[]{:S(2)}, u32[]{:S(2)}) collective-permute-start(bf16[592,128]{1,0:T(8,128)(2,1)S(1)} %collective-permute-done.3.refs_5_.near_second), channel_id=1, source_target_pairs={{4,1},{5,0},{0,9},{1,8},{8,13},{9,12},{12,5},{13,4},{6,3},{7,2},{2... | collective-permute-start | bytes 454664 | tf_op jit(solution)/shard_map/ppermute | solution.py:342
  16.6 4.2 %collective-permute-start.12 = (bf16[592,128]{1,0:T(8,128)(2,1)S(1)}, bf16[592,128]{1,0:T(8,128)(2,1)S(1)}, u32[]{:S(2)}, u32[]{:S(2)}) collective-permute-start(bf16[592,128]{1,0:T(8,128)(2,1)S(1)} %collective-permute-done.3.refs_5_.near_second), channel_id=1, source_target_pairs={{0,1},{1,0},{2,3},{3,2},{4,5},{5,4},{6,7},{7,6},{8,9},{9,8},{10,11... | collective-permute-start | bytes 454664 | tf_op jit(solution)/shard_map/ppermute | solution.py:356
  17.0 9.7 %collective-permute-start.9 = (bf16[592,128]{1,0:T(8,128)(2,1)S(1)}, bf16[592,128]{1,0:T(8,128)(2,1)S(1)}, u32[]{:S(2)}, u32[]{:S(2)}) collective-permute-start(bf16[592,128]{1,0:T(8,128)(2,1)S(1)} %collective-permute-done.5.refs_0_), channel_id=1, source_target_pairs={{0,3},{1,2},{2,1},{3,0},{4,7},{5,6},{6,5},{7,4},{8,11},{9,10},{10,... | collective-permute-start | bytes 454664 | tf_op jit(solution)/shard_map/ppermute | solution.py:353
  18.1 9.4 %collective-permute-start = (bf16[1168,128]{1,0:T(8,128)(2,1)S(1)}, bf16[1168,128]{1,0:T(8,128)(2,1)S(1)}, u32[]{:S(2)}, u32[]{:S(2)}) collective-permute-start(bf16[1168,128]{1,0:T(8,128)(2,1)S(1)} %get-tuple-element.30.own), channel_id=1, source_target_pairs={{0,1},{1,0},{2,3},{3,2},{4,5},{5,4},{6,7},{7,6},{8,9},{9,8},{10,11... | collective-permute-start | bytes 897032 | tf_op jit(solution)/shard_map/ppermute | solution.py:356
  22.0 1.7 %collective-permute-start.15 = (bf16[64,896]{1,0:T(8,128)(2,1)S(1)}, bf16[64,896]{1,0:T(8,128)(2,1)S(1)}, u32[]{:S(2)}, u32[]{:S(2)}) collective-permute-start(bf16[64,896]{1,0:T(8,128)(2,1)S(1)} %get-tuple-element.51), channel_id=1, source_target_pairs={{0,1},{1,0},{2,3},{3,2},{4,5},{5,4},{6,7},{7,6},{8,9},{9,8},{10,11... | collective-permute-start | bytes 344072 | tf_op jit(solution)/shard_map/ppermute | solution.py:356
  22.7 1.3 %collective-permute-start.13 = (bf16[64,896]{1,0:T(8,128)(2,1)S(1)}, bf16[64,896]{1,0:T(8,128)(2,1)S(1)}, u32[]{:S(2)}, u32[]{:S(2)}) collective-permute-start(bf16[64,896]{1,0:T(8,128)(2,1)S(1)} %get-tuple-element.48), channel_id=1, source_target_pairs={{0,1},{1,0},{2,3},{3,2},{4,5},{5,4},{6,7},{7,6},{8,9},{9,8},{10,11... | collective-permute-start | bytes 344072 | tf_op jit(solution)/shard_map/ppermute | solution.py:356
  22.8 1.4 %collective-permute-start.14 = (bf16[64,896]{1,0:T(8,128)(2,1)S(1)}, bf16[64,896]{1,0:T(8,128)(2,1)S(1)}, u32[]{:S(2)}, u32[]{:S(2)}) collective-permute-start(bf16[64,896]{1,0:T(8,128)(2,1)S(1)} %get-tuple-element.49), channel_id=1, source_target_pairs={{0,1},{1,0},{2,3},{3,2},{4,5},{5,4},{6,7},{7,6},{8,9},{9,8},{10,11... | collective-permute-start | bytes 344072 | tf_op jit(solution)/shard_map/ppermute | solution.py:356
  24.5 10.2 %collective-permute-start.16 = (bf16[1168,128]{1,0:T(8,128)(2,1)S(1)}, bf16[1168,128]{1,0:T(8,128)(2,1)S(1)}, u32[]{:S(2)}, u32[]{:S(2)}) collective-permute-start(bf16[1168,128]{1,0:T(8,128)(2,1)S(1)} %shard_map.42), channel_id=1, source_target_pairs={{0,5},{1,4},{8,1},{9,0},{12,9},{13,8},{4,13},{5,12},{2,7},{3,6},{1... | collective-permute-start | bytes 897032 | tf_op jit(solution)/shard_map/ppermute | solution.py:350
  26.7 5.8 %collective-permute-start.10 = (bf16[592,128]{1,0:T(8,128)(2,1)S(1)}, bf16[592,128]{1,0:T(8,128)(2,1)S(1)}, u32[]{:S(2)}, u32[]{:S(2)}) collective-permute-start(bf16[592,128]{1,0:T(8,128)(2,1)S(1)} %collective-permute-done.7.refs_1_), channel_id=1, source_target_pairs={{0,3},{1,2},{2,1},{3,0},{4,7},{5,6},{6,5},{7,4},{8,11},{9,10},{10,... | collective-permute-start | bytes 454664 | tf_op jit(solution)/shard_map/ppermute | solution.py:353
  33.5 1.6 %collective-permute-start.17 = (bf16[64,896]{1,0:T(8,128)(2,1)S(1)}, bf16[64,896]{1,0:T(8,128)(2,1)S(1)}, u32[]{:S(2)}, u32[]{:S(2)}) collective-permute-start(bf16[64,896]{1,0:T(8,128)(2,1)S(1)} %get-tuple-element.52), channel_id=1, source_target_pairs={{0,1},{1,0},{2,3},{3,2},{4,5},{5,4},{6,7},{7,6},{8,9},{9,8},{10,11... | collective-permute-start | bytes 344072 | tf_op jit(solution)/shard_map/ppermute | solution.py:356
  34.2 1.3 %collective-permute-start.18 = (bf16[64,896]{1,0:T(8,128)(2,1)S(1)}, bf16[64,896]{1,0:T(8,128)(2,1)S(1)}, u32[]{:S(2)}, u32[]{:S(2)}) collective-permute-start(bf16[64,896]{1,0:T(8,128)(2,1)S(1)} %get-tuple-element.53), channel_id=1, source_target_pairs={{0,1},{1,0},{2,3},{3,2},{4,5},{5,4},{6,7},{7,6},{8,9},{9,8},{10,11... | collective-permute-start | bytes 344072 | tf_op jit(solution)/shard_map/ppermute | solution.py:356
  34.3 1.4 %collective-permute-start.19 = (bf16[64,896]{1,0:T(8,128)(2,1)S(1)}, bf16[64,896]{1,0:T(8,128)(2,1)S(1)}, u32[]{:S(2)}, u32[]{:S(2)}) collective-permute-start(bf16[64,896]{1,0:T(8,128)(2,1)S(1)} %get-tuple-element.54), channel_id=1, source_target_pairs={{0,1},{1,0},{2,3},{3,2},{4,5},{5,4},{6,7},{7,6},{8,9},{9,8},{10,11... | collective-permute-start | bytes 344072 | tf_op jit(solution)/shard_map/ppermute | solution.py:356

commit v34 on v32

--- a/solution.py
+++ b/solution.py
@@ -255,15 +255,25 @@
     store_theirs(numer[rows_here:], denom[rows_here:], theirs)
 
 
-def last_kernel(mine, returned, *refs):
-    *parts, out, staged, sems = refs
+def join_kernel(own, info, first, second, mine, *refs):
+    *parts, out = refs
+    rows_here = out.shape[0]
+    numer, denom = add_theirs(mine, parts)
+    blocks = take_blocks([first, second], 1, rows_here)
+    left = left_rows((own,), rows_here)
+    store_sides(*add_blocks(left, info, blocks, numer, denom), [out])
+
+
+def last_kernel(own, info, first, second, total, returned, out, staged, sems):
     rows_here, width = out.shape
     half = rows_here // 2
-    numer, denom = add_theirs(mine, parts)
-    numer = numer + from_slabs(returned, rows_here).astype(F32)
+    blocks = take_blocks([first, second], 1, rows_here)
+    left = left_rows((own,), rows_here)
+    numer = total[:, :width] + from_slabs(returned, rows_here).astype(F32)
     lines = returned[returned.shape[0] - LINES :, :].astype(F32)[:4, :half]
-    total = lines[0:2] + lines[2:4]
-    denom = denom + to_column(jnp.concatenate([total[0:1], total[1:2]], axis=1))
+    added = lines[0:2] + lines[2:4]
+    added = to_column(jnp.concatenate([added[0:1], added[1:2]], axis=1))
+    numer, denom = add_blocks(left, info, blocks, numer, total[:, width : width + 1] + added)
     share = 1.0 / denom
     count = rows_here // 4
     copies = []
@@ -392,11 +402,19 @@
     left = (whole, other_core(whole))
     early = across_by[:-1] + along_by[1:-1]
     mine, theirs, info = start_both(left, early, (rows_here, width + 128))
-    late = [along_by[-1], across_by[-1]]
-    mine, *theirs = add_both((*left, info), late, (mine, theirs))
-    out = finish(
-        (rows_here, width), [mine, returned, *[other_core(part) for part in theirs]]
-    )
+    mine, *theirs = add_both((*left, info), [along_by[-1]], (mine, theirs))
+    last_first, last_second = across_by[-1]
+    back = [other_core(part) for part in theirs[:-1]]
+    last_first, theirs[-1] = together(last_first, theirs[-1])
+    last_second, *back = together(last_second, *back, other_core(theirs[-1]))
+    last = [other_core(last_first), other_core(last_second)]
+    (total,) = call(
+        join_kernel,
+        [((rows_here, width + 128), F32)],
+        [whole, info, last_first, last_second, mine, *back],
+        {4: 0},
+    )
+    out = finish((rows_here, width), [whole, info, *last, total, returned])
     return out
 
 

time: 35.3 us -> 40.9 us (1.16)
  waiting for transfers between devices: 8.46 us -> 13.1 us
  Pallas kernels: 5.19 us -> 6 us
    ppermute x1, waiting for transfers between devices: 1 us -> 4.13 us  [back_along(): return lax.ppermute(rows, ('blk', 'pair'), hops)]
    ppermute x6, waiting for transfers between devices: 4.09 us -> 6.96 us  [across(): return lax.ppermute(rows, ('sub', 'pair'), [(0, 3), (1, 2), (2, 1), (3, 0)])]
    ppermute x4, waiting for transfers between devices: 2.39 us -> 1.33 us  [along(): return lax.ppermute(rows, ('blk', 'pair'), hops)]
    ppermute x9 -> x11, starting transfers between devices: 2.83 us -> 3.82 us  [other_core(): return lax.ppermute(rows, 'pair', [(0, 1), (1, 0)])]
    ppermute x1, starting transfers between devices: 0.83 us -> 0.01 us  [back_along(): return lax.ppermute(rows, ('blk', 'pair'), hops)]
    pallas_call x6 -> x7, Pallas kernels: 4.16 us -> 4.73 us  [call(): pl.pallas_call(kernel, out_shape=[jax.ShapeDtypeStruct(shape, dtype) for...]
    ppermute x9 -> x11, waiting for transfers between devices: 0.98 us -> 0.64 us  [other_core(): return lax.ppermute(rows, 'pair', [(0, 1), (1, 0)])]
  transfers between devices with their start and end apart: 20 -> 22, of which waited for: 6 -> 8; matrix products, arithmetic and copies ran while one was open for 0% -> 0% of each run, Pallas kernels for 12% -> 12%
where the time goes in v34:
time: 40.9 us; the launch traced here: 40.7 us
  starting transfers between devices  19.9 us (49%)
  waiting for transfers between devices  13.1 us (32%)
  Pallas kernels  6 us (15%)
  local copies, waits for them, and re-layouts  1.64 us (4%)
    ppermute x4, starting transfers between devices, along(): return lax.ppermute(rows, ('blk', 'pair'), hops)  9.73 us
    ppermute x6, waiting for transfers between devices, across(): return lax.ppermute(rows, ('sub', 'pair'), [(0, 3), (1, 2), (2, 1), (3, 0)])  6.96 us
    ppermute x6, starting transfers between devices, across(): return lax.ppermute(rows, ('sub', 'pair'), [(0, 3), (1, 2), (2, 1), (3, 0)])  6.36 us
    pallas_call x7, Pallas kernels, call(): pl.pallas_call(kernel, out_shape=[jax.ShapeDtypeStruct(shape, dtype) for...  4.73 us
    ppermute x1, waiting for transfers between devices, back_along(): return lax.ppermute(rows, ('blk', 'pair'), hops)  4.13 us
    ppermute x11, starting transfers between devices, other_core(): return lax.ppermute(rows, 'pair', [(0, 1), (1, 0)])  3.82 us
    unnamed x6, local copies, waits for them, and re-layouts  1.64 us
    ppermute x4, waiting for transfers between devices, along(): return lax.ppermute(rows, ('blk', 'pair'), hops)  1.33 us
  transfers between devices with their start and end apart: 22, of which 8 were waited for; matrix products, arithmetic and copies ran while one was open for 0% of the time, Pallas kernels for 12%

profile of v34, /device:TPU:0, one launch (start us, length us, event | category | flops | bytes accessed | tf_op | source)
XLA Modules:
  0.0 40.7 jit_solution(16583472822863622758)
XLA Ops:
  0.0 0.0 copy-start
  0.0 1.0 %copy-done = bf16[192,768]{1,0:T(8,128)(2,1)S(1)} copy-done((bf16[192,768]{1,0:T(8,128)(2,1)S(1)}, bf16[192,768]{1,0:T(8,128)(2,1)}, u32[]{:S(2)}) %copy-start) | copy-done | bytes 294936
  1.0 0.0 copy-start.2
  1.0 3.5 %collective-permute-start.1 = (bf16[592,128]{1,0:T(8,128)(2,1)S(1)}, bf16[592,128]{1,0:T(8,128)(2,1)S(1)}, u32[]{:S(2)}, u32[]{:S(2)}) collective-permute-start(bf16[592,128]{1,0:T(8,128)(2,1)S(1)} %shard_map.38.refs_0_), channel_id=1, source_target_pairs={{4,1},{5,0},{0,9},{1,8},{8,13},{9,12},{12,5},{13,4},{6,3},{7,2},{2... | collective-permute-start | bytes 454664 | tf_op jit(solution)/shard_map/ppermute | solution.py:352
  4.5 1.8 %collective-permute-start.2 = (bf16[592,128]{1,0:T(8,128)(2,1)S(1)}, bf16[592,128]{1,0:T(8,128)(2,1)S(1)}, u32[]{:S(2)}, u32[]{:S(2)}) collective-permute-start(bf16[592,128]{1,0:T(8,128)(2,1)S(1)} %shard_map.38.refs_0_), channel_id=1, source_target_pairs={{0,3},{1,2},{2,1},{3,0},{4,7},{5,6},{6,5},{7,4},{8,11},{9,10},{10,... | collective-permute-start | bytes 454664 | tf_op jit(solution)/shard_map/ppermute | solution.py:363
  6.3 0.0 copy-start.1
  6.3 0.0 copy-done.2
  6.3 0.7 %copy-done.1 = s32[192,1]{0,1:T(1,128)S(1)} copy-done((s32[192,1]{0,1:T(1,128)S(1)}, s32[192,1]{0,1:T(1,128)}, u32[]{:S(2)}) %copy-start.1) | copy-done | bytes 792
  7.0 0.1 shard_map.37
  7.1 1.1 %collective-permute-start.3 = (bf16[592,128]{1,0:T(8,128)(2,1)S(1)}, bf16[592,128]{1,0:T(8,128)(2,1)S(1)}, u32[]{:S(2)}, u32[]{:S(2)}) collective-permute-start(bf16[592,128]{1,0:T(8,128)(2,1)S(1)} %get-tuple-element.38.refs_1_), channel_id=1, source_target_pairs={{4,1},{5,0},{0,9},{1,8},{8,13},{9,12},{12,5},{13,4},{6,3},{7,2},{2... | collective-permute-start | bytes 454664 | tf_op jit(solution)/shard_map/ppermute | solution.py:352
  8.1 0.8 %collective-permute-start.4 = (bf16[592,128]{1,0:T(8,128)(2,1)S(1)}, bf16[592,128]{1,0:T(8,128)(2,1)S(1)}, u32[]{:S(2)}, u32[]{:S(2)}) collective-permute-start(bf16[592,128]{1,0:T(8,128)(2,1)S(1)} %get-tuple-element.38.refs_1_), channel_id=1, source_target_pairs={{0,3},{1,2},{2,1},{3,0},{4,7},{5,6},{6,5},{7,4},{8,11},{9,10},{10,... | collective-permute-start | bytes 454664 | tf_op jit(solution)/shard_map/ppermute | solution.py:363
  8.9 0.0 collective-permute-done.1.refs_4_.near_first
  8.9 1.3 %collective-permute-done.2.refs_0_.refs_2_ = bf16[592,128]{1,0:T(8,128)(2,1)S(1)} collective-permute-done((bf16[592,128]{1,0:T(8,128)(2,1)S(1)}, bf16[592,128]{1,0:T(8,128)(2,1)S(1)}, u32[]{:S(2)}, u32[]{:S(2)}) %collective-permute-start.2) | collective-permute-done | bytes 151584 | tf_op jit(solution)/shard_map/ppermute | solution.py:363
  10.3 2.3 %collective-permute-start.5 = (bf16[592,128]{1,0:T(8,128)(2,1)S(1)}, bf16[592,128]{1,0:T(8,128)(2,1)S(1)}, u32[]{:S(2)}, u32[]{:S(2)}) collective-permute-start(bf16[592,128]{1,0:T(8,128)(2,1)S(1)} %collective-permute-done.1.refs_4_.near_first), channel_id=1, source_target_pairs={{4,1},{5,0},{0,9},{1,8},{8,13},{9,12},{12,5},{13,4},{6,3},{7,2},{2... | collective-permute-start | bytes 454664 | tf_op jit(solution)/shard_map/ppermute | solution.py:352
  12.6 0.8 %collective-permute-start.6 = (bf16[592,128]{1,0:T(8,128)(2,1)S(1)}, bf16[592,128]{1,0:T(8,128)(2,1)S(1)}, u32[]{:S(2)}, u32[]{:S(2)}) collective-permute-start(bf16[592,128]{1,0:T(8,128)(2,1)S(1)} %collective-permute-done.1.refs_4_.near_first), channel_id=1, source_target_pairs={{0,3},{1,2},{2,1},{3,0},{4,7},{5,6},{6,5},{7,4},{8,11},{9,10},{10,... | collective-permute-start | bytes 454664 | tf_op jit(solution)/shard_map/ppermute | solution.py:363
  13.4 1.1 %collective-permute-start.16 = (bf16[592,128]{1,0:T(8,128)(2,1)S(1)}, bf16[592,128]{1,0:T(8,128)(2,1)S(1)}, u32[]{:S(2)}, u32[]{:S(2)}) collective-permute-start(bf16[592,128]{1,0:T(8,128)(2,1)S(1)} %collective-permute-done.1.refs_4_.near_first), channel_id=1, source_target_pairs={{0,1},{1,0},{2,3},{3,2},{4,5},{5,4},{6,7},{7,6},{8,9},{9,8},{10,11... | collective-permute-start | bytes 454664 | tf_op jit(solution)/shard_map/ppermute | solution.py:366
  14.5 0.0 collective-permute-done.3.refs_5_.near_second
  14.5 0.0 collective-permute-start
  14.5 0.0 collective-permute-done.4.refs_1_.refs_3_
  14.5 0.5 %collective-permute-start.17 = (bf16[592,128]{1,0:T(8,128)(2,1)S(1)}, bf16[592,128]{1,0:T(8,128)(2,1)S(1)}, u32[]{:S(2)}, u32[]{:S(2)}) collective-permute-start(bf16[592,128]{1,0:T(8,128)(2,1)S(1)} %collective-permute-done.3.refs_5_.near_second), channel_id=1, source_target_pairs={{0,1},{1,0},{2,3},{3,2},{4,5},{5,4},{6,7},{7,6},{8,9},{9,8},{10,11... | collective-permute-start | bytes 454664 | tf_op jit(solution)/shard_map/ppermute | solution.py:366
  15.0 1.0 %collective-permute-done.5.refs_0_ = bf16[592,128]{1,0:T(8,128)(2,1)S(1)} collective-permute-done((bf16[592,128]{1,0:T(8,128)(2,1)S(1)}, bf16[592,128]{1,0:T(8,128)(2,1)S(1)}, u32[]{:S(2)}, u32[]{:S(2)}) %collective-permute-start.5) | collective-permute-done | bytes 151584 | tf_op jit(solution)/shard_map/ppermute | solution.py:352
  16.0 2.8 %collective-permute-start.7 = (bf16[592,128]{1,0:T(8,128)(2,1)S(1)}, bf16[592,128]{1,0:T(8,128)(2,1)S(1)}, u32[]{:S(2)}, u32[]{:S(2)}) collective-permute-start(bf16[592,128]{1,0:T(8,128)(2,1)S(1)} %collective-permute-done.3.refs_5_.near_second), channel_id=1, source_target_pairs={{4,1},{5,0},{0,9},{1,8},{8,13},{9,12},{12,5},{13,4},{6,3},{7,2},{2... | collective-permute-start | bytes 454664 | tf_op jit(solution)/shard_map/ppermute | solution.py:352
  18.8 0.0 collective-permute-done.6.refs_2_
  18.8 0.9 %collective-permute-start.8 = (bf16[592,128]{1,0:T(8,128)(2,1)S(1)}, bf16[592,128]{1,0:T(8,128)(2,1)S(1)}, u32[]{:S(2)}, u32[]{:S(2)}) collective-permute-start(bf16[592,128]{1,0:T(8,128)(2,1)S(1)} %collective-permute-done.3.refs_5_.near_second), channel_id=1, source_target_pairs={{0,3},{1,2},{2,1},{3,0},{4,7},{5,6},{6,5},{7,4},{8,11},{9,10},{10,... | collective-permute-start | bytes 454664 | tf_op jit(solution)/shard_map/ppermute | solution.py:363
  19.7 0.0 collective-permute-done.16.over_first
  19.7 0.9 %collective-permute-start.9 = (bf16[592,128]{1,0:T(8,128)(2,1)S(1)}, bf16[592,128]{1,0:T(8,128)(2,1)S(1)}, u32[]{:S(2)}, u32[]{:S(2)}) collective-permute-start(bf16[592,128]{1,0:T(8,128)(2,1)S(1)} %collective-permute-done.5.refs_0_), channel_id=1, source_target_pairs={{0,3},{1,2},{2,1},{3,0},{4,7},{5,6},{6,5},{7,4},{8,11},{9,10},{10,... | collective-permute-start | bytes 454664 | tf_op jit(solution)/shard_map/ppermute | solution.py:363
  20.5 0.0 collective-permute-done.17.over_second
  20.5 1.1 %shard_map.42 = (f32[192,896]{1,0:T(8,128)S(1)}, bf16[64,896]{1,0:T(8,128)(2,1)S(1)}, bf16[64,896]{1,0:T(8,128)(2,1)S(1)}, bf16[64,896]{1,0:T(8,128)(2,1)S(1)}) custom-call(bf16[592,128]{1,0:T(8,128)(2,1)S(1)} %collective-permute-done.1.refs_4_.near_first, bf16[592,128]{1,0:T(8,128)(2,1)S(1)} %collective-permute-done.3.refs_5_.near_second, ...), custom_call_target="tpu_custom_call" | custom-call | tf_op jit(solution)/shard_map/pallas_call | solution.py:294
  21.7 0.1 collective-permute-start.18
  21.8 0.4 collective-permute-done.7.refs_1_
  22.1 0.2 collective-permute-start.19
  22.3 2.6 %collective-permute-done.8.refs_3_ = bf16[592,128]{1,0:T(8,128)(2,1)S(1)} collective-permute-done((bf16[592,128]{1,0:T(8,128)(2,1)S(1)}, bf16[592,128]{1,0:T(8,128)(2,1)S(1)}, u32[]{:S(2)}, u32[]{:S(2)}) %collective-permute-start.8) | collective-permute-done | bytes 151584 | tf_op jit(solution)/shard_map/ppermute | solution.py:363
  24.9 0.3 collective-permute-start.20
  25.2 3.0 %collective-permute-done.9.first = bf16[592,128]{1,0:T(8,128)(2,1)S(1)} collective-permute-done((bf16[592,128]{1,0:T(8,128)(2,1)S(1)}, bf16[592,128]{1,0:T(8,128)(2,1)S(1)}, u32[]{:S(2)}, u32[]{:S(2)}) %collective-permute-start.9) | collective-permute-done | bytes 151584 | tf_op jit(solution)/shard_map/ppermute | solution.py:363
  28.2 1.2 %collective-permute-start.11 = (bf16[592,128]{1,0:T(8,128)(2,1)S(1)}, bf16[592,128]{1,0:T(8,128)(2,1)S(1)}, u32[]{:S(2)}, u32[]{:S(2)}) collective-permute-start(bf16[592,128]{1,0:T(8,128)(2,1)S(1)} %collective-permute-done.7.refs_1_), channel_id=1, source_target_pairs={{0,3},{1,2},{2,1},{3,0},{4,7},{5,6},{6,5},{7,4},{8,11},{9,10},{10,... | collective-permute-start | bytes 454664 | tf_op jit(solution)/shard_map/ppermute | solution.py:363
  29.4 0.0 collective-permute-done.18.refs_0_
  29.4 0.0 collective-permute-done.19.refs_1_
  29.4 0.0 collective-permute-done.20.refs_2_
  29.4 0.3 shard_map.43
  29.7 0.0 collective-permute-start.21
  29.7 0.0 collective-permute-done.other
  29.7 1.5 %shard_map.39 = (f32[192,896]{1,0:T(8,128)S(1)}, f32[192,896]{1,0:T(8,128)S(1)}, f32[384,128]{1,0:T(8,128)S(1)}) custom-call(bf16[1168,128]{1,0:T(8,128)(2,1)S(1)} %get-tuple-element.36.own, bf16[1168,128]{1,0:T(8,128)(2,1)S(1)} %collective-permute-done.other, bf16[592,128]{1,0:T(8,128)(2,1)S(1)} %collective-permute-done.2.refs_0_.refs_2_, ...), custom_call_target="tpu_custom_call" | custom-call | tf_op jit(solution)/shard_map/pallas_call | solution.py:294
  31.3 0.9 %shard_map.40 = (f32[192,896]{1,0:T(8,128)S(1)}, bf16[64,896]{1,0:T(8,128)(2,1)S(1)}, bf16[64,896]{1,0:T(8,128)(2,1)S(1)}, bf16[64,896]{1,0:T(8,128)(2,1)S(1)}) custom-call(bf16[1168,128]{1,0:T(8,128)(2,1)S(1)} %get-tuple-element.36.own, bf16[1168,128]{1,0:T(8,128)(2,1)S(1)} %collective-permute-done.other, ...), custom_call_target="tpu_custom_call", output_to_operand_aliasing={{0}: (5, {})} | custom-call | tf_op jit(solution)/shard_map/pallas_call | solution.py:294
  32.2 0.5 %collective-permute-start.12 = (bf16[64,896]{1,0:T(8,128)(2,1)S(1)}, bf16[64,896]{1,0:T(8,128)(2,1)S(1)}, u32[]{:S(2)}, u32[]{:S(2)}) collective-permute-start(bf16[64,896]{1,0:T(8,128)(2,1)S(1)} %get-tuple-element.53), channel_id=1, source_target_pairs={{0,1},{1,0},{2,3},{3,2},{4,5},{5,4},{6,7},{7,6},{8,9},{9,8},{10,11... | collective-permute-start | bytes 344072 | tf_op jit(solution)/shard_map/ppermute | solution.py:366
  32.7 0.1 collective-permute-start.13
  32.8 0.4 %collective-permute-start.14 = (bf16[64,896]{1,0:T(8,128)(2,1)S(1)}, bf16[64,896]{1,0:T(8,128)(2,1)S(1)}, u32[]{:S(2)}, u32[]{:S(2)}) collective-permute-start(bf16[64,896]{1,0:T(8,128)(2,1)S(1)} %get-tuple-element.55), channel_id=1, source_target_pairs={{0,1},{1,0},{2,3},{3,2},{4,5},{5,4},{6,7},{7,6},{8,9},{9,8},{10,11... | collective-permute-start | bytes 344072 | tf_op jit(solution)/shard_map/ppermute | solution.py:366
  33.2 0.5 %collective-permute-done.12.refs_0_ = bf16[64,896]{1,0:T(8,128)(2,1)S(1)} collective-permute-done((bf16[64,896]{1,0:T(8,128)(2,1)S(1)}, bf16[64,896]{1,0:T(8,128)(2,1)S(1)}, u32[]{:S(2)}, u32[]{:S(2)}) %collective-permute-start.12) | collective-permute-done | bytes 114720 | tf_op jit(solution)/shard_map/ppermute | solution.py:366
  33.6 0.4 collective-permute-start.10
  34.0 0.0 collective-permute-done.13.refs_1_
  34.0 0.2 collective-permute-done.14.refs_2_
  34.2 0.0 collective-permute-done.11.second
  34.2 0.4 collective-permute-start.15
  34.5 0.8 %shard_map.41.total = f32[192,896]{1,0:T(8,128)S(1)} custom-call(bf16[1168,128]{1,0:T(8,128)(2,1)S(1)} %get-tuple-element.36.own, f32[384,128]{1,0:T(8,128)S(1)} %get-tuple-element.45.info, bf16[592,128]{1,0:T(8,128)(2,1)S(1)} %collective-permute-done.9.first, bf16[592,128]{1,0:T(8,128)(2,1)S(1)} %collective-permute-done.11.second, ...), custom_call_target="tpu_custom_call", output_to_operand_aliasing={{}: (4, {})} | custom-call | tf_op jit(solution)/shard_map/pallas_call | solution.py:294
  35.3 0.0 collective-permute-done.10.first
  35.3 4.1 %collective-permute-done.21.returned = bf16[1168,128]{1,0:T(8,128)(2,1)S(1)} collective-permute-done((bf16[1168,128]{1,0:T(8,128)(2,1)S(1)}, bf16[1168,128]{1,0:T(8,128)(2,1)S(1)}, u32[]{:S(2)}, u32[]{:S(2)}) %collective-permute-start.21) | collective-permute-done | bytes 299040 | tf_op jit(solution)/shard_map/ppermute | solution.py:360
  39.4 0.0 collective-permute-done.15.second
  39.4 1.3 %shard_map.44 = bf16[192,768]{1,0:T(8,128)(2,1)} custom-call(bf16[1168,128]{1,0:T(8,128)(2,1)S(1)} %get-tuple-element.36.own, f32[384,128]{1,0:T(8,128)S(1)} %get-tuple-element.45.info, bf16[592,128]{1,0:T(8,128)(2,1)S(1)} %collective-permute-done.10.first, bf16[592,128]{1,0:T(8,128)(2,1)S(1)} %collective-permute-done.15.second, ...), custom_call_target="tpu_custom_call" | custom-call | tf_op jit(solution)/shard_map/pallas_call | solution.py:320
  (1 shorter events, 0.0 us)
Async XLA Ops:
  0.0 1.0 %copy-start = (bf16[192,768]{1,0:T(8,128)(2,1)S(1)}, bf16[192,768]{1,0:T(8,128)(2,1)}, u32[]{:S(2)}) copy-start(bf16[192,768]{1,0:T(8,128)(2,1)} %rows.3) | copy-start | bytes 884740
  1.0 5.3 %copy-start.2 = (s32[192]{0:T(256)S(1)}, s32[192]{0:T(256)}, u32[]{:S(2)}) copy-start(s32[192]{0:T(256)} %param.5) | copy-start | bytes 2308
  1.0 7.9 %collective-permute-start.1 = (bf16[592,128]{1,0:T(8,128)(2,1)S(1)}, bf16[592,128]{1,0:T(8,128)(2,1)S(1)}, u32[]{:S(2)}, u32[]{:S(2)}) collective-permute-start(bf16[592,128]{1,0:T(8,128)(2,1)S(1)} %shard_map.38.refs_0_), channel_id=1, source_target_pairs={{4,1},{5,0},{0,9},{1,8},{8,13},{9,12},{12,5},{13,4},{6,3},{7,2},{2... | collective-permute-start | bytes 454664 | tf_op jit(solution)/shard_map/ppermute | solution.py:352
  4.5 5.8 %collective-permute-start.2 = (bf16[592,128]{1,0:T(8,128)(2,1)S(1)}, bf16[592,128]{1,0:T(8,128)(2,1)S(1)}, u32[]{:S(2)}, u32[]{:S(2)}) collective-permute-start(bf16[592,128]{1,0:T(8,128)(2,1)S(1)} %shard_map.38.refs_0_), channel_id=1, source_target_pairs={{0,3},{1,2},{2,1},{3,0},{4,7},{5,6},{6,5},{7,4},{8,11},{9,10},{10,... | collective-permute-start | bytes 454664 | tf_op jit(solution)/shard_map/ppermute | solution.py:363
  6.3 0.7 %copy-start.1 = (s32[192,1]{0,1:T(1,128)S(1)}, s32[192,1]{0,1:T(1,128)}, u32[]{:S(2)}) copy-start(s32[192,1]{0,1:T(1,128)} %param.4) | copy-start | bytes 2308
  7.1 7.4 %collective-permute-start.3 = (bf16[592,128]{1,0:T(8,128)(2,1)S(1)}, bf16[592,128]{1,0:T(8,128)(2,1)S(1)}, u32[]{:S(2)}, u32[]{:S(2)}) collective-permute-start(bf16[592,128]{1,0:T(8,128)(2,1)S(1)} %get-tuple-element.38.refs_1_), channel_id=1, source_target_pairs={{4,1},{5,0},{0,9},{1,8},{8,13},{9,12},{12,5},{13,4},{6,3},{7,2},{2... | collective-permute-start | bytes 454664 | tf_op jit(solution)/shard_map/ppermute | solution.py:352
  8.1 6.4 %collective-permute-start.4 = (bf16[592,128]{1,0:T(8,128)(2,1)S(1)}, bf16[592,128]{1,0:T(8,128)(2,1)S(1)}, u32[]{:S(2)}, u32[]{:S(2)}) collective-permute-start(bf16[592,128]{1,0:T(8,128)(2,1)S(1)} %get-tuple-element.38.refs_1_), channel_id=1, source_target_pairs={{0,3},{1,2},{2,1},{3,0},{4,7},{5,6},{6,5},{7,4},{8,11},{9,10},{10,... | collective-permute-start | bytes 454664 | tf_op jit(solution)/shard_map/ppermute | solution.py:363
  10.3 5.7 %collective-permute-start.5 = (bf16[592,128]{1,0:T(8,128)(2,1)S(1)}, bf16[592,128]{1,0:T(8,128)(2,1)S(1)}, u32[]{:S(2)}, u32[]{:S(2)}) collective-permute-start(bf16[592,128]{1,0:T(8,128)(2,1)S(1)} %collective-permute-done.1.refs_4_.near_first), channel_id=1, source_target_pairs={{4,1},{5,0},{0,9},{1,8},{8,13},{9,12},{12,5},{13,4},{6,3},{7,2},{2... | collective-permute-start | bytes 454664 | tf_op jit(solution)/shard_map/ppermute | solution.py:352
  12.6 6.2 %collective-permute-start.6 = (bf16[592,128]{1,0:T(8,128)(2,1)S(1)}, bf16[592,128]{1,0:T(8,128)(2,1)S(1)}, u32[]{:S(2)}, u32[]{:S(2)}) collective-permute-start(bf16[592,128]{1,0:T(8,128)(2,1)S(1)} %collective-permute-done.1.refs_4_.near_first), channel_id=1, source_target_pairs={{0,3},{1,2},{2,1},{3,0},{4,7},{5,6},{6,5},{7,4},{8,11},{9,10},{10,... | collective-permute-start | bytes 454664 | tf_op jit(solution)/shard_map/ppermute | solution.py:363
  13.4 6.2 %collective-permute-start.16 = (bf16[592,128]{1,0:T(8,128)(2,1)S(1)}, bf16[592,128]{1,0:T(8,128)(2,1)S(1)}, u32[]{:S(2)}, u32[]{:S(2)}) collective-permute-start(bf16[592,128]{1,0:T(8,128)(2,1)S(1)} %collective-permute-done.1.refs_4_.near_first), channel_id=1, source_target_pairs={{0,1},{1,0},{2,3},{3,2},{4,5},{5,4},{6,7},{7,6},{8,9},{9,8},{10,11... | collective-permute-start | bytes 454664 | tf_op jit(solution)/shard_map/ppermute | solution.py:366
  14.5 15.2 %collective-permute-start = (bf16[1168,128]{1,0:T(8,128)(2,1)S(1)}, bf16[1168,128]{1,0:T(8,128)(2,1)S(1)}, u32[]{:S(2)}, u32[]{:S(2)}) collective-permute-start(bf16[1168,128]{1,0:T(8,128)(2,1)S(1)} %get-tuple-element.36.own), channel_id=1, source_target_pairs={{0,1},{1,0},{2,3},{3,2},{4,5},{5,4},{6,7},{7,6},{8,9},{9,8},{10,11... | collective-permute-start | bytes 897032 | tf_op jit(solution)/shard_map/ppermute | solution.py:366
  14.5 6.0 %collective-permute-start.17 = (bf16[592,128]{1,0:T(8,128)(2,1)S(1)}, bf16[592,128]{1,0:T(8,128)(2,1)S(1)}, u32[]{:S(2)}, u32[]{:S(2)}) collective-permute-start(bf16[592,128]{1,0:T(8,128)(2,1)S(1)} %collective-permute-done.3.refs_5_.near_second), channel_id=1, source_target_pairs={{0,1},{1,0},{2,3},{3,2},{4,5},{5,4},{6,7},{7,6},{8,9},{9,8},{10,11... | collective-permute-start | bytes 454664 | tf_op jit(solution)/shard_map/ppermute | solution.py:366
  16.0 6.2 %collective-permute-start.7 = (bf16[592,128]{1,0:T(8,128)(2,1)S(1)}, bf16[592,128]{1,0:T(8,128)(2,1)S(1)}, u32[]{:S(2)}, u32[]{:S(2)}) collective-permute-start(bf16[592,128]{1,0:T(8,128)(2,1)S(1)} %collective-permute-done.3.refs_5_.near_second), channel_id=1, source_target_pairs={{4,1},{5,0},{0,9},{1,8},{8,13},{9,12},{12,5},{13,4},{6,3},{7,2},{2... | collective-permute-start | bytes 454664 | tf_op jit(solution)/shard_map/ppermute | solution.py:352
  18.8 6.2 %collective-permute-start.8 = (bf16[592,128]{1,0:T(8,128)(2,1)S(1)}, bf16[592,128]{1,0:T(8,128)(2,1)S(1)}, u32[]{:S(2)}, u32[]{:S(2)}) collective-permute-start(bf16[592,128]{1,0:T(8,128)(2,1)S(1)} %collective-permute-done.3.refs_5_.near_second), channel_id=1, source_target_pairs={{0,3},{1,2},{2,1},{3,0},{4,7},{5,6},{6,5},{7,4},{8,11},{9,10},{10,... | collective-permute-start | bytes 454664 | tf_op jit(solution)/shard_map/ppermute | solution.py:363
  19.7 8.5 %collective-permute-start.9 = (bf16[592,128]{1,0:T(8,128)(2,1)S(1)}, bf16[592,128]{1,0:T(8,128)(2,1)S(1)}, u32[]{:S(2)}, u32[]{:S(2)}) collective-permute-start(bf16[592,128]{1,0:T(8,128)(2,1)S(1)} %collective-permute-done.5.refs_0_), channel_id=1, source_target_pairs={{0,3},{1,2},{2,1},{3,0},{4,7},{5,6},{6,5},{7,4},{8,11},{9,10},{10,... | collective-permute-start | bytes 454664 | tf_op jit(solution)/shard_map/ppermute | solution.py:363
  21.7 7.7 %collective-permute-start.18 = (bf16[64,896]{1,0:T(8,128)(2,1)S(1)}, bf16[64,896]{1,0:T(8,128)(2,1)S(1)}, u32[]{:S(2)}, u32[]{:S(2)}) collective-permute-start(bf16[64,896]{1,0:T(8,128)(2,1)S(1)} %get-tuple-element.64), channel_id=1, source_target_pairs={{0,1},{1,0},{2,3},{3,2},{4,5},{5,4},{6,7},{7,6},{8,9},{9,8},{10,11... | collective-permute-start | bytes 344072 | tf_op jit(solution)/shard_map/ppermute | solution.py:366
  22.1 7.3 %collective-permute-start.19 = (bf16[64,896]{1,0:T(8,128)(2,1)S(1)}, bf16[64,896]{1,0:T(8,128)(2,1)S(1)}, u32[]{:S(2)}, u32[]{:S(2)}) collective-permute-start(bf16[64,896]{1,0:T(8,128)(2,1)S(1)} %get-tuple-element.65), channel_id=1, source_target_pairs={{0,1},{1,0},{2,3},{3,2},{4,5},{5,4},{6,7},{7,6},{8,9},{9,8},{10,11... | collective-permute-start | bytes 344072 | tf_op jit(solution)/shard_map/ppermute | solution.py:366
  24.9 4.5 %collective-permute-start.20 = (bf16[64,896]{1,0:T(8,128)(2,1)S(1)}, bf16[64,896]{1,0:T(8,128)(2,1)S(1)}, u32[]{:S(2)}, u32[]{:S(2)}) collective-permute-start(bf16[64,896]{1,0:T(8,128)(2,1)S(1)} %get-tuple-element.66), channel_id=1, source_target_pairs={{0,1},{1,0},{2,3},{3,2},{4,5},{5,4},{6,7},{7,6},{8,9},{9,8},{10,11... | collective-permute-start | bytes 344072 | tf_op jit(solution)/shard_map/ppermute | solution.py:366
  28.2 6.0 %collective-permute-start.11 = (bf16[592,128]{1,0:T(8,128)(2,1)S(1)}, bf16[592,128]{1,0:T(8,128)(2,1)S(1)}, u32[]{:S(2)}, u32[]{:S(2)}) collective-permute-start(bf16[592,128]{1,0:T(8,128)(2,1)S(1)} %collective-permute-done.7.refs_1_), channel_id=1, source_target_pairs={{0,3},{1,2},{2,1},{3,0},{4,7},{5,6},{6,5},{7,4},{8,11},{9,10},{10,... | collective-permute-start | bytes 454664 | tf_op jit(solution)/shard_map/ppermute | solution.py:363
  29.7 9.7 %collective-permute-start.21 = (bf16[1168,128]{1,0:T(8,128)(2,1)S(1)}, bf16[1168,128]{1,0:T(8,128)(2,1)S(1)}, u32[]{:S(2)}, u32[]{:S(2)}) collective-permute-start(bf16[1168,128]{1,0:T(8,128)(2,1)S(1)} %shard_map.43), channel_id=1, source_target_pairs={{0,5},{1,4},{8,1},{9,0},{12,9},{13,8},{4,13},{5,12},{2,7},{3,6},{1... | collective-permute-start | bytes 897032 | tf_op jit(solution)/shard_map/ppermute | solution.py:360
  32.2 1.5 %collective-permute-start.12 = (bf16[64,896]{1,0:T(8,128)(2,1)S(1)}, bf16[64,896]{1,0:T(8,128)(2,1)S(1)}, u32[]{:S(2)}, u32[]{:S(2)}) collective-permute-start(bf16[64,896]{1,0:T(8,128)(2,1)S(1)} %get-tuple-element.53), channel_id=1, source_target_pairs={{0,1},{1,0},{2,3},{3,2},{4,5},{5,4},{6,7},{7,6},{8,9},{9,8},{10,11... | collective-permute-start | bytes 344072 | tf_op jit(solution)/shard_map/ppermute | solution.py:366
  32.7 1.3 %collective-permute-start.13 = (bf16[64,896]{1,0:T(8,128)(2,1)S(1)}, bf16[64,896]{1,0:T(8,128)(2,1)S(1)}, u32[]{:S(2)}, u32[]{:S(2)}) collective-permute-start(bf16[64,896]{1,0:T(8,128)(2,1)S(1)} %get-tuple-element.54), channel_id=1, source_target_pairs={{0,1},{1,0},{2,3},{3,2},{4,5},{5,4},{6,7},{7,6},{8,9},{9,8},{10,11... | collective-permute-start | bytes 344072 | tf_op jit(solution)/shard_map/ppermute | solution.py:366
  32.8 1.4 %collective-permute-start.14 = (bf16[64,896]{1,0:T(8,128)(2,1)S(1)}, bf16[64,896]{1,0:T(8,128)(2,1)S(1)}, u32[]{:S(2)}, u32[]{:S(2)}) collective-permute-start(bf16[64,896]{1,0:T(8,128)(2,1)S(1)} %get-tuple-element.55), channel_id=1, source_target_pairs={{0,1},{1,0},{2,3},{3,2},{4,5},{5,4},{6,7},{7,6},{8,9},{9,8},{10,11... | collective-permute-start | bytes 344072 | tf_op jit(solution)/shard_map/ppermute | solution.py:366
  33.6 1.6 %collective-permute-start.10 = (bf16[592,128]{1,0:T(8,128)(2,1)S(1)}, bf16[592,128]{1,0:T(8,128)(2,1)S(1)}, u32[]{:S(2)}, u32[]{:S(2)}) collective-permute-start(bf16[592,128]{1,0:T(8,128)(2,1)S(1)} %collective-permute-done.9.first), channel_id=1, source_target_pairs={{0,1},{1,0},{2,3},{3,2},{4,5},{5,4},{6,7},{7,6},{8,9},{9,8},{10,11... | collective-permute-start | bytes 454664 | tf_op jit(solution)/shard_map/ppermute | solution.py:366
  34.2 5.3 %collective-permute-start.15 = (bf16[592,128]{1,0:T(8,128)(2,1)S(1)}, bf16[592,128]{1,0:T(8,128)(2,1)S(1)}, u32[]{:S(2)}, u32[]{:S(2)}) collective-permute-start(bf16[592,128]{1,0:T(8,128)(2,1)S(1)} %collective-permute-done.11.second), channel_id=1, source_target_pairs={{0,1},{1,0},{2,3},{3,2},{4,5},{5,4},{6,7},{7,6},{8,9},{9,8},{10,11... | collective-permute-start | bytes 454664 | tf_op jit(solution)/shard_map/ppermute | solution.py:366

commit v35 on v32

--- a/solution.py
+++ b/solution.py
@@ -170,11 +170,12 @@
     high = denom.astype(BF16).astype(F32)
     lane = lax.broadcasted_iota(jnp.int32, (denom.shape[0], 128), 1)
     pair = jnp.where(lane == 0, high, denom - high).astype(BF16)
-    count, wide = outs[0].shape
+    count = outs[0].shape[0]
+    width = numer.shape[1]
     for part, out in enumerate(outs):
         rows = slice(part * count, (part + 1) * count)
-        out[:, : wide - 128] = numer[rows].astype(BF16)
-        out[:, wide - 128 :] = pair[rows]
+        out[:, :width] = numer[rows].astype(BF16)
+        out[:, width : width + 128] = pair[rows]
 
 
 def add_theirs(mine, parts):
@@ -376,7 +377,7 @@
     near_sum, *over_sum = call(
         back_kernel,
         [((rows_here, width + 128), F32)]
-        + [((rows_here // PARTS, width + 128), BF16)] * PARTS,
+        + [((rows_here // PARTS, width + 256), BF16)] * PARTS,
         [*near, *over, first, second, *across_by[0]],
     )
     near_sum, _ = together(near_sum, along_by[2][1])
@@ -390,9 +391,9 @@
     last_half, first_crossed = together(along_by[-1][1], first_crossed)
     across_by.append((first_crossed, across(last_half)))
     left = (whole, other_core(whole))
-    early = across_by[:-1] + along_by[1:-1]
+    early = across_by[:-1] + along_by[1:]
     mine, theirs, info = start_both(left, early, (rows_here, width + 128))
-    late = [along_by[-1], across_by[-1]]
+    late = [across_by[-1]]
     mine, *theirs = add_both((*left, info), late, (mine, theirs))
     out = finish(
         (rows_here, width), [mine, returned, *[other_core(part) for part in theirs]]

time: 35.3 us -> 35.8 us (1.014)
  waiting for transfers between devices: 8.46 us -> 8.85 us
    ppermute x6, waiting for transfers between devices: 4.09 us -> 5.58 us  [across(): return lax.ppermute(rows, ('sub', 'pair'), [(0, 3), (1, 2), (2, 1), (3, 0)])]
    ppermute x1, waiting for transfers between devices: 1 us -> 0.01 us  [back_along(): return lax.ppermute(rows, ('blk', 'pair'), hops)]
    ppermute x6, starting transfers between devices: 6.7 us -> 7.13 us  [across(): return lax.ppermute(rows, ('sub', 'pair'), [(0, 3), (1, 2), (2, 1), (3, 0)])]
    ppermute x9, starting transfers between devices: 2.83 us -> 2.43 us  [other_core(): return lax.ppermute(rows, 'pair', [(0, 1), (1, 0)])]
  transfers between devices with their start and end apart: 20 -> 20, of which waited for: 6 -> 8; matrix products, arithmetic and copies ran while one was open for 0% -> 0% of each run, Pallas kernels for 12% -> 12%
where the time goes in v35:
time: 35.8 us; the launch traced here: 35.6 us
  starting transfers between devices  19.8 us (55%)
  waiting for transfers between devices  8.85 us (25%)
  Pallas kernels  5.31 us (15%)
  local copies, waits for them, and re-layouts  1.64 us (5%)
    ppermute x4, starting transfers between devices, along(): return lax.ppermute(rows, ('blk', 'pair'), hops)  9.42 us
    ppermute x6, starting transfers between devices, across(): return lax.ppermute(rows, ('sub', 'pair'), [(0, 3), (1, 2), (2, 1), (3, 0)])  7.13 us
    ppermute x6, waiting for transfers between devices, across(): return lax.ppermute(rows, ('sub', 'pair'), [(0, 3), (1, 2), (2, 1), (3, 0)])  5.58 us
    pallas_call x6, Pallas kernels, call(): pl.pallas_call(kernel, out_shape=[jax.ShapeDtypeStruct(shape, dtype) for...  4.29 us
    ppermute x9, starting transfers between devices, other_core(): return lax.ppermute(rows, 'pair', [(0, 1), (1, 0)])  2.43 us
    ppermute x4, waiting for transfers between devices, along(): return lax.ppermute(rows, ('blk', 'pair'), hops)  2.27 us
    unnamed x6, local copies, waits for them, and re-layouts  1.64 us
    pallas_call x1, Pallas kernels, finish(): pl.pallas_call(last_kernel, out_shape=jax.ShapeDtypeStruct(shape, BF16),...  1.03 us
  transfers between devices with their start and end apart: 20, of which 8 were waited for; matrix products, arithmetic and copies ran while one was open for 0% of the time, Pallas kernels for 12%

profile of v35, /device:TPU:0, one launch (start us, length us, event | category | flops | bytes accessed | tf_op | source)
XLA Modules:
  0.0 35.6 jit_solution(4177553215008655989)
XLA Ops:
  0.0 0.0 copy-start
  0.0 1.0 %copy-done = bf16[192,768]{1,0:T(8,128)(2,1)S(1)} copy-done((bf16[192,768]{1,0:T(8,128)(2,1)S(1)}, bf16[192,768]{1,0:T(8,128)(2,1)}, u32[]{:S(2)}) %copy-start) | copy-done | bytes 294936
  1.0 0.0 copy-start.2
  1.0 2.4 %collective-permute-start.2 = (bf16[592,128]{1,0:T(8,128)(2,1)S(1)}, bf16[592,128]{1,0:T(8,128)(2,1)S(1)}, u32[]{:S(2)}, u32[]{:S(2)}) collective-permute-start(bf16[592,128]{1,0:T(8,128)(2,1)S(1)} %shard_map.38.refs_0_), channel_id=1, source_target_pairs={{0,3},{1,2},{2,1},{3,0},{4,7},{5,6},{6,5},{7,4},{8,11},{9,10},{10,... | collective-permute-start | bytes 454664 | tf_op jit(solution)/shard_map/ppermute | solution.py:354
  3.4 2.9 %collective-permute-start.1 = (bf16[592,128]{1,0:T(8,128)(2,1)S(1)}, bf16[592,128]{1,0:T(8,128)(2,1)S(1)}, u32[]{:S(2)}, u32[]{:S(2)}) collective-permute-start(bf16[592,128]{1,0:T(8,128)(2,1)S(1)} %shard_map.38.refs_0_), channel_id=1, source_target_pairs={{4,1},{5,0},{0,9},{1,8},{8,13},{9,12},{12,5},{13,4},{6,3},{7,2},{2... | collective-permute-start | bytes 454664 | tf_op jit(solution)/shard_map/ppermute | solution.py:343
  6.3 0.0 copy-start.1
  6.3 0.0 copy-done.2
  6.3 0.7 %copy-done.1 = s32[192,1]{0,1:T(1,128)S(1)} copy-done((s32[192,1]{0,1:T(1,128)S(1)}, s32[192,1]{0,1:T(1,128)}, u32[]{:S(2)}) %copy-start.1) | copy-done | bytes 792
  7.0 0.1 shard_map.37
  7.1 0.1 collective-permute-start.4
  7.2 1.8 %collective-permute-start.3 = (bf16[592,128]{1,0:T(8,128)(2,1)S(1)}, bf16[592,128]{1,0:T(8,128)(2,1)S(1)}, u32[]{:S(2)}, u32[]{:S(2)}) collective-permute-start(bf16[592,128]{1,0:T(8,128)(2,1)S(1)} %get-tuple-element.32.refs_1_), channel_id=1, source_target_pairs={{4,1},{5,0},{0,9},{1,8},{8,13},{9,12},{12,5},{13,4},{6,3},{7,2},{2... | collective-permute-start | bytes 454664 | tf_op jit(solution)/shard_map/ppermute | solution.py:343
  9.0 0.0 collective-permute-done.2.refs_0_.refs_2_
  9.0 1.3 %collective-permute-done.1.refs_4_.near_first = bf16[592,128]{1,0:T(8,128)(2,1)S(1)} collective-permute-done((bf16[592,128]{1,0:T(8,128)(2,1)S(1)}, bf16[592,128]{1,0:T(8,128)(2,1)S(1)}, u32[]{:S(2)}, u32[]{:S(2)}) %collective-permute-start.1) | collective-permute-done | bytes 151584 | tf_op jit(solution)/shard_map/ppermute | solution.py:343
  10.2 0.0 collective-permute-start.6
  10.2 3.1 %collective-permute-start.5 = (bf16[592,128]{1,0:T(8,128)(2,1)S(1)}, bf16[592,128]{1,0:T(8,128)(2,1)S(1)}, u32[]{:S(2)}, u32[]{:S(2)}) collective-permute-start(bf16[592,128]{1,0:T(8,128)(2,1)S(1)} %collective-permute-done.1.refs_4_.near_first), channel_id=1, source_target_pairs={{4,1},{5,0},{0,9},{1,8},{8,13},{9,12},{12,5},{13,4},{6,3},{7,2},{2... | collective-permute-start | bytes 454664 | tf_op jit(solution)/shard_map/ppermute | solution.py:343
  13.3 0.0 collective-permute-start.11
  13.3 0.0 collective-permute-done.4.refs_1_.refs_3_
  13.4 0.0 collective-permute-done.3.refs_5_.near_second
  13.4 0.5 %collective-permute-start.12 = (bf16[592,128]{1,0:T(8,128)(2,1)S(1)}, bf16[592,128]{1,0:T(8,128)(2,1)S(1)}, u32[]{:S(2)}, u32[]{:S(2)}) collective-permute-start(bf16[592,128]{1,0:T(8,128)(2,1)S(1)} %collective-permute-done.3.refs_5_.near_second), channel_id=1, source_target_pairs={{0,1},{1,0},{2,3},{3,2},{4,5},{5,4},{6,7},{7,6},{8,9},{9,8},{10,11... | collective-permute-start | bytes 454664 | tf_op jit(solution)/shard_map/ppermute | solution.py:357
  13.8 1.7 %collective-permute-start.8 = (bf16[592,128]{1,0:T(8,128)(2,1)S(1)}, bf16[592,128]{1,0:T(8,128)(2,1)S(1)}, u32[]{:S(2)}, u32[]{:S(2)}) collective-permute-start(bf16[592,128]{1,0:T(8,128)(2,1)S(1)} %collective-permute-done.3.refs_5_.near_second), channel_id=1, source_target_pairs={{0,3},{1,2},{2,1},{3,0},{4,7},{5,6},{6,5},{7,4},{8,11},{9,10},{10,... | collective-permute-start | bytes 454664 | tf_op jit(solution)/shard_map/ppermute | solution.py:354
  15.6 1.0 %collective-permute-done.6.refs_2_ = bf16[592,128]{1,0:T(8,128)(2,1)S(1)} collective-permute-done((bf16[592,128]{1,0:T(8,128)(2,1)S(1)}, bf16[592,128]{1,0:T(8,128)(2,1)S(1)}, u32[]{:S(2)}, u32[]{:S(2)}) %collective-permute-start.6) | collective-permute-done | bytes 151584 | tf_op jit(solution)/shard_map/ppermute | solution.py:354
  16.6 1.7 %collective-permute-start.7 = (bf16[592,128]{1,0:T(8,128)(2,1)S(1)}, bf16[592,128]{1,0:T(8,128)(2,1)S(1)}, u32[]{:S(2)}, u32[]{:S(2)}) collective-permute-start(bf16[592,128]{1,0:T(8,128)(2,1)S(1)} %collective-permute-done.3.refs_5_.near_second), channel_id=1, source_target_pairs={{4,1},{5,0},{0,9},{1,8},{8,13},{9,12},{12,5},{13,4},{6,3},{7,2},{2... | collective-permute-start | bytes 454664 | tf_op jit(solution)/shard_map/ppermute | solution.py:343
  18.3 0.0 collective-permute-done.5.refs_6_
  18.3 0.0 collective-permute-done.11.over_first
  18.3 0.0 collective-permute-done.12.over_second
  18.3 1.1 %shard_map.41 = (f32[192,896]{1,0:T(8,128)S(1)}, bf16[64,1024]{1,0:T(8,128)(2,1)S(1)}, bf16[64,1024]{1,0:T(8,128)(2,1)S(1)}, bf16[64,1024]{1,0:T(8,128)(2,1)S(1)}) custom-call(bf16[592,128]{1,0:T(8,128)(2,1)S(1)} %collective-permute-done.1.refs_4_.near_first, bf16[592,128]{1,0:T(8,128)(2,1)S(1)} %collective-permute-done.3.refs_5_.near_second, ...), custom_call_target="tpu_custom_call" | custom-call | tf_op jit(solution)/shard_map/pallas_call | solution.py:285
  19.4 0.1 collective-permute-start.13
  19.5 0.5 %collective-permute-start.14 = (bf16[64,1024]{1,0:T(8,128)(2,1)S(1)}, bf16[64,1024]{1,0:T(8,128)(2,1)S(1)}, u32[]{:S(2)}, u32[]{:S(2)}) collective-permute-start(bf16[64,1024]{1,0:T(8,128)(2,1)S(1)} %get-tuple-element.50), channel_id=1, source_target_pairs={{0,1},{1,0},{2,3},{3,2},{4,5},{5,4},{6,7},{7,6},{8,9},{9,8},{10,11... | collective-permute-start | bytes 393224 | tf_op jit(solution)/shard_map/ppermute | solution.py:357
  20.0 0.1 collective-permute-start.15
  20.1 0.0 collective-permute-done.8.refs_3_
  20.1 1.4 %collective-permute-start.9 = (bf16[592,128]{1,0:T(8,128)(2,1)S(1)}, bf16[592,128]{1,0:T(8,128)(2,1)S(1)}, u32[]{:S(2)}, u32[]{:S(2)}) collective-permute-start(bf16[592,128]{1,0:T(8,128)(2,1)S(1)} %collective-permute-done.5.refs_6_), channel_id=1, source_target_pairs={{0,3},{1,2},{2,1},{3,0},{4,7},{5,6},{6,5},{7,4},{8,11},{9,10},{10,... | collective-permute-start | bytes 454664 | tf_op jit(solution)/shard_map/ppermute | solution.py:354
  21.5 1.0 %collective-permute-done.7.refs_7_ = bf16[592,128]{1,0:T(8,128)(2,1)S(1)} collective-permute-done((bf16[592,128]{1,0:T(8,128)(2,1)S(1)}, bf16[592,128]{1,0:T(8,128)(2,1)S(1)}, u32[]{:S(2)}, u32[]{:S(2)}) %collective-permute-start.7) | collective-permute-done | bytes 151584 | tf_op jit(solution)/shard_map/ppermute | solution.py:343
  22.5 0.1 collective-permute-start
  22.7 0.0 collective-permute-done.13.refs_0_
  22.7 0.0 collective-permute-done.14.refs_1_
  22.7 0.0 collective-permute-done.15.refs_2_
  22.7 0.3 shard_map.42
  23.0 0.8 %collective-permute-start.16 = (bf16[1168,128]{1,0:T(8,128)(2,1)S(1)}, bf16[1168,128]{1,0:T(8,128)(2,1)S(1)}, u32[]{:S(2)}, u32[]{:S(2)}) collective-permute-start(bf16[1168,128]{1,0:T(8,128)(2,1)S(1)} %shard_map.42), channel_id=1, source_target_pairs={{0,5},{1,4},{8,1},{9,0},{12,9},{13,8},{4,13},{5,12},{2,7},{3,6},{1... | collective-permute-start | bytes 897032 | tf_op jit(solution)/shard_map/ppermute | solution.py:351
  23.8 2.0 %collective-permute-done.9.refs_0_ = bf16[592,128]{1,0:T(8,128)(2,1)S(1)} collective-permute-done((bf16[592,128]{1,0:T(8,128)(2,1)S(1)}, bf16[592,128]{1,0:T(8,128)(2,1)S(1)}, u32[]{:S(2)}, u32[]{:S(2)}) %collective-permute-start.9) | collective-permute-done | bytes 151584 | tf_op jit(solution)/shard_map/ppermute | solution.py:354
  25.8 1.4 %collective-permute-start.10 = (bf16[592,128]{1,0:T(8,128)(2,1)S(1)}, bf16[592,128]{1,0:T(8,128)(2,1)S(1)}, u32[]{:S(2)}, u32[]{:S(2)}) collective-permute-start(bf16[592,128]{1,0:T(8,128)(2,1)S(1)} %collective-permute-done.7.refs_7_), channel_id=1, source_target_pairs={{0,3},{1,2},{2,1},{3,0},{4,7},{5,6},{6,5},{7,4},{8,11},{9,10},{10,... | collective-permute-start | bytes 454664 | tf_op jit(solution)/shard_map/ppermute | solution.py:354
  27.2 0.0 collective-permute-done.other
  27.2 1.8 %shard_map.39 = (f32[192,896]{1,0:T(8,128)S(1)}, f32[192,896]{1,0:T(8,128)S(1)}, f32[384,128]{1,0:T(8,128)S(1)}) custom-call(bf16[1168,128]{1,0:T(8,128)(2,1)S(1)} %get-tuple-element.30.own, bf16[1168,128]{1,0:T(8,128)(2,1)S(1)} %collective-permute-done.other, bf16[592,128]{1,0:T(8,128)(2,1)S(1)} %collective-permute-done.2.refs_0_.refs_2_, ...), custom_call_target="tpu_custom_call" | custom-call | tf_op jit(solution)/shard_map/pallas_call | solution.py:285
  29.0 2.5 %collective-permute-done.10.refs_1_ = bf16[592,128]{1,0:T(8,128)(2,1)S(1)} collective-permute-done((bf16[592,128]{1,0:T(8,128)(2,1)S(1)}, bf16[592,128]{1,0:T(8,128)(2,1)S(1)}, u32[]{:S(2)}, u32[]{:S(2)}) %collective-permute-start.10) | collective-permute-done | bytes 151584 | tf_op jit(solution)/shard_map/ppermute | solution.py:354
  31.6 0.9 %shard_map.40 = (f32[192,896]{1,0:T(8,128)S(1)}, bf16[64,896]{1,0:T(8,128)(2,1)S(1)}, bf16[64,896]{1,0:T(8,128)(2,1)S(1)}, bf16[64,896]{1,0:T(8,128)(2,1)S(1)}) custom-call(bf16[1168,128]{1,0:T(8,128)(2,1)S(1)} %get-tuple-element.30.own, bf16[1168,128]{1,0:T(8,128)(2,1)S(1)} %collective-permute-done.other, ...), custom_call_target="tpu_custom_call", output_to_operand_aliasing={{0}: (5, {})} | custom-call | tf_op jit(solution)/shard_map/pallas_call | solution.py:285
  32.4 0.7 %collective-permute-start.17 = (bf16[64,896]{1,0:T(8,128)(2,1)S(1)}, bf16[64,896]{1,0:T(8,128)(2,1)S(1)}, u32[]{:S(2)}, u32[]{:S(2)}) collective-permute-start(bf16[64,896]{1,0:T(8,128)(2,1)S(1)} %get-tuple-element.52), channel_id=1, source_target_pairs={{0,1},{1,0},{2,3},{3,2},{4,5},{5,4},{6,7},{7,6},{8,9},{9,8},{10,11... | collective-permute-start | bytes 344072 | tf_op jit(solution)/shard_map/ppermute | solution.py:357
  33.1 0.1 collective-permute-start.18
  33.2 0.4 %collective-permute-start.19 = (bf16[64,896]{1,0:T(8,128)(2,1)S(1)}, bf16[64,896]{1,0:T(8,128)(2,1)S(1)}, u32[]{:S(2)}, u32[]{:S(2)}) collective-permute-start(bf16[64,896]{1,0:T(8,128)(2,1)S(1)} %get-tuple-element.54), channel_id=1, source_target_pairs={{0,1},{1,0},{2,3},{3,2},{4,5},{5,4},{6,7},{7,6},{8,9},{9,8},{10,11... | collective-permute-start | bytes 344072 | tf_op jit(solution)/shard_map/ppermute | solution.py:357
  33.6 0.5 %collective-permute-done.17.refs_0_ = bf16[64,896]{1,0:T(8,128)(2,1)S(1)} collective-permute-done((bf16[64,896]{1,0:T(8,128)(2,1)S(1)}, bf16[64,896]{1,0:T(8,128)(2,1)S(1)}, u32[]{:S(2)}, u32[]{:S(2)}) %collective-permute-start.17) | collective-permute-done | bytes 114720 | tf_op jit(solution)/shard_map/ppermute | solution.py:357
  34.1 0.4 %collective-permute-done.18.refs_1_ = bf16[64,896]{1,0:T(8,128)(2,1)S(1)} collective-permute-done((bf16[64,896]{1,0:T(8,128)(2,1)S(1)}, bf16[64,896]{1,0:T(8,128)(2,1)S(1)}, u32[]{:S(2)}, u32[]{:S(2)}) %collective-permute-start.18) | collective-permute-done | bytes 114720 | tf_op jit(solution)/shard_map/ppermute | solution.py:357
  34.4 0.2 collective-permute-done.19.refs_2_
  34.6 0.0 collective-permute-done.16.returned
  34.6 1.0 %shard_map.43 = bf16[192,768]{1,0:T(8,128)(2,1)} custom-call(f32[192,896]{1,0:T(8,128)S(1)} %get-tuple-element.45.mine, bf16[1168,128]{1,0:T(8,128)(2,1)S(1)} %collective-permute-done.16.returned, bf16[64,896]{1,0:T(8,128)(2,1)S(1)} %collective-permute-done.17.refs_0_, bf16[64,896]{1,0:T(8,128)(2,1)S(1)} %collective-permute-done.18.refs_1_, ...), custom_call_target="tpu_custom_call" | custom-call | tf_op jit(solution)/shard_map/pallas_call | solution.py:311
  (1 shorter events, 0.0 us)
Async XLA Ops:
  0.0 1.0 %copy-start = (bf16[192,768]{1,0:T(8,128)(2,1)S(1)}, bf16[192,768]{1,0:T(8,128)(2,1)}, u32[]{:S(2)}) copy-start(bf16[192,768]{1,0:T(8,128)(2,1)} %rows.3) | copy-start | bytes 884740
  1.0 5.3 %copy-start.2 = (s32[192]{0:T(256)S(1)}, s32[192]{0:T(256)}, u32[]{:S(2)}) copy-start(s32[192]{0:T(256)} %param.5) | copy-start | bytes 2308
  1.0 8.0 %collective-permute-start.2 = (bf16[592,128]{1,0:T(8,128)(2,1)S(1)}, bf16[592,128]{1,0:T(8,128)(2,1)S(1)}, u32[]{:S(2)}, u32[]{:S(2)}) collective-permute-start(bf16[592,128]{1,0:T(8,128)(2,1)S(1)} %shard_map.38.refs_0_), channel_id=1, source_target_pairs={{0,3},{1,2},{2,1},{3,0},{4,7},{5,6},{6,5},{7,4},{8,11},{9,10},{10,... | collective-permute-start | bytes 454664 | tf_op jit(solution)/shard_map/ppermute | solution.py:354
  3.4 6.8 %collective-permute-start.1 = (bf16[592,128]{1,0:T(8,128)(2,1)S(1)}, bf16[592,128]{1,0:T(8,128)(2,1)S(1)}, u32[]{:S(2)}, u32[]{:S(2)}) collective-permute-start(bf16[592,128]{1,0:T(8,128)(2,1)S(1)} %shard_map.38.refs_0_), channel_id=1, source_target_pairs={{4,1},{5,0},{0,9},{1,8},{8,13},{9,12},{12,5},{13,4},{6,3},{7,2},{2... | collective-permute-start | bytes 454664 | tf_op jit(solution)/shard_map/ppermute | solution.py:343
  6.3 0.7 %copy-start.1 = (s32[192,1]{0,1:T(1,128)S(1)}, s32[192,1]{0,1:T(1,128)}, u32[]{:S(2)}) copy-start(s32[192,1]{0,1:T(1,128)} %param.4) | copy-start | bytes 2308
  7.1 6.3 %collective-permute-start.4 = (bf16[592,128]{1,0:T(8,128)(2,1)S(1)}, bf16[592,128]{1,0:T(8,128)(2,1)S(1)}, u32[]{:S(2)}, u32[]{:S(2)}) collective-permute-start(bf16[592,128]{1,0:T(8,128)(2,1)S(1)} %get-tuple-element.32.refs_1_), channel_id=1, source_target_pairs={{0,3},{1,2},{2,1},{3,0},{4,7},{5,6},{6,5},{7,4},{8,11},{9,10},{10,... | collective-permute-start | bytes 454664 | tf_op jit(solution)/shard_map/ppermute | solution.py:354
  7.2 6.2 %collective-permute-start.3 = (bf16[592,128]{1,0:T(8,128)(2,1)S(1)}, bf16[592,128]{1,0:T(8,128)(2,1)S(1)}, u32[]{:S(2)}, u32[]{:S(2)}) collective-permute-start(bf16[592,128]{1,0:T(8,128)(2,1)S(1)} %get-tuple-element.32.refs_1_), channel_id=1, source_target_pairs={{4,1},{5,0},{0,9},{1,8},{8,13},{9,12},{12,5},{13,4},{6,3},{7,2},{2... | collective-permute-start | bytes 454664 | tf_op jit(solution)/shard_map/ppermute | solution.py:343
  10.2 6.4 %collective-permute-start.6 = (bf16[592,128]{1,0:T(8,128)(2,1)S(1)}, bf16[592,128]{1,0:T(8,128)(2,1)S(1)}, u32[]{:S(2)}, u32[]{:S(2)}) collective-permute-start(bf16[592,128]{1,0:T(8,128)(2,1)S(1)} %collective-permute-done.1.refs_4_.near_first), channel_id=1, source_target_pairs={{0,3},{1,2},{2,1},{3,0},{4,7},{5,6},{6,5},{7,4},{8,11},{9,10},{10,... | collective-permute-start | bytes 454664 | tf_op jit(solution)/shard_map/ppermute | solution.py:354
  10.2 8.1 %collective-permute-start.5 = (bf16[592,128]{1,0:T(8,128)(2,1)S(1)}, bf16[592,128]{1,0:T(8,128)(2,1)S(1)}, u32[]{:S(2)}, u32[]{:S(2)}) collective-permute-start(bf16[592,128]{1,0:T(8,128)(2,1)S(1)} %collective-permute-done.1.refs_4_.near_first), channel_id=1, source_target_pairs={{4,1},{5,0},{0,9},{1,8},{8,13},{9,12},{12,5},{13,4},{6,3},{7,2},{2... | collective-permute-start | bytes 454664 | tf_op jit(solution)/shard_map/ppermute | solution.py:343
  13.3 5.0 %collective-permute-start.11 = (bf16[592,128]{1,0:T(8,128)(2,1)S(1)}, bf16[592,128]{1,0:T(8,128)(2,1)S(1)}, u32[]{:S(2)}, u32[]{:S(2)}) collective-permute-start(bf16[592,128]{1,0:T(8,128)(2,1)S(1)} %collective-permute-done.1.refs_4_.near_first), channel_id=1, source_target_pairs={{0,1},{1,0},{2,3},{3,2},{4,5},{5,4},{6,7},{7,6},{8,9},{9,8},{10,11... | collective-permute-start | bytes 454664 | tf_op jit(solution)/shard_map/ppermute | solution.py:357
  13.4 4.9 %collective-permute-start.12 = (bf16[592,128]{1,0:T(8,128)(2,1)S(1)}, bf16[592,128]{1,0:T(8,128)(2,1)S(1)}, u32[]{:S(2)}, u32[]{:S(2)}) collective-permute-start(bf16[592,128]{1,0:T(8,128)(2,1)S(1)} %collective-permute-done.3.refs_5_.near_second), channel_id=1, source_target_pairs={{0,1},{1,0},{2,3},{3,2},{4,5},{5,4},{6,7},{7,6},{8,9},{9,8},{10,11... | collective-permute-start | bytes 454664 | tf_op jit(solution)/shard_map/ppermute | solution.py:357
  13.8 6.3 %collective-permute-start.8 = (bf16[592,128]{1,0:T(8,128)(2,1)S(1)}, bf16[592,128]{1,0:T(8,128)(2,1)S(1)}, u32[]{:S(2)}, u32[]{:S(2)}) collective-permute-start(bf16[592,128]{1,0:T(8,128)(2,1)S(1)} %collective-permute-done.3.refs_5_.near_second), channel_id=1, source_target_pairs={{0,3},{1,2},{2,1},{3,0},{4,7},{5,6},{6,5},{7,4},{8,11},{9,10},{10,... | collective-permute-start | bytes 454664 | tf_op jit(solution)/shard_map/ppermute | solution.py:354
  16.6 5.9 %collective-permute-start.7 = (bf16[592,128]{1,0:T(8,128)(2,1)S(1)}, bf16[592,128]{1,0:T(8,128)(2,1)S(1)}, u32[]{:S(2)}, u32[]{:S(2)}) collective-permute-start(bf16[592,128]{1,0:T(8,128)(2,1)S(1)} %collective-permute-done.3.refs_5_.near_second), channel_id=1, source_target_pairs={{4,1},{5,0},{0,9},{1,8},{8,13},{9,12},{12,5},{13,4},{6,3},{7,2},{2... | collective-permute-start | bytes 454664 | tf_op jit(solution)/shard_map/ppermute | solution.py:343
  19.4 3.2 %collective-permute-start.13 = (bf16[64,1024]{1,0:T(8,128)(2,1)S(1)}, bf16[64,1024]{1,0:T(8,128)(2,1)S(1)}, u32[]{:S(2)}, u32[]{:S(2)}) collective-permute-start(bf16[64,1024]{1,0:T(8,128)(2,1)S(1)} %get-tuple-element.49), channel_id=1, source_target_pairs={{0,1},{1,0},{2,3},{3,2},{4,5},{5,4},{6,7},{7,6},{8,9},{9,8},{10,11... | collective-permute-start | bytes 393224 | tf_op jit(solution)/shard_map/ppermute | solution.py:357
  19.5 3.1 %collective-permute-start.14 = (bf16[64,1024]{1,0:T(8,128)(2,1)S(1)}, bf16[64,1024]{1,0:T(8,128)(2,1)S(1)}, u32[]{:S(2)}, u32[]{:S(2)}) collective-permute-start(bf16[64,1024]{1,0:T(8,128)(2,1)S(1)} %get-tuple-element.50), channel_id=1, source_target_pairs={{0,1},{1,0},{2,3},{3,2},{4,5},{5,4},{6,7},{7,6},{8,9},{9,8},{10,11... | collective-permute-start | bytes 393224 | tf_op jit(solution)/shard_map/ppermute | solution.py:357
  20.0 2.6 %collective-permute-start.15 = (bf16[64,1024]{1,0:T(8,128)(2,1)S(1)}, bf16[64,1024]{1,0:T(8,128)(2,1)S(1)}, u32[]{:S(2)}, u32[]{:S(2)}) collective-permute-start(bf16[64,1024]{1,0:T(8,128)(2,1)S(1)} %get-tuple-element.51), channel_id=1, source_target_pairs={{0,1},{1,0},{2,3},{3,2},{4,5},{5,4},{6,7},{7,6},{8,9},{9,8},{10,11... | collective-permute-start | bytes 393224 | tf_op jit(solution)/shard_map/ppermute | solution.py:357
  20.1 5.7 %collective-permute-start.9 = (bf16[592,128]{1,0:T(8,128)(2,1)S(1)}, bf16[592,128]{1,0:T(8,128)(2,1)S(1)}, u32[]{:S(2)}, u32[]{:S(2)}) collective-permute-start(bf16[592,128]{1,0:T(8,128)(2,1)S(1)} %collective-permute-done.5.refs_6_), channel_id=1, source_target_pairs={{0,3},{1,2},{2,1},{3,0},{4,7},{5,6},{6,5},{7,4},{8,11},{9,10},{10,... | collective-permute-start | bytes 454664 | tf_op jit(solution)/shard_map/ppermute | solution.py:354
  22.5 4.6 %collective-permute-start = (bf16[1168,128]{1,0:T(8,128)(2,1)S(1)}, bf16[1168,128]{1,0:T(8,128)(2,1)S(1)}, u32[]{:S(2)}, u32[]{:S(2)}) collective-permute-start(bf16[1168,128]{1,0:T(8,128)(2,1)S(1)} %get-tuple-element.30.own), channel_id=1, source_target_pairs={{0,1},{1,0},{2,3},{3,2},{4,5},{5,4},{6,7},{7,6},{8,9},{9,8},{10,11... | collective-permute-start | bytes 897032 | tf_op jit(solution)/shard_map/ppermute | solution.py:357
  23.0 11.6 %collective-permute-start.16 = (bf16[1168,128]{1,0:T(8,128)(2,1)S(1)}, bf16[1168,128]{1,0:T(8,128)(2,1)S(1)}, u32[]{:S(2)}, u32[]{:S(2)}) collective-permute-start(bf16[1168,128]{1,0:T(8,128)(2,1)S(1)} %shard_map.42), channel_id=1, source_target_pairs={{0,5},{1,4},{8,1},{9,0},{12,9},{13,8},{4,13},{5,12},{2,7},{3,6},{1... | collective-permute-start | bytes 897032 | tf_op jit(solution)/shard_map/ppermute | solution.py:351
  25.8 5.8 %collective-permute-start.10 = (bf16[592,128]{1,0:T(8,128)(2,1)S(1)}, bf16[592,128]{1,0:T(8,128)(2,1)S(1)}, u32[]{:S(2)}, u32[]{:S(2)}) collective-permute-start(bf16[592,128]{1,0:T(8,128)(2,1)S(1)} %collective-permute-done.7.refs_7_), channel_id=1, source_target_pairs={{0,3},{1,2},{2,1},{3,0},{4,7},{5,6},{6,5},{7,4},{8,11},{9,10},{10,... | collective-permute-start | bytes 454664 | tf_op jit(solution)/shard_map/ppermute | solution.py:354
  32.4 1.6 %collective-permute-start.17 = (bf16[64,896]{1,0:T(8,128)(2,1)S(1)}, bf16[64,896]{1,0:T(8,128)(2,1)S(1)}, u32[]{:S(2)}, u32[]{:S(2)}) collective-permute-start(bf16[64,896]{1,0:T(8,128)(2,1)S(1)} %get-tuple-element.52), channel_id=1, source_target_pairs={{0,1},{1,0},{2,3},{3,2},{4,5},{5,4},{6,7},{7,6},{8,9},{9,8},{10,11... | collective-permute-start | bytes 344072 | tf_op jit(solution)/shard_map/ppermute | solution.py:357
  33.1 1.3 %collective-permute-start.18 = (bf16[64,896]{1,0:T(8,128)(2,1)S(1)}, bf16[64,896]{1,0:T(8,128)(2,1)S(1)}, u32[]{:S(2)}, u32[]{:S(2)}) collective-permute-start(bf16[64,896]{1,0:T(8,128)(2,1)S(1)} %get-tuple-element.53), channel_id=1, source_target_pairs={{0,1},{1,0},{2,3},{3,2},{4,5},{5,4},{6,7},{7,6},{8,9},{9,8},{10,11... | collective-permute-start | bytes 344072 | tf_op jit(solution)/shard_map/ppermute | solution.py:357
  33.2 1.4 %collective-permute-start.19 = (bf16[64,896]{1,0:T(8,128)(2,1)S(1)}, bf16[64,896]{1,0:T(8,128)(2,1)S(1)}, u32[]{:S(2)}, u32[]{:S(2)}) collective-permute-start(bf16[64,896]{1,0:T(8,128)(2,1)S(1)} %get-tuple-element.54), channel_id=1, source_target_pairs={{0,1},{1,0},{2,3},{3,2},{4,5},{5,4},{6,7},{7,6},{8,9},{9,8},{10,11... | collective-permute-start | bytes 344072 | tf_op jit(solution)/shard_map/ppermute | solution.py:357

commit v36 on v32

--- a/solution.py
+++ b/solution.py
@@ -390,9 +390,9 @@
     last_half, first_crossed = together(along_by[-1][1], first_crossed)
     across_by.append((first_crossed, across(last_half)))
     left = (whole, other_core(whole))
-    early = across_by[:-1] + along_by[1:-1]
+    early = across_by[:-1] + along_by[1:]
     mine, theirs, info = start_both(left, early, (rows_here, width + 128))
-    late = [along_by[-1], across_by[-1]]
+    late = [across_by[-1]]
     mine, *theirs = add_both((*left, info), late, (mine, theirs))
     out = finish(
         (rows_here, width), [mine, returned, *[other_core(part) for part in theirs]]

time: 35.3 us -> 35.3 us (level)
  no operation moved by 1% of the time
where the time goes in v36:
time: 35.3 us; the launch traced here: 35.1 us
  starting transfers between devices  19.8 us (56%)
  waiting for transfers between devices  8.36 us (24%)
  Pallas kernels  5.29 us (15%)
  local copies, waits for them, and re-layouts  1.64 us (5%)
    ppermute x4, starting transfers between devices, along(): return lax.ppermute(rows, ('blk', 'pair'), hops)  9.42 us
    ppermute x6, starting transfers between devices, across(): return lax.ppermute(rows, ('sub', 'pair'), [(0, 3), (1, 2), (2, 1), (3, 0)])  6.7 us
    pallas_call x6, Pallas kernels, call(): pl.pallas_call(kernel, out_shape=[jax.ShapeDtypeStruct(shape, dtype) for...  4.26 us
    ppermute x6, waiting for transfers between devices, across(): return lax.ppermute(rows, ('sub', 'pair'), [(0, 3), (1, 2), (2, 1), (3, 0)])  3.78 us
    ppermute x9, starting transfers between devices, other_core(): return lax.ppermute(rows, 'pair', [(0, 1), (1, 0)])  2.83 us
    ppermute x4, waiting for transfers between devices, along(): return lax.ppermute(rows, ('blk', 'pair'), hops)  2.4 us
    unnamed x6, local copies, waits for them, and re-layouts  1.64 us
    ppermute x1, waiting for transfers between devices, back_along(): return lax.ppermute(rows, ('blk', 'pair'), hops)  1.21 us
  transfers between devices with their start and end apart: 20, of which 6 were waited for; matrix products, arithmetic and copies ran while one was open for 0% of the time, Pallas kernels for 12%

profile of v36, /device:TPU:0, one launch (start us, length us, event | category | flops | bytes accessed | tf_op | source)
XLA Modules:
  0.0 35.1 jit_solution(7888513644176750331)
XLA Ops:
  0.0 0.0 copy-start
  0.0 1.0 %copy-done = bf16[192,768]{1,0:T(8,128)(2,1)S(1)} copy-done((bf16[192,768]{1,0:T(8,128)(2,1)S(1)}, bf16[192,768]{1,0:T(8,128)(2,1)}, u32[]{:S(2)}) %copy-start) | copy-done | bytes 294936
  1.0 0.0 copy-start.2
  1.0 2.4 %collective-permute-start.2 = (bf16[592,128]{1,0:T(8,128)(2,1)S(1)}, bf16[592,128]{1,0:T(8,128)(2,1)S(1)}, u32[]{:S(2)}, u32[]{:S(2)}) collective-permute-start(bf16[592,128]{1,0:T(8,128)(2,1)S(1)} %shard_map.38.refs_0_), channel_id=1, source_target_pairs={{0,3},{1,2},{2,1},{3,0},{4,7},{5,6},{6,5},{7,4},{8,11},{9,10},{10,... | collective-permute-start | bytes 454664 | tf_op jit(solution)/shard_map/ppermute | solution.py:353
  3.4 2.9 %collective-permute-start.1 = (bf16[592,128]{1,0:T(8,128)(2,1)S(1)}, bf16[592,128]{1,0:T(8,128)(2,1)S(1)}, u32[]{:S(2)}, u32[]{:S(2)}) collective-permute-start(bf16[592,128]{1,0:T(8,128)(2,1)S(1)} %shard_map.38.refs_0_), channel_id=1, source_target_pairs={{4,1},{5,0},{0,9},{1,8},{8,13},{9,12},{12,5},{13,4},{6,3},{7,2},{2... | collective-permute-start | bytes 454664 | tf_op jit(solution)/shard_map/ppermute | solution.py:342
  6.3 0.0 copy-start.1
  6.3 0.0 copy-done.2
  6.3 0.7 %copy-done.1 = s32[192,1]{0,1:T(1,128)S(1)} copy-done((s32[192,1]{0,1:T(1,128)S(1)}, s32[192,1]{0,1:T(1,128)}, u32[]{:S(2)}) %copy-start.1) | copy-done | bytes 792
  7.0 0.1 shard_map.37
  7.1 0.1 collective-permute-start.4
  7.2 1.8 %collective-permute-start.3 = (bf16[592,128]{1,0:T(8,128)(2,1)S(1)}, bf16[592,128]{1,0:T(8,128)(2,1)S(1)}, u32[]{:S(2)}, u32[]{:S(2)}) collective-permute-start(bf16[592,128]{1,0:T(8,128)(2,1)S(1)} %get-tuple-element.32.refs_1_), channel_id=1, source_target_pairs={{4,1},{5,0},{0,9},{1,8},{8,13},{9,12},{12,5},{13,4},{6,3},{7,2},{2... | collective-permute-start | bytes 454664 | tf_op jit(solution)/shard_map/ppermute | solution.py:342
  9.0 0.0 collective-permute-done.2.refs_0_.refs_2_
  9.0 1.3 %collective-permute-done.1.refs_4_.near_first = bf16[592,128]{1,0:T(8,128)(2,1)S(1)} collective-permute-done((bf16[592,128]{1,0:T(8,128)(2,1)S(1)}, bf16[592,128]{1,0:T(8,128)(2,1)S(1)}, u32[]{:S(2)}, u32[]{:S(2)}) %collective-permute-start.1) | collective-permute-done | bytes 151584 | tf_op jit(solution)/shard_map/ppermute | solution.py:342
  10.2 0.0 collective-permute-start.6
  10.2 3.1 %collective-permute-start.5 = (bf16[592,128]{1,0:T(8,128)(2,1)S(1)}, bf16[592,128]{1,0:T(8,128)(2,1)S(1)}, u32[]{:S(2)}, u32[]{:S(2)}) collective-permute-start(bf16[592,128]{1,0:T(8,128)(2,1)S(1)} %collective-permute-done.1.refs_4_.near_first), channel_id=1, source_target_pairs={{4,1},{5,0},{0,9},{1,8},{8,13},{9,12},{12,5},{13,4},{6,3},{7,2},{2... | collective-permute-start | bytes 454664 | tf_op jit(solution)/shard_map/ppermute | solution.py:342
  13.3 0.0 collective-permute-start.11
  13.3 0.0 collective-permute-done.4.refs_1_.refs_3_
  13.4 0.0 collective-permute-done.3.refs_5_.near_second
  13.4 0.5 %collective-permute-start.12 = (bf16[592,128]{1,0:T(8,128)(2,1)S(1)}, bf16[592,128]{1,0:T(8,128)(2,1)S(1)}, u32[]{:S(2)}, u32[]{:S(2)}) collective-permute-start(bf16[592,128]{1,0:T(8,128)(2,1)S(1)} %collective-permute-done.3.refs_5_.near_second), channel_id=1, source_target_pairs={{0,1},{1,0},{2,3},{3,2},{4,5},{5,4},{6,7},{7,6},{8,9},{9,8},{10,11... | collective-permute-start | bytes 454664 | tf_op jit(solution)/shard_map/ppermute | solution.py:356
  13.8 1.7 %collective-permute-start.8 = (bf16[592,128]{1,0:T(8,128)(2,1)S(1)}, bf16[592,128]{1,0:T(8,128)(2,1)S(1)}, u32[]{:S(2)}, u32[]{:S(2)}) collective-permute-start(bf16[592,128]{1,0:T(8,128)(2,1)S(1)} %collective-permute-done.3.refs_5_.near_second), channel_id=1, source_target_pairs={{0,3},{1,2},{2,1},{3,0},{4,7},{5,6},{6,5},{7,4},{8,11},{9,10},{10,... | collective-permute-start | bytes 454664 | tf_op jit(solution)/shard_map/ppermute | solution.py:353
  15.6 1.0 %collective-permute-done.6.refs_2_ = bf16[592,128]{1,0:T(8,128)(2,1)S(1)} collective-permute-done((bf16[592,128]{1,0:T(8,128)(2,1)S(1)}, bf16[592,128]{1,0:T(8,128)(2,1)S(1)}, u32[]{:S(2)}, u32[]{:S(2)}) %collective-permute-start.6) | collective-permute-done | bytes 151584 | tf_op jit(solution)/shard_map/ppermute | solution.py:353
  16.6 1.7 %collective-permute-start.7 = (bf16[592,128]{1,0:T(8,128)(2,1)S(1)}, bf16[592,128]{1,0:T(8,128)(2,1)S(1)}, u32[]{:S(2)}, u32[]{:S(2)}) collective-permute-start(bf16[592,128]{1,0:T(8,128)(2,1)S(1)} %collective-permute-done.3.refs_5_.near_second), channel_id=1, source_target_pairs={{4,1},{5,0},{0,9},{1,8},{8,13},{9,12},{12,5},{13,4},{6,3},{7,2},{2... | collective-permute-start | bytes 454664 | tf_op jit(solution)/shard_map/ppermute | solution.py:342
  18.3 0.0 collective-permute-done.5.refs_6_
  18.3 1.1 %collective-permute-start.9 = (bf16[592,128]{1,0:T(8,128)(2,1)S(1)}, bf16[592,128]{1,0:T(8,128)(2,1)S(1)}, u32[]{:S(2)}, u32[]{:S(2)}) collective-permute-start(bf16[592,128]{1,0:T(8,128)(2,1)S(1)} %collective-permute-done.5.refs_6_), channel_id=1, source_target_pairs={{0,3},{1,2},{2,1},{3,0},{4,7},{5,6},{6,5},{7,4},{8,11},{9,10},{10,... | collective-permute-start | bytes 454664 | tf_op jit(solution)/shard_map/ppermute | solution.py:353
  19.4 0.0 collective-permute-done.11.over_first
  19.4 0.3 collective-permute-start
  19.7 0.0 collective-permute-done.12.over_second
  19.7 1.1 %shard_map.41 = (f32[192,896]{1,0:T(8,128)S(1)}, bf16[64,896]{1,0:T(8,128)(2,1)S(1)}, bf16[64,896]{1,0:T(8,128)(2,1)S(1)}, bf16[64,896]{1,0:T(8,128)(2,1)S(1)}) custom-call(bf16[592,128]{1,0:T(8,128)(2,1)S(1)} %collective-permute-done.1.refs_4_.near_first, bf16[592,128]{1,0:T(8,128)(2,1)S(1)} %collective-permute-done.3.refs_5_.near_second, ...), custom_call_target="tpu_custom_call" | custom-call | tf_op jit(solution)/shard_map/pallas_call | solution.py:284
  20.8 0.3 collective-permute-start.13
  21.1 0.0 collective-permute-done.8.refs_3_
  21.1 0.3 collective-permute-start.14
  21.4 1.1 %collective-permute-done.7.refs_7_ = bf16[592,128]{1,0:T(8,128)(2,1)S(1)} collective-permute-done((bf16[592,128]{1,0:T(8,128)(2,1)S(1)}, bf16[592,128]{1,0:T(8,128)(2,1)S(1)}, u32[]{:S(2)}, u32[]{:S(2)}) %collective-permute-start.7) | collective-permute-done | bytes 151584 | tf_op jit(solution)/shard_map/ppermute | solution.py:342
  22.5 0.4 %collective-permute-start.15 = (bf16[64,896]{1,0:T(8,128)(2,1)S(1)}, bf16[64,896]{1,0:T(8,128)(2,1)S(1)}, u32[]{:S(2)}, u32[]{:S(2)}) collective-permute-start(bf16[64,896]{1,0:T(8,128)(2,1)S(1)} %get-tuple-element.51), channel_id=1, source_target_pairs={{0,1},{1,0},{2,3},{3,2},{4,5},{5,4},{6,7},{7,6},{8,9},{9,8},{10,11... | collective-permute-start | bytes 344072 | tf_op jit(solution)/shard_map/ppermute | solution.py:356
  23.0 0.0 collective-permute-done.13.refs_0_
  23.0 0.0 collective-permute-done.14.refs_1_
  23.0 1.0 %collective-permute-done.15.refs_2_ = bf16[64,896]{1,0:T(8,128)(2,1)S(1)} collective-permute-done((bf16[64,896]{1,0:T(8,128)(2,1)S(1)}, bf16[64,896]{1,0:T(8,128)(2,1)S(1)}, u32[]{:S(2)}, u32[]{:S(2)}) %collective-permute-start.15) | collective-permute-done | bytes 114720 | tf_op jit(solution)/shard_map/ppermute | solution.py:356
  23.9 0.3 shard_map.42
  24.2 0.8 %collective-permute-start.16 = (bf16[1168,128]{1,0:T(8,128)(2,1)S(1)}, bf16[1168,128]{1,0:T(8,128)(2,1)S(1)}, u32[]{:S(2)}, u32[]{:S(2)}) collective-permute-start(bf16[1168,128]{1,0:T(8,128)(2,1)S(1)} %shard_map.42), channel_id=1, source_target_pairs={{0,5},{1,4},{8,1},{9,0},{12,9},{13,8},{4,13},{5,12},{2,7},{3,6},{1... | collective-permute-start | bytes 897032 | tf_op jit(solution)/shard_map/ppermute | solution.py:350
  25.1 0.0 collective-permute-done.9.refs_0_
  25.1 1.3 %collective-permute-start.10 = (bf16[592,128]{1,0:T(8,128)(2,1)S(1)}, bf16[592,128]{1,0:T(8,128)(2,1)S(1)}, u32[]{:S(2)}, u32[]{:S(2)}) collective-permute-start(bf16[592,128]{1,0:T(8,128)(2,1)S(1)} %collective-permute-done.7.refs_7_), channel_id=1, source_target_pairs={{0,3},{1,2},{2,1},{3,0},{4,7},{5,6},{6,5},{7,4},{8,11},{9,10},{10,... | collective-permute-start | bytes 454664 | tf_op jit(solution)/shard_map/ppermute | solution.py:353
  26.4 0.0 collective-permute-done.other
  26.4 1.8 %shard_map.39 = (f32[192,896]{1,0:T(8,128)S(1)}, f32[192,896]{1,0:T(8,128)S(1)}, f32[384,128]{1,0:T(8,128)S(1)}) custom-call(bf16[1168,128]{1,0:T(8,128)(2,1)S(1)} %get-tuple-element.30.own, bf16[1168,128]{1,0:T(8,128)(2,1)S(1)} %collective-permute-done.other, bf16[592,128]{1,0:T(8,128)(2,1)S(1)} %collective-permute-done.2.refs_0_.refs_2_, ...), custom_call_target="tpu_custom_call" | custom-call | tf_op jit(solution)/shard_map/pallas_call | solution.py:284
  28.2 2.7 %collective-permute-done.10.refs_1_ = bf16[592,128]{1,0:T(8,128)(2,1)S(1)} collective-permute-done((bf16[592,128]{1,0:T(8,128)(2,1)S(1)}, bf16[592,128]{1,0:T(8,128)(2,1)S(1)}, u32[]{:S(2)}, u32[]{:S(2)}) %collective-permute-start.10) | collective-permute-done | bytes 151584 | tf_op jit(solution)/shard_map/ppermute | solution.py:353
  30.9 0.9 %shard_map.40 = (f32[192,896]{1,0:T(8,128)S(1)}, bf16[64,896]{1,0:T(8,128)(2,1)S(1)}, bf16[64,896]{1,0:T(8,128)(2,1)S(1)}, bf16[64,896]{1,0:T(8,128)(2,1)S(1)}) custom-call(bf16[1168,128]{1,0:T(8,128)(2,1)S(1)} %get-tuple-element.30.own, bf16[1168,128]{1,0:T(8,128)(2,1)S(1)} %collective-permute-done.other, ...), custom_call_target="tpu_custom_call", output_to_operand_aliasing={{0}: (5, {})} | custom-call | tf_op jit(solution)/shard_map/pallas_call | solution.py:284
  31.8 0.5 %collective-permute-start.17 = (bf16[64,896]{1,0:T(8,128)(2,1)S(1)}, bf16[64,896]{1,0:T(8,128)(2,1)S(1)}, u32[]{:S(2)}, u32[]{:S(2)}) collective-permute-start(bf16[64,896]{1,0:T(8,128)(2,1)S(1)} %get-tuple-element.52), channel_id=1, source_target_pairs={{0,1},{1,0},{2,3},{3,2},{4,5},{5,4},{6,7},{7,6},{8,9},{9,8},{10,11... | collective-permute-start | bytes 344072 | tf_op jit(solution)/shard_map/ppermute | solution.py:356
  32.4 0.1 collective-permute-start.18
  32.4 0.4 %collective-permute-start.19 = (bf16[64,896]{1,0:T(8,128)(2,1)S(1)}, bf16[64,896]{1,0:T(8,128)(2,1)S(1)}, u32[]{:S(2)}, u32[]{:S(2)}) collective-permute-start(bf16[64,896]{1,0:T(8,128)(2,1)S(1)} %get-tuple-element.54), channel_id=1, source_target_pairs={{0,1},{1,0},{2,3},{3,2},{4,5},{5,4},{6,7},{7,6},{8,9},{9,8},{10,11... | collective-permute-start | bytes 344072 | tf_op jit(solution)/shard_map/ppermute | solution.py:356
  32.9 1.2 %collective-permute-done.16.returned = bf16[1168,128]{1,0:T(8,128)(2,1)S(1)} collective-permute-done((bf16[1168,128]{1,0:T(8,128)(2,1)S(1)}, bf16[1168,128]{1,0:T(8,128)(2,1)S(1)}, u32[]{:S(2)}, u32[]{:S(2)}) %collective-permute-start.16) | collective-permute-done | bytes 299040 | tf_op jit(solution)/shard_map/ppermute | solution.py:350
  34.1 0.0 collective-permute-done.17.refs_0_
  34.1 0.0 collective-permute-done.18.refs_1_
  34.1 0.0 collective-permute-done.19.refs_2_
  34.1 1.0 %shard_map.43 = bf16[192,768]{1,0:T(8,128)(2,1)} custom-call(f32[192,896]{1,0:T(8,128)S(1)} %get-tuple-element.45.mine, bf16[1168,128]{1,0:T(8,128)(2,1)S(1)} %collective-permute-done.16.returned, bf16[64,896]{1,0:T(8,128)(2,1)S(1)} %collective-permute-done.17.refs_0_, bf16[64,896]{1,0:T(8,128)(2,1)S(1)} %collective-permute-done.18.refs_1_, ...), custom_call_target="tpu_custom_call" | custom-call | tf_op jit(solution)/shard_map/pallas_call | solution.py:310
  (1 shorter events, 0.0 us)
Async XLA Ops:
  0.0 1.0 %copy-start = (bf16[192,768]{1,0:T(8,128)(2,1)S(1)}, bf16[192,768]{1,0:T(8,128)(2,1)}, u32[]{:S(2)}) copy-start(bf16[192,768]{1,0:T(8,128)(2,1)} %rows.3) | copy-start | bytes 884740
  1.0 5.3 %copy-start.2 = (s32[192]{0:T(256)S(1)}, s32[192]{0:T(256)}, u32[]{:S(2)}) copy-start(s32[192]{0:T(256)} %param.5) | copy-start | bytes 2308
  1.0 8.0 %collective-permute-start.2 = (bf16[592,128]{1,0:T(8,128)(2,1)S(1)}, bf16[592,128]{1,0:T(8,128)(2,1)S(1)}, u32[]{:S(2)}, u32[]{:S(2)}) collective-permute-start(bf16[592,128]{1,0:T(8,128)(2,1)S(1)} %shard_map.38.refs_0_), channel_id=1, source_target_pairs={{0,3},{1,2},{2,1},{3,0},{4,7},{5,6},{6,5},{7,4},{8,11},{9,10},{10,... | collective-permute-start | bytes 454664 | tf_op jit(solution)/shard_map/ppermute | solution.py:353
  3.4 6.8 %collective-permute-start.1 = (bf16[592,128]{1,0:T(8,128)(2,1)S(1)}, bf16[592,128]{1,0:T(8,128)(2,1)S(1)}, u32[]{:S(2)}, u32[]{:S(2)}) collective-permute-start(bf16[592,128]{1,0:T(8,128)(2,1)S(1)} %shard_map.38.refs_0_), channel_id=1, source_target_pairs={{4,1},{5,0},{0,9},{1,8},{8,13},{9,12},{12,5},{13,4},{6,3},{7,2},{2... | collective-permute-start | bytes 454664 | tf_op jit(solution)/shard_map/ppermute | solution.py:342
  6.3 0.7 %copy-start.1 = (s32[192,1]{0,1:T(1,128)S(1)}, s32[192,1]{0,1:T(1,128)}, u32[]{:S(2)}) copy-start(s32[192,1]{0,1:T(1,128)} %param.4) | copy-start | bytes 2308
  7.1 6.3 %collective-permute-start.4 = (bf16[592,128]{1,0:T(8,128)(2,1)S(1)}, bf16[592,128]{1,0:T(8,128)(2,1)S(1)}, u32[]{:S(2)}, u32[]{:S(2)}) collective-permute-start(bf16[592,128]{1,0:T(8,128)(2,1)S(1)} %get-tuple-element.32.refs_1_), channel_id=1, source_target_pairs={{0,3},{1,2},{2,1},{3,0},{4,7},{5,6},{6,5},{7,4},{8,11},{9,10},{10,... | collective-permute-start | bytes 454664 | tf_op jit(solution)/shard_map/ppermute | solution.py:353
  7.2 6.2 %collective-permute-start.3 = (bf16[592,128]{1,0:T(8,128)(2,1)S(1)}, bf16[592,128]{1,0:T(8,128)(2,1)S(1)}, u32[]{:S(2)}, u32[]{:S(2)}) collective-permute-start(bf16[592,128]{1,0:T(8,128)(2,1)S(1)} %get-tuple-element.32.refs_1_), channel_id=1, source_target_pairs={{4,1},{5,0},{0,9},{1,8},{8,13},{9,12},{12,5},{13,4},{6,3},{7,2},{2... | collective-permute-start | bytes 454664 | tf_op jit(solution)/shard_map/ppermute | solution.py:342
  10.2 6.4 %collective-permute-start.6 = (bf16[592,128]{1,0:T(8,128)(2,1)S(1)}, bf16[592,128]{1,0:T(8,128)(2,1)S(1)}, u32[]{:S(2)}, u32[]{:S(2)}) collective-permute-start(bf16[592,128]{1,0:T(8,128)(2,1)S(1)} %collective-permute-done.1.refs_4_.near_first), channel_id=1, source_target_pairs={{0,3},{1,2},{2,1},{3,0},{4,7},{5,6},{6,5},{7,4},{8,11},{9,10},{10,... | collective-permute-start | bytes 454664 | tf_op jit(solution)/shard_map/ppermute | solution.py:353
  10.2 8.1 %collective-permute-start.5 = (bf16[592,128]{1,0:T(8,128)(2,1)S(1)}, bf16[592,128]{1,0:T(8,128)(2,1)S(1)}, u32[]{:S(2)}, u32[]{:S(2)}) collective-permute-start(bf16[592,128]{1,0:T(8,128)(2,1)S(1)} %collective-permute-done.1.refs_4_.near_first), channel_id=1, source_target_pairs={{4,1},{5,0},{0,9},{1,8},{8,13},{9,12},{12,5},{13,4},{6,3},{7,2},{2... | collective-permute-start | bytes 454664 | tf_op jit(solution)/shard_map/ppermute | solution.py:342
  13.3 6.1 %collective-permute-start.11 = (bf16[592,128]{1,0:T(8,128)(2,1)S(1)}, bf16[592,128]{1,0:T(8,128)(2,1)S(1)}, u32[]{:S(2)}, u32[]{:S(2)}) collective-permute-start(bf16[592,128]{1,0:T(8,128)(2,1)S(1)} %collective-permute-done.1.refs_4_.near_first), channel_id=1, source_target_pairs={{0,1},{1,0},{2,3},{3,2},{4,5},{5,4},{6,7},{7,6},{8,9},{9,8},{10,11... | collective-permute-start | bytes 454664 | tf_op jit(solution)/shard_map/ppermute | solution.py:356
  13.4 6.3 %collective-permute-start.12 = (bf16[592,128]{1,0:T(8,128)(2,1)S(1)}, bf16[592,128]{1,0:T(8,128)(2,1)S(1)}, u32[]{:S(2)}, u32[]{:S(2)}) collective-permute-start(bf16[592,128]{1,0:T(8,128)(2,1)S(1)} %collective-permute-done.3.refs_5_.near_second), channel_id=1, source_target_pairs={{0,1},{1,0},{2,3},{3,2},{4,5},{5,4},{6,7},{7,6},{8,9},{9,8},{10,11... | collective-permute-start | bytes 454664 | tf_op jit(solution)/shard_map/ppermute | solution.py:356
  13.8 7.2 %collective-permute-start.8 = (bf16[592,128]{1,0:T(8,128)(2,1)S(1)}, bf16[592,128]{1,0:T(8,128)(2,1)S(1)}, u32[]{:S(2)}, u32[]{:S(2)}) collective-permute-start(bf16[592,128]{1,0:T(8,128)(2,1)S(1)} %collective-permute-done.3.refs_5_.near_second), channel_id=1, source_target_pairs={{0,3},{1,2},{2,1},{3,0},{4,7},{5,6},{6,5},{7,4},{8,11},{9,10},{10,... | collective-permute-start | bytes 454664 | tf_op jit(solution)/shard_map/ppermute | solution.py:353
  16.6 5.9 %collective-permute-start.7 = (bf16[592,128]{1,0:T(8,128)(2,1)S(1)}, bf16[592,128]{1,0:T(8,128)(2,1)S(1)}, u32[]{:S(2)}, u32[]{:S(2)}) collective-permute-start(bf16[592,128]{1,0:T(8,128)(2,1)S(1)} %collective-permute-done.3.refs_5_.near_second), channel_id=1, source_target_pairs={{4,1},{5,0},{0,9},{1,8},{8,13},{9,12},{12,5},{13,4},{6,3},{7,2},{2... | collective-permute-start | bytes 454664 | tf_op jit(solution)/shard_map/ppermute | solution.py:342
  18.3 6.8 %collective-permute-start.9 = (bf16[592,128]{1,0:T(8,128)(2,1)S(1)}, bf16[592,128]{1,0:T(8,128)(2,1)S(1)}, u32[]{:S(2)}, u32[]{:S(2)}) collective-permute-start(bf16[592,128]{1,0:T(8,128)(2,1)S(1)} %collective-permute-done.5.refs_6_), channel_id=1, source_target_pairs={{0,3},{1,2},{2,1},{3,0},{4,7},{5,6},{6,5},{7,4},{8,11},{9,10},{10,... | collective-permute-start | bytes 454664 | tf_op jit(solution)/shard_map/ppermute | solution.py:353
  19.4 7.0 %collective-permute-start = (bf16[1168,128]{1,0:T(8,128)(2,1)S(1)}, bf16[1168,128]{1,0:T(8,128)(2,1)S(1)}, u32[]{:S(2)}, u32[]{:S(2)}) collective-permute-start(bf16[1168,128]{1,0:T(8,128)(2,1)S(1)} %get-tuple-element.30.own), channel_id=1, source_target_pairs={{0,1},{1,0},{2,3},{3,2},{4,5},{5,4},{6,7},{7,6},{8,9},{9,8},{10,11... | collective-permute-start | bytes 897032 | tf_op jit(solution)/shard_map/ppermute | solution.py:356
  20.8 2.1 %collective-permute-start.13 = (bf16[64,896]{1,0:T(8,128)(2,1)S(1)}, bf16[64,896]{1,0:T(8,128)(2,1)S(1)}, u32[]{:S(2)}, u32[]{:S(2)}) collective-permute-start(bf16[64,896]{1,0:T(8,128)(2,1)S(1)} %get-tuple-element.49), channel_id=1, source_target_pairs={{0,1},{1,0},{2,3},{3,2},{4,5},{5,4},{6,7},{7,6},{8,9},{9,8},{10,11... | collective-permute-start | bytes 344072 | tf_op jit(solution)/shard_map/ppermute | solution.py:356
  21.1 1.9 %collective-permute-start.14 = (bf16[64,896]{1,0:T(8,128)(2,1)S(1)}, bf16[64,896]{1,0:T(8,128)(2,1)S(1)}, u32[]{:S(2)}, u32[]{:S(2)}) collective-permute-start(bf16[64,896]{1,0:T(8,128)(2,1)S(1)} %get-tuple-element.50), channel_id=1, source_target_pairs={{0,1},{1,0},{2,3},{3,2},{4,5},{5,4},{6,7},{7,6},{8,9},{9,8},{10,11... | collective-permute-start | bytes 344072 | tf_op jit(solution)/shard_map/ppermute | solution.py:356
  22.5 1.4 %collective-permute-start.15 = (bf16[64,896]{1,0:T(8,128)(2,1)S(1)}, bf16[64,896]{1,0:T(8,128)(2,1)S(1)}, u32[]{:S(2)}, u32[]{:S(2)}) collective-permute-start(bf16[64,896]{1,0:T(8,128)(2,1)S(1)} %get-tuple-element.51), channel_id=1, source_target_pairs={{0,1},{1,0},{2,3},{3,2},{4,5},{5,4},{6,7},{7,6},{8,9},{9,8},{10,11... | collective-permute-start | bytes 344072 | tf_op jit(solution)/shard_map/ppermute | solution.py:356
  24.2 9.9 %collective-permute-start.16 = (bf16[1168,128]{1,0:T(8,128)(2,1)S(1)}, bf16[1168,128]{1,0:T(8,128)(2,1)S(1)}, u32[]{:S(2)}, u32[]{:S(2)}) collective-permute-start(bf16[1168,128]{1,0:T(8,128)(2,1)S(1)} %shard_map.42), channel_id=1, source_target_pairs={{0,5},{1,4},{8,1},{9,0},{12,9},{13,8},{4,13},{5,12},{2,7},{3,6},{1... | collective-permute-start | bytes 897032 | tf_op jit(solution)/shard_map/ppermute | solution.py:350
  25.1 5.9 %collective-permute-start.10 = (bf16[592,128]{1,0:T(8,128)(2,1)S(1)}, bf16[592,128]{1,0:T(8,128)(2,1)S(1)}, u32[]{:S(2)}, u32[]{:S(2)}) collective-permute-start(bf16[592,128]{1,0:T(8,128)(2,1)S(1)} %collective-permute-done.7.refs_7_), channel_id=1, source_target_pairs={{0,3},{1,2},{2,1},{3,0},{4,7},{5,6},{6,5},{7,4},{8,11},{9,10},{10,... | collective-permute-start | bytes 454664 | tf_op jit(solution)/shard_map/ppermute | solution.py:353
  31.8 2.2 %collective-permute-start.17 = (bf16[64,896]{1,0:T(8,128)(2,1)S(1)}, bf16[64,896]{1,0:T(8,128)(2,1)S(1)}, u32[]{:S(2)}, u32[]{:S(2)}) collective-permute-start(bf16[64,896]{1,0:T(8,128)(2,1)S(1)} %get-tuple-element.52), channel_id=1, source_target_pairs={{0,1},{1,0},{2,3},{3,2},{4,5},{5,4},{6,7},{7,6},{8,9},{9,8},{10,11... | collective-permute-start | bytes 344072 | tf_op jit(solution)/shard_map/ppermute | solution.py:356
  32.4 1.7 %collective-permute-start.18 = (bf16[64,896]{1,0:T(8,128)(2,1)S(1)}, bf16[64,896]{1,0:T(8,128)(2,1)S(1)}, u32[]{:S(2)}, u32[]{:S(2)}) collective-permute-start(bf16[64,896]{1,0:T(8,128)(2,1)S(1)} %get-tuple-element.53), channel_id=1, source_target_pairs={{0,1},{1,0},{2,3},{3,2},{4,5},{5,4},{6,7},{7,6},{8,9},{9,8},{10,11... | collective-permute-start | bytes 344072 | tf_op jit(solution)/shard_map/ppermute | solution.py:356
  32.4 1.6 %collective-permute-start.19 = (bf16[64,896]{1,0:T(8,128)(2,1)S(1)}, bf16[64,896]{1,0:T(8,128)(2,1)S(1)}, u32[]{:S(2)}, u32[]{:S(2)}) collective-permute-start(bf16[64,896]{1,0:T(8,128)(2,1)S(1)} %get-tuple-element.54), channel_id=1, source_target_pairs={{0,1},{1,0},{2,3},{3,2},{4,5},{5,4},{6,7},{7,6},{8,9},{9,8},{10,11... | collective-permute-start | bytes 344072 | tf_op jit(solution)/shard_map/ppermute | solution.py:356

commit v37 on v36

--- a/solution.py
+++ b/solution.py
@@ -355,7 +355,7 @@
     def other_core(rows):
         return lax.ppermute(rows, "pair", [(0, 1), (1, 0)])
 
-    (first,) = call(first_pack_kernel, [((slabs * half + LINES, 128), BF16)], [embeddings])
+    (first,) = call(first_pack_kernel, [((slabs * half + LINES // 2, 128), BF16)], [embeddings])
     whole, second = call(
         pack_kernel,
         [((slabs * count + LINES, 128), BF16) for count in (rows_here, half)],

time: 35.3 us -> 34.9 us (0.989)
  waiting for transfers between devices: 8.36 us -> 7.41 us
  starting transfers between devices: 19.8 us -> 20.3 us
    ppermute x1, starting transfers between devices: 0.83 us -> 2.17 us  [back_along(): return lax.ppermute(rows, ('blk', 'pair'), hops)]
    ppermute x1, waiting for transfers between devices: 1.21 us -> 0.01 us  [back_along(): return lax.ppermute(rows, ('blk', 'pair'), hops)]
    ppermute x9, waiting for transfers between devices: 0.98 us -> 2.12 us  [other_core(): return lax.ppermute(rows, 'pair', [(0, 1), (1, 0)])]
    ppermute x6, starting transfers between devices: 6.7 us -> 5.84 us  [across(): return lax.ppermute(rows, ('sub', 'pair'), [(0, 3), (1, 2), (2, 1), (3, 0)])]
    ppermute x4, waiting for transfers between devices: 2.4 us -> 1.82 us  [along(): return lax.ppermute(rows, ('blk', 'pair'), hops)]
  transfers between devices with their start and end apart: 20 -> 20, of which waited for: 6 -> 9; matrix products, arithmetic and copies ran while one was open for 0% -> 0% of each run, Pallas kernels for 12% -> 12%
where the time goes in v37:
time: 34.9 us; the launch traced here: 34.7 us
  starting transfers between devices  20.3 us (58%)
  waiting for transfers between devices  7.41 us (21%)
  Pallas kernels  5.3 us (15%)
  local copies, waits for them, and re-layouts  1.64 us (5%)
    ppermute x4, starting transfers between devices, along(): return lax.ppermute(rows, ('blk', 'pair'), hops)  9.53 us
    ppermute x6, starting transfers between devices, across(): return lax.ppermute(rows, ('sub', 'pair'), [(0, 3), (1, 2), (2, 1), (3, 0)])  5.84 us
    pallas_call x6, Pallas kernels, call(): pl.pallas_call(kernel, out_shape=[jax.ShapeDtypeStruct(shape, dtype) for...  4.28 us
    ppermute x6, waiting for transfers between devices, across(): return lax.ppermute(rows, ('sub', 'pair'), [(0, 3), (1, 2), (2, 1), (3, 0)])  3.47 us
    ppermute x9, starting transfers between devices, other_core(): return lax.ppermute(rows, 'pair', [(0, 1), (1, 0)])  2.75 us
    ppermute x1, starting transfers between devices, back_along(): return lax.ppermute(rows, ('blk', 'pair'), hops)  2.17 us
    ppermute x9, waiting for transfers between devices, other_core(): return lax.ppermute(rows, 'pair', [(0, 1), (1, 0)])  2.12 us
    ppermute x4, waiting for transfers between devices, along(): return lax.ppermute(rows, ('blk', 'pair'), hops)  1.82 us
  transfers between devices with their start and end apart: 20, of which 9 were waited for; matrix products, arithmetic and copies ran while one was open for 0% of the time, Pallas kernels for 12%

profile of v37, /device:TPU:0, one launch (start us, length us, event | category | flops | bytes accessed | tf_op | source)
XLA Modules:
  0.0 34.7 jit_solution(6697615137632430204)
XLA Ops:
  0.0 0.0 copy-start
  0.0 1.0 %copy-done = bf16[192,768]{1,0:T(8,128)(2,1)S(1)} copy-done((bf16[192,768]{1,0:T(8,128)(2,1)S(1)}, bf16[192,768]{1,0:T(8,128)(2,1)}, u32[]{:S(2)}) %copy-start) | copy-done | bytes 294936
  1.0 0.0 copy-start.2
  1.0 2.4 %collective-permute-start.2 = (bf16[584,128]{1,0:T(8,128)(2,1)S(1)}, bf16[584,128]{1,0:T(8,128)(2,1)S(1)}, u32[]{:S(2)}, u32[]{:S(2)}) collective-permute-start(bf16[584,128]{1,0:T(8,128)(2,1)S(1)} %shard_map.38.refs_0_), channel_id=1, source_target_pairs={{0,3},{1,2},{2,1},{3,0},{4,7},{5,6},{6,5},{7,4},{8,11},{9,10},{10,... | collective-permute-start | bytes 448520 | tf_op jit(solution)/shard_map/ppermute | solution.py:353
  3.4 2.9 %collective-permute-start.1 = (bf16[584,128]{1,0:T(8,128)(2,1)S(1)}, bf16[584,128]{1,0:T(8,128)(2,1)S(1)}, u32[]{:S(2)}, u32[]{:S(2)}) collective-permute-start(bf16[584,128]{1,0:T(8,128)(2,1)S(1)} %shard_map.38.refs_0_), channel_id=1, source_target_pairs={{4,1},{5,0},{0,9},{1,8},{8,13},{9,12},{12,5},{13,4},{6,3},{7,2},{2... | collective-permute-start | bytes 448520 | tf_op jit(solution)/shard_map/ppermute | solution.py:342
  6.3 0.0 copy-start.1
  6.3 0.0 copy-done.2
  6.3 0.7 %copy-done.1 = s32[192,1]{0,1:T(1,128)S(1)} copy-done((s32[192,1]{0,1:T(1,128)S(1)}, s32[192,1]{0,1:T(1,128)}, u32[]{:S(2)}) %copy-start.1) | copy-done | bytes 792
  7.0 0.1 shard_map.37
  7.1 0.1 collective-permute-start.4
  7.2 1.8 %collective-permute-start.3 = (bf16[592,128]{1,0:T(8,128)(2,1)S(1)}, bf16[592,128]{1,0:T(8,128)(2,1)S(1)}, u32[]{:S(2)}, u32[]{:S(2)}) collective-permute-start(bf16[592,128]{1,0:T(8,128)(2,1)S(1)} %get-tuple-element.32.refs_1_), channel_id=1, source_target_pairs={{4,1},{5,0},{0,9},{1,8},{8,13},{9,12},{12,5},{13,4},{6,3},{7,2},{2... | collective-permute-start | bytes 454664 | tf_op jit(solution)/shard_map/ppermute | solution.py:342
  9.0 0.0 collective-permute-done.2.refs_0_.refs_2_
  9.0 1.2 %collective-permute-done.1.refs_4_.near_first = bf16[584,128]{1,0:T(8,128)(2,1)S(1)} collective-permute-done((bf16[584,128]{1,0:T(8,128)(2,1)S(1)}, bf16[584,128]{1,0:T(8,128)(2,1)S(1)}, u32[]{:S(2)}, u32[]{:S(2)}) %collective-permute-start.1) | collective-permute-done | bytes 149536 | tf_op jit(solution)/shard_map/ppermute | solution.py:342
  10.1 0.0 collective-permute-start.6
  10.1 3.1 %collective-permute-start.5 = (bf16[584,128]{1,0:T(8,128)(2,1)S(1)}, bf16[584,128]{1,0:T(8,128)(2,1)S(1)}, u32[]{:S(2)}, u32[]{:S(2)}) collective-permute-start(bf16[584,128]{1,0:T(8,128)(2,1)S(1)} %collective-permute-done.1.refs_4_.near_first), channel_id=1, source_target_pairs={{4,1},{5,0},{0,9},{1,8},{8,13},{9,12},{12,5},{13,4},{6,3},{7,2},{2... | collective-permute-start | bytes 448520 | tf_op jit(solution)/shard_map/ppermute | solution.py:342
  13.2 0.1 collective-permute-done.4.refs_1_.refs_3_
  13.4 0.0 collective-permute-done.3.refs_5_.near_second
  13.4 0.2 collective-permute-start.12
  13.5 1.5 %collective-permute-start.8 = (bf16[592,128]{1,0:T(8,128)(2,1)S(1)}, bf16[592,128]{1,0:T(8,128)(2,1)S(1)}, u32[]{:S(2)}, u32[]{:S(2)}) collective-permute-start(bf16[592,128]{1,0:T(8,128)(2,1)S(1)} %collective-permute-done.3.refs_5_.near_second), channel_id=1, source_target_pairs={{0,3},{1,2},{2,1},{3,0},{4,7},{5,6},{6,5},{7,4},{8,11},{9,10},{10,... | collective-permute-start | bytes 454664 | tf_op jit(solution)/shard_map/ppermute | solution.py:353
  15.1 1.8 %collective-permute-start.7 = (bf16[592,128]{1,0:T(8,128)(2,1)S(1)}, bf16[592,128]{1,0:T(8,128)(2,1)S(1)}, u32[]{:S(2)}, u32[]{:S(2)}) collective-permute-start(bf16[592,128]{1,0:T(8,128)(2,1)S(1)} %collective-permute-done.3.refs_5_.near_second), channel_id=1, source_target_pairs={{4,1},{5,0},{0,9},{1,8},{8,13},{9,12},{12,5},{13,4},{6,3},{7,2},{2... | collective-permute-start | bytes 454664 | tf_op jit(solution)/shard_map/ppermute | solution.py:342
  16.9 0.0 collective-permute-done.6.refs_2_
  16.9 0.0 collective-permute-start.11
  16.9 0.0 collective-permute-done.5.refs_6_
  16.9 1.2 %collective-permute-start.9 = (bf16[584,128]{1,0:T(8,128)(2,1)S(1)}, bf16[584,128]{1,0:T(8,128)(2,1)S(1)}, u32[]{:S(2)}, u32[]{:S(2)}) collective-permute-start(bf16[584,128]{1,0:T(8,128)(2,1)S(1)} %collective-permute-done.5.refs_6_), channel_id=1, source_target_pairs={{0,3},{1,2},{2,1},{3,0},{4,7},{5,6},{6,5},{7,4},{8,11},{9,10},{10,... | collective-permute-start | bytes 448520 | tf_op jit(solution)/shard_map/ppermute | solution.py:353
  18.1 0.2 collective-permute-done.11.over_first
  18.2 0.1 collective-permute-start
  18.4 0.0 collective-permute-done.12.over_second
  18.4 1.1 %shard_map.41 = (f32[192,896]{1,0:T(8,128)S(1)}, bf16[64,896]{1,0:T(8,128)(2,1)S(1)}, bf16[64,896]{1,0:T(8,128)(2,1)S(1)}, bf16[64,896]{1,0:T(8,128)(2,1)S(1)}) custom-call(bf16[584,128]{1,0:T(8,128)(2,1)S(1)} %collective-permute-done.1.refs_4_.near_first, bf16[592,128]{1,0:T(8,128)(2,1)S(1)} %collective-permute-done.3.refs_5_.near_second, ...), custom_call_target="tpu_custom_call" | custom-call | tf_op jit(solution)/shard_map/pallas_call | solution.py:284
  19.5 0.4 %collective-permute-start.13 = (bf16[64,896]{1,0:T(8,128)(2,1)S(1)}, bf16[64,896]{1,0:T(8,128)(2,1)S(1)}, u32[]{:S(2)}, u32[]{:S(2)}) collective-permute-start(bf16[64,896]{1,0:T(8,128)(2,1)S(1)} %get-tuple-element.49), channel_id=1, source_target_pairs={{0,1},{1,0},{2,3},{3,2},{4,5},{5,4},{6,7},{7,6},{8,9},{9,8},{10,11... | collective-permute-start | bytes 344072 | tf_op jit(solution)/shard_map/ppermute | solution.py:356
  19.9 0.0 collective-permute-done.8.refs_3_
  19.9 0.1 collective-permute-start.14
  20.1 0.6 %collective-permute-done.7.refs_7_ = bf16[592,128]{1,0:T(8,128)(2,1)S(1)} collective-permute-done((bf16[592,128]{1,0:T(8,128)(2,1)S(1)}, bf16[592,128]{1,0:T(8,128)(2,1)S(1)}, u32[]{:S(2)}, u32[]{:S(2)}) %collective-permute-start.7) | collective-permute-done | bytes 151584 | tf_op jit(solution)/shard_map/ppermute | solution.py:342
  20.7 0.7 %collective-permute-start.15 = (bf16[64,896]{1,0:T(8,128)(2,1)S(1)}, bf16[64,896]{1,0:T(8,128)(2,1)S(1)}, u32[]{:S(2)}, u32[]{:S(2)}) collective-permute-start(bf16[64,896]{1,0:T(8,128)(2,1)S(1)} %get-tuple-element.51), channel_id=1, source_target_pairs={{0,1},{1,0},{2,3},{3,2},{4,5},{5,4},{6,7},{7,6},{8,9},{9,8},{10,11... | collective-permute-start | bytes 344072 | tf_op jit(solution)/shard_map/ppermute | solution.py:356
  21.4 0.0 collective-permute-done.13.refs_0_
  21.4 0.0 collective-permute-done.14.refs_1_
  21.4 1.0 %collective-permute-done.15.refs_2_ = bf16[64,896]{1,0:T(8,128)(2,1)S(1)} collective-permute-done((bf16[64,896]{1,0:T(8,128)(2,1)S(1)}, bf16[64,896]{1,0:T(8,128)(2,1)S(1)}, u32[]{:S(2)}, u32[]{:S(2)}) %collective-permute-start.15) | collective-permute-done | bytes 114720 | tf_op jit(solution)/shard_map/ppermute | solution.py:356
  22.4 0.3 shard_map.42
  22.7 2.2 %collective-permute-start.16 = (bf16[1168,128]{1,0:T(8,128)(2,1)S(1)}, bf16[1168,128]{1,0:T(8,128)(2,1)S(1)}, u32[]{:S(2)}, u32[]{:S(2)}) collective-permute-start(bf16[1168,128]{1,0:T(8,128)(2,1)S(1)} %shard_map.42), channel_id=1, source_target_pairs={{0,5},{1,4},{8,1},{9,0},{12,9},{13,8},{4,13},{5,12},{2,7},{3,6},{1... | collective-permute-start | bytes 897032 | tf_op jit(solution)/shard_map/ppermute | solution.py:350
  24.8 0.0 collective-permute-done.9.refs_0_
  24.9 0.6 %collective-permute-start.10 = (bf16[592,128]{1,0:T(8,128)(2,1)S(1)}, bf16[592,128]{1,0:T(8,128)(2,1)S(1)}, u32[]{:S(2)}, u32[]{:S(2)}) collective-permute-start(bf16[592,128]{1,0:T(8,128)(2,1)S(1)} %collective-permute-done.7.refs_7_), channel_id=1, source_target_pairs={{0,3},{1,2},{2,1},{3,0},{4,7},{5,6},{6,5},{7,4},{8,11},{9,10},{10,... | collective-permute-start | bytes 454664 | tf_op jit(solution)/shard_map/ppermute | solution.py:353
  25.4 0.0 collective-permute-done.other
  25.4 1.9 %shard_map.39 = (f32[192,896]{1,0:T(8,128)S(1)}, f32[192,896]{1,0:T(8,128)S(1)}, f32[384,128]{1,0:T(8,128)S(1)}) custom-call(bf16[1168,128]{1,0:T(8,128)(2,1)S(1)} %get-tuple-element.30.own, bf16[1168,128]{1,0:T(8,128)(2,1)S(1)} %collective-permute-done.other, bf16[584,128]{1,0:T(8,128)(2,1)S(1)} %collective-permute-done.2.refs_0_.refs_2_, ...), custom_call_target="tpu_custom_call" | custom-call | tf_op jit(solution)/shard_map/pallas_call | solution.py:284
  27.3 3.3 %collective-permute-done.10.refs_1_ = bf16[592,128]{1,0:T(8,128)(2,1)S(1)} collective-permute-done((bf16[592,128]{1,0:T(8,128)(2,1)S(1)}, bf16[592,128]{1,0:T(8,128)(2,1)S(1)}, u32[]{:S(2)}, u32[]{:S(2)}) %collective-permute-start.10) | collective-permute-done | bytes 151584 | tf_op jit(solution)/shard_map/ppermute | solution.py:353
  30.6 0.9 %shard_map.40 = (f32[192,896]{1,0:T(8,128)S(1)}, bf16[64,896]{1,0:T(8,128)(2,1)S(1)}, bf16[64,896]{1,0:T(8,128)(2,1)S(1)}, bf16[64,896]{1,0:T(8,128)(2,1)S(1)}) custom-call(bf16[1168,128]{1,0:T(8,128)(2,1)S(1)} %get-tuple-element.30.own, bf16[1168,128]{1,0:T(8,128)(2,1)S(1)} %collective-permute-done.other, ...), custom_call_target="tpu_custom_call", output_to_operand_aliasing={{0}: (5, {})} | custom-call | tf_op jit(solution)/shard_map/pallas_call | solution.py:284
  31.5 0.6 %collective-permute-start.17 = (bf16[64,896]{1,0:T(8,128)(2,1)S(1)}, bf16[64,896]{1,0:T(8,128)(2,1)S(1)}, u32[]{:S(2)}, u32[]{:S(2)}) collective-permute-start(bf16[64,896]{1,0:T(8,128)(2,1)S(1)} %get-tuple-element.52), channel_id=1, source_target_pairs={{0,1},{1,0},{2,3},{3,2},{4,5},{5,4},{6,7},{7,6},{8,9},{9,8},{10,11... | collective-permute-start | bytes 344072 | tf_op jit(solution)/shard_map/ppermute | solution.py:356
  32.2 0.1 collective-permute-start.18
  32.3 0.4 %collective-permute-start.19 = (bf16[64,896]{1,0:T(8,128)(2,1)S(1)}, bf16[64,896]{1,0:T(8,128)(2,1)S(1)}, u32[]{:S(2)}, u32[]{:S(2)}) collective-permute-start(bf16[64,896]{1,0:T(8,128)(2,1)S(1)} %get-tuple-element.54), channel_id=1, source_target_pairs={{0,1},{1,0},{2,3},{3,2},{4,5},{5,4},{6,7},{7,6},{8,9},{9,8},{10,11... | collective-permute-start | bytes 344072 | tf_op jit(solution)/shard_map/ppermute | solution.py:356
  32.7 0.5 %collective-permute-done.17.refs_0_ = bf16[64,896]{1,0:T(8,128)(2,1)S(1)} collective-permute-done((bf16[64,896]{1,0:T(8,128)(2,1)S(1)}, bf16[64,896]{1,0:T(8,128)(2,1)S(1)}, u32[]{:S(2)}, u32[]{:S(2)}) %collective-permute-start.17) | collective-permute-done | bytes 114720 | tf_op jit(solution)/shard_map/ppermute | solution.py:356
  33.1 0.4 %collective-permute-done.18.refs_1_ = bf16[64,896]{1,0:T(8,128)(2,1)S(1)} collective-permute-done((bf16[64,896]{1,0:T(8,128)(2,1)S(1)}, bf16[64,896]{1,0:T(8,128)(2,1)S(1)}, u32[]{:S(2)}, u32[]{:S(2)}) %collective-permute-start.18) | collective-permute-done | bytes 114720 | tf_op jit(solution)/shard_map/ppermute | solution.py:356
  33.5 0.2 collective-permute-done.19.refs_2_
  33.7 0.0 collective-permute-done.16.returned
  33.7 1.0 %shard_map.43 = bf16[192,768]{1,0:T(8,128)(2,1)} custom-call(f32[192,896]{1,0:T(8,128)S(1)} %get-tuple-element.45.mine, bf16[1168,128]{1,0:T(8,128)(2,1)S(1)} %collective-permute-done.16.returned, bf16[64,896]{1,0:T(8,128)(2,1)S(1)} %collective-permute-done.17.refs_0_, bf16[64,896]{1,0:T(8,128)(2,1)S(1)} %collective-permute-done.18.refs_1_, ...), custom_call_target="tpu_custom_call" | custom-call | tf_op jit(solution)/shard_map/pallas_call | solution.py:310
  (1 shorter events, 0.0 us)
Async XLA Ops:
  0.0 1.0 %copy-start = (bf16[192,768]{1,0:T(8,128)(2,1)S(1)}, bf16[192,768]{1,0:T(8,128)(2,1)}, u32[]{:S(2)}) copy-start(bf16[192,768]{1,0:T(8,128)(2,1)} %rows.3) | copy-start | bytes 884740
  1.0 5.3 %copy-start.2 = (s32[192]{0:T(256)S(1)}, s32[192]{0:T(256)}, u32[]{:S(2)}) copy-start(s32[192]{0:T(256)} %param.5) | copy-start | bytes 2308
  1.0 8.0 %collective-permute-start.2 = (bf16[584,128]{1,0:T(8,128)(2,1)S(1)}, bf16[584,128]{1,0:T(8,128)(2,1)S(1)}, u32[]{:S(2)}, u32[]{:S(2)}) collective-permute-start(bf16[584,128]{1,0:T(8,128)(2,1)S(1)} %shard_map.38.refs_0_), channel_id=1, source_target_pairs={{0,3},{1,2},{2,1},{3,0},{4,7},{5,6},{6,5},{7,4},{8,11},{9,10},{10,... | collective-permute-start | bytes 448520 | tf_op jit(solution)/shard_map/ppermute | solution.py:353
  3.4 6.7 %collective-permute-start.1 = (bf16[584,128]{1,0:T(8,128)(2,1)S(1)}, bf16[584,128]{1,0:T(8,128)(2,1)S(1)}, u32[]{:S(2)}, u32[]{:S(2)}) collective-permute-start(bf16[584,128]{1,0:T(8,128)(2,1)S(1)} %shard_map.38.refs_0_), channel_id=1, source_target_pairs={{4,1},{5,0},{0,9},{1,8},{8,13},{9,12},{12,5},{13,4},{6,3},{7,2},{2... | collective-permute-start | bytes 448520 | tf_op jit(solution)/shard_map/ppermute | solution.py:342
  6.3 0.7 %copy-start.1 = (s32[192,1]{0,1:T(1,128)S(1)}, s32[192,1]{0,1:T(1,128)}, u32[]{:S(2)}) copy-start(s32[192,1]{0,1:T(1,128)} %param.4) | copy-start | bytes 2308
  7.1 6.3 %collective-permute-start.4 = (bf16[592,128]{1,0:T(8,128)(2,1)S(1)}, bf16[592,128]{1,0:T(8,128)(2,1)S(1)}, u32[]{:S(2)}, u32[]{:S(2)}) collective-permute-start(bf16[592,128]{1,0:T(8,128)(2,1)S(1)} %get-tuple-element.32.refs_1_), channel_id=1, source_target_pairs={{0,3},{1,2},{2,1},{3,0},{4,7},{5,6},{6,5},{7,4},{8,11},{9,10},{10,... | collective-permute-start | bytes 454664 | tf_op jit(solution)/shard_map/ppermute | solution.py:353
  7.2 6.2 %collective-permute-start.3 = (bf16[592,128]{1,0:T(8,128)(2,1)S(1)}, bf16[592,128]{1,0:T(8,128)(2,1)S(1)}, u32[]{:S(2)}, u32[]{:S(2)}) collective-permute-start(bf16[592,128]{1,0:T(8,128)(2,1)S(1)} %get-tuple-element.32.refs_1_), channel_id=1, source_target_pairs={{4,1},{5,0},{0,9},{1,8},{8,13},{9,12},{12,5},{13,4},{6,3},{7,2},{2... | collective-permute-start | bytes 454664 | tf_op jit(solution)/shard_map/ppermute | solution.py:342
  10.1 6.7 %collective-permute-start.6 = (bf16[584,128]{1,0:T(8,128)(2,1)S(1)}, bf16[584,128]{1,0:T(8,128)(2,1)S(1)}, u32[]{:S(2)}, u32[]{:S(2)}) collective-permute-start(bf16[584,128]{1,0:T(8,128)(2,1)S(1)} %collective-permute-done.1.refs_4_.near_first), channel_id=1, source_target_pairs={{0,3},{1,2},{2,1},{3,0},{4,7},{5,6},{6,5},{7,4},{8,11},{9,10},{10,... | collective-permute-start | bytes 448520 | tf_op jit(solution)/shard_map/ppermute | solution.py:353
  10.1 6.8 %collective-permute-start.5 = (bf16[584,128]{1,0:T(8,128)(2,1)S(1)}, bf16[584,128]{1,0:T(8,128)(2,1)S(1)}, u32[]{:S(2)}, u32[]{:S(2)}) collective-permute-start(bf16[584,128]{1,0:T(8,128)(2,1)S(1)} %collective-permute-done.1.refs_4_.near_first), channel_id=1, source_target_pairs={{4,1},{5,0},{0,9},{1,8},{8,13},{9,12},{12,5},{13,4},{6,3},{7,2},{2... | collective-permute-start | bytes 448520 | tf_op jit(solution)/shard_map/ppermute | solution.py:342
  13.4 5.0 %collective-permute-start.12 = (bf16[592,128]{1,0:T(8,128)(2,1)S(1)}, bf16[592,128]{1,0:T(8,128)(2,1)S(1)}, u32[]{:S(2)}, u32[]{:S(2)}) collective-permute-start(bf16[592,128]{1,0:T(8,128)(2,1)S(1)} %collective-permute-done.3.refs_5_.near_second), channel_id=1, source_target_pairs={{0,1},{1,0},{2,3},{3,2},{4,5},{5,4},{6,7},{7,6},{8,9},{9,8},{10,11... | collective-permute-start | bytes 454664 | tf_op jit(solution)/shard_map/ppermute | solution.py:356
  13.5 6.4 %collective-permute-start.8 = (bf16[592,128]{1,0:T(8,128)(2,1)S(1)}, bf16[592,128]{1,0:T(8,128)(2,1)S(1)}, u32[]{:S(2)}, u32[]{:S(2)}) collective-permute-start(bf16[592,128]{1,0:T(8,128)(2,1)S(1)} %collective-permute-done.3.refs_5_.near_second), channel_id=1, source_target_pairs={{0,3},{1,2},{2,1},{3,0},{4,7},{5,6},{6,5},{7,4},{8,11},{9,10},{10,... | collective-permute-start | bytes 454664 | tf_op jit(solution)/shard_map/ppermute | solution.py:353
  15.1 5.7 %collective-permute-start.7 = (bf16[592,128]{1,0:T(8,128)(2,1)S(1)}, bf16[592,128]{1,0:T(8,128)(2,1)S(1)}, u32[]{:S(2)}, u32[]{:S(2)}) collective-permute-start(bf16[592,128]{1,0:T(8,128)(2,1)S(1)} %collective-permute-done.3.refs_5_.near_second), channel_id=1, source_target_pairs={{4,1},{5,0},{0,9},{1,8},{8,13},{9,12},{12,5},{13,4},{6,3},{7,2},{2... | collective-permute-start | bytes 454664 | tf_op jit(solution)/shard_map/ppermute | solution.py:342
  16.9 1.4 %collective-permute-start.11 = (bf16[584,128]{1,0:T(8,128)(2,1)S(1)}, bf16[584,128]{1,0:T(8,128)(2,1)S(1)}, u32[]{:S(2)}, u32[]{:S(2)}) collective-permute-start(bf16[584,128]{1,0:T(8,128)(2,1)S(1)} %collective-permute-done.1.refs_4_.near_first), channel_id=1, source_target_pairs={{0,1},{1,0},{2,3},{3,2},{4,5},{5,4},{6,7},{7,6},{8,9},{9,8},{10,11... | collective-permute-start | bytes 448520 | tf_op jit(solution)/shard_map/ppermute | solution.py:356
  16.9 8.0 %collective-permute-start.9 = (bf16[584,128]{1,0:T(8,128)(2,1)S(1)}, bf16[584,128]{1,0:T(8,128)(2,1)S(1)}, u32[]{:S(2)}, u32[]{:S(2)}) collective-permute-start(bf16[584,128]{1,0:T(8,128)(2,1)S(1)} %collective-permute-done.5.refs_6_), channel_id=1, source_target_pairs={{0,3},{1,2},{2,1},{3,0},{4,7},{5,6},{6,5},{7,4},{8,11},{9,10},{10,... | collective-permute-start | bytes 448520 | tf_op jit(solution)/shard_map/ppermute | solution.py:353
  18.2 7.2 %collective-permute-start = (bf16[1168,128]{1,0:T(8,128)(2,1)S(1)}, bf16[1168,128]{1,0:T(8,128)(2,1)S(1)}, u32[]{:S(2)}, u32[]{:S(2)}) collective-permute-start(bf16[1168,128]{1,0:T(8,128)(2,1)S(1)} %get-tuple-element.30.own), channel_id=1, source_target_pairs={{0,1},{1,0},{2,3},{3,2},{4,5},{5,4},{6,7},{7,6},{8,9},{9,8},{10,11... | collective-permute-start | bytes 897032 | tf_op jit(solution)/shard_map/ppermute | solution.py:356
  19.5 1.9 %collective-permute-start.13 = (bf16[64,896]{1,0:T(8,128)(2,1)S(1)}, bf16[64,896]{1,0:T(8,128)(2,1)S(1)}, u32[]{:S(2)}, u32[]{:S(2)}) collective-permute-start(bf16[64,896]{1,0:T(8,128)(2,1)S(1)} %get-tuple-element.49), channel_id=1, source_target_pairs={{0,1},{1,0},{2,3},{3,2},{4,5},{5,4},{6,7},{7,6},{8,9},{9,8},{10,11... | collective-permute-start | bytes 344072 | tf_op jit(solution)/shard_map/ppermute | solution.py:356
  19.9 1.5 %collective-permute-start.14 = (bf16[64,896]{1,0:T(8,128)(2,1)S(1)}, bf16[64,896]{1,0:T(8,128)(2,1)S(1)}, u32[]{:S(2)}, u32[]{:S(2)}) collective-permute-start(bf16[64,896]{1,0:T(8,128)(2,1)S(1)} %get-tuple-element.50), channel_id=1, source_target_pairs={{0,1},{1,0},{2,3},{3,2},{4,5},{5,4},{6,7},{7,6},{8,9},{9,8},{10,11... | collective-permute-start | bytes 344072 | tf_op jit(solution)/shard_map/ppermute | solution.py:356
  20.7 1.6 %collective-permute-start.15 = (bf16[64,896]{1,0:T(8,128)(2,1)S(1)}, bf16[64,896]{1,0:T(8,128)(2,1)S(1)}, u32[]{:S(2)}, u32[]{:S(2)}) collective-permute-start(bf16[64,896]{1,0:T(8,128)(2,1)S(1)} %get-tuple-element.51), channel_id=1, source_target_pairs={{0,1},{1,0},{2,3},{3,2},{4,5},{5,4},{6,7},{7,6},{8,9},{9,8},{10,11... | collective-permute-start | bytes 344072 | tf_op jit(solution)/shard_map/ppermute | solution.py:356
  22.7 11.0 %collective-permute-start.16 = (bf16[1168,128]{1,0:T(8,128)(2,1)S(1)}, bf16[1168,128]{1,0:T(8,128)(2,1)S(1)}, u32[]{:S(2)}, u32[]{:S(2)}) collective-permute-start(bf16[1168,128]{1,0:T(8,128)(2,1)S(1)} %shard_map.42), channel_id=1, source_target_pairs={{0,5},{1,4},{8,1},{9,0},{12,9},{13,8},{4,13},{5,12},{2,7},{3,6},{1... | collective-permute-start | bytes 897032 | tf_op jit(solution)/shard_map/ppermute | solution.py:350
  24.9 5.8 %collective-permute-start.10 = (bf16[592,128]{1,0:T(8,128)(2,1)S(1)}, bf16[592,128]{1,0:T(8,128)(2,1)S(1)}, u32[]{:S(2)}, u32[]{:S(2)}) collective-permute-start(bf16[592,128]{1,0:T(8,128)(2,1)S(1)} %collective-permute-done.7.refs_7_), channel_id=1, source_target_pairs={{0,3},{1,2},{2,1},{3,0},{4,7},{5,6},{6,5},{7,4},{8,11},{9,10},{10,... | collective-permute-start | bytes 454664 | tf_op jit(solution)/shard_map/ppermute | solution.py:353
  31.5 1.6 %collective-permute-start.17 = (bf16[64,896]{1,0:T(8,128)(2,1)S(1)}, bf16[64,896]{1,0:T(8,128)(2,1)S(1)}, u32[]{:S(2)}, u32[]{:S(2)}) collective-permute-start(bf16[64,896]{1,0:T(8,128)(2,1)S(1)} %get-tuple-element.52), channel_id=1, source_target_pairs={{0,1},{1,0},{2,3},{3,2},{4,5},{5,4},{6,7},{7,6},{8,9},{9,8},{10,11... | collective-permute-start | bytes 344072 | tf_op jit(solution)/shard_map/ppermute | solution.py:356
  32.2 1.3 %collective-permute-start.18 = (bf16[64,896]{1,0:T(8,128)(2,1)S(1)}, bf16[64,896]{1,0:T(8,128)(2,1)S(1)}, u32[]{:S(2)}, u32[]{:S(2)}) collective-permute-start(bf16[64,896]{1,0:T(8,128)(2,1)S(1)} %get-tuple-element.53), channel_id=1, source_target_pairs={{0,1},{1,0},{2,3},{3,2},{4,5},{5,4},{6,7},{7,6},{8,9},{9,8},{10,11... | collective-permute-start | bytes 344072 | tf_op jit(solution)/shard_map/ppermute | solution.py:356
  32.3 1.4 %collective-permute-start.19 = (bf16[64,896]{1,0:T(8,128)(2,1)S(1)}, bf16[64,896]{1,0:T(8,128)(2,1)S(1)}, u32[]{:S(2)}, u32[]{:S(2)}) collective-permute-start(bf16[64,896]{1,0:T(8,128)(2,1)S(1)} %get-tuple-element.54), channel_id=1, source_target_pairs={{0,1},{1,0},{2,3},{3,2},{4,5},{5,4},{6,7},{7,6},{8,9},{9,8},{10,11... | collective-permute-start | bytes 344072 | tf_op jit(solution)/shard_map/ppermute | solution.py:356

commit v38 on v37

--- a/solution.py
+++ b/solution.py
@@ -301,7 +301,7 @@
 def add_both(left, right, before):
     args = list(left) + [half for block in right for half in block] + list(before)
     rows_here, wide = before[0].shape
-    shapes = [((rows_here, wide), F32)] + [((rows_here // PARTS, wide), BF16)] * PARTS
+    shapes = [((rows_here, wide), F32)] + [((rows_here // 2, wide), BF16)] * 2
     kernel = functools.partial(both_kernel, len(right))
     return call(kernel, shapes, args, {len(args) - 2: 0})
 

time: 34.9 us -> 36.4 us (1.043)
  waiting for transfers between devices: 7.41 us -> 9.48 us
  starting transfers between devices: 20.3 us -> 19.8 us
    ppermute x1, waiting for transfers between devices: 0.01 us -> 3.39 us  [back_along(): return lax.ppermute(rows, ('blk', 'pair'), hops)]
    ppermute x9 -> x8, waiting for transfers between devices: 2.12 us -> 0.02 us  [other_core(): return lax.ppermute(rows, 'pair', [(0, 1), (1, 0)])]
    ppermute x4, waiting for transfers between devices: 1.82 us -> 2.39 us  [along(): return lax.ppermute(rows, ('blk', 'pair'), hops)]
    ppermute x9 -> x8, starting transfers between devices: 2.75 us -> 2.37 us  [other_core(): return lax.ppermute(rows, 'pair', [(0, 1), (1, 0)])]
  transfers between devices with their start and end apart: 20 -> 19, of which waited for: 9 -> 7; matrix products, arithmetic and copies ran while one was open for 0% -> 0% of each run, Pallas kernels for 12% -> 12%
where the time goes in v38:
time: 36.4 us; the launch traced here: 36.2 us
  starting transfers between devices  19.8 us (54%)
  waiting for transfers between devices  9.48 us (26%)
  Pallas kernels  5.32 us (15%)
  local copies, waits for them, and re-layouts  1.64 us (5%)
    ppermute x4, starting transfers between devices, along(): return lax.ppermute(rows, ('blk', 'pair'), hops)  9.38 us
    ppermute x6, starting transfers between devices, across(): return lax.ppermute(rows, ('sub', 'pair'), [(0, 3), (1, 2), (2, 1), (3, 0)])  6.18 us
    pallas_call x6, Pallas kernels, call(): pl.pallas_call(kernel, out_shape=[jax.ShapeDtypeStruct(shape, dtype) for...  4.29 us
    ppermute x6, waiting for transfers between devices, across(): return lax.ppermute(rows, ('sub', 'pair'), [(0, 3), (1, 2), (2, 1), (3, 0)])  3.68 us
    ppermute x1, waiting for transfers between devices, back_along(): return lax.ppermute(rows, ('blk', 'pair'), hops)  3.39 us
    ppermute x4, waiting for transfers between devices, along(): return lax.ppermute(rows, ('blk', 'pair'), hops)  2.39 us
    ppermute x8, starting transfers between devices, other_core(): return lax.ppermute(rows, 'pair', [(0, 1), (1, 0)])  2.37 us
    ppermute x1, starting transfers between devices, back_along(): return lax.ppermute(rows, ('blk', 'pair'), hops)  1.82 us
  transfers between devices with their start and end apart: 19, of which 7 were waited for; matrix products, arithmetic and copies ran while one was open for 0% of the time, Pallas kernels for 12%

profile of v38, /device:TPU:0, one launch (start us, length us, event | category | flops | bytes accessed | tf_op | source)
XLA Modules:
  0.0 36.2 jit_solution(15576048353362578715)
XLA Ops:
  0.0 0.0 copy-start
  0.0 1.0 %copy-done = bf16[192,768]{1,0:T(8,128)(2,1)S(1)} copy-done((bf16[192,768]{1,0:T(8,128)(2,1)S(1)}, bf16[192,768]{1,0:T(8,128)(2,1)}, u32[]{:S(2)}) %copy-start) | copy-done | bytes 294936
  1.0 0.0 copy-start.2
  1.0 2.4 %collective-permute-start.2 = (bf16[584,128]{1,0:T(8,128)(2,1)S(1)}, bf16[584,128]{1,0:T(8,128)(2,1)S(1)}, u32[]{:S(2)}, u32[]{:S(2)}) collective-permute-start(bf16[584,128]{1,0:T(8,128)(2,1)S(1)} %shard_map.38.refs_0_), channel_id=1, source_target_pairs={{0,3},{1,2},{2,1},{3,0},{4,7},{5,6},{6,5},{7,4},{8,11},{9,10},{10,... | collective-permute-start | bytes 448520 | tf_op jit(solution)/shard_map/ppermute | solution.py:353
  3.4 2.9 %collective-permute-start.1 = (bf16[584,128]{1,0:T(8,128)(2,1)S(1)}, bf16[584,128]{1,0:T(8,128)(2,1)S(1)}, u32[]{:S(2)}, u32[]{:S(2)}) collective-permute-start(bf16[584,128]{1,0:T(8,128)(2,1)S(1)} %shard_map.38.refs_0_), channel_id=1, source_target_pairs={{4,1},{5,0},{0,9},{1,8},{8,13},{9,12},{12,5},{13,4},{6,3},{7,2},{2... | collective-permute-start | bytes 448520 | tf_op jit(solution)/shard_map/ppermute | solution.py:342
  6.3 0.0 copy-start.1
  6.3 0.0 copy-done.2
  6.3 0.7 %copy-done.1 = s32[192,1]{0,1:T(1,128)S(1)} copy-done((s32[192,1]{0,1:T(1,128)S(1)}, s32[192,1]{0,1:T(1,128)}, u32[]{:S(2)}) %copy-start.1) | copy-done | bytes 792
  7.0 0.1 shard_map.37
  7.1 0.1 collective-permute-start.4
  7.2 1.8 %collective-permute-start.3 = (bf16[592,128]{1,0:T(8,128)(2,1)S(1)}, bf16[592,128]{1,0:T(8,128)(2,1)S(1)}, u32[]{:S(2)}, u32[]{:S(2)}) collective-permute-start(bf16[592,128]{1,0:T(8,128)(2,1)S(1)} %get-tuple-element.31.refs_1_), channel_id=1, source_target_pairs={{4,1},{5,0},{0,9},{1,8},{8,13},{9,12},{12,5},{13,4},{6,3},{7,2},{2... | collective-permute-start | bytes 454664 | tf_op jit(solution)/shard_map/ppermute | solution.py:342
  9.0 0.0 collective-permute-done.2.refs_0_.refs_2_
  9.0 1.2 %collective-permute-done.1.refs_4_.near_first = bf16[584,128]{1,0:T(8,128)(2,1)S(1)} collective-permute-done((bf16[584,128]{1,0:T(8,128)(2,1)S(1)}, bf16[584,128]{1,0:T(8,128)(2,1)S(1)}, u32[]{:S(2)}, u32[]{:S(2)}) %collective-permute-start.1) | collective-permute-done | bytes 149536 | tf_op jit(solution)/shard_map/ppermute | solution.py:342
  10.1 0.0 collective-permute-start.6
  10.1 3.1 %collective-permute-start.5 = (bf16[584,128]{1,0:T(8,128)(2,1)S(1)}, bf16[584,128]{1,0:T(8,128)(2,1)S(1)}, u32[]{:S(2)}, u32[]{:S(2)}) collective-permute-start(bf16[584,128]{1,0:T(8,128)(2,1)S(1)} %collective-permute-done.1.refs_4_.near_first), channel_id=1, source_target_pairs={{4,1},{5,0},{0,9},{1,8},{8,13},{9,12},{12,5},{13,4},{6,3},{7,2},{2... | collective-permute-start | bytes 448520 | tf_op jit(solution)/shard_map/ppermute | solution.py:342
  13.2 0.1 collective-permute-start.11
  13.3 0.1 collective-permute-done.4.refs_1_.refs_3_
  13.4 0.0 collective-permute-done.3.refs_5_.near_second
  13.4 0.4 %collective-permute-start.12 = (bf16[592,128]{1,0:T(8,128)(2,1)S(1)}, bf16[592,128]{1,0:T(8,128)(2,1)S(1)}, u32[]{:S(2)}, u32[]{:S(2)}) collective-permute-start(bf16[592,128]{1,0:T(8,128)(2,1)S(1)} %collective-permute-done.3.refs_5_.near_second), channel_id=1, source_target_pairs={{0,1},{1,0},{2,3},{3,2},{4,5},{5,4},{6,7},{7,6},{8,9},{9,8},{10,11... | collective-permute-start | bytes 454664 | tf_op jit(solution)/shard_map/ppermute | solution.py:356
  13.8 1.7 %collective-permute-start.8 = (bf16[592,128]{1,0:T(8,128)(2,1)S(1)}, bf16[592,128]{1,0:T(8,128)(2,1)S(1)}, u32[]{:S(2)}, u32[]{:S(2)}) collective-permute-start(bf16[592,128]{1,0:T(8,128)(2,1)S(1)} %collective-permute-done.3.refs_5_.near_second), channel_id=1, source_target_pairs={{0,3},{1,2},{2,1},{3,0},{4,7},{5,6},{6,5},{7,4},{8,11},{9,10},{10,... | collective-permute-start | bytes 454664 | tf_op jit(solution)/shard_map/ppermute | solution.py:353
  15.5 1.1 %collective-permute-done.6.refs_2_ = bf16[584,128]{1,0:T(8,128)(2,1)S(1)} collective-permute-done((bf16[584,128]{1,0:T(8,128)(2,1)S(1)}, bf16[584,128]{1,0:T(8,128)(2,1)S(1)}, u32[]{:S(2)}, u32[]{:S(2)}) %collective-permute-start.6) | collective-permute-done | bytes 149536 | tf_op jit(solution)/shard_map/ppermute | solution.py:353
  16.6 1.6 %collective-permute-start.7 = (bf16[592,128]{1,0:T(8,128)(2,1)S(1)}, bf16[592,128]{1,0:T(8,128)(2,1)S(1)}, u32[]{:S(2)}, u32[]{:S(2)}) collective-permute-start(bf16[592,128]{1,0:T(8,128)(2,1)S(1)} %collective-permute-done.3.refs_5_.near_second), channel_id=1, source_target_pairs={{4,1},{5,0},{0,9},{1,8},{8,13},{9,12},{12,5},{13,4},{6,3},{7,2},{2... | collective-permute-start | bytes 454664 | tf_op jit(solution)/shard_map/ppermute | solution.py:342
  18.2 0.0 collective-permute-done.5.refs_6_
  18.2 1.0 %collective-permute-start.9 = (bf16[584,128]{1,0:T(8,128)(2,1)S(1)}, bf16[584,128]{1,0:T(8,128)(2,1)S(1)}, u32[]{:S(2)}, u32[]{:S(2)}) collective-permute-start(bf16[584,128]{1,0:T(8,128)(2,1)S(1)} %collective-permute-done.5.refs_6_), channel_id=1, source_target_pairs={{0,3},{1,2},{2,1},{3,0},{4,7},{5,6},{6,5},{7,4},{8,11},{9,10},{10,... | collective-permute-start | bytes 448520 | tf_op jit(solution)/shard_map/ppermute | solution.py:353
  19.2 0.0 collective-permute-done.11.over_first
  19.2 0.4 collective-permute-start
  19.5 0.0 collective-permute-done.12.over_second
  19.6 1.1 %shard_map.41 = (f32[192,896]{1,0:T(8,128)S(1)}, bf16[64,896]{1,0:T(8,128)(2,1)S(1)}, bf16[64,896]{1,0:T(8,128)(2,1)S(1)}, bf16[64,896]{1,0:T(8,128)(2,1)S(1)}) custom-call(bf16[584,128]{1,0:T(8,128)(2,1)S(1)} %collective-permute-done.1.refs_4_.near_first, bf16[592,128]{1,0:T(8,128)(2,1)S(1)} %collective-permute-done.3.refs_5_.near_second, ...), custom_call_target="tpu_custom_call" | custom-call | tf_op jit(solution)/shard_map/pallas_call | solution.py:284
  20.7 0.2 collective-permute-start.13
  20.9 0.0 collective-permute-done.8.refs_3_
  20.9 0.4 collective-permute-start.14
  21.3 1.2 %collective-permute-done.7.refs_7_ = bf16[592,128]{1,0:T(8,128)(2,1)S(1)} collective-permute-done((bf16[592,128]{1,0:T(8,128)(2,1)S(1)}, bf16[592,128]{1,0:T(8,128)(2,1)S(1)}, u32[]{:S(2)}, u32[]{:S(2)}) %collective-permute-start.7) | collective-permute-done | bytes 151584 | tf_op jit(solution)/shard_map/ppermute | solution.py:342
  22.5 0.4 %collective-permute-start.15 = (bf16[64,896]{1,0:T(8,128)(2,1)S(1)}, bf16[64,896]{1,0:T(8,128)(2,1)S(1)}, u32[]{:S(2)}, u32[]{:S(2)}) collective-permute-start(bf16[64,896]{1,0:T(8,128)(2,1)S(1)} %get-tuple-element.50), channel_id=1, source_target_pairs={{0,1},{1,0},{2,3},{3,2},{4,5},{5,4},{6,7},{7,6},{8,9},{9,8},{10,11... | collective-permute-start | bytes 344072 | tf_op jit(solution)/shard_map/ppermute | solution.py:356
  22.9 1.3 %collective-permute-done.9.refs_0_ = bf16[584,128]{1,0:T(8,128)(2,1)S(1)} collective-permute-done((bf16[584,128]{1,0:T(8,128)(2,1)S(1)}, bf16[584,128]{1,0:T(8,128)(2,1)S(1)}, u32[]{:S(2)}, u32[]{:S(2)}) %collective-permute-start.9) | collective-permute-done | bytes 149536 | tf_op jit(solution)/shard_map/ppermute | solution.py:353
  24.2 0.9 %collective-permute-start.10 = (bf16[592,128]{1,0:T(8,128)(2,1)S(1)}, bf16[592,128]{1,0:T(8,128)(2,1)S(1)}, u32[]{:S(2)}, u32[]{:S(2)}) collective-permute-start(bf16[592,128]{1,0:T(8,128)(2,1)S(1)} %collective-permute-done.7.refs_7_), channel_id=1, source_target_pairs={{0,3},{1,2},{2,1},{3,0},{4,7},{5,6},{6,5},{7,4},{8,11},{9,10},{10,... | collective-permute-start | bytes 454664 | tf_op jit(solution)/shard_map/ppermute | solution.py:353
  25.0 0.0 collective-permute-done.13.refs_0_
  25.1 0.0 collective-permute-done.14.refs_1_
  25.1 0.0 collective-permute-done.15.refs_2_
  25.1 0.3 shard_map.42
  25.4 1.8 %collective-permute-start.16 = (bf16[1168,128]{1,0:T(8,128)(2,1)S(1)}, bf16[1168,128]{1,0:T(8,128)(2,1)S(1)}, u32[]{:S(2)}, u32[]{:S(2)}) collective-permute-start(bf16[1168,128]{1,0:T(8,128)(2,1)S(1)} %shard_map.42), channel_id=1, source_target_pairs={{0,5},{1,4},{8,1},{9,0},{12,9},{13,8},{4,13},{5,12},{2,7},{3,6},{1... | collective-permute-start | bytes 897032 | tf_op jit(solution)/shard_map/ppermute | solution.py:350
  27.2 0.0 collective-permute-done.other
  27.2 1.9 %shard_map.39 = (f32[192,896]{1,0:T(8,128)S(1)}, f32[192,896]{1,0:T(8,128)S(1)}, f32[384,128]{1,0:T(8,128)S(1)}) custom-call(bf16[1168,128]{1,0:T(8,128)(2,1)S(1)} %get-tuple-element.29.own, bf16[1168,128]{1,0:T(8,128)(2,1)S(1)} %collective-permute-done.other, bf16[584,128]{1,0:T(8,128)(2,1)S(1)} %collective-permute-done.2.refs_0_.refs_2_, ...), custom_call_target="tpu_custom_call" | custom-call | tf_op jit(solution)/shard_map/pallas_call | solution.py:284
  29.1 1.3 %collective-permute-done.10.refs_1_ = bf16[592,128]{1,0:T(8,128)(2,1)S(1)} collective-permute-done((bf16[592,128]{1,0:T(8,128)(2,1)S(1)}, bf16[592,128]{1,0:T(8,128)(2,1)S(1)}, u32[]{:S(2)}, u32[]{:S(2)}) %collective-permute-start.10) | collective-permute-done | bytes 151584 | tf_op jit(solution)/shard_map/ppermute | solution.py:353
  30.3 0.9 %shard_map.40 = (f32[192,896]{1,0:T(8,128)S(1)}, bf16[96,896]{1,0:T(8,128)(2,1)S(1)}, bf16[96,896]{1,0:T(8,128)(2,1)S(1)}) custom-call(bf16[1168,128]{1,0:T(8,128)(2,1)S(1)} %get-tuple-element.29.own, bf16[1168,128]{1,0:T(8,128)(2,1)S(1)} %collective-permute-done.other, f32[384,128]{1,0:T(8,128)S(1)} %get-tuple-element.39.info, ...), custom_call_target="tpu_custom_call", output_to_operand_aliasing={{0}: (5, {})} | custom-call | tf_op jit(solution)/shard_map/pallas_call | solution.py:284
  31.2 0.3 collective-permute-start.17
  31.5 0.3 collective-permute-start.18
  31.8 3.4 %collective-permute-done.16.returned = bf16[1168,128]{1,0:T(8,128)(2,1)S(1)} collective-permute-done((bf16[1168,128]{1,0:T(8,128)(2,1)S(1)}, bf16[1168,128]{1,0:T(8,128)(2,1)S(1)}, u32[]{:S(2)}, u32[]{:S(2)}) %collective-permute-start.16) | collective-permute-done | bytes 299040 | tf_op jit(solution)/shard_map/ppermute | solution.py:350
  35.2 0.0 collective-permute-done.17.refs_0_
  35.2 0.0 collective-permute-done.18.refs_1_
  35.2 1.0 %shard_map.43 = bf16[192,768]{1,0:T(8,128)(2,1)} custom-call(f32[192,896]{1,0:T(8,128)S(1)} %get-tuple-element.44.mine, bf16[1168,128]{1,0:T(8,128)(2,1)S(1)} %collective-permute-done.16.returned, bf16[96,896]{1,0:T(8,128)(2,1)S(1)} %collective-permute-done.17.refs_0_, bf16[96,896]{1,0:T(8,128)(2,1)S(1)} %collective-permute-done.18.refs_1_), custom_call_target="tpu_custom_call" | custom-call | tf_op jit(solution)/shard_map/pallas_call | solution.py:310
  (1 shorter events, 0.0 us)
Async XLA Ops:
  0.0 1.0 %copy-start = (bf16[192,768]{1,0:T(8,128)(2,1)S(1)}, bf16[192,768]{1,0:T(8,128)(2,1)}, u32[]{:S(2)}) copy-start(bf16[192,768]{1,0:T(8,128)(2,1)} %rows.3) | copy-start | bytes 884740
  1.0 5.3 %copy-start.2 = (s32[192]{0:T(256)S(1)}, s32[192]{0:T(256)}, u32[]{:S(2)}) copy-start(s32[192]{0:T(256)} %param.5) | copy-start | bytes 2308
  1.0 8.0 %collective-permute-start.2 = (bf16[584,128]{1,0:T(8,128)(2,1)S(1)}, bf16[584,128]{1,0:T(8,128)(2,1)S(1)}, u32[]{:S(2)}, u32[]{:S(2)}) collective-permute-start(bf16[584,128]{1,0:T(8,128)(2,1)S(1)} %shard_map.38.refs_0_), channel_id=1, source_target_pairs={{0,3},{1,2},{2,1},{3,0},{4,7},{5,6},{6,5},{7,4},{8,11},{9,10},{10,... | collective-permute-start | bytes 448520 | tf_op jit(solution)/shard_map/ppermute | solution.py:353
  3.4 6.7 %collective-permute-start.1 = (bf16[584,128]{1,0:T(8,128)(2,1)S(1)}, bf16[584,128]{1,0:T(8,128)(2,1)S(1)}, u32[]{:S(2)}, u32[]{:S(2)}) collective-permute-start(bf16[584,128]{1,0:T(8,128)(2,1)S(1)} %shard_map.38.refs_0_), channel_id=1, source_target_pairs={{4,1},{5,0},{0,9},{1,8},{8,13},{9,12},{12,5},{13,4},{6,3},{7,2},{2... | collective-permute-start | bytes 448520 | tf_op jit(solution)/shard_map/ppermute | solution.py:342
  6.3 0.7 %copy-start.1 = (s32[192,1]{0,1:T(1,128)S(1)}, s32[192,1]{0,1:T(1,128)}, u32[]{:S(2)}) copy-start(s32[192,1]{0,1:T(1,128)} %param.4) | copy-start | bytes 2308
  7.1 6.3 %collective-permute-start.4 = (bf16[592,128]{1,0:T(8,128)(2,1)S(1)}, bf16[592,128]{1,0:T(8,128)(2,1)S(1)}, u32[]{:S(2)}, u32[]{:S(2)}) collective-permute-start(bf16[592,128]{1,0:T(8,128)(2,1)S(1)} %get-tuple-element.31.refs_1_), channel_id=1, source_target_pairs={{0,3},{1,2},{2,1},{3,0},{4,7},{5,6},{6,5},{7,4},{8,11},{9,10},{10,... | collective-permute-start | bytes 454664 | tf_op jit(solution)/shard_map/ppermute | solution.py:353
  7.2 6.2 %collective-permute-start.3 = (bf16[592,128]{1,0:T(8,128)(2,1)S(1)}, bf16[592,128]{1,0:T(8,128)(2,1)S(1)}, u32[]{:S(2)}, u32[]{:S(2)}) collective-permute-start(bf16[592,128]{1,0:T(8,128)(2,1)S(1)} %get-tuple-element.31.refs_1_), channel_id=1, source_target_pairs={{4,1},{5,0},{0,9},{1,8},{8,13},{9,12},{12,5},{13,4},{6,3},{7,2},{2... | collective-permute-start | bytes 454664 | tf_op jit(solution)/shard_map/ppermute | solution.py:342
  10.1 6.4 %collective-permute-start.6 = (bf16[584,128]{1,0:T(8,128)(2,1)S(1)}, bf16[584,128]{1,0:T(8,128)(2,1)S(1)}, u32[]{:S(2)}, u32[]{:S(2)}) collective-permute-start(bf16[584,128]{1,0:T(8,128)(2,1)S(1)} %collective-permute-done.1.refs_4_.near_first), channel_id=1, source_target_pairs={{0,3},{1,2},{2,1},{3,0},{4,7},{5,6},{6,5},{7,4},{8,11},{9,10},{10,... | collective-permute-start | bytes 448520 | tf_op jit(solution)/shard_map/ppermute | solution.py:353
  10.1 8.1 %collective-permute-start.5 = (bf16[584,128]{1,0:T(8,128)(2,1)S(1)}, bf16[584,128]{1,0:T(8,128)(2,1)S(1)}, u32[]{:S(2)}, u32[]{:S(2)}) collective-permute-start(bf16[584,128]{1,0:T(8,128)(2,1)S(1)} %collective-permute-done.1.refs_4_.near_first), channel_id=1, source_target_pairs={{4,1},{5,0},{0,9},{1,8},{8,13},{9,12},{12,5},{13,4},{6,3},{7,2},{2... | collective-permute-start | bytes 448520 | tf_op jit(solution)/shard_map/ppermute | solution.py:342
  13.2 6.0 %collective-permute-start.11 = (bf16[584,128]{1,0:T(8,128)(2,1)S(1)}, bf16[584,128]{1,0:T(8,128)(2,1)S(1)}, u32[]{:S(2)}, u32[]{:S(2)}) collective-permute-start(bf16[584,128]{1,0:T(8,128)(2,1)S(1)} %collective-permute-done.1.refs_4_.near_first), channel_id=1, source_target_pairs={{0,1},{1,0},{2,3},{3,2},{4,5},{5,4},{6,7},{7,6},{8,9},{9,8},{10,11... | collective-permute-start | bytes 448520 | tf_op jit(solution)/shard_map/ppermute | solution.py:356
  13.4 6.2 %collective-permute-start.12 = (bf16[592,128]{1,0:T(8,128)(2,1)S(1)}, bf16[592,128]{1,0:T(8,128)(2,1)S(1)}, u32[]{:S(2)}, u32[]{:S(2)}) collective-permute-start(bf16[592,128]{1,0:T(8,128)(2,1)S(1)} %collective-permute-done.3.refs_5_.near_second), channel_id=1, source_target_pairs={{0,1},{1,0},{2,3},{3,2},{4,5},{5,4},{6,7},{7,6},{8,9},{9,8},{10,11... | collective-permute-start | bytes 454664 | tf_op jit(solution)/shard_map/ppermute | solution.py:356
  13.8 7.2 %collective-permute-start.8 = (bf16[592,128]{1,0:T(8,128)(2,1)S(1)}, bf16[592,128]{1,0:T(8,128)(2,1)S(1)}, u32[]{:S(2)}, u32[]{:S(2)}) collective-permute-start(bf16[592,128]{1,0:T(8,128)(2,1)S(1)} %collective-permute-done.3.refs_5_.near_second), channel_id=1, source_target_pairs={{0,3},{1,2},{2,1},{3,0},{4,7},{5,6},{6,5},{7,4},{8,11},{9,10},{10,... | collective-permute-start | bytes 454664 | tf_op jit(solution)/shard_map/ppermute | solution.py:353
  16.6 5.9 %collective-permute-start.7 = (bf16[592,128]{1,0:T(8,128)(2,1)S(1)}, bf16[592,128]{1,0:T(8,128)(2,1)S(1)}, u32[]{:S(2)}, u32[]{:S(2)}) collective-permute-start(bf16[592,128]{1,0:T(8,128)(2,1)S(1)} %collective-permute-done.3.refs_5_.near_second), channel_id=1, source_target_pairs={{4,1},{5,0},{0,9},{1,8},{8,13},{9,12},{12,5},{13,4},{6,3},{7,2},{2... | collective-permute-start | bytes 454664 | tf_op jit(solution)/shard_map/ppermute | solution.py:342
  18.2 6.0 %collective-permute-start.9 = (bf16[584,128]{1,0:T(8,128)(2,1)S(1)}, bf16[584,128]{1,0:T(8,128)(2,1)S(1)}, u32[]{:S(2)}, u32[]{:S(2)}) collective-permute-start(bf16[584,128]{1,0:T(8,128)(2,1)S(1)} %collective-permute-done.5.refs_6_), channel_id=1, source_target_pairs={{0,3},{1,2},{2,1},{3,0},{4,7},{5,6},{6,5},{7,4},{8,11},{9,10},{10,... | collective-permute-start | bytes 448520 | tf_op jit(solution)/shard_map/ppermute | solution.py:353
  19.2 8.0 %collective-permute-start = (bf16[1168,128]{1,0:T(8,128)(2,1)S(1)}, bf16[1168,128]{1,0:T(8,128)(2,1)S(1)}, u32[]{:S(2)}, u32[]{:S(2)}) collective-permute-start(bf16[1168,128]{1,0:T(8,128)(2,1)S(1)} %get-tuple-element.29.own), channel_id=1, source_target_pairs={{0,1},{1,0},{2,3},{3,2},{4,5},{5,4},{6,7},{7,6},{8,9},{9,8},{10,11... | collective-permute-start | bytes 897032 | tf_op jit(solution)/shard_map/ppermute | solution.py:356
  20.7 4.4 %collective-permute-start.13 = (bf16[64,896]{1,0:T(8,128)(2,1)S(1)}, bf16[64,896]{1,0:T(8,128)(2,1)S(1)}, u32[]{:S(2)}, u32[]{:S(2)}) collective-permute-start(bf16[64,896]{1,0:T(8,128)(2,1)S(1)} %get-tuple-element.48), channel_id=1, source_target_pairs={{0,1},{1,0},{2,3},{3,2},{4,5},{5,4},{6,7},{7,6},{8,9},{9,8},{10,11... | collective-permute-start | bytes 344072 | tf_op jit(solution)/shard_map/ppermute | solution.py:356
  20.9 4.1 %collective-permute-start.14 = (bf16[64,896]{1,0:T(8,128)(2,1)S(1)}, bf16[64,896]{1,0:T(8,128)(2,1)S(1)}, u32[]{:S(2)}, u32[]{:S(2)}) collective-permute-start(bf16[64,896]{1,0:T(8,128)(2,1)S(1)} %get-tuple-element.49), channel_id=1, source_target_pairs={{0,1},{1,0},{2,3},{3,2},{4,5},{5,4},{6,7},{7,6},{8,9},{9,8},{10,11... | collective-permute-start | bytes 344072 | tf_op jit(solution)/shard_map/ppermute | solution.py:356
  22.5 2.6 %collective-permute-start.15 = (bf16[64,896]{1,0:T(8,128)(2,1)S(1)}, bf16[64,896]{1,0:T(8,128)(2,1)S(1)}, u32[]{:S(2)}, u32[]{:S(2)}) collective-permute-start(bf16[64,896]{1,0:T(8,128)(2,1)S(1)} %get-tuple-element.50), channel_id=1, source_target_pairs={{0,1},{1,0},{2,3},{3,2},{4,5},{5,4},{6,7},{7,6},{8,9},{9,8},{10,11... | collective-permute-start | bytes 344072 | tf_op jit(solution)/shard_map/ppermute | solution.py:356
  24.2 6.2 %collective-permute-start.10 = (bf16[592,128]{1,0:T(8,128)(2,1)S(1)}, bf16[592,128]{1,0:T(8,128)(2,1)S(1)}, u32[]{:S(2)}, u32[]{:S(2)}) collective-permute-start(bf16[592,128]{1,0:T(8,128)(2,1)S(1)} %collective-permute-done.7.refs_7_), channel_id=1, source_target_pairs={{0,3},{1,2},{2,1},{3,0},{4,7},{5,6},{6,5},{7,4},{8,11},{9,10},{10,... | collective-permute-start | bytes 454664 | tf_op jit(solution)/shard_map/ppermute | solution.py:353
  25.4 9.8 %collective-permute-start.16 = (bf16[1168,128]{1,0:T(8,128)(2,1)S(1)}, bf16[1168,128]{1,0:T(8,128)(2,1)S(1)}, u32[]{:S(2)}, u32[]{:S(2)}) collective-permute-start(bf16[1168,128]{1,0:T(8,128)(2,1)S(1)} %shard_map.42), channel_id=1, source_target_pairs={{0,5},{1,4},{8,1},{9,0},{12,9},{13,8},{4,13},{5,12},{2,7},{3,6},{1... | collective-permute-start | bytes 897032 | tf_op jit(solution)/shard_map/ppermute | solution.py:350
  31.2 4.0 %collective-permute-start.17 = (bf16[96,896]{1,0:T(8,128)(2,1)S(1)}, bf16[96,896]{1,0:T(8,128)(2,1)S(1)}, u32[]{:S(2)}, u32[]{:S(2)}) collective-permute-start(bf16[96,896]{1,0:T(8,128)(2,1)S(1)} %get-tuple-element.51), channel_id=1, source_target_pairs={{0,1},{1,0},{2,3},{3,2},{4,5},{5,4},{6,7},{7,6},{8,9},{9,8},{10,11... | collective-permute-start | bytes 516104 | tf_op jit(solution)/shard_map/ppermute | solution.py:356
  31.5 3.7 %collective-permute-start.18 = (bf16[96,896]{1,0:T(8,128)(2,1)S(1)}, bf16[96,896]{1,0:T(8,128)(2,1)S(1)}, u32[]{:S(2)}, u32[]{:S(2)}) collective-permute-start(bf16[96,896]{1,0:T(8,128)(2,1)S(1)} %get-tuple-element.52), channel_id=1, source_target_pairs={{0,1},{1,0},{2,3},{3,2},{4,5},{5,4},{6,7},{7,6},{8,9},{9,8},{10,11... | collective-permute-start | bytes 516104 | tf_op jit(solution)/shard_map/ppermute | solution.py:356
